TPU v7x, 32 devices: a whole 2x2x4 slice. The times are simulated.
32 devices in a mesh: grp: 2 (over x), blk: 16 (over z, y, core).
Axes of the slice: x: 2, y: 2, z: 4, core: 2. Of those that a mesh axis runs over, the one named last changes fastest.
Arguments:
- grad_out: bfloat16 [64, 14336], P(('grp', 'blk')), parts along dimension 0, may hold values from -6 to 6
- activations: bfloat16 [64, 4096], P(('grp', 'blk')), parts along dimension 0, may hold values from -6 to 6
- basis_out: bfloat16 [14336, 14336], P(None, 'blk'), may hold values from -0.046875 to 0.046875
- basis_in: bfloat16 [4096, 4096], P(None, 'blk'), may hold values from -0.09375 to 0.09375
- eigenvalues: float32 [14336, 4096], P('blk'), may hold values from 0.02 to 0.5
- tile_order: int32 [32], replicated, may hold values from 0 to 31, each once
- block_map: int32 [16], replicated, may hold values from 0 to 15, each once
Outputs:
- precond_window: float32 [1536, 512], P(('grp', 'blk')), parts along dimension 0
There are 2 independent parts, one for each index of `grp`. A program takes and returns all parts, laid end to end along the dimension named above; an argument that names none is the same for every part. Nothing has to cross between parts.
Inputs may be any that keep to these rules, and one draw needn't show every extreme that they name: tile_order is a permutation. block_map is a permutation; activations' rows s * 2 onward belong to token block block_map[s].
All inputs are finite; a program needn't handle non-finite values.
Results may differ from a plain program's by a relative error of at most 0.0055.
Values may be sent and summed in bfloat16 or wider, within the bound.
No kernel may reach another device: no remote copies, remote signals or barrier semaphores. Data moves between devices by JAX's collectives and lax.ppermute only.
A program may use at most 192 MiB of HBM per device.

v0:
```python
import jax
import jax.numpy as jnp
from jax import lax
from jax.sharding import PartitionSpec as P

WR = 768
WC = 512


def split_dot(left, right, data_left):
    if data_left:
        upper = left.astype(jnp.bfloat16)
        lower = (left - upper.astype(jnp.float32)).astype(jnp.bfloat16)
        return jnp.dot(upper, right, preferred_element_type=jnp.float32) + jnp.dot(
            lower, right, preferred_element_type=jnp.float32
        )
    upper = right.astype(jnp.bfloat16)
    lower = (right - upper.astype(jnp.float32)).astype(jnp.bfloat16)
    return jnp.dot(left, upper, preferred_element_type=jnp.float32) + jnp.dot(
        left, lower, preferred_element_type=jnp.float32
    )


def body(grad_out, activations, basis_out, basis_in, eigenvalues, tile_order, block_map):
    n_blocks = lax.axis_size("blk")
    tile_width = basis_out.shape[1]
    tok_rows = grad_out.shape[0]
    full_in = eigenvalues.shape[1]
    rotated_out = jnp.dot(
        lax.all_gather(grad_out, "blk", axis=0, tiled=True),
        basis_out,
        preferred_element_type=jnp.float32,
    ).astype(jnp.bfloat16)
    in_tile = jnp.dot(
        lax.all_gather(activations, "blk", axis=0, tiled=True),
        basis_in,
        preferred_element_type=jnp.float32,
    ).astype(jnp.bfloat16)
    rotated_in = lax.all_gather(in_tile, "blk", axis=1, tiled=True)
    all_tokens = rotated_out.shape[0]
    aligned_out = jnp.take(
        rotated_out.reshape(n_blocks, tok_rows, tile_width), block_map, axis=0
    ).reshape(all_tokens, tile_width)
    grad_tile = (
        lax.dot_general(
            aligned_out, rotated_in, (((0,), (0,)), ((), ())), preferred_element_type=jnp.float32
        )
        / all_tokens
    )
    tile_count = tile_order.shape[0]
    damped = jnp.take(
        eigenvalues.reshape(tile_width, tile_count, full_in // tile_count), tile_order, axis=1
    ).reshape(tile_width, full_in)
    scaled = grad_tile / damped
    out_window = basis_out[:WR]
    in_rows = lax.all_gather(basis_in[:WC], "blk", axis=1, tiled=True)
    projected = split_dot(scaled, in_rows.T, True)
    return lax.psum_scatter(
        split_dot(out_window, projected, False), "blk", scatter_dimension=0, tiled=True
    )


def solution(mesh):
    placed = (
        P(("grp", "blk"), None),
        P(("grp", "blk"), None),
        P(None, "blk"),
        P(None, "blk"),
        P("blk", None),
        P(),
        P(),
    )
    return jax.shard_map(
        body, mesh=mesh, in_specs=placed, out_specs=P(("grp", "blk"), None), check_vma=False
    )
```

profile of v0, /device:TPU:0, one launch (start us, length us, event | category | flops | bytes accessed | tf_op | source)
XLA Modules:
  0.0 233.4 jit_solution(17506375566196760382)
XLA Ops:
  6.5 1.7 slice.6
  8.2 0.0 reduce-scatter.4.cloned.1.call-start
  8.3 16.2 %copy.15 = f32[896,4096]{0,1:T(8,128)} copy(f32[896,4096]{1,0:T(8,128)} %param.11) | data formatting | bytes 29360128 | tf_op args[4]
  24.5 16.1 %copy.16 = f32[896,32,128]{2,0,1:T(8,128)} copy(f32[896,32,128]{0,2,1:T(8,128)} %bitcast.23) | data formatting | bytes 29360128 | tf_op jit(solution)/shard_map/reshape | solution.py:52
  40.6 29.7 %all-gather = bf16[16,2,14336]{2,1,0:T(2,128)(2,1)S(1)} all-gather(bf16[1,2,14336]{2,1,0:T(2,128)(2,1)S(1)} %bitcast.24), channel_id=1, replica_groups=mesh['grp'=2,'blk'=16] {'blk'}, dimensions={0}, use_global_device_ids=true | all-gather | bytes 974848 | tf_op jit(solution)/shard_map/all_gather | solution.py:30
  70.4 0.3 reshape.43
  70.7 10.6 %convolution_convert_fusion = bf16[32,896]{1,0:T(8,128)(2,1)S(1)} fusion(bf16[32,14336]{1,0:T(8,128)(2,1)S(1)} %reshape.43, bf16[14336,896]{1,0:T(8,128)(2,1)} %param.9), kind=kOutput, calls=%fused_computation.15 | convolution fusion | flops 822112256 | bytes 26664960 | tf_op jit(solution)/shard_map/dot_general | solution.py:29
  81.4 0.7 gather_fusion
  82.1 18.0 %all-gather.1 = bf16[16,2,4096]{2,1,0:T(2,128)(2,1)S(1)} all-gather(bf16[1,2,4096]{2,1,0:T(2,128)(2,1)S(1)} %bitcast.25), channel_id=1, replica_groups=mesh['grp'=2,'blk'=16] {'blk'}, dimensions={0}, use_global_device_ids=true | all-gather | bytes 278528 | tf_op jit(solution)/shard_map/all_gather | solution.py:35
  100.1 0.1 reshape.45
  100.2 0.1 broadcast_in_dim.32
  100.3 0.1 broadcast_in_dim.33
  100.4 12.0 %gather_fusion.1 = f32[32,896,128]{2,1,0:T(8,128)} fusion(f32[896,32,128]{2,0,1:T(8,128)} %copy.16, s32[1024]{0:T(1024)S(1)} %pad_clamp_fusion), kind=kCustom, calls=%fused_computation.1 | custom fusion | bytes 29360256 | tf_op jit(solution)/shard_map/jit(_take)/gather | solution.py:51
  112.4 0.5 convolution_convert_fusion.1
  112.8 19.8 %all_gather.14 = bf16[32,4096]{1,0:T(8,128)(2,1)S(1)} all-gather(bf16[32,256]{1,0:T(8,128)(2,1)S(1)} %convolution_convert_fusion.1), channel_id=1, replica_groups=mesh['grp'=2,'blk'=16] {'blk'}, dimensions={1}, use_global_device_ids=true | all-gather | bytes 278528 | tf_op jit(solution)/shard_map/all_gather | solution.py:39
  132.7 0.1 broadcast_bitcast_fusion
  132.7 9.5 %fusion = f32[896,4096]{1,0:T(8,128)} fusion(bf16[32,4096]{1,0:T(8,128)(2,1)S(1)} %all_gather.14, pred[4096]{0:T(1024)(128)(4,1)S(1)} %broadcast_bitcast_fusion, bf16[32,896]{1,0:T(8,128)(2,1)S(1)} %gather.13, pred[32]{0:T(512)(128)(4,1)S(1)} %broadcast_in_dim.33, f32[32,896,128]{2,1,0:T(8,128)} %gather_fusion.1), kind=kOutput, calls=%fused_computation.3 | convolution fusion | flops 245919744 | bytes 29683744 | tf_op jit(solution)/shard_map/dot_general | solution.py:45
  142.3 13.3 %fusion.1 = f32[896,512]{1,0:T(8,128)S(1)} fusion(bf16[512,4096]{1,0:T(8,128)(2,1)} %all-gather.4.cloned.1.call-done, f32[896,4096]{1,0:T(8,128)} %fusion), kind=kOutput, calls=%fused_computation.5 | convolution fusion | flops 3772776448 | bytes 20709376 | tf_op jit(solution)/shard_map/dot_general | solution.py:14
  155.6 7.5 %fusion.5 = f32[896,512]{1,0:T(8,128)S(1)} fusion(f32[896,512]{1,0:T(8,128)S(1)} %fusion.1, bf16[512,4096]{1,0:T(8,128)(2,1)S(1)} %copy-done.3, f32[896,4096]{1,0:T(8,128)} %fusion), kind=kOutput, calls=%fused_computation.11 | convolution fusion | flops 3762225152 | bytes 22544384 | tf_op jit(solution)/shard_map/dot_general | solution.py:14
  163.2 2.4 %fusion.9 = f32[512,768]{1,0:T(8,128)S(1)} fusion(bf16[14336,896]{1,0:T(8,128)(2,1)} %param.9, f32[896,512]{1,0:T(8,128)S(1)} %fusion.5), kind=kOutput, calls=%fused_computation.13 | convolution fusion | flops 705101824 | bytes 4784128 | tf_op jit(solution)/shard_map/dot_general | solution.py:19
  165.6 2.4 %add_bitcast_fusion = f32[768,512]{0,1:T(8,128)S(1)} fusion(f32[512,768]{1,0:T(8,128)S(1)} %fusion.9, bf16[14336,896]{1,0:T(8,128)(2,1)} %param.9, f32[896,512]{1,0:T(8,128)S(1)} %fusion.5), kind=kOutput, calls=%fused_computation.10 | convolution fusion | flops 706871296 | bytes 6356992 | tf_op jit(solution)/shard_map/dot_general | solution.py:19
  168.0 1.6 copy.19
  169.6 0.0 reduce-scatter.4.cloned.1.call-update
  169.6 56.9 %reduce-scatter.4.cloned.1.call-done = f32[48,512]{1,0:T(8,128)} async-done(((f32[768,512]{1,0:T(8,128)}), f32[48,512]{1,0:T(8,128)}) %reduce-scatter.4.cloned.1.call-update) | async-done | bytes 98320 | tf_op jit(solution)/shard_map/reduce_scatter | solution.py:58
  (23 shorter events, 0.1 us)
Async XLA Ops:
  6.5 135.7 %all-gather.4.cloned.1.call-start = ((), (), s32[]{:S(2)}) async-start(), calls=%async_computation.1 | async-start | bytes 4456448 | tf_op jit(solution)/shard_map/all_gather | solution.py:56
  8.2 218.3 %reduce-scatter.4.cloned.1.call-start = ((), (), s32[]{:S(2)}) async-start(), calls=%async_computation.2 | async-start | bytes 1671168 | tf_op jit(solution)/shard_map/reduce_scatter | solution.py:58
  24.5 16.1 %copy-start.1 = (bf16[2,14336]{1,0:T(2,128)(2,1)S(1)}, bf16[2,14336]{1,0:T(2,128)(2,1)}, u32[]{:S(2)}) copy-start(bf16[2,14336]{1,0:T(2,128)(2,1)} %param.7) | copy-start | bytes 172036
  70.7 10.6 %copy-start.4 = (s32[16]{0:T(128)S(1)}, s32[16]{0:T(128)}, u32[]{:S(2)}) copy-start(s32[16]{0:T(128)} %param.13) | copy-start | bytes 196
  70.7 11.4 %copy-start.2 = (bf16[2,4096]{1,0:T(2,128)(2,1)S(1)}, bf16[2,4096]{1,0:T(2,128)(2,1)}, u32[]{:S(2)}) copy-start(bf16[2,4096]{1,0:T(2,128)(2,1)} %param.8) | copy-start | bytes 49156
  70.7 29.7 %copy-start.5 = (s32[32]{0:T(128)S(1)}, s32[32]{0:T(128)}, u32[]{:S(2)}) copy-start(s32[32]{0:T(128)} %param.12) | copy-start | bytes 388
  100.4 12.0 %copy-start = (bf16[4096,256]{1,0:T(8,128)(2,1)S(1)}, bf16[4096,256]{1,0:T(8,128)(2,1)}, u32[]{:S(2)}) copy-start(bf16[4096,256]{1,0:T(8,128)(2,1)} %param.10) | copy-start | bytes 6291460
  142.3 13.4 %copy-start.3 = (bf16[512,4096]{1,0:T(8,128)(2,1)S(1)}, bf16[512,4096]{1,0:T(8,128)(2,1)}, u32[]{:S(2)}) copy-start(bf16[512,4096]{1,0:T(8,128)(2,1)} %all-gather.4.cloned.1.call-done) | copy-start | bytes 12582916
Sparse Core Ops, SparseCore 0:
  9.5 63.0 all-gather.3
  169.7 56.7 reduce-scatter.3
where the time goes:
time: 234 us; the launch traced here: 233 us
  blocking collectives  67.5 us (29%)
  waiting for transfers between devices  57 us (24%)
  local copies, waits for them, and re-layouts  49 us (21%)
  matrix products  46.2 us (20%)
  between operations  13.6 us (6%)
    reduce_scatter x1, waiting for transfers between devices, body(): lax.psum_scatter(split_dot(out_window, projected, False), 'blk', scatter_...  56.9 us
    all_gather x1, blocking collectives, body(): lax.all_gather(grad_out, 'blk', axis=0, tiled=True)  29.7 us
    all_gather x1, blocking collectives, body(): rotated_in = lax.all_gather(in_tile, 'blk', axis=1, tiled=True)  19.8 us
    unnamed x16, local copies, waits for them, and re-layouts  18.3 us
    all_gather x1, blocking collectives, body(): lax.all_gather(activations, 'blk', axis=0, tiled=True)  18 us
    reshape x1, local copies, waits for them, and re-layouts, body(): eigenvalues.reshape(tile_width, tile_count, full_in // tile_count)  16.1 us
    dot_general x1, matrix products, split_dot(): jnp.dot(lower, right, preferred_element_type=jnp.float32)  13.3 us
    gather x1, local copies, waits for them, and re-layouts, body(): jnp.take(eigenvalues.reshape(tile_width, tile_count, full_in // tile_coun...  12 us
  transfers between devices with their start and end apart: 2, of which 1 were waited for; matrix products, arithmetic and copies ran while one was open for 28% of the time, Pallas kernels for 0%

commit v1 on v0

v1 whole, which is shorter than its diff:
```python
import functools

import jax
import jax.numpy as jnp
import numpy as np
from jax import lax
from jax.experimental import pallas as pl
from jax.experimental.pallas import tpu as pltpu
from jax.sharding import PartitionSpec as P

WR = 768
WC = 512
LANES = 128
MIB = 1 << 20


def ring_of(n):
    chips = n // 2
    return [*range(0, chips, 2), *range(chips - 1, 0, -2)]


def shift_pairs(n, by):
    ring = ring_of(n)
    return [
        (2 * ring[p] + c, 2 * ring[(p + by) % len(ring)] + c)
        for p in range(len(ring))
        for c in range(2)
    ]


def xor_pairs(n, key):
    return [(b, b ^ (2 * key)) for b in range(n)]


def core_pairs(n):
    return [(b, b ^ 1) for b in range(n)]


def ring_sources(n):
    ring = ring_of(n)
    table = np.zeros((n, n), np.int32)
    for b in range(n):
        place = ring.index(b // 2)
        for k in range(n // 2):
            chip = ring[(place - k) % len(ring)]
            table[b, k] = 2 * chip + b % 2
            table[b, n // 2 + k] = 2 * chip + 1 - b % 2
    return table


def xor_sources(n):
    table = np.zeros((n, n), np.int32)
    for b in range(n):
        for k in range(n // 2):
            table[b, k] = 2 * (b // 2 ^ k) + b % 2
            table[b, n // 2 + k] = 2 * (b // 2 ^ k) + 1 - b % 2
    return table


def place_of(table):
    return np.argsort(table, axis=1).astype(np.int32)


def ring_gather(x, n, far_right):
    chips = n // 2
    pieces = [None] * chips
    pieces[0] = x
    right, left = x, x
    for step in range(1, chips // 2 + 1):
        if step < chips // 2 or far_right:
            right = lax.ppermute(right, "blk", shift_pairs(n, 1))
            pieces[step] = right
        if step < chips // 2 or not far_right:
            left = lax.ppermute(left, "blk", shift_pairs(n, -1))
            pieces[chips - step] = left
    return pieces


def direct_gather(x, n):
    return [x] + [lax.ppermute(x, "blk", xor_pairs(n, k)) for k in range(1, n // 2)]


def rotate_in_kernel(lower, near_ref, far_ref, basis_ref, order_ref, message_ref):
    acts = jnp.concatenate([near_ref[...], far_ref[...]], axis=0)
    rotated = jnp.dot(acts, basis_ref[...], preferred_element_type=jnp.float32)
    ordered = jnp.dot(
        order_ref[...], rotated.astype(jnp.bfloat16), preferred_element_type=jnp.float32
    )
    half = message_ref.shape[0] - ordered.shape[0]
    message_ref[:half, :] = basis_ref[lower : lower + half, :]
    message_ref[half:, :] = ordered.astype(jnp.bfloat16)


def rotate_out_kernel(near_ref, far_ref, basis_ref, order_ref, out_ref, total):
    step = pl.program_id(0)

    @pl.when(step == 0)
    def _():
        total[...] = jnp.zeros_like(total)

    grads = jnp.concatenate([near_ref[...], far_ref[...]], axis=0)
    total[...] += jnp.dot(grads, basis_ref[...], preferred_element_type=jnp.float32)

    @pl.when(step == pl.num_programs(0) - 1)
    def _():
        aligned = jnp.dot(
            order_ref[...], total[...].astype(jnp.bfloat16), preferred_element_type=jnp.float32
        )
        out_ref[...] = aligned.T.astype(jnp.bfloat16)


def window_kernel(
    n,
    scale,
    tiles_ref,
    sources_ref,
    blocks_ref,
    aligned_ref,
    window_ref,
    eigen_ref,
    *refs,
):
    pieces = refs[: 2 * n]
    send_ref, keep_ref = refs[2 * n : 2 * n + 2]
    basis, rotated, damped, projected, result, piece_sem, eigen_sem = refs[2 * n + 2 :]
    width = basis.shape[2]
    half = basis.shape[1] // 2
    per_piece = width // LANES

    def eigen_copy(at):
        source = sources_ref[at // per_piece] * per_piece + at % per_piece
        column = pl.multiple_of(tiles_ref[source] * LANES, LANES)
        return pltpu.make_async_copy(
            eigen_ref.at[:, pl.ds(column, LANES)], damped.at[at], eigen_sem.at[at]
        )

    def piece_copies(at):
        upper, lower = pieces[2 * at], pieces[2 * at + 1]
        return (
            pltpu.make_async_copy(upper, basis.at[at, pl.ds(0, half)], piece_sem.at[at, 0]),
            pltpu.make_async_copy(
                lower.at[pl.ds(0, half)], basis.at[at, pl.ds(half, half)], piece_sem.at[at, 1]
            ),
            pltpu.make_async_copy(
                lower.at[pl.ds(half, rotated.shape[1])], rotated.at[at], piece_sem.at[at, 2]
            ),
        )

    for at in range(n):
        for copy in piece_copies(at):
            copy.start()
        for tile in range(per_piece):
            eigen_copy(at * per_piece + tile).start()
    projected[...] = jnp.zeros_like(projected)
    for at in range(n):
        for copy in piece_copies(at):
            copy.wait()

    @pl.loop(0, n)
    def _(at):
        grad = jnp.dot(aligned_ref[...], rotated[at], preferred_element_type=jnp.float32)
        parts = []
        for tile in range(per_piece):
            eigen_copy(at * per_piece + tile).wait()
            columns = grad[:, tile * LANES : (tile + 1) * LANES]
            parts.append((columns / damped[at * per_piece + tile]).astype(jnp.bfloat16))
        scaled = jnp.concatenate(parts, axis=1)
        projected[...] += lax.dot_general(
            scaled, basis[at], (((1,), (1,)), ((), ())), preferred_element_type=jnp.float32
        )

    result[...] = scale * jnp.dot(
        window_ref[...], projected[...].astype(jnp.bfloat16), preferred_element_type=jnp.float32
    )
    rows = keep_ref.shape[1]
    for k in range(n // 2):
        keep_ref[k] = result[pl.ds(pl.multiple_of(blocks_ref[k] * rows, rows), rows), :]
        other = result[pl.ds(pl.multiple_of(blocks_ref[n // 2 + k] * rows, rows), rows), :]
        send_ref[k] = other.astype(jnp.bfloat16)


def add_core_kernel(keep_ref, got_ref, own_ref, *out_refs):
    own_ref[...] = keep_ref[0] + got_ref[0].astype(jnp.float32)
    for k, out_ref in enumerate(out_refs, 1):
        out_ref[...] = (keep_ref[k] + got_ref[k].astype(jnp.float32)).astype(jnp.bfloat16)


def add_chips_kernel(own_ref, *refs):
    total = own_ref[...]
    for ref in refs[:-1]:
        total += ref[...].astype(jnp.float32)
    refs[-1][...] = total


VMEM = pl.BlockSpec(memory_space=pltpu.VMEM)
SMEM = pl.BlockSpec(memory_space=pltpu.SMEM)
ANY = pl.BlockSpec(memory_space=pl.ANY)


def one_hot(index):
    columns = lax.broadcasted_iota(jnp.int32, (index.shape[0], index.shape[0]), 1)
    return (index[:, None] == columns).astype(jnp.bfloat16)


def rows_of(blocks, tok_rows):
    return (blocks[:, None] * tok_rows + jnp.arange(tok_rows)[None, :]).reshape(-1)


def ring_body(n, grad_out, activations, basis_out, basis_in, eigenvalues, tile_order, block_map):
    tok_rows, full_out = grad_out.shape
    tile_width = basis_out.shape[1]
    full_in, in_width = basis_in.shape
    tokens = n * tok_rows
    half = WC // 2
    me = lax.axis_index("blk")
    pick = lambda table: lax.dynamic_index_in_dim(jnp.asarray(table), me, 0, keepdims=False)

    acts = jnp.concatenate(direct_gather(activations, n), axis=0)
    acts_far = lax.ppermute(acts, "blk", core_pairs(n))
    order_in = one_hot(rows_of(pick(place_of(xor_sources(n))), tok_rows))
    message = pl.pallas_call(
        functools.partial(rotate_in_kernel, half),
        out_shape=jax.ShapeDtypeStruct((half + tokens, in_width), jnp.bfloat16),
        in_specs=[VMEM] * 4,
        out_specs=VMEM,
        compiler_params=pltpu.CompilerParams(vmem_limit_bytes=16 * MIB),
        name="rotate_in",
    )(acts, acts_far, basis_in, order_in)

    grads = jnp.concatenate(ring_gather(grad_out, n, True), axis=0)
    grads_far = lax.ppermute(grads, "blk", core_pairs(n))
    order_out = one_hot(rows_of(jnp.take(pick(place_of(ring_sources(n))), block_map), tok_rows))
    depth = 1024
    aligned = pl.pallas_call(
        rotate_out_kernel,
        grid=(full_out // depth,),
        out_shape=jax.ShapeDtypeStruct((tile_width, tokens), jnp.bfloat16),
        in_specs=[
            pl.BlockSpec((tokens // 2, depth), lambda k: (0, k)),
            pl.BlockSpec((tokens // 2, depth), lambda k: (0, k)),
            pl.BlockSpec((depth, tile_width), lambda k: (k, 0)),
            pl.BlockSpec((tokens, tokens), lambda k: (0, 0)),
        ],
        out_specs=pl.BlockSpec((tile_width, tokens), lambda k: (0, 0)),
        scratch_shapes=[pltpu.VMEM((tokens, tile_width), jnp.float32)],
        compiler_params=pltpu.CompilerParams(vmem_limit_bytes=24 * MIB),
        cost_estimate=pl.CostEstimate(
            flops=2 * tokens * full_out * tile_width,
            bytes_accessed=2 * full_out * tile_width,
            transcendentals=0,
        ),
        name="rotate_out",
    )(grads, grads_far, basis_out, order_out)

    upper = ring_gather(basis_in[:half], n, True)
    lower = ring_gather(message, n, False)
    swap = lambda x: lax.ppermute(x, "blk", core_pairs(n))
    pieces = []
    for top, bottom in zip(upper, lower):
        pieces += [top, bottom]
    pieces += [swap(piece) for piece in pieces]

    rows = WR // n
    send, keep = pl.pallas_call(
        functools.partial(window_kernel, n, 1.0 / tokens),
        out_shape=(
            jax.ShapeDtypeStruct((n // 2, rows, WC), jnp.bfloat16),
            jax.ShapeDtypeStruct((n // 2, rows, WC), jnp.float32),
        ),
        grid=(1,),
        in_specs=[
            SMEM,
            SMEM,
            SMEM,
            pl.BlockSpec((tile_width, tokens), lambda i: (0, 0)),
            pl.BlockSpec((WR, tile_width), lambda i: (0, 0)),
        ]
        + [ANY] * (2 * n + 1),
        out_specs=(VMEM, VMEM),
        scratch_shapes=[
            pltpu.VMEM((n, WC, in_width), jnp.bfloat16),
            pltpu.VMEM((n, tokens, in_width), jnp.bfloat16),
            pltpu.VMEM((full_in // LANES, tile_width, LANES), jnp.float32),
            pltpu.VMEM((tile_width, WC), jnp.float32),
            pltpu.VMEM((WR, WC), jnp.float32),
            pltpu.SemaphoreType.DMA((n, 3)),
            pltpu.SemaphoreType.DMA((full_in // LANES,)),
        ],
        compiler_params=pltpu.CompilerParams(vmem_limit_bytes=48 * MIB),
        cost_estimate=pl.CostEstimate(
            flops=2 * tile_width * full_in * (WC + tokens) + 2 * WR * tile_width * WC,
            bytes_accessed=4 * tile_width * full_in + 2 * WC * full_in,
            transcendentals=0,
        ),
        name="window",
    )(
        tile_order,
        pick(ring_sources(n)),
        pick(xor_sources(n)),
        aligned,
        basis_out,
        eigenvalues,
        *pieces,
    )

    got = swap(send)
    block = jax.ShapeDtypeStruct((rows, WC), jnp.bfloat16)
    own, *parts = pl.pallas_call(
        add_core_kernel,
        out_shape=[jax.ShapeDtypeStruct((rows, WC), jnp.float32)] + [block] * (n // 2 - 1),
        in_specs=[VMEM, VMEM],
        out_specs=[VMEM] * (n // 2),
        name="add_core",
    )(keep, got)
    arrived = [lax.ppermute(x, "blk", xor_pairs(n, k)) for k, x in enumerate(parts, 1)]
    return pl.pallas_call(
        add_chips_kernel,
        out_shape=jax.ShapeDtypeStruct((rows, WC), jnp.float32),
        in_specs=[VMEM] * (n // 2),
        out_specs=VMEM,
        name="add_chips",
    )(own, *arrived)


def gather_body(grad_out, activations, basis_out, basis_in, eigenvalues, tile_order, block_map):
    n_blocks = lax.axis_size("blk")
    tile_width = basis_out.shape[1]
    tok_rows = grad_out.shape[0]
    full_in = eigenvalues.shape[1]
    tokens = n_blocks * tok_rows
    dot = functools.partial(jnp.dot, preferred_element_type=jnp.float32)
    in_rows = lax.all_gather(basis_in[:WC], "blk", axis=1, tiled=True)
    acts = lax.all_gather(activations, "blk", axis=0, tiled=True)
    in_tile = dot(acts, basis_in).astype(jnp.bfloat16)
    rotated_in = lax.all_gather(in_tile, "blk", axis=1, tiled=True)
    grads = lax.all_gather(grad_out, "blk", axis=0, tiled=True)
    rotated_out = dot(grads, basis_out).astype(jnp.bfloat16)
    aligned = jnp.take(
        rotated_out.reshape(n_blocks, tok_rows, tile_width), block_map, axis=0
    ).reshape(tokens, tile_width)
    grad_tile = dot(aligned.T, rotated_in) / tokens
    damped = jnp.take(
        eigenvalues.reshape(tile_width, full_in // LANES, LANES), tile_order, axis=1
    ).reshape(tile_width, full_in)
    scaled = (grad_tile / damped).astype(jnp.bfloat16)
    projected = dot(scaled, in_rows.T).astype(jnp.bfloat16)
    return lax.psum_scatter(
        dot(basis_out[:WR], projected), "blk", scatter_dimension=0, tiled=True
    )


def solution(mesh):
    n = mesh.shape["blk"]

    def body(*args):
        wide = args[3].shape[1] % LANES == 0 and args[2].shape[1] % LANES == 0
        if wide and WR % (16 * n) == 0:
            return ring_body(n, *args)
        return gather_body(*args)

    placed = (
        P(("grp", "blk"), None),
        P(("grp", "blk"), None),
        P(None, "blk"),
        P(None, "blk"),
        P("blk", None),
        P(),
        P(),
    )
    return jax.shard_map(
        body, mesh=mesh, in_specs=placed, out_specs=P(("grp", "blk"), None), check_vma=False
    )
```

time: 234 us -> 125 us (0.53)
  blocking collectives: 67.5 us -> 0 us
  starting transfers between devices: 0.04 us -> 50.5 us
  matrix products: 46.2 us -> 0 us
  waiting for transfers between devices: 57 us -> 19.4 us
  Pallas kernels: 0 us -> 32.1 us
  local copies, waits for them, and re-layouts: 49 us -> 18.9 us
  between operations: 13.6 us -> 0.25 us
  other arithmetic: 0.04 us -> 3.55 us
    all_gather x3 -> x0, blocking collectives: 67.5 us -> none  [the longest x1 29.7 us: body(): lax.all_gather(grad_out, 'blk', axis=0, tiled=True)]
    reduce_scatter x1 -> x0, waiting for transfers between devices: 56.9 us -> none  [body(): lax.psum_scatter(split_dot(out_window, projected, False), 'blk', scatter_...]
    ppermute x0 -> x54, starting transfers between devices: none -> 50.5 us  [the longest x11 15 us: ring_gather(): right = lax.ppermute(right, 'blk', shift_pairs(n, 1))]
    dot_general x7 -> x0, matrix products: 46.2 us -> none  [the longest x1 13.3 us: split_dot(): jnp.dot(lower, right, preferred_element_type=jnp.float32)]
    pallas_call x0 -> x5, Pallas kernels: none -> 32.1 us  [the longest x1 21.6 us: ring_body(): pl.pallas_call(functools.partial(window_kernel, n, 1.0 / tokens), out_sha...]
    ppermute x0 -> x54, waiting for transfers between devices: none -> 19.4 us  [the longest x10 6.19 us: ring_gather(): left = lax.ppermute(left, 'blk', shift_pairs(n, -1))]
    reshape x2 -> x0, local copies, waits for them, and re-layouts: 16.2 us -> none  [the longest x1 16.1 us: body(): eigenvalues.reshape(tile_width, tile_count, full_in // tile_count)]
    gather x3 -> x1, local copies, waits for them, and re-layouts: 12.7 us -> 0.66 us  [ring_body(): jnp.take(pick(place_of(ring_sources(n))), block_map)]
  transfers between devices with their start and end apart: 2 -> 54, of which waited for: 1 -> 12; matrix products, arithmetic and copies ran while one was open for 28% -> 8% of each run, Pallas kernels for 0% -> 5%
where the time goes in v1:
time: 125 us
  starting transfers between devices  50.5 us (40%)
  Pallas kernels  32.1 us (26%)
  waiting for transfers between devices  19.4 us (16%)
  local copies, waits for them, and re-layouts  18.9 us (15%)
  other arithmetic  3.55 us (3%)
    pallas_call x1, Pallas kernels, ring_body(): pl.pallas_call(functools.partial(window_kernel, n, 1.0 / tokens), out_sha...  21.6 us
    ppermute x11, starting transfers between devices, ring_gather(): right = lax.ppermute(right, 'blk', shift_pairs(n, 1))  15 us
    unnamed x28, local copies, waits for them, and re-layouts  12.8 us
    ppermute x7, starting transfers between devices, direct_gather(): lax.ppermute(x, 'blk', xor_pairs(n, k))  11.4 us
    ppermute x7, starting transfers between devices, ring_body(): lax.ppermute(x, 'blk', xor_pairs(n, k))  11.2 us
    ppermute x10, starting transfers between devices, ring_gather(): left = lax.ppermute(left, 'blk', shift_pairs(n, -1))  10.2 us
    pallas_call x1, Pallas kernels, ring_body(): pl.pallas_call(rotate_out_kernel, grid=(full_out // depth,), out_shape=ja...  6.28 us
    ppermute x10, waiting for transfers between devices, ring_gather(): left = lax.ppermute(left, 'blk', shift_pairs(n, -1))  6.19 us
  transfers between devices with their start and end apart: 54, of which 12 were waited for; matrix products, arithmetic and copies ran while one was open for 8% of the time, Pallas kernels for 5%

profile of v1, /device:TPU:0, one launch (start us, length us, event | category | flops | bytes accessed | tf_op | source)
XLA Modules:
  0.0 124.8 jit_solution(17679174610618242209)
XLA Ops:
  0.0 3.0 %collective-permute-start = (bf16[2,14336]{1,0:T(2,128)(2,1)}, bf16[2,14336]{1,0:T(2,128)(2,1)S(1)}, u32[]{:S(2)}, u32[]{:S(2)}) collective-permute-start(bf16[2,14336]{1,0:T(2,128)(2,1)} %param.11), channel_id=1, source_target_pairs={{0,4},{1,5},{4,8},{5,9},{8,12},{9,13},{12,14},{13,15},{14,10},{15,... | collective-permute-start | bytes 172040 | tf_op jit(solution)/shard_map/ppermute | solution.py:71
  3.0 3.5 %collective-permute-start.13 = (bf16[2,4096]{1,0:T(2,128)(2,1)}, bf16[2,4096]{1,0:T(2,128)(2,1)S(1)}, u32[]{:S(2)}, u32[]{:S(2)}) collective-permute-start(bf16[2,4096]{1,0:T(2,128)(2,1)} %param.12), channel_id=1, source_target_pairs={{0,12},{1,13},{2,14},{3,15},{4,8},{5,9},{6,10},{7,11},{8,4},{9,5},... | collective-permute-start | bytes 49160 | tf_op jit(solution)/shard_map/ppermute | solution.py:80
  6.6 2.8 %collective-permute-start.11 = (bf16[2,4096]{1,0:T(2,128)(2,1)}, bf16[2,4096]{1,0:T(2,128)(2,1)S(1)}, u32[]{:S(2)}, u32[]{:S(2)}) collective-permute-start(bf16[2,4096]{1,0:T(2,128)(2,1)} %param.12), channel_id=1, source_target_pairs={{0,8},{1,9},{2,10},{3,11},{4,12},{5,13},{6,14},{7,15},{8,0},{9,1},... | collective-permute-start | bytes 49160 | tf_op jit(solution)/shard_map/ppermute | solution.py:80
  10.0 2.4 %collective-permute-start.9 = (bf16[2,4096]{1,0:T(2,128)(2,1)}, bf16[2,4096]{1,0:T(2,128)(2,1)S(1)}, u32[]{:S(2)}, u32[]{:S(2)}) collective-permute-start(bf16[2,4096]{1,0:T(2,128)(2,1)} %param.12), channel_id=1, source_target_pairs={{0,4},{1,5},{2,6},{3,7},{4,0},{5,1},{6,2},{7,3},{8,12},{9,13},{10,... | collective-permute-start | bytes 49160 | tf_op jit(solution)/shard_map/ppermute | solution.py:80
  12.9 1.5 %collective-permute-start.14 = (bf16[2,4096]{1,0:T(2,128)(2,1)}, bf16[2,4096]{1,0:T(2,128)(2,1)S(1)}, u32[]{:S(2)}, u32[]{:S(2)}) collective-permute-start(bf16[2,4096]{1,0:T(2,128)(2,1)} %param.12), channel_id=1, source_target_pairs={{0,14},{1,15},{2,12},{3,13},{4,10},{5,11},{6,8},{7,9},{8,6},{9,7},... | collective-permute-start | bytes 49160 | tf_op jit(solution)/shard_map/ppermute | solution.py:80
  20.8 1.5 %collective-permute-start.5 = (bf16[2,14336]{1,0:T(2,128)(2,1)S(1)}, bf16[2,14336]{1,0:T(2,128)(2,1)S(1)}, u32[]{:S(2)}, u32[]{:S(2)}) collective-permute-start(bf16[2,14336]{1,0:T(2,128)(2,1)S(1)} %collective-permute-done.4), channel_id=1, source_target_pairs={{0,2},{1,3},{4,0},{5,1},{8,4},{9,5},{12,8},{13,9},{14,12},{15,13},... | collective-permute-start | bytes 172040 | tf_op jit(solution)/shard_map/ppermute | solution.py:74
  23.0 2.3 %collective-permute-done.5 = bf16[2,14336]{1,0:T(2,128)(2,1)S(1)} collective-permute-done((bf16[2,14336]{1,0:T(2,128)(2,1)S(1)}, bf16[2,14336]{1,0:T(2,128)(2,1)S(1)}, u32[]{:S(2)}, u32[]{:S(2)}) %collective-permute-start.5) | collective-permute-done | bytes 57376 | tf_op jit(solution)/shard_map/ppermute | solution.py:74
  28.8 1.6 %copy-done.1 = bf16[4096,256]{1,0:T(8,128)(2,1)S(1)} copy-done((bf16[4096,256]{1,0:T(8,128)(2,1)S(1)}, bf16[4096,256]{1,0:T(8,128)(2,1)}, u32[]{:S(2)}) %copy-start.1) | copy-done | bytes 2097176
  34.6 2.9 %collective-permute-done.28.refs_12_ = bf16[256,256]{1,0:T(8,128)(2,1)S(1)} collective-permute-done((bf16[256,256]{1,0:T(8,128)(2,1)S(1)}, bf16[256,256]{1,0:T(8,128)(2,1)S(1)}, u32[]{:S(2)}, u32[]{:S(2)}) %collective-permute-start.28) | collective-permute-done | bytes 131104 | tf_op jit(solution)/shard_map/ppermute | solution.py:74
  41.1 1.5 %concatenate.6.near_ref = bf16[16,14336]{1,0:T(8,128)(2,1)S(1)} concatenate(bf16[2,14336]{1,0:T(2,128)(2,1)} %param.11, bf16[2,14336]{1,0:T(2,128)(2,1)S(1)} %collective-permute-done, bf16[2,14336]{1,0:T(2,128)(2,1)S(1)} %collective-permute-done.1, bf16[2,14336]{1,0:T(2,128)(2,1)S(1)} %collective-permute-done.2, bf16[2,14336]{1,0:T(2,128)(2,1)S(1)} %collective-permute-done.3, ...), dimensions={0} | concatenate | bytes 917504 | tf_op jit(solution)/shard_map/concatenate | solution.py:230
  46.8 2.0 %collective-permute-done.20.refs_6_ = bf16[256,256]{1,0:T(8,128)(2,1)} collective-permute-done((bf16[256,256]{1,0:T(8,128)(2,1)S(1)}, bf16[256,256]{1,0:T(8,128)(2,1)}, u32[]{:S(2)}, u32[]{:S(2)}) %collective-permute-start.20) | collective-permute-done | bytes 131104 | tf_op jit(solution)/shard_map/ppermute | solution.py:71
  55.3 1.7 %collective-permute-start.21 = (bf16[288,256]{1,0:T(8,128)(2,1)S(1)}, bf16[288,256]{1,0:T(8,128)(2,1)S(1)}, u32[]{:S(2)}, u32[]{:S(2)}) collective-permute-start(bf16[288,256]{1,0:T(8,128)(2,1)S(1)} %collective-permute-done.19.refs_5_), channel_id=1, source_target_pairs={{0,4},{1,5},{4,8},{5,9},{8,12},{9,13},{12,14},{13,15},{14,10},{15,... | collective-permute-start | bytes 442376 | tf_op jit(solution)/shard_map/ppermute | solution.py:71
  58.4 1.8 %collective-permute-done.22.refs_8_ = bf16[256,256]{1,0:T(8,128)(2,1)S(1)} collective-permute-done((bf16[256,256]{1,0:T(8,128)(2,1)}, bf16[256,256]{1,0:T(8,128)(2,1)S(1)}, u32[]{:S(2)}, u32[]{:S(2)}) %collective-permute-start.22) | collective-permute-done | bytes 131104 | tf_op jit(solution)/shard_map/ppermute | solution.py:71
  60.8 1.7 %collective-permute-done.21.refs_7_ = bf16[288,256]{1,0:T(8,128)(2,1)S(1)} collective-permute-done((bf16[288,256]{1,0:T(8,128)(2,1)S(1)}, bf16[288,256]{1,0:T(8,128)(2,1)S(1)}, u32[]{:S(2)}, u32[]{:S(2)}) %collective-permute-start.21) | collective-permute-done | bytes 147488 | tf_op jit(solution)/shard_map/ppermute | solution.py:71
  63.8 8.3 %copy-done = bf16[14336,896]{1,0:T(8,128)(2,1)S(1)} copy-done((bf16[14336,896]{1,0:T(8,128)(2,1)S(1)}, bf16[14336,896]{1,0:T(8,128)(2,1)}, u32[]{:S(2)}) %copy-start) | copy-done | bytes 25690136
  72.1 6.3 %rotate_out.1.aligned_ref = bf16[896,32]{1,0:T(8,128)(2,1)S(1)} custom-call(bf16[16,14336]{1,0:T(8,128)(2,1)S(1)} %concatenate.6.near_ref, bf16[16,14336]{1,0:T(8,128)(2,1)S(1)} %collective-permute-done.7.far_ref, bf16[14336,896]{1,0:T(8,128)(2,1)S(1)} %copy-done, bf16[32,32]{1,0:T(8,128)(2,1)S(1)} %fusion.order_ref), custom_call_target="tpu_custom_call" | custom-call | flops 822083584 | bytes 25690112 | tf_op jit(solution)/shard_map/rotate_out/pallas_call | solution.py:234
  78.5 21.6 %window.1 = (bf16[8,48,512]{2,1,0:T(8,128)(2,1)S(1)}, f32[8,48,512]{2,1,0:T(8,128)S(1)}) custom-call(s32[32]{0:T(128)S(1)} %copy-done.5, s32[16]{0:T(128)S(1)} %get-tuple-element.25.sources_ref, s32[16]{0:T(128)S(1)} %get-tuple-element.26.blocks_ref, bf16[896,32]{1,0:T(8,128)(2,1)S(1)} %rotate_out.1.aligned_ref, bf16[14336,896]{1,0:T(8,128)(2,1)} %window_ref.1, ...), custom_call_target="tpu_custom_call" | custom-call | flops 4697620480 | bytes 18874368 | tf_op jit(solution)/shard_map/window/pallas_call | solution.py:264
  103.5 2.0 %add_core.1 = (f32[48,512]{1,0:T(8,128)}, bf16[48,512]{1,0:T(8,128)(2,1)}, bf16[48,512]{1,0:T(8,128)(2,1)}, bf16[48,512]{1,0:T(8,128)(2,1)}, bf16[48,512]{1,0:T(...) custom-call(f32[8,48,512]{2,1,0:T(8,128)} %copy-done.2, ...), custom_call_target="tpu_custom_call" | custom-call | tf_op jit(solution)/shard_map/add_core/pallas_call | solution.py:308
  106.5 1.9 %collective-permute-start.48 = (bf16[48,512]{1,0:T(8,128)(2,1)}, bf16[48,512]{1,0:T(8,128)(2,1)S(1)}, u32[]{:S(2)}, u32[]{:S(2)}) collective-permute-start(bf16[48,512]{1,0:T(8,128)(2,1)} %get-tuple-element.19), channel_id=1, source_target_pairs={{0,4},{1,5},{2,6},{3,7},{4,0},{5,1},{6,2},{7,3},{8,12},{9,13},{10,... | collective-permute-start | bytes 147464 | tf_op jit(solution)/shard_map/ppermute | solution.py:315
  109.0 2.5 %collective-permute-start.50 = (bf16[48,512]{1,0:T(8,128)(2,1)}, bf16[48,512]{1,0:T(8,128)(2,1)S(1)}, u32[]{:S(2)}, u32[]{:S(2)}) collective-permute-start(bf16[48,512]{1,0:T(8,128)(2,1)} %get-tuple-element.21), channel_id=1, source_target_pairs={{0,8},{1,9},{2,10},{3,11},{4,12},{5,13},{6,14},{7,15},{8,0},{9,1},... | collective-permute-start | bytes 147464 | tf_op jit(solution)/shard_map/ppermute | solution.py:315
  112.3 3.1 %collective-permute-start.52 = (bf16[48,512]{1,0:T(8,128)(2,1)}, bf16[48,512]{1,0:T(8,128)(2,1)S(1)}, u32[]{:S(2)}, u32[]{:S(2)}) collective-permute-start(bf16[48,512]{1,0:T(8,128)(2,1)} %get-tuple-element.23), channel_id=1, source_target_pairs={{0,12},{1,13},{2,14},{3,15},{4,8},{5,9},{6,10},{7,11},{8,4},{9,5},... | collective-permute-start | bytes 147464 | tf_op jit(solution)/shard_map/ppermute | solution.py:315
  116.7 1.8 %collective-permute-done.51.refs_4_ = bf16[48,512]{1,0:T(8,128)(2,1)S(1)} collective-permute-done((bf16[48,512]{1,0:T(8,128)(2,1)}, bf16[48,512]{1,0:T(8,128)(2,1)S(1)}, u32[]{:S(2)}, u32[]{:S(2)}) %collective-permute-start.51) | collective-permute-done | bytes 49184 | tf_op jit(solution)/shard_map/ppermute | solution.py:315
  118.5 3.9 %collective-permute-done.53.refs_6_ = bf16[48,512]{1,0:T(8,128)(2,1)S(1)} collective-permute-done((bf16[48,512]{1,0:T(8,128)(2,1)}, bf16[48,512]{1,0:T(8,128)(2,1)S(1)}, u32[]{:S(2)}, u32[]{:S(2)}) %collective-permute-start.53) | collective-permute-done | bytes 49184 | tf_op jit(solution)/shard_map/ppermute | solution.py:315
  123.1 1.7 %add_chips.1 = f32[48,512]{1,0:T(8,128)} custom-call(f32[48,512]{1,0:T(8,128)} %get-tuple-element.17.own_ref, bf16[48,512]{1,0:T(8,128)(2,1)} %copy-done.7, bf16[48,512]{1,0:T(8,128)(2,1)} %copy-done.8, bf16[48,512]{1,0:T(8,128)(2,1)} %copy-done.9, bf16[48,512]{1,0:T(8,128)(2,1)} %copy-done.10, bf16[48,512]{1,0:T(8,128)(2,1)} %copy-done.11, ...), custom_call_target="tpu_custom_call" | custom-call | tf_op jit(solution)/shard_map/add_chips/pallas_call | solution.py:316
  (132 shorter events, 41.1 us)
Async XLA Ops:
  0.0 15.8 %collective-permute-start = (bf16[2,14336]{1,0:T(2,128)(2,1)}, bf16[2,14336]{1,0:T(2,128)(2,1)S(1)}, u32[]{:S(2)}, u32[]{:S(2)}) collective-permute-start(bf16[2,14336]{1,0:T(2,128)(2,1)} %param.11), channel_id=1, source_target_pairs={{0,4},{1,5},{4,8},{5,9},{8,12},{9,13},{12,14},{13,15},{14,10},{15,... | collective-permute-start | bytes 172040 | tf_op jit(solution)/shard_map/ppermute | solution.py:71
  3.0 7.0 %collective-permute-start.13 = (bf16[2,4096]{1,0:T(2,128)(2,1)}, bf16[2,4096]{1,0:T(2,128)(2,1)S(1)}, u32[]{:S(2)}, u32[]{:S(2)}) collective-permute-start(bf16[2,4096]{1,0:T(2,128)(2,1)} %param.12), channel_id=1, source_target_pairs={{0,12},{1,13},{2,14},{3,15},{4,8},{5,9},{6,10},{7,11},{8,4},{9,5},... | collective-permute-start | bytes 49160 | tf_op jit(solution)/shard_map/ppermute | solution.py:80
  6.6 6.4 %collective-permute-start.11 = (bf16[2,4096]{1,0:T(2,128)(2,1)}, bf16[2,4096]{1,0:T(2,128)(2,1)S(1)}, u32[]{:S(2)}, u32[]{:S(2)}) collective-permute-start(bf16[2,4096]{1,0:T(2,128)(2,1)} %param.12), channel_id=1, source_target_pairs={{0,8},{1,9},{2,10},{3,11},{4,12},{5,13},{6,14},{7,15},{8,0},{9,1},... | collective-permute-start | bytes 49160 | tf_op jit(solution)/shard_map/ppermute | solution.py:80
  10.0 8.1 %collective-permute-start.9 = (bf16[2,4096]{1,0:T(2,128)(2,1)}, bf16[2,4096]{1,0:T(2,128)(2,1)S(1)}, u32[]{:S(2)}, u32[]{:S(2)}) collective-permute-start(bf16[2,4096]{1,0:T(2,128)(2,1)} %param.12), channel_id=1, source_target_pairs={{0,4},{1,5},{2,6},{3,7},{4,0},{5,1},{6,2},{7,3},{8,12},{9,13},{10,... | collective-permute-start | bytes 49160 | tf_op jit(solution)/shard_map/ppermute | solution.py:80
  12.9 6.8 %collective-permute-start.14 = (bf16[2,4096]{1,0:T(2,128)(2,1)}, bf16[2,4096]{1,0:T(2,128)(2,1)S(1)}, u32[]{:S(2)}, u32[]{:S(2)}) collective-permute-start(bf16[2,4096]{1,0:T(2,128)(2,1)} %param.12), channel_id=1, source_target_pairs={{0,14},{1,15},{2,12},{3,13},{4,10},{5,11},{6,8},{7,9},{8,6},{9,7},... | collective-permute-start | bytes 49160 | tf_op jit(solution)/shard_map/ppermute | solution.py:80
  15.8 6.5 %collective-permute-start.1 = (bf16[2,14336]{1,0:T(2,128)(2,1)S(1)}, bf16[2,14336]{1,0:T(2,128)(2,1)S(1)}, u32[]{:S(2)}, u32[]{:S(2)}) collective-permute-start(bf16[2,14336]{1,0:T(2,128)(2,1)S(1)} %collective-permute-done), channel_id=1, source_target_pairs={{0,4},{1,5},{4,8},{5,9},{8,12},{9,13},{12,14},{13,15},{14,10},{15,... | collective-permute-start | bytes 172040 | tf_op jit(solution)/shard_map/ppermute | solution.py:71
  18.1 12.9 %collective-permute-start.30 = (bf16[256,256]{1,0:T(8,128)(2,1)S(1)}, bf16[256,256]{1,0:T(8,128)(2,1)S(1)}, u32[]{:S(2)}, u32[]{:S(2)}) collective-permute-start(bf16[256,256]{1,0:T(8,128)(2,1)S(1)} %slice.3.refs_0_), channel_id=1, source_target_pairs={{0,1},{1,0},{2,3},{3,2},{4,5},{5,4},{6,7},{7,6},{8,9},{9,8},{10,11... | collective-permute-start | bytes 393224 | tf_op jit(solution)/shard_map/ppermute | solution.py:257
  18.2 12.8 %collective-permute-start.27 = (bf16[256,256]{1,0:T(8,128)(2,1)S(1)}, bf16[256,256]{1,0:T(8,128)(2,1)S(1)}, u32[]{:S(2)}, u32[]{:S(2)}) collective-permute-start(bf16[256,256]{1,0:T(8,128)(2,1)S(1)} %slice.3.refs_0_), channel_id=1, source_target_pairs={{0,2},{1,3},{4,0},{5,1},{8,4},{9,5},{12,8},{13,9},{14,12},{15,13},... | collective-permute-start | bytes 393224 | tf_op jit(solution)/shard_map/ppermute | solution.py:74
  31.0 8.8 %collective-permute-start.31 = (bf16[288,256]{1,0:T(8,128)(2,1)S(1)}, bf16[288,256]{1,0:T(8,128)(2,1)S(1)}, u32[]{:S(2)}, u32[]{:S(2)}) collective-permute-start(bf16[288,256]{1,0:T(8,128)(2,1)S(1)} %rotate_in.1.refs_1_), channel_id=1, source_target_pairs={{0,1},{1,0},{2,3},{3,2},{4,5},{5,4},{6,7},{7,6},{8,9},{9,8},{10,11... | collective-permute-start | bytes 442376 | tf_op jit(solution)/shard_map/ppermute | solution.py:257
  33.6 9.1 %collective-permute-start.23 = (bf16[288,256]{1,0:T(8,128)(2,1)S(1)}, bf16[288,256]{1,0:T(8,128)(2,1)S(1)}, u32[]{:S(2)}, u32[]{:S(2)}) collective-permute-start(bf16[288,256]{1,0:T(8,128)(2,1)S(1)} %rotate_in.1.refs_1_), channel_id=1, source_target_pairs={{0,2},{1,3},{4,0},{5,1},{8,4},{9,5},{12,8},{13,9},{14,12},{15,13},... | collective-permute-start | bytes 442376 | tf_op jit(solution)/shard_map/ppermute | solution.py:74
  42.7 19.8 %collective-permute-start.7 = (bf16[16,14336]{1,0:T(8,128)(2,1)S(1)}, bf16[16,14336]{1,0:T(8,128)(2,1)S(1)}, u32[]{:S(2)}, u32[]{:S(2)}) collective-permute-start(bf16[16,14336]{1,0:T(8,128)(2,1)S(1)} %concatenate.6.near_ref), channel_id=1, source_target_pairs={{0,1},{1,0},{2,3},{3,2},{4,5},{5,4},{6,7},{7,6},{8,9},{9,8},{10,11... | collective-permute-start | bytes 1376264 | tf_op jit(solution)/shard_map/ppermute | solution.py:231
  53.9 6.4 %collective-permute-start.22 = (bf16[256,256]{1,0:T(8,128)(2,1)}, bf16[256,256]{1,0:T(8,128)(2,1)S(1)}, u32[]{:S(2)}, u32[]{:S(2)}) collective-permute-start(bf16[256,256]{1,0:T(8,128)(2,1)} %collective-permute-done.20.refs_6_), channel_id=1, source_target_pairs={{0,4},{1,5},{4,8},{5,9},{8,12},{9,13},{12,14},{13,15},{14,10},{15,... | collective-permute-start | bytes 393224 | tf_op jit(solution)/shard_map/ppermute | solution.py:71
  55.3 7.2 %collective-permute-start.21 = (bf16[288,256]{1,0:T(8,128)(2,1)S(1)}, bf16[288,256]{1,0:T(8,128)(2,1)S(1)}, u32[]{:S(2)}, u32[]{:S(2)}) collective-permute-start(bf16[288,256]{1,0:T(8,128)(2,1)S(1)} %collective-permute-done.19.refs_5_), channel_id=1, source_target_pairs={{0,4},{1,5},{4,8},{5,9},{8,12},{9,13},{12,14},{13,15},{14,10},{15,... | collective-permute-start | bytes 442376 | tf_op jit(solution)/shard_map/ppermute | solution.py:71
  60.3 18.1 %collective-permute-start.35 = (bf16[288,256]{1,0:T(8,128)(2,1)S(1)}, bf16[288,256]{1,0:T(8,128)(2,1)S(1)}, u32[]{:S(2)}, u32[]{:S(2)}) collective-permute-start(bf16[288,256]{1,0:T(8,128)(2,1)S(1)} %collective-permute-done.19.refs_5_), channel_id=1, source_target_pairs={{0,1},{1,0},{2,3},{3,2},{4,5},{5,4},{6,7},{7,6},{8,9},{9,8},{10,11... | collective-permute-start | bytes 442376 | tf_op jit(solution)/shard_map/ppermute | solution.py:257
  60.3 18.1 %collective-permute-start.38 = (bf16[256,256]{1,0:T(8,128)(2,1)S(1)}, bf16[256,256]{1,0:T(8,128)(2,1)S(1)}, u32[]{:S(2)}, u32[]{:S(2)}) collective-permute-start(bf16[256,256]{1,0:T(8,128)(2,1)S(1)} %collective-permute-done.22.refs_8_), channel_id=1, source_target_pairs={{0,1},{1,0},{2,3},{3,2},{4,5},{5,4},{6,7},{7,6},{8,9},{9,8},{10,11... | collective-permute-start | bytes 393224 | tf_op jit(solution)/shard_map/ppermute | solution.py:257
  62.5 15.9 %collective-permute-start.41 = (bf16[288,256]{1,0:T(8,128)(2,1)S(1)}, bf16[288,256]{1,0:T(8,128)(2,1)S(1)}, u32[]{:S(2)}, u32[]{:S(2)}) collective-permute-start(bf16[288,256]{1,0:T(8,128)(2,1)S(1)} %collective-permute-done.25.refs_11_), channel_id=1, source_target_pairs={{0,1},{1,0},{2,3},{3,2},{4,5},{5,4},{6,7},{7,6},{8,9},{9,8},{10,11... | collective-permute-start | bytes 442376 | tf_op jit(solution)/shard_map/ppermute | solution.py:257
  62.5 15.9 %collective-permute-start.37 = (bf16[288,256]{1,0:T(8,128)(2,1)S(1)}, bf16[288,256]{1,0:T(8,128)(2,1)S(1)}, u32[]{:S(2)}, u32[]{:S(2)}) collective-permute-start(bf16[288,256]{1,0:T(8,128)(2,1)S(1)} %collective-permute-done.21.refs_7_), channel_id=1, source_target_pairs={{0,1},{1,0},{2,3},{3,2},{4,5},{5,4},{6,7},{7,6},{8,9},{9,8},{10,11... | collective-permute-start | bytes 442376 | tf_op jit(solution)/shard_map/ppermute | solution.py:257
  63.0 15.4 %collective-permute-start.39 = (bf16[288,256]{1,0:T(8,128)(2,1)S(1)}, bf16[288,256]{1,0:T(8,128)(2,1)S(1)}, u32[]{:S(2)}, u32[]{:S(2)}) collective-permute-start(bf16[288,256]{1,0:T(8,128)(2,1)S(1)} %collective-permute-done.26.refs_9_), channel_id=1, source_target_pairs={{0,1},{1,0},{2,3},{3,2},{4,5},{5,4},{6,7},{7,6},{8,9},{9,8},{10,11... | collective-permute-start | bytes 442376 | tf_op jit(solution)/shard_map/ppermute | solution.py:257
  105.5 6.8 %collective-permute-start.47 = (bf16[48,512]{1,0:T(8,128)(2,1)}, bf16[48,512]{1,0:T(8,128)(2,1)S(1)}, u32[]{:S(2)}, u32[]{:S(2)}) collective-permute-start(bf16[48,512]{1,0:T(8,128)(2,1)} %get-tuple-element.18), channel_id=1, source_target_pairs={{0,2},{1,3},{2,0},{3,1},{4,6},{5,7},{6,4},{7,5},{8,10},{9,11},{10,... | collective-permute-start | bytes 147464 | tf_op jit(solution)/shard_map/ppermute | solution.py:315
  106.5 9.0 %collective-permute-start.48 = (bf16[48,512]{1,0:T(8,128)(2,1)}, bf16[48,512]{1,0:T(8,128)(2,1)S(1)}, u32[]{:S(2)}, u32[]{:S(2)}) collective-permute-start(bf16[48,512]{1,0:T(8,128)(2,1)} %get-tuple-element.19), channel_id=1, source_target_pairs={{0,4},{1,5},{2,6},{3,7},{4,0},{5,1},{6,2},{7,3},{8,12},{9,13},{10,... | collective-permute-start | bytes 147464 | tf_op jit(solution)/shard_map/ppermute | solution.py:315
  108.3 8.4 %collective-permute-start.49 = (bf16[48,512]{1,0:T(8,128)(2,1)}, bf16[48,512]{1,0:T(8,128)(2,1)S(1)}, u32[]{:S(2)}, u32[]{:S(2)}) collective-permute-start(bf16[48,512]{1,0:T(8,128)(2,1)} %get-tuple-element.20), channel_id=1, source_target_pairs={{0,6},{1,7},{2,4},{3,5},{4,2},{5,3},{6,0},{7,1},{8,14},{9,15},{10,... | collective-permute-start | bytes 147464 | tf_op jit(solution)/shard_map/ppermute | solution.py:315
  109.0 7.7 %collective-permute-start.50 = (bf16[48,512]{1,0:T(8,128)(2,1)}, bf16[48,512]{1,0:T(8,128)(2,1)S(1)}, u32[]{:S(2)}, u32[]{:S(2)}) collective-permute-start(bf16[48,512]{1,0:T(8,128)(2,1)} %get-tuple-element.21), channel_id=1, source_target_pairs={{0,8},{1,9},{2,10},{3,11},{4,12},{5,13},{6,14},{7,15},{8,0},{9,1},... | collective-permute-start | bytes 147464 | tf_op jit(solution)/shard_map/ppermute | solution.py:315
  111.5 7.0 %collective-permute-start.51 = (bf16[48,512]{1,0:T(8,128)(2,1)}, bf16[48,512]{1,0:T(8,128)(2,1)S(1)}, u32[]{:S(2)}, u32[]{:S(2)}) collective-permute-start(bf16[48,512]{1,0:T(8,128)(2,1)} %get-tuple-element.22), channel_id=1, source_target_pairs={{0,10},{1,11},{2,8},{3,9},{4,14},{5,15},{6,12},{7,13},{8,2},{9,3},... | collective-permute-start | bytes 147464 | tf_op jit(solution)/shard_map/ppermute | solution.py:315
  115.5 7.0 %collective-permute-start.53 = (bf16[48,512]{1,0:T(8,128)(2,1)}, bf16[48,512]{1,0:T(8,128)(2,1)S(1)}, u32[]{:S(2)}, u32[]{:S(2)}) collective-permute-start(bf16[48,512]{1,0:T(8,128)(2,1)} %get-tuple-element.24), channel_id=1, source_target_pairs={{0,14},{1,15},{2,12},{3,13},{4,10},{5,11},{6,8},{7,9},{8,6},{9,7},... | collective-permute-start | bytes 147464 | tf_op jit(solution)/shard_map/ppermute | solution.py:315
  (44 other events, 242.8 us)

commit v2 on v1

v2 whole, which is shorter than its diff:
```python
import functools

import jax
import jax.numpy as jnp
import numpy as np
from jax import lax
from jax.experimental import pallas as pl
from jax.experimental.pallas import tpu as pltpu
from jax.sharding import PartitionSpec as P

WR = 768
WC = 512
LANES = 128
MIB = 1 << 20


def ring_of(n):
    chips = n // 2
    return [*range(0, chips, 2), *range(chips - 1, 0, -2)]


def shift_pairs(n, by):
    ring = ring_of(n)
    return [
        (2 * ring[p] + c, 2 * ring[(p + by) % len(ring)] + c)
        for p in range(len(ring))
        for c in range(2)
    ]


def xor_pairs(n, key):
    return [(b, b ^ key) for b in range(n)]


def swap(x, n):
    return lax.ppermute(x, "blk", xor_pairs(n, 1))


def planes(n):
    return [list(range(c, n, 2)) for c in range(2)]


def ring_sources(n):
    ring = ring_of(n)
    table = np.zeros((n, n), np.int32)
    for b in range(n):
        place = ring.index(b // 2)
        for k in range(n // 2):
            chip = ring[(place - k) % len(ring)]
            table[b, k] = 2 * chip + b % 2
            table[b, n // 2 + k] = 2 * chip + 1 - b % 2
    return table


def plane_sources(n):
    return np.array([[2 * (k % (n // 2)) + (b + k // (n // 2)) % 2 for k in range(n)] for b in range(n)], np.int32)


def doubled_sources(n):
    keys = [0]
    step = n // 4
    while step:
        keys += [k ^ step for k in keys]
        step //= 2
    return np.array([[b ^ (2 * k + c) for c in range(2) for k in keys] for b in range(n)], np.int32)


def place_of(table):
    return np.argsort(table, axis=1).astype(np.int32)


def ring_gather(x, n):
    chips = n // 2
    pieces = [None] * chips
    pieces[0] = x
    right, left = x, x
    for step in range(1, chips // 2 + 1):
        right = lax.ppermute(right, "blk", shift_pairs(n, 1))
        pieces[step] = right
        if step < chips // 2:
            left = lax.ppermute(left, "blk", shift_pairs(n, -1))
            pieces[chips - step] = left
    return pieces


def doubling_gather(x, n):
    x = x[None]
    step = n // 2
    while step > 1:
        x = jnp.concatenate([x, lax.ppermute(x, "blk", xor_pairs(n, step))], axis=0)
        step //= 2
    return x


def plane_exchange(x, n):
    return lax.all_to_all(x, "blk", 0, 0, axis_index_groups=planes(n), tiled=True)


def plane_gather(x, n):
    return plane_exchange(jnp.broadcast_to(x[None], (n // 2, *x.shape)), n)


def rotate_in_kernel(near_ref, far_ref, basis_ref, order_ref, out_ref):
    acts = jnp.concatenate([near_ref[...], far_ref[...]], axis=0)
    rotated = jnp.dot(acts, basis_ref[...], preferred_element_type=jnp.float32)
    ordered = jnp.dot(
        order_ref[...], rotated.astype(jnp.bfloat16), preferred_element_type=jnp.float32
    )
    out_ref[...] = ordered.astype(jnp.bfloat16)


def rotate_out_kernel(near_ref, far_ref, basis_ref, order_ref, out_ref, total):
    step = pl.program_id(0)

    @pl.when(step == 0)
    def _():
        total[...] = jnp.zeros_like(total)

    grads = jnp.concatenate([near_ref[...], far_ref[...]], axis=0)
    total[...] += jnp.dot(grads, basis_ref[...], preferred_element_type=jnp.float32)

    @pl.when(step == pl.num_programs(0) - 1)
    def _():
        aligned = jnp.dot(
            order_ref[...], total[...].astype(jnp.bfloat16), preferred_element_type=jnp.float32
        )
        out_ref[...] = aligned.T.astype(jnp.bfloat16)


def scale_kernel(tiles_ref, me_ref, aligned_ref, near_ref, far_ref, *refs):
    out_ref = refs[-1]
    at = pl.program_id(0)
    mine = lax.rem(at, 2) == me_ref[0]
    rotated = jnp.where(mine, near_ref[at // 2], far_ref[at // 2])
    grad = jnp.dot(aligned_ref[...], rotated, preferred_element_type=jnp.float32)
    for tile, damped_ref in enumerate(refs[:-1]):
        lanes = slice(tile * LANES, (tile + 1) * LANES)
        damped = damped_ref[...]
        inverse = pl.reciprocal(damped, approx=True)
        inverse = inverse * (2.0 - damped * inverse)
        out_ref[:, lanes] = (grad[:, lanes] * inverse).astype(jnp.bfloat16)


def window_kernel(n, scale, sources_ref, blocks_ref, window_ref, scaled_ref, *refs):
    pieces = refs[:n]
    send_ref, keep_ref = refs[n : n + 2]
    basis, projected, result, sem = refs[n + 2 :]
    chips = n // 2
    width = basis.shape[2]

    def copy_of(at):
        return pltpu.make_async_copy(pieces[at], basis.at[at % chips, at // chips], sem.at[at])

    for at in range(n):
        copy_of(at).start()
    projected[...] = jnp.zeros_like(projected)
    for at in range(n):
        copy_of(at).wait()

    @pl.loop(0, chips)
    def _(at):
        total = projected[...]
        for other in range(2):
            source = sources_ref[other * chips + at]
            columns = pl.ds(pl.multiple_of(source * width, width), width)
            total += jnp.dot(
                scaled_ref[:, columns], basis[at, other], preferred_element_type=jnp.float32
            )
        projected[...] = total

    result[...] = scale * jnp.dot(
        window_ref[...], projected[...].astype(jnp.bfloat16), preferred_element_type=jnp.float32
    )
    rows = keep_ref.shape[1]
    for k in range(chips):
        keep_ref[k] = result[pl.ds(pl.multiple_of(blocks_ref[k] * rows, rows), rows), :]
        other = result[pl.ds(pl.multiple_of(blocks_ref[chips + k] * rows, rows), rows), :]
        send_ref[k] = other.astype(jnp.bfloat16)


def add_core_kernel(keep_ref, got_ref, out_ref):
    out_ref[...] = (keep_ref[...] + got_ref[...].astype(jnp.float32)).astype(jnp.bfloat16)


def add_chips_kernel(parts_ref, out_ref):
    out_ref[...] = jnp.sum(parts_ref[...].astype(jnp.float32), axis=0)


VMEM = pl.BlockSpec(memory_space=pltpu.VMEM)
SMEM = pl.BlockSpec(memory_space=pltpu.SMEM)
ANY = pl.BlockSpec(memory_space=pl.ANY)


def one_hot(index):
    columns = lax.broadcasted_iota(jnp.int32, (index.shape[0], index.shape[0]), 1)
    return (index[:, None] == columns).astype(jnp.bfloat16)


def rows_of(blocks, tok_rows):
    return (blocks[:, None] * tok_rows + jnp.arange(tok_rows)[None, :]).reshape(-1)


def ring_body(n, grad_out, activations, basis_out, basis_in, eigenvalues, tile_order, block_map):
    tok_rows, full_out = grad_out.shape
    tile_width = basis_out.shape[1]
    full_in, in_width = basis_in.shape
    tokens = n * tok_rows
    chips = n // 2
    me = lax.axis_index("blk")
    pick = lambda table: lax.dynamic_index_in_dim(jnp.asarray(table), me, 0, keepdims=False)

    acts = plane_gather(activations, n).reshape(tokens // 2, full_in)
    order_in = one_hot(rows_of(pick(place_of(plane_sources(n))), tok_rows))
    rotated = pl.pallas_call(
        rotate_in_kernel,
        out_shape=jax.ShapeDtypeStruct((tokens, in_width), jnp.bfloat16),
        in_specs=[VMEM] * 4,
        out_specs=VMEM,
        compiler_params=pltpu.CompilerParams(vmem_limit_bytes=16 * MIB),
        name="rotate_in",
    )(acts, swap(acts, n), basis_in, order_in)
    rotated = plane_gather(rotated, n)
    rotated_far = swap(rotated, n)

    grads = doubling_gather(grad_out, n).reshape(tokens // 2, full_out)
    order_out = one_hot(rows_of(jnp.take(pick(place_of(doubled_sources(n))), block_map), tok_rows))
    depth = 1024
    aligned = pl.pallas_call(
        rotate_out_kernel,
        grid=(full_out // depth,),
        out_shape=jax.ShapeDtypeStruct((tile_width, tokens), jnp.bfloat16),
        in_specs=[
            pl.BlockSpec((tokens // 2, depth), lambda k: (0, k)),
            pl.BlockSpec((tokens // 2, depth), lambda k: (0, k)),
            pl.BlockSpec((depth, tile_width), lambda k: (k, 0)),
            pl.BlockSpec((tokens, tokens), lambda k: (0, 0)),
        ],
        out_specs=pl.BlockSpec((tile_width, tokens), lambda k: (0, 0)),
        scratch_shapes=[pltpu.VMEM((tokens, tile_width), jnp.float32)],
        compiler_params=pltpu.CompilerParams(vmem_limit_bytes=44 * MIB),
        cost_estimate=pl.CostEstimate(
            flops=2 * tokens * full_out * tile_width,
            bytes_accessed=2 * full_out * tile_width,
            transcendentals=0,
        ),
        name="rotate_out",
    )(grads, swap(grads, n), basis_out, order_out)

    per_piece = in_width // LANES

    def eigen_spec(tile):
        return pl.BlockSpec(
            (tile_width, LANES), lambda j, tiles, core: (0, tiles[j * per_piece + tile])
        )

    whole = lambda *shape: pl.BlockSpec(shape, lambda j, tiles, core: (0,) * len(shape))
    scaled = pl.pallas_call(
        scale_kernel,
        out_shape=jax.ShapeDtypeStruct((tile_width, full_in), jnp.bfloat16),
        grid_spec=pltpu.PrefetchScalarGridSpec(
            num_scalar_prefetch=2,
            grid=(n,),
            in_specs=[
                whole(tile_width, tokens),
                whole(chips, tokens, in_width),
                whole(chips, tokens, in_width),
            ]
            + [eigen_spec(tile) for tile in range(per_piece)],
            out_specs=pl.BlockSpec((tile_width, in_width), lambda j, tiles, core: (0, j)),
        ),
        compiler_params=pltpu.CompilerParams(vmem_limit_bytes=48 * MIB),
        cost_estimate=pl.CostEstimate(
            flops=2 * tile_width * full_in * tokens,
            bytes_accessed=6 * tile_width * full_in,
            transcendentals=tile_width * full_in,
        ),
        name="scale",
    )(
        tile_order,
        lax.rem(me, 2).reshape(1),
        aligned,
        rotated,
        rotated_far,
        *[eigenvalues] * per_piece,
    )

    pieces = ring_gather(basis_in[:WC].T, n)
    pieces += [swap(piece, n) for piece in pieces]

    rows = WR // n
    send, keep = pl.pallas_call(
        functools.partial(window_kernel, n, 1.0 / tokens),
        out_shape=(
            jax.ShapeDtypeStruct((chips, rows, WC), jnp.bfloat16),
            jax.ShapeDtypeStruct((chips, rows, WC), jnp.float32),
        ),
        grid=(1,),
        in_specs=[
            SMEM,
            SMEM,
            pl.BlockSpec((WR, tile_width), lambda i: (0, 0)),
            pl.BlockSpec((tile_width, full_in), lambda i: (0, 0)),
        ]
        + [ANY] * n,
        out_specs=(VMEM, VMEM),
        scratch_shapes=[
            pltpu.VMEM((chips, 2, in_width, WC), jnp.bfloat16),
            pltpu.VMEM((tile_width, WC), jnp.float32),
            pltpu.VMEM((WR, WC), jnp.float32),
            pltpu.SemaphoreType.DMA((n,)),
        ],
        compiler_params=pltpu.CompilerParams(vmem_limit_bytes=40 * MIB),
        cost_estimate=pl.CostEstimate(
            flops=2 * tile_width * full_in * WC + 2 * WR * tile_width * WC,
            bytes_accessed=2 * tile_width * full_in + 2 * WC * full_in,
            transcendentals=0,
        ),
        name="window",
    )(pick(ring_sources(n)), pick(plane_sources(n)), basis_out, scaled, *pieces)

    summed = pl.pallas_call(
        add_core_kernel,
        out_shape=jax.ShapeDtypeStruct((chips, rows, WC), jnp.bfloat16),
        in_specs=[VMEM, VMEM],
        out_specs=VMEM,
        name="add_core",
    )(keep, swap(send, n))
    return pl.pallas_call(
        add_chips_kernel,
        out_shape=jax.ShapeDtypeStruct((rows, WC), jnp.float32),
        in_specs=[VMEM],
        out_specs=VMEM,
        name="add_chips",
    )(plane_exchange(summed, n))


def gather_body(grad_out, activations, basis_out, basis_in, eigenvalues, tile_order, block_map):
    n_blocks = lax.axis_size("blk")
    tile_width = basis_out.shape[1]
    tok_rows = grad_out.shape[0]
    full_in = eigenvalues.shape[1]
    tokens = n_blocks * tok_rows
    dot = functools.partial(jnp.dot, preferred_element_type=jnp.float32)
    in_rows = lax.all_gather(basis_in[:WC], "blk", axis=1, tiled=True)
    acts = lax.all_gather(activations, "blk", axis=0, tiled=True)
    in_tile = dot(acts, basis_in).astype(jnp.bfloat16)
    rotated_in = lax.all_gather(in_tile, "blk", axis=1, tiled=True)
    grads = lax.all_gather(grad_out, "blk", axis=0, tiled=True)
    rotated_out = dot(grads, basis_out).astype(jnp.bfloat16)
    aligned = jnp.take(
        rotated_out.reshape(n_blocks, tok_rows, tile_width), block_map, axis=0
    ).reshape(tokens, tile_width)
    grad_tile = dot(aligned.T, rotated_in) / tokens
    damped = jnp.take(
        eigenvalues.reshape(tile_width, full_in // LANES, LANES), tile_order, axis=1
    ).reshape(tile_width, full_in)
    scaled = (grad_tile / damped).astype(jnp.bfloat16)
    projected = dot(scaled, in_rows.T).astype(jnp.bfloat16)
    return lax.psum_scatter(
        dot(basis_out[:WR], projected), "blk", scatter_dimension=0, tiled=True
    )


def solution(mesh):
    n = mesh.shape["blk"]

    def body(*args):
        wide = args[3].shape[1] % LANES == 0 and args[2].shape[1] % LANES == 0
        if wide and WR % (16 * n) == 0:
            return ring_body(n, *args)
        return gather_body(*args)

    placed = (
        P(("grp", "blk"), None),
        P(("grp", "blk"), None),
        P(None, "blk"),
        P(None, "blk"),
        P("blk", None),
        P(),
        P(),
    )
    return jax.shard_map(
        body, mesh=mesh, in_specs=placed, out_specs=P(("grp", "blk"), None), check_vma=False
    )
```

time: 125 us -> 122 us (0.976)
  starting transfers between devices: 50.5 us -> 26.8 us
  blocking collectives: 0 us -> 17.4 us
  Pallas kernels: 32.1 us -> 44.1 us
  local copies, waits for them, and re-layouts: 18.9 us -> 11.3 us
  waiting for transfers between devices: 19.4 us -> 15.4 us
  other arithmetic: 3.55 us -> 5.93 us
    all_to_all x0 -> x1, blocking collectives: none -> 17.4 us  [plane_exchange(): lax.all_to_all(x, 'blk', 0, 0, axis_index_groups=planes(n), tiled=True)]
    pallas_call x2 -> x3, Pallas kernels: 2.57 us -> 18.1 us  [the longest x1 15.4 us: ring_body(): pl.pallas_call(scale_kernel, out_shape=jax.ShapeDtypeStruct((tile_width,...]
    ppermute x33 -> x15, starting transfers between devices: 25.4 us -> 10.7 us  [the longest x3 7.13 us: doubling_gather(): x = jnp.concatenate([x, lax.ppermute(x, 'blk', xor_pairs(n, step))], axis=0)]
    pallas_call x1, Pallas kernels: 21.6 us -> 9.19 us  [ring_body(): pl.pallas_call(functools.partial(window_kernel, n, 1.0 / tokens), out_sha...]
    ppermute x11 -> x4, starting transfers between devices: 15 us -> 3.64 us  [ring_gather(): right = lax.ppermute(right, 'blk', shift_pairs(n, 1))]
    pallas_call x1, Pallas kernels: 6.28 us -> 15.1 us  [ring_body(): pl.pallas_call(rotate_out_kernel, grid=(full_out // depth,), out_shape=ja...]
    all_to_all x0 -> x2, starting transfers between devices: none -> 8.26 us  [plane_exchange(): lax.all_to_all(x, 'blk', 0, 0, axis_index_groups=planes(n), tiled=True)]
    unnamed x28 -> x11, local copies, waits for them, and re-layouts: 12.8 us -> 6.46 us
  transfers between devices with their start and end apart: 54 -> 24, of which waited for: 12 -> 8; matrix products, arithmetic and copies ran while one was open for 8% -> 8% of each run, Pallas kernels for 5% -> 26%
where the time goes in v2:
time: 122 us; the launch traced here: 121 us
  Pallas kernels  44.1 us (36%)
  starting transfers between devices  26.8 us (22%)
  blocking collectives  17.4 us (14%)
  waiting for transfers between devices  15.4 us (13%)
  local copies, waits for them, and re-layouts  11.3 us (9%)
  other arithmetic  5.93 us (5%)
    all_to_all x1, blocking collectives, plane_exchange(): lax.all_to_all(x, 'blk', 0, 0, axis_index_groups=planes(n), tiled=True)  17.4 us
    pallas_call x1, Pallas kernels, ring_body(): pl.pallas_call(scale_kernel, out_shape=jax.ShapeDtypeStruct((tile_width,...  15.4 us
    pallas_call x1, Pallas kernels, ring_body(): pl.pallas_call(rotate_out_kernel, grid=(full_out // depth,), out_shape=ja...  15.1 us
    pallas_call x1, Pallas kernels, ring_body(): pl.pallas_call(functools.partial(window_kernel, n, 1.0 / tokens), out_sha...  9.19 us
    all_to_all x2, starting transfers between devices, plane_exchange(): lax.all_to_all(x, 'blk', 0, 0, axis_index_groups=planes(n), tiled=True)  8.26 us
    ppermute x4, waiting for transfers between devices, ring_gather(): right = lax.ppermute(right, 'blk', shift_pairs(n, 1))  7.48 us
    ppermute x3, starting transfers between devices, doubling_gather(): x = jnp.concatenate([x, lax.ppermute(x, 'blk', xor_pairs(n, step))], axis=0)  7.13 us
    unnamed x11, local copies, waits for them, and re-layouts  6.46 us
  transfers between devices with their start and end apart: 24, of which 8 were waited for; matrix products, arithmetic and copies ran while one was open for 8% of the time, Pallas kernels for 26%

profile of v2, /device:TPU:0, one launch (start us, length us, event | category | flops | bytes accessed | tf_op | source)
XLA Modules:
  0.0 121.1 jit_solution(16942429468783292285)
XLA Ops:
  1.6 2.6 %collective-permute-start.10 = (bf16[256,512]{1,0:T(8,128)(2,1)S(1)}, bf16[256,512]{1,0:T(8,128)(2,1)S(1)}, u32[]{:S(2)}, u32[]{:S(2)}) collective-permute-start(bf16[256,512]{1,0:T(8,128)(2,1)S(1)} %bitcast.12), channel_id=1, source_target_pairs={{0,2},{1,3},{4,0},{5,1},{8,4},{9,5},{12,8},{13,9},{14,12},{15,13},... | collective-permute-start | bytes 786440 | tf_op jit(solution)/shard_map/ppermute | solution.py:81
  4.4 3.0 %collective-permute-start = (bf16[1,2,14336]{2,1,0:T(2,128)(2,1)}, bf16[1,2,14336]{2,1,0:T(2,128)(2,1)S(1)}, u32[]{:S(2)}, u32[]{:S(2)}) collective-permute-start(bf16[1,2,14336]{2,1,0:T(2,128)(2,1)} %bitcast.15), channel_id=1, source_target_pairs={{0,8},{1,9},{2,10},{3,11},{4,12},{5,13},{6,14},{7,15},{8,0},{9,1},... | collective-permute-start | bytes 172040 | tf_op jit(solution)/shard_map/ppermute | solution.py:90
  7.3 1.4 %broadcast_in_dim.11 = bf16[8,2,4096]{2,1,0:T(2,128)(2,1)} broadcast(bf16[2,4096]{1,0:T(2,128)(2,1)} %param.12), dimensions={1,2} | broadcast | bytes 147456 | tf_op jit(solution)/shard_map/broadcast_in_dim | solution.py:100
  8.8 3.8 %all-to-all-start = ((bf16[8,2,4096]{2,1,0:T(2,128)(2,1)}), bf16[8,2,4096]{2,1,0:T(2,128)(2,1)S(1)}, u32[]{:S(2)}, u32[]{:S(2)}) async-start(bf16[8,2,4096]{2,1,0:T(2,128)(2,1)} %broadcast_in_dim.11), calls=%async_computation | async-start | bytes 262144 | tf_op jit(solution)/shard_map/all_to_all | solution.py:96
  13.3 1.7 %collective-permute-done = bf16[1,2,14336]{2,1,0:T(2,128)(2,1)S(1)} collective-permute-done((bf16[1,2,14336]{2,1,0:T(2,128)(2,1)}, bf16[1,2,14336]{2,1,0:T(2,128)(2,1)S(1)}, u32[]{:S(2)}, u32[]{:S(2)}) %collective-permute-start) | collective-permute-done | bytes 57376 | tf_op jit(solution)/shard_map/ppermute | solution.py:90
  15.9 1.3 %collective-permute-start.1 = (bf16[2,2,14336]{2,1,0:T(2,128)(2,1)S(1)}, bf16[2,2,14336]{2,1,0:T(2,128)(2,1)S(1)}, u32[]{:S(2)}, u32[]{:S(2)}) collective-permute-start(bf16[2,2,14336]{2,1,0:T(2,128)(2,1)S(1)} %pad_maximum_fusion.2), channel_id=1, source_target_pairs={{0,4},{1,5},{2,6},{3,7},{4,0},{5,1},{6,2},{7,3},{8,12},{9,13},{10,... | collective-permute-start | bytes 344072 | tf_op jit(solution)/shard_map/ppermute | solution.py:90
  17.4 3.4 %collective-permute-done.1 = bf16[2,2,14336]{2,1,0:T(2,128)(2,1)S(1)} collective-permute-done((bf16[2,2,14336]{2,1,0:T(2,128)(2,1)S(1)}, bf16[2,2,14336]{2,1,0:T(2,128)(2,1)S(1)}, u32[]{:S(2)}, u32[]{:S(2)}) %collective-permute-start.1) | collective-permute-done | bytes 114720 | tf_op jit(solution)/shard_map/ppermute | solution.py:90
  20.8 1.1 pad_maximum_fusion.1
  21.9 2.8 %collective-permute-start.2 = (bf16[4,2,14336]{2,1,0:T(2,128)(2,1)S(1)}, bf16[4,2,14336]{2,1,0:T(2,128)(2,1)S(1)}, u32[]{:S(2)}, u32[]{:S(2)}) collective-permute-start(bf16[4,2,14336]{2,1,0:T(2,128)(2,1)S(1)} %pad_maximum_fusion.1), channel_id=1, source_target_pairs={{0,2},{1,3},{2,0},{3,1},{4,6},{5,7},{6,4},{7,5},{8,10},{9,11},{10,... | collective-permute-start | bytes 688136 | tf_op jit(solution)/shard_map/ppermute | solution.py:90
  26.7 1.6 %collective-permute-start.11 = (bf16[256,512]{1,0:T(8,128)(2,1)S(1)}, bf16[256,512]{1,0:T(8,128)(2,1)S(1)}, u32[]{:S(2)}, u32[]{:S(2)}) collective-permute-start(bf16[256,512]{1,0:T(8,128)(2,1)S(1)} %collective-permute-done.10.refs_7_), channel_id=1, source_target_pairs={{0,2},{1,3},{4,0},{5,1},{8,4},{9,5},{12,8},{13,9},{14,12},{15,13},... | collective-permute-start | bytes 786440 | tf_op jit(solution)/shard_map/ppermute | solution.py:81
  28.3 1.6 %copy-done.1 = bf16[4096,256]{1,0:T(8,128)(2,1)S(1)} copy-done((bf16[4096,256]{1,0:T(8,128)(2,1)S(1)}, bf16[4096,256]{1,0:T(8,128)(2,1)}, u32[]{:S(2)}) %copy-start.1) | copy-done | bytes 2097176
  31.2 4.5 %all-to-all-start.1 = ((bf16[8,32,256]{2,1,0:T(8,128)(2,1)}), bf16[8,32,256]{2,1,0:T(8,128)(2,1)S(1)}, u32[]{:S(2)}, u32[]{:S(2)}) async-start(bf16[8,32,256]{2,1,0:T(8,128)(2,1)} %broadcast_in_dim.13), calls=%async_computation.1 | async-start | bytes 262144 | tf_op jit(solution)/shard_map/all_to_all | solution.py:96
  35.7 2.1 %collective-permute-start.8 = (bf16[256,512]{1,0:T(8,128)(2,1)S(1)}, bf16[256,512]{1,0:T(8,128)(2,1)S(1)}, u32[]{:S(2)}, u32[]{:S(2)}) collective-permute-start(bf16[256,512]{1,0:T(8,128)(2,1)S(1)} %collective-permute-done.7.refs_2_), channel_id=1, source_target_pairs={{0,4},{1,5},{4,8},{5,9},{8,12},{9,13},{12,14},{13,15},{14,10},{15,... | collective-permute-start | bytes 786440 | tf_op jit(solution)/shard_map/ppermute | solution.py:78
  37.7 1.5 %pad_maximum_fusion = bf16[8,2,14336]{2,1,0:T(2,128)(2,1)S(1)} fusion(bf16[4,2,14336]{2,1,0:T(2,128)(2,1)S(1)} %collective-permute-done.2, bf16[2,2,14336]{2,1,0:T(2,128)(2,1)S(1)} %collective-permute-done.1, bf16[1,2,14336]{2,1,0:T(2,128)(2,1)S(1)} %collective-permute-done, bf16[1,2,14336]{2,1,0:T(2,128)(2,1)} %bitcast.18), kind=kLoop, calls=%fused_computation.1 | loop fusion | flops 688128 | bytes 917504 | tf_op jit(solution)/shard_map/concatenate | solution.py:90
  40.7 4.3 %collective-permute-done.8.refs_3_ = bf16[256,512]{1,0:T(8,128)(2,1)S(1)} collective-permute-done((bf16[256,512]{1,0:T(8,128)(2,1)S(1)}, bf16[256,512]{1,0:T(8,128)(2,1)S(1)}, u32[]{:S(2)}, u32[]{:S(2)}) %collective-permute-start.8) | collective-permute-done | bytes 262176 | tf_op jit(solution)/shard_map/ppermute | solution.py:78
  49.6 3.1 %collective-permute-done.9.refs_4_ = bf16[256,512]{1,0:T(8,128)(2,1)} collective-permute-done((bf16[256,512]{1,0:T(8,128)(2,1)S(1)}, bf16[256,512]{1,0:T(8,128)(2,1)}, u32[]{:S(2)}, u32[]{:S(2)}) %collective-permute-start.9) | collective-permute-done | bytes 262176 | tf_op jit(solution)/shard_map/ppermute | solution.py:78
  53.5 15.1 %rotate_out.1.aligned_ref = bf16[896,32]{1,0:T(8,128)(2,1)S(1)} custom-call(bf16[16,14336]{1,0:T(8,128)(2,1)S(1)} %reshape.59.near_ref, bf16[16,14336]{1,0:T(8,128)(2,1)S(1)} %collective-permute-done.3.far_ref, bf16[14336,896]{1,0:T(8,128)(2,1)} %window_ref.1, bf16[32,32]{1,0:T(8,128)(2,1)S(1)} %fusion.order_ref), custom_call_target="tpu_custom_call" | custom-call | flops 822083584 | bytes 25690112 | tf_op jit(solution)/shard_map/rotate_out/pallas_call | solution.py:228
  68.7 15.4 %scale.1.scaled_ref = bf16[896,4096]{1,0:T(8,128)(2,1)} custom-call(s32[32]{0:T(128)S(1)} %copy-done.3, s32[1]{0:T(128)} %bitcast.2.me_ref, bf16[896,32]{1,0:T(8,128)(2,1)S(1)} %rotate_out.1.aligned_ref, bf16[8,32,256]{2,1,0:T(8,128)(2,1)S(1)} %all-to-all-done.1.near_ref, bf16[8,32,256]{2,1,0:T(8,128)(2,1)S(1)} %collective-permute-done.5.far_ref, ...), custom_call_target="tpu_custom_call" | custom-call | flops 234881024 | bytes 22020096 | tf_op jit(solution)/shard_map/scale/pallas_call | solution.py:257
  84.1 3.1 %copy-done = bf16[896,4096]{1,0:T(8,128)(2,1)S(1)} copy-done((bf16[896,4096]{1,0:T(8,128)(2,1)S(1)}, bf16[896,4096]{1,0:T(8,128)(2,1)}, u32[]{:S(2)}) %copy-start) | copy-done | bytes 7340056
  87.2 9.2 %window.1 = (bf16[8,48,512]{2,1,0:T(8,128)(2,1)S(1)}, f32[8,48,512]{2,1,0:T(8,128)S(1)}) custom-call(s32[16]{0:T(128)S(1)} %get-tuple-element.9.sources_ref, s32[16]{0:T(128)S(1)} %get-tuple-element.10.blocks_ref, bf16[14336,896]{1,0:T(8,128)(2,1)} %window_ref.1, bf16[896,4096]{1,0:T(8,128)(2,1)S(1)} %copy-done, bf16[256,512]{1,0:T(8,128)(2,1)S(1)} %bitcast.14, ...), custom_call_target="tpu_custom_call" | custom-call | flops 4462739456 | bytes 11534336 | tf_op jit(solution)/shard_map/window/pallas_call | solution.py:291
  97.9 1.3 %collective-permute-done.21.got_ref = bf16[8,48,512]{2,1,0:T(8,128)(2,1)S(1)} collective-permute-done((bf16[8,48,512]{2,1,0:T(8,128)(2,1)S(1)}, bf16[8,48,512]{2,1,0:T(8,128)(2,1)S(1)}, u32[]{:S(2)}, u32[]{:S(2)}) %collective-permute-start.21) | collective-permute-done | bytes 393248 | tf_op jit(solution)/shard_map/ppermute | solution.py:36
  100.0 2.1 %add_core.1 = bf16[8,48,512]{2,1,0:T(8,128)(2,1)} custom-call(f32[8,48,512]{2,1,0:T(8,128)} %copy-done.2, bf16[8,48,512]{2,1,0:T(8,128)(2,1)} %copy-done.4), custom_call_target="tpu_custom_call" | custom-call | tf_op jit(solution)/shard_map/add_core/pallas_call | solution.py:321
  102.0 17.4 %all_to_all.15.parts_ref = bf16[8,48,512]{2,1,0:T(8,128)(2,1)} all-to-all(bf16[8,48,512]{2,1,0:T(8,128)(2,1)} %add_core.1), channel_id=1, replica_groups={{0,2,4,6,8,10,12,14},{1,3,5,7,9,11,13,15},{16,18,20,22,24,26,28,30},{17..., dimensions={0} | all-to-all | bytes 786432 | tf_op jit(solution)/shard_map/all_to_all | solution.py:96
  119.4 1.7 %add_chips.1 = f32[48,512]{1,0:T(8,128)} custom-call(bf16[8,48,512]{2,1,0:T(8,128)(2,1)} %all_to_all.15.parts_ref), custom_call_target="tpu_custom_call" | custom-call | tf_op jit(solution)/shard_map/add_chips/pallas_call | solution.py:328
  (62 shorter events, 15.8 us)
Async XLA Ops:
  1.1 39.0 %collective-permute-start.13 = (bf16[256,512]{1,0:T(8,128)(2,1)S(1)}, bf16[256,512]{1,0:T(8,128)(2,1)S(1)}, u32[]{:S(2)}, u32[]{:S(2)}) collective-permute-start(bf16[256,512]{1,0:T(8,128)(2,1)S(1)} %bitcast.11), channel_id=1, source_target_pairs={{0,1},{1,0},{2,3},{3,2},{4,5},{5,4},{6,7},{7,6},{8,9},{9,8},{10,11... | collective-permute-start | bytes 786440 | tf_op jit(solution)/shard_map/ppermute | solution.py:36
  1.6 24.4 %collective-permute-start.10 = (bf16[256,512]{1,0:T(8,128)(2,1)S(1)}, bf16[256,512]{1,0:T(8,128)(2,1)S(1)}, u32[]{:S(2)}, u32[]{:S(2)}) collective-permute-start(bf16[256,512]{1,0:T(8,128)(2,1)S(1)} %bitcast.12), channel_id=1, source_target_pairs={{0,2},{1,3},{4,0},{5,1},{8,4},{9,5},{12,8},{13,9},{14,12},{15,13},... | collective-permute-start | bytes 786440 | tf_op jit(solution)/shard_map/ppermute | solution.py:81
  4.2 20.5 %collective-permute-start.6 = (bf16[256,512]{1,0:T(8,128)(2,1)S(1)}, bf16[256,512]{1,0:T(8,128)(2,1)S(1)}, u32[]{:S(2)}, u32[]{:S(2)}) collective-permute-start(bf16[256,512]{1,0:T(8,128)(2,1)S(1)} %bitcast.13), channel_id=1, source_target_pairs={{0,4},{1,5},{4,8},{5,9},{8,12},{9,13},{12,14},{13,15},{14,10},{15,... | collective-permute-start | bytes 786440 | tf_op jit(solution)/shard_map/ppermute | solution.py:78
  4.4 10.6 %collective-permute-start = (bf16[1,2,14336]{2,1,0:T(2,128)(2,1)}, bf16[1,2,14336]{2,1,0:T(2,128)(2,1)S(1)}, u32[]{:S(2)}, u32[]{:S(2)}) collective-permute-start(bf16[1,2,14336]{2,1,0:T(2,128)(2,1)} %bitcast.15), channel_id=1, source_target_pairs={{0,8},{1,9},{2,10},{3,11},{4,12},{5,13},{6,14},{7,15},{8,0},{9,1},... | collective-permute-start | bytes 172040 | tf_op jit(solution)/shard_map/ppermute | solution.py:90
  8.8 16.5 %all-to-all-start = ((bf16[8,2,4096]{2,1,0:T(2,128)(2,1)}), bf16[8,2,4096]{2,1,0:T(2,128)(2,1)S(1)}, u32[]{:S(2)}, u32[]{:S(2)}) async-start(bf16[8,2,4096]{2,1,0:T(2,128)(2,1)} %broadcast_in_dim.11), calls=%async_computation | async-start | bytes 262144 | tf_op jit(solution)/shard_map/all_to_all | solution.py:96
  15.9 4.9 %collective-permute-start.1 = (bf16[2,2,14336]{2,1,0:T(2,128)(2,1)S(1)}, bf16[2,2,14336]{2,1,0:T(2,128)(2,1)S(1)}, u32[]{:S(2)}, u32[]{:S(2)}) collective-permute-start(bf16[2,2,14336]{2,1,0:T(2,128)(2,1)S(1)} %pad_maximum_fusion.2), channel_id=1, source_target_pairs={{0,4},{1,5},{2,6},{3,7},{4,0},{5,1},{6,2},{7,3},{8,12},{9,13},{10,... | collective-permute-start | bytes 344072 | tf_op jit(solution)/shard_map/ppermute | solution.py:90
  21.9 15.8 %collective-permute-start.2 = (bf16[4,2,14336]{2,1,0:T(2,128)(2,1)S(1)}, bf16[4,2,14336]{2,1,0:T(2,128)(2,1)S(1)}, u32[]{:S(2)}, u32[]{:S(2)}) collective-permute-start(bf16[4,2,14336]{2,1,0:T(2,128)(2,1)S(1)} %pad_maximum_fusion.1), channel_id=1, source_target_pairs={{0,2},{1,3},{2,0},{3,1},{4,6},{5,7},{6,4},{7,5},{8,10},{9,11},{10,... | collective-permute-start | bytes 688136 | tf_op jit(solution)/shard_map/ppermute | solution.py:90
  24.8 10.9 %collective-permute-start.7 = (bf16[256,512]{1,0:T(8,128)(2,1)S(1)}, bf16[256,512]{1,0:T(8,128)(2,1)S(1)}, u32[]{:S(2)}, u32[]{:S(2)}) collective-permute-start(bf16[256,512]{1,0:T(8,128)(2,1)S(1)} %collective-permute-done.6.refs_1_), channel_id=1, source_target_pairs={{0,4},{1,5},{4,8},{5,9},{8,12},{9,13},{12,14},{13,15},{14,10},{15,... | collective-permute-start | bytes 786440 | tf_op jit(solution)/shard_map/ppermute | solution.py:78
  25.3 1.4 %collective-permute-start.4 = (bf16[16,4096]{1,0:T(8,128)(2,1)S(1)}, bf16[16,4096]{1,0:T(8,128)(2,1)S(1)}, u32[]{:S(2)}, u32[]{:S(2)}) collective-permute-start(bf16[16,4096]{1,0:T(8,128)(2,1)S(1)} %reshape.60.near_ref), channel_id=1, source_target_pairs={{0,1},{1,0},{2,3},{3,2},{4,5},{5,4},{6,7},{7,6},{8,9},{9,8},{10,11... | collective-permute-start | bytes 393224 | tf_op jit(solution)/shard_map/ppermute | solution.py:36
  26.0 20.7 %collective-permute-start.20 = (bf16[256,512]{1,0:T(8,128)(2,1)S(1)}, bf16[256,512]{1,0:T(8,128)(2,1)S(1)}, u32[]{:S(2)}, u32[]{:S(2)}) collective-permute-start(bf16[256,512]{1,0:T(8,128)(2,1)S(1)} %collective-permute-done.10.refs_7_), channel_id=1, source_target_pairs={{0,1},{1,0},{2,3},{3,2},{4,5},{5,4},{6,7},{7,6},{8,9},{9,8},{10,11... | collective-permute-start | bytes 786440 | tf_op jit(solution)/shard_map/ppermute | solution.py:36
  26.7 14.0 %collective-permute-start.11 = (bf16[256,512]{1,0:T(8,128)(2,1)S(1)}, bf16[256,512]{1,0:T(8,128)(2,1)S(1)}, u32[]{:S(2)}, u32[]{:S(2)}) collective-permute-start(bf16[256,512]{1,0:T(8,128)(2,1)S(1)} %collective-permute-done.10.refs_7_), channel_id=1, source_target_pairs={{0,2},{1,3},{4,0},{5,1},{8,4},{9,5},{12,8},{13,9},{14,12},{15,13},... | collective-permute-start | bytes 786440 | tf_op jit(solution)/shard_map/ppermute | solution.py:81
  31.2 15.6 %all-to-all-start.1 = ((bf16[8,32,256]{2,1,0:T(8,128)(2,1)}), bf16[8,32,256]{2,1,0:T(8,128)(2,1)S(1)}, u32[]{:S(2)}, u32[]{:S(2)}) async-start(bf16[8,32,256]{2,1,0:T(8,128)(2,1)} %broadcast_in_dim.13), calls=%async_computation.1 | async-start | bytes 262144 | tf_op jit(solution)/shard_map/all_to_all | solution.py:96
  35.7 9.4 %collective-permute-start.8 = (bf16[256,512]{1,0:T(8,128)(2,1)S(1)}, bf16[256,512]{1,0:T(8,128)(2,1)S(1)}, u32[]{:S(2)}, u32[]{:S(2)}) collective-permute-start(bf16[256,512]{1,0:T(8,128)(2,1)S(1)} %collective-permute-done.7.refs_2_), channel_id=1, source_target_pairs={{0,4},{1,5},{4,8},{5,9},{8,12},{9,13},{12,14},{13,15},{14,10},{15,... | collective-permute-start | bytes 786440 | tf_op jit(solution)/shard_map/ppermute | solution.py:78
  39.4 9.7 %collective-permute-start.3 = (bf16[16,14336]{1,0:T(8,128)(2,1)S(1)}, bf16[16,14336]{1,0:T(8,128)(2,1)S(1)}, u32[]{:S(2)}, u32[]{:S(2)}) collective-permute-start(bf16[16,14336]{1,0:T(8,128)(2,1)S(1)} %reshape.59.near_ref), channel_id=1, source_target_pairs={{0,1},{1,0},{2,3},{3,2},{4,5},{5,4},{6,7},{7,6},{8,9},{9,8},{10,11... | collective-permute-start | bytes 1376264 | tf_op jit(solution)/shard_map/ppermute | solution.py:36
  40.1 6.9 %collective-permute-start.14 = (bf16[256,512]{1,0:T(8,128)(2,1)S(1)}, bf16[256,512]{1,0:T(8,128)(2,1)S(1)}, u32[]{:S(2)}, u32[]{:S(2)}) collective-permute-start(bf16[256,512]{1,0:T(8,128)(2,1)S(1)} %collective-permute-done.6.refs_1_), channel_id=1, source_target_pairs={{0,1},{1,0},{2,3},{3,2},{4,5},{5,4},{6,7},{7,6},{8,9},{9,8},{10,11... | collective-permute-start | bytes 786440 | tf_op jit(solution)/shard_map/ppermute | solution.py:36
  40.7 8.4 %collective-permute-start.12 = (bf16[256,512]{1,0:T(8,128)(2,1)S(1)}, bf16[256,512]{1,0:T(8,128)(2,1)}, u32[]{:S(2)}, u32[]{:S(2)}) collective-permute-start(bf16[256,512]{1,0:T(8,128)(2,1)S(1)} %collective-permute-done.11.refs_6_), channel_id=1, source_target_pairs={{0,2},{1,3},{4,0},{5,1},{8,4},{9,5},{12,8},{13,9},{14,12},{15,13},... | collective-permute-start | bytes 786440 | tf_op jit(solution)/shard_map/ppermute | solution.py:81
  45.0 7.7 %collective-permute-start.9 = (bf16[256,512]{1,0:T(8,128)(2,1)S(1)}, bf16[256,512]{1,0:T(8,128)(2,1)}, u32[]{:S(2)}, u32[]{:S(2)}) collective-permute-start(bf16[256,512]{1,0:T(8,128)(2,1)S(1)} %collective-permute-done.8.refs_3_), channel_id=1, source_target_pairs={{0,4},{1,5},{4,8},{5,9},{8,12},{9,13},{12,14},{13,15},{14,10},{15,... | collective-permute-start | bytes 786440 | tf_op jit(solution)/shard_map/ppermute | solution.py:78
  46.8 1.4 %collective-permute-start.5 = (bf16[8,32,256]{2,1,0:T(8,128)(2,1)S(1)}, bf16[8,32,256]{2,1,0:T(8,128)(2,1)S(1)}, u32[]{:S(2)}, u32[]{:S(2)}) collective-permute-start(bf16[8,32,256]{2,1,0:T(8,128)(2,1)S(1)} %all-to-all-done.1.near_ref), channel_id=1, source_target_pairs={{0,1},{1,0},{2,3},{3,2},{4,5},{5,4},{6,7},{7,6},{8,9},{9,8},{10,11... | collective-permute-start | bytes 393224 | tf_op jit(solution)/shard_map/ppermute | solution.py:36
  47.0 37.1 %collective-permute-start.19 = (bf16[256,512]{1,0:T(8,128)(2,1)S(1)}, bf16[256,512]{1,0:T(8,128)(2,1)}, u32[]{:S(2)}, u32[]{:S(2)}) collective-permute-start(bf16[256,512]{1,0:T(8,128)(2,1)S(1)} %collective-permute-done.11.refs_6_), channel_id=1, source_target_pairs={{0,1},{1,0},{2,3},{3,2},{4,5},{5,4},{6,7},{7,6},{8,9},{9,8},{10,11... | collective-permute-start | bytes 786440 | tf_op jit(solution)/shard_map/ppermute | solution.py:36
  48.2 35.9 %collective-permute-start.15 = (bf16[256,512]{1,0:T(8,128)(2,1)S(1)}, bf16[256,512]{1,0:T(8,128)(2,1)}, u32[]{:S(2)}, u32[]{:S(2)}) collective-permute-start(bf16[256,512]{1,0:T(8,128)(2,1)S(1)} %collective-permute-done.7.refs_2_), channel_id=1, source_target_pairs={{0,1},{1,0},{2,3},{3,2},{4,5},{5,4},{6,7},{7,6},{8,9},{9,8},{10,11... | collective-permute-start | bytes 786440 | tf_op jit(solution)/shard_map/ppermute | solution.py:36
  49.1 35.0 %collective-permute-start.16 = (bf16[256,512]{1,0:T(8,128)(2,1)S(1)}, bf16[256,512]{1,0:T(8,128)(2,1)}, u32[]{:S(2)}, u32[]{:S(2)}) collective-permute-start(bf16[256,512]{1,0:T(8,128)(2,1)S(1)} %collective-permute-done.8.refs_3_), channel_id=1, source_target_pairs={{0,1},{1,0},{2,3},{3,2},{4,5},{5,4},{6,7},{7,6},{8,9},{9,8},{10,11... | collective-permute-start | bytes 786440 | tf_op jit(solution)/shard_map/ppermute | solution.py:36
  49.1 35.0 %collective-permute-start.18 = (bf16[256,512]{1,0:T(8,128)(2,1)}, bf16[256,512]{1,0:T(8,128)(2,1)}, u32[]{:S(2)}, u32[]{:S(2)}) collective-permute-start(bf16[256,512]{1,0:T(8,128)(2,1)} %collective-permute-done.12.refs_5_), channel_id=1, source_target_pairs={{0,1},{1,0},{2,3},{3,2},{4,5},{5,4},{6,7},{7,6},{8,9},{9,8},{10,11... | collective-permute-start | bytes 786440 | tf_op jit(solution)/shard_map/ppermute | solution.py:36
  52.7 31.4 %collective-permute-start.17 = (bf16[256,512]{1,0:T(8,128)(2,1)}, bf16[256,512]{1,0:T(8,128)(2,1)}, u32[]{:S(2)}, u32[]{:S(2)}) collective-permute-start(bf16[256,512]{1,0:T(8,128)(2,1)} %collective-permute-done.9.refs_4_), channel_id=1, source_target_pairs={{0,1},{1,0},{2,3},{3,2},{4,5},{5,4},{6,7},{7,6},{8,9},{9,8},{10,11... | collective-permute-start | bytes 786440 | tf_op jit(solution)/shard_map/ppermute | solution.py:36
  97.3 1.9 %collective-permute-start.21 = (bf16[8,48,512]{2,1,0:T(8,128)(2,1)S(1)}, bf16[8,48,512]{2,1,0:T(8,128)(2,1)S(1)}, u32[]{:S(2)}, u32[]{:S(2)}) collective-permute-start(bf16[8,48,512]{2,1,0:T(8,128)(2,1)S(1)} %get-tuple-element.8), channel_id=1, source_target_pairs={{0,1},{1,0},{2,3},{3,2},{4,5},{5,4},{6,7},{7,6},{8,9},{9,8},{10,11... | collective-permute-start | bytes 1179656 | tf_op jit(solution)/shard_map/ppermute | solution.py:36
  (5 other events, 39.3 us)

commit v3 on v2

--- a/solution.py
+++ b/solution.py
@@ -69,20 +69,6 @@
     return np.argsort(table, axis=1).astype(np.int32)
 
 
-def ring_gather(x, n):
-    chips = n // 2
-    pieces = [None] * chips
-    pieces[0] = x
-    right, left = x, x
-    for step in range(1, chips // 2 + 1):
-        right = lax.ppermute(right, "blk", shift_pairs(n, 1))
-        pieces[step] = right
-        if step < chips // 2:
-            left = lax.ppermute(left, "blk", shift_pairs(n, -1))
-            pieces[chips - step] = left
-    return pieces
-
-
 def doubling_gather(x, n):
     x = x[None]
     step = n // 2
@@ -109,36 +95,61 @@
     out_ref[...] = ordered.astype(jnp.bfloat16)
 
 
-def rotate_out_kernel(near_ref, far_ref, basis_ref, order_ref, out_ref, total):
-    step = pl.program_id(0)
-
-    @pl.when(step == 0)
-    def _():
-        total[...] = jnp.zeros_like(total)
-
-    grads = jnp.concatenate([near_ref[...], far_ref[...]], axis=0)
-    total[...] += jnp.dot(grads, basis_ref[...], preferred_element_type=jnp.float32)
-
-    @pl.when(step == pl.num_programs(0) - 1)
-    def _():
-        aligned = jnp.dot(
-            order_ref[...], total[...].astype(jnp.bfloat16), preferred_element_type=jnp.float32
-        )
-        out_ref[...] = aligned.T.astype(jnp.bfloat16)
-
-
-def scale_kernel(tiles_ref, me_ref, aligned_ref, near_ref, far_ref, *refs):
-    out_ref = refs[-1]
-    at = pl.program_id(0)
-    mine = lax.rem(at, 2) == me_ref[0]
-    rotated = jnp.where(mine, near_ref[at // 2], far_ref[at // 2])
-    grad = jnp.dot(aligned_ref[...], rotated, preferred_element_type=jnp.float32)
-    for tile, damped_ref in enumerate(refs[:-1]):
-        lanes = slice(tile * LANES, (tile + 1) * LANES)
-        damped = damped_ref[...]
-        inverse = pl.reciprocal(damped, approx=True)
-        inverse = inverse * (2.0 - damped * inverse)
-        out_ref[:, lanes] = (grad[:, lanes] * inverse).astype(jnp.bfloat16)
+def rotate_out_kernel(near_ref, far_ref, basis_ref, order_ref, out_ref, basis, total, sem):
+    steps, depth = basis.shape[:2]
+
+    def copy_of(step):
+        rows = pl.ds(pl.multiple_of(step * depth, depth), depth)
+        return pltpu.make_async_copy(basis_ref.at[rows], basis.at[step], sem.at[step])
+
+    @pl.loop(0, steps)
+    def _(step):
+        copy_of(step).start()
+
+    total[...] = jnp.zeros_like(total)
+
+    @pl.loop(0, steps)
+    def _(step):
+        columns = pl.ds(pl.multiple_of(step * depth, depth), depth)
+        grads = jnp.concatenate([near_ref[:, columns], far_ref[:, columns]], axis=0)
+        copy_of(step).wait()
+        total[...] += jnp.dot(grads, basis[step], preferred_element_type=jnp.float32)
+
+    aligned = jnp.dot(
+        order_ref[...], total[...].astype(jnp.bfloat16), preferred_element_type=jnp.float32
+    )
+    out_ref[...] = aligned.T.astype(jnp.bfloat16)
+
+
+def scale_kernel(
+    tiles_ref, me_ref, aligned_ref, near_ref, far_ref, eigen_ref, out_ref, damped, sem
+):
+    tiles = damped.shape[0]
+    width = near_ref.shape[2]
+    per_piece = width // LANES
+
+    def copy_of(tile):
+        columns = pl.ds(pl.multiple_of(tiles_ref[tile] * LANES, LANES), LANES)
+        return pltpu.make_async_copy(eigen_ref.at[:, columns], damped.at[tile], sem.at[tile])
+
+    @pl.loop(0, tiles)
+    def _(tile):
+        copy_of(tile).start()
+
+    @pl.loop(0, tiles // per_piece)
+    def _(at):
+        mine = lax.rem(at, 2) == me_ref[0]
+        rotated = jnp.where(mine, near_ref[at // 2], far_ref[at // 2])
+        grad = jnp.dot(aligned_ref[...], rotated, preferred_element_type=jnp.float32)
+        for part in range(per_piece):
+            tile = at * per_piece + part
+            copy_of(tile).wait()
+            eigen = damped[tile]
+            inverse = pl.reciprocal(eigen, approx=True)
+            inverse = inverse * (2.0 - eigen * inverse)
+            columns = pl.ds(pl.multiple_of(tile * LANES, LANES), LANES)
+            scaled = grad[:, part * LANES : (part + 1) * LANES] * inverse
+            out_ref[:, columns] = scaled.astype(jnp.bfloat16)
 
 
 def window_kernel(n, scale, sources_ref, blocks_ref, window_ref, scaled_ref, *refs):
@@ -220,73 +231,69 @@
         name="rotate_in",
     )(acts, swap(acts, n), basis_in, order_in)
     rotated = plane_gather(rotated, n)
+
+    own = basis_in[:WC].T
+    right = [own]
+    left = [own]
+    early = max(chips // 2 - 2, 1)
+    for _ in range(early):
+        right.append(lax.ppermute(right[-1], "blk", shift_pairs(n, 1)))
+        left.append(lax.ppermute(left[-1], "blk", shift_pairs(n, -1)))
+
+    grads = doubling_gather(grad_out, n).reshape(tokens // 2, full_out)
+    grads_far = swap(grads, n)
+    order_out = one_hot(rows_of(jnp.take(pick(place_of(doubled_sources(n))), block_map), tok_rows))
+    grads, grads_far, rotated, right[-1], left[-1] = lax.optimization_barrier(
+        (grads, grads_far, rotated, right[-1], left[-1])
+    )
     rotated_far = swap(rotated, n)
-
-    grads = doubling_gather(grad_out, n).reshape(tokens // 2, full_out)
-    order_out = one_hot(rows_of(jnp.take(pick(place_of(doubled_sources(n))), block_map), tok_rows))
+    for _ in range(early, chips // 2 - 1):
+        right.append(lax.ppermute(right[-1], "blk", shift_pairs(n, 1)))
+        left.append(lax.ppermute(left[-1], "blk", shift_pairs(n, -1)))
     depth = 1024
     aligned = pl.pallas_call(
         rotate_out_kernel,
-        grid=(full_out // depth,),
         out_shape=jax.ShapeDtypeStruct((tile_width, tokens), jnp.bfloat16),
-        in_specs=[
-            pl.BlockSpec((tokens // 2, depth), lambda k: (0, k)),
-            pl.BlockSpec((tokens // 2, depth), lambda k: (0, k)),
-            pl.BlockSpec((depth, tile_width), lambda k: (k, 0)),
-            pl.BlockSpec((tokens, tokens), lambda k: (0, 0)),
+        in_specs=[VMEM, VMEM, ANY, VMEM],
+        out_specs=VMEM,
+        scratch_shapes=[
+            pltpu.VMEM((full_out // depth, depth, tile_width), jnp.bfloat16),
+            pltpu.VMEM((tokens, tile_width), jnp.float32),
+            pltpu.SemaphoreType.DMA((full_out // depth,)),
         ],
-        out_specs=pl.BlockSpec((tile_width, tokens), lambda k: (0, 0)),
-        scratch_shapes=[pltpu.VMEM((tokens, tile_width), jnp.float32)],
-        compiler_params=pltpu.CompilerParams(vmem_limit_bytes=44 * MIB),
+        compiler_params=pltpu.CompilerParams(vmem_limit_bytes=40 * MIB),
         cost_estimate=pl.CostEstimate(
             flops=2 * tokens * full_out * tile_width,
             bytes_accessed=2 * full_out * tile_width,
             transcendentals=0,
         ),
         name="rotate_out",
-    )(grads, swap(grads, n), basis_out, order_out)
-
-    per_piece = in_width // LANES
-
-    def eigen_spec(tile):
-        return pl.BlockSpec(
-            (tile_width, LANES), lambda j, tiles, core: (0, tiles[j * per_piece + tile])
-        )
-
-    whole = lambda *shape: pl.BlockSpec(shape, lambda j, tiles, core: (0,) * len(shape))
+    )(grads, grads_far, basis_out, order_out)
+
+    aligned, right[-1], left[-1] = lax.optimization_barrier((aligned, right[-1], left[-1]))
+    right.append(lax.ppermute(right[-1], "blk", shift_pairs(n, 1)))
+    tiles = full_in // LANES
     scaled = pl.pallas_call(
         scale_kernel,
         out_shape=jax.ShapeDtypeStruct((tile_width, full_in), jnp.bfloat16),
-        grid_spec=pltpu.PrefetchScalarGridSpec(
-            num_scalar_prefetch=2,
-            grid=(n,),
-            in_specs=[
-                whole(tile_width, tokens),
-                whole(chips, tokens, in_width),
-                whole(chips, tokens, in_width),
-            ]
-            + [eigen_spec(tile) for tile in range(per_piece)],
-            out_specs=pl.BlockSpec((tile_width, in_width), lambda j, tiles, core: (0, j)),
-        ),
-        compiler_params=pltpu.CompilerParams(vmem_limit_bytes=48 * MIB),
+        in_specs=[SMEM, SMEM, VMEM, VMEM, VMEM, ANY],
+        out_specs=VMEM,
+        scratch_shapes=[
+            pltpu.VMEM((tiles, tile_width, LANES), jnp.float32),
+            pltpu.SemaphoreType.DMA((tiles,)),
+        ],
+        compiler_params=pltpu.CompilerParams(vmem_limit_bytes=40 * MIB),
         cost_estimate=pl.CostEstimate(
             flops=2 * tile_width * full_in * tokens,
             bytes_accessed=6 * tile_width * full_in,
             transcendentals=tile_width * full_in,
         ),
         name="scale",
-    )(
-        tile_order,
-        lax.rem(me, 2).reshape(1),
-        aligned,
-        rotated,
-        rotated_far,
-        *[eigenvalues] * per_piece,
-    )
-
-    pieces = ring_gather(basis_in[:WC].T, n)
+    )(tile_order, lax.rem(me, 2).reshape(1), aligned, rotated, rotated_far, eigenvalues)
+
+    scaled, right[-1] = lax.optimization_barrier((scaled, right[-1]))
+    pieces = right + left[:0:-1]
     pieces += [swap(piece, n) for piece in pieces]
-
     rows = WR // n
     send, keep = pl.pallas_call(
         functools.partial(window_kernel, n, 1.0 / tokens),
@@ -299,7 +306,7 @@
             SMEM,
             SMEM,
             pl.BlockSpec((WR, tile_width), lambda i: (0, 0)),
-            pl.BlockSpec((tile_width, full_in), lambda i: (0, 0)),
+            VMEM,
         ]
         + [ANY] * n,
         out_specs=(VMEM, VMEM),
@@ -309,7 +316,7 @@
             pltpu.VMEM((WR, WC), jnp.float32),
             pltpu.SemaphoreType.DMA((n,)),
         ],
-        compiler_params=pltpu.CompilerParams(vmem_limit_bytes=40 * MIB),
+        compiler_params=pltpu.CompilerParams(vmem_limit_bytes=36 * MIB),
         cost_estimate=pl.CostEstimate(
             flops=2 * tile_width * full_in * WC + 2 * WR * tile_width * WC,
             bytes_accessed=2 * tile_width * full_in + 2 * WC * full_in,
@@ -323,6 +330,7 @@
         out_shape=jax.ShapeDtypeStruct((chips, rows, WC), jnp.bfloat16),
         in_specs=[VMEM, VMEM],
         out_specs=VMEM,
+        compiler_params=pltpu.CompilerParams(vmem_limit_bytes=8 * MIB),
         name="add_core",
     )(keep, swap(send, n))
     return pl.pallas_call(
@@ -330,6 +338,7 @@
         out_shape=jax.ShapeDtypeStruct((rows, WC), jnp.float32),
         in_specs=[VMEM],
         out_specs=VMEM,
+        compiler_params=pltpu.CompilerParams(vmem_limit_bytes=4 * MIB),
         name="add_chips",
     )(plane_exchange(summed, n))
 

time: 122 us -> 102 us (0.84)
  Pallas kernels: 44.1 us -> 28.9 us
  local copies, waits for them, and re-layouts: 11.3 us -> 6.57 us
  waiting for transfers between devices: 15.4 us -> 18.1 us
  blocking collectives: 17.4 us -> 15.7 us
    ppermute x7, waiting for transfers between devices: 8.25 us -> 0.02 us  [the longest x4 0.01 us: ring_body(): right.append(lax.ppermute(right[-1], 'blk', shift_pairs(n, 1)))]
    all_to_all x2, waiting for transfers between devices: 0.01 us -> 6.5 us  [plane_exchange(): lax.all_to_all(x, 'blk', 0, 0, axis_index_groups=planes(n), tiled=True)]
    pallas_call x1, Pallas kernels: 15.1 us -> 9.17 us  [ring_body(): pl.pallas_call(rotate_out_kernel, out_shape=jax.ShapeDtypeStruct((tile_wi...]
    pallas_call x1, Pallas kernels: 15.4 us -> 9.57 us  [ring_body(): pl.pallas_call(scale_kernel, out_shape=jax.ShapeDtypeStruct((tile_width,...]
    unnamed x11 -> x5, local copies, waits for them, and re-layouts: 6.46 us -> 1.73 us
    ppermute x3, waiting for transfers between devices: 5.01 us -> 7.91 us  [doubling_gather(): x = jnp.concatenate([x, lax.ppermute(x, 'blk', xor_pairs(n, step))], axis=0)]
    pallas_call x1, Pallas kernels: 2.06 us -> 0.09 us  [ring_body(): pl.pallas_call(add_core_kernel, out_shape=jax.ShapeDtypeStruct((chips, ro...]
    all_to_all x1, blocking collectives: 17.4 us -> 15.7 us  [plane_exchange(): lax.all_to_all(x, 'blk', 0, 0, axis_index_groups=planes(n), tiled=True)]
  transfers between devices with their start and end apart: 24 -> 24, of which waited for: 8 -> 8; matrix products, arithmetic and copies ran while one was open for 8% -> 10% of each run, Pallas kernels for 26% -> 19%
where the time goes in v3:
time: 102 us; the launch traced here: 101 us
  Pallas kernels  28.9 us (28%)
  starting transfers between devices  25.6 us (25%)
  waiting for transfers between devices  18.1 us (18%)
  blocking collectives  15.7 us (15%)
  local copies, waits for them, and re-layouts  6.57 us (6%)
  other arithmetic  5.93 us (6%)
    all_to_all x1, blocking collectives, plane_exchange(): lax.all_to_all(x, 'blk', 0, 0, axis_index_groups=planes(n), tiled=True)  15.7 us
    pallas_call x1, Pallas kernels, ring_body(): pl.pallas_call(scale_kernel, out_shape=jax.ShapeDtypeStruct((tile_width,...  9.57 us
    pallas_call x1, Pallas kernels, ring_body(): pl.pallas_call(rotate_out_kernel, out_shape=jax.ShapeDtypeStruct((tile_wi...  9.17 us
    pallas_call x1, Pallas kernels, ring_body(): pl.pallas_call(functools.partial(window_kernel, n, 1.0 / tokens), out_sha...  8.8 us
    all_to_all x2, starting transfers between devices, plane_exchange(): lax.all_to_all(x, 'blk', 0, 0, axis_index_groups=planes(n), tiled=True)  8.62 us
    ppermute x3, waiting for transfers between devices, doubling_gather(): x = jnp.concatenate([x, lax.ppermute(x, 'blk', xor_pairs(n, step))], axis=0)  7.91 us
    ppermute x3, starting transfers between devices, ring_body(): left.append(lax.ppermute(left[-1], 'blk', shift_pairs(n, -1)))  7.12 us
    ppermute x3, starting transfers between devices, doubling_gather(): x = jnp.concatenate([x, lax.ppermute(x, 'blk', xor_pairs(n, step))], axis=0)  6.76 us
  transfers between devices with their start and end apart: 24, of which 8 were waited for; matrix products, arithmetic and copies ran while one was open for 10% of the time, Pallas kernels for 19%

profile of v3, /device:TPU:0, one launch (start us, length us, event | category | flops | bytes accessed | tf_op | source)
XLA Modules:
  0.0 101.0 jit_solution(5201068199703616919)
XLA Ops:
  0.0 1.0 slice.3
  1.1 3.0 %collective-permute-start.7 = (bf16[256,512]{1,0:T(8,128)(2,1)S(1)}, bf16[256,512]{1,0:T(8,128)(2,1)S(1)}, u32[]{:S(2)}, u32[]{:S(2)}) collective-permute-start(bf16[256,512]{1,0:T(8,128)(2,1)S(1)} %bitcast.11), channel_id=1, source_target_pairs={{0,2},{1,3},{4,0},{5,1},{8,4},{9,5},{12,8},{13,9},{14,12},{15,13},... | collective-permute-start | bytes 786440 | tf_op jit(solution)/shard_map/ppermute | solution.py:241
  4.3 3.0 %collective-permute-start = (bf16[1,2,14336]{2,1,0:T(2,128)(2,1)}, bf16[1,2,14336]{2,1,0:T(2,128)(2,1)S(1)}, u32[]{:S(2)}, u32[]{:S(2)}) collective-permute-start(bf16[1,2,14336]{2,1,0:T(2,128)(2,1)} %bitcast.15), channel_id=1, source_target_pairs={{0,8},{1,9},{2,10},{3,11},{4,12},{5,13},{6,14},{7,15},{8,0},{9,1},... | collective-permute-start | bytes 172040 | tf_op jit(solution)/shard_map/ppermute | solution.py:76
  7.2 1.4 %broadcast_in_dim.10 = bf16[8,2,4096]{2,1,0:T(2,128)(2,1)} broadcast(bf16[2,4096]{1,0:T(2,128)(2,1)} %param.12), dimensions={1,2} | broadcast | bytes 147456 | tf_op jit(solution)/shard_map/broadcast_in_dim | solution.py:86
  8.7 3.8 %all-to-all-start = ((bf16[8,2,4096]{2,1,0:T(2,128)(2,1)}), bf16[8,2,4096]{2,1,0:T(2,128)(2,1)S(1)}, u32[]{:S(2)}, u32[]{:S(2)}) async-start(bf16[8,2,4096]{2,1,0:T(2,128)(2,1)} %broadcast_in_dim.10), calls=%async_computation | async-start | bytes 262144 | tf_op jit(solution)/shard_map/all_to_all | solution.py:82
  13.2 1.0 %collective-permute-done = bf16[1,2,14336]{2,1,0:T(2,128)(2,1)S(1)} collective-permute-done((bf16[1,2,14336]{2,1,0:T(2,128)(2,1)}, bf16[1,2,14336]{2,1,0:T(2,128)(2,1)S(1)}, u32[]{:S(2)}, u32[]{:S(2)}) %collective-permute-start) | collective-permute-done | bytes 57376 | tf_op jit(solution)/shard_map/ppermute | solution.py:76
  14.2 1.0 pad_maximum_fusion.2
  15.2 1.1 %collective-permute-start.1 = (bf16[2,2,14336]{2,1,0:T(2,128)(2,1)S(1)}, bf16[2,2,14336]{2,1,0:T(2,128)(2,1)S(1)}, u32[]{:S(2)}, u32[]{:S(2)}) collective-permute-start(bf16[2,2,14336]{2,1,0:T(2,128)(2,1)S(1)} %pad_maximum_fusion.2), channel_id=1, source_target_pairs={{0,4},{1,5},{2,6},{3,7},{4,0},{5,1},{6,2},{7,3},{8,12},{9,13},{10,... | collective-permute-start | bytes 344072 | tf_op jit(solution)/shard_map/ppermute | solution.py:76
  16.4 3.8 %collective-permute-done.1 = bf16[2,2,14336]{2,1,0:T(2,128)(2,1)S(1)} collective-permute-done((bf16[2,2,14336]{2,1,0:T(2,128)(2,1)S(1)}, bf16[2,2,14336]{2,1,0:T(2,128)(2,1)S(1)}, u32[]{:S(2)}, u32[]{:S(2)}) %collective-permute-start.1) | collective-permute-done | bytes 114720 | tf_op jit(solution)/shard_map/ppermute | solution.py:76
  20.3 1.1 %pad_maximum_fusion.1 = bf16[4,2,14336]{2,1,0:T(2,128)(2,1)S(1)} fusion(bf16[2,2,14336]{2,1,0:T(2,128)(2,1)S(1)} %collective-permute-done.1, bf16[1,2,14336]{2,1,0:T(2,128)(2,1)S(1)} %collective-permute-done, bf16[1,2,14336]{2,1,0:T(2,128)(2,1)} %bitcast.17), kind=kLoop, calls=%fused_computation.2 | loop fusion | flops 229376 | bytes 458752 | tf_op jit(solution)/shard_map/concatenate | solution.py:76
  21.4 2.7 %collective-permute-start.2 = (bf16[4,2,14336]{2,1,0:T(2,128)(2,1)S(1)}, bf16[4,2,14336]{2,1,0:T(2,128)(2,1)S(1)}, u32[]{:S(2)}, u32[]{:S(2)}) collective-permute-start(bf16[4,2,14336]{2,1,0:T(2,128)(2,1)S(1)} %pad_maximum_fusion.1), channel_id=1, source_target_pairs={{0,2},{1,3},{2,0},{3,1},{4,6},{5,7},{6,4},{7,5},{8,10},{9,11},{10,... | collective-permute-start | bytes 688136 | tf_op jit(solution)/shard_map/ppermute | solution.py:76
  25.0 3.0 %collective-permute-done.2 = bf16[4,2,14336]{2,1,0:T(2,128)(2,1)S(1)} collective-permute-done((bf16[4,2,14336]{2,1,0:T(2,128)(2,1)S(1)}, bf16[4,2,14336]{2,1,0:T(2,128)(2,1)S(1)}, u32[]{:S(2)}, u32[]{:S(2)}) %collective-permute-start.2) | collective-permute-done | bytes 229408 | tf_op jit(solution)/shard_map/ppermute | solution.py:76
  28.1 1.5 %pad_maximum_fusion = bf16[8,2,14336]{2,1,0:T(2,128)(2,1)S(1)} fusion(bf16[4,2,14336]{2,1,0:T(2,128)(2,1)S(1)} %collective-permute-done.2, bf16[2,2,14336]{2,1,0:T(2,128)(2,1)S(1)} %collective-permute-done.1, bf16[1,2,14336]{2,1,0:T(2,128)(2,1)S(1)} %collective-permute-done, bf16[1,2,14336]{2,1,0:T(2,128)(2,1)} %bitcast.18), kind=kLoop, calls=%fused_computation.1 | loop fusion | flops 688128 | bytes 917504 | tf_op jit(solution)/shard_map/concatenate | solution.py:76
  30.5 2.1 %collective-permute-start.8 = (bf16[256,512]{1,0:T(8,128)(2,1)S(1)}, bf16[256,512]{1,0:T(8,128)(2,1)S(1)}, u32[]{:S(2)}, u32[]{:S(2)}) collective-permute-start(bf16[256,512]{1,0:T(8,128)(2,1)S(1)} %collective-permute-done.7.refs_7_), channel_id=1, source_target_pairs={{0,2},{1,3},{4,0},{5,1},{8,4},{9,5},{12,8},{13,9},{14,12},{15,13},... | collective-permute-start | bytes 786440 | tf_op jit(solution)/shard_map/ppermute | solution.py:241
  32.6 1.6 %copy-done = bf16[4096,256]{1,0:T(8,128)(2,1)S(1)} copy-done((bf16[4096,256]{1,0:T(8,128)(2,1)S(1)}, bf16[4096,256]{1,0:T(8,128)(2,1)}, u32[]{:S(2)}) %copy-start) | copy-done | bytes 2097176
  35.4 4.8 %all-to-all-start.1 = ((bf16[8,32,256]{2,1,0:T(8,128)(2,1)}), bf16[8,32,256]{2,1,0:T(8,128)(2,1)S(1)}, u32[]{:S(2)}, u32[]{:S(2)}) async-start(bf16[8,32,256]{2,1,0:T(8,128)(2,1)} %broadcast_in_dim.11), calls=%async_computation.1 | async-start | bytes 262144 | tf_op jit(solution)/shard_map/all_to_all | solution.py:82
  41.1 6.5 %all-to-all-done.1.near_ref = bf16[8,32,256]{2,1,0:T(8,128)(2,1)S(1)} async-done(((bf16[8,32,256]{2,1,0:T(8,128)(2,1)}), bf16[8,32,256]{2,1,0:T(8,128)(2,1)S(1)}, u32[]{:S(2)}, u32[]{:S(2)}) %all-to-all-start.1) | async-done | bytes 131104 | tf_op jit(solution)/shard_map/all_to_all | solution.py:82
  47.6 2.0 %collective-permute-start.10 = (bf16[256,512]{1,0:T(8,128)(2,1)S(1)}, bf16[256,512]{1,0:T(8,128)(2,1)S(1)}, u32[]{:S(2)}, u32[]{:S(2)}) collective-permute-start(bf16[256,512]{1,0:T(8,128)(2,1)S(1)} %collective-permute-done.8.refs_6_), channel_id=1, source_target_pairs={{0,2},{1,3},{4,0},{5,1},{8,4},{9,5},{12,8},{13,9},{14,12},{15,13},... | collective-permute-start | bytes 786440 | tf_op jit(solution)/shard_map/ppermute | solution.py:252
  49.7 9.2 %rotate_out.1.aligned_ref = bf16[896,32]{1,0:T(8,128)(2,1)S(1)} custom-call(bf16[16,14336]{1,0:T(8,128)(2,1)S(1)} %reshape.59.near_ref, bf16[16,14336]{1,0:T(8,128)(2,1)S(1)} %collective-permute-done.3.far_ref, bf16[14336,896]{1,0:T(8,128)(2,1)} %window_ref.1, bf16[32,32]{1,0:T(8,128)(2,1)S(1)} %fusion.1.order_ref), custom_call_target="tpu_custom_call" | custom-call | flops 822083584 | bytes 25690112 | tf_op jit(solution)/shard_map/rotate_out/pallas_call | solution.py:254
  60.0 1.3 %collective-permute-done.11.far_ref = bf16[8,32,256]{2,1,0:T(8,128)(2,1)S(1)} collective-permute-done((bf16[8,32,256]{2,1,0:T(8,128)(2,1)S(1)}, bf16[8,32,256]{2,1,0:T(8,128)(2,1)S(1)}, u32[]{:S(2)}, u32[]{:S(2)}) %collective-permute-start.11) | collective-permute-done | bytes 131104 | tf_op jit(solution)/shard_map/ppermute | solution.py:36
  61.6 9.6 %scale.1.scaled_ref = bf16[896,4096]{1,0:T(8,128)(2,1)S(1)} custom-call(s32[32]{0:T(128)S(1)} %copy-done.1, s32[1]{0:T(128)} %bitcast.2.me_ref, bf16[896,32]{1,0:T(8,128)(2,1)S(1)} %rotate_out.1.aligned_ref, bf16[8,32,256]{2,1,0:T(8,128)(2,1)S(1)} %all-to-all-done.1.near_ref, bf16[8,32,256]{2,1,0:T(8,128)(2,1)S(1)} %collective-permute-done.11.far_ref, ...), custom_call_target="tpu_custom_call" | custom-call | flops 234881024 | bytes 22020096 | tf_op jit(solution)/shard_map/scale/pallas_call | solution.py:276
  73.9 8.8 %window.1 = (bf16[8,48,512]{2,1,0:T(8,128)(2,1)S(1)}, f32[8,48,512]{2,1,0:T(8,128)S(1)}) custom-call(s32[16]{0:T(128)S(1)} %get-tuple-element.29.sources_ref, s32[16]{0:T(128)S(1)} %get-tuple-element.30.blocks_ref, bf16[14336,896]{1,0:T(8,128)(2,1)} %window_ref.1, bf16[896,4096]{1,0:T(8,128)(2,1)S(1)} %scale.1.scaled_ref, bf16[256,512]{1,0:T(8,128)(2,1)S(1)} %bitcast.14, ...), custom_call_target="tpu_custom_call" | custom-call | flops 4462739456 | bytes 11534336 | tf_op jit(solution)/shard_map/window/pallas_call | solution.py:298
  83.0 1.5 %collective-permute-done.21.got_ref = bf16[8,48,512]{2,1,0:T(8,128)(2,1)S(1)} collective-permute-done((bf16[8,48,512]{2,1,0:T(8,128)(2,1)S(1)}, bf16[8,48,512]{2,1,0:T(8,128)(2,1)S(1)}, u32[]{:S(2)}, u32[]{:S(2)}) %collective-permute-start.21) | collective-permute-done | bytes 393248 | tf_op jit(solution)/shard_map/ppermute | solution.py:36
  84.6 15.7 %all_to_all.15.parts_ref = bf16[8,48,512]{2,1,0:T(8,128)(2,1)S(1)} all-to-all(bf16[8,48,512]{2,1,0:T(8,128)(2,1)S(1)} %add_core.1), channel_id=1, replica_groups={{0,2,4,6,8,10,12,14},{1,3,5,7,9,11,13,15},{16,18,20,22,24,26,28,30},{17..., dimensions={0} | all-to-all | bytes 786432 | tf_op jit(solution)/shard_map/all_to_all | solution.py:82
  (56 shorter events, 10.3 us)
Async XLA Ops:
  1.1 29.4 %collective-permute-start.7 = (bf16[256,512]{1,0:T(8,128)(2,1)S(1)}, bf16[256,512]{1,0:T(8,128)(2,1)S(1)}, u32[]{:S(2)}, u32[]{:S(2)}) collective-permute-start(bf16[256,512]{1,0:T(8,128)(2,1)S(1)} %bitcast.11), channel_id=1, source_target_pairs={{0,2},{1,3},{4,0},{5,1},{8,4},{9,5},{12,8},{13,9},{14,12},{15,13},... | collective-permute-start | bytes 786440 | tf_op jit(solution)/shard_map/ppermute | solution.py:241
  4.1 28.4 %collective-permute-start.5 = (bf16[256,512]{1,0:T(8,128)(2,1)S(1)}, bf16[256,512]{1,0:T(8,128)(2,1)S(1)}, u32[]{:S(2)}, u32[]{:S(2)}) collective-permute-start(bf16[256,512]{1,0:T(8,128)(2,1)S(1)} %bitcast.12), channel_id=1, source_target_pairs={{0,4},{1,5},{4,8},{5,9},{8,12},{9,13},{12,14},{13,15},{14,10},{15,... | collective-permute-start | bytes 786440 | tf_op jit(solution)/shard_map/ppermute | solution.py:240
  4.3 10.0 %collective-permute-start = (bf16[1,2,14336]{2,1,0:T(2,128)(2,1)}, bf16[1,2,14336]{2,1,0:T(2,128)(2,1)S(1)}, u32[]{:S(2)}, u32[]{:S(2)}) collective-permute-start(bf16[1,2,14336]{2,1,0:T(2,128)(2,1)} %bitcast.15), channel_id=1, source_target_pairs={{0,8},{1,9},{2,10},{3,11},{4,12},{5,13},{6,14},{7,15},{8,0},{9,1},... | collective-permute-start | bytes 172040 | tf_op jit(solution)/shard_map/ppermute | solution.py:76
  8.7 16.2 %all-to-all-start = ((bf16[8,2,4096]{2,1,0:T(2,128)(2,1)}), bf16[8,2,4096]{2,1,0:T(2,128)(2,1)S(1)}, u32[]{:S(2)}, u32[]{:S(2)}) async-start(bf16[8,2,4096]{2,1,0:T(2,128)(2,1)} %broadcast_in_dim.10), calls=%async_computation | async-start | bytes 262144 | tf_op jit(solution)/shard_map/all_to_all | solution.py:82
  15.2 5.0 %collective-permute-start.1 = (bf16[2,2,14336]{2,1,0:T(2,128)(2,1)S(1)}, bf16[2,2,14336]{2,1,0:T(2,128)(2,1)S(1)}, u32[]{:S(2)}, u32[]{:S(2)}) collective-permute-start(bf16[2,2,14336]{2,1,0:T(2,128)(2,1)S(1)} %pad_maximum_fusion.2), channel_id=1, source_target_pairs={{0,4},{1,5},{2,6},{3,7},{4,0},{5,1},{6,2},{7,3},{8,12},{9,13},{10,... | collective-permute-start | bytes 344072 | tf_op jit(solution)/shard_map/ppermute | solution.py:76
  21.4 6.7 %collective-permute-start.2 = (bf16[4,2,14336]{2,1,0:T(2,128)(2,1)S(1)}, bf16[4,2,14336]{2,1,0:T(2,128)(2,1)S(1)}, u32[]{:S(2)}, u32[]{:S(2)}) collective-permute-start(bf16[4,2,14336]{2,1,0:T(2,128)(2,1)S(1)} %pad_maximum_fusion.1), channel_id=1, source_target_pairs={{0,2},{1,3},{2,0},{3,1},{4,6},{5,7},{6,4},{7,5},{8,10},{9,11},{10,... | collective-permute-start | bytes 688136 | tf_op jit(solution)/shard_map/ppermute | solution.py:76
  25.0 7.6 %collective-permute-start.4 = (bf16[16,4096]{1,0:T(8,128)(2,1)S(1)}, bf16[16,4096]{1,0:T(8,128)(2,1)S(1)}, u32[]{:S(2)}, u32[]{:S(2)}) collective-permute-start(bf16[16,4096]{1,0:T(8,128)(2,1)S(1)} %reshape.60.near_ref), channel_id=1, source_target_pairs={{0,1},{1,0},{2,3},{3,2},{4,5},{5,4},{6,7},{7,6},{8,9},{9,8},{10,11... | collective-permute-start | bytes 393224 | tf_op jit(solution)/shard_map/ppermute | solution.py:36
  29.7 17.9 %collective-permute-start.3 = (bf16[16,14336]{1,0:T(8,128)(2,1)S(1)}, bf16[16,14336]{1,0:T(8,128)(2,1)S(1)}, u32[]{:S(2)}, u32[]{:S(2)}) collective-permute-start(bf16[16,14336]{1,0:T(8,128)(2,1)S(1)} %reshape.59.near_ref), channel_id=1, source_target_pairs={{0,1},{1,0},{2,3},{3,2},{4,5},{5,4},{6,7},{7,6},{8,9},{9,8},{10,11... | collective-permute-start | bytes 1376264 | tf_op jit(solution)/shard_map/ppermute | solution.py:36
  30.5 10.6 %collective-permute-start.8 = (bf16[256,512]{1,0:T(8,128)(2,1)S(1)}, bf16[256,512]{1,0:T(8,128)(2,1)S(1)}, u32[]{:S(2)}, u32[]{:S(2)}) collective-permute-start(bf16[256,512]{1,0:T(8,128)(2,1)S(1)} %collective-permute-done.7.refs_7_), channel_id=1, source_target_pairs={{0,2},{1,3},{4,0},{5,1},{8,4},{9,5},{12,8},{13,9},{14,12},{15,13},... | collective-permute-start | bytes 786440 | tf_op jit(solution)/shard_map/ppermute | solution.py:241
  32.6 8.5 %collective-permute-start.6 = (bf16[256,512]{1,0:T(8,128)(2,1)S(1)}, bf16[256,512]{1,0:T(8,128)(2,1)S(1)}, u32[]{:S(2)}, u32[]{:S(2)}) collective-permute-start(bf16[256,512]{1,0:T(8,128)(2,1)S(1)} %collective-permute-done.5.refs_1_), channel_id=1, source_target_pairs={{0,4},{1,5},{4,8},{5,9},{8,12},{9,13},{12,14},{13,15},{14,10},{15,... | collective-permute-start | bytes 786440 | tf_op jit(solution)/shard_map/ppermute | solution.py:240
  35.4 12.2 %all-to-all-start.1 = ((bf16[8,32,256]{2,1,0:T(8,128)(2,1)}), bf16[8,32,256]{2,1,0:T(8,128)(2,1)S(1)}, u32[]{:S(2)}, u32[]{:S(2)}) async-start(bf16[8,32,256]{2,1,0:T(8,128)(2,1)} %broadcast_in_dim.11), calls=%async_computation.1 | async-start | bytes 262144 | tf_op jit(solution)/shard_map/all_to_all | solution.py:82
  47.6 11.3 %collective-permute-start.9 = (bf16[256,512]{1,0:T(8,128)(2,1)S(1)}, bf16[256,512]{1,0:T(8,128)(2,1)S(1)}, u32[]{:S(2)}, u32[]{:S(2)}) collective-permute-start(bf16[256,512]{1,0:T(8,128)(2,1)S(1)} %collective-permute-done.6.refs_2_), channel_id=1, source_target_pairs={{0,4},{1,5},{4,8},{5,9},{8,12},{9,13},{12,14},{13,15},{14,10},{15,... | collective-permute-start | bytes 786440 | tf_op jit(solution)/shard_map/ppermute | solution.py:251
  47.6 11.3 %collective-permute-start.10 = (bf16[256,512]{1,0:T(8,128)(2,1)S(1)}, bf16[256,512]{1,0:T(8,128)(2,1)S(1)}, u32[]{:S(2)}, u32[]{:S(2)}) collective-permute-start(bf16[256,512]{1,0:T(8,128)(2,1)S(1)} %collective-permute-done.8.refs_6_), channel_id=1, source_target_pairs={{0,2},{1,3},{4,0},{5,1},{8,4},{9,5},{12,8},{13,9},{14,12},{15,13},... | collective-permute-start | bytes 786440 | tf_op jit(solution)/shard_map/ppermute | solution.py:252
  58.9 12.3 %collective-permute-start.12 = (bf16[256,512]{1,0:T(8,128)(2,1)S(1)}, bf16[256,512]{1,0:T(8,128)(2,1)S(1)}, u32[]{:S(2)}, u32[]{:S(2)}) collective-permute-start(bf16[256,512]{1,0:T(8,128)(2,1)S(1)} %collective-permute-done.9.refs_3_), channel_id=1, source_target_pairs={{0,4},{1,5},{4,8},{5,9},{8,12},{9,13},{12,14},{13,15},{14,10},{15,... | collective-permute-start | bytes 786440 | tf_op jit(solution)/shard_map/ppermute | solution.py:274
  58.9 12.5 %collective-permute-start.13 = (bf16[256,512]{1,0:T(8,128)(2,1)S(1)}, bf16[256,512]{1,0:T(8,128)(2,1)S(1)}, u32[]{:S(2)}, u32[]{:S(2)}) collective-permute-start(bf16[256,512]{1,0:T(8,128)(2,1)S(1)} %bitcast.13), channel_id=1, source_target_pairs={{0,1},{1,0},{2,3},{3,2},{4,5},{5,4},{6,7},{7,6},{8,9},{9,8},{10,11... | collective-permute-start | bytes 786440 | tf_op jit(solution)/shard_map/ppermute | solution.py:36
  59.0 12.8 %collective-permute-start.20 = (bf16[256,512]{1,0:T(8,128)(2,1)S(1)}, bf16[256,512]{1,0:T(8,128)(2,1)S(1)}, u32[]{:S(2)}, u32[]{:S(2)}) collective-permute-start(bf16[256,512]{1,0:T(8,128)(2,1)S(1)} %collective-permute-done.7.refs_7_), channel_id=1, source_target_pairs={{0,1},{1,0},{2,3},{3,2},{4,5},{5,4},{6,7},{7,6},{8,9},{9,8},{10,11... | collective-permute-start | bytes 786440 | tf_op jit(solution)/shard_map/ppermute | solution.py:36
  59.5 12.5 %collective-permute-start.14 = (bf16[256,512]{1,0:T(8,128)(2,1)S(1)}, bf16[256,512]{1,0:T(8,128)(2,1)}, u32[]{:S(2)}, u32[]{:S(2)}) collective-permute-start(bf16[256,512]{1,0:T(8,128)(2,1)S(1)} %collective-permute-done.5.refs_1_), channel_id=1, source_target_pairs={{0,1},{1,0},{2,3},{3,2},{4,5},{5,4},{6,7},{7,6},{8,9},{9,8},{10,11... | collective-permute-start | bytes 786440 | tf_op jit(solution)/shard_map/ppermute | solution.py:36
  59.6 1.7 %collective-permute-start.11 = (bf16[8,32,256]{2,1,0:T(8,128)(2,1)S(1)}, bf16[8,32,256]{2,1,0:T(8,128)(2,1)S(1)}, u32[]{:S(2)}, u32[]{:S(2)}) collective-permute-start(bf16[8,32,256]{2,1,0:T(8,128)(2,1)S(1)} %all-to-all-done.1.near_ref), channel_id=1, source_target_pairs={{0,1},{1,0},{2,3},{3,2},{4,5},{5,4},{6,7},{7,6},{8,9},{9,8},{10,11... | collective-permute-start | bytes 393224 | tf_op jit(solution)/shard_map/ppermute | solution.py:36
  61.3 11.7 %collective-permute-start.15 = (bf16[256,512]{1,0:T(8,128)(2,1)S(1)}, bf16[256,512]{1,0:T(8,128)(2,1)S(1)}, u32[]{:S(2)}, u32[]{:S(2)}) collective-permute-start(bf16[256,512]{1,0:T(8,128)(2,1)S(1)} %collective-permute-done.6.refs_2_), channel_id=1, source_target_pairs={{0,1},{1,0},{2,3},{3,2},{4,5},{5,4},{6,7},{7,6},{8,9},{9,8},{10,11... | collective-permute-start | bytes 786440 | tf_op jit(solution)/shard_map/ppermute | solution.py:36
  71.2 1.8 %collective-permute-start.19 = (bf16[256,512]{1,0:T(8,128)(2,1)S(1)}, bf16[256,512]{1,0:T(8,128)(2,1)S(1)}, u32[]{:S(2)}, u32[]{:S(2)}) collective-permute-start(bf16[256,512]{1,0:T(8,128)(2,1)S(1)} %collective-permute-done.8.refs_6_), channel_id=1, source_target_pairs={{0,1},{1,0},{2,3},{3,2},{4,5},{5,4},{6,7},{7,6},{8,9},{9,8},{10,11... | collective-permute-start | bytes 786440 | tf_op jit(solution)/shard_map/ppermute | solution.py:36
  71.5 2.1 %collective-permute-start.16 = (bf16[256,512]{1,0:T(8,128)(2,1)S(1)}, bf16[256,512]{1,0:T(8,128)(2,1)S(1)}, u32[]{:S(2)}, u32[]{:S(2)}) collective-permute-start(bf16[256,512]{1,0:T(8,128)(2,1)S(1)} %collective-permute-done.9.refs_3_), channel_id=1, source_target_pairs={{0,1},{1,0},{2,3},{3,2},{4,5},{5,4},{6,7},{7,6},{8,9},{9,8},{10,11... | collective-permute-start | bytes 786440 | tf_op jit(solution)/shard_map/ppermute | solution.py:36
  71.8 1.8 %collective-permute-start.18 = (bf16[256,512]{1,0:T(8,128)(2,1)S(1)}, bf16[256,512]{1,0:T(8,128)(2,1)S(1)}, u32[]{:S(2)}, u32[]{:S(2)}) collective-permute-start(bf16[256,512]{1,0:T(8,128)(2,1)S(1)} %collective-permute-done.10.refs_5_), channel_id=1, source_target_pairs={{0,1},{1,0},{2,3},{3,2},{4,5},{5,4},{6,7},{7,6},{8,9},{9,8},{10,11... | collective-permute-start | bytes 786440 | tf_op jit(solution)/shard_map/ppermute | solution.py:36
  72.0 1.9 %collective-permute-start.17 = (bf16[256,512]{1,0:T(8,128)(2,1)S(1)}, bf16[256,512]{1,0:T(8,128)(2,1)S(1)}, u32[]{:S(2)}, u32[]{:S(2)}) collective-permute-start(bf16[256,512]{1,0:T(8,128)(2,1)S(1)} %collective-permute-done.12.refs_4_), channel_id=1, source_target_pairs={{0,1},{1,0},{2,3},{3,2},{4,5},{5,4},{6,7},{7,6},{8,9},{9,8},{10,11... | collective-permute-start | bytes 786440 | tf_op jit(solution)/shard_map/ppermute | solution.py:36
  82.7 1.8 %collective-permute-start.21 = (bf16[8,48,512]{2,1,0:T(8,128)(2,1)S(1)}, bf16[8,48,512]{2,1,0:T(8,128)(2,1)S(1)}, u32[]{:S(2)}, u32[]{:S(2)}) collective-permute-start(bf16[8,48,512]{2,1,0:T(8,128)(2,1)S(1)} %get-tuple-element.28), channel_id=1, source_target_pairs={{0,1},{1,0},{2,3},{3,2},{4,5},{5,4},{6,7},{7,6},{8,9},{9,8},{10,11... | collective-permute-start | bytes 1179656 | tf_op jit(solution)/shard_map/ppermute | solution.py:36
  (2 other events, 33.4 us)

commit v4 on v3

v4 whole, which is shorter than its diff:
```python
import functools

import jax
import jax.numpy as jnp
from jax import lax
from jax.experimental import pallas as pl
from jax.experimental.pallas import tpu as pltpu
from jax.sharding import PartitionSpec as P

WR = 768
WC = 512
LANES = 128
MIB = 1 << 20


def ring_of(n):
    chips = n // 2
    return [*range(0, chips, 2), *range(chips - 1, 0, -2)]


def shift_pairs(n, by):
    ring = ring_of(n)
    return [
        (2 * ring[p] + c, 2 * ring[(p + by) % len(ring)] + c)
        for p in range(len(ring))
        for c in range(2)
    ]


def ring_source(me, steps, other, chips):
    chip, core = me // 2, lax.rem(me, 2)
    place = jnp.where(lax.rem(chip, 2) == 0, chip // 2, chips - 1 - chip // 2)
    place = lax.rem(place + chips - steps, chips)
    chip = jnp.where(place < chips // 2, 2 * place, 2 * (chips - 1 - place) + 1)
    return 2 * chip + (core ^ other)


def xor_pairs(n, key):
    return [(b, b ^ key) for b in range(n)]


def swap(x, n):
    return lax.ppermute(x, "blk", xor_pairs(n, 1))


def plane_exchange(x, n):
    planes = [list(range(c, n, 2)) for c in range(2)]
    return lax.all_to_all(x, "blk", 0, 0, axis_index_groups=planes, tiled=True)


def bits_of(size):
    return size.bit_length() - 1


def held_tokens(me, tokens, tok_rows):
    row = lax.broadcasted_iota(jnp.int32, (tokens, tokens), 1)
    chips = tokens // tok_rows // 2
    place = (row >> bits_of(tok_rows)) & (chips - 1)
    chip = jnp.zeros_like(row)
    for bit in range(bits_of(chips)):
        chip |= ((place >> bit) & 1) << (bits_of(chips) - 1 - bit)
    other = row >> bits_of(tokens // 2)
    device = me ^ (2 * chip + other)
    return (device << bits_of(tok_rows)) + (row & (tok_rows - 1))


def reorder(wanted, held, rotated):
    order = jnp.where(wanted == held, 1.0, 0.0).astype(jnp.bfloat16)
    return jnp.dot(order, rotated.astype(jnp.bfloat16), preferred_element_type=jnp.float32)


def rotate_in_kernel(tok_rows, first, me_ref, near_ref, far_ref, basis_ref, out_ref, basis, sem):
    steps, depth = basis.shape[:2]
    tokens = out_ref.shape[1]

    def copy_of(step):
        return pltpu.make_async_copy(
            basis_ref.at[pl.ds(step * depth, depth)], basis.at[step], sem.at[step]
        )

    for step in range(steps):
        copy_of(step).start()
    rotated = jnp.zeros((tokens, basis.shape[2]), jnp.float32)
    for step in range(steps):
        columns = slice(first + step * depth, first + (step + 1) * depth)
        acts = jnp.concatenate([near_ref[:, columns], far_ref[:, columns]], axis=0)
        copy_of(step).wait()
        rotated += jnp.dot(acts, basis[step], preferred_element_type=jnp.float32)
    wanted = lax.broadcasted_iota(jnp.int32, (tokens, tokens), 0)
    held = held_tokens(me_ref[0], tokens, tok_rows)
    ordered = reorder(wanted, held, rotated).astype(jnp.bfloat16)
    for copy in range(out_ref.shape[0]):
        out_ref[copy] = ordered


def rotate_out_kernel(
    tok_rows, me_ref, map_ref, near_ref, far_ref, basis_ref, out_ref, basis, total, sem
):
    steps, depth = basis.shape[:2]
    tokens = total.shape[0]

    def copy_of(step):
        rows = pl.ds(pl.multiple_of(step * depth, depth), depth)
        return pltpu.make_async_copy(basis_ref.at[rows], basis.at[step], sem.at[step])

    @pl.loop(0, steps)
    def _(step):
        copy_of(step).start()

    total[...] = jnp.zeros_like(total)

    @pl.loop(0, steps)
    def _(step):
        columns = pl.ds(pl.multiple_of(step * depth, depth), depth)
        grads = jnp.concatenate([near_ref[:, columns], far_ref[:, columns]], axis=0)
        copy_of(step).wait()
        total[...] += jnp.dot(grads, basis[step], preferred_element_type=jnp.float32)

    row = lax.broadcasted_iota(jnp.int32, (tokens, tokens), 0)
    block = row >> bits_of(tok_rows)
    wanted = jnp.zeros_like(row)
    for stored in range(tokens // tok_rows):
        wanted = jnp.where(block == stored, map_ref[stored] * tok_rows, wanted)
    wanted += row & (tok_rows - 1)
    held = held_tokens(me_ref[0], tokens, tok_rows)
    out_ref[...] = reorder(wanted, held, total[...]).T.astype(jnp.bfloat16)


def scale_kernel(
    tiles_ref, me_ref, aligned_ref, near_ref, far_ref, eigen_ref, out_ref, damped, sem
):
    blocks, depth = damped.shape[:2]
    chips, _, width = near_ref.shape

    def copy_of(block):
        rows = pl.ds(pl.multiple_of(block * depth, depth), depth)
        return pltpu.make_async_copy(eigen_ref.at[rows], damped.at[block], sem.at[block])

    @pl.loop(0, blocks)
    def _(block):
        copy_of(block).start()

    odd = lax.rem(me_ref[0], 2) == 1

    @pl.loop(0, blocks)
    def _(block):
        rows = pl.ds(pl.multiple_of(block * depth, depth), depth)
        aligned = aligned_ref[rows, :]
        copy_of(block).wait()
        for at in range(2 * chips):
            mine = odd if at % 2 else jnp.logical_not(odd)
            rotated = jnp.where(mine, near_ref[at // 2], far_ref[at // 2])
            grad = jnp.dot(aligned, rotated, preferred_element_type=jnp.float32)
            for first in range(0, width, LANES):
                tile = (at * width + first) // LANES
                lanes = pl.ds(pl.multiple_of(tiles_ref[tile] * LANES, LANES), LANES)
                eigen = damped[block, :, lanes]
                inverse = pl.reciprocal(eigen, approx=True)
                inverse = inverse * (2.0 - eigen * inverse)
                scaled = grad[:, first : first + LANES] * inverse
                out_ref[rows, tile * LANES : (tile + 1) * LANES] = scaled.astype(jnp.bfloat16)


def window_kernel(n, begun, scale, me_ref, window_ref, scaled_ref, *refs):
    pieces = refs[:n]
    send_ref, keep_ref = refs[n : n + 2]
    basis, projected, result, sem = refs[n + 2 :]
    chips = n // 2
    width = basis.shape[2]
    me = me_ref[0]

    for other in range(2):
        for at, piece in zip(begun, pieces[other * chips : (other + 1) * chips]):
            pltpu.make_async_copy(piece, basis.at[at, other], sem.at[at, other]).start()
    projected[...] = jnp.zeros_like(projected)

    @pl.loop(0, chips)
    def _(at):
        total = projected[...]
        for other in range(2):
            source = ring_source(me, at, other, chips)
            columns = pl.ds(pl.multiple_of(source * width, width), width)
            place = basis.at[at, other]
            pltpu.make_async_copy(place, place, sem.at[at, other]).wait()
            total += jnp.dot(
                scaled_ref[:, columns], basis[at, other], preferred_element_type=jnp.float32
            )
        projected[...] = total

    result[...] = scale * jnp.dot(
        window_ref[...], projected[...].astype(jnp.bfloat16), preferred_element_type=jnp.float32
    )
    rows = keep_ref.shape[1]
    core = lax.rem(me, 2)
    for k in range(chips):
        mine = pl.ds(pl.multiple_of((2 * k + core) * rows, rows), rows)
        keep_ref[k] = result[mine, :]
        other = pl.ds(pl.multiple_of((2 * k + 1 - core) * rows, rows), rows)
        send_ref[k] = result[other, :].astype(jnp.bfloat16)


def add_core_kernel(keep_ref, got_ref, out_ref):
    out_ref[...] = (keep_ref[...] + got_ref[...].astype(jnp.float32)).astype(jnp.bfloat16)


def add_chips_kernel(parts_ref, out_ref):
    out_ref[...] = jnp.sum(parts_ref[...].astype(jnp.float32), axis=0)


VMEM = pl.BlockSpec(memory_space=pltpu.VMEM)
SMEM = pl.BlockSpec(memory_space=pltpu.SMEM)
ANY = pl.BlockSpec(memory_space=pl.ANY)


def after(first, *others):
    return lax.optimization_barrier((first, *others))


def ring_body(n, grad_out, activations, basis_out, basis_in, eigenvalues, tile_order, block_map):
    tok_rows, full_out = grad_out.shape
    tile_width = basis_out.shape[1]
    full_in, in_width = basis_in.shape
    tokens = n * tok_rows
    chips = n // 2
    me = lax.axis_index("blk").reshape(1)
    to_right = lambda x: lax.ppermute(x, "blk", shift_pairs(n, 1))
    to_left = lambda x: lax.ppermute(x, "blk", shift_pairs(n, -1))

    both = jnp.concatenate([grad_out, activations], axis=1)[None]
    own = basis_in[:WC].T
    right, left = [own], [own]
    steps = chips // 2
    key = n // 2
    while key > 1:
        got = lax.ppermute(both, "blk", xor_pairs(n, key))
        if key <= 4 and len(right) < steps - 1:
            right.append(to_right(right[-1]))
            left.append(to_left(left[-1]))
            got, right[-1], left[-1] = after(got, right[-1], left[-1])
        both = jnp.concatenate([both, got], axis=0)
        key //= 2
    while len(right) < steps - 1:
        right.append(to_right(right[-1]))
        left.append(to_left(left[-1]))
    both = both.reshape(tokens // 2, full_out + full_in)
    both_far = swap(both, n)

    parts = 4
    rotated = pl.pallas_call(
        functools.partial(rotate_in_kernel, tok_rows, full_out),
        out_shape=jax.ShapeDtypeStruct((chips, tokens, in_width), jnp.bfloat16),
        in_specs=[SMEM, VMEM, VMEM, ANY],
        out_specs=VMEM,
        scratch_shapes=[
            pltpu.VMEM((parts, full_in // parts, in_width), jnp.bfloat16),
            pltpu.SemaphoreType.DMA((parts,)),
        ],
        compiler_params=pltpu.CompilerParams(vmem_limit_bytes=16 * MIB),
        name="rotate_in",
    )(me, both, both_far, basis_in)
    near = right[:-1] + left[1:-1]
    far = [swap(piece, n) for piece in near]
    both, both_far, rotated, right[-1], left[-1], *far = after(
        both, both_far, rotated, right[-1], left[-1], *far
    )
    late = [right[-1], left[-1]]
    rotated = plane_exchange(rotated, n)
    while len(right) < steps:
        right.append(to_right(right[-1]))
        left.append(to_left(left[-1]))

    depth = 1024
    aligned = pl.pallas_call(
        functools.partial(rotate_out_kernel, tok_rows),
        out_shape=jax.ShapeDtypeStruct((tile_width, tokens), jnp.bfloat16),
        in_specs=[SMEM, SMEM, VMEM, VMEM, ANY],
        out_specs=VMEM,
        scratch_shapes=[
            pltpu.VMEM((full_out // depth, depth, tile_width), jnp.bfloat16),
            pltpu.VMEM((tokens, tile_width), jnp.float32),
            pltpu.SemaphoreType.DMA((full_out // depth,)),
        ],
        compiler_params=pltpu.CompilerParams(vmem_limit_bytes=40 * MIB),
        cost_estimate=pl.CostEstimate(
            flops=2 * tokens * full_out * tile_width,
            bytes_accessed=2 * full_out * tile_width,
            transcendentals=0,
        ),
        name="rotate_out",
    )(me, block_map, both, both_far, basis_out)

    aligned, rotated, right[-1], left[-1] = after(aligned, rotated, right[-1], left[-1])
    rotated_far = swap(rotated, n)
    near += late
    late = [swap(piece, n) for piece in late]
    aligned, rotated_far, *late = after(aligned, rotated_far, *late)
    far += late
    late = [right[-1], left[-1], to_right(right[-1])]
    blocks = 8
    scaled = pl.pallas_call(
        scale_kernel,
        out_shape=jax.ShapeDtypeStruct((tile_width, full_in), jnp.bfloat16),
        in_specs=[SMEM, SMEM, VMEM, VMEM, VMEM, ANY],
        out_specs=VMEM,
        scratch_shapes=[
            pltpu.VMEM((blocks, tile_width // blocks, full_in), jnp.float32),
            pltpu.SemaphoreType.DMA((blocks,)),
        ],
        compiler_params=pltpu.CompilerParams(vmem_limit_bytes=40 * MIB),
        cost_estimate=pl.CostEstimate(
            flops=2 * tile_width * full_in * tokens,
            bytes_accessed=6 * tile_width * full_in,
            transcendentals=tile_width * full_in,
        ),
        name="scale",
    )(tile_order, me, aligned, rotated, rotated_far, eigenvalues)

    scaled, *late = after(scaled, *late)
    near += late
    far += [swap(piece, n) for piece in late]
    begun = [*range(steps - 2), *range(chips - 1, chips - steps + 2, -1)]
    begun += [steps - 2, chips - steps + 2, steps - 1, chips - steps + 1, steps]

    rows = WR // n
    send, keep = pl.pallas_call(
        functools.partial(window_kernel, n, begun, 1.0 / tokens),
        out_shape=(
            jax.ShapeDtypeStruct((chips, rows, WC), jnp.bfloat16),
            jax.ShapeDtypeStruct((chips, rows, WC), jnp.float32),
        ),
        grid=(1,),
        in_specs=[SMEM, pl.BlockSpec((WR, tile_width), lambda i: (0, 0)), VMEM] + [ANY] * n,
        out_specs=(VMEM, VMEM),
        scratch_shapes=[
            pltpu.VMEM((chips, 2, in_width, WC), jnp.bfloat16),
            pltpu.VMEM((tile_width, WC), jnp.float32),
            pltpu.VMEM((WR, WC), jnp.float32),
            pltpu.SemaphoreType.DMA((chips, 2)),
        ],
        compiler_params=pltpu.CompilerParams(vmem_limit_bytes=36 * MIB),
        cost_estimate=pl.CostEstimate(
            flops=2 * tile_width * full_in * WC + 2 * WR * tile_width * WC,
            bytes_accessed=2 * tile_width * full_in + 2 * WC * full_in,
            transcendentals=0,
        ),
        name="window",
    )(me, basis_out, scaled, *near, *far)

    summed = pl.pallas_call(
        add_core_kernel,
        out_shape=jax.ShapeDtypeStruct((chips, rows, WC), jnp.bfloat16),
        in_specs=[VMEM, VMEM],
        out_specs=VMEM,
        compiler_params=pltpu.CompilerParams(vmem_limit_bytes=8 * MIB),
        name="add_core",
    )(keep, swap(send, n))
    return pl.pallas_call(
        add_chips_kernel,
        out_shape=jax.ShapeDtypeStruct((rows, WC), jnp.float32),
        in_specs=[VMEM],
        out_specs=VMEM,
        compiler_params=pltpu.CompilerParams(vmem_limit_bytes=4 * MIB),
        name="add_chips",
    )(plane_exchange(summed, n))


def gather_body(grad_out, activations, basis_out, basis_in, eigenvalues, tile_order, block_map):
    n_blocks = lax.axis_size("blk")
    tile_width = basis_out.shape[1]
    tok_rows = grad_out.shape[0]
    full_in = eigenvalues.shape[1]
    tokens = n_blocks * tok_rows
    dot = functools.partial(jnp.dot, preferred_element_type=jnp.float32)
    in_rows = lax.all_gather(basis_in[:WC], "blk", axis=1, tiled=True)
    acts = lax.all_gather(activations, "blk", axis=0, tiled=True)
    in_tile = dot(acts, basis_in).astype(jnp.bfloat16)
    rotated_in = lax.all_gather(in_tile, "blk", axis=1, tiled=True)
    grads = lax.all_gather(grad_out, "blk", axis=0, tiled=True)
    rotated_out = dot(grads, basis_out).astype(jnp.bfloat16)
    aligned = jnp.take(
        rotated_out.reshape(n_blocks, tok_rows, tile_width), block_map, axis=0
    ).reshape(tokens, tile_width)
    grad_tile = dot(aligned.T, rotated_in) / tokens
    damped = jnp.take(
        eigenvalues.reshape(tile_width, full_in // LANES, LANES), tile_order, axis=1
    ).reshape(tile_width, full_in)
    scaled = (grad_tile / damped).astype(jnp.bfloat16)
    projected = dot(scaled, in_rows.T).astype(jnp.bfloat16)
    return lax.psum_scatter(
        dot(basis_out[:WR], projected), "blk", scatter_dimension=0, tiled=True
    )


def solution(mesh):
    n = mesh.shape["blk"]

    def body(*args):
        wide = args[3].shape[1] % LANES == 0 and args[2].shape[1] % LANES == 0
        doubles = n & (n - 1) == 0 and args[0].shape[0] & (args[0].shape[0] - 1) == 0
        if wide and doubles and WR % (16 * n) == 0:
            return ring_body(n, *args)
        return gather_body(*args)

    placed = (
        P(("grp", "blk"), None),
        P(("grp", "blk"), None),
        P(None, "blk"),
        P(None, "blk"),
        P("blk", None),
        P(),
        P(),
    )
    return jax.shard_map(
        body, mesh=mesh, in_specs=placed, out_specs=P(("grp", "blk"), None), check_vma=False
    )
```

time: 102 us -> 98.9 us (0.970)
  waiting for transfers between devices: 18.1 us -> 22.1 us
  other arithmetic: 5.93 us -> 2.38 us
  local copies, waits for them, and re-layouts: 6.57 us -> 4.29 us
  starting transfers between devices: 25.6 us -> 24.1 us
    ppermute x10, waiting for transfers between devices: 7.92 us -> 16.5 us  [the longest x4 9.12 us: ring_body(): to_right = lambda x: lax.ppermute(x, 'blk', shift_pairs(n, 1))]
    all_to_all x2 -> x1, waiting for transfers between devices: 6.5 us -> 0.01 us  [plane_exchange(): return lax.all_to_all(x, 'blk', 0, 0, axis_index_groups=planes, tiled=True)]
    all_to_all x2 -> x1, starting transfers between devices: 8.62 us -> 5.16 us  [plane_exchange(): return lax.all_to_all(x, 'blk', 0, 0, axis_index_groups=planes, tiled=True)]
    pallas_call x1, Pallas kernels: 9.57 us -> 6.94 us  [ring_body(): pl.pallas_call(scale_kernel, out_shape=jax.ShapeDtypeStruct((tile_width,...]
    ppermute x10, starting transfers between devices: 14.1 us -> 16.5 us  [the longest x3 8.33 us: ring_body(): got = lax.ppermute(both, 'blk', xor_pairs(n, key))]
    pallas_call x3, Pallas kernels: 18.5 us -> 21 us  [the longest x1 9.74 us: ring_body(): pl.pallas_call(functools.partial(rotate_out_kernel, tok_rows), out_shape=...]
    concatenate x3, other arithmetic: 3.61 us -> 1.47 us  [ring_body(): both = jnp.concatenate([both, got], axis=0)]
    broadcast_in_dim x2 -> x0, local copies, waits for them, and re-layouts: 2.11 us -> none  [plane_gather(): return plane_exchange(jnp.broadcast_to(x[None], (n // 2, *x.shape)), n)]
  transfers between devices with their start and end apart: 24 -> 22, of which waited for: 8 -> 9; matrix products, arithmetic and copies ran while one was open for 10% -> 1% of each run, Pallas kernels for 19% -> 19%
where the time goes in v4:
time: 98.9 us; the launch traced here: 98.5 us
  Pallas kernels  28.7 us (29%)
  starting transfers between devices  24.1 us (24%)
  waiting for transfers between devices  22.1 us (22%)
  blocking collectives  16.7 us (17%)
  local copies, waits for them, and re-layouts  4.29 us (4%)
  other arithmetic  2.38 us (2%)
    all_to_all x1, blocking collectives, plane_exchange(): return lax.all_to_all(x, 'blk', 0, 0, axis_index_groups=planes, tiled=True)  16.7 us
    pallas_call x1, Pallas kernels, ring_body(): pl.pallas_call(functools.partial(rotate_out_kernel, tok_rows), out_shape=...  9.74 us
    pallas_call x1, Pallas kernels, ring_body(): pl.pallas_call(functools.partial(window_kernel, n, begun, 1.0 / tokens),...  9.47 us
    ppermute x4, waiting for transfers between devices, ring_body(): to_right = lambda x: lax.ppermute(x, 'blk', shift_pairs(n, 1))  9.12 us
    ppermute x3, starting transfers between devices, ring_body(): got = lax.ppermute(both, 'blk', xor_pairs(n, key))  8.33 us
    ppermute x3, waiting for transfers between devices, ring_body(): got = lax.ppermute(both, 'blk', xor_pairs(n, key))  7.35 us
    pallas_call x1, Pallas kernels, ring_body(): pl.pallas_call(scale_kernel, out_shape=jax.ShapeDtypeStruct((tile_width,...  6.94 us
    ppermute x11, waiting for transfers between devices, swap(): return lax.ppermute(x, 'blk', xor_pairs(n, 1))  5.63 us
  transfers between devices with their start and end apart: 22, of which 9 were waited for; matrix products, arithmetic and copies ran while one was open for 1% of the time, Pallas kernels for 19%

profile of v4, /device:TPU:0, one launch (start us, length us, event | category | flops | bytes accessed | tf_op | source)
XLA Modules:
  0.0 98.5 jit_solution(2056998386646884650)
XLA Ops:
  0.0 0.9 maximum_bitcast_fusion
  0.9 4.1 %collective-permute-start = (bf16[1,2,18432]{2,1,0:T(2,128)(2,1)S(1)}, bf16[1,2,18432]{2,1,0:T(2,128)(2,1)S(1)}, u32[]{:S(2)}, u32[]{:S(2)}) collective-permute-start(bf16[1,2,18432]{2,1,0:T(2,128)(2,1)S(1)} %maximum_bitcast_fusion), channel_id=1, source_target_pairs={{0,8},{1,9},{2,10},{3,11},{4,12},{5,13},{6,14},{7,15},{8,0},{9,1},... | collective-permute-start | bytes 221192 | tf_op jit(solution)/shard_map/ppermute | solution.py:235
  5.0 1.0 slice.3
  6.1 1.6 %collective-permute-start.3 = (bf16[256,512]{1,0:T(8,128)(2,1)S(1)}, bf16[256,512]{1,0:T(8,128)(2,1)S(1)}, u32[]{:S(2)}, u32[]{:S(2)}) collective-permute-start(bf16[256,512]{1,0:T(8,128)(2,1)S(1)} %bitcast.4), channel_id=1, source_target_pairs={{0,2},{1,3},{4,0},{5,1},{8,4},{9,5},{12,8},{13,9},{14,12},{15,13},... | collective-permute-start | bytes 786440 | tf_op jit(solution)/shard_map/ppermute | solution.py:227
  8.7 1.4 %collective-permute-start.1 = (bf16[2,2,18432]{2,1,0:T(2,128)(2,1)S(1)}, bf16[2,2,18432]{2,1,0:T(2,128)(2,1)S(1)}, u32[]{:S(2)}, u32[]{:S(2)}) collective-permute-start(bf16[2,2,18432]{2,1,0:T(2,128)(2,1)S(1)} %pad_maximum_fusion.2), channel_id=1, source_target_pairs={{0,4},{1,5},{2,6},{3,7},{4,0},{5,1},{6,2},{7,3},{8,12},{9,13},{10,... | collective-permute-start | bytes 442376 | tf_op jit(solution)/shard_map/ppermute | solution.py:235
  10.2 7.0 %collective-permute-done.1 = bf16[2,2,18432]{2,1,0:T(2,128)(2,1)S(1)} collective-permute-done((bf16[2,2,18432]{2,1,0:T(2,128)(2,1)S(1)}, bf16[2,2,18432]{2,1,0:T(2,128)(2,1)S(1)}, u32[]{:S(2)}, u32[]{:S(2)}) %collective-permute-start.1) | collective-permute-done | bytes 147488 | tf_op jit(solution)/shard_map/ppermute | solution.py:235
  17.6 2.8 %collective-permute-start.4 = (bf16[4,2,18432]{2,1,0:T(2,128)(2,1)S(1)}, bf16[4,2,18432]{2,1,0:T(2,128)(2,1)S(1)}, u32[]{:S(2)}, u32[]{:S(2)}) collective-permute-start(bf16[4,2,18432]{2,1,0:T(2,128)(2,1)S(1)} %pad_maximum_fusion.1), channel_id=1, source_target_pairs={{0,2},{1,3},{2,0},{3,1},{4,6},{5,7},{6,4},{7,5},{8,10},{9,11},{10,... | collective-permute-start | bytes 884744 | tf_op jit(solution)/shard_map/ppermute | solution.py:235
  20.7 1.7 %collective-permute-start.6 = (bf16[256,512]{1,0:T(8,128)(2,1)S(1)}, bf16[256,512]{1,0:T(8,128)(2,1)S(1)}, u32[]{:S(2)}, u32[]{:S(2)}) collective-permute-start(bf16[256,512]{1,0:T(8,128)(2,1)S(1)} %collective-permute-done.3.refs_2_), channel_id=1, source_target_pairs={{0,2},{1,3},{4,0},{5,1},{8,4},{9,5},{12,8},{13,9},{14,12},{15,13},... | collective-permute-start | bytes 786440 | tf_op jit(solution)/shard_map/ppermute | solution.py:227
  22.5 9.1 %collective-permute-done.5.refs_3_ = bf16[256,512]{1,0:T(8,128)(2,1)S(1)} collective-permute-done((bf16[256,512]{1,0:T(8,128)(2,1)S(1)}, bf16[256,512]{1,0:T(8,128)(2,1)S(1)}, u32[]{:S(2)}, u32[]{:S(2)}) %collective-permute-start.5) | collective-permute-done | bytes 262176 | tf_op jit(solution)/shard_map/ppermute | solution.py:226
  31.6 0.8 pad_maximum_fusion
  33.7 1.0 collective-permute-done.7.far_ref
  34.7 1.6 %copy-done = bf16[4096,256]{1,0:T(8,128)(2,1)S(1)} copy-done((bf16[4096,256]{1,0:T(8,128)(2,1)S(1)}, bf16[4096,256]{1,0:T(8,128)(2,1)}, u32[]{:S(2)}) %copy-start) | copy-done | bytes 2097176
  36.3 1.8 %rotate_in.1 = bf16[8,32,256]{2,1,0:T(8,128)(2,1)} custom-call(s32[1]{0:T(128)} %bitcast.me_ref, bf16[16,18432]{1,0:T(8,128)(2,1)S(1)} %reshape.7.near_ref, bf16[16,18432]{1,0:T(8,128)(2,1)S(1)} %collective-permute-done.7.far_ref, bf16[4096,256]{1,0:T(8,128)(2,1)S(1)} %copy-done), custom_call_target="tpu_custom_call" | custom-call | tf_op jit(solution)/shard_map/rotate_in/pallas_call | solution.py:249
  38.1 0.7 copy-done.1
  38.9 2.0 %collective-permute-start.12 = (bf16[256,512]{1,0:T(8,128)(2,1)S(1)}, bf16[256,512]{1,0:T(8,128)(2,1)}, u32[]{:S(2)}, u32[]{:S(2)}) collective-permute-start(bf16[256,512]{1,0:T(8,128)(2,1)S(1)} %collective-permute-done.6.refs_4_), channel_id=1, source_target_pairs={{0,2},{1,3},{4,0},{5,1},{8,4},{9,5},{12,8},{13,9},{14,12},{15,13},... | collective-permute-start | bytes 786440 | tf_op jit(solution)/shard_map/ppermute | solution.py:227
  40.9 5.2 %all-to-all-start = ((bf16[8,32,256]{2,1,0:T(8,128)(2,1)}), bf16[8,32,256]{2,1,0:T(8,128)(2,1)S(1)}, u32[]{:S(2)}, u32[]{:S(2)}) async-start(bf16[8,32,256]{2,1,0:T(8,128)(2,1)} %rotate_in.1), calls=%async_computation | async-start | bytes 262144 | tf_op jit(solution)/shard_map/all_to_all | solution.py:48
  47.2 9.7 %rotate_out.1.aligned_ref = bf16[896,32]{1,0:T(8,128)(2,1)S(1)} custom-call(s32[1]{0:T(128)} %bitcast.me_ref, s32[16]{0:T(128)S(1)} %copy-done.3, bf16[16,18432]{1,0:T(8,128)(2,1)S(1)} %reshape.7.near_ref, bf16[16,18432]{1,0:T(8,128)(2,1)S(1)} %collective-permute-done.7.far_ref, bf16[14336,896]{1,0:T(8,128)(2,1)} %window_ref.1), custom_call_target="tpu_custom_call" | custom-call | flops 822083584 | bytes 25690112 | tf_op jit(solution)/shard_map/rotate_out/pallas_call | solution.py:273
  57.0 2.1 %collective-permute-start.16 = (bf16[256,512]{1,0:T(8,128)(2,1)}, bf16[256,512]{1,0:T(8,128)(2,1)S(1)}, u32[]{:S(2)}, u32[]{:S(2)}) collective-permute-start(bf16[256,512]{1,0:T(8,128)(2,1)} %collective-permute-done.11.refs_5_), channel_id=1, source_target_pairs={{0,4},{1,5},{4,8},{5,9},{8,12},{9,13},{12,14},{13,15},{14,10},{15,... | collective-permute-start | bytes 786440 | tf_op jit(solution)/shard_map/ppermute | solution.py:226
  59.1 1.3 %collective-permute-done.13.far_ref = bf16[8,32,256]{2,1,0:T(8,128)(2,1)S(1)} collective-permute-done((bf16[8,32,256]{2,1,0:T(8,128)(2,1)S(1)}, bf16[8,32,256]{2,1,0:T(8,128)(2,1)S(1)}, u32[]{:S(2)}, u32[]{:S(2)}) %collective-permute-start.13) | collective-permute-done | bytes 131104 | tf_op jit(solution)/shard_map/ppermute | solution.py:43
  60.4 6.9 %scale.1.scaled_ref = bf16[896,4096]{1,0:T(8,128)(2,1)S(1)} custom-call(s32[32]{0:T(128)S(1)} %copy-done.4, s32[1]{0:T(128)} %bitcast.me_ref, bf16[896,32]{1,0:T(8,128)(2,1)S(1)} %rotate_out.1.aligned_ref, bf16[8,32,256]{2,1,0:T(8,128)(2,1)S(1)} %all-to-all-done.near_ref, bf16[8,32,256]{2,1,0:T(8,128)(2,1)S(1)} %collective-permute-done.13.far_ref, ...), custom_call_target="tpu_custom_call" | custom-call | flops 234881024 | bytes 22020096 | tf_op jit(solution)/shard_map/scale/pallas_call | solution.py:300
  68.1 1.1 %collective-permute-done.17.refs_13_ = bf16[256,512]{1,0:T(8,128)(2,1)S(1)} collective-permute-done((bf16[256,512]{1,0:T(8,128)(2,1)}, bf16[256,512]{1,0:T(8,128)(2,1)S(1)}, u32[]{:S(2)}, u32[]{:S(2)}) %collective-permute-start.17) | collective-permute-done | bytes 262176 | tf_op jit(solution)/shard_map/ppermute | solution.py:43
  69.7 9.5 %window.1 = (bf16[8,48,512]{2,1,0:T(8,128)(2,1)S(1)}, f32[8,48,512]{2,1,0:T(8,128)S(1)}) custom-call(s32[1]{0:T(128)} %bitcast.me_ref, bf16[14336,896]{1,0:T(8,128)(2,1)} %window_ref.1, bf16[896,4096]{1,0:T(8,128)(2,1)S(1)} %scale.1.scaled_ref, bf16[256,512]{1,0:T(8,128)(2,1)S(1)} %bitcast.7, bf16[256,512]{1,0:T(8,128)(2,1)S(1)} %collective-permute-done.2.refs_1_, ...), custom_call_target="tpu_custom_call" | custom-call | flops 4462739456 | bytes 11534336 | tf_op jit(solution)/shard_map/window/pallas_call | solution.py:325
  79.3 1.7 %collective-permute-done.20.got_ref = bf16[8,48,512]{2,1,0:T(8,128)(2,1)S(1)} collective-permute-done((bf16[8,48,512]{2,1,0:T(8,128)(2,1)S(1)}, bf16[8,48,512]{2,1,0:T(8,128)(2,1)S(1)}, u32[]{:S(2)}, u32[]{:S(2)}) %collective-permute-start.20) | collective-permute-done | bytes 393248 | tf_op jit(solution)/shard_map/ppermute | solution.py:43
  81.1 16.7 %all_to_all.10.parts_ref = bf16[8,48,512]{2,1,0:T(8,128)(2,1)S(1)} all-to-all(bf16[8,48,512]{2,1,0:T(8,128)(2,1)S(1)} %add_core.1), channel_id=1, replica_groups={{0,2,4,6,8,10,12,14},{1,3,5,7,9,11,13,15},{16,18,20,22,24,26,28,30},{17..., dimensions={0} | all-to-all | bytes 786432 | tf_op jit(solution)/shard_map/all_to_all | solution.py:48
  (44 shorter events, 6.6 us)
Async XLA Ops:
  0.9 7.6 %collective-permute-start = (bf16[1,2,18432]{2,1,0:T(2,128)(2,1)S(1)}, bf16[1,2,18432]{2,1,0:T(2,128)(2,1)S(1)}, u32[]{:S(2)}, u32[]{:S(2)}) collective-permute-start(bf16[1,2,18432]{2,1,0:T(2,128)(2,1)S(1)} %maximum_bitcast_fusion), channel_id=1, source_target_pairs={{0,8},{1,9},{2,10},{3,11},{4,12},{5,13},{6,14},{7,15},{8,0},{9,1},... | collective-permute-start | bytes 221192 | tf_op jit(solution)/shard_map/ppermute | solution.py:235
  6.1 11.1 %collective-permute-start.3 = (bf16[256,512]{1,0:T(8,128)(2,1)S(1)}, bf16[256,512]{1,0:T(8,128)(2,1)S(1)}, u32[]{:S(2)}, u32[]{:S(2)}) collective-permute-start(bf16[256,512]{1,0:T(8,128)(2,1)S(1)} %bitcast.4), channel_id=1, source_target_pairs={{0,2},{1,3},{4,0},{5,1},{8,4},{9,5},{12,8},{13,9},{14,12},{15,13},... | collective-permute-start | bytes 786440 | tf_op jit(solution)/shard_map/ppermute | solution.py:227
  7.7 9.5 %collective-permute-start.2 = (bf16[256,512]{1,0:T(8,128)(2,1)S(1)}, bf16[256,512]{1,0:T(8,128)(2,1)S(1)}, u32[]{:S(2)}, u32[]{:S(2)}) collective-permute-start(bf16[256,512]{1,0:T(8,128)(2,1)S(1)} %bitcast.5), channel_id=1, source_target_pairs={{0,4},{1,5},{4,8},{5,9},{8,12},{9,13},{12,14},{13,15},{14,10},{15,... | collective-permute-start | bytes 786440 | tf_op jit(solution)/shard_map/ppermute | solution.py:226
  8.7 8.5 %collective-permute-start.1 = (bf16[2,2,18432]{2,1,0:T(2,128)(2,1)S(1)}, bf16[2,2,18432]{2,1,0:T(2,128)(2,1)S(1)}, u32[]{:S(2)}, u32[]{:S(2)}) collective-permute-start(bf16[2,2,18432]{2,1,0:T(2,128)(2,1)S(1)} %pad_maximum_fusion.2), channel_id=1, source_target_pairs={{0,4},{1,5},{2,6},{3,7},{4,0},{5,1},{6,2},{7,3},{8,12},{9,13},{10,... | collective-permute-start | bytes 442376 | tf_op jit(solution)/shard_map/ppermute | solution.py:235
  17.6 13.9 %collective-permute-start.4 = (bf16[4,2,18432]{2,1,0:T(2,128)(2,1)S(1)}, bf16[4,2,18432]{2,1,0:T(2,128)(2,1)S(1)}, u32[]{:S(2)}, u32[]{:S(2)}) collective-permute-start(bf16[4,2,18432]{2,1,0:T(2,128)(2,1)S(1)} %pad_maximum_fusion.1), channel_id=1, source_target_pairs={{0,2},{1,3},{2,0},{3,1},{4,6},{5,7},{6,4},{7,5},{8,10},{9,11},{10,... | collective-permute-start | bytes 884744 | tf_op jit(solution)/shard_map/ppermute | solution.py:235
  20.4 11.1 %collective-permute-start.5 = (bf16[256,512]{1,0:T(8,128)(2,1)S(1)}, bf16[256,512]{1,0:T(8,128)(2,1)S(1)}, u32[]{:S(2)}, u32[]{:S(2)}) collective-permute-start(bf16[256,512]{1,0:T(8,128)(2,1)S(1)} %collective-permute-done.2.refs_1_), channel_id=1, source_target_pairs={{0,4},{1,5},{4,8},{5,9},{8,12},{9,13},{12,14},{13,15},{14,10},{15,... | collective-permute-start | bytes 786440 | tf_op jit(solution)/shard_map/ppermute | solution.py:226
  20.7 10.9 %collective-permute-start.6 = (bf16[256,512]{1,0:T(8,128)(2,1)S(1)}, bf16[256,512]{1,0:T(8,128)(2,1)S(1)}, u32[]{:S(2)}, u32[]{:S(2)}) collective-permute-start(bf16[256,512]{1,0:T(8,128)(2,1)S(1)} %collective-permute-done.3.refs_2_), channel_id=1, source_target_pairs={{0,2},{1,3},{4,0},{5,1},{8,4},{9,5},{12,8},{13,9},{14,12},{15,13},... | collective-permute-start | bytes 786440 | tf_op jit(solution)/shard_map/ppermute | solution.py:227
  32.6 2.1 %collective-permute-start.7 = (bf16[16,18432]{1,0:T(8,128)(2,1)S(1)}, bf16[16,18432]{1,0:T(8,128)(2,1)S(1)}, u32[]{:S(2)}, u32[]{:S(2)}) collective-permute-start(bf16[16,18432]{1,0:T(8,128)(2,1)S(1)} %reshape.7.near_ref), channel_id=1, source_target_pairs={{0,1},{1,0},{2,3},{3,2},{4,5},{5,4},{6,7},{7,6},{8,9},{9,8},{10,11... | collective-permute-start | bytes 1769480 | tf_op jit(solution)/shard_map/ppermute | solution.py:43
  32.7 5.4 %collective-permute-start.8 = (bf16[256,512]{1,0:T(8,128)(2,1)S(1)}, bf16[256,512]{1,0:T(8,128)(2,1)S(1)}, u32[]{:S(2)}, u32[]{:S(2)}) collective-permute-start(bf16[256,512]{1,0:T(8,128)(2,1)S(1)} %bitcast.6), channel_id=1, source_target_pairs={{0,1},{1,0},{2,3},{3,2},{4,5},{5,4},{6,7},{7,6},{8,9},{9,8},{10,11... | collective-permute-start | bytes 786440 | tf_op jit(solution)/shard_map/ppermute | solution.py:43
  33.2 4.9 %collective-permute-start.9 = (bf16[256,512]{1,0:T(8,128)(2,1)S(1)}, bf16[256,512]{1,0:T(8,128)(2,1)S(1)}, u32[]{:S(2)}, u32[]{:S(2)}) collective-permute-start(bf16[256,512]{1,0:T(8,128)(2,1)S(1)} %collective-permute-done.2.refs_1_), channel_id=1, source_target_pairs={{0,1},{1,0},{2,3},{3,2},{4,5},{5,4},{6,7},{7,6},{8,9},{9,8},{10,11... | collective-permute-start | bytes 786440 | tf_op jit(solution)/shard_map/ppermute | solution.py:43
  33.3 4.8 %collective-permute-start.10 = (bf16[256,512]{1,0:T(8,128)(2,1)S(1)}, bf16[256,512]{1,0:T(8,128)(2,1)S(1)}, u32[]{:S(2)}, u32[]{:S(2)}) collective-permute-start(bf16[256,512]{1,0:T(8,128)(2,1)S(1)} %collective-permute-done.3.refs_2_), channel_id=1, source_target_pairs={{0,1},{1,0},{2,3},{3,2},{4,5},{5,4},{6,7},{7,6},{8,9},{9,8},{10,11... | collective-permute-start | bytes 786440 | tf_op jit(solution)/shard_map/ppermute | solution.py:43
  36.3 24.1 %copy-start.4 = (s32[32]{0:T(128)S(1)}, s32[32]{0:T(128)}, u32[]{:S(2)}) copy-start(s32[32]{0:T(128)} %tiles_ref.1) | copy-start | bytes 388
  38.9 18.1 %collective-permute-start.11 = (bf16[256,512]{1,0:T(8,128)(2,1)S(1)}, bf16[256,512]{1,0:T(8,128)(2,1)}, u32[]{:S(2)}, u32[]{:S(2)}) collective-permute-start(bf16[256,512]{1,0:T(8,128)(2,1)S(1)} %collective-permute-done.5.refs_3_), channel_id=1, source_target_pairs={{0,4},{1,5},{4,8},{5,9},{8,12},{9,13},{12,14},{13,15},{14,10},{15,... | collective-permute-start | bytes 786440 | tf_op jit(solution)/shard_map/ppermute | solution.py:226
  38.9 18.1 %collective-permute-start.12 = (bf16[256,512]{1,0:T(8,128)(2,1)S(1)}, bf16[256,512]{1,0:T(8,128)(2,1)}, u32[]{:S(2)}, u32[]{:S(2)}) collective-permute-start(bf16[256,512]{1,0:T(8,128)(2,1)S(1)} %collective-permute-done.6.refs_4_), channel_id=1, source_target_pairs={{0,2},{1,3},{4,0},{5,1},{8,4},{9,5},{12,8},{13,9},{14,12},{15,13},... | collective-permute-start | bytes 786440 | tf_op jit(solution)/shard_map/ppermute | solution.py:227
  40.9 16.1 %all-to-all-start = ((bf16[8,32,256]{2,1,0:T(8,128)(2,1)}), bf16[8,32,256]{2,1,0:T(8,128)(2,1)S(1)}, u32[]{:S(2)}, u32[]{:S(2)}) async-start(bf16[8,32,256]{2,1,0:T(8,128)(2,1)} %rotate_in.1), calls=%async_computation | async-start | bytes 262144 | tf_op jit(solution)/shard_map/all_to_all | solution.py:48
  46.0 13.0 %collective-permute-start.14 = (bf16[256,512]{1,0:T(8,128)(2,1)S(1)}, bf16[256,512]{1,0:T(8,128)(2,1)}, u32[]{:S(2)}, u32[]{:S(2)}) collective-permute-start(bf16[256,512]{1,0:T(8,128)(2,1)S(1)} %collective-permute-done.5.refs_3_), channel_id=1, source_target_pairs={{0,1},{1,0},{2,3},{3,2},{4,5},{5,4},{6,7},{7,6},{8,9},{9,8},{10,11... | collective-permute-start | bytes 786440 | tf_op jit(solution)/shard_map/ppermute | solution.py:43
  46.0 13.0 %collective-permute-start.15 = (bf16[256,512]{1,0:T(8,128)(2,1)S(1)}, bf16[256,512]{1,0:T(8,128)(2,1)}, u32[]{:S(2)}, u32[]{:S(2)}) collective-permute-start(bf16[256,512]{1,0:T(8,128)(2,1)S(1)} %collective-permute-done.6.refs_4_), channel_id=1, source_target_pairs={{0,1},{1,0},{2,3},{3,2},{4,5},{5,4},{6,7},{7,6},{8,9},{9,8},{10,11... | collective-permute-start | bytes 786440 | tf_op jit(solution)/shard_map/ppermute | solution.py:43
  57.0 12.8 %copy-start.2 = (bf16[256,512]{1,0:T(8,128)(2,1)S(1)}, bf16[256,512]{1,0:T(8,128)(2,1)}, u32[]{:S(2)}) copy-start(bf16[256,512]{1,0:T(8,128)(2,1)} %copy-done.1) | copy-start | bytes 786436
  57.0 10.4 %collective-permute-start.16 = (bf16[256,512]{1,0:T(8,128)(2,1)}, bf16[256,512]{1,0:T(8,128)(2,1)S(1)}, u32[]{:S(2)}, u32[]{:S(2)}) collective-permute-start(bf16[256,512]{1,0:T(8,128)(2,1)} %collective-permute-done.11.refs_5_), channel_id=1, source_target_pairs={{0,4},{1,5},{4,8},{5,9},{8,12},{9,13},{12,14},{13,15},{14,10},{15,... | collective-permute-start | bytes 786440 | tf_op jit(solution)/shard_map/ppermute | solution.py:226
  59.1 1.3 %collective-permute-start.13 = (bf16[8,32,256]{2,1,0:T(8,128)(2,1)S(1)}, bf16[8,32,256]{2,1,0:T(8,128)(2,1)S(1)}, u32[]{:S(2)}, u32[]{:S(2)}) collective-permute-start(bf16[8,32,256]{2,1,0:T(8,128)(2,1)S(1)} %all-to-all-done.near_ref), channel_id=1, source_target_pairs={{0,1},{1,0},{2,3},{3,2},{4,5},{5,4},{6,7},{7,6},{8,9},{9,8},{10,11... | collective-permute-start | bytes 393224 | tf_op jit(solution)/shard_map/ppermute | solution.py:43
  67.4 1.8 %collective-permute-start.17 = (bf16[256,512]{1,0:T(8,128)(2,1)}, bf16[256,512]{1,0:T(8,128)(2,1)S(1)}, u32[]{:S(2)}, u32[]{:S(2)}) collective-permute-start(bf16[256,512]{1,0:T(8,128)(2,1)} %collective-permute-done.11.refs_5_), channel_id=1, source_target_pairs={{0,1},{1,0},{2,3},{3,2},{4,5},{5,4},{6,7},{7,6},{8,9},{9,8},{10,11... | collective-permute-start | bytes 786440 | tf_op jit(solution)/shard_map/ppermute | solution.py:43
  67.6 2.0 %collective-permute-start.18 = (bf16[256,512]{1,0:T(8,128)(2,1)}, bf16[256,512]{1,0:T(8,128)(2,1)S(1)}, u32[]{:S(2)}, u32[]{:S(2)}) collective-permute-start(bf16[256,512]{1,0:T(8,128)(2,1)} %collective-permute-done.12.refs_6_), channel_id=1, source_target_pairs={{0,1},{1,0},{2,3},{3,2},{4,5},{5,4},{6,7},{7,6},{8,9},{9,8},{10,11... | collective-permute-start | bytes 786440 | tf_op jit(solution)/shard_map/ppermute | solution.py:43
  68.0 1.8 %collective-permute-start.19 = (bf16[256,512]{1,0:T(8,128)(2,1)S(1)}, bf16[256,512]{1,0:T(8,128)(2,1)S(1)}, u32[]{:S(2)}, u32[]{:S(2)}) collective-permute-start(bf16[256,512]{1,0:T(8,128)(2,1)S(1)} %collective-permute-done.16.refs_7_), channel_id=1, source_target_pairs={{0,1},{1,0},{2,3},{3,2},{4,5},{5,4},{6,7},{7,6},{8,9},{9,8},{10,11... | collective-permute-start | bytes 786440 | tf_op jit(solution)/shard_map/ppermute | solution.py:43
  79.2 1.8 %collective-permute-start.20 = (bf16[8,48,512]{2,1,0:T(8,128)(2,1)S(1)}, bf16[8,48,512]{2,1,0:T(8,128)(2,1)S(1)}, u32[]{:S(2)}, u32[]{:S(2)}) collective-permute-start(bf16[8,48,512]{2,1,0:T(8,128)(2,1)S(1)} %get-tuple-element.60), channel_id=1, source_target_pairs={{0,1},{1,0},{2,3},{3,2},{4,5},{5,4},{6,7},{7,6},{8,9},{9,8},{10,11... | collective-permute-start | bytes 1179656 | tf_op jit(solution)/shard_map/ppermute | solution.py:43
  (3 other events, 3.0 us)

commit v5 on v4

v5 whole, which is shorter than its diff:
```python
import functools

import jax
import jax.numpy as jnp
from jax import lax
from jax.experimental import pallas as pl
from jax.experimental.pallas import tpu as pltpu
from jax.sharding import PartitionSpec as P

WR = 768
WC = 512
LANES = 128
MIB = 1 << 20


def ring_of(n):
    chips = n // 2
    return [*range(0, chips, 2), *range(chips - 1, 0, -2)]


def shift_pairs(n, by):
    ring = ring_of(n)
    return [
        (2 * ring[p] + c, 2 * ring[(p + by) % len(ring)] + c)
        for p in range(len(ring))
        for c in range(2)
    ]


def ring_source(me, steps, other, chips):
    chip, core = me // 2, lax.rem(me, 2)
    place = jnp.where(lax.rem(chip, 2) == 0, chip // 2, chips - 1 - chip // 2)
    place = lax.rem(place + chips - steps, chips)
    chip = jnp.where(place < chips // 2, 2 * place, 2 * (chips - 1 - place) + 1)
    return 2 * chip + (core ^ other)


def xor_pairs(n, key):
    return [(b, b ^ key) for b in range(n)]


def swap(x, n):
    return lax.ppermute(x, "blk", xor_pairs(n, 1))


def plane_exchange(x, n):
    planes = [list(range(c, n, 2)) for c in range(2)]
    return lax.all_to_all(x, "blk", 0, 0, axis_index_groups=planes, tiled=True)


def bits_of(size):
    return size.bit_length() - 1


def held_tokens(me, tokens, tok_rows):
    row = lax.broadcasted_iota(jnp.int32, (tokens, tokens), 1)
    chips = tokens // tok_rows // 2
    place = (row >> bits_of(tok_rows)) & (chips - 1)
    chip = jnp.zeros_like(row)
    for bit in range(bits_of(chips)):
        chip |= ((place >> bit) & 1) << (bits_of(chips) - 1 - bit)
    other = row >> bits_of(tokens // 2)
    device = me ^ (2 * chip + other)
    return (device << bits_of(tok_rows)) + (row & (tok_rows - 1))


def plane_tokens(me, tokens, tok_rows):
    row = lax.broadcasted_iota(jnp.int32, (tokens, tokens), 1)
    chips = tokens // tok_rows // 2
    chip = (row >> bits_of(tok_rows)) & (chips - 1)
    core = (me & 1) ^ (row >> bits_of(tokens // 2))
    return ((2 * chip + core) << bits_of(tok_rows)) + (row & (tok_rows - 1))


def reorder(wanted, held, rotated):
    order = jnp.where(wanted == held, 1.0, 0.0).astype(jnp.bfloat16)
    return jnp.dot(order, rotated.astype(jnp.bfloat16), preferred_element_type=jnp.float32)


def rotate_in_kernel(tok_rows, scalars_ref, near_ref, far_ref, basis_ref, out_ref):
    tokens = out_ref.shape[1]
    acts = jnp.concatenate([near_ref[...], far_ref[...]], axis=0)
    rotated = jnp.dot(acts, basis_ref[...], preferred_element_type=jnp.float32)
    wanted = lax.broadcasted_iota(jnp.int32, (tokens, tokens), 0)
    ordered = reorder(wanted, plane_tokens(scalars_ref[0], tokens, tok_rows), rotated)
    for copy in range(out_ref.shape[0]):
        out_ref[copy] = ordered.astype(jnp.bfloat16)


def rotate_out_kernel(
    tok_rows, map_at, scalars_ref, near_ref, far_ref, basis_ref, out_ref, basis, total, sem
):
    steps, depth = basis.shape[:2]
    tokens = total.shape[0]

    def copy_of(step):
        rows = pl.ds(pl.multiple_of(step * depth, depth), depth)
        return pltpu.make_async_copy(basis_ref.at[rows], basis.at[step], sem.at[step])

    @pl.loop(0, steps)
    def _(step):
        copy_of(step).start()

    total[...] = jnp.zeros_like(total)

    @pl.loop(0, steps)
    def _(step):
        columns = pl.ds(pl.multiple_of(step * depth, depth), depth)
        grads = jnp.concatenate([near_ref[:, columns], far_ref[:, columns]], axis=0)
        copy_of(step).wait()
        total[...] += jnp.dot(grads, basis[step], preferred_element_type=jnp.float32)

    row = lax.broadcasted_iota(jnp.int32, (tokens, tokens), 0)
    block = row >> bits_of(tok_rows)
    wanted = jnp.zeros_like(row)
    for stored in range(tokens // tok_rows):
        wanted = jnp.where(block == stored, scalars_ref[map_at + stored] * tok_rows, wanted)
    wanted += row & (tok_rows - 1)
    held = held_tokens(scalars_ref[0], tokens, tok_rows)
    out_ref[...] = reorder(wanted, held, total[...]).T.astype(jnp.bfloat16)


def scale_kernel(
    begun, tiles_at, scalars_ref, aligned_ref, near_ref, far_ref, eigen_ref, out_ref, damped, sem
):
    blocks, depth = damped.shape[:2]
    chips, _, width = near_ref.shape

    def copy_of(block):
        rows = pl.ds(pl.multiple_of(block * depth, depth), depth)
        return pltpu.make_async_copy(eigen_ref.at[rows], damped.at[block], sem.at[block])

    @pl.loop(0, blocks)
    def _(block):
        copy_of(block).start()

    @pl.loop(0, blocks)
    def _(block):
        rows = pl.ds(pl.multiple_of(block * depth, depth), depth)
        aligned = aligned_ref[rows, :]
        copy_of(block).wait()
        place = 0
        for steps in begun:
            for other, rotated_ref in enumerate((near_ref, far_ref)):
                source = ring_source(scalars_ref[0], steps, other, chips)
                grad = jnp.dot(
                    aligned, rotated_ref[source // 2], preferred_element_type=jnp.float32
                )
                for first in range(0, width, LANES):
                    tile = scalars_ref[tiles_at + (source * width + first) // LANES]
                    lanes = pl.ds(pl.multiple_of(tile * LANES, LANES), LANES)
                    eigen = damped[block, :, lanes]
                    inverse = pl.reciprocal(eigen, approx=True)
                    inverse = inverse * (2.0 - eigen * inverse)
                    scaled = grad[:, first : first + LANES] * inverse
                    out_ref[rows, place : place + LANES] = scaled.astype(jnp.bfloat16)
                    place += LANES


def project_kernel(cuts, scaled_ref, *refs):
    pieces = refs[:-3]
    out_ref, basis, sem = refs[-3:]
    width = pieces[0].shape[0]
    rows = out_ref.shape[0] // 2
    copies = [
        pltpu.make_async_copy(piece, basis.at[pl.ds(at * width, width)], sem.at[at])
        for at, piece in enumerate(pieces)
    ]
    for copy in copies:
        copy.start()
    for first, last in zip(cuts[:-1], cuts[1:]):
        for copy in copies[first:last]:
            copy.wait()
        deep = slice(first * width, last * width)

        @pl.loop(0, 2)
        def _(half):
            block = pl.ds(pl.multiple_of(half * rows, rows), rows)
            part = jnp.dot(
                scaled_ref[block, deep], basis[deep, :], preferred_element_type=jnp.float32
            )
            out_ref[block, :] = part if first == 0 else out_ref[block, :] + part


def window_kernel(scale, scalars_ref, window_ref, scaled_ref, projected_ref, *refs):
    pieces = refs[:-3]
    send_ref, keep_ref, result = refs[-3:]
    chips, rows, _ = keep_ref.shape
    width = pieces[0].shape[0]
    total = projected_ref[...]
    for at, piece in enumerate(pieces, scaled_ref.shape[1] // width - len(pieces)):
        total += jnp.dot(
            scaled_ref[:, at * width : (at + 1) * width],
            piece[...],
            preferred_element_type=jnp.float32,
        )
    result[...] = scale * jnp.dot(
        window_ref[...], total.astype(jnp.bfloat16), preferred_element_type=jnp.float32
    )
    core = lax.rem(scalars_ref[0], 2)
    for k in range(chips):
        mine = pl.ds(pl.multiple_of((2 * k + core) * rows, rows), rows)
        keep_ref[k] = result[mine, :]
        other = pl.ds(pl.multiple_of((2 * k + 1 - core) * rows, rows), rows)
        send_ref[k] = result[other, :].astype(jnp.bfloat16)


def add_core_kernel(keep_ref, got_ref, out_ref):
    out_ref[...] = (keep_ref[...] + got_ref[...].astype(jnp.float32)).astype(jnp.bfloat16)


def add_chips_kernel(parts_ref, out_ref):
    out_ref[...] = jnp.sum(parts_ref[...].astype(jnp.float32), axis=0)


VMEM = pl.BlockSpec(memory_space=pltpu.VMEM)
SMEM = pl.BlockSpec(memory_space=pltpu.SMEM)
ANY = pl.BlockSpec(memory_space=pl.ANY)


def after(first, *others):
    return lax.optimization_barrier((first, *others))


def ring_body(n, grad_out, activations, basis_out, basis_in, eigenvalues, tile_order, block_map):
    tok_rows, full_out = grad_out.shape
    tile_width = basis_out.shape[1]
    full_in, in_width = basis_in.shape
    tokens = n * tok_rows
    chips = n // 2
    me = lax.axis_index("blk").reshape(1)
    scalars = jnp.concatenate([me, tile_order, block_map])
    to_right = lambda x: lax.ppermute(x, "blk", shift_pairs(n, 1))
    to_left = lambda x: lax.ppermute(x, "blk", shift_pairs(n, -1))
    steps = chips // 2

    own = basis_in[:WC].T

    acts = jnp.broadcast_to(activations[None], (chips, *activations.shape))
    acts = plane_exchange(acts, n).reshape(tokens // 2, full_in)
    rotated = pl.pallas_call(
        functools.partial(rotate_in_kernel, tok_rows),
        out_shape=jax.ShapeDtypeStruct((chips, tokens, in_width), jnp.bfloat16),
        in_specs=[SMEM, VMEM, VMEM, VMEM],
        out_specs=VMEM,
        compiler_params=pltpu.CompilerParams(vmem_limit_bytes=8 * MIB),
        name="rotate_in",
    )(scalars, acts, swap(acts, n), basis_in)
    rotated = plane_exchange(rotated, n)
    rotated_far = swap(rotated, n)

    right, left = [own], [own]
    while len(right) < max(steps - 2, 2):
        right.append(to_right(right[-1]))
        left.append(to_left(left[-1]))

    grads = grad_out[None]
    key = n // 2
    while key > 1:
        got = lax.ppermute(grads, "blk", xor_pairs(n, key))
        if key == 2:
            got, rotated, rotated_far, right[-1], left[-1] = after(
                got, rotated, rotated_far, right[-1], left[-1]
            )
        grads = jnp.concatenate([grads, got], axis=0)
        key //= 2
    grads = grads.reshape(tokens // 2, full_out)
    grads_far = swap(grads, n)
    right.append(to_right(right[-1]))
    left.append(to_left(left[-1]))

    depth = 1024
    aligned = pl.pallas_call(
        functools.partial(rotate_out_kernel, tok_rows, 1 + full_in // LANES),
        out_shape=jax.ShapeDtypeStruct((tile_width, tokens), jnp.bfloat16),
        in_specs=[SMEM, VMEM, VMEM, ANY],
        out_specs=VMEM,
        scratch_shapes=[
            pltpu.VMEM((full_out // depth, depth, tile_width), jnp.bfloat16),
            pltpu.VMEM((tokens, tile_width), jnp.float32),
            pltpu.SemaphoreType.DMA((full_out // depth,)),
        ],
        compiler_params=pltpu.CompilerParams(vmem_limit_bytes=40 * MIB),
        cost_estimate=pl.CostEstimate(
            flops=2 * tokens * full_out * tile_width,
            bytes_accessed=2 * full_out * tile_width,
            transcendentals=0,
        ),
        name="rotate_out",
    )(scalars, grads, grads_far, basis_out)

    aligned, right[-1], left[-1] = after(aligned, right[-1], left[-1])
    right.append(to_right(right[-1]))
    left.append(to_left(left[-1]))
    begun = [0] + [at for step in range(1, steps) for at in (step, chips - step)] + [steps]
    blocks = 8
    scaled = pl.pallas_call(
        functools.partial(scale_kernel, begun, 1),
        out_shape=jax.ShapeDtypeStruct((tile_width, full_in), jnp.bfloat16),
        in_specs=[SMEM, VMEM, VMEM, VMEM, ANY],
        out_specs=VMEM,
        scratch_shapes=[
            pltpu.VMEM((blocks, tile_width // blocks, full_in), jnp.float32),
            pltpu.SemaphoreType.DMA((blocks,)),
        ],
        compiler_params=pltpu.CompilerParams(vmem_limit_bytes=40 * MIB),
        cost_estimate=pl.CostEstimate(
            flops=2 * tile_width * full_in * tokens,
            bytes_accessed=6 * tile_width * full_in,
            transcendentals=tile_width * full_in,
        ),
        name="scale",
    )(scalars, aligned, rotated, rotated_far, eigenvalues)

    scaled, right[-1], left[-1] = after(scaled, right[-1], left[-1])
    last = to_right(right[-1])
    pieces = []
    for at in begun[:-1]:
        near = right[at] if at < steps else left[chips - at]
        pieces += [near, swap(near, n)]
    projected = pl.pallas_call(
        functools.partial(project_kernel, (0, 6, len(pieces))),
        out_shape=jax.ShapeDtypeStruct((tile_width, WC), jnp.float32),
        in_specs=[VMEM] + [ANY] * len(pieces),
        out_specs=VMEM,
        scratch_shapes=[
            pltpu.VMEM((len(pieces) * in_width, WC), jnp.bfloat16),
            pltpu.SemaphoreType.DMA((len(pieces),)),
        ],
        compiler_params=pltpu.CompilerParams(vmem_limit_bytes=24 * MIB),
        cost_estimate=pl.CostEstimate(
            flops=2 * tile_width * full_in * WC,
            bytes_accessed=2 * tile_width * full_in + 2 * WC * full_in,
            transcendentals=0,
        ),
        name="project",
    )(scaled, *pieces)

    projected, last = after(projected, last)
    rows = WR // n
    send, keep = pl.pallas_call(
        functools.partial(window_kernel, 1.0 / tokens),
        out_shape=(
            jax.ShapeDtypeStruct((chips, rows, WC), jnp.bfloat16),
            jax.ShapeDtypeStruct((chips, rows, WC), jnp.float32),
        ),
        grid=(1,),
        in_specs=[SMEM, pl.BlockSpec((WR, tile_width), lambda i: (0, 0))] + [VMEM] * 4,
        out_specs=(VMEM, VMEM),
        scratch_shapes=[pltpu.VMEM((WR, WC), jnp.float32)],
        compiler_params=pltpu.CompilerParams(vmem_limit_bytes=36 * MIB),
        cost_estimate=pl.CostEstimate(
            flops=2 * WR * tile_width * WC,
            bytes_accessed=2 * WR * tile_width + 12 * WR * WC,
            transcendentals=0,
        ),
        name="window",
    )(scalars, basis_out, scaled, projected, last, swap(last, n))

    summed = pl.pallas_call(
        add_core_kernel,
        out_shape=jax.ShapeDtypeStruct((chips, rows, WC), jnp.bfloat16),
        in_specs=[VMEM, VMEM],
        out_specs=VMEM,
        compiler_params=pltpu.CompilerParams(vmem_limit_bytes=8 * MIB),
        name="add_core",
    )(keep, swap(send, n))
    return pl.pallas_call(
        add_chips_kernel,
        out_shape=jax.ShapeDtypeStruct((rows, WC), jnp.float32),
        in_specs=[VMEM],
        out_specs=VMEM,
        compiler_params=pltpu.CompilerParams(vmem_limit_bytes=4 * MIB),
        name="add_chips",
    )(plane_exchange(summed, n))


def gather_body(grad_out, activations, basis_out, basis_in, eigenvalues, tile_order, block_map):
    n_blocks = lax.axis_size("blk")
    tile_width = basis_out.shape[1]
    tok_rows = grad_out.shape[0]
    full_in = eigenvalues.shape[1]
    tokens = n_blocks * tok_rows
    dot = functools.partial(jnp.dot, preferred_element_type=jnp.float32)
    in_rows = lax.all_gather(basis_in[:WC], "blk", axis=1, tiled=True)
    acts = lax.all_gather(activations, "blk", axis=0, tiled=True)
    in_tile = dot(acts, basis_in).astype(jnp.bfloat16)
    rotated_in = lax.all_gather(in_tile, "blk", axis=1, tiled=True)
    grads = lax.all_gather(grad_out, "blk", axis=0, tiled=True)
    rotated_out = dot(grads, basis_out).astype(jnp.bfloat16)
    aligned = jnp.take(
        rotated_out.reshape(n_blocks, tok_rows, tile_width), block_map, axis=0
    ).reshape(tokens, tile_width)
    grad_tile = dot(aligned.T, rotated_in) / tokens
    damped = jnp.take(
        eigenvalues.reshape(tile_width, full_in // LANES, LANES), tile_order, axis=1
    ).reshape(tile_width, full_in)
    scaled = (grad_tile / damped).astype(jnp.bfloat16)
    projected = dot(scaled, in_rows.T).astype(jnp.bfloat16)
    return lax.psum_scatter(
        dot(basis_out[:WR], projected), "blk", scatter_dimension=0, tiled=True
    )


def solution(mesh):
    n = mesh.shape["blk"]

    def body(*args):
        wide = args[3].shape[1] % LANES == 0 and args[2].shape[1] % LANES == 0
        doubles = n & (n - 1) == 0 and args[0].shape[0] & (args[0].shape[0] - 1) == 0
        if wide and doubles and WR % (16 * n) == 0:
            return ring_body(n, *args)
        return gather_body(*args)

    placed = (
        P(("grp", "blk"), None),
        P(("grp", "blk"), None),
        P(None, "blk"),
        P(None, "blk"),
        P("blk", None),
        P(),
        P(),
    )
    return jax.shard_map(
        body, mesh=mesh, in_specs=placed, out_specs=P(("grp", "blk"), None), check_vma=False
    )
```

time: 98.9 us -> 97.2 us (0.983)
  waiting for transfers between devices: 22.1 us -> 17.6 us
  starting transfers between devices: 24.1 us -> 26.3 us
  other arithmetic: 2.38 us -> 4.36 us
  Pallas kernels: 28.7 us -> 27 us
    all_to_all x1 -> x2, waiting for transfers between devices: 0.01 us -> 9.19 us  [plane_exchange(): return lax.all_to_all(x, 'blk', 0, 0, axis_index_groups=planes, tiled=True)]
    ppermute x4, waiting for transfers between devices: 9.12 us -> 2.48 us  [ring_body(): to_right = lambda x: lax.ppermute(x, 'blk', shift_pairs(n, 1))]
    all_to_all x1 -> x2, starting transfers between devices: 5.16 us -> 10.7 us  [plane_exchange(): return lax.all_to_all(x, 'blk', 0, 0, axis_index_groups=planes, tiled=True)]
    ppermute x3, waiting for transfers between devices: 7.35 us -> 2.58 us  [ring_body(): got = lax.ppermute(grads, 'blk', xor_pairs(n, key))]
    ppermute x3, starting transfers between devices: 5.34 us -> 1.92 us  [ring_body(): to_left = lambda x: lax.ppermute(x, 'blk', shift_pairs(n, -1))]
    ppermute x4, starting transfers between devices: 2.86 us -> 5.78 us  [ring_body(): to_right = lambda x: lax.ppermute(x, 'blk', shift_pairs(n, 1))]
    concatenate x3 -> x4, other arithmetic: 1.47 us -> 4.36 us  [the longest x3 3.61 us: ring_body(): grads = jnp.concatenate([grads, got], axis=0)]
    ppermute x3, starting transfers between devices: 8.33 us -> 5.89 us  [ring_body(): got = lax.ppermute(grads, 'blk', xor_pairs(n, key))]
  transfers between devices with their start and end apart: 22 -> 24, of which waited for: 9 -> 8; matrix products, arithmetic and copies ran while one was open for 1% -> 4% of each run, Pallas kernels for 19% -> 24%
where the time goes in v5:
time: 97.2 us; the launch traced here: 96.6 us
  Pallas kernels  27 us (28%)
  starting transfers between devices  26.3 us (27%)
  waiting for transfers between devices  17.6 us (18%)
  blocking collectives  16.9 us (17%)
  local copies, waits for them, and re-layouts  4.36 us (4%)
  other arithmetic  4.36 us (4%)
    all_to_all x1, blocking collectives, plane_exchange(): return lax.all_to_all(x, 'blk', 0, 0, axis_index_groups=planes, tiled=True)  16.9 us
    all_to_all x2, starting transfers between devices, plane_exchange(): return lax.all_to_all(x, 'blk', 0, 0, axis_index_groups=planes, tiled=True)  10.7 us
    pallas_call x1, Pallas kernels, ring_body(): pl.pallas_call(functools.partial(rotate_out_kernel, tok_rows, 1 + full_in...  9.74 us
    all_to_all x2, waiting for transfers between devices, plane_exchange(): return lax.all_to_all(x, 'blk', 0, 0, axis_index_groups=planes, tiled=True)  9.19 us
    pallas_call x1, Pallas kernels, ring_body(): pl.pallas_call(functools.partial(scale_kernel, begun, 1), out_shape=jax.S...  7.2 us
    ppermute x3, starting transfers between devices, ring_body(): got = lax.ppermute(grads, 'blk', xor_pairs(n, key))  5.89 us
    ppermute x4, starting transfers between devices, ring_body(): to_right = lambda x: lax.ppermute(x, 'blk', shift_pairs(n, 1))  5.78 us
    pallas_call x1, Pallas kernels, ring_body(): pl.pallas_call(functools.partial(project_kernel, (0, 6, len(pieces))), ou...  4.49 us
  transfers between devices with their start and end apart: 24, of which 8 were waited for; matrix products, arithmetic and copies ran while one was open for 4% of the time, Pallas kernels for 24%

profile of v5, /device:TPU:0, one launch (start us, length us, event | category | flops | bytes accessed | tf_op | source)
XLA Modules:
  0.0 96.6 jit_solution(11007336856950869786)
XLA Ops:
  0.0 1.4 %broadcast_in_dim.10 = bf16[8,2,4096]{2,1,0:T(2,128)(2,1)} broadcast(bf16[2,4096]{1,0:T(2,128)(2,1)} %param.8), dimensions={1,2} | broadcast | bytes 147456 | tf_op jit(solution)/shard_map/broadcast_in_dim | solution.py:239
  1.4 7.3 %all-to-all-start = ((bf16[8,2,4096]{2,1,0:T(2,128)(2,1)}), bf16[8,2,4096]{2,1,0:T(2,128)(2,1)S(1)}, u32[]{:S(2)}, u32[]{:S(2)}) async-start(bf16[8,2,4096]{2,1,0:T(2,128)(2,1)} %broadcast_in_dim.10), calls=%async_computation | async-start | bytes 262144 | tf_op jit(solution)/shard_map/all_to_all | solution.py:48
  8.7 2.9 %collective-permute-start = (bf16[1,2,14336]{2,1,0:T(2,128)(2,1)}, bf16[1,2,14336]{2,1,0:T(2,128)(2,1)S(1)}, u32[]{:S(2)}, u32[]{:S(2)}) collective-permute-start(bf16[1,2,14336]{2,1,0:T(2,128)(2,1)} %bitcast.7), channel_id=1, source_target_pairs={{0,8},{1,9},{2,10},{3,11},{4,12},{5,13},{6,14},{7,15},{8,0},{9,1},... | collective-permute-start | bytes 172040 | tf_op jit(solution)/shard_map/ppermute | solution.py:260
  11.6 5.0 %all-to-all-done = bf16[8,2,4096]{2,1,0:T(2,128)(2,1)S(1)} async-done(((bf16[8,2,4096]{2,1,0:T(2,128)(2,1)}), bf16[8,2,4096]{2,1,0:T(2,128)(2,1)S(1)}, u32[]{:S(2)}, u32[]{:S(2)}) %all-to-all-start) | async-done | bytes 131104 | tf_op jit(solution)/shard_map/all_to_all | solution.py:48
  20.2 1.3 %collective-permute-start.5 = (bf16[256,512]{1,0:T(8,128)(2,1)S(1)}, bf16[256,512]{1,0:T(8,128)(2,1)S(1)}, u32[]{:S(2)}, u32[]{:S(2)}) collective-permute-start(bf16[256,512]{1,0:T(8,128)(2,1)S(1)} %bitcast.3), channel_id=1, source_target_pairs={{0,4},{1,5},{4,8},{5,9},{8,12},{9,13},{12,14},{13,15},{14,10},{15,... | collective-permute-start | bytes 786440 | tf_op jit(solution)/shard_map/ppermute | solution.py:233
  23.1 1.6 %copy-done = bf16[4096,256]{1,0:T(8,128)(2,1)S(1)} copy-done((bf16[4096,256]{1,0:T(8,128)(2,1)S(1)}, bf16[4096,256]{1,0:T(8,128)(2,1)}, u32[]{:S(2)}) %copy-start) | copy-done | bytes 2097176
  24.7 1.8 %rotate_in.1 = bf16[8,32,256]{2,1,0:T(8,128)(2,1)} custom-call(s32[49]{0:T(128)S(1)} %pad_add_fusion.scalars_ref, bf16[16,4096]{1,0:T(8,128)(2,1)S(1)} %reshape.11.near_ref, bf16[16,4096]{1,0:T(8,128)(2,1)S(1)} %collective-permute-done.3.far_ref, bf16[4096,256]{1,0:T(8,128)(2,1)S(1)} %copy-done), custom_call_target="tpu_custom_call" | custom-call | tf_op jit(solution)/shard_map/rotate_in/pallas_call | solution.py:241
  26.4 3.4 %all-to-all-start.1 = ((bf16[8,32,256]{2,1,0:T(8,128)(2,1)}), bf16[8,32,256]{2,1,0:T(8,128)(2,1)S(1)}, u32[]{:S(2)}, u32[]{:S(2)}) async-start(bf16[8,32,256]{2,1,0:T(8,128)(2,1)} %rotate_in.1), calls=%async_computation.1 | async-start | bytes 262144 | tf_op jit(solution)/shard_map/all_to_all | solution.py:48
  29.8 1.2 %pad_maximum_fusion.1 = bf16[4,2,14336]{2,1,0:T(2,128)(2,1)S(1)} fusion(bf16[2,2,14336]{2,1,0:T(2,128)(2,1)S(1)} %collective-permute-done.1, bf16[1,2,14336]{2,1,0:T(2,128)(2,1)S(1)} %collective-permute-done, bf16[1,2,14336]{2,1,0:T(2,128)(2,1)} %bitcast.9), kind=kLoop, calls=%fused_computation.1 | loop fusion | flops 229376 | bytes 458752 | tf_op jit(solution)/shard_map/concatenate | solution.py:265
  31.0 2.1 %collective-permute-start.2 = (bf16[4,2,14336]{2,1,0:T(2,128)(2,1)S(1)}, bf16[4,2,14336]{2,1,0:T(2,128)(2,1)S(1)}, u32[]{:S(2)}, u32[]{:S(2)}) collective-permute-start(bf16[4,2,14336]{2,1,0:T(2,128)(2,1)S(1)} %pad_maximum_fusion.1), channel_id=1, source_target_pairs={{0,2},{1,3},{2,0},{3,1},{4,6},{5,7},{6,4},{7,5},{8,10},{9,11},{10,... | collective-permute-start | bytes 688136 | tf_op jit(solution)/shard_map/ppermute | solution.py:260
  33.1 4.2 %all-to-all-done.1.near_ref = bf16[8,32,256]{2,1,0:T(8,128)(2,1)S(1)} async-done(((bf16[8,32,256]{2,1,0:T(8,128)(2,1)}), bf16[8,32,256]{2,1,0:T(8,128)(2,1)S(1)}, u32[]{:S(2)}, u32[]{:S(2)}) %all-to-all-start.1) | async-done | bytes 131104 | tf_op jit(solution)/shard_map/all_to_all | solution.py:48
  37.3 2.1 %collective-permute-done.2 = bf16[4,2,14336]{2,1,0:T(2,128)(2,1)S(1)} collective-permute-done((bf16[4,2,14336]{2,1,0:T(2,128)(2,1)S(1)}, bf16[4,2,14336]{2,1,0:T(2,128)(2,1)S(1)}, u32[]{:S(2)}, u32[]{:S(2)}) %collective-permute-start.2) | collective-permute-done | bytes 229408 | tf_op jit(solution)/shard_map/ppermute | solution.py:260
  39.4 1.5 %pad_maximum_fusion = bf16[8,2,14336]{2,1,0:T(2,128)(2,1)S(1)} fusion(bf16[4,2,14336]{2,1,0:T(2,128)(2,1)S(1)} %collective-permute-done.2, bf16[2,2,14336]{2,1,0:T(2,128)(2,1)S(1)} %collective-permute-done.1, bf16[1,2,14336]{2,1,0:T(2,128)(2,1)S(1)} %collective-permute-done, bf16[1,2,14336]{2,1,0:T(2,128)(2,1)} %bitcast.10), kind=kLoop, calls=%fused_computation | loop fusion | flops 688128 | bytes 917504 | tf_op jit(solution)/shard_map/concatenate | solution.py:265
  41.1 1.5 %collective-permute-start.8 = (bf16[256,512]{1,0:T(8,128)(2,1)S(1)}, bf16[256,512]{1,0:T(8,128)(2,1)S(1)}, u32[]{:S(2)}, u32[]{:S(2)}) collective-permute-start(bf16[256,512]{1,0:T(8,128)(2,1)S(1)} %collective-permute-done.5.refs_2_), channel_id=1, source_target_pairs={{0,4},{1,5},{4,8},{5,9},{8,12},{9,13},{12,14},{13,15},{14,10},{15,... | collective-permute-start | bytes 786440 | tf_op jit(solution)/shard_map/ppermute | solution.py:233
  43.2 9.7 %rotate_out.1.aligned_ref = bf16[896,32]{1,0:T(8,128)(2,1)S(1)} custom-call(s32[49]{0:T(128)S(1)} %pad_add_fusion.scalars_ref, bf16[16,14336]{1,0:T(8,128)(2,1)S(1)} %reshape.12.near_ref, bf16[16,14336]{1,0:T(8,128)(2,1)S(1)} %collective-permute-done.7.far_ref, bf16[14336,896]{1,0:T(8,128)(2,1)} %window_ref.1), custom_call_target="tpu_custom_call" | custom-call | flops 822083584 | bytes 25690112 | tf_op jit(solution)/shard_map/rotate_out/pallas_call | solution.py:273
  53.0 1.5 %collective-permute-start.10 = (bf16[256,512]{1,0:T(8,128)(2,1)S(1)}, bf16[256,512]{1,0:T(8,128)(2,1)S(1)}, u32[]{:S(2)}, u32[]{:S(2)}) collective-permute-start(bf16[256,512]{1,0:T(8,128)(2,1)S(1)} %collective-permute-done.8.refs_6_), channel_id=1, source_target_pairs={{0,4},{1,5},{4,8},{5,9},{8,12},{9,13},{12,14},{13,15},{14,10},{15,... | collective-permute-start | bytes 786440 | tf_op jit(solution)/shard_map/ppermute | solution.py:233
  55.6 7.2 %scale.1.scaled_ref = bf16[896,4096]{1,0:T(8,128)(2,1)S(1)} custom-call(s32[49]{0:T(128)S(1)} %pad_add_fusion.scalars_ref, bf16[896,32]{1,0:T(8,128)(2,1)S(1)} %rotate_out.1.aligned_ref, bf16[8,32,256]{2,1,0:T(8,128)(2,1)S(1)} %all-to-all-done.1.near_ref, bf16[8,32,256]{2,1,0:T(8,128)(2,1)S(1)} %collective-permute-done.4.far_ref, f32[896,4096]{1,0:T(8,128)} %eigen_ref.1), custom_call_target="tpu_custom_call" | custom-call | flops 234881024 | bytes 22020096 | tf_op jit(solution)/shard_map/scale/pallas_call | solution.py:297
  64.0 1.5 %collective-permute-start.19 = (bf16[256,512]{1,0:T(8,128)(2,1)S(1)}, bf16[256,512]{1,0:T(8,128)(2,1)S(1)}, u32[]{:S(2)}, u32[]{:S(2)}) collective-permute-start(bf16[256,512]{1,0:T(8,128)(2,1)S(1)} %collective-permute-done.10.refs_10_), channel_id=1, source_target_pairs={{0,4},{1,5},{4,8},{5,9},{8,12},{9,13},{12,14},{13,15},{14,10},{15,... | collective-permute-start | bytes 786440 | tf_op jit(solution)/shard_map/ppermute | solution.py:233
  65.7 4.5 %project.1.projected_ref = f32[896,512]{1,0:T(8,128)S(1)} custom-call(bf16[896,4096]{1,0:T(8,128)(2,1)S(1)} %scale.1.scaled_ref, bf16[256,512]{1,0:T(8,128)(2,1)S(1)} %bitcast.6, bf16[256,512]{1,0:T(8,128)(2,1)S(1)} %collective-permute-done.12.refs_1_, bf16[256,512]{1,0:T(8,128)(2,1)S(1)} %collective-permute-done.5.refs_2_, ...), custom_call_target="tpu_custom_call" | custom-call | flops 3758096384 | bytes 11534336 | tf_op jit(solution)/shard_map/project/pallas_call | solution.py:321
  70.2 2.5 %collective-permute-done.19.refs_0_ = bf16[256,512]{1,0:T(8,128)(2,1)S(1)} collective-permute-done((bf16[256,512]{1,0:T(8,128)(2,1)S(1)}, bf16[256,512]{1,0:T(8,128)(2,1)S(1)}, u32[]{:S(2)}, u32[]{:S(2)}) %collective-permute-start.19) | collective-permute-done | bytes 262176 | tf_op jit(solution)/shard_map/ppermute | solution.py:233
  72.6 1.5 %collective-permute-done.20.refs_1_ = bf16[256,512]{1,0:T(8,128)(2,1)S(1)} collective-permute-done((bf16[256,512]{1,0:T(8,128)(2,1)S(1)}, bf16[256,512]{1,0:T(8,128)(2,1)S(1)}, u32[]{:S(2)}, u32[]{:S(2)}) %collective-permute-start.20) | collective-permute-done | bytes 262176 | tf_op jit(solution)/shard_map/ppermute | solution.py:43
  74.2 3.0 %window.1 = (bf16[8,48,512]{2,1,0:T(8,128)(2,1)S(1)}, f32[8,48,512]{2,1,0:T(8,128)S(1)}) custom-call(s32[49]{0:T(128)S(1)} %pad_add_fusion.scalars_ref, bf16[14336,896]{1,0:T(8,128)(2,1)} %window_ref.1, bf16[896,4096]{1,0:T(8,128)(2,1)S(1)} %scale.1.scaled_ref, f32[896,512]{1,0:T(8,128)S(1)} %project.1.projected_ref, ...), custom_call_target="tpu_custom_call" | custom-call | flops 704643072 | bytes 6094848 | tf_op jit(solution)/shard_map/window/pallas_call | solution.py:341
  77.4 1.6 %collective-permute-done.21.got_ref = bf16[8,48,512]{2,1,0:T(8,128)(2,1)S(1)} collective-permute-done((bf16[8,48,512]{2,1,0:T(8,128)(2,1)S(1)}, bf16[8,48,512]{2,1,0:T(8,128)(2,1)S(1)}, u32[]{:S(2)}, u32[]{:S(2)}) %collective-permute-start.21) | collective-permute-done | bytes 393248 | tf_op jit(solution)/shard_map/ppermute | solution.py:43
  79.0 16.9 %all_to_all.15.parts_ref = bf16[8,48,512]{2,1,0:T(8,128)(2,1)S(1)} all-to-all(bf16[8,48,512]{2,1,0:T(8,128)(2,1)S(1)} %add_core.1), channel_id=1, replica_groups={{0,2,4,6,8,10,12,14},{1,3,5,7,9,11,13,15},{16,18,20,22,24,26,28,30},{17..., dimensions={0} | all-to-all | bytes 786432 | tf_op jit(solution)/shard_map/all_to_all | solution.py:48
  (43 shorter events, 9.4 us)
Async XLA Ops:
  1.4 15.2 %all-to-all-start = ((bf16[8,2,4096]{2,1,0:T(2,128)(2,1)}), bf16[8,2,4096]{2,1,0:T(2,128)(2,1)S(1)}, u32[]{:S(2)}, u32[]{:S(2)}) async-start(bf16[8,2,4096]{2,1,0:T(2,128)(2,1)} %broadcast_in_dim.10), calls=%async_computation | async-start | bytes 262144 | tf_op jit(solution)/shard_map/all_to_all | solution.py:48
  8.7 8.5 %collective-permute-start = (bf16[1,2,14336]{2,1,0:T(2,128)(2,1)}, bf16[1,2,14336]{2,1,0:T(2,128)(2,1)S(1)}, u32[]{:S(2)}, u32[]{:S(2)}) collective-permute-start(bf16[1,2,14336]{2,1,0:T(2,128)(2,1)} %bitcast.7), channel_id=1, source_target_pairs={{0,8},{1,9},{2,10},{3,11},{4,12},{5,13},{6,14},{7,15},{8,0},{9,1},... | collective-permute-start | bytes 172040 | tf_op jit(solution)/shard_map/ppermute | solution.py:260
  16.7 6.4 %collective-permute-start.3 = (bf16[16,4096]{1,0:T(8,128)(2,1)S(1)}, bf16[16,4096]{1,0:T(8,128)(2,1)S(1)}, u32[]{:S(2)}, u32[]{:S(2)}) collective-permute-start(bf16[16,4096]{1,0:T(8,128)(2,1)S(1)} %reshape.11.near_ref), channel_id=1, source_target_pairs={{0,1},{1,0},{2,3},{3,2},{4,5},{5,4},{6,7},{7,6},{8,9},{9,8},{10,11... | collective-permute-start | bytes 393224 | tf_op jit(solution)/shard_map/ppermute | solution.py:43
  18.2 11.6 %collective-permute-start.1 = (bf16[2,2,14336]{2,1,0:T(2,128)(2,1)S(1)}, bf16[2,2,14336]{2,1,0:T(2,128)(2,1)S(1)}, u32[]{:S(2)}, u32[]{:S(2)}) collective-permute-start(bf16[2,2,14336]{2,1,0:T(2,128)(2,1)S(1)} %pad_maximum_fusion.2), channel_id=1, source_target_pairs={{0,4},{1,5},{2,6},{3,7},{4,0},{5,1},{6,2},{7,3},{8,12},{9,13},{10,... | collective-permute-start | bytes 344072 | tf_op jit(solution)/shard_map/ppermute | solution.py:260
  20.2 17.1 %collective-permute-start.5 = (bf16[256,512]{1,0:T(8,128)(2,1)S(1)}, bf16[256,512]{1,0:T(8,128)(2,1)S(1)}, u32[]{:S(2)}, u32[]{:S(2)}) collective-permute-start(bf16[256,512]{1,0:T(8,128)(2,1)S(1)} %bitcast.3), channel_id=1, source_target_pairs={{0,4},{1,5},{4,8},{5,9},{8,12},{9,13},{12,14},{13,15},{14,10},{15,... | collective-permute-start | bytes 786440 | tf_op jit(solution)/shard_map/ppermute | solution.py:233
  21.5 15.8 %collective-permute-start.6 = (bf16[256,512]{1,0:T(8,128)(2,1)S(1)}, bf16[256,512]{1,0:T(8,128)(2,1)S(1)}, u32[]{:S(2)}, u32[]{:S(2)}) collective-permute-start(bf16[256,512]{1,0:T(8,128)(2,1)S(1)} %bitcast.4), channel_id=1, source_target_pairs={{0,2},{1,3},{4,0},{5,1},{8,4},{9,5},{12,8},{13,9},{14,12},{15,13},... | collective-permute-start | bytes 786440 | tf_op jit(solution)/shard_map/ppermute | solution.py:234
  26.4 10.8 %all-to-all-start.1 = ((bf16[8,32,256]{2,1,0:T(8,128)(2,1)}), bf16[8,32,256]{2,1,0:T(8,128)(2,1)S(1)}, u32[]{:S(2)}, u32[]{:S(2)}) async-start(bf16[8,32,256]{2,1,0:T(8,128)(2,1)} %rotate_in.1), calls=%async_computation.1 | async-start | bytes 262144 | tf_op jit(solution)/shard_map/all_to_all | solution.py:48
  31.0 8.4 %collective-permute-start.2 = (bf16[4,2,14336]{2,1,0:T(2,128)(2,1)S(1)}, bf16[4,2,14336]{2,1,0:T(2,128)(2,1)S(1)}, u32[]{:S(2)}, u32[]{:S(2)}) collective-permute-start(bf16[4,2,14336]{2,1,0:T(2,128)(2,1)S(1)} %pad_maximum_fusion.1), channel_id=1, source_target_pairs={{0,2},{1,3},{2,0},{3,1},{4,6},{5,7},{6,4},{7,5},{8,10},{9,11},{10,... | collective-permute-start | bytes 688136 | tf_op jit(solution)/shard_map/ppermute | solution.py:260
  37.3 2.1 %collective-permute-start.4 = (bf16[8,32,256]{2,1,0:T(8,128)(2,1)S(1)}, bf16[8,32,256]{2,1,0:T(8,128)(2,1)S(1)}, u32[]{:S(2)}, u32[]{:S(2)}) collective-permute-start(bf16[8,32,256]{2,1,0:T(8,128)(2,1)S(1)} %all-to-all-done.1.near_ref), channel_id=1, source_target_pairs={{0,1},{1,0},{2,3},{3,2},{4,5},{5,4},{6,7},{7,6},{8,9},{9,8},{10,11... | collective-permute-start | bytes 393224 | tf_op jit(solution)/shard_map/ppermute | solution.py:43
  41.1 2.2 %collective-permute-start.7 = (bf16[16,14336]{1,0:T(8,128)(2,1)S(1)}, bf16[16,14336]{1,0:T(8,128)(2,1)S(1)}, u32[]{:S(2)}, u32[]{:S(2)}) collective-permute-start(bf16[16,14336]{1,0:T(8,128)(2,1)S(1)} %reshape.12.near_ref), channel_id=1, source_target_pairs={{0,1},{1,0},{2,3},{3,2},{4,5},{5,4},{6,7},{7,6},{8,9},{9,8},{10,11... | collective-permute-start | bytes 1376264 | tf_op jit(solution)/shard_map/ppermute | solution.py:43
  41.1 11.8 %collective-permute-start.8 = (bf16[256,512]{1,0:T(8,128)(2,1)S(1)}, bf16[256,512]{1,0:T(8,128)(2,1)S(1)}, u32[]{:S(2)}, u32[]{:S(2)}) collective-permute-start(bf16[256,512]{1,0:T(8,128)(2,1)S(1)} %collective-permute-done.5.refs_2_), channel_id=1, source_target_pairs={{0,4},{1,5},{4,8},{5,9},{8,12},{9,13},{12,14},{13,15},{14,10},{15,... | collective-permute-start | bytes 786440 | tf_op jit(solution)/shard_map/ppermute | solution.py:233
  42.7 10.3 %collective-permute-start.9 = (bf16[256,512]{1,0:T(8,128)(2,1)S(1)}, bf16[256,512]{1,0:T(8,128)(2,1)S(1)}, u32[]{:S(2)}, u32[]{:S(2)}) collective-permute-start(bf16[256,512]{1,0:T(8,128)(2,1)S(1)} %collective-permute-done.6.refs_4_), channel_id=1, source_target_pairs={{0,2},{1,3},{4,0},{5,1},{8,4},{9,5},{12,8},{13,9},{14,12},{15,13},... | collective-permute-start | bytes 786440 | tf_op jit(solution)/shard_map/ppermute | solution.py:234
  53.0 9.8 %collective-permute-start.10 = (bf16[256,512]{1,0:T(8,128)(2,1)S(1)}, bf16[256,512]{1,0:T(8,128)(2,1)S(1)}, u32[]{:S(2)}, u32[]{:S(2)}) collective-permute-start(bf16[256,512]{1,0:T(8,128)(2,1)S(1)} %collective-permute-done.8.refs_6_), channel_id=1, source_target_pairs={{0,4},{1,5},{4,8},{5,9},{8,12},{9,13},{12,14},{13,15},{14,10},{15,... | collective-permute-start | bytes 786440 | tf_op jit(solution)/shard_map/ppermute | solution.py:233
  54.5 8.9 %collective-permute-start.11 = (bf16[256,512]{1,0:T(8,128)(2,1)S(1)}, bf16[256,512]{1,0:T(8,128)(2,1)S(1)}, u32[]{:S(2)}, u32[]{:S(2)}) collective-permute-start(bf16[256,512]{1,0:T(8,128)(2,1)S(1)} %collective-permute-done.9.refs_8_), channel_id=1, source_target_pairs={{0,2},{1,3},{4,0},{5,1},{8,4},{9,5},{12,8},{13,9},{14,12},{15,13},... | collective-permute-start | bytes 786440 | tf_op jit(solution)/shard_map/ppermute | solution.py:234
  55.1 8.4 %collective-permute-start.12 = (bf16[256,512]{1,0:T(8,128)(2,1)S(1)}, bf16[256,512]{1,0:T(8,128)(2,1)S(1)}, u32[]{:S(2)}, u32[]{:S(2)}) collective-permute-start(bf16[256,512]{1,0:T(8,128)(2,1)S(1)} %bitcast.5), channel_id=1, source_target_pairs={{0,1},{1,0},{2,3},{3,2},{4,5},{5,4},{6,7},{7,6},{8,9},{9,8},{10,11... | collective-permute-start | bytes 786440 | tf_op jit(solution)/shard_map/ppermute | solution.py:43
  55.1 8.8 %collective-permute-start.13 = (bf16[256,512]{1,0:T(8,128)(2,1)S(1)}, bf16[256,512]{1,0:T(8,128)(2,1)S(1)}, u32[]{:S(2)}, u32[]{:S(2)}) collective-permute-start(bf16[256,512]{1,0:T(8,128)(2,1)S(1)} %collective-permute-done.5.refs_2_), channel_id=1, source_target_pairs={{0,1},{1,0},{2,3},{3,2},{4,5},{5,4},{6,7},{7,6},{8,9},{9,8},{10,11... | collective-permute-start | bytes 786440 | tf_op jit(solution)/shard_map/ppermute | solution.py:43
  55.6 8.4 %collective-permute-start.14 = (bf16[256,512]{1,0:T(8,128)(2,1)S(1)}, bf16[256,512]{1,0:T(8,128)(2,1)S(1)}, u32[]{:S(2)}, u32[]{:S(2)}) collective-permute-start(bf16[256,512]{1,0:T(8,128)(2,1)S(1)} %collective-permute-done.6.refs_4_), channel_id=1, source_target_pairs={{0,1},{1,0},{2,3},{3,2},{4,5},{5,4},{6,7},{7,6},{8,9},{9,8},{10,11... | collective-permute-start | bytes 786440 | tf_op jit(solution)/shard_map/ppermute | solution.py:43
  62.8 2.7 %collective-permute-start.15 = (bf16[256,512]{1,0:T(8,128)(2,1)S(1)}, bf16[256,512]{1,0:T(8,128)(2,1)S(1)}, u32[]{:S(2)}, u32[]{:S(2)}) collective-permute-start(bf16[256,512]{1,0:T(8,128)(2,1)S(1)} %collective-permute-done.8.refs_6_), channel_id=1, source_target_pairs={{0,1},{1,0},{2,3},{3,2},{4,5},{5,4},{6,7},{7,6},{8,9},{9,8},{10,11... | collective-permute-start | bytes 786440 | tf_op jit(solution)/shard_map/ppermute | solution.py:43
  63.4 2.1 %collective-permute-start.16 = (bf16[256,512]{1,0:T(8,128)(2,1)S(1)}, bf16[256,512]{1,0:T(8,128)(2,1)S(1)}, u32[]{:S(2)}, u32[]{:S(2)}) collective-permute-start(bf16[256,512]{1,0:T(8,128)(2,1)S(1)} %collective-permute-done.9.refs_8_), channel_id=1, source_target_pairs={{0,1},{1,0},{2,3},{3,2},{4,5},{5,4},{6,7},{7,6},{8,9},{9,8},{10,11... | collective-permute-start | bytes 786440 | tf_op jit(solution)/shard_map/ppermute | solution.py:43
  63.5 2.0 %collective-permute-start.17 = (bf16[256,512]{1,0:T(8,128)(2,1)S(1)}, bf16[256,512]{1,0:T(8,128)(2,1)S(1)}, u32[]{:S(2)}, u32[]{:S(2)}) collective-permute-start(bf16[256,512]{1,0:T(8,128)(2,1)S(1)} %collective-permute-done.10.refs_10_), channel_id=1, source_target_pairs={{0,1},{1,0},{2,3},{3,2},{4,5},{5,4},{6,7},{7,6},{8,9},{9,8},{10,11... | collective-permute-start | bytes 786440 | tf_op jit(solution)/shard_map/ppermute | solution.py:43
  63.9 1.8 %collective-permute-start.18 = (bf16[256,512]{1,0:T(8,128)(2,1)S(1)}, bf16[256,512]{1,0:T(8,128)(2,1)S(1)}, u32[]{:S(2)}, u32[]{:S(2)}) collective-permute-start(bf16[256,512]{1,0:T(8,128)(2,1)S(1)} %collective-permute-done.11.refs_12_), channel_id=1, source_target_pairs={{0,1},{1,0},{2,3},{3,2},{4,5},{5,4},{6,7},{7,6},{8,9},{9,8},{10,11... | collective-permute-start | bytes 786440 | tf_op jit(solution)/shard_map/ppermute | solution.py:43
  64.0 8.7 %collective-permute-start.19 = (bf16[256,512]{1,0:T(8,128)(2,1)S(1)}, bf16[256,512]{1,0:T(8,128)(2,1)S(1)}, u32[]{:S(2)}, u32[]{:S(2)}) collective-permute-start(bf16[256,512]{1,0:T(8,128)(2,1)S(1)} %collective-permute-done.10.refs_10_), channel_id=1, source_target_pairs={{0,4},{1,5},{4,8},{5,9},{8,12},{9,13},{12,14},{13,15},{14,10},{15,... | collective-permute-start | bytes 786440 | tf_op jit(solution)/shard_map/ppermute | solution.py:233
  72.6 1.5 %collective-permute-start.20 = (bf16[256,512]{1,0:T(8,128)(2,1)S(1)}, bf16[256,512]{1,0:T(8,128)(2,1)S(1)}, u32[]{:S(2)}, u32[]{:S(2)}) collective-permute-start(bf16[256,512]{1,0:T(8,128)(2,1)S(1)} %collective-permute-done.19.refs_0_), channel_id=1, source_target_pairs={{0,1},{1,0},{2,3},{3,2},{4,5},{5,4},{6,7},{7,6},{8,9},{9,8},{10,11... | collective-permute-start | bytes 786440 | tf_op jit(solution)/shard_map/ppermute | solution.py:43
  77.2 1.8 %collective-permute-start.21 = (bf16[8,48,512]{2,1,0:T(8,128)(2,1)S(1)}, bf16[8,48,512]{2,1,0:T(8,128)(2,1)S(1)}, u32[]{:S(2)}, u32[]{:S(2)}) collective-permute-start(bf16[8,48,512]{2,1,0:T(8,128)(2,1)S(1)} %get-tuple-element.34), channel_id=1, source_target_pairs={{0,1},{1,0},{2,3},{3,2},{4,5},{5,4},{6,7},{7,6},{8,9},{9,8},{10,11... | collective-permute-start | bytes 1179656 | tf_op jit(solution)/shard_map/ppermute | solution.py:43
  (1 other events, 1.6 us)

commit v6 on v5

--- a/solution.py
+++ b/solution.py
@@ -43,9 +43,9 @@
     return lax.ppermute(x, "blk", xor_pairs(n, 1))
 
 
-def plane_exchange(x, n):
-    planes = [list(range(c, n, 2)) for c in range(2)]
-    return lax.all_to_all(x, "blk", 0, 0, axis_index_groups=planes, tiled=True)
+def exchange(x, n, stride):
+    groups = [list(range(first, n, stride)) for first in range(stride)]
+    return lax.all_to_all(x, "blk", 0, 0, axis_index_groups=groups, tiled=True)
 
 
 def bits_of(size):
@@ -64,31 +64,24 @@
     return (device << bits_of(tok_rows)) + (row & (tok_rows - 1))
 
 
-def plane_tokens(me, tokens, tok_rows):
-    row = lax.broadcasted_iota(jnp.int32, (tokens, tokens), 1)
-    chips = tokens // tok_rows // 2
-    chip = (row >> bits_of(tok_rows)) & (chips - 1)
-    core = (me & 1) ^ (row >> bits_of(tokens // 2))
-    return ((2 * chip + core) << bits_of(tok_rows)) + (row & (tok_rows - 1))
-
-
 def reorder(wanted, held, rotated):
     order = jnp.where(wanted == held, 1.0, 0.0).astype(jnp.bfloat16)
     return jnp.dot(order, rotated.astype(jnp.bfloat16), preferred_element_type=jnp.float32)
 
 
-def rotate_in_kernel(tok_rows, scalars_ref, near_ref, far_ref, basis_ref, out_ref):
+def rotate_in_kernel(tok_rows, near_ref, far_ref, basis_ref, out_ref):
     tokens = out_ref.shape[1]
     acts = jnp.concatenate([near_ref[...], far_ref[...]], axis=0)
     rotated = jnp.dot(acts, basis_ref[...], preferred_element_type=jnp.float32)
     wanted = lax.broadcasted_iota(jnp.int32, (tokens, tokens), 0)
-    ordered = reorder(wanted, plane_tokens(scalars_ref[0], tokens, tok_rows), rotated)
+    held = held_tokens(lax.axis_index("blk"), tokens, tok_rows)
+    ordered = reorder(wanted, held, rotated).astype(jnp.bfloat16)
     for copy in range(out_ref.shape[0]):
-        out_ref[copy] = ordered.astype(jnp.bfloat16)
+        out_ref[copy] = ordered
 
 
 def rotate_out_kernel(
-    tok_rows, map_at, scalars_ref, near_ref, far_ref, basis_ref, out_ref, basis, total, sem
+    tok_rows, near_ref, far_ref, basis_ref, map_ref, out_ref, basis, total, stored_map, sem
 ):
     steps, depth = basis.shape[:2]
     tokens = total.shape[0]
@@ -101,6 +94,8 @@
     def _(step):
         copy_of(step).start()
 
+    map_copy = pltpu.make_async_copy(map_ref, stored_map, sem.at[steps])
+    map_copy.start()
     total[...] = jnp.zeros_like(total)
 
     @pl.loop(0, steps)
@@ -110,18 +105,19 @@
         copy_of(step).wait()
         total[...] += jnp.dot(grads, basis[step], preferred_element_type=jnp.float32)
 
+    map_copy.wait()
     row = lax.broadcasted_iota(jnp.int32, (tokens, tokens), 0)
     block = row >> bits_of(tok_rows)
     wanted = jnp.zeros_like(row)
     for stored in range(tokens // tok_rows):
-        wanted = jnp.where(block == stored, scalars_ref[map_at + stored] * tok_rows, wanted)
+        wanted = jnp.where(block == stored, stored_map[stored] * tok_rows, wanted)
     wanted += row & (tok_rows - 1)
-    held = held_tokens(scalars_ref[0], tokens, tok_rows)
+    held = held_tokens(lax.axis_index("blk"), tokens, tok_rows)
     out_ref[...] = reorder(wanted, held, total[...]).T.astype(jnp.bfloat16)
 
 
 def scale_kernel(
-    begun, tiles_at, scalars_ref, aligned_ref, near_ref, far_ref, eigen_ref, out_ref, damped, sem
+    begun, aligned_ref, near_ref, far_ref, tiles_ref, eigen_ref, out_ref, damped, tiles, sem
 ):
     blocks, depth = damped.shape[:2]
     chips, _, width = near_ref.shape
@@ -130,9 +126,15 @@
         rows = pl.ds(pl.multiple_of(block * depth, depth), depth)
         return pltpu.make_async_copy(eigen_ref.at[rows], damped.at[block], sem.at[block])
 
+    tiles_copy = pltpu.make_async_copy(tiles_ref, tiles, sem.at[blocks])
+    tiles_copy.start()
+
     @pl.loop(0, blocks)
     def _(block):
         copy_of(block).start()
+
+    tiles_copy.wait()
+    me = lax.axis_index("blk")
 
     @pl.loop(0, blocks)
     def _(block):
@@ -142,12 +144,12 @@
         place = 0
         for steps in begun:
             for other, rotated_ref in enumerate((near_ref, far_ref)):
-                source = ring_source(scalars_ref[0], steps, other, chips)
+                source = ring_source(me, steps, other, chips)
                 grad = jnp.dot(
                     aligned, rotated_ref[source // 2], preferred_element_type=jnp.float32
                 )
                 for first in range(0, width, LANES):
-                    tile = scalars_ref[tiles_at + (source * width + first) // LANES]
+                    tile = tiles[(source * width + first) // LANES]
                     lanes = pl.ds(pl.multiple_of(tile * LANES, LANES), LANES)
                     eigen = damped[block, :, lanes]
                     inverse = pl.reciprocal(eigen, approx=True)
@@ -157,15 +159,19 @@
                     place += LANES
 
 
-def project_kernel(cuts, scaled_ref, *refs):
-    pieces = refs[:-3]
-    out_ref, basis, sem = refs[-3:]
+def project_kernel(cuts, scaled_ref, basis_out_ref, *refs):
+    pieces = refs[:-4]
+    out_ref, window_ref, basis, sem = refs[-4:]
     width = pieces[0].shape[0]
     rows = out_ref.shape[0] // 2
     copies = [
         pltpu.make_async_copy(piece, basis.at[pl.ds(at * width, width)], sem.at[at])
         for at, piece in enumerate(pieces)
     ]
+    window_copy = pltpu.make_async_copy(
+        basis_out_ref.at[pl.ds(0, window_ref.shape[0])], window_ref, sem.at[len(pieces)]
+    )
+    window_copy.start()
     for copy in copies:
         copy.start()
     for first, last in zip(cuts[:-1], cuts[1:]):
@@ -181,8 +187,10 @@
             )
             out_ref[block, :] = part if first == 0 else out_ref[block, :] + part
 
-
-def window_kernel(scale, scalars_ref, window_ref, scaled_ref, projected_ref, *refs):
+    window_copy.wait()
+
+
+def window_kernel(scale, window_ref, scaled_ref, projected_ref, *refs):
     pieces = refs[:-3]
     send_ref, keep_ref, result = refs[-3:]
     chips, rows, _ = keep_ref.shape
@@ -197,7 +205,7 @@
     result[...] = scale * jnp.dot(
         window_ref[...], total.astype(jnp.bfloat16), preferred_element_type=jnp.float32
     )
-    core = lax.rem(scalars_ref[0], 2)
+    core = lax.rem(lax.axis_index("blk"), 2)
     for k in range(chips):
         mine = pl.ds(pl.multiple_of((2 * k + core) * rows, rows), rows)
         keep_ref[k] = result[mine, :]
@@ -205,8 +213,17 @@
         send_ref[k] = result[other, :].astype(jnp.bfloat16)
 
 
-def add_core_kernel(keep_ref, got_ref, out_ref):
-    out_ref[...] = (keep_ref[...] + got_ref[...].astype(jnp.float32)).astype(jnp.bfloat16)
+def add_core_kernel(keep_ref, got_ref, mine_ref, send_ref):
+    side = lax.rem(lax.axis_index("blk") // 2, 2)
+    for pair in range(mine_ref.shape[0]):
+        mine, other = 2 * pair + side, 2 * pair + 1 - side
+        mine_ref[pair] = keep_ref[mine] + got_ref[mine].astype(jnp.float32)
+        sent = keep_ref[other] + got_ref[other].astype(jnp.float32)
+        send_ref[pair] = sent.astype(jnp.bfloat16)
+
+
+def add_pair_kernel(mine_ref, got_ref, out_ref):
+    out_ref[...] = (mine_ref[...] + got_ref[...].astype(jnp.float32)).astype(jnp.bfloat16)
 
 
 def add_chips_kernel(parts_ref, out_ref):
@@ -228,57 +245,61 @@
     full_in, in_width = basis_in.shape
     tokens = n * tok_rows
     chips = n // 2
-    me = lax.axis_index("blk").reshape(1)
-    scalars = jnp.concatenate([me, tile_order, block_map])
     to_right = lambda x: lax.ppermute(x, "blk", shift_pairs(n, 1))
     to_left = lambda x: lax.ppermute(x, "blk", shift_pairs(n, -1))
     steps = chips // 2
 
     own = basis_in[:WC].T
 
-    acts = jnp.broadcast_to(activations[None], (chips, *activations.shape))
-    acts = plane_exchange(acts, n).reshape(tokens // 2, full_in)
-    rotated = pl.pallas_call(
-        functools.partial(rotate_in_kernel, tok_rows),
-        out_shape=jax.ShapeDtypeStruct((chips, tokens, in_width), jnp.bfloat16),
-        in_specs=[SMEM, VMEM, VMEM, VMEM],
-        out_specs=VMEM,
-        compiler_params=pltpu.CompilerParams(vmem_limit_bytes=8 * MIB),
-        name="rotate_in",
-    )(scalars, acts, swap(acts, n), basis_in)
-    rotated = plane_exchange(rotated, n)
-    rotated_far = swap(rotated, n)
-
+    both = jnp.concatenate([grad_out, activations], axis=1)[None]
+    key = n // 2
+    while key > 2:
+        got = lax.ppermute(both, "blk", xor_pairs(n, key))
+        key //= 2
+        if key > 2:
+            both = jnp.concatenate([both, got], axis=0)
+
+    got, own = after(got, own)
     right, left = [own], [own]
     while len(right) < max(steps - 2, 2):
         right.append(to_right(right[-1]))
         left.append(to_left(left[-1]))
 
-    grads = grad_out[None]
-    key = n // 2
-    while key > 1:
-        got = lax.ppermute(grads, "blk", xor_pairs(n, key))
-        if key == 2:
-            got, rotated, rotated_far, right[-1], left[-1] = after(
-                got, rotated, rotated_far, right[-1], left[-1]
-            )
-        grads = jnp.concatenate([grads, got], axis=0)
-        key //= 2
-    grads = grads.reshape(tokens // 2, full_out)
+    acts = jnp.concatenate([both[..., full_out:], got[..., full_out:]], axis=0)
+    grads = jnp.concatenate([both[..., :full_out], got[..., :full_out]], axis=0)
+    got = lax.ppermute(acts, "blk", xor_pairs(n, 2))
+    acts = jnp.concatenate([acts, got], axis=0).reshape(tokens // 2, full_in)
+    rotated = pl.pallas_call(
+        functools.partial(rotate_in_kernel, tok_rows),
+        out_shape=jax.ShapeDtypeStruct((chips, tokens, in_width), jnp.bfloat16),
+        in_specs=[VMEM, VMEM, VMEM],
+        out_specs=VMEM,
+        compiler_params=pltpu.CompilerParams(vmem_limit_bytes=8 * MIB),
+        name="rotate_in",
+    )(acts, swap(acts, n), basis_in)
+    rotated = exchange(rotated, n, 2)
+    got = lax.ppermute(grads, "blk", xor_pairs(n, 2))
+    got, rotated, right[-1], left[-1] = after(got, rotated, right[-1], left[-1])
+    rotated_far = swap(rotated, n)
+    grads = jnp.concatenate([grads, got], axis=0).reshape(tokens // 2, full_out)
     grads_far = swap(grads, n)
+    near = [right[0]] + [x for pair in zip(right[1:], left[1:]) for x in pair]
+    far = [swap(piece, n) for piece in near]
+    grads, grads_far, rotated_far, *far = after(grads, grads_far, rotated_far, *far)
     right.append(to_right(right[-1]))
     left.append(to_left(left[-1]))
 
     depth = 1024
     aligned = pl.pallas_call(
-        functools.partial(rotate_out_kernel, tok_rows, 1 + full_in // LANES),
+        functools.partial(rotate_out_kernel, tok_rows),
         out_shape=jax.ShapeDtypeStruct((tile_width, tokens), jnp.bfloat16),
-        in_specs=[SMEM, VMEM, VMEM, ANY],
+        in_specs=[VMEM, VMEM, ANY, ANY],
         out_specs=VMEM,
         scratch_shapes=[
             pltpu.VMEM((full_out // depth, depth, tile_width), jnp.bfloat16),
             pltpu.VMEM((tokens, tile_width), jnp.float32),
-            pltpu.SemaphoreType.DMA((full_out // depth,)),
+            pltpu.SMEM(block_map.shape, jnp.int32),
+            pltpu.SemaphoreType.DMA((full_out // depth + 1,)),
         ],
         compiler_params=pltpu.CompilerParams(vmem_limit_bytes=40 * MIB),
         cost_estimate=pl.CostEstimate(
@@ -287,7 +308,7 @@
             transcendentals=0,
         ),
         name="rotate_out",
-    )(scalars, grads, grads_far, basis_out)
+    )(grads, grads_far, basis_out, block_map)
 
     aligned, right[-1], left[-1] = after(aligned, right[-1], left[-1])
     right.append(to_right(right[-1]))
@@ -295,13 +316,14 @@
     begun = [0] + [at for step in range(1, steps) for at in (step, chips - step)] + [steps]
     blocks = 8
     scaled = pl.pallas_call(
-        functools.partial(scale_kernel, begun, 1),
+        functools.partial(scale_kernel, begun),
         out_shape=jax.ShapeDtypeStruct((tile_width, full_in), jnp.bfloat16),
-        in_specs=[SMEM, VMEM, VMEM, VMEM, ANY],
+        in_specs=[VMEM, VMEM, VMEM, ANY, ANY],
         out_specs=VMEM,
         scratch_shapes=[
             pltpu.VMEM((blocks, tile_width // blocks, full_in), jnp.float32),
-            pltpu.SemaphoreType.DMA((blocks,)),
+            pltpu.SMEM(tile_order.shape, jnp.int32),
+            pltpu.SemaphoreType.DMA((blocks + 1,)),
         ],
         compiler_params=pltpu.CompilerParams(vmem_limit_bytes=40 * MIB),
         cost_estimate=pl.CostEstimate(
@@ -310,22 +332,25 @@
             transcendentals=tile_width * full_in,
         ),
         name="scale",
-    )(scalars, aligned, rotated, rotated_far, eigenvalues)
+    )(aligned, rotated, rotated_far, tile_order, eigenvalues)
 
     scaled, right[-1], left[-1] = after(scaled, right[-1], left[-1])
     last = to_right(right[-1])
-    pieces = []
-    for at in begun[:-1]:
-        near = right[at] if at < steps else left[chips - at]
-        pieces += [near, swap(near, n)]
-    projected = pl.pallas_call(
+    for at in begun[len(near) : -1]:
+        near.append(right[at] if at < steps else left[chips - at])
+        far.append(swap(near[-1], n))
+    pieces = [piece for pair in zip(near, far) for piece in pair]
+    projected, window = pl.pallas_call(
         functools.partial(project_kernel, (0, 6, len(pieces))),
-        out_shape=jax.ShapeDtypeStruct((tile_width, WC), jnp.float32),
-        in_specs=[VMEM] + [ANY] * len(pieces),
-        out_specs=VMEM,
+        out_shape=(
+            jax.ShapeDtypeStruct((tile_width, WC), jnp.float32),
+            jax.ShapeDtypeStruct((WR, tile_width), jnp.bfloat16),
+        ),
+        in_specs=[VMEM] + [ANY] * (len(pieces) + 1),
+        out_specs=(VMEM, VMEM),
         scratch_shapes=[
             pltpu.VMEM((len(pieces) * in_width, WC), jnp.bfloat16),
-            pltpu.SemaphoreType.DMA((len(pieces),)),
+            pltpu.SemaphoreType.DMA((len(pieces) + 1,)),
         ],
         compiler_params=pltpu.CompilerParams(vmem_limit_bytes=24 * MIB),
         cost_estimate=pl.CostEstimate(
@@ -334,7 +359,7 @@
             transcendentals=0,
         ),
         name="project",
-    )(scaled, *pieces)
+    )(scaled, basis_out, *pieces)
 
     projected, last = after(projected, last)
     rows = WR // n
@@ -344,35 +369,48 @@
             jax.ShapeDtypeStruct((chips, rows, WC), jnp.bfloat16),
             jax.ShapeDtypeStruct((chips, rows, WC), jnp.float32),
         ),
-        grid=(1,),
-        in_specs=[SMEM, pl.BlockSpec((WR, tile_width), lambda i: (0, 0))] + [VMEM] * 4,
+        in_specs=[VMEM] * 5,
         out_specs=(VMEM, VMEM),
         scratch_shapes=[pltpu.VMEM((WR, WC), jnp.float32)],
-        compiler_params=pltpu.CompilerParams(vmem_limit_bytes=36 * MIB),
+        compiler_params=pltpu.CompilerParams(vmem_limit_bytes=24 * MIB),
         cost_estimate=pl.CostEstimate(
             flops=2 * WR * tile_width * WC,
             bytes_accessed=2 * WR * tile_width + 12 * WR * WC,
             transcendentals=0,
         ),
         name="window",
-    )(scalars, basis_out, scaled, projected, last, swap(last, n))
-
+    )(window, scaled, projected, last, swap(last, n))
+
+    small = pltpu.CompilerParams(vmem_limit_bytes=8 * MIB)
+    half = (chips // 2, rows, WC)
+    mine, send = pl.pallas_call(
+        add_core_kernel,
+        out_shape=(
+            jax.ShapeDtypeStruct(half, jnp.float32),
+            jax.ShapeDtypeStruct(half, jnp.bfloat16),
+        ),
+        in_specs=[VMEM, VMEM],
+        out_specs=(VMEM, VMEM),
+        compiler_params=small,
+        name="add_core",
+    )(keep, swap(send, n))
+    got = lax.ppermute(send, "blk", xor_pairs(n, 2))
     summed = pl.pallas_call(
-        add_core_kernel,
-        out_shape=jax.ShapeDtypeStruct((chips, rows, WC), jnp.bfloat16),
+        add_pair_kernel,
+        out_shape=jax.ShapeDtypeStruct(half, jnp.bfloat16),
         in_specs=[VMEM, VMEM],
         out_specs=VMEM,
-        compiler_params=pltpu.CompilerParams(vmem_limit_bytes=8 * MIB),
-        name="add_core",
-    )(keep, swap(send, n))
+        compiler_params=small,
+        name="add_pair",
+    )(mine, got)
     return pl.pallas_call(
         add_chips_kernel,
         out_shape=jax.ShapeDtypeStruct((rows, WC), jnp.float32),
         in_specs=[VMEM],
         out_specs=VMEM,
-        compiler_params=pltpu.CompilerParams(vmem_limit_bytes=4 * MIB),
+        compiler_params=small,
         name="add_chips",
-    )(plane_exchange(summed, n))
+    )(exchange(summed, n, 4))
 
 
 def gather_body(grad_out, activations, basis_out, basis_in, eigenvalues, tile_order, block_map):

time: 97.2 us -> 92.5 us (0.952)
  waiting for transfers between devices: 17.6 us -> 29.9 us
  blocking collectives: 16.9 us -> 9.8 us
  Pallas kernels: 27 us -> 23.6 us
  starting transfers between devices: 26.3 us -> 23.1 us
  other arithmetic: 4.36 us -> 2.53 us
  local copies, waits for them, and re-layouts: 4.36 us -> 3.04 us
    ppermute x3 -> x5, waiting for transfers between devices: 2.58 us -> 14.6 us  [the longest x2 7.23 us: ring_body(): got = lax.ppermute(both, 'blk', xor_pairs(n, key))]
    all_to_all x1, blocking collectives: 16.9 us -> 9.8 us  [exchange(): return lax.all_to_all(x, 'blk', 0, 0, axis_index_groups=groups, tiled=True)]
    all_to_all x2 -> x1, starting transfers between devices: 10.7 us -> 5.35 us  [exchange(): return lax.all_to_all(x, 'blk', 0, 0, axis_index_groups=groups, tiled=True)]
    ppermute x4, starting transfers between devices: 5.78 us -> 1.31 us  [ring_body(): to_right = lambda x: lax.ppermute(x, 'blk', shift_pairs(n, 1))]
    ppermute x3 -> x5, starting transfers between devices: 5.89 us -> 9.02 us  [the longest x2 4.82 us: ring_body(): got = lax.ppermute(both, 'blk', xor_pairs(n, key))]
    ppermute x3, starting transfers between devices: 1.92 us -> 4.88 us  [ring_body(): to_left = lambda x: lax.ppermute(x, 'blk', shift_pairs(n, -1))]
    concatenate x4 -> x7, other arithmetic: 4.36 us -> 1.61 us  [the longest x1 0.62 us: ring_body(): grads = jnp.concatenate([grads, got], axis=0).reshape(tokens // 2, full_out)]
    ppermute x12, waiting for transfers between devices: 3.32 us -> 5.59 us  [swap(): return lax.ppermute(x, 'blk', xor_pairs(n, 1))]
  transfers between devices with their start and end apart: 24 -> 25, of which waited for: 8 -> 12; matrix products, arithmetic and copies ran while one was open for 4% -> 2% of each run, Pallas kernels for 24% -> 23%
where the time goes in v6:
time: 92.5 us; the launch traced here: 92.2 us
  waiting for transfers between devices  29.9 us (32%)
  Pallas kernels  23.6 us (26%)
  starting transfers between devices  23.1 us (25%)
  blocking collectives  9.8 us (11%)
  local copies, waits for them, and re-layouts  3.04 us (3%)
  other arithmetic  2.53 us (3%)
    all_to_all x1, blocking collectives, exchange(): return lax.all_to_all(x, 'blk', 0, 0, axis_index_groups=groups, tiled=True)  9.8 us
    pallas_call x1, Pallas kernels, ring_body(): pl.pallas_call(functools.partial(rotate_out_kernel, tok_rows), out_shape=...  9.23 us
    all_to_all x1, waiting for transfers between devices, exchange(): return lax.all_to_all(x, 'blk', 0, 0, axis_index_groups=groups, tiled=True)  7.32 us
    ppermute x2, waiting for transfers between devices, ring_body(): got = lax.ppermute(both, 'blk', xor_pairs(n, key))  7.23 us
    ppermute x1, waiting for transfers between devices, ring_body(): got = lax.ppermute(send, 'blk', xor_pairs(n, 2))  6.38 us
    pallas_call x1, Pallas kernels, ring_body(): pl.pallas_call(functools.partial(scale_kernel, begun), out_shape=jax.Shap...  6.24 us
    ppermute x12, waiting for transfers between devices, swap(): return lax.ppermute(x, 'blk', xor_pairs(n, 1))  5.59 us
    all_to_all x1, starting transfers between devices, exchange(): return lax.all_to_all(x, 'blk', 0, 0, axis_index_groups=groups, tiled=True)  5.35 us
  transfers between devices with their start and end apart: 25, of which 12 were waited for; matrix products, arithmetic and copies ran while one was open for 2% of the time, Pallas kernels for 23%

profile of v6, /device:TPU:0, one launch (start us, length us, event | category | flops | bytes accessed | tf_op | source)
XLA Modules:
  0.0 92.2 jit_solution(11643996478957850176)
XLA Ops:
  0.9 4.1 %collective-permute-start = (bf16[1,2,18432]{2,1,0:T(2,128)(2,1)S(1)}, bf16[1,2,18432]{2,1,0:T(2,128)(2,1)S(1)}, u32[]{:S(2)}, u32[]{:S(2)}) collective-permute-start(bf16[1,2,18432]{2,1,0:T(2,128)(2,1)S(1)} %maximum_bitcast_fusion), channel_id=1, source_target_pairs={{0,8},{1,9},{2,10},{3,11},{4,12},{5,13},{6,14},{7,15},{8,0},{9,1},... | collective-permute-start | bytes 221192 | tf_op jit(solution)/shard_map/ppermute | solution.py:257
  5.0 1.0 %slice.16 = bf16[512,256]{1,0:T(8,128)(2,1)S(1)} slice(bf16[4096,256]{1,0:T(8,128)(2,1)} %basis_ref.2), slice={[0:512], [0:256]} | slice | bytes 524288 | tf_op jit(solution)/shard_map/slice | solution.py:252
  6.1 2.8 %collective-permute-done = bf16[1,2,18432]{2,1,0:T(2,128)(2,1)S(1)} collective-permute-done((bf16[1,2,18432]{2,1,0:T(2,128)(2,1)S(1)}, bf16[1,2,18432]{2,1,0:T(2,128)(2,1)S(1)}, u32[]{:S(2)}, u32[]{:S(2)}) %collective-permute-start) | collective-permute-done | bytes 73760 | tf_op jit(solution)/shard_map/ppermute | solution.py:257
  9.9 4.4 %collective-permute-done.1 = bf16[2,2,18432]{2,1,0:T(2,128)(2,1)S(1)} collective-permute-done((bf16[2,2,18432]{2,1,0:T(2,128)(2,1)S(1)}, bf16[2,2,18432]{2,1,0:T(2,128)(2,1)S(1)}, u32[]{:S(2)}, u32[]{:S(2)}) %collective-permute-start.1) | collective-permute-done | bytes 147488 | tf_op jit(solution)/shard_map/ppermute | solution.py:257
  14.5 1.8 %collective-permute-start.3 = (bf16[4,2,4096]{2,1,0:T(2,128)(2,1)S(1)}, bf16[4,2,4096]{2,1,0:T(2,128)(2,1)S(1)}, u32[]{:S(2)}, u32[]{:S(2)}) collective-permute-start(bf16[4,2,4096]{2,1,0:T(2,128)(2,1)S(1)} %pad_maximum_fusion.4), channel_id=1, source_target_pairs={{0,2},{1,3},{2,0},{3,1},{4,6},{5,7},{6,4},{7,5},{8,10},{9,11},{10,... | collective-permute-start | bytes 196616 | tf_op jit(solution)/shard_map/ppermute | solution.py:270
  17.4 1.2 %collective-permute-start.6 = (bf16[256,512]{1,0:T(8,128)(2,1)S(1)}, bf16[256,512]{1,0:T(8,128)(2,1)S(1)}, u32[]{:S(2)}, u32[]{:S(2)}) collective-permute-start(bf16[256,512]{1,0:T(8,128)(2,1)S(1)} %bitcast.4), channel_id=1, source_target_pairs={{0,2},{1,3},{4,0},{5,1},{8,4},{9,5},{12,8},{13,9},{14,12},{15,13},... | collective-permute-start | bytes 786440 | tf_op jit(solution)/shard_map/ppermute | solution.py:249
  18.6 1.0 %collective-permute-done.3 = bf16[4,2,4096]{2,1,0:T(2,128)(2,1)S(1)} collective-permute-done((bf16[4,2,4096]{2,1,0:T(2,128)(2,1)S(1)}, bf16[4,2,4096]{2,1,0:T(2,128)(2,1)S(1)}, u32[]{:S(2)}, u32[]{:S(2)}) %collective-permute-start.3) | collective-permute-done | bytes 65568 | tf_op jit(solution)/shard_map/ppermute | solution.py:270
  20.2 1.8 %collective-permute-start.2 = (bf16[4,2,14336]{2,1,0:T(2,128)(2,1)S(1)}, bf16[4,2,14336]{2,1,0:T(2,128)(2,1)S(1)}, u32[]{:S(2)}, u32[]{:S(2)}) collective-permute-start(bf16[4,2,14336]{2,1,0:T(2,128)(2,1)S(1)} %pad_maximum_fusion.1), channel_id=1, source_target_pairs={{0,2},{1,3},{2,0},{3,1},{4,6},{5,7},{6,4},{7,5},{8,10},{9,11},{10,... | collective-permute-start | bytes 688136 | tf_op jit(solution)/shard_map/ppermute | solution.py:281
  22.0 1.6 %copy-done = bf16[4096,256]{1,0:T(8,128)(2,1)S(1)} copy-done((bf16[4096,256]{1,0:T(8,128)(2,1)S(1)}, bf16[4096,256]{1,0:T(8,128)(2,1)}, u32[]{:S(2)}) %copy-start) | copy-done | bytes 2097176
  23.6 1.2 %rotate_in.1 = bf16[8,32,256]{2,1,0:T(8,128)(2,1)} custom-call(bf16[16,4096]{1,0:T(8,128)(2,1)S(1)} %reshape.6.near_ref, bf16[16,4096]{1,0:T(8,128)(2,1)S(1)} %collective-permute-done.4.far_ref, bf16[4096,256]{1,0:T(8,128)(2,1)S(1)} %copy-done), custom_call_target="tpu_custom_call" | custom-call | tf_op jit(solution)/shard_map/rotate_in/pallas_call | solution.py:272
  24.8 5.4 %all-to-all-start = ((bf16[8,32,256]{2,1,0:T(8,128)(2,1)}), bf16[8,32,256]{2,1,0:T(8,128)(2,1)S(1)}, u32[]{:S(2)}, u32[]{:S(2)}) async-start(bf16[8,32,256]{2,1,0:T(8,128)(2,1)} %rotate_in.1), calls=%async_computation | async-start | bytes 262144 | tf_op jit(solution)/shard_map/all_to_all | solution.py:48
  30.2 7.3 %all-to-all-done.near_ref = bf16[8,32,256]{2,1,0:T(8,128)(2,1)S(1)} async-done(((bf16[8,32,256]{2,1,0:T(8,128)(2,1)}), bf16[8,32,256]{2,1,0:T(8,128)(2,1)S(1)}, u32[]{:S(2)}, u32[]{:S(2)}) %all-to-all-start) | async-done | bytes 131104 | tf_op jit(solution)/shard_map/all_to_all | solution.py:48
  39.5 1.1 %collective-permute-done.9.refs_1_ = bf16[256,512]{1,0:T(8,128)(2,1)S(1)} collective-permute-done((bf16[256,512]{1,0:T(8,128)(2,1)S(1)}, bf16[256,512]{1,0:T(8,128)(2,1)S(1)}, u32[]{:S(2)}, u32[]{:S(2)}) %collective-permute-start.9) | collective-permute-done | bytes 262176 | tf_op jit(solution)/shard_map/ppermute | solution.py:43
  40.8 1.8 %collective-permute-start.13 = (bf16[256,512]{1,0:T(8,128)(2,1)S(1)}, bf16[256,512]{1,0:T(8,128)(2,1)S(1)}, u32[]{:S(2)}, u32[]{:S(2)}) collective-permute-start(bf16[256,512]{1,0:T(8,128)(2,1)S(1)} %collective-permute-done.6.refs_4_), channel_id=1, source_target_pairs={{0,2},{1,3},{4,0},{5,1},{8,4},{9,5},{12,8},{13,9},{14,12},{15,13},... | collective-permute-start | bytes 786440 | tf_op jit(solution)/shard_map/ppermute | solution.py:249
  42.6 9.2 %rotate_out.1.aligned_ref = bf16[896,32]{1,0:T(8,128)(2,1)S(1)} custom-call(bf16[16,14336]{1,0:T(8,128)(2,1)S(1)} %reshape.7.near_ref, bf16[16,14336]{1,0:T(8,128)(2,1)S(1)} %collective-permute-done.7.far_ref, bf16[14336,896]{1,0:T(8,128)(2,1)} %basis_out_ref.1, s32[16]{0:T(128)S(1)} %copy-done.2), custom_call_target="tpu_custom_call" | custom-call | flops 822083584 | bytes 25690112 | tf_op jit(solution)/shard_map/rotate_out/pallas_call | solution.py:293
  52.1 1.8 %collective-permute-start.15 = (bf16[256,512]{1,0:T(8,128)(2,1)S(1)}, bf16[256,512]{1,0:T(8,128)(2,1)S(1)}, u32[]{:S(2)}, u32[]{:S(2)}) collective-permute-start(bf16[256,512]{1,0:T(8,128)(2,1)S(1)} %collective-permute-done.13.refs_8_), channel_id=1, source_target_pairs={{0,2},{1,3},{4,0},{5,1},{8,4},{9,5},{12,8},{13,9},{14,12},{15,13},... | collective-permute-start | bytes 786440 | tf_op jit(solution)/shard_map/ppermute | solution.py:249
  54.5 6.2 %scale.1.scaled_ref = bf16[896,4096]{1,0:T(8,128)(2,1)S(1)} custom-call(bf16[896,32]{1,0:T(8,128)(2,1)S(1)} %rotate_out.1.aligned_ref, bf16[8,32,256]{2,1,0:T(8,128)(2,1)S(1)} %all-to-all-done.near_ref, bf16[8,32,256]{2,1,0:T(8,128)(2,1)S(1)} %collective-permute-done.8.far_ref, s32[32]{0:T(128)S(1)} %copy-done.1, f32[896,4096]{1,0:T(8,128)} %eigen_ref.1), custom_call_target="tpu_custom_call" | custom-call | flops 234881024 | bytes 22020096 | tf_op jit(solution)/shard_map/scale/pallas_call | solution.py:318
  62.7 4.5 %project.1 = (f32[896,512]{1,0:T(8,128)S(1)}, bf16[768,896]{1,0:T(8,128)(2,1)S(1)}) custom-call(bf16[896,4096]{1,0:T(8,128)(2,1)S(1)} %scale.1.scaled_ref, bf16[14336,896]{1,0:T(8,128)(2,1)} %basis_out_ref.1, bf16[256,512]{1,0:T(8,128)(2,1)S(1)} %bitcast.6, bf16[256,512]{1,0:T(8,128)(2,1)S(1)} %collective-permute-done.9.refs_1_, ...), custom_call_target="tpu_custom_call" | custom-call | flops 3758096384 | bytes 11534336 | tf_op jit(solution)/shard_map/project/pallas_call | solution.py:343
  67.2 2.4 %collective-permute-done.20.refs_0_ = bf16[256,512]{1,0:T(8,128)(2,1)S(1)} collective-permute-done((bf16[256,512]{1,0:T(8,128)(2,1)S(1)}, bf16[256,512]{1,0:T(8,128)(2,1)S(1)}, u32[]{:S(2)}, u32[]{:S(2)}) %collective-permute-start.20) | collective-permute-done | bytes 262176 | tf_op jit(solution)/shard_map/ppermute | solution.py:248
  69.6 1.5 %collective-permute-done.21.refs_1_ = bf16[256,512]{1,0:T(8,128)(2,1)S(1)} collective-permute-done((bf16[256,512]{1,0:T(8,128)(2,1)S(1)}, bf16[256,512]{1,0:T(8,128)(2,1)S(1)}, u32[]{:S(2)}, u32[]{:S(2)}) %collective-permute-start.21) | collective-permute-done | bytes 262176 | tf_op jit(solution)/shard_map/ppermute | solution.py:43
  71.2 1.6 %window.1 = (bf16[8,48,512]{2,1,0:T(8,128)(2,1)S(1)}, f32[8,48,512]{2,1,0:T(8,128)S(1)}) custom-call(bf16[768,896]{1,0:T(8,128)(2,1)S(1)} %get-tuple-element.49.window_ref, bf16[896,4096]{1,0:T(8,128)(2,1)S(1)} %scale.1.scaled_ref, f32[896,512]{1,0:T(8,128)S(1)} %get-tuple-element.51.projected_ref, bf16[256,512]{1,0:T(8,128)(2,1)S(1)} %collective-permute-done.20.refs_0_, ...), custom_call_target="tpu_custom_call" | custom-call | flops 704643072 | bytes 6094848 | tf_op jit(solution)/shard_map/window/pallas_call | solution.py:366
  73.0 1.6 %collective-permute-done.22.got_ref = bf16[8,48,512]{2,1,0:T(8,128)(2,1)S(1)} collective-permute-done((bf16[8,48,512]{2,1,0:T(8,128)(2,1)S(1)}, bf16[8,48,512]{2,1,0:T(8,128)(2,1)S(1)}, u32[]{:S(2)}, u32[]{:S(2)}) %collective-permute-start.22) | collective-permute-done | bytes 393248 | tf_op jit(solution)/shard_map/ppermute | solution.py:43
  75.3 6.4 %collective-permute-done.23.got_ref = bf16[4,48,512]{2,1,0:T(8,128)(2,1)S(1)} collective-permute-done((bf16[4,48,512]{2,1,0:T(8,128)(2,1)S(1)}, bf16[4,48,512]{2,1,0:T(8,128)(2,1)S(1)}, u32[]{:S(2)}, u32[]{:S(2)}) %collective-permute-start.23) | collective-permute-done | bytes 196640 | tf_op jit(solution)/shard_map/ppermute | solution.py:397
  81.7 9.8 %all_to_all.10.parts_ref = bf16[4,48,512]{2,1,0:T(8,128)(2,1)S(1)} all-to-all(bf16[4,48,512]{2,1,0:T(8,128)(2,1)S(1)} %add_pair.1), channel_id=1, replica_groups={{0,4,8,12},{1,5,9,13},{2,6,10,14},{3,7,11,15},{16,20,24,28},{17,21,25,2..., dimensions={0} | all-to-all | bytes 393216 | tf_op jit(solution)/shard_map/all_to_all | solution.py:48
  (55 shorter events, 10.4 us)
Async XLA Ops:
  0.9 8.0 %collective-permute-start = (bf16[1,2,18432]{2,1,0:T(2,128)(2,1)S(1)}, bf16[1,2,18432]{2,1,0:T(2,128)(2,1)S(1)}, u32[]{:S(2)}, u32[]{:S(2)}) collective-permute-start(bf16[1,2,18432]{2,1,0:T(2,128)(2,1)S(1)} %maximum_bitcast_fusion), channel_id=1, source_target_pairs={{0,8},{1,9},{2,10},{3,11},{4,12},{5,13},{6,14},{7,15},{8,0},{9,1},... | collective-permute-start | bytes 221192 | tf_op jit(solution)/shard_map/ppermute | solution.py:257
  9.1 5.2 %collective-permute-start.1 = (bf16[2,2,18432]{2,1,0:T(2,128)(2,1)S(1)}, bf16[2,2,18432]{2,1,0:T(2,128)(2,1)S(1)}, u32[]{:S(2)}, u32[]{:S(2)}) collective-permute-start(bf16[2,2,18432]{2,1,0:T(2,128)(2,1)S(1)} %pad_maximum_fusion.3), channel_id=1, source_target_pairs={{0,4},{1,5},{2,6},{3,7},{4,0},{5,1},{6,2},{7,3},{8,12},{9,13},{10,... | collective-permute-start | bytes 442376 | tf_op jit(solution)/shard_map/ppermute | solution.py:257
  14.5 5.1 %collective-permute-start.3 = (bf16[4,2,4096]{2,1,0:T(2,128)(2,1)S(1)}, bf16[4,2,4096]{2,1,0:T(2,128)(2,1)S(1)}, u32[]{:S(2)}, u32[]{:S(2)}) collective-permute-start(bf16[4,2,4096]{2,1,0:T(2,128)(2,1)S(1)} %pad_maximum_fusion.4), channel_id=1, source_target_pairs={{0,2},{1,3},{2,0},{3,1},{4,6},{5,7},{6,4},{7,5},{8,10},{9,11},{10,... | collective-permute-start | bytes 196616 | tf_op jit(solution)/shard_map/ppermute | solution.py:270
  16.5 13.6 %collective-permute-start.5 = (bf16[256,512]{1,0:T(8,128)(2,1)S(1)}, bf16[256,512]{1,0:T(8,128)(2,1)S(1)}, u32[]{:S(2)}, u32[]{:S(2)}) collective-permute-start(bf16[256,512]{1,0:T(8,128)(2,1)S(1)} %bitcast.3), channel_id=1, source_target_pairs={{0,4},{1,5},{4,8},{5,9},{8,12},{9,13},{12,14},{13,15},{14,10},{15,... | collective-permute-start | bytes 786440 | tf_op jit(solution)/shard_map/ppermute | solution.py:248
  17.4 12.8 %collective-permute-start.6 = (bf16[256,512]{1,0:T(8,128)(2,1)S(1)}, bf16[256,512]{1,0:T(8,128)(2,1)S(1)}, u32[]{:S(2)}, u32[]{:S(2)}) collective-permute-start(bf16[256,512]{1,0:T(8,128)(2,1)S(1)} %bitcast.4), channel_id=1, source_target_pairs={{0,2},{1,3},{4,0},{5,1},{8,4},{9,5},{12,8},{13,9},{14,12},{15,13},... | collective-permute-start | bytes 786440 | tf_op jit(solution)/shard_map/ppermute | solution.py:249
  19.8 2.1 %collective-permute-start.4 = (bf16[16,4096]{1,0:T(8,128)(2,1)S(1)}, bf16[16,4096]{1,0:T(8,128)(2,1)S(1)}, u32[]{:S(2)}, u32[]{:S(2)}) collective-permute-start(bf16[16,4096]{1,0:T(8,128)(2,1)S(1)} %reshape.6.near_ref), channel_id=1, source_target_pairs={{0,1},{1,0},{2,3},{3,2},{4,5},{5,4},{6,7},{7,6},{8,9},{9,8},{10,11... | collective-permute-start | bytes 393224 | tf_op jit(solution)/shard_map/ppermute | solution.py:43
  20.2 9.9 %collective-permute-start.2 = (bf16[4,2,14336]{2,1,0:T(2,128)(2,1)S(1)}, bf16[4,2,14336]{2,1,0:T(2,128)(2,1)S(1)}, u32[]{:S(2)}, u32[]{:S(2)}) collective-permute-start(bf16[4,2,14336]{2,1,0:T(2,128)(2,1)S(1)} %pad_maximum_fusion.1), channel_id=1, source_target_pairs={{0,2},{1,3},{2,0},{3,1},{4,6},{5,7},{6,4},{7,5},{8,10},{9,11},{10,... | collective-permute-start | bytes 688136 | tf_op jit(solution)/shard_map/ppermute | solution.py:281
  24.8 12.7 %all-to-all-start = ((bf16[8,32,256]{2,1,0:T(8,128)(2,1)}), bf16[8,32,256]{2,1,0:T(8,128)(2,1)S(1)}, u32[]{:S(2)}, u32[]{:S(2)}) async-start(bf16[8,32,256]{2,1,0:T(8,128)(2,1)} %rotate_in.1), calls=%async_computation | async-start | bytes 262144 | tf_op jit(solution)/shard_map/all_to_all | solution.py:48
  38.3 4.3 %collective-permute-start.7 = (bf16[16,14336]{1,0:T(8,128)(2,1)S(1)}, bf16[16,14336]{1,0:T(8,128)(2,1)S(1)}, u32[]{:S(2)}, u32[]{:S(2)}) collective-permute-start(bf16[16,14336]{1,0:T(8,128)(2,1)S(1)} %reshape.7.near_ref), channel_id=1, source_target_pairs={{0,1},{1,0},{2,3},{3,2},{4,5},{5,4},{6,7},{7,6},{8,9},{9,8},{10,11... | collective-permute-start | bytes 1376264 | tf_op jit(solution)/shard_map/ppermute | solution.py:43
  38.4 2.2 %collective-permute-start.9 = (bf16[256,512]{1,0:T(8,128)(2,1)S(1)}, bf16[256,512]{1,0:T(8,128)(2,1)S(1)}, u32[]{:S(2)}, u32[]{:S(2)}) collective-permute-start(bf16[256,512]{1,0:T(8,128)(2,1)S(1)} %bitcast.5), channel_id=1, source_target_pairs={{0,1},{1,0},{2,3},{3,2},{4,5},{5,4},{6,7},{7,6},{8,9},{9,8},{10,11... | collective-permute-start | bytes 786440 | tf_op jit(solution)/shard_map/ppermute | solution.py:43
  38.9 1.9 %collective-permute-start.8 = (bf16[8,32,256]{2,1,0:T(8,128)(2,1)S(1)}, bf16[8,32,256]{2,1,0:T(8,128)(2,1)S(1)}, u32[]{:S(2)}, u32[]{:S(2)}) collective-permute-start(bf16[8,32,256]{2,1,0:T(8,128)(2,1)S(1)} %all-to-all-done.near_ref), channel_id=1, source_target_pairs={{0,1},{1,0},{2,3},{3,2},{4,5},{5,4},{6,7},{7,6},{8,9},{9,8},{10,11... | collective-permute-start | bytes 393224 | tf_op jit(solution)/shard_map/ppermute | solution.py:43
  39.0 3.6 %collective-permute-start.10 = (bf16[256,512]{1,0:T(8,128)(2,1)S(1)}, bf16[256,512]{1,0:T(8,128)(2,1)S(1)}, u32[]{:S(2)}, u32[]{:S(2)}) collective-permute-start(bf16[256,512]{1,0:T(8,128)(2,1)S(1)} %collective-permute-done.5.refs_2_), channel_id=1, source_target_pairs={{0,1},{1,0},{2,3},{3,2},{4,5},{5,4},{6,7},{7,6},{8,9},{9,8},{10,11... | collective-permute-start | bytes 786440 | tf_op jit(solution)/shard_map/ppermute | solution.py:43
  39.4 3.2 %collective-permute-start.11 = (bf16[256,512]{1,0:T(8,128)(2,1)S(1)}, bf16[256,512]{1,0:T(8,128)(2,1)S(1)}, u32[]{:S(2)}, u32[]{:S(2)}) collective-permute-start(bf16[256,512]{1,0:T(8,128)(2,1)S(1)} %collective-permute-done.6.refs_4_), channel_id=1, source_target_pairs={{0,1},{1,0},{2,3},{3,2},{4,5},{5,4},{6,7},{7,6},{8,9},{9,8},{10,11... | collective-permute-start | bytes 786440 | tf_op jit(solution)/shard_map/ppermute | solution.py:43
  40.6 11.3 %collective-permute-start.12 = (bf16[256,512]{1,0:T(8,128)(2,1)S(1)}, bf16[256,512]{1,0:T(8,128)(2,1)S(1)}, u32[]{:S(2)}, u32[]{:S(2)}) collective-permute-start(bf16[256,512]{1,0:T(8,128)(2,1)S(1)} %collective-permute-done.5.refs_2_), channel_id=1, source_target_pairs={{0,4},{1,5},{4,8},{5,9},{8,12},{9,13},{12,14},{13,15},{14,10},{15,... | collective-permute-start | bytes 786440 | tf_op jit(solution)/shard_map/ppermute | solution.py:248
  40.8 11.1 %collective-permute-start.13 = (bf16[256,512]{1,0:T(8,128)(2,1)S(1)}, bf16[256,512]{1,0:T(8,128)(2,1)S(1)}, u32[]{:S(2)}, u32[]{:S(2)}) collective-permute-start(bf16[256,512]{1,0:T(8,128)(2,1)S(1)} %collective-permute-done.6.refs_4_), channel_id=1, source_target_pairs={{0,2},{1,3},{4,0},{5,1},{8,4},{9,5},{12,8},{13,9},{14,12},{15,13},... | collective-permute-start | bytes 786440 | tf_op jit(solution)/shard_map/ppermute | solution.py:249
  51.9 8.8 %collective-permute-start.14 = (bf16[256,512]{1,0:T(8,128)(2,1)S(1)}, bf16[256,512]{1,0:T(8,128)(2,1)S(1)}, u32[]{:S(2)}, u32[]{:S(2)}) collective-permute-start(bf16[256,512]{1,0:T(8,128)(2,1)S(1)} %collective-permute-done.12.refs_6_), channel_id=1, source_target_pairs={{0,4},{1,5},{4,8},{5,9},{8,12},{9,13},{12,14},{13,15},{14,10},{15,... | collective-permute-start | bytes 786440 | tf_op jit(solution)/shard_map/ppermute | solution.py:248
  52.1 8.6 %collective-permute-start.15 = (bf16[256,512]{1,0:T(8,128)(2,1)S(1)}, bf16[256,512]{1,0:T(8,128)(2,1)S(1)}, u32[]{:S(2)}, u32[]{:S(2)}) collective-permute-start(bf16[256,512]{1,0:T(8,128)(2,1)S(1)} %collective-permute-done.13.refs_8_), channel_id=1, source_target_pairs={{0,2},{1,3},{4,0},{5,1},{8,4},{9,5},{12,8},{13,9},{14,12},{15,13},... | collective-permute-start | bytes 786440 | tf_op jit(solution)/shard_map/ppermute | solution.py:249
  54.0 7.5 %collective-permute-start.16 = (bf16[256,512]{1,0:T(8,128)(2,1)S(1)}, bf16[256,512]{1,0:T(8,128)(2,1)S(1)}, u32[]{:S(2)}, u32[]{:S(2)}) collective-permute-start(bf16[256,512]{1,0:T(8,128)(2,1)S(1)} %collective-permute-done.12.refs_6_), channel_id=1, source_target_pairs={{0,1},{1,0},{2,3},{3,2},{4,5},{5,4},{6,7},{7,6},{8,9},{9,8},{10,11... | collective-permute-start | bytes 786440 | tf_op jit(solution)/shard_map/ppermute | solution.py:43
  54.0 7.5 %collective-permute-start.17 = (bf16[256,512]{1,0:T(8,128)(2,1)S(1)}, bf16[256,512]{1,0:T(8,128)(2,1)S(1)}, u32[]{:S(2)}, u32[]{:S(2)}) collective-permute-start(bf16[256,512]{1,0:T(8,128)(2,1)S(1)} %collective-permute-done.13.refs_8_), channel_id=1, source_target_pairs={{0,1},{1,0},{2,3},{3,2},{4,5},{5,4},{6,7},{7,6},{8,9},{9,8},{10,11... | collective-permute-start | bytes 786440 | tf_op jit(solution)/shard_map/ppermute | solution.py:43
  60.8 1.6 %collective-permute-start.18 = (bf16[256,512]{1,0:T(8,128)(2,1)S(1)}, bf16[256,512]{1,0:T(8,128)(2,1)S(1)}, u32[]{:S(2)}, u32[]{:S(2)}) collective-permute-start(bf16[256,512]{1,0:T(8,128)(2,1)S(1)} %collective-permute-done.14.refs_10_), channel_id=1, source_target_pairs={{0,1},{1,0},{2,3},{3,2},{4,5},{5,4},{6,7},{7,6},{8,9},{9,8},{10,11... | collective-permute-start | bytes 786440 | tf_op jit(solution)/shard_map/ppermute | solution.py:43
  60.8 1.9 %collective-permute-start.19 = (bf16[256,512]{1,0:T(8,128)(2,1)S(1)}, bf16[256,512]{1,0:T(8,128)(2,1)S(1)}, u32[]{:S(2)}, u32[]{:S(2)}) collective-permute-start(bf16[256,512]{1,0:T(8,128)(2,1)S(1)} %collective-permute-done.15.refs_12_), channel_id=1, source_target_pairs={{0,1},{1,0},{2,3},{3,2},{4,5},{5,4},{6,7},{7,6},{8,9},{9,8},{10,11... | collective-permute-start | bytes 786440 | tf_op jit(solution)/shard_map/ppermute | solution.py:43
  61.3 8.3 %collective-permute-start.20 = (bf16[256,512]{1,0:T(8,128)(2,1)S(1)}, bf16[256,512]{1,0:T(8,128)(2,1)S(1)}, u32[]{:S(2)}, u32[]{:S(2)}) collective-permute-start(bf16[256,512]{1,0:T(8,128)(2,1)S(1)} %collective-permute-done.14.refs_10_), channel_id=1, source_target_pairs={{0,4},{1,5},{4,8},{5,9},{8,12},{9,13},{12,14},{13,15},{14,10},{15,... | collective-permute-start | bytes 786440 | tf_op jit(solution)/shard_map/ppermute | solution.py:248
  72.8 1.8 %collective-permute-start.22 = (bf16[8,48,512]{2,1,0:T(8,128)(2,1)S(1)}, bf16[8,48,512]{2,1,0:T(8,128)(2,1)S(1)}, u32[]{:S(2)}, u32[]{:S(2)}) collective-permute-start(bf16[8,48,512]{2,1,0:T(8,128)(2,1)S(1)} %get-tuple-element.54), channel_id=1, source_target_pairs={{0,1},{1,0},{2,3},{3,2},{4,5},{5,4},{6,7},{7,6},{8,9},{9,8},{10,11... | collective-permute-start | bytes 1179656 | tf_op jit(solution)/shard_map/ppermute | solution.py:43
  74.6 7.0 %collective-permute-start.23 = (bf16[4,48,512]{2,1,0:T(8,128)(2,1)S(1)}, bf16[4,48,512]{2,1,0:T(8,128)(2,1)S(1)}, u32[]{:S(2)}, u32[]{:S(2)}) collective-permute-start(bf16[4,48,512]{2,1,0:T(8,128)(2,1)S(1)} %get-tuple-element.56), channel_id=1, source_target_pairs={{0,2},{1,3},{2,0},{3,1},{4,6},{5,7},{6,4},{7,5},{8,10},{9,11},{10,... | collective-permute-start | bytes 589832 | tf_op jit(solution)/shard_map/ppermute | solution.py:397
  (4 other events, 61.9 us)

commit v7 on v6

--- a/solution.py
+++ b/solution.py
@@ -72,7 +72,9 @@
 def rotate_in_kernel(tok_rows, near_ref, far_ref, basis_ref, out_ref):
     tokens = out_ref.shape[1]
     acts = jnp.concatenate([near_ref[...], far_ref[...]], axis=0)
-    rotated = jnp.dot(acts, basis_ref[...], preferred_element_type=jnp.float32)
+    rotated = lax.dot_general(
+        acts, basis_ref[...], (((1,), (1,)), ((), ())), preferred_element_type=jnp.float32
+    )
     wanted = lax.broadcasted_iota(jnp.int32, (tokens, tokens), 0)
     held = held_tokens(lax.axis_index("blk"), tokens, tok_rows)
     ordered = reorder(wanted, held, rotated).astype(jnp.bfloat16)
@@ -196,12 +198,9 @@
     chips, rows, _ = keep_ref.shape
     width = pieces[0].shape[0]
     total = projected_ref[...]
-    for at, piece in enumerate(pieces, scaled_ref.shape[1] // width - len(pieces)):
-        total += jnp.dot(
-            scaled_ref[:, at * width : (at + 1) * width],
-            piece[...],
-            preferred_element_type=jnp.float32,
-        )
+    first = scaled_ref.shape[1] - width * len(pieces)
+    basis = jnp.concatenate([piece[...] for piece in pieces], axis=0)
+    total += jnp.dot(scaled_ref[:, first:], basis, preferred_element_type=jnp.float32)
     result[...] = scale * jnp.dot(
         window_ref[...], total.astype(jnp.bfloat16), preferred_element_type=jnp.float32
     )
@@ -222,12 +221,20 @@
         send_ref[pair] = sent.astype(jnp.bfloat16)
 
 
-def add_pair_kernel(mine_ref, got_ref, out_ref):
-    out_ref[...] = (mine_ref[...] + got_ref[...].astype(jnp.float32)).astype(jnp.bfloat16)
-
-
-def add_chips_kernel(parts_ref, out_ref):
-    out_ref[...] = jnp.sum(parts_ref[...].astype(jnp.float32), axis=0)
+def add_pair_kernel(mine_ref, got_ref, own_ref, *send_refs):
+    me = lax.axis_index("blk") // 4
+    own_ref[...] = mine_ref[me] + got_ref[me].astype(jnp.float32)
+    for key, send_ref in enumerate(send_refs, 1):
+        other = me ^ key
+        sent = mine_ref[other] + got_ref[other].astype(jnp.float32)
+        send_ref[...] = sent.astype(jnp.bfloat16)
+
+
+def add_chips_kernel(own_ref, *refs):
+    total = own_ref[...]
+    for ref in refs[:-1]:
+        total += ref[...].astype(jnp.float32)
+    refs[-1][...] = total
 
 
 VMEM = pl.BlockSpec(memory_space=pltpu.VMEM)
@@ -249,7 +256,10 @@
     to_left = lambda x: lax.ppermute(x, "blk", shift_pairs(n, -1))
     steps = chips // 2
 
+    turned = basis_in.T
     own = basis_in[:WC].T
+
+    right, left = [own, to_right(own)], [own, to_left(own)]
 
     both = jnp.concatenate([grad_out, activations], axis=1)[None]
     key = n // 2
@@ -258,16 +268,14 @@
         key //= 2
         if key > 2:
             both = jnp.concatenate([both, got], axis=0)
-
-    got, own = after(got, own)
-    right, left = [own], [own]
-    while len(right) < max(steps - 2, 2):
-        right.append(to_right(right[-1]))
-        left.append(to_left(left[-1]))
-
+    got, turned = after(got, turned)
     acts = jnp.concatenate([both[..., full_out:], got[..., full_out:]], axis=0)
     grads = jnp.concatenate([both[..., :full_out], got[..., :full_out]], axis=0)
     got = lax.ppermute(acts, "blk", xor_pairs(n, 2))
+    got, right[-1], left[-1] = after(got, right[-1], left[-1])
+    while len(right) < steps - 1:
+        right.append(to_right(right[-1]))
+        left.append(to_left(left[-1]))
     acts = jnp.concatenate([acts, got], axis=0).reshape(tokens // 2, full_in)
     rotated = pl.pallas_call(
         functools.partial(rotate_in_kernel, tok_rows),
@@ -276,16 +284,12 @@
         out_specs=VMEM,
         compiler_params=pltpu.CompilerParams(vmem_limit_bytes=8 * MIB),
         name="rotate_in",
-    )(acts, swap(acts, n), basis_in)
-    rotated = exchange(rotated, n, 2)
+    )(acts, swap(acts, n), turned)
     got = lax.ppermute(grads, "blk", xor_pairs(n, 2))
     got, rotated, right[-1], left[-1] = after(got, rotated, right[-1], left[-1])
-    rotated_far = swap(rotated, n)
+    rotated = exchange(rotated, n, 2)
     grads = jnp.concatenate([grads, got], axis=0).reshape(tokens // 2, full_out)
     grads_far = swap(grads, n)
-    near = [right[0]] + [x for pair in zip(right[1:], left[1:]) for x in pair]
-    far = [swap(piece, n) for piece in near]
-    grads, grads_far, rotated_far, *far = after(grads, grads_far, rotated_far, *far)
     right.append(to_right(right[-1]))
     left.append(to_left(left[-1]))
 
@@ -310,9 +314,10 @@
         name="rotate_out",
     )(grads, grads_far, basis_out, block_map)
 
-    aligned, right[-1], left[-1] = after(aligned, right[-1], left[-1])
-    right.append(to_right(right[-1]))
-    left.append(to_left(left[-1]))
+    aligned, rotated, right[-1], left[-1] = after(aligned, rotated, right[-1], left[-1])
+    rotated_far = swap(rotated, n)
+    cut = in_width // 2
+    last = [to_right(right[-1][:cut]), to_left(left[-1][cut:])]
     begun = [0] + [at for step in range(1, steps) for at in (step, chips - step)] + [steps]
     blocks = 8
     scaled = pl.pallas_call(
@@ -334,11 +339,10 @@
         name="scale",
     )(aligned, rotated, rotated_far, tile_order, eigenvalues)
 
-    scaled, right[-1], left[-1] = after(scaled, right[-1], left[-1])
-    last = to_right(right[-1])
-    for at in begun[len(near) : -1]:
-        near.append(right[at] if at < steps else left[chips - at])
-        far.append(swap(near[-1], n))
+    scaled, *last = after(scaled, *last)
+    last += [swap(piece, n) for piece in last]
+    near = [right[at] if at < steps else left[chips - at] for at in begun[:-1]]
+    far = [swap(piece, n) for piece in near]
     pieces = [piece for pair in zip(near, far) for piece in pair]
     projected, window = pl.pallas_call(
         functools.partial(project_kernel, (0, 6, len(pieces))),
@@ -361,7 +365,6 @@
         name="project",
     )(scaled, basis_out, *pieces)
 
-    projected, last = after(projected, last)
     rows = WR // n
     send, keep = pl.pallas_call(
         functools.partial(window_kernel, 1.0 / tokens),
@@ -369,7 +372,7 @@
             jax.ShapeDtypeStruct((chips, rows, WC), jnp.bfloat16),
             jax.ShapeDtypeStruct((chips, rows, WC), jnp.float32),
         ),
-        in_specs=[VMEM] * 5,
+        in_specs=[VMEM] * 7,
         out_specs=(VMEM, VMEM),
         scratch_shapes=[pltpu.VMEM((WR, WC), jnp.float32)],
         compiler_params=pltpu.CompilerParams(vmem_limit_bytes=24 * MIB),
@@ -379,7 +382,7 @@
             transcendentals=0,
         ),
         name="window",
-    )(window, scaled, projected, last, swap(last, n))
+    )(window, scaled, projected, *last)
 
     small = pltpu.CompilerParams(vmem_limit_bytes=8 * MIB)
     half = (chips // 2, rows, WC)
@@ -395,22 +398,25 @@
         name="add_core",
     )(keep, swap(send, n))
     got = lax.ppermute(send, "blk", xor_pairs(n, 2))
-    summed = pl.pallas_call(
+    block = (rows, WC)
+    own, *sends = pl.pallas_call(
         add_pair_kernel,
-        out_shape=jax.ShapeDtypeStruct(half, jnp.bfloat16),
+        out_shape=[jax.ShapeDtypeStruct(block, jnp.float32)]
+        + [jax.ShapeDtypeStruct(block, jnp.bfloat16)] * (chips // 2 - 1),
         in_specs=[VMEM, VMEM],
-        out_specs=VMEM,
+        out_specs=[VMEM] * (chips // 2),
         compiler_params=small,
         name="add_pair",
     )(mine, got)
+    arrived = [lax.ppermute(x, "blk", xor_pairs(n, 4 * k)) for k, x in enumerate(sends, 1)]
     return pl.pallas_call(
         add_chips_kernel,
-        out_shape=jax.ShapeDtypeStruct((rows, WC), jnp.float32),
-        in_specs=[VMEM],
+        out_shape=jax.ShapeDtypeStruct(block, jnp.float32),
+        in_specs=[VMEM] * (chips // 2),
         out_specs=VMEM,
         compiler_params=small,
         name="add_chips",
-    )(exchange(summed, n, 4))
+    )(own, *arrived)
 
 
 def gather_body(grad_out, activations, basis_out, basis_in, eigenvalues, tile_order, block_map):

time: 92.5 us -> 92.7 us (level)
  blocking collectives: 9.8 us -> 0 us
  starting transfers between devices: 23.1 us -> 29.3 us
  other arithmetic: 2.53 us -> 4.8 us
  Pallas kernels: 23.6 us -> 24.8 us
  local copies, waits for them, and re-layouts: 3.04 us -> 4.21 us
  waiting for transfers between devices: 29.9 us -> 28.9 us
    all_to_all x1 -> x0, blocking collectives: 9.8 us -> none  [exchange(): return lax.all_to_all(x, 'blk', 0, 0, axis_index_groups=groups, tiled=True)]
    all_to_all x1, waiting for transfers between devices: 7.32 us -> 0.01 us  [exchange(): return lax.all_to_all(x, 'blk', 0, 0, axis_index_groups=groups, tiled=True)]
    ppermute x0 -> x3, waiting for transfers between devices: none -> 4.52 us  [ring_body(): lax.ppermute(x, 'blk', xor_pairs(n, 4 * k))]
    ppermute x0 -> x3, starting transfers between devices: none -> 4.45 us  [ring_body(): lax.ppermute(x, 'blk', xor_pairs(n, 4 * k))]
    ppermute x3 -> x4, waiting for transfers between devices: 0.01 us -> 2.99 us  [ring_body(): to_left = lambda x: lax.ppermute(x, 'blk', shift_pairs(n, -1))]
    ppermute x12 -> x13, waiting for transfers between devices: 5.59 us -> 2.98 us  [swap(): return lax.ppermute(x, 'blk', xor_pairs(n, 1))]
    ppermute x4, waiting for transfers between devices: 2.41 us -> 4.45 us  [ring_body(): to_right = lambda x: lax.ppermute(x, 'blk', shift_pairs(n, 1))]
    all_to_all x1, starting transfers between devices: 5.35 us -> 3.46 us  [exchange(): return lax.all_to_all(x, 'blk', 0, 0, axis_index_groups=groups, tiled=True)]
  transfers between devices with their start and end apart: 25 -> 30, of which waited for: 12 -> 11; matrix products, arithmetic and copies ran while one was open for 2% -> 7% of each run, Pallas kernels for 23% -> 24%
where the time goes in v7:
time: 92.7 us; the launch traced here: 92.4 us
  starting transfers between devices  29.3 us (32%)
  waiting for transfers between devices  28.9 us (31%)
  Pallas kernels  24.8 us (27%)
  other arithmetic  4.8 us (5%)
  local copies, waits for them, and re-layouts  4.21 us (5%)
    pallas_call x1, Pallas kernels, ring_body(): pl.pallas_call(functools.partial(rotate_out_kernel, tok_rows), out_shape=...  9.22 us
    ppermute x2, waiting for transfers between devices, ring_body(): got = lax.ppermute(both, 'blk', xor_pairs(n, key))  6.82 us
    ppermute x4, starting transfers between devices, ring_body(): to_left = lambda x: lax.ppermute(x, 'blk', shift_pairs(n, -1))  6.72 us
    pallas_call x1, Pallas kernels, ring_body(): pl.pallas_call(functools.partial(scale_kernel, begun), out_shape=jax.Shap...  6.23 us
    ppermute x2, starting transfers between devices, ring_body(): got = lax.ppermute(both, 'blk', xor_pairs(n, key))  5.74 us
    pallas_call x1, Pallas kernels, ring_body(): pl.pallas_call(functools.partial(project_kernel, (0, 6, len(pieces))), ou...  5.5 us
    ppermute x1, waiting for transfers between devices, ring_body(): got = lax.ppermute(send, 'blk', xor_pairs(n, 2))  5.48 us
    ppermute x3, waiting for transfers between devices, ring_body(): lax.ppermute(x, 'blk', xor_pairs(n, 4 * k))  4.52 us
  transfers between devices with their start and end apart: 30, of which 11 were waited for; matrix products, arithmetic and copies ran while one was open for 7% of the time, Pallas kernels for 24%

profile of v7, /device:TPU:0, one launch (start us, length us, event | category | flops | bytes accessed | tf_op | source)
XLA Modules:
  0.0 92.4 jit_solution(4405052946273239886)
XLA Ops:
  0.9 4.1 %collective-permute-start = (bf16[1,2,18432]{2,1,0:T(2,128)(2,1)S(1)}, bf16[1,2,18432]{2,1,0:T(2,128)(2,1)S(1)}, u32[]{:S(2)}, u32[]{:S(2)}) collective-permute-start(bf16[1,2,18432]{2,1,0:T(2,128)(2,1)S(1)} %maximum_bitcast_fusion), channel_id=1, source_target_pairs={{0,8},{1,9},{2,10},{3,11},{4,12},{5,13},{6,14},{7,15},{8,0},{9,1},... | collective-permute-start | bytes 221192 | tf_op jit(solution)/shard_map/ppermute | solution.py:267
  5.0 2.9 %copy.8 = bf16[4096,256]{0,1:T(8,128)(2,1)S(1)} copy(bf16[4096,256]{1,0:T(8,128)(2,1)} %param.10) | data formatting | bytes 4194304 | tf_op args[3]
  8.0 1.6 %collective-permute-start.5 = (bf16[256,512]{1,0:T(8,128)(2,1)S(1)}, bf16[256,512]{1,0:T(8,128)(2,1)S(1)}, u32[]{:S(2)}, u32[]{:S(2)}) collective-permute-start(bf16[256,512]{1,0:T(8,128)(2,1)S(1)} %slice_bitcast_fusion.refs_0_), channel_id=1, source_target_pairs={{0,2},{1,3},{4,0},{5,1},{8,4},{9,5},{12,8},{13,9},{14,12},{15,13},... | collective-permute-start | bytes 786440 | tf_op jit(solution)/shard_map/ppermute | solution.py:256
  10.2 1.6 %collective-permute-start.1 = (bf16[2,2,18432]{2,1,0:T(2,128)(2,1)S(1)}, bf16[2,2,18432]{2,1,0:T(2,128)(2,1)S(1)}, u32[]{:S(2)}, u32[]{:S(2)}) collective-permute-start(bf16[2,2,18432]{2,1,0:T(2,128)(2,1)S(1)} %pad_maximum_fusion.3), channel_id=1, source_target_pairs={{0,4},{1,5},{2,6},{3,7},{4,0},{5,1},{6,2},{7,3},{8,12},{9,13},{10,... | collective-permute-start | bytes 442376 | tf_op jit(solution)/shard_map/ppermute | solution.py:267
  12.1 6.8 %collective-permute-done.1 = bf16[2,2,18432]{2,1,0:T(2,128)(2,1)S(1)} collective-permute-done((bf16[2,2,18432]{2,1,0:T(2,128)(2,1)S(1)}, bf16[2,2,18432]{2,1,0:T(2,128)(2,1)S(1)}, u32[]{:S(2)}, u32[]{:S(2)}) %collective-permute-start.1) | collective-permute-done | bytes 147488 | tf_op jit(solution)/shard_map/ppermute | solution.py:267
  19.2 2.9 %collective-permute-start.3 = (bf16[4,2,4096]{2,1,0:T(2,128)(2,1)S(1)}, bf16[4,2,4096]{2,1,0:T(2,128)(2,1)S(1)}, u32[]{:S(2)}, u32[]{:S(2)}) collective-permute-start(bf16[4,2,4096]{2,1,0:T(2,128)(2,1)S(1)} %pad_maximum_fusion.4), channel_id=1, source_target_pairs={{0,2},{1,3},{2,0},{3,1},{4,6},{5,7},{6,4},{7,5},{8,10},{9,11},{10,... | collective-permute-start | bytes 196616 | tf_op jit(solution)/shard_map/ppermute | solution.py:274
  23.1 1.6 %collective-permute-done.3 = bf16[4,2,4096]{2,1,0:T(2,128)(2,1)S(1)} collective-permute-done((bf16[4,2,4096]{2,1,0:T(2,128)(2,1)S(1)}, bf16[4,2,4096]{2,1,0:T(2,128)(2,1)S(1)}, u32[]{:S(2)}, u32[]{:S(2)}) %collective-permute-start.3) | collective-permute-done | bytes 65568 | tf_op jit(solution)/shard_map/ppermute | solution.py:274
  31.9 2.9 %collective-permute-done.7.refs_6_ = bf16[256,512]{1,0:T(8,128)(2,1)S(1)} collective-permute-done((bf16[256,512]{1,0:T(8,128)(2,1)S(1)}, bf16[256,512]{1,0:T(8,128)(2,1)S(1)}, u32[]{:S(2)}, u32[]{:S(2)}) %collective-permute-start.7) | collective-permute-done | bytes 262176 | tf_op jit(solution)/shard_map/ppermute | solution.py:255
  34.8 1.6 %pad_maximum_fusion = bf16[8,2,14336]{2,1,0:T(2,128)(2,1)S(1)} fusion(bf16[4,2,14336]{2,1,0:T(2,128)(2,1)} %collective-permute-done.2, bf16[2,2,14336]{2,1,0:T(2,128)(2,1)S(1)} %copy-done.3, bf16[2,2,14336]{2,1,0:T(2,128)(2,1)S(1)} %copy-done.5), kind=kLoop, calls=%fused_computation | loop fusion | flops 458752 | bytes 917504 | tf_op jit(solution)/shard_map/concatenate | solution.py:291
  36.7 2.0 %collective-permute-start.11 = (bf16[256,512]{1,0:T(8,128)(2,1)S(1)}, bf16[256,512]{1,0:T(8,128)(2,1)S(1)}, u32[]{:S(2)}, u32[]{:S(2)}) collective-permute-start(bf16[256,512]{1,0:T(8,128)(2,1)S(1)} %collective-permute-done.8.refs_8_), channel_id=1, source_target_pairs={{0,2},{1,3},{4,0},{5,1},{8,4},{9,5},{12,8},{13,9},{14,12},{15,13},... | collective-permute-start | bytes 786440 | tf_op jit(solution)/shard_map/ppermute | solution.py:256
  38.7 3.5 %all-to-all-start = ((bf16[8,32,256]{2,1,0:T(8,128)(2,1)}), bf16[8,32,256]{2,1,0:T(8,128)(2,1)S(1)}, u32[]{:S(2)}, u32[]{:S(2)}) async-start(bf16[8,32,256]{2,1,0:T(8,128)(2,1)} %rotate_in.1), calls=%async_computation | async-start | bytes 262144 | tf_op jit(solution)/shard_map/all_to_all | solution.py:48
  42.8 9.2 %rotate_out.1.aligned_ref = bf16[896,32]{1,0:T(8,128)(2,1)S(1)} custom-call(bf16[16,14336]{1,0:T(8,128)(2,1)S(1)} %reshape.7.near_ref, bf16[16,14336]{1,0:T(8,128)(2,1)S(1)} %collective-permute-done.9.far_ref, bf16[14336,896]{1,0:T(8,128)(2,1)} %basis_out_ref.1, s32[16]{0:T(128)S(1)} %copy-done.1), custom_call_target="tpu_custom_call" | custom-call | flops 822083584 | bytes 25690112 | tf_op jit(solution)/shard_map/rotate_out/pallas_call | solution.py:297
  52.1 2.0 %collective-permute-start.14 = (bf16[128,512]{1,0:T(8,128)(2,1)S(1)}, bf16[128,512]{1,0:T(8,128)(2,1)S(1)}, u32[]{:S(2)}, u32[]{:S(2)}) collective-permute-start(bf16[128,512]{1,0:T(8,128)(2,1)S(1)} %slice.27), channel_id=1, source_target_pairs={{0,2},{1,3},{4,0},{5,1},{8,4},{9,5},{12,8},{13,9},{14,12},{15,13},... | collective-permute-start | bytes 393224 | tf_op jit(solution)/shard_map/ppermute | solution.py:256
  54.8 3.0 %collective-permute-done.14.refs_1_ = bf16[128,512]{1,0:T(8,128)(2,1)S(1)} collective-permute-done((bf16[128,512]{1,0:T(8,128)(2,1)S(1)}, bf16[128,512]{1,0:T(8,128)(2,1)S(1)}, u32[]{:S(2)}, u32[]{:S(2)}) %collective-permute-start.14) | collective-permute-done | bytes 131104 | tf_op jit(solution)/shard_map/ppermute | solution.py:256
  57.8 1.5 %collective-permute-done.13.refs_0_ = bf16[128,512]{1,0:T(8,128)(2,1)S(1)} collective-permute-done((bf16[128,512]{1,0:T(8,128)(2,1)S(1)}, bf16[128,512]{1,0:T(8,128)(2,1)S(1)}, u32[]{:S(2)}, u32[]{:S(2)}) %collective-permute-start.13) | collective-permute-done | bytes 131104 | tf_op jit(solution)/shard_map/ppermute | solution.py:255
  59.8 6.2 %scale.1.scaled_ref = bf16[896,4096]{1,0:T(8,128)(2,1)S(1)} custom-call(bf16[896,32]{1,0:T(8,128)(2,1)S(1)} %rotate_out.1.aligned_ref, bf16[8,32,256]{2,1,0:T(8,128)(2,1)S(1)} %all-to-all-done.near_ref, bf16[8,32,256]{2,1,0:T(8,128)(2,1)S(1)} %collective-permute-done.12.far_ref, s32[32]{0:T(128)S(1)} %copy-done, f32[896,4096]{1,0:T(8,128)} %eigen_ref.1), custom_call_target="tpu_custom_call" | custom-call | flops 234881024 | bytes 22020096 | tf_op jit(solution)/shard_map/scale/pallas_call | solution.py:323
  66.7 5.5 %project.1 = (f32[896,512]{1,0:T(8,128)S(1)}, bf16[768,896]{1,0:T(8,128)(2,1)S(1)}) custom-call(bf16[896,4096]{1,0:T(8,128)(2,1)S(1)} %scale.1.scaled_ref, bf16[14336,896]{1,0:T(8,128)(2,1)} %basis_out_ref.1, bf16[256,512]{1,0:T(8,128)(2,1)S(1)} %slice_bitcast_fusion.refs_0_, bf16[256,512]{1,0:T(8,128)(2,1)S(1)} %collective-permute-done.15.refs_1_, ...), custom_call_target="tpu_custom_call" | custom-call | flops 3758096384 | bytes 11534336 | tf_op jit(solution)/shard_map/project/pallas_call | solution.py:347
  72.2 1.6 %window.1 = (bf16[8,48,512]{2,1,0:T(8,128)(2,1)S(1)}, f32[8,48,512]{2,1,0:T(8,128)S(1)}) custom-call(bf16[768,896]{1,0:T(8,128)(2,1)S(1)} %get-tuple-element.45.window_ref, bf16[896,4096]{1,0:T(8,128)(2,1)S(1)} %scale.1.scaled_ref, f32[896,512]{1,0:T(8,128)S(1)} %get-tuple-element.46.projected_ref, bf16[128,512]{1,0:T(8,128)(2,1)S(1)} %collective-permute-done.13.refs_0_, ...), custom_call_target="tpu_custom_call" | custom-call | flops 704643072 | bytes 6094848 | tf_op jit(solution)/shard_map/window/pallas_call | solution.py:369
  74.0 1.6 %collective-permute-done.24.got_ref = bf16[8,48,512]{2,1,0:T(8,128)(2,1)S(1)} collective-permute-done((bf16[8,48,512]{2,1,0:T(8,128)(2,1)S(1)}, bf16[8,48,512]{2,1,0:T(8,128)(2,1)S(1)}, u32[]{:S(2)}, u32[]{:S(2)}) %collective-permute-start.24) | collective-permute-done | bytes 393248 | tf_op jit(solution)/shard_map/ppermute | solution.py:43
  75.7 1.5 %collective-permute-start.25 = (bf16[4,48,512]{2,1,0:T(8,128)(2,1)S(1)}, bf16[4,48,512]{2,1,0:T(8,128)(2,1)S(1)}, u32[]{:S(2)}, u32[]{:S(2)}) collective-permute-start(bf16[4,48,512]{2,1,0:T(8,128)(2,1)S(1)} %get-tuple-element.52), channel_id=1, source_target_pairs={{0,2},{1,3},{2,0},{3,1},{4,6},{5,7},{6,4},{7,5},{8,10},{9,11},{10,... | collective-permute-start | bytes 589832 | tf_op jit(solution)/shard_map/ppermute | solution.py:400
  77.2 5.5 %collective-permute-done.25.got_ref = bf16[4,48,512]{2,1,0:T(8,128)(2,1)S(1)} collective-permute-done((bf16[4,48,512]{2,1,0:T(8,128)(2,1)S(1)}, bf16[4,48,512]{2,1,0:T(8,128)(2,1)S(1)}, u32[]{:S(2)}, u32[]{:S(2)}) %collective-permute-start.25) | collective-permute-done | bytes 196640 | tf_op jit(solution)/shard_map/ppermute | solution.py:400
  84.0 1.8 %collective-permute-start.27 = (bf16[48,512]{1,0:T(8,128)(2,1)S(1)}, bf16[48,512]{1,0:T(8,128)(2,1)S(1)}, u32[]{:S(2)}, u32[]{:S(2)}) collective-permute-start(bf16[48,512]{1,0:T(8,128)(2,1)S(1)} %get-tuple-element.55), channel_id=1, source_target_pairs={{0,8},{1,9},{2,10},{3,11},{4,12},{5,13},{6,14},{7,15},{8,0},{9,1},... | collective-permute-start | bytes 147464 | tf_op jit(solution)/shard_map/ppermute | solution.py:411
  87.2 2.9 %collective-permute-done.27.refs_1_ = bf16[48,512]{1,0:T(8,128)(2,1)S(1)} collective-permute-done((bf16[48,512]{1,0:T(8,128)(2,1)S(1)}, bf16[48,512]{1,0:T(8,128)(2,1)S(1)}, u32[]{:S(2)}, u32[]{:S(2)}) %collective-permute-start.27) | collective-permute-done | bytes 49184 | tf_op jit(solution)/shard_map/ppermute | solution.py:411
  90.1 1.6 %collective-permute-done.28.refs_2_ = bf16[48,512]{1,0:T(8,128)(2,1)S(1)} collective-permute-done((bf16[48,512]{1,0:T(8,128)(2,1)S(1)}, bf16[48,512]{1,0:T(8,128)(2,1)S(1)}, u32[]{:S(2)}, u32[]{:S(2)}) %collective-permute-start.28) | collective-permute-done | bytes 49184 | tf_op jit(solution)/shard_map/ppermute | solution.py:411
  (72 shorter events, 16.5 us)
Async XLA Ops:
  0.9 9.1 %collective-permute-start = (bf16[1,2,18432]{2,1,0:T(2,128)(2,1)S(1)}, bf16[1,2,18432]{2,1,0:T(2,128)(2,1)S(1)}, u32[]{:S(2)}, u32[]{:S(2)}) collective-permute-start(bf16[1,2,18432]{2,1,0:T(2,128)(2,1)S(1)} %maximum_bitcast_fusion), channel_id=1, source_target_pairs={{0,8},{1,9},{2,10},{3,11},{4,12},{5,13},{6,14},{7,15},{8,0},{9,1},... | collective-permute-start | bytes 221192 | tf_op jit(solution)/shard_map/ppermute | solution.py:267
  8.0 15.1 %collective-permute-start.5 = (bf16[256,512]{1,0:T(8,128)(2,1)S(1)}, bf16[256,512]{1,0:T(8,128)(2,1)S(1)}, u32[]{:S(2)}, u32[]{:S(2)}) collective-permute-start(bf16[256,512]{1,0:T(8,128)(2,1)S(1)} %slice_bitcast_fusion.refs_0_), channel_id=1, source_target_pairs={{0,2},{1,3},{4,0},{5,1},{8,4},{9,5},{12,8},{13,9},{14,12},{15,13},... | collective-permute-start | bytes 786440 | tf_op jit(solution)/shard_map/ppermute | solution.py:256
  9.5 13.5 %collective-permute-start.4 = (bf16[256,512]{1,0:T(8,128)(2,1)S(1)}, bf16[256,512]{1,0:T(8,128)(2,1)S(1)}, u32[]{:S(2)}, u32[]{:S(2)}) collective-permute-start(bf16[256,512]{1,0:T(8,128)(2,1)S(1)} %slice_bitcast_fusion.refs_0_), channel_id=1, source_target_pairs={{0,4},{1,5},{4,8},{5,9},{8,12},{9,13},{12,14},{13,15},{14,10},{15,... | collective-permute-start | bytes 786440 | tf_op jit(solution)/shard_map/ppermute | solution.py:255
  10.2 8.7 %collective-permute-start.1 = (bf16[2,2,18432]{2,1,0:T(2,128)(2,1)S(1)}, bf16[2,2,18432]{2,1,0:T(2,128)(2,1)S(1)}, u32[]{:S(2)}, u32[]{:S(2)}) collective-permute-start(bf16[2,2,18432]{2,1,0:T(2,128)(2,1)S(1)} %pad_maximum_fusion.3), channel_id=1, source_target_pairs={{0,4},{1,5},{2,6},{3,7},{4,0},{5,1},{6,2},{7,3},{8,12},{9,13},{10,... | collective-permute-start | bytes 442376 | tf_op jit(solution)/shard_map/ppermute | solution.py:267
  23.0 8.9 %collective-permute-start.2 = (bf16[4,2,14336]{2,1,0:T(2,128)(2,1)}, bf16[4,2,14336]{2,1,0:T(2,128)(2,1)}, u32[]{:S(2)}, u32[]{:S(2)}) collective-permute-start(bf16[4,2,14336]{2,1,0:T(2,128)(2,1)} %pad_maximum_fusion.1), channel_id=1, source_target_pairs={{0,2},{1,3},{2,0},{3,1},{4,6},{5,7},{6,4},{7,5},{8,10},{9,11},{10,... | collective-permute-start | bytes 688136 | tf_op jit(solution)/shard_map/ppermute | solution.py:288
  24.7 10.2 %collective-permute-start.7 = (bf16[256,512]{1,0:T(8,128)(2,1)S(1)}, bf16[256,512]{1,0:T(8,128)(2,1)S(1)}, u32[]{:S(2)}, u32[]{:S(2)}) collective-permute-start(bf16[256,512]{1,0:T(8,128)(2,1)S(1)} %collective-permute-done.4.refs_2_), channel_id=1, source_target_pairs={{0,4},{1,5},{4,8},{5,9},{8,12},{9,13},{12,14},{13,15},{14,10},{15,... | collective-permute-start | bytes 786440 | tf_op jit(solution)/shard_map/ppermute | solution.py:255
  25.9 8.9 %collective-permute-start.8 = (bf16[256,512]{1,0:T(8,128)(2,1)S(1)}, bf16[256,512]{1,0:T(8,128)(2,1)S(1)}, u32[]{:S(2)}, u32[]{:S(2)}) collective-permute-start(bf16[256,512]{1,0:T(8,128)(2,1)S(1)} %collective-permute-done.5.refs_4_), channel_id=1, source_target_pairs={{0,2},{1,3},{4,0},{5,1},{8,4},{9,5},{12,8},{13,9},{14,12},{15,13},... | collective-permute-start | bytes 786440 | tf_op jit(solution)/shard_map/ppermute | solution.py:256
  36.6 6.2 %collective-permute-start.9 = (bf16[16,14336]{1,0:T(8,128)(2,1)S(1)}, bf16[16,14336]{1,0:T(8,128)(2,1)S(1)}, u32[]{:S(2)}, u32[]{:S(2)}) collective-permute-start(bf16[16,14336]{1,0:T(8,128)(2,1)S(1)} %reshape.7.near_ref), channel_id=1, source_target_pairs={{0,1},{1,0},{2,3},{3,2},{4,5},{5,4},{6,7},{7,6},{8,9},{9,8},{10,11... | collective-permute-start | bytes 1376264 | tf_op jit(solution)/shard_map/ppermute | solution.py:43
  36.7 15.4 %collective-permute-start.10 = (bf16[256,512]{1,0:T(8,128)(2,1)S(1)}, bf16[256,512]{1,0:T(8,128)(2,1)S(1)}, u32[]{:S(2)}, u32[]{:S(2)}) collective-permute-start(bf16[256,512]{1,0:T(8,128)(2,1)S(1)} %collective-permute-done.7.refs_6_), channel_id=1, source_target_pairs={{0,4},{1,5},{4,8},{5,9},{8,12},{9,13},{12,14},{13,15},{14,10},{15,... | collective-permute-start | bytes 786440 | tf_op jit(solution)/shard_map/ppermute | solution.py:255
  36.7 15.3 %collective-permute-start.11 = (bf16[256,512]{1,0:T(8,128)(2,1)S(1)}, bf16[256,512]{1,0:T(8,128)(2,1)S(1)}, u32[]{:S(2)}, u32[]{:S(2)}) collective-permute-start(bf16[256,512]{1,0:T(8,128)(2,1)S(1)} %collective-permute-done.8.refs_8_), channel_id=1, source_target_pairs={{0,2},{1,3},{4,0},{5,1},{8,4},{9,5},{12,8},{13,9},{14,12},{15,13},... | collective-permute-start | bytes 786440 | tf_op jit(solution)/shard_map/ppermute | solution.py:256
  38.7 13.3 %all-to-all-start = ((bf16[8,32,256]{2,1,0:T(8,128)(2,1)}), bf16[8,32,256]{2,1,0:T(8,128)(2,1)S(1)}, u32[]{:S(2)}, u32[]{:S(2)}) async-start(bf16[8,32,256]{2,1,0:T(8,128)(2,1)} %rotate_in.1), calls=%async_computation | async-start | bytes 262144 | tf_op jit(solution)/shard_map/all_to_all | solution.py:48
  42.2 12.0 %collective-permute-start.15 = (bf16[256,512]{1,0:T(8,128)(2,1)S(1)}, bf16[256,512]{1,0:T(8,128)(2,1)S(1)}, u32[]{:S(2)}, u32[]{:S(2)}) collective-permute-start(bf16[256,512]{1,0:T(8,128)(2,1)S(1)} %slice_bitcast_fusion.refs_0_), channel_id=1, source_target_pairs={{0,1},{1,0},{2,3},{3,2},{4,5},{5,4},{6,7},{7,6},{8,9},{9,8},{10,11... | collective-permute-start | bytes 786440 | tf_op jit(solution)/shard_map/ppermute | solution.py:43
  42.3 12.4 %collective-permute-start.16 = (bf16[256,512]{1,0:T(8,128)(2,1)S(1)}, bf16[256,512]{1,0:T(8,128)(2,1)}, u32[]{:S(2)}, u32[]{:S(2)}) collective-permute-start(bf16[256,512]{1,0:T(8,128)(2,1)S(1)} %collective-permute-done.4.refs_2_), channel_id=1, source_target_pairs={{0,1},{1,0},{2,3},{3,2},{4,5},{5,4},{6,7},{7,6},{8,9},{9,8},{10,11... | collective-permute-start | bytes 786440 | tf_op jit(solution)/shard_map/ppermute | solution.py:43
  52.1 5.7 %collective-permute-start.14 = (bf16[128,512]{1,0:T(8,128)(2,1)S(1)}, bf16[128,512]{1,0:T(8,128)(2,1)S(1)}, u32[]{:S(2)}, u32[]{:S(2)}) collective-permute-start(bf16[128,512]{1,0:T(8,128)(2,1)S(1)} %slice.27), channel_id=1, source_target_pairs={{0,2},{1,3},{4,0},{5,1},{8,4},{9,5},{12,8},{13,9},{14,12},{15,13},... | collective-permute-start | bytes 393224 | tf_op jit(solution)/shard_map/ppermute | solution.py:256
  54.2 11.9 %collective-permute-start.17 = (bf16[256,512]{1,0:T(8,128)(2,1)S(1)}, bf16[256,512]{1,0:T(8,128)(2,1)S(1)}, u32[]{:S(2)}, u32[]{:S(2)}) collective-permute-start(bf16[256,512]{1,0:T(8,128)(2,1)S(1)} %collective-permute-done.5.refs_4_), channel_id=1, source_target_pairs={{0,1},{1,0},{2,3},{3,2},{4,5},{5,4},{6,7},{7,6},{8,9},{9,8},{10,11... | collective-permute-start | bytes 786440 | tf_op jit(solution)/shard_map/ppermute | solution.py:43
  54.7 11.4 %collective-permute-start.18 = (bf16[256,512]{1,0:T(8,128)(2,1)S(1)}, bf16[256,512]{1,0:T(8,128)(2,1)S(1)}, u32[]{:S(2)}, u32[]{:S(2)}) collective-permute-start(bf16[256,512]{1,0:T(8,128)(2,1)S(1)} %collective-permute-done.7.refs_6_), channel_id=1, source_target_pairs={{0,1},{1,0},{2,3},{3,2},{4,5},{5,4},{6,7},{7,6},{8,9},{9,8},{10,11... | collective-permute-start | bytes 786440 | tf_op jit(solution)/shard_map/ppermute | solution.py:43
  57.8 8.9 %collective-permute-start.19 = (bf16[256,512]{1,0:T(8,128)(2,1)S(1)}, bf16[256,512]{1,0:T(8,128)(2,1)S(1)}, u32[]{:S(2)}, u32[]{:S(2)}) collective-permute-start(bf16[256,512]{1,0:T(8,128)(2,1)S(1)} %collective-permute-done.8.refs_8_), channel_id=1, source_target_pairs={{0,1},{1,0},{2,3},{3,2},{4,5},{5,4},{6,7},{7,6},{8,9},{9,8},{10,11... | collective-permute-start | bytes 786440 | tf_op jit(solution)/shard_map/ppermute | solution.py:43
  59.3 7.4 %collective-permute-start.20 = (bf16[256,512]{1,0:T(8,128)(2,1)S(1)}, bf16[256,512]{1,0:T(8,128)(2,1)S(1)}, u32[]{:S(2)}, u32[]{:S(2)}) collective-permute-start(bf16[256,512]{1,0:T(8,128)(2,1)S(1)} %collective-permute-done.10.refs_10_), channel_id=1, source_target_pairs={{0,1},{1,0},{2,3},{3,2},{4,5},{5,4},{6,7},{7,6},{8,9},{9,8},{10,11... | collective-permute-start | bytes 786440 | tf_op jit(solution)/shard_map/ppermute | solution.py:43
  59.3 7.4 %collective-permute-start.21 = (bf16[256,512]{1,0:T(8,128)(2,1)S(1)}, bf16[256,512]{1,0:T(8,128)(2,1)S(1)}, u32[]{:S(2)}, u32[]{:S(2)}) collective-permute-start(bf16[256,512]{1,0:T(8,128)(2,1)S(1)} %collective-permute-done.11.refs_12_), channel_id=1, source_target_pairs={{0,1},{1,0},{2,3},{3,2},{4,5},{5,4},{6,7},{7,6},{8,9},{9,8},{10,11... | collective-permute-start | bytes 786440 | tf_op jit(solution)/shard_map/ppermute | solution.py:43
  66.1 6.1 %collective-permute-start.22 = (bf16[128,512]{1,0:T(8,128)(2,1)S(1)}, bf16[128,512]{1,0:T(8,128)(2,1)S(1)}, u32[]{:S(2)}, u32[]{:S(2)}) collective-permute-start(bf16[128,512]{1,0:T(8,128)(2,1)S(1)} %collective-permute-done.13.refs_0_), channel_id=1, source_target_pairs={{0,1},{1,0},{2,3},{3,2},{4,5},{5,4},{6,7},{7,6},{8,9},{9,8},{10,11... | collective-permute-start | bytes 393224 | tf_op jit(solution)/shard_map/ppermute | solution.py:43
  66.2 6.0 %collective-permute-start.23 = (bf16[128,512]{1,0:T(8,128)(2,1)S(1)}, bf16[128,512]{1,0:T(8,128)(2,1)S(1)}, u32[]{:S(2)}, u32[]{:S(2)}) collective-permute-start(bf16[128,512]{1,0:T(8,128)(2,1)S(1)} %collective-permute-done.14.refs_1_), channel_id=1, source_target_pairs={{0,1},{1,0},{2,3},{3,2},{4,5},{5,4},{6,7},{7,6},{8,9},{9,8},{10,11... | collective-permute-start | bytes 393224 | tf_op jit(solution)/shard_map/ppermute | solution.py:43
  75.7 7.0 %collective-permute-start.25 = (bf16[4,48,512]{2,1,0:T(8,128)(2,1)S(1)}, bf16[4,48,512]{2,1,0:T(8,128)(2,1)S(1)}, u32[]{:S(2)}, u32[]{:S(2)}) collective-permute-start(bf16[4,48,512]{2,1,0:T(8,128)(2,1)S(1)} %get-tuple-element.52), channel_id=1, source_target_pairs={{0,2},{1,3},{2,0},{3,1},{4,6},{5,7},{6,4},{7,5},{8,10},{9,11},{10,... | collective-permute-start | bytes 589832 | tf_op jit(solution)/shard_map/ppermute | solution.py:400
  84.0 6.2 %collective-permute-start.27 = (bf16[48,512]{1,0:T(8,128)(2,1)S(1)}, bf16[48,512]{1,0:T(8,128)(2,1)S(1)}, u32[]{:S(2)}, u32[]{:S(2)}) collective-permute-start(bf16[48,512]{1,0:T(8,128)(2,1)S(1)} %get-tuple-element.55), channel_id=1, source_target_pairs={{0,8},{1,9},{2,10},{3,11},{4,12},{5,13},{6,14},{7,15},{8,0},{9,1},... | collective-permute-start | bytes 147464 | tf_op jit(solution)/shard_map/ppermute | solution.py:411
  85.8 5.9 %collective-permute-start.28 = (bf16[48,512]{1,0:T(8,128)(2,1)S(1)}, bf16[48,512]{1,0:T(8,128)(2,1)S(1)}, u32[]{:S(2)}, u32[]{:S(2)}) collective-permute-start(bf16[48,512]{1,0:T(8,128)(2,1)S(1)} %get-tuple-element.56), channel_id=1, source_target_pairs={{0,12},{1,13},{2,14},{3,15},{4,8},{5,9},{6,10},{7,11},{8,4},{9,5},... | collective-permute-start | bytes 147464 | tf_op jit(solution)/shard_map/ppermute | solution.py:411
  (12 other events, 86.0 us)

commit v8 on v7

--- a/solution.py
+++ b/solution.py
@@ -54,11 +54,9 @@
 
 def held_tokens(me, tokens, tok_rows):
     row = lax.broadcasted_iota(jnp.int32, (tokens, tokens), 1)
-    chips = tokens // tok_rows // 2
-    place = (row >> bits_of(tok_rows)) & (chips - 1)
-    chip = jnp.zeros_like(row)
-    for bit in range(bits_of(chips)):
-        chip |= ((place >> bit) & 1) << (bits_of(chips) - 1 - bit)
+    pairs = tokens // tok_rows // 4
+    place = row >> bits_of(tok_rows)
+    chip = 2 * (place & (pairs - 1)) + ((place >> bits_of(pairs)) & 1)
     other = row >> bits_of(tokens // 2)
     device = me ^ (2 * chip + other)
     return (device << bits_of(tok_rows)) + (row & (tok_rows - 1))
@@ -67,6 +65,14 @@
 def reorder(wanted, held, rotated):
     order = jnp.where(wanted == held, 1.0, 0.0).astype(jnp.bfloat16)
     return jnp.dot(order, rotated.astype(jnp.bfloat16), preferred_element_type=jnp.float32)
+
+
+def part_kernel(*refs):
+    grads_ref, acts_ref = refs[-2:]
+    first = grads_ref.shape[2]
+    for at, ref in enumerate(refs[:-2]):
+        grads_ref[at] = ref[:, :first]
+        acts_ref[at] = ref[:, first:]
 
 
 def rotate_in_kernel(tok_rows, near_ref, far_ref, basis_ref, out_ref):
@@ -212,29 +218,48 @@
         send_ref[k] = result[other, :].astype(jnp.bfloat16)
 
 
-def add_core_kernel(keep_ref, got_ref, mine_ref, send_ref):
+def add_core_kernel(keep_ref, got_ref, pair_mine_ref, pair_send_ref, axis_mine_ref, *axis_refs):
+    chip = lax.axis_index("blk") // 2
+    side, place = lax.rem(chip, 2), chip // 2
+    pairs, _, half = pair_mine_ref.shape
+    first, last = slice(0, half), slice(half, 2 * half)
+
+    def total(at, columns):
+        return keep_ref[at, :, columns] + got_ref[at, :, columns].astype(jnp.float32)
+
+    for pair in range(pairs):
+        pair_mine_ref[pair] = total(2 * pair + side, first)
+        pair_send_ref[pair] = total(2 * pair + 1 - side, first).astype(jnp.bfloat16)
+    for other in range(2):
+        axis_mine_ref[other] = total(2 * place + other, last)
+        for key, axis_ref in enumerate(axis_refs, 1):
+            axis_ref[other] = total(2 * (place ^ key) + other, last).astype(jnp.bfloat16)
+
+
+def add_pair_kernel(mine_ref, got_ref, own_ref, *send_refs):
+    place = lax.axis_index("blk") // 4
+    for key, ref in enumerate((own_ref, *send_refs)):
+        at = place ^ key
+        ref[...] = (mine_ref[at] + got_ref[at].astype(jnp.float32)).astype(ref.dtype)
+
+
+def add_axis_kernel(mine_ref, *refs):
+    own_ref, send_ref = refs[-2:]
     side = lax.rem(lax.axis_index("blk") // 2, 2)
-    for pair in range(mine_ref.shape[0]):
-        mine, other = 2 * pair + side, 2 * pair + 1 - side
-        mine_ref[pair] = keep_ref[mine] + got_ref[mine].astype(jnp.float32)
-        sent = keep_ref[other] + got_ref[other].astype(jnp.float32)
-        send_ref[pair] = sent.astype(jnp.bfloat16)
-
-
-def add_pair_kernel(mine_ref, got_ref, own_ref, *send_refs):
-    me = lax.axis_index("blk") // 4
-    own_ref[...] = mine_ref[me] + got_ref[me].astype(jnp.float32)
-    for key, send_ref in enumerate(send_refs, 1):
-        other = me ^ key
-        sent = mine_ref[other] + got_ref[other].astype(jnp.float32)
-        send_ref[...] = sent.astype(jnp.bfloat16)
-
-
-def add_chips_kernel(own_ref, *refs):
-    total = own_ref[...]
+    for ref, at in ((own_ref, side), (send_ref, 1 - side)):
+        total = mine_ref[at]
+        for got_ref in refs[:-2]:
+            total += got_ref[at].astype(jnp.float32)
+        ref[...] = total.astype(ref.dtype)
+
+
+def add_last_kernel(first_ref, last_ref, last_got_ref, *refs):
+    half = first_ref.shape[1]
+    total = first_ref[...]
     for ref in refs[:-1]:
         total += ref[...].astype(jnp.float32)
-    refs[-1][...] = total
+    refs[-1][:, :half] = total
+    refs[-1][:, half:] = last_ref[...] + last_got_ref[...].astype(jnp.float32)
 
 
 VMEM = pl.BlockSpec(memory_space=pltpu.VMEM)
@@ -259,24 +284,31 @@
     turned = basis_in.T
     own = basis_in[:WC].T
 
-    right, left = [own, to_right(own)], [own, to_left(own)]
-
-    both = jnp.concatenate([grad_out, activations], axis=1)[None]
-    key = n // 2
-    while key > 2:
-        got = lax.ppermute(both, "blk", xor_pairs(n, key))
-        key //= 2
-        if key > 2:
-            both = jnp.concatenate([both, got], axis=0)
-    got, turned = after(got, turned)
-    acts = jnp.concatenate([both[..., full_out:], got[..., full_out:]], axis=0)
-    grads = jnp.concatenate([both[..., :full_out], got[..., :full_out]], axis=0)
-    got = lax.ppermute(acts, "blk", xor_pairs(n, 2))
-    got, right[-1], left[-1] = after(got, right[-1], left[-1])
-    while len(right) < steps - 1:
+    pairs = chips // 2
+    both = jnp.concatenate([grad_out, activations], axis=1)
+    got = [lax.ppermute(both, "blk", xor_pairs(n, 4 * key)) for key in range(1, pairs)]
+    both, turned, *got = after(both, turned, *got)
+    grads, acts = pl.pallas_call(
+        part_kernel,
+        out_shape=(
+            jax.ShapeDtypeStruct((pairs, tok_rows, full_out), jnp.bfloat16),
+            jax.ShapeDtypeStruct((pairs, tok_rows, full_in), jnp.bfloat16),
+        ),
+        in_specs=[VMEM] * pairs,
+        out_specs=(VMEM, VMEM),
+        compiler_params=pltpu.CompilerParams(vmem_limit_bytes=8 * MIB),
+        name="part",
+    )(both, *got)
+    acts_got = lax.ppermute(acts, "blk", xor_pairs(n, 2))
+    grads_got = lax.ppermute(grads, "blk", xor_pairs(n, 2))
+
+    acts_got, own = after(acts_got, own)
+    right, left = [own], [own]
+    while len(right) < steps - 2:
         right.append(to_right(right[-1]))
         left.append(to_left(left[-1]))
-    acts = jnp.concatenate([acts, got], axis=0).reshape(tokens // 2, full_in)
+
+    acts = jnp.concatenate([acts, acts_got], axis=0).reshape(tokens // 2, full_in)
     rotated = pl.pallas_call(
         functools.partial(rotate_in_kernel, tok_rows),
         out_shape=jax.ShapeDtypeStruct((chips, tokens, in_width), jnp.bfloat16),
@@ -285,11 +317,12 @@
         compiler_params=pltpu.CompilerParams(vmem_limit_bytes=8 * MIB),
         name="rotate_in",
     )(acts, swap(acts, n), turned)
-    got = lax.ppermute(grads, "blk", xor_pairs(n, 2))
-    got, rotated, right[-1], left[-1] = after(got, rotated, right[-1], left[-1])
+    grads_got, rotated, right[-1], left[-1] = after(grads_got, rotated, right[-1], left[-1])
     rotated = exchange(rotated, n, 2)
-    grads = jnp.concatenate([grads, got], axis=0).reshape(tokens // 2, full_out)
+    grads = jnp.concatenate([grads, grads_got], axis=0).reshape(tokens // 2, full_out)
     grads_far = swap(grads, n)
+    near = [right[0], right[1], left[1]]
+    far = [swap(piece, n) for piece in near]
     right.append(to_right(right[-1]))
     left.append(to_left(left[-1]))
 
@@ -314,10 +347,14 @@
         name="rotate_out",
     )(grads, grads_far, basis_out, block_map)
 
-    aligned, rotated, right[-1], left[-1] = after(aligned, rotated, right[-1], left[-1])
+    aligned, rotated, right[-1], left[-1], *far = after(
+        aligned, rotated, right[-1], left[-1], *far
+    )
     rotated_far = swap(rotated, n)
-    cut = in_width // 2
-    last = [to_right(right[-1][:cut]), to_left(left[-1][cut:])]
+    near += [right[-1], left[-1]]
+    far += [swap(right[-1], n), swap(left[-1], n)]
+    right.append(to_right(right[-1]))
+    left.append(to_left(left[-1]))
     begun = [0] + [at for step in range(1, steps) for at in (step, chips - step)] + [steps]
     blocks = 8
     scaled = pl.pallas_call(
@@ -339,10 +376,11 @@
         name="scale",
     )(aligned, rotated, rotated_far, tile_order, eigenvalues)
 
-    scaled, *last = after(scaled, *last)
-    last += [swap(piece, n) for piece in last]
-    near = [right[at] if at < steps else left[chips - at] for at in begun[:-1]]
-    far = [swap(piece, n) for piece in near]
+    scaled, right[-1], left[-1], *far = after(scaled, right[-1], left[-1], *far)
+    cut = in_width // 2
+    last = [to_right(right[-1][:cut]), to_left(left[-1][cut:])]
+    near += [right[-1], left[-1]]
+    far += [swap(right[-1], n), swap(left[-1], n)]
     pieces = [piece for pair in zip(near, far) for piece in pair]
     projected, window = pl.pallas_call(
         functools.partial(project_kernel, (0, 6, len(pieces))),
@@ -365,6 +403,8 @@
         name="project",
     )(scaled, basis_out, *pieces)
 
+    projected, *last = after(projected, *last)
+    last += [swap(piece, n) for piece in last]
     rows = WR // n
     send, keep = pl.pallas_call(
         functools.partial(window_kernel, 1.0 / tokens),
@@ -384,39 +424,42 @@
         name="window",
     )(window, scaled, projected, *last)
 
-    small = pltpu.CompilerParams(vmem_limit_bytes=8 * MIB)
-    half = (chips // 2, rows, WC)
-    mine, send = pl.pallas_call(
+    def add(kernel, shapes, *operands):
+        return pl.pallas_call(
+            kernel,
+            out_shape=shapes,
+            in_specs=[VMEM] * len(operands),
+            out_specs=[VMEM] * len(shapes),
+            compiler_params=pltpu.CompilerParams(vmem_limit_bytes=8 * MIB),
+            name=kernel.__name__[:-7],
+        )(*operands)
+
+    exact = lambda *shape: jax.ShapeDtypeStruct((*shape, rows, WC // 2), jnp.float32)
+    sent = lambda *shape: jax.ShapeDtypeStruct((*shape, rows, WC // 2), jnp.bfloat16)
+    to_pair = lambda x: lax.ppermute(x, "blk", xor_pairs(n, 2))
+    to_axis = lambda xs: [
+        lax.ppermute(x, "blk", xor_pairs(n, 4 * key)) for key, x in enumerate(xs, 1)
+    ]
+    pair_mine, pair_send, axis_mine, *axis_sends = add(
         add_core_kernel,
-        out_shape=(
-            jax.ShapeDtypeStruct(half, jnp.float32),
-            jax.ShapeDtypeStruct(half, jnp.bfloat16),
-        ),
-        in_specs=[VMEM, VMEM],
-        out_specs=(VMEM, VMEM),
-        compiler_params=small,
-        name="add_core",
-    )(keep, swap(send, n))
-    got = lax.ppermute(send, "blk", xor_pairs(n, 2))
-    block = (rows, WC)
-    own, *sends = pl.pallas_call(
-        add_pair_kernel,
-        out_shape=[jax.ShapeDtypeStruct(block, jnp.float32)]
-        + [jax.ShapeDtypeStruct(block, jnp.bfloat16)] * (chips // 2 - 1),
-        in_specs=[VMEM, VMEM],
-        out_specs=[VMEM] * (chips // 2),
-        compiler_params=small,
-        name="add_pair",
-    )(mine, got)
-    arrived = [lax.ppermute(x, "blk", xor_pairs(n, 4 * k)) for k, x in enumerate(sends, 1)]
-    return pl.pallas_call(
-        add_chips_kernel,
-        out_shape=jax.ShapeDtypeStruct(block, jnp.float32),
-        in_specs=[VMEM] * (chips // 2),
-        out_specs=VMEM,
-        compiler_params=small,
-        name="add_chips",
-    )(own, *arrived)
+        [exact(pairs), sent(pairs), exact(2)] + [sent(2)] * (pairs - 1),
+        keep,
+        swap(send, n),
+    )
+    first, *first_sends = add(
+        add_pair_kernel, [exact()] + [sent()] * (pairs - 1), pair_mine, to_pair(pair_send)
+    )
+    last, last_send = add(
+        add_axis_kernel, [exact(), sent()], axis_mine, *to_axis(axis_sends)
+    )
+    return add(
+        add_last_kernel,
+        [jax.ShapeDtypeStruct((rows, WC), jnp.float32)],
+        first,
+        last,
+        to_pair(last_send),
+        *to_axis(first_sends),
+    )[0]
 
 
 def gather_body(grad_out, activations, basis_out, basis_in, eigenvalues, tile_order, block_map):

time: 92.7 us -> 88.7 us (0.957)
  waiting for transfers between devices: 28.9 us -> 23.6 us
  starting transfers between devices: 29.3 us -> 34.2 us
  other arithmetic: 4.8 us -> 1.71 us
  Pallas kernels: 24.8 us -> 23.8 us
    ppermute x4, starting transfers between devices: 6.72 us -> 2.03 us  [ring_body(): to_left = lambda x: lax.ppermute(x, 'blk', shift_pairs(n, -1))]
    ppermute x4, starting transfers between devices: 1.96 us -> 6.23 us  [ring_body(): to_right = lambda x: lax.ppermute(x, 'blk', shift_pairs(n, 1))]
    ppermute x8 -> x13, starting transfers between devices: 14.6 us -> 18.8 us  [the longest x6 8.83 us: ring_body(): lax.ppermute(x, 'blk', xor_pairs(n, 4 * key))]
    ppermute x8 -> x13, waiting for transfers between devices: 18.5 us -> 14.5 us  [the longest x6 8.24 us: ring_body(): lax.ppermute(x, 'blk', xor_pairs(n, 4 * key))]
    ppermute x13, waiting for transfers between devices: 2.98 us -> 5.34 us  [swap(): return lax.ppermute(x, 'blk', xor_pairs(n, 1))]
    ppermute x4, waiting for transfers between devices: 2.99 us -> 0.78 us  [ring_body(): to_left = lambda x: lax.ppermute(x, 'blk', shift_pairs(n, -1))]
    concatenate x7 -> x2, other arithmetic: 3.89 us -> 1.71 us  [the longest x1 1.53 us: ring_body(): jnp.concatenate([grads, grads_got], axis=0).reshape(tokens // 2, full_out)]
    ppermute x4, waiting for transfers between devices: 4.45 us -> 2.93 us  [ring_body(): to_right = lambda x: lax.ppermute(x, 'blk', shift_pairs(n, 1))]
  transfers between devices with their start and end apart: 30 -> 35, of which waited for: 11 -> 14; matrix products, arithmetic and copies ran while one was open for 7% -> 4% of each run, Pallas kernels for 24% -> 24%
where the time goes in v8:
time: 88.7 us; the launch traced here: 88.3 us
  starting transfers between devices  34.2 us (39%)
  Pallas kernels  23.8 us (27%)
  waiting for transfers between devices  23.6 us (27%)
  local copies, waits for them, and re-layouts  4.79 us (5%)
  other arithmetic  1.71 us (2%)
    pallas_call x1, Pallas kernels, ring_body(): pl.pallas_call(functools.partial(rotate_out_kernel, tok_rows), out_shape=...  9.23 us
    ppermute x6, starting transfers between devices, ring_body(): lax.ppermute(x, 'blk', xor_pairs(n, 4 * key))  8.83 us
    ppermute x6, waiting for transfers between devices, ring_body(): lax.ppermute(x, 'blk', xor_pairs(n, 4 * key))  8.24 us
    pallas_call x1, Pallas kernels, ring_body(): pl.pallas_call(functools.partial(scale_kernel, begun), out_shape=jax.Shap...  6.26 us
    ppermute x4, starting transfers between devices, ring_body(): to_right = lambda x: lax.ppermute(x, 'blk', shift_pairs(n, 1))  6.23 us
    ppermute x3, starting transfers between devices, ring_body(): lax.ppermute(both, 'blk', xor_pairs(n, 4 * key))  5.68 us
    ppermute x13, waiting for transfers between devices, swap(): return lax.ppermute(x, 'blk', xor_pairs(n, 1))  5.34 us
    pallas_call x1, Pallas kernels, ring_body(): pl.pallas_call(functools.partial(project_kernel, (0, 6, len(pieces))), ou...  4.37 us
  transfers between devices with their start and end apart: 35, of which 14 were waited for; matrix products, arithmetic and copies ran while one was open for 4% of the time, Pallas kernels for 24%

profile of v8, /device:TPU:0, one launch (start us, length us, event | category | flops | bytes accessed | tf_op | source)
XLA Modules:
  0.0 88.3 jit_solution(4456147934265919567)
XLA Ops:
  1.6 3.1 %collective-permute-start = (bf16[2,18432]{1,0:T(2,128)(2,1)S(1)}, bf16[2,18432]{1,0:T(2,128)(2,1)S(1)}, u32[]{:S(2)}, u32[]{:S(2)}) collective-permute-start(bf16[2,18432]{1,0:T(2,128)(2,1)S(1)} %constant_dynamic-update-slice_fusion.refs_0_), channel_id=1, source_target_pairs={{0,4},{1,5},{2,6},{3,7},{4,0},{5,1},{6,2},{7,3},{8,12},{9,13},{10,... | collective-permute-start | bytes 221192 | tf_op jit(solution)/shard_map/ppermute | solution.py:289
  4.7 2.6 %collective-permute-start.1 = (bf16[2,18432]{1,0:T(2,128)(2,1)S(1)}, bf16[2,18432]{1,0:T(2,128)(2,1)S(1)}, u32[]{:S(2)}, u32[]{:S(2)}) collective-permute-start(bf16[2,18432]{1,0:T(2,128)(2,1)S(1)} %constant_dynamic-update-slice_fusion.refs_0_), channel_id=1, source_target_pairs={{0,8},{1,9},{2,10},{3,11},{4,12},{5,13},{6,14},{7,15},{8,0},{9,1},... | collective-permute-start | bytes 221192 | tf_op jit(solution)/shard_map/ppermute | solution.py:289
  7.3 2.9 %copy.8 = bf16[4096,256]{0,1:T(8,128)(2,1)S(1)} copy(bf16[4096,256]{1,0:T(8,128)(2,1)} %param.10) | data formatting | bytes 4194304 | tf_op args[3]
  10.2 2.3 %collective-permute-done.1.refs_2_ = bf16[2,18432]{1,0:T(2,128)(2,1)S(1)} collective-permute-done((bf16[2,18432]{1,0:T(2,128)(2,1)S(1)}, bf16[2,18432]{1,0:T(2,128)(2,1)S(1)}, u32[]{:S(2)}, u32[]{:S(2)}) %collective-permute-start.1) | collective-permute-done | bytes 73760 | tf_op jit(solution)/shard_map/ppermute | solution.py:289
  13.6 1.6 %collective-permute-start.4 = (bf16[4,2,4096]{2,1,0:T(2,128)(2,1)S(1)}, bf16[4,2,4096]{2,1,0:T(2,128)(2,1)S(1)}, u32[]{:S(2)}, u32[]{:S(2)}) collective-permute-start(bf16[4,2,4096]{2,1,0:T(2,128)(2,1)S(1)} %get-tuple-element.57), channel_id=1, source_target_pairs={{0,2},{1,3},{2,0},{3,1},{4,6},{5,7},{6,4},{7,5},{8,10},{9,11},{10,... | collective-permute-start | bytes 196616 | tf_op jit(solution)/shard_map/ppermute | solution.py:302
  15.7 2.9 %collective-permute-done.4 = bf16[4,2,4096]{2,1,0:T(2,128)(2,1)S(1)} collective-permute-done((bf16[4,2,4096]{2,1,0:T(2,128)(2,1)S(1)}, bf16[4,2,4096]{2,1,0:T(2,128)(2,1)S(1)}, u32[]{:S(2)}, u32[]{:S(2)}) %collective-permute-start.4) | collective-permute-done | bytes 65568 | tf_op jit(solution)/shard_map/ppermute | solution.py:302
  22.3 1.5 %rotate_in.1 = bf16[8,32,256]{2,1,0:T(8,128)(2,1)} custom-call(bf16[16,4096]{1,0:T(8,128)(2,1)S(1)} %reshape.6.near_ref, bf16[16,4096]{1,0:T(8,128)(2,1)S(1)} %collective-permute-done.5.far_ref, bf16[256,4096]{1,0:T(8,128)(2,1)S(1)} %bitcast.3), custom_call_target="tpu_custom_call" | custom-call | tf_op jit(solution)/shard_map/rotate_in/pallas_call | solution.py:312
  23.9 2.9 %collective-permute-done.6.refs_2_ = bf16[256,512]{1,0:T(8,128)(2,1)S(1)} collective-permute-done((bf16[256,512]{1,0:T(8,128)(2,1)S(1)}, bf16[256,512]{1,0:T(8,128)(2,1)S(1)}, u32[]{:S(2)}, u32[]{:S(2)}) %collective-permute-start.6) | collective-permute-done | bytes 262176 | tf_op jit(solution)/shard_map/ppermute | solution.py:280
  26.8 1.5 %pad_maximum_fusion = bf16[8,2,14336]{2,1,0:T(2,128)(2,1)S(1)} fusion(bf16[4,2,14336]{2,1,0:T(2,128)(2,1)} %collective-permute-done.3, bf16[4,2,14336]{2,1,0:T(2,128)(2,1)S(1)} %get-tuple-element.56), kind=kLoop, calls=%fused_computation | loop fusion | flops 229376 | bytes 917504 | tf_op jit(solution)/shard_map/concatenate | solution.py:322
  31.6 4.0 %all-to-all-start = ((bf16[8,32,256]{2,1,0:T(8,128)(2,1)}), bf16[8,32,256]{2,1,0:T(8,128)(2,1)S(1)}, u32[]{:S(2)}, u32[]{:S(2)}) async-start(bf16[8,32,256]{2,1,0:T(8,128)(2,1)} %rotate_in.1), calls=%async_computation | async-start | bytes 262144 | tf_op jit(solution)/shard_map/all_to_all | solution.py:48
  35.7 9.2 %rotate_out.1.aligned_ref = bf16[896,32]{1,0:T(8,128)(2,1)S(1)} custom-call(bf16[16,14336]{1,0:T(8,128)(2,1)S(1)} %reshape.7.near_ref, bf16[16,14336]{1,0:T(8,128)(2,1)S(1)} %collective-permute-done.8.far_ref, bf16[14336,896]{1,0:T(8,128)(2,1)} %basis_out_ref.1, s32[16]{0:T(128)S(1)} %copy-done.1), custom_call_target="tpu_custom_call" | custom-call | flops 822083584 | bytes 25690112 | tf_op jit(solution)/shard_map/rotate_out/pallas_call | solution.py:330
  45.0 2.1 %collective-permute-start.15 = (bf16[256,512]{1,0:T(8,128)(2,1)}, bf16[256,512]{1,0:T(8,128)(2,1)S(1)}, u32[]{:S(2)}, u32[]{:S(2)}) collective-permute-start(bf16[256,512]{1,0:T(8,128)(2,1)} %collective-permute-done.9.refs_6_), channel_id=1, source_target_pairs={{0,4},{1,5},{4,8},{5,9},{8,12},{9,13},{12,14},{13,15},{14,10},{15,... | collective-permute-start | bytes 786440 | tf_op jit(solution)/shard_map/ppermute | solution.py:280
  47.6 1.6 %collective-permute-done.14.far_ref = bf16[8,32,256]{2,1,0:T(8,128)(2,1)S(1)} collective-permute-done((bf16[8,32,256]{2,1,0:T(8,128)(2,1)S(1)}, bf16[8,32,256]{2,1,0:T(8,128)(2,1)S(1)}, u32[]{:S(2)}, u32[]{:S(2)}) %collective-permute-start.14) | collective-permute-done | bytes 131104 | tf_op jit(solution)/shard_map/ppermute | solution.py:43
  49.2 6.3 %scale.1.scaled_ref = bf16[896,4096]{1,0:T(8,128)(2,1)S(1)} custom-call(bf16[896,32]{1,0:T(8,128)(2,1)S(1)} %rotate_out.1.aligned_ref, bf16[8,32,256]{2,1,0:T(8,128)(2,1)S(1)} %all-to-all-done.near_ref, bf16[8,32,256]{2,1,0:T(8,128)(2,1)S(1)} %collective-permute-done.14.far_ref, s32[32]{0:T(128)S(1)} %copy-done, f32[896,4096]{1,0:T(8,128)} %eigen_ref.1), custom_call_target="tpu_custom_call" | custom-call | flops 234881024 | bytes 22020096 | tf_op jit(solution)/shard_map/scale/pallas_call | solution.py:360
  56.1 1.9 %collective-permute-start.21 = (bf16[128,512]{1,0:T(8,128)(2,1)S(1)}, bf16[128,512]{1,0:T(8,128)(2,1)S(1)}, u32[]{:S(2)}, u32[]{:S(2)}) collective-permute-start(bf16[128,512]{1,0:T(8,128)(2,1)S(1)} %slice.10), channel_id=1, source_target_pairs={{0,4},{1,5},{4,8},{5,9},{8,12},{9,13},{12,14},{13,15},{14,10},{15,... | collective-permute-start | bytes 393224 | tf_op jit(solution)/shard_map/ppermute | solution.py:280
  58.2 4.4 %project.1 = (f32[896,512]{1,0:T(8,128)S(1)}, bf16[768,896]{1,0:T(8,128)(2,1)S(1)}) custom-call(bf16[896,4096]{1,0:T(8,128)(2,1)S(1)} %scale.1.scaled_ref, bf16[14336,896]{1,0:T(8,128)(2,1)} %basis_out_ref.1, bf16[256,512]{1,0:T(8,128)(2,1)S(1)} %slice_bitcast_fusion.refs_0_, bf16[256,512]{1,0:T(8,128)(2,1)S(1)} %collective-permute-done.11.refs_1_, ...), custom_call_target="tpu_custom_call" | custom-call | flops 3758096384 | bytes 11534336 | tf_op jit(solution)/shard_map/project/pallas_call | solution.py:385
  64.9 1.6 %window.1 = (bf16[8,48,512]{2,1,0:T(8,128)(2,1)S(1)}, f32[8,48,512]{2,1,0:T(8,128)S(1)}) custom-call(bf16[768,896]{1,0:T(8,128)(2,1)S(1)} %get-tuple-element.80.window_ref, bf16[896,4096]{1,0:T(8,128)(2,1)S(1)} %scale.1.scaled_ref, f32[896,512]{1,0:T(8,128)S(1)} %get-tuple-element.82.projected_ref, bf16[128,512]{1,0:T(8,128)(2,1)S(1)} %collective-permute-done.21.refs_0_, ...), custom_call_target="tpu_custom_call" | custom-call | flops 704643072 | bytes 6094848 | tf_op jit(solution)/shard_map/window/pallas_call | solution.py:409
  69.7 1.4 %collective-permute-start.27 = (bf16[2,48,256]{2,1,0:T(8,128)(2,1)S(1)}, bf16[2,48,256]{2,1,0:T(8,128)(2,1)S(1)}, u32[]{:S(2)}, u32[]{:S(2)}) collective-permute-start(bf16[2,48,256]{2,1,0:T(8,128)(2,1)S(1)} %get-tuple-element.91), channel_id=1, source_target_pairs={{0,4},{1,5},{2,6},{3,7},{4,0},{5,1},{6,2},{7,3},{8,12},{9,13},{10,... | collective-permute-start | bytes 147464 | tf_op jit(solution)/shard_map/ppermute | solution.py:441
  71.1 2.4 %collective-permute-start.28 = (bf16[2,48,256]{2,1,0:T(8,128)(2,1)S(1)}, bf16[2,48,256]{2,1,0:T(8,128)(2,1)S(1)}, u32[]{:S(2)}, u32[]{:S(2)}) collective-permute-start(bf16[2,48,256]{2,1,0:T(8,128)(2,1)S(1)} %get-tuple-element.92), channel_id=1, source_target_pairs={{0,8},{1,9},{2,10},{3,11},{4,12},{5,13},{6,14},{7,15},{8,0},{9,1},... | collective-permute-start | bytes 147464 | tf_op jit(solution)/shard_map/ppermute | solution.py:441
  74.1 3.1 %collective-permute-done.28.refs_1_ = bf16[2,48,256]{2,1,0:T(8,128)(2,1)S(1)} collective-permute-done((bf16[2,48,256]{2,1,0:T(8,128)(2,1)S(1)}, bf16[2,48,256]{2,1,0:T(8,128)(2,1)S(1)}, u32[]{:S(2)}, u32[]{:S(2)}) %collective-permute-start.28) | collective-permute-done | bytes 49184 | tf_op jit(solution)/shard_map/ppermute | solution.py:441
  77.2 2.3 %collective-permute-done.29.refs_2_ = bf16[2,48,256]{2,1,0:T(8,128)(2,1)S(1)} collective-permute-done((bf16[2,48,256]{2,1,0:T(8,128)(2,1)S(1)}, bf16[2,48,256]{2,1,0:T(8,128)(2,1)S(1)}, u32[]{:S(2)}, u32[]{:S(2)}) %collective-permute-start.29) | collective-permute-done | bytes 49184 | tf_op jit(solution)/shard_map/ppermute | solution.py:441
  80.4 1.6 %collective-permute-start.32 = (bf16[48,256]{1,0:T(8,128)(2,1)S(1)}, bf16[48,256]{1,0:T(8,128)(2,1)S(1)}, u32[]{:S(2)}, u32[]{:S(2)}) collective-permute-start(bf16[48,256]{1,0:T(8,128)(2,1)S(1)} %get-tuple-element.97), channel_id=1, source_target_pairs={{0,8},{1,9},{2,10},{3,11},{4,12},{5,13},{6,14},{7,15},{8,0},{9,1},... | collective-permute-start | bytes 73736 | tf_op jit(solution)/shard_map/ppermute | solution.py:441
  82.0 2.7 %collective-permute-start.33 = (bf16[48,256]{1,0:T(8,128)(2,1)S(1)}, bf16[48,256]{1,0:T(8,128)(2,1)S(1)}, u32[]{:S(2)}, u32[]{:S(2)}) collective-permute-start(bf16[48,256]{1,0:T(8,128)(2,1)S(1)} %get-tuple-element.98), channel_id=1, source_target_pairs={{0,12},{1,13},{2,14},{3,15},{4,8},{5,9},{6,10},{7,11},{8,4},{9,5},... | collective-permute-start | bytes 73736 | tf_op jit(solution)/shard_map/ppermute | solution.py:441
  85.2 2.5 %collective-permute-done.33.refs_2_ = bf16[48,256]{1,0:T(8,128)(2,1)S(1)} collective-permute-done((bf16[48,256]{1,0:T(8,128)(2,1)S(1)}, bf16[48,256]{1,0:T(8,128)(2,1)S(1)}, u32[]{:S(2)}, u32[]{:S(2)}) %collective-permute-start.33) | collective-permute-done | bytes 24608 | tf_op jit(solution)/shard_map/ppermute | solution.py:441
  (70 shorter events, 19.6 us)
Async XLA Ops:
  1.6 8.6 %collective-permute-start = (bf16[2,18432]{1,0:T(2,128)(2,1)S(1)}, bf16[2,18432]{1,0:T(2,128)(2,1)S(1)}, u32[]{:S(2)}, u32[]{:S(2)}) collective-permute-start(bf16[2,18432]{1,0:T(2,128)(2,1)S(1)} %constant_dynamic-update-slice_fusion.refs_0_), channel_id=1, source_target_pairs={{0,4},{1,5},{2,6},{3,7},{4,0},{5,1},{6,2},{7,3},{8,12},{9,13},{10,... | collective-permute-start | bytes 221192 | tf_op jit(solution)/shard_map/ppermute | solution.py:289
  4.7 7.8 %collective-permute-start.1 = (bf16[2,18432]{1,0:T(2,128)(2,1)S(1)}, bf16[2,18432]{1,0:T(2,128)(2,1)S(1)}, u32[]{:S(2)}, u32[]{:S(2)}) collective-permute-start(bf16[2,18432]{1,0:T(2,128)(2,1)S(1)} %constant_dynamic-update-slice_fusion.refs_0_), channel_id=1, source_target_pairs={{0,8},{1,9},{2,10},{3,11},{4,12},{5,13},{6,14},{7,15},{8,0},{9,1},... | collective-permute-start | bytes 221192 | tf_op jit(solution)/shard_map/ppermute | solution.py:289
  7.3 6.3 %collective-permute-start.2 = (bf16[2,18432]{1,0:T(2,128)(2,1)S(1)}, bf16[2,18432]{1,0:T(2,128)(2,1)S(1)}, u32[]{:S(2)}, u32[]{:S(2)}) collective-permute-start(bf16[2,18432]{1,0:T(2,128)(2,1)S(1)} %constant_dynamic-update-slice_fusion.refs_0_), channel_id=1, source_target_pairs={{0,12},{1,13},{2,14},{3,15},{4,8},{5,9},{6,10},{7,11},{8,4},{9,5},... | collective-permute-start | bytes 221192 | tf_op jit(solution)/shard_map/ppermute | solution.py:289
  13.6 5.1 %collective-permute-start.4 = (bf16[4,2,4096]{2,1,0:T(2,128)(2,1)S(1)}, bf16[4,2,4096]{2,1,0:T(2,128)(2,1)S(1)}, u32[]{:S(2)}, u32[]{:S(2)}) collective-permute-start(bf16[4,2,4096]{2,1,0:T(2,128)(2,1)S(1)} %get-tuple-element.57), channel_id=1, source_target_pairs={{0,2},{1,3},{2,0},{3,1},{4,6},{5,7},{6,4},{7,5},{8,10},{9,11},{10,... | collective-permute-start | bytes 196616 | tf_op jit(solution)/shard_map/ppermute | solution.py:302
  15.2 8.7 %collective-permute-start.3 = (bf16[4,2,14336]{2,1,0:T(2,128)(2,1)S(1)}, bf16[4,2,14336]{2,1,0:T(2,128)(2,1)}, u32[]{:S(2)}, u32[]{:S(2)}) collective-permute-start(bf16[4,2,14336]{2,1,0:T(2,128)(2,1)S(1)} %get-tuple-element.56), channel_id=1, source_target_pairs={{0,2},{1,3},{2,0},{3,1},{4,6},{5,7},{6,4},{7,5},{8,10},{9,11},{10,... | collective-permute-start | bytes 688136 | tf_op jit(solution)/shard_map/ppermute | solution.py:303
  18.7 8.1 %collective-permute-start.6 = (bf16[256,512]{1,0:T(8,128)(2,1)S(1)}, bf16[256,512]{1,0:T(8,128)(2,1)S(1)}, u32[]{:S(2)}, u32[]{:S(2)}) collective-permute-start(bf16[256,512]{1,0:T(8,128)(2,1)S(1)} %slice_bitcast_fusion.refs_0_), channel_id=1, source_target_pairs={{0,4},{1,5},{4,8},{5,9},{8,12},{9,13},{12,14},{13,15},{14,10},{15,... | collective-permute-start | bytes 786440 | tf_op jit(solution)/shard_map/ppermute | solution.py:280
  19.7 7.1 %collective-permute-start.7 = (bf16[256,512]{1,0:T(8,128)(2,1)S(1)}, bf16[256,512]{1,0:T(8,128)(2,1)S(1)}, u32[]{:S(2)}, u32[]{:S(2)}) collective-permute-start(bf16[256,512]{1,0:T(8,128)(2,1)S(1)} %slice_bitcast_fusion.refs_0_), channel_id=1, source_target_pairs={{0,2},{1,3},{4,0},{5,1},{8,4},{9,5},{12,8},{13,9},{14,12},{15,13},... | collective-permute-start | bytes 786440 | tf_op jit(solution)/shard_map/ppermute | solution.py:281
  28.6 16.3 %collective-permute-start.11 = (bf16[256,512]{1,0:T(8,128)(2,1)S(1)}, bf16[256,512]{1,0:T(8,128)(2,1)S(1)}, u32[]{:S(2)}, u32[]{:S(2)}) collective-permute-start(bf16[256,512]{1,0:T(8,128)(2,1)S(1)} %slice_bitcast_fusion.refs_0_), channel_id=1, source_target_pairs={{0,1},{1,0},{2,3},{3,2},{4,5},{5,4},{6,7},{7,6},{8,9},{9,8},{10,11... | collective-permute-start | bytes 786440 | tf_op jit(solution)/shard_map/ppermute | solution.py:43
  29.1 15.8 %collective-permute-start.10 = (bf16[256,512]{1,0:T(8,128)(2,1)S(1)}, bf16[256,512]{1,0:T(8,128)(2,1)S(1)}, u32[]{:S(2)}, u32[]{:S(2)}) collective-permute-start(bf16[256,512]{1,0:T(8,128)(2,1)S(1)} %collective-permute-done.7.refs_4_), channel_id=1, source_target_pairs={{0,2},{1,3},{4,0},{5,1},{8,4},{9,5},{12,8},{13,9},{14,12},{15,13},... | collective-permute-start | bytes 786440 | tf_op jit(solution)/shard_map/ppermute | solution.py:281
  30.0 15.0 %collective-permute-start.13 = (bf16[256,512]{1,0:T(8,128)(2,1)S(1)}, bf16[256,512]{1,0:T(8,128)(2,1)S(1)}, u32[]{:S(2)}, u32[]{:S(2)}) collective-permute-start(bf16[256,512]{1,0:T(8,128)(2,1)S(1)} %collective-permute-done.7.refs_4_), channel_id=1, source_target_pairs={{0,1},{1,0},{2,3},{3,2},{4,5},{5,4},{6,7},{7,6},{8,9},{9,8},{10,11... | collective-permute-start | bytes 786440 | tf_op jit(solution)/shard_map/ppermute | solution.py:43
  30.0 14.9 %collective-permute-start.12 = (bf16[256,512]{1,0:T(8,128)(2,1)S(1)}, bf16[256,512]{1,0:T(8,128)(2,1)S(1)}, u32[]{:S(2)}, u32[]{:S(2)}) collective-permute-start(bf16[256,512]{1,0:T(8,128)(2,1)S(1)} %collective-permute-done.6.refs_2_), channel_id=1, source_target_pairs={{0,1},{1,0},{2,3},{3,2},{4,5},{5,4},{6,7},{7,6},{8,9},{9,8},{10,11... | collective-permute-start | bytes 786440 | tf_op jit(solution)/shard_map/ppermute | solution.py:43
  30.5 14.5 %collective-permute-start.9 = (bf16[256,512]{1,0:T(8,128)(2,1)S(1)}, bf16[256,512]{1,0:T(8,128)(2,1)}, u32[]{:S(2)}, u32[]{:S(2)}) collective-permute-start(bf16[256,512]{1,0:T(8,128)(2,1)S(1)} %collective-permute-done.6.refs_2_), channel_id=1, source_target_pairs={{0,4},{1,5},{4,8},{5,9},{8,12},{9,13},{12,14},{13,15},{14,10},{15,... | collective-permute-start | bytes 786440 | tf_op jit(solution)/shard_map/ppermute | solution.py:280
  31.6 13.3 %all-to-all-start = ((bf16[8,32,256]{2,1,0:T(8,128)(2,1)}), bf16[8,32,256]{2,1,0:T(8,128)(2,1)S(1)}, u32[]{:S(2)}, u32[]{:S(2)}) async-start(bf16[8,32,256]{2,1,0:T(8,128)(2,1)} %rotate_in.1), calls=%async_computation | async-start | bytes 262144 | tf_op jit(solution)/shard_map/all_to_all | solution.py:48
  45.0 10.5 %collective-permute-start.15 = (bf16[256,512]{1,0:T(8,128)(2,1)}, bf16[256,512]{1,0:T(8,128)(2,1)S(1)}, u32[]{:S(2)}, u32[]{:S(2)}) collective-permute-start(bf16[256,512]{1,0:T(8,128)(2,1)} %collective-permute-done.9.refs_6_), channel_id=1, source_target_pairs={{0,4},{1,5},{4,8},{5,9},{8,12},{9,13},{12,14},{13,15},{14,10},{15,... | collective-permute-start | bytes 786440 | tf_op jit(solution)/shard_map/ppermute | solution.py:280
  47.0 8.4 %collective-permute-start.16 = (bf16[256,512]{1,0:T(8,128)(2,1)S(1)}, bf16[256,512]{1,0:T(8,128)(2,1)S(1)}, u32[]{:S(2)}, u32[]{:S(2)}) collective-permute-start(bf16[256,512]{1,0:T(8,128)(2,1)S(1)} %collective-permute-done.10.refs_8_), channel_id=1, source_target_pairs={{0,2},{1,3},{4,0},{5,1},{8,4},{9,5},{12,8},{13,9},{14,12},{15,13},... | collective-permute-start | bytes 786440 | tf_op jit(solution)/shard_map/ppermute | solution.py:281
  47.1 8.4 %collective-permute-start.17 = (bf16[256,512]{1,0:T(8,128)(2,1)}, bf16[256,512]{1,0:T(8,128)(2,1)S(1)}, u32[]{:S(2)}, u32[]{:S(2)}) collective-permute-start(bf16[256,512]{1,0:T(8,128)(2,1)} %collective-permute-done.9.refs_6_), channel_id=1, source_target_pairs={{0,1},{1,0},{2,3},{3,2},{4,5},{5,4},{6,7},{7,6},{8,9},{9,8},{10,11... | collective-permute-start | bytes 786440 | tf_op jit(solution)/shard_map/ppermute | solution.py:43
  47.1 8.4 %collective-permute-start.18 = (bf16[256,512]{1,0:T(8,128)(2,1)S(1)}, bf16[256,512]{1,0:T(8,128)(2,1)S(1)}, u32[]{:S(2)}, u32[]{:S(2)}) collective-permute-start(bf16[256,512]{1,0:T(8,128)(2,1)S(1)} %collective-permute-done.10.refs_8_), channel_id=1, source_target_pairs={{0,1},{1,0},{2,3},{3,2},{4,5},{5,4},{6,7},{7,6},{8,9},{9,8},{10,11... | collective-permute-start | bytes 786440 | tf_op jit(solution)/shard_map/ppermute | solution.py:43
  56.1 6.5 %collective-permute-start.21 = (bf16[128,512]{1,0:T(8,128)(2,1)S(1)}, bf16[128,512]{1,0:T(8,128)(2,1)S(1)}, u32[]{:S(2)}, u32[]{:S(2)}) collective-permute-start(bf16[128,512]{1,0:T(8,128)(2,1)S(1)} %slice.10), channel_id=1, source_target_pairs={{0,4},{1,5},{4,8},{5,9},{8,12},{9,13},{12,14},{13,15},{14,10},{15,... | collective-permute-start | bytes 393224 | tf_op jit(solution)/shard_map/ppermute | solution.py:280
  58.1 5.3 %collective-permute-start.22 = (bf16[128,512]{1,0:T(8,128)(2,1)S(1)}, bf16[128,512]{1,0:T(8,128)(2,1)S(1)}, u32[]{:S(2)}, u32[]{:S(2)}) collective-permute-start(bf16[128,512]{1,0:T(8,128)(2,1)S(1)} %slice.11), channel_id=1, source_target_pairs={{0,2},{1,3},{4,0},{5,1},{8,4},{9,5},{12,8},{13,9},{14,12},{15,13},... | collective-permute-start | bytes 393224 | tf_op jit(solution)/shard_map/ppermute | solution.py:281
  68.4 11.9 %collective-permute-start.26 = (bf16[4,48,256]{2,1,0:T(8,128)(2,1)S(1)}, bf16[4,48,256]{2,1,0:T(8,128)(2,1)S(1)}, u32[]{:S(2)}, u32[]{:S(2)}) collective-permute-start(bf16[4,48,256]{2,1,0:T(8,128)(2,1)S(1)} %get-tuple-element.88), channel_id=1, source_target_pairs={{0,2},{1,3},{2,0},{3,1},{4,6},{5,7},{6,4},{7,5},{8,10},{9,11},{10,... | collective-permute-start | bytes 294920 | tf_op jit(solution)/shard_map/ppermute | solution.py:439
  71.1 6.0 %collective-permute-start.28 = (bf16[2,48,256]{2,1,0:T(8,128)(2,1)S(1)}, bf16[2,48,256]{2,1,0:T(8,128)(2,1)S(1)}, u32[]{:S(2)}, u32[]{:S(2)}) collective-permute-start(bf16[2,48,256]{2,1,0:T(8,128)(2,1)S(1)} %get-tuple-element.92), channel_id=1, source_target_pairs={{0,8},{1,9},{2,10},{3,11},{4,12},{5,13},{6,14},{7,15},{8,0},{9,1},... | collective-permute-start | bytes 147464 | tf_op jit(solution)/shard_map/ppermute | solution.py:441
  73.5 5.9 %collective-permute-start.29 = (bf16[2,48,256]{2,1,0:T(8,128)(2,1)S(1)}, bf16[2,48,256]{2,1,0:T(8,128)(2,1)S(1)}, u32[]{:S(2)}, u32[]{:S(2)}) collective-permute-start(bf16[2,48,256]{2,1,0:T(8,128)(2,1)S(1)} %get-tuple-element.93), channel_id=1, source_target_pairs={{0,12},{1,13},{2,14},{3,15},{4,8},{5,9},{6,10},{7,11},{8,4},{9,5},... | collective-permute-start | bytes 147464 | tf_op jit(solution)/shard_map/ppermute | solution.py:441
  79.5 5.3 %collective-permute-start.30 = (bf16[48,256]{1,0:T(8,128)(2,1)S(1)}, bf16[48,256]{1,0:T(8,128)(2,1)S(1)}, u32[]{:S(2)}, u32[]{:S(2)}) collective-permute-start(bf16[48,256]{1,0:T(8,128)(2,1)S(1)} %get-tuple-element.95), channel_id=1, source_target_pairs={{0,2},{1,3},{2,0},{3,1},{4,6},{5,7},{6,4},{7,5},{8,10},{9,11},{10,... | collective-permute-start | bytes 73736 | tf_op jit(solution)/shard_map/ppermute | solution.py:439
  82.0 5.6 %collective-permute-start.33 = (bf16[48,256]{1,0:T(8,128)(2,1)S(1)}, bf16[48,256]{1,0:T(8,128)(2,1)S(1)}, u32[]{:S(2)}, u32[]{:S(2)}) collective-permute-start(bf16[48,256]{1,0:T(8,128)(2,1)S(1)} %get-tuple-element.98), channel_id=1, source_target_pairs={{0,12},{1,13},{2,14},{3,15},{4,8},{5,9},{6,10},{7,11},{8,4},{9,5},... | collective-permute-start | bytes 73736 | tf_op jit(solution)/shard_map/ppermute | solution.py:441
  (13 other events, 56.8 us)

commit v9 on v7

--- a/solution.py
+++ b/solution.py
@@ -54,11 +54,9 @@
 
 def held_tokens(me, tokens, tok_rows):
     row = lax.broadcasted_iota(jnp.int32, (tokens, tokens), 1)
-    chips = tokens // tok_rows // 2
-    place = (row >> bits_of(tok_rows)) & (chips - 1)
-    chip = jnp.zeros_like(row)
-    for bit in range(bits_of(chips)):
-        chip |= ((place >> bit) & 1) << (bits_of(chips) - 1 - bit)
+    pairs = tokens // tok_rows // 4
+    place = row >> bits_of(tok_rows)
+    chip = 2 * (place & (pairs - 1)) + ((place >> bits_of(pairs)) & 1)
     other = row >> bits_of(tokens // 2)
     device = me ^ (2 * chip + other)
     return (device << bits_of(tok_rows)) + (row & (tok_rows - 1))
@@ -67,6 +65,14 @@
 def reorder(wanted, held, rotated):
     order = jnp.where(wanted == held, 1.0, 0.0).astype(jnp.bfloat16)
     return jnp.dot(order, rotated.astype(jnp.bfloat16), preferred_element_type=jnp.float32)
+
+
+def part_kernel(*refs):
+    grads_ref, acts_ref = refs[-2:]
+    first = grads_ref.shape[2]
+    for at, ref in enumerate(refs[:-2]):
+        grads_ref[at] = ref[0, :, :first]
+        acts_ref[at] = ref[0, :, first:]
 
 
 def rotate_in_kernel(tok_rows, near_ref, far_ref, basis_ref, out_ref):
@@ -82,15 +88,44 @@
         out_ref[copy] = ordered
 
 
+def hold_kernel(basis_ref, held_ref, sem):
+    steps, depth = held_ref.shape[:2]
+    copies = [
+        pltpu.make_async_copy(
+            basis_ref.at[pl.ds(step * depth, depth)], held_ref.at[step], sem.at[step]
+        )
+        for step in range(steps)
+    ]
+    for copy in copies:
+        copy.start()
+    for copy in copies:
+        copy.wait()
+
+
 def rotate_out_kernel(
-    tok_rows, near_ref, far_ref, basis_ref, map_ref, out_ref, basis, total, stored_map, sem
+    tok_rows,
+    near_ref,
+    far_ref,
+    held_ref,
+    basis_ref,
+    map_ref,
+    out_ref,
+    basis,
+    total,
+    stored_map,
+    sem,
 ):
     steps, depth = basis.shape[:2]
+    ahead = held_ref.shape[0]
     tokens = total.shape[0]
 
     def copy_of(step):
-        rows = pl.ds(pl.multiple_of(step * depth, depth), depth)
+        rows = pl.ds(pl.multiple_of((ahead + step) * depth, depth), depth)
         return pltpu.make_async_copy(basis_ref.at[rows], basis.at[step], sem.at[step])
+
+    def grads_of(step):
+        columns = pl.ds(pl.multiple_of(step * depth, depth), depth)
+        return jnp.concatenate([near_ref[:, columns], far_ref[:, columns]], axis=0)
 
     @pl.loop(0, steps)
     def _(step):
@@ -100,12 +135,16 @@
     map_copy.start()
     total[...] = jnp.zeros_like(total)
 
+    @pl.loop(0, ahead)
+    def _(step):
+        total[...] += jnp.dot(grads_of(step), held_ref[step], preferred_element_type=jnp.float32)
+
     @pl.loop(0, steps)
     def _(step):
-        columns = pl.ds(pl.multiple_of(step * depth, depth), depth)
-        grads = jnp.concatenate([near_ref[:, columns], far_ref[:, columns]], axis=0)
         copy_of(step).wait()
-        total[...] += jnp.dot(grads, basis[step], preferred_element_type=jnp.float32)
+        total[...] += jnp.dot(
+            grads_of(ahead + step), basis[step], preferred_element_type=jnp.float32
+        )
 
     map_copy.wait()
     row = lax.broadcasted_iota(jnp.int32, (tokens, tokens), 0)
@@ -212,22 +251,11 @@
         send_ref[k] = result[other, :].astype(jnp.bfloat16)
 
 
-def add_core_kernel(keep_ref, got_ref, mine_ref, send_ref):
-    side = lax.rem(lax.axis_index("blk") // 2, 2)
-    for pair in range(mine_ref.shape[0]):
-        mine, other = 2 * pair + side, 2 * pair + 1 - side
-        mine_ref[pair] = keep_ref[mine] + got_ref[mine].astype(jnp.float32)
-        sent = keep_ref[other] + got_ref[other].astype(jnp.float32)
-        send_ref[pair] = sent.astype(jnp.bfloat16)
-
-
-def add_pair_kernel(mine_ref, got_ref, own_ref, *send_refs):
-    me = lax.axis_index("blk") // 4
-    own_ref[...] = mine_ref[me] + got_ref[me].astype(jnp.float32)
-    for key, send_ref in enumerate(send_refs, 1):
-        other = me ^ key
-        sent = mine_ref[other] + got_ref[other].astype(jnp.float32)
-        send_ref[...] = sent.astype(jnp.bfloat16)
+def add_core_kernel(keys, keep_ref, got_ref, own_ref, *send_refs):
+    chip = lax.axis_index("blk") // 2
+    for key, ref in zip((0, *keys), (own_ref, *send_refs)):
+        at = chip ^ key
+        ref[...] = (keep_ref[at] + got_ref[at].astype(jnp.float32)).astype(ref.dtype)
 
 
 def add_chips_kernel(own_ref, *refs):
@@ -259,24 +287,41 @@
     turned = basis_in.T
     own = basis_in[:WC].T
 
+    pairs = chips // 2
+    both = jnp.concatenate([grad_out, activations], axis=1)[None]
+    got = [lax.ppermute(both, "blk", xor_pairs(n, 4 * key)) for key in range(1, pairs)]
+    both, turned, *got = after(both, turned, *got)
+    grads, acts = pl.pallas_call(
+        part_kernel,
+        out_shape=(
+            jax.ShapeDtypeStruct((pairs, tok_rows, full_out), jnp.bfloat16),
+            jax.ShapeDtypeStruct((pairs, tok_rows, full_in), jnp.bfloat16),
+        ),
+        in_specs=[VMEM] * pairs,
+        out_specs=(VMEM, VMEM),
+        compiler_params=pltpu.CompilerParams(vmem_limit_bytes=8 * MIB),
+        name="part",
+    )(both, *got)
+    acts, grads, own = after(acts, grads, own)
+    acts_got = lax.ppermute(acts, "blk", xor_pairs(n, 2))
+    grads_got = lax.ppermute(grads, "blk", xor_pairs(n, 2))
     right, left = [own, to_right(own)], [own, to_left(own)]
 
-    both = jnp.concatenate([grad_out, activations], axis=1)[None]
-    key = n // 2
-    while key > 2:
-        got = lax.ppermute(both, "blk", xor_pairs(n, key))
-        key //= 2
-        if key > 2:
-            both = jnp.concatenate([both, got], axis=0)
-    got, turned = after(got, turned)
-    acts = jnp.concatenate([both[..., full_out:], got[..., full_out:]], axis=0)
-    grads = jnp.concatenate([both[..., :full_out], got[..., :full_out]], axis=0)
-    got = lax.ppermute(acts, "blk", xor_pairs(n, 2))
-    got, right[-1], left[-1] = after(got, right[-1], left[-1])
-    while len(right) < steps - 1:
-        right.append(to_right(right[-1]))
-        left.append(to_left(left[-1]))
-    acts = jnp.concatenate([acts, got], axis=0).reshape(tokens // 2, full_in)
+    depth, ahead = 1024, 4
+    held = pl.pallas_call(
+        hold_kernel,
+        out_shape=jax.ShapeDtypeStruct((ahead, depth, tile_width), jnp.bfloat16),
+        in_specs=[ANY],
+        out_specs=VMEM,
+        scratch_shapes=[pltpu.SemaphoreType.DMA((ahead,))],
+        compiler_params=pltpu.CompilerParams(vmem_limit_bytes=40 * MIB),
+        cost_estimate=pl.CostEstimate(
+            flops=0, bytes_accessed=4 * ahead * depth * tile_width, transcendentals=0
+        ),
+        name="hold",
+    )(basis_out)
+
+    acts = jnp.concatenate([acts, acts_got], axis=0).reshape(tokens // 2, full_in)
     rotated = pl.pallas_call(
         functools.partial(rotate_in_kernel, tok_rows),
         out_shape=jax.ShapeDtypeStruct((chips, tokens, in_width), jnp.bfloat16),
@@ -285,25 +330,35 @@
         compiler_params=pltpu.CompilerParams(vmem_limit_bytes=8 * MIB),
         name="rotate_in",
     )(acts, swap(acts, n), turned)
-    got = lax.ppermute(grads, "blk", xor_pairs(n, 2))
-    got, rotated, right[-1], left[-1] = after(got, rotated, right[-1], left[-1])
+    grads_got, rotated, held, own_far, right[-1], left[-1] = after(
+        grads_got, rotated, held, swap(own, n), right[-1], left[-1]
+    )
     rotated = exchange(rotated, n, 2)
-    grads = jnp.concatenate([grads, got], axis=0).reshape(tokens // 2, full_out)
+    near = [right[0], right[1], left[1]]
+    while len(right) < steps - 1:
+        right.append(to_right(right[-1]))
+        left.append(to_left(left[-1]))
+    grads = jnp.concatenate([grads, grads_got], axis=0).reshape(tokens // 2, full_out)
     grads_far = swap(grads, n)
+    far = [swap(piece, n) for piece in near[1:]]
+    grads, grads_far, right[-1], left[-1], *far = after(
+        grads, grads_far, right[-1], left[-1], *far
+    )
+    near += [right[-1], left[-1]]
+    far = [own_far, *far, swap(right[-1], n), swap(left[-1], n)]
     right.append(to_right(right[-1]))
     left.append(to_left(left[-1]))
 
-    depth = 1024
     aligned = pl.pallas_call(
         functools.partial(rotate_out_kernel, tok_rows),
         out_shape=jax.ShapeDtypeStruct((tile_width, tokens), jnp.bfloat16),
-        in_specs=[VMEM, VMEM, ANY, ANY],
+        in_specs=[VMEM, VMEM, VMEM, ANY, ANY],
         out_specs=VMEM,
         scratch_shapes=[
-            pltpu.VMEM((full_out // depth, depth, tile_width), jnp.bfloat16),
+            pltpu.VMEM((full_out // depth - ahead, depth, tile_width), jnp.bfloat16),
             pltpu.VMEM((tokens, tile_width), jnp.float32),
             pltpu.SMEM(block_map.shape, jnp.int32),
-            pltpu.SemaphoreType.DMA((full_out // depth + 1,)),
+            pltpu.SemaphoreType.DMA((full_out // depth - ahead + 1,)),
         ],
         compiler_params=pltpu.CompilerParams(vmem_limit_bytes=40 * MIB),
         cost_estimate=pl.CostEstimate(
@@ -312,12 +367,16 @@
             transcendentals=0,
         ),
         name="rotate_out",
-    )(grads, grads_far, basis_out, block_map)
-
-    aligned, rotated, right[-1], left[-1] = after(aligned, rotated, right[-1], left[-1])
+    )(grads, grads_far, held, basis_out, block_map)
+
+    aligned, rotated, right[-1], left[-1], *far = after(
+        aligned, rotated, right[-1], left[-1], *far
+    )
     rotated_far = swap(rotated, n)
     cut = in_width // 2
     last = [to_right(right[-1][:cut]), to_left(left[-1][cut:])]
+    near += [right[-1], left[-1]]
+    far += [swap(piece, n) for piece in near[len(far) :]]
     begun = [0] + [at for step in range(1, steps) for at in (step, chips - step)] + [steps]
     blocks = 8
     scaled = pl.pallas_call(
@@ -339,10 +398,10 @@
         name="scale",
     )(aligned, rotated, rotated_far, tile_order, eigenvalues)
 
-    scaled, *last = after(scaled, *last)
+    scaled, *last = after(scaled, *last, *far[-2:])
+    far[-2:] = last[2:]
+    last = last[:2]
     last += [swap(piece, n) for piece in last]
-    near = [right[at] if at < steps else left[chips - at] for at in begun[:-1]]
-    far = [swap(piece, n) for piece in near]
     pieces = [piece for pair in zip(near, far) for piece in pair]
     projected, window = pl.pallas_call(
         functools.partial(project_kernel, (0, 6, len(pieces))),
@@ -384,35 +443,22 @@
         name="window",
     )(window, scaled, projected, *last)
 
+    keys = sorted(range(1, chips), key=lambda key: -(key & -2))
     small = pltpu.CompilerParams(vmem_limit_bytes=8 * MIB)
-    half = (chips // 2, rows, WC)
-    mine, send = pl.pallas_call(
-        add_core_kernel,
-        out_shape=(
-            jax.ShapeDtypeStruct(half, jnp.float32),
-            jax.ShapeDtypeStruct(half, jnp.bfloat16),
-        ),
+    own, *sends = pl.pallas_call(
+        functools.partial(add_core_kernel, keys),
+        out_shape=[jax.ShapeDtypeStruct((rows, WC), jnp.float32)]
+        + [jax.ShapeDtypeStruct((rows, WC), jnp.bfloat16)] * len(keys),
         in_specs=[VMEM, VMEM],
-        out_specs=(VMEM, VMEM),
+        out_specs=[VMEM] * chips,
         compiler_params=small,
         name="add_core",
     )(keep, swap(send, n))
-    got = lax.ppermute(send, "blk", xor_pairs(n, 2))
-    block = (rows, WC)
-    own, *sends = pl.pallas_call(
-        add_pair_kernel,
-        out_shape=[jax.ShapeDtypeStruct(block, jnp.float32)]
-        + [jax.ShapeDtypeStruct(block, jnp.bfloat16)] * (chips // 2 - 1),
-        in_specs=[VMEM, VMEM],
-        out_specs=[VMEM] * (chips // 2),
-        compiler_params=small,
-        name="add_pair",
-    )(mine, got)
-    arrived = [lax.ppermute(x, "blk", xor_pairs(n, 4 * k)) for k, x in enumerate(sends, 1)]
+    arrived = [lax.ppermute(x, "blk", xor_pairs(n, 2 * key)) for key, x in zip(keys, sends)]
     return pl.pallas_call(
         add_chips_kernel,
-        out_shape=jax.ShapeDtypeStruct(block, jnp.float32),
-        in_specs=[VMEM] * (chips // 2),
+        out_shape=jax.ShapeDtypeStruct((rows, WC), jnp.float32),
+        in_specs=[VMEM] * chips,
         out_specs=VMEM,
         compiler_params=small,
         name="add_chips",

time: 92.7 us -> 90 us (0.971)
  waiting for transfers between devices: 28.9 us -> 14.9 us
  local copies, waits for them, and re-layouts: 4.21 us -> 10.8 us
  starting transfers between devices: 29.3 us -> 35.5 us
  other arithmetic: 4.8 us -> 3.27 us
    ppermute x8 -> x12, waiting for transfers between devices: 18.5 us -> 7.06 us  [the longest x7 3.06 us: ring_body(): lax.ppermute(x, 'blk', xor_pairs(n, 2 * key))]
    unnamed x13, local copies, waits for them, and re-layouts: 2.94 us -> 9.63 us
    ppermute x8 -> x12, starting transfers between devices: 14.6 us -> 20 us  [the longest x7 12.2 us: ring_body(): lax.ppermute(x, 'blk', xor_pairs(n, 2 * key))]
    pallas_call x3 -> x4, Pallas kernels: 0.76 us -> 3.97 us  [the longest x1 3.19 us: ring_body(): pl.pallas_call(hold_kernel, out_shape=jax.ShapeDtypeStruct((ahead, depth,...]
    ppermute x4, waiting for transfers between devices: 2.99 us -> 0.01 us  [ring_body(): to_left = lambda x: lax.ppermute(x, 'blk', shift_pairs(n, -1))]
    pallas_call x1, Pallas kernels: 9.22 us -> 7.09 us  [ring_body(): pl.pallas_call(functools.partial(rotate_out_kernel, tok_rows), out_shape=...]
    ppermute x4, waiting for transfers between devices: 4.45 us -> 6.26 us  [ring_body(): to_right = lambda x: lax.ppermute(x, 'blk', shift_pairs(n, 1))]
    ppermute x4, starting transfers between devices: 6.72 us -> 5.09 us  [ring_body(): to_left = lambda x: lax.ppermute(x, 'blk', shift_pairs(n, -1))]
  transfers between devices with their start and end apart: 30 -> 34, of which waited for: 11 -> 9; matrix products, arithmetic and copies ran while one was open for 7% -> 5% of each run, Pallas kernels for 24% -> 25%
where the time goes in v9:
time: 90 us; the launch traced here: 89.6 us
  starting transfers between devices  35.5 us (39%)
  Pallas kernels  24.8 us (28%)
  waiting for transfers between devices  14.9 us (17%)
  local copies, waits for them, and re-layouts  10.8 us (12%)
  other arithmetic  3.27 us (4%)
    ppermute x7, starting transfers between devices, ring_body(): lax.ppermute(x, 'blk', xor_pairs(n, 2 * key))  12.2 us
    unnamed x13, local copies, waits for them, and re-layouts  9.63 us
    pallas_call x1, Pallas kernels, ring_body(): pl.pallas_call(functools.partial(rotate_out_kernel, tok_rows), out_shape=...  7.09 us
    ppermute x4, waiting for transfers between devices, ring_body(): to_right = lambda x: lax.ppermute(x, 'blk', shift_pairs(n, 1))  6.26 us
    pallas_call x1, Pallas kernels, ring_body(): pl.pallas_call(functools.partial(scale_kernel, begun), out_shape=jax.Shap...  6.23 us
    ppermute x3, starting transfers between devices, ring_body(): lax.ppermute(both, 'blk', xor_pairs(n, 4 * key))  5.76 us
    ppermute x4, starting transfers between devices, ring_body(): to_left = lambda x: lax.ppermute(x, 'blk', shift_pairs(n, -1))  5.09 us
    all_to_all x1, starting transfers between devices, exchange(): return lax.all_to_all(x, 'blk', 0, 0, axis_index_groups=groups, tiled=True)  4.85 us
  transfers between devices with their start and end apart: 34, of which 9 were waited for; matrix products, arithmetic and copies ran while one was open for 5% of the time, Pallas kernels for 25%

profile of v9, /device:TPU:0, one launch (start us, length us, event | category | flops | bytes accessed | tf_op | source)
XLA Modules:
  0.0 89.6 jit_solution(10132656019094273818)
XLA Ops:
  0.9 5.1 %collective-permute-start.2 = (bf16[1,2,18432]{2,1,0:T(2,128)(2,1)S(1)}, bf16[1,2,18432]{2,1,0:T(2,128)(2,1)S(1)}, u32[]{:S(2)}, u32[]{:S(2)}) collective-permute-start(bf16[1,2,18432]{2,1,0:T(2,128)(2,1)S(1)} %maximum_bitcast_fusion.refs_0_), channel_id=1, source_target_pairs={{0,12},{1,13},{2,14},{3,15},{4,8},{5,9},{6,10},{7,11},{8,4},{9,5},... | collective-permute-start | bytes 221192 | tf_op jit(solution)/shard_map/ppermute | solution.py:292
  6.7 2.9 %copy.8 = bf16[4096,256]{0,1:T(8,128)(2,1)S(1)} copy(bf16[4096,256]{1,0:T(8,128)(2,1)} %param.10) | data formatting | bytes 4194304 | tf_op args[3]
  9.6 2.6 %collective-permute-done.1.refs_2_ = bf16[1,2,18432]{2,1,0:T(2,128)(2,1)S(1)} collective-permute-done((bf16[1,2,18432]{2,1,0:T(2,128)(2,1)S(1)}, bf16[1,2,18432]{2,1,0:T(2,128)(2,1)S(1)}, u32[]{:S(2)}, u32[]{:S(2)}) %collective-permute-start.1) | collective-permute-done | bytes 73760 | tf_op jit(solution)/shard_map/ppermute | solution.py:292
  12.3 1.6 %collective-permute-start.4 = (bf16[4,2,4096]{2,1,0:T(2,128)(2,1)S(1)}, bf16[4,2,4096]{2,1,0:T(2,128)(2,1)S(1)}, u32[]{:S(2)}, u32[]{:S(2)}) collective-permute-start(bf16[4,2,4096]{2,1,0:T(2,128)(2,1)S(1)} %get-tuple-element.60), channel_id=1, source_target_pairs={{0,2},{1,3},{2,0},{3,1},{4,6},{5,7},{6,4},{7,5},{8,10},{9,11},{10,... | collective-permute-start | bytes 196616 | tf_op jit(solution)/shard_map/ppermute | solution.py:306
  14.4 1.5 %collective-permute-start.7 = (bf16[256,512]{1,0:T(8,128)(2,1)S(1)}, bf16[256,512]{1,0:T(8,128)(2,1)S(1)}, u32[]{:S(2)}, u32[]{:S(2)}) collective-permute-start(bf16[256,512]{1,0:T(8,128)(2,1)S(1)} %slice_bitcast_fusion.refs_0_), channel_id=1, source_target_pairs={{0,4},{1,5},{4,8},{5,9},{8,12},{9,13},{12,14},{13,15},{14,10},{15,... | collective-permute-start | bytes 786440 | tf_op jit(solution)/shard_map/ppermute | solution.py:283
  19.2 3.2 %hold.1.held_ref = bf16[4,1024,896]{2,1,0:T(8,128)(2,1)S(1)} custom-call(bf16[14336,896]{1,0:T(8,128)(2,1)} %basis_out_ref.1), custom_call_target="tpu_custom_call" | custom-call | bytes 14680064 | tf_op jit(solution)/shard_map/hold/pallas_call | solution.py:311
  22.4 2.9 %copy-done = bf16[4,1024,896]{2,1,0:T(8,128)(2,1)} copy-done((bf16[4,1024,896]{2,1,0:T(8,128)(2,1)}, bf16[4,1024,896]{2,1,0:T(8,128)(2,1)S(1)}, u32[]{:S(2)}) %copy-start) | copy-done | bytes 7340056
  25.3 1.5 %rotate_in.1 = bf16[8,32,256]{2,1,0:T(8,128)(2,1)} custom-call(bf16[16,4096]{1,0:T(8,128)(2,1)S(1)} %reshape.6.near_ref, bf16[16,4096]{1,0:T(8,128)(2,1)S(1)} %collective-permute-done.5.far_ref, bf16[256,4096]{1,0:T(8,128)(2,1)S(1)} %bitcast.5), custom_call_target="tpu_custom_call" | custom-call | tf_op jit(solution)/shard_map/rotate_in/pallas_call | solution.py:325
  27.2 1.5 %pad_maximum_fusion = bf16[8,2,14336]{2,1,0:T(2,128)(2,1)S(1)} fusion(bf16[4,2,14336]{2,1,0:T(2,128)(2,1)} %collective-permute-done.3, bf16[4,2,14336]{2,1,0:T(2,128)(2,1)S(1)} %get-tuple-element.59), kind=kLoop, calls=%fused_computation | loop fusion | flops 229376 | bytes 917504 | tf_op jit(solution)/shard_map/concatenate | solution.py:341
  29.6 1.9 %collective-permute-start.11 = (bf16[256,512]{1,0:T(8,128)(2,1)S(1)}, bf16[256,512]{1,0:T(8,128)(2,1)}, u32[]{:S(2)}, u32[]{:S(2)}) collective-permute-start(bf16[256,512]{1,0:T(8,128)(2,1)S(1)} %collective-permute-done.8.refs_4_), channel_id=1, source_target_pairs={{0,2},{1,3},{4,0},{5,1},{8,4},{9,5},{12,8},{13,9},{14,12},{15,13},... | collective-permute-start | bytes 786440 | tf_op jit(solution)/shard_map/ppermute | solution.py:284
  31.6 6.3 %collective-permute-done.10.refs_6_ = bf16[256,512]{1,0:T(8,128)(2,1)S(1)} collective-permute-done((bf16[256,512]{1,0:T(8,128)(2,1)S(1)}, bf16[256,512]{1,0:T(8,128)(2,1)S(1)}, u32[]{:S(2)}, u32[]{:S(2)}) %collective-permute-start.10) | collective-permute-done | bytes 262176 | tf_op jit(solution)/shard_map/ppermute | solution.py:283
  38.6 1.5 %collective-permute-start.14 = (bf16[256,512]{1,0:T(8,128)(2,1)S(1)}, bf16[256,512]{1,0:T(8,128)(2,1)S(1)}, u32[]{:S(2)}, u32[]{:S(2)}) collective-permute-start(bf16[256,512]{1,0:T(8,128)(2,1)S(1)} %collective-permute-done.10.refs_6_), channel_id=1, source_target_pairs={{0,4},{1,5},{4,8},{5,9},{8,12},{9,13},{12,14},{13,15},{14,10},{15,... | collective-permute-start | bytes 786440 | tf_op jit(solution)/shard_map/ppermute | solution.py:283
  40.9 4.8 %all-to-all-start = ((bf16[8,32,256]{2,1,0:T(8,128)(2,1)}), bf16[8,32,256]{2,1,0:T(8,128)(2,1)S(1)}, u32[]{:S(2)}, u32[]{:S(2)}) async-start(bf16[8,32,256]{2,1,0:T(8,128)(2,1)} %rotate_in.1), calls=%async_computation | async-start | bytes 262144 | tf_op jit(solution)/shard_map/all_to_all | solution.py:48
  45.8 3.1 %copy-done.1 = bf16[4,1024,896]{2,1,0:T(8,128)(2,1)S(1)} copy-done((bf16[4,1024,896]{2,1,0:T(8,128)(2,1)S(1)}, bf16[4,1024,896]{2,1,0:T(8,128)(2,1)}, u32[]{:S(2)}) %copy-start.1) | copy-done | bytes 7340056
  48.9 7.1 %rotate_out.1.aligned_ref = bf16[896,32]{1,0:T(8,128)(2,1)S(1)} custom-call(bf16[16,14336]{1,0:T(8,128)(2,1)S(1)} %reshape.7.near_ref, bf16[16,14336]{1,0:T(8,128)(2,1)S(1)} %collective-permute-done.9.far_ref, bf16[4,1024,896]{2,1,0:T(8,128)(2,1)S(1)} %copy-done.1, bf16[14336,896]{1,0:T(8,128)(2,1)} %basis_out_ref.1, s32[16]{0:T(128)S(1)} %copy-done.5), custom_call_target="tpu_custom_call" | custom-call | flops 822083584 | bytes 25690112 | tf_op jit(solution)/shard_map/rotate_out/pallas_call | solution.py:352
  56.7 2.1 %collective-permute-start.20 = (bf16[128,512]{1,0:T(8,128)(2,1)S(1)}, bf16[128,512]{1,0:T(8,128)(2,1)S(1)}, u32[]{:S(2)}, u32[]{:S(2)}) collective-permute-start(bf16[128,512]{1,0:T(8,128)(2,1)S(1)} %slice.11), channel_id=1, source_target_pairs={{0,2},{1,3},{4,0},{5,1},{8,4},{9,5},{12,8},{13,9},{14,12},{15,13},... | collective-permute-start | bytes 393224 | tf_op jit(solution)/shard_map/ppermute | solution.py:284
  58.8 6.2 %scale.1.scaled_ref = bf16[896,4096]{1,0:T(8,128)(2,1)S(1)} custom-call(bf16[896,32]{1,0:T(8,128)(2,1)S(1)} %rotate_out.1.aligned_ref, bf16[8,32,256]{2,1,0:T(8,128)(2,1)S(1)} %all-to-all-done.near_ref, bf16[8,32,256]{2,1,0:T(8,128)(2,1)S(1)} %collective-permute-done.18.far_ref, s32[32]{0:T(128)S(1)} %copy-done.4, f32[896,4096]{1,0:T(8,128)} %eigen_ref.1), custom_call_target="tpu_custom_call" | custom-call | flops 234881024 | bytes 22020096 | tf_op jit(solution)/shard_map/scale/pallas_call | solution.py:382
  65.7 4.4 %project.1 = (f32[896,512]{1,0:T(8,128)S(1)}, bf16[768,896]{1,0:T(8,128)(2,1)S(1)}) custom-call(bf16[896,4096]{1,0:T(8,128)(2,1)S(1)} %scale.1.scaled_ref, bf16[14336,896]{1,0:T(8,128)(2,1)} %basis_out_ref.1, bf16[256,512]{1,0:T(8,128)(2,1)S(1)} %slice_bitcast_fusion.refs_0_, bf16[256,512]{1,0:T(8,128)(2,1)S(1)} %collective-permute-done.6.refs_1_, ...), custom_call_target="tpu_custom_call" | custom-call | flops 3758096384 | bytes 11534336 | tf_op jit(solution)/shard_map/project/pallas_call | solution.py:406
  70.1 1.6 %window.1 = (bf16[8,48,512]{2,1,0:T(8,128)(2,1)S(1)}, f32[8,48,512]{2,1,0:T(8,128)S(1)}) custom-call(bf16[768,896]{1,0:T(8,128)(2,1)S(1)} %get-tuple-element.87.window_ref, bf16[896,4096]{1,0:T(8,128)(2,1)S(1)} %scale.1.scaled_ref, f32[896,512]{1,0:T(8,128)S(1)} %get-tuple-element.88.projected_ref, bf16[128,512]{1,0:T(8,128)(2,1)S(1)} %collective-permute-done.19.refs_0_, ...), custom_call_target="tpu_custom_call" | custom-call | flops 704643072 | bytes 6094848 | tf_op jit(solution)/shard_map/window/pallas_call | solution.py:428
  72.0 1.5 %collective-permute-done.25.got_ref = bf16[8,48,512]{2,1,0:T(8,128)(2,1)S(1)} collective-permute-done((bf16[8,48,512]{2,1,0:T(8,128)(2,1)S(1)}, bf16[8,48,512]{2,1,0:T(8,128)(2,1)S(1)}, u32[]{:S(2)}, u32[]{:S(2)}) %collective-permute-start.25) | collective-permute-done | bytes 393248 | tf_op jit(solution)/shard_map/ppermute | solution.py:43
  73.6 3.9 %collective-permute-start.26 = (bf16[48,512]{1,0:T(8,128)(2,1)S(1)}, bf16[48,512]{1,0:T(8,128)(2,1)S(1)}, u32[]{:S(2)}, u32[]{:S(2)}) collective-permute-start(bf16[48,512]{1,0:T(8,128)(2,1)S(1)} %get-tuple-element.94), channel_id=1, source_target_pairs={{0,12},{1,13},{2,14},{3,15},{4,8},{5,9},{6,10},{7,11},{8,4},{9,5},... | collective-permute-start | bytes 147464 | tf_op jit(solution)/shard_map/ppermute | solution.py:457
  77.5 1.4 %collective-permute-start.27 = (bf16[48,512]{1,0:T(8,128)(2,1)S(1)}, bf16[48,512]{1,0:T(8,128)(2,1)S(1)}, u32[]{:S(2)}, u32[]{:S(2)}) collective-permute-start(bf16[48,512]{1,0:T(8,128)(2,1)S(1)} %get-tuple-element.95), channel_id=1, source_target_pairs={{0,14},{1,15},{2,12},{3,13},{4,10},{5,11},{6,8},{7,9},{8,6},{9,7},... | collective-permute-start | bytes 147464 | tf_op jit(solution)/shard_map/ppermute | solution.py:457
  79.5 1.9 %collective-permute-start.29 = (bf16[48,512]{1,0:T(8,128)(2,1)S(1)}, bf16[48,512]{1,0:T(8,128)(2,1)S(1)}, u32[]{:S(2)}, u32[]{:S(2)}) collective-permute-start(bf16[48,512]{1,0:T(8,128)(2,1)S(1)} %get-tuple-element.97), channel_id=1, source_target_pairs={{0,10},{1,11},{2,8},{3,9},{4,14},{5,15},{6,12},{7,13},{8,2},{9,3},... | collective-permute-start | bytes 147464 | tf_op jit(solution)/shard_map/ppermute | solution.py:457
  82.8 2.0 %collective-permute-start.31 = (bf16[48,512]{1,0:T(8,128)(2,1)S(1)}, bf16[48,512]{1,0:T(8,128)(2,1)S(1)}, u32[]{:S(2)}, u32[]{:S(2)}) collective-permute-start(bf16[48,512]{1,0:T(8,128)(2,1)S(1)} %get-tuple-element.99), channel_id=1, source_target_pairs={{0,6},{1,7},{2,4},{3,5},{4,2},{5,3},{6,0},{7,1},{8,14},{9,15},{10,... | collective-permute-start | bytes 147464 | tf_op jit(solution)/shard_map/ppermute | solution.py:457
  (74 shorter events, 16.6 us)
Async XLA Ops:
  0.9 8.7 %collective-permute-start.2 = (bf16[1,2,18432]{2,1,0:T(2,128)(2,1)S(1)}, bf16[1,2,18432]{2,1,0:T(2,128)(2,1)S(1)}, u32[]{:S(2)}, u32[]{:S(2)}) collective-permute-start(bf16[1,2,18432]{2,1,0:T(2,128)(2,1)S(1)} %maximum_bitcast_fusion.refs_0_), channel_id=1, source_target_pairs={{0,12},{1,13},{2,14},{3,15},{4,8},{5,9},{6,10},{7,11},{8,4},{9,5},... | collective-permute-start | bytes 221192 | tf_op jit(solution)/shard_map/ppermute | solution.py:292
  6.0 6.2 %collective-permute-start.1 = (bf16[1,2,18432]{2,1,0:T(2,128)(2,1)S(1)}, bf16[1,2,18432]{2,1,0:T(2,128)(2,1)S(1)}, u32[]{:S(2)}, u32[]{:S(2)}) collective-permute-start(bf16[1,2,18432]{2,1,0:T(2,128)(2,1)S(1)} %maximum_bitcast_fusion.refs_0_), channel_id=1, source_target_pairs={{0,8},{1,9},{2,10},{3,11},{4,12},{5,13},{6,14},{7,15},{8,0},{9,1},... | collective-permute-start | bytes 221192 | tf_op jit(solution)/shard_map/ppermute | solution.py:292
  6.0 6.2 %collective-permute-start = (bf16[1,2,18432]{2,1,0:T(2,128)(2,1)S(1)}, bf16[1,2,18432]{2,1,0:T(2,128)(2,1)S(1)}, u32[]{:S(2)}, u32[]{:S(2)}) collective-permute-start(bf16[1,2,18432]{2,1,0:T(2,128)(2,1)S(1)} %maximum_bitcast_fusion.refs_0_), channel_id=1, source_target_pairs={{0,4},{1,5},{2,6},{3,7},{4,0},{5,1},{6,2},{7,3},{8,12},{9,13},{10,... | collective-permute-start | bytes 221192 | tf_op jit(solution)/shard_map/ppermute | solution.py:292
  13.9 13.4 %collective-permute-start.8 = (bf16[256,512]{1,0:T(8,128)(2,1)S(1)}, bf16[256,512]{1,0:T(8,128)(2,1)S(1)}, u32[]{:S(2)}, u32[]{:S(2)}) collective-permute-start(bf16[256,512]{1,0:T(8,128)(2,1)S(1)} %slice_bitcast_fusion.refs_0_), channel_id=1, source_target_pairs={{0,2},{1,3},{4,0},{5,1},{8,4},{9,5},{12,8},{13,9},{14,12},{15,13},... | collective-permute-start | bytes 786440 | tf_op jit(solution)/shard_map/ppermute | solution.py:284
  14.4 12.9 %collective-permute-start.7 = (bf16[256,512]{1,0:T(8,128)(2,1)S(1)}, bf16[256,512]{1,0:T(8,128)(2,1)S(1)}, u32[]{:S(2)}, u32[]{:S(2)}) collective-permute-start(bf16[256,512]{1,0:T(8,128)(2,1)S(1)} %slice_bitcast_fusion.refs_0_), channel_id=1, source_target_pairs={{0,4},{1,5},{4,8},{5,9},{8,12},{9,13},{12,14},{13,15},{14,10},{15,... | collective-permute-start | bytes 786440 | tf_op jit(solution)/shard_map/ppermute | solution.py:283
  15.9 11.4 %collective-permute-start.6 = (bf16[256,512]{1,0:T(8,128)(2,1)S(1)}, bf16[256,512]{1,0:T(8,128)(2,1)S(1)}, u32[]{:S(2)}, u32[]{:S(2)}) collective-permute-start(bf16[256,512]{1,0:T(8,128)(2,1)S(1)} %slice_bitcast_fusion.refs_0_), channel_id=1, source_target_pairs={{0,1},{1,0},{2,3},{3,2},{4,5},{5,4},{6,7},{7,6},{8,9},{9,8},{10,11... | collective-permute-start | bytes 786440 | tf_op jit(solution)/shard_map/ppermute | solution.py:43
  15.9 11.3 %collective-permute-start.3 = (bf16[4,2,14336]{2,1,0:T(2,128)(2,1)S(1)}, bf16[4,2,14336]{2,1,0:T(2,128)(2,1)}, u32[]{:S(2)}, u32[]{:S(2)}) collective-permute-start(bf16[4,2,14336]{2,1,0:T(2,128)(2,1)S(1)} %get-tuple-element.59), channel_id=1, source_target_pairs={{0,2},{1,3},{2,0},{3,1},{4,6},{5,7},{6,4},{7,5},{8,10},{9,11},{10,... | collective-permute-start | bytes 688136 | tf_op jit(solution)/shard_map/ppermute | solution.py:307
  29.0 9.6 %collective-permute-start.9 = (bf16[16,14336]{1,0:T(8,128)(2,1)S(1)}, bf16[16,14336]{1,0:T(8,128)(2,1)S(1)}, u32[]{:S(2)}, u32[]{:S(2)}) collective-permute-start(bf16[16,14336]{1,0:T(8,128)(2,1)S(1)} %reshape.7.near_ref), channel_id=1, source_target_pairs={{0,1},{1,0},{2,3},{3,2},{4,5},{5,4},{6,7},{7,6},{8,9},{9,8},{10,11... | collective-permute-start | bytes 1376264 | tf_op jit(solution)/shard_map/ppermute | solution.py:43
  29.5 8.3 %collective-permute-start.10 = (bf16[256,512]{1,0:T(8,128)(2,1)S(1)}, bf16[256,512]{1,0:T(8,128)(2,1)S(1)}, u32[]{:S(2)}, u32[]{:S(2)}) collective-permute-start(bf16[256,512]{1,0:T(8,128)(2,1)S(1)} %collective-permute-done.7.refs_2_), channel_id=1, source_target_pairs={{0,4},{1,5},{4,8},{5,9},{8,12},{9,13},{12,14},{13,15},{14,10},{15,... | collective-permute-start | bytes 786440 | tf_op jit(solution)/shard_map/ppermute | solution.py:283
  29.5 8.3 %collective-permute-start.13 = (bf16[256,512]{1,0:T(8,128)(2,1)S(1)}, bf16[256,512]{1,0:T(8,128)(2,1)S(1)}, u32[]{:S(2)}, u32[]{:S(2)}) collective-permute-start(bf16[256,512]{1,0:T(8,128)(2,1)S(1)} %collective-permute-done.8.refs_4_), channel_id=1, source_target_pairs={{0,1},{1,0},{2,3},{3,2},{4,5},{5,4},{6,7},{7,6},{8,9},{9,8},{10,11... | collective-permute-start | bytes 786440 | tf_op jit(solution)/shard_map/ppermute | solution.py:43
  29.6 9.0 %collective-permute-start.11 = (bf16[256,512]{1,0:T(8,128)(2,1)S(1)}, bf16[256,512]{1,0:T(8,128)(2,1)}, u32[]{:S(2)}, u32[]{:S(2)}) collective-permute-start(bf16[256,512]{1,0:T(8,128)(2,1)S(1)} %collective-permute-done.8.refs_4_), channel_id=1, source_target_pairs={{0,2},{1,3},{4,0},{5,1},{8,4},{9,5},{12,8},{13,9},{14,12},{15,13},... | collective-permute-start | bytes 786440 | tf_op jit(solution)/shard_map/ppermute | solution.py:284
  38.6 17.4 %collective-permute-start.16 = (bf16[256,512]{1,0:T(8,128)(2,1)S(1)}, bf16[256,512]{1,0:T(8,128)(2,1)}, u32[]{:S(2)}, u32[]{:S(2)}) collective-permute-start(bf16[256,512]{1,0:T(8,128)(2,1)S(1)} %collective-permute-done.10.refs_6_), channel_id=1, source_target_pairs={{0,1},{1,0},{2,3},{3,2},{4,5},{5,4},{6,7},{7,6},{8,9},{9,8},{10,11... | collective-permute-start | bytes 786440 | tf_op jit(solution)/shard_map/ppermute | solution.py:43
  38.6 17.4 %collective-permute-start.14 = (bf16[256,512]{1,0:T(8,128)(2,1)S(1)}, bf16[256,512]{1,0:T(8,128)(2,1)S(1)}, u32[]{:S(2)}, u32[]{:S(2)}) collective-permute-start(bf16[256,512]{1,0:T(8,128)(2,1)S(1)} %collective-permute-done.10.refs_6_), channel_id=1, source_target_pairs={{0,4},{1,5},{4,8},{5,9},{8,12},{9,13},{12,14},{13,15},{14,10},{15,... | collective-permute-start | bytes 786440 | tf_op jit(solution)/shard_map/ppermute | solution.py:283
  40.1 15.9 %collective-permute-start.17 = (bf16[256,512]{1,0:T(8,128)(2,1)}, bf16[256,512]{1,0:T(8,128)(2,1)}, u32[]{:S(2)}, u32[]{:S(2)}) collective-permute-start(bf16[256,512]{1,0:T(8,128)(2,1)} %collective-permute-done.11.refs_8_), channel_id=1, source_target_pairs={{0,1},{1,0},{2,3},{3,2},{4,5},{5,4},{6,7},{7,6},{8,9},{9,8},{10,11... | collective-permute-start | bytes 786440 | tf_op jit(solution)/shard_map/ppermute | solution.py:43
  40.3 15.7 %collective-permute-start.15 = (bf16[256,512]{1,0:T(8,128)(2,1)}, bf16[256,512]{1,0:T(8,128)(2,1)S(1)}, u32[]{:S(2)}, u32[]{:S(2)}) collective-permute-start(bf16[256,512]{1,0:T(8,128)(2,1)} %collective-permute-done.11.refs_8_), channel_id=1, source_target_pairs={{0,2},{1,3},{4,0},{5,1},{8,4},{9,5},{12,8},{13,9},{14,12},{15,13},... | collective-permute-start | bytes 786440 | tf_op jit(solution)/shard_map/ppermute | solution.py:284
  40.9 15.0 %all-to-all-start = ((bf16[8,32,256]{2,1,0:T(8,128)(2,1)}), bf16[8,32,256]{2,1,0:T(8,128)(2,1)S(1)}, u32[]{:S(2)}, u32[]{:S(2)}) async-start(bf16[8,32,256]{2,1,0:T(8,128)(2,1)} %rotate_in.1), calls=%async_computation | async-start | bytes 262144 | tf_op jit(solution)/shard_map/all_to_all | solution.py:48
  56.0 9.1 %collective-permute-start.21 = (bf16[256,512]{1,0:T(8,128)(2,1)S(1)}, bf16[256,512]{1,0:T(8,128)(2,1)S(1)}, u32[]{:S(2)}, u32[]{:S(2)}) collective-permute-start(bf16[256,512]{1,0:T(8,128)(2,1)S(1)} %collective-permute-done.14.refs_10_), channel_id=1, source_target_pairs={{0,1},{1,0},{2,3},{3,2},{4,5},{5,4},{6,7},{7,6},{8,9},{9,8},{10,11... | collective-permute-start | bytes 786440 | tf_op jit(solution)/shard_map/ppermute | solution.py:43
  56.1 9.0 %collective-permute-start.22 = (bf16[256,512]{1,0:T(8,128)(2,1)S(1)}, bf16[256,512]{1,0:T(8,128)(2,1)S(1)}, u32[]{:S(2)}, u32[]{:S(2)}) collective-permute-start(bf16[256,512]{1,0:T(8,128)(2,1)S(1)} %collective-permute-done.15.refs_12_), channel_id=1, source_target_pairs={{0,1},{1,0},{2,3},{3,2},{4,5},{5,4},{6,7},{7,6},{8,9},{9,8},{10,11... | collective-permute-start | bytes 786440 | tf_op jit(solution)/shard_map/ppermute | solution.py:43
  56.7 8.4 %collective-permute-start.20 = (bf16[128,512]{1,0:T(8,128)(2,1)S(1)}, bf16[128,512]{1,0:T(8,128)(2,1)S(1)}, u32[]{:S(2)}, u32[]{:S(2)}) collective-permute-start(bf16[128,512]{1,0:T(8,128)(2,1)S(1)} %slice.11), channel_id=1, source_target_pairs={{0,2},{1,3},{4,0},{5,1},{8,4},{9,5},{12,8},{13,9},{14,12},{15,13},... | collective-permute-start | bytes 393224 | tf_op jit(solution)/shard_map/ppermute | solution.py:284
  58.8 6.3 %collective-permute-start.19 = (bf16[128,512]{1,0:T(8,128)(2,1)S(1)}, bf16[128,512]{1,0:T(8,128)(2,1)S(1)}, u32[]{:S(2)}, u32[]{:S(2)}) collective-permute-start(bf16[128,512]{1,0:T(8,128)(2,1)S(1)} %slice.10), channel_id=1, source_target_pairs={{0,4},{1,5},{4,8},{5,9},{8,12},{9,13},{12,14},{13,15},{14,10},{15,... | collective-permute-start | bytes 393224 | tf_op jit(solution)/shard_map/ppermute | solution.py:283
  73.6 9.2 %collective-permute-start.26 = (bf16[48,512]{1,0:T(8,128)(2,1)S(1)}, bf16[48,512]{1,0:T(8,128)(2,1)S(1)}, u32[]{:S(2)}, u32[]{:S(2)}) collective-permute-start(bf16[48,512]{1,0:T(8,128)(2,1)S(1)} %get-tuple-element.94), channel_id=1, source_target_pairs={{0,12},{1,13},{2,14},{3,15},{4,8},{5,9},{6,10},{7,11},{8,4},{9,5},... | collective-permute-start | bytes 147464 | tf_op jit(solution)/shard_map/ppermute | solution.py:457
  77.5 7.3 %collective-permute-start.27 = (bf16[48,512]{1,0:T(8,128)(2,1)S(1)}, bf16[48,512]{1,0:T(8,128)(2,1)S(1)}, u32[]{:S(2)}, u32[]{:S(2)}) collective-permute-start(bf16[48,512]{1,0:T(8,128)(2,1)S(1)} %get-tuple-element.95), channel_id=1, source_target_pairs={{0,14},{1,15},{2,12},{3,13},{4,10},{5,11},{6,8},{7,9},{8,6},{9,7},... | collective-permute-start | bytes 147464 | tf_op jit(solution)/shard_map/ppermute | solution.py:457
  78.9 7.4 %collective-permute-start.28 = (bf16[48,512]{1,0:T(8,128)(2,1)S(1)}, bf16[48,512]{1,0:T(8,128)(2,1)S(1)}, u32[]{:S(2)}, u32[]{:S(2)}) collective-permute-start(bf16[48,512]{1,0:T(8,128)(2,1)S(1)} %get-tuple-element.96), channel_id=1, source_target_pairs={{0,8},{1,9},{2,10},{3,11},{4,12},{5,13},{6,14},{7,15},{8,0},{9,1},... | collective-permute-start | bytes 147464 | tf_op jit(solution)/shard_map/ppermute | solution.py:457
  79.5 7.5 %collective-permute-start.29 = (bf16[48,512]{1,0:T(8,128)(2,1)S(1)}, bf16[48,512]{1,0:T(8,128)(2,1)S(1)}, u32[]{:S(2)}, u32[]{:S(2)}) collective-permute-start(bf16[48,512]{1,0:T(8,128)(2,1)S(1)} %get-tuple-element.97), channel_id=1, source_target_pairs={{0,10},{1,11},{2,8},{3,9},{4,14},{5,15},{6,12},{7,13},{8,2},{9,3},... | collective-permute-start | bytes 147464 | tf_op jit(solution)/shard_map/ppermute | solution.py:457
  (16 other events, 88.7 us)

commit v10 on v9

v10 whole, which is shorter than its diff:
```python
import functools

import jax
import jax.numpy as jnp
from jax import lax
from jax.experimental import pallas as pl
from jax.experimental.pallas import tpu as pltpu
from jax.sharding import PartitionSpec as P

WR = 768
WC = 512
LANES = 128
MIB = 1 << 20


def xor_pairs(n, key):
    return [(b, b ^ key) for b in range(n)]


def swap(x, n):
    return lax.ppermute(x, "blk", xor_pairs(n, 1))


def exchange(x, n, stride):
    groups = [list(range(first, n, stride)) for first in range(stride)]
    return lax.all_to_all(x, "blk", 0, 0, axis_index_groups=groups, tiled=True)


def bits_of(size):
    return size.bit_length() - 1


def held_tokens(me, tokens, tok_rows):
    row = lax.broadcasted_iota(jnp.int32, (tokens, tokens), 1)
    pairs = tokens // tok_rows // 4
    place = row >> bits_of(tok_rows)
    chip = 2 * (place & (pairs - 1)) + ((place >> bits_of(pairs)) & 1)
    other = row >> bits_of(tokens // 2)
    device = me ^ (2 * chip + other)
    return (device << bits_of(tok_rows)) + (row & (tok_rows - 1))


def reorder(wanted, held, rotated):
    order = jnp.where(wanted == held, 1.0, 0.0).astype(jnp.bfloat16)
    return jnp.dot(order, rotated.astype(jnp.bfloat16), preferred_element_type=jnp.float32)


def part_kernel(*refs):
    grads_ref, acts_ref = refs[-2:]
    first = grads_ref.shape[2]
    for at, ref in enumerate(refs[:-2]):
        grads_ref[at] = ref[0, :, :first]
        acts_ref[at] = ref[0, :, first:]


def rotate_in_kernel(tok_rows, near_ref, far_ref, basis_ref, out_ref):
    tokens = out_ref.shape[1]
    acts = jnp.concatenate([near_ref[...], far_ref[...]], axis=0)
    rotated = jnp.dot(acts, basis_ref[...], preferred_element_type=jnp.float32)
    wanted = lax.broadcasted_iota(jnp.int32, (tokens, tokens), 0)
    held = held_tokens(lax.axis_index("blk"), tokens, tok_rows)
    ordered = reorder(wanted, held, rotated).astype(jnp.bfloat16)
    for copy in range(out_ref.shape[0]):
        out_ref[copy] = ordered


def rotate_out_kernel(
    tok_rows, near_ref, far_ref, basis_ref, map_ref, out_ref, basis, total, stored_map, sem
):
    steps, depth = basis.shape[:2]
    tokens = total.shape[0]

    def copy_of(step):
        rows = pl.ds(pl.multiple_of(step * depth, depth), depth)
        return pltpu.make_async_copy(basis_ref.at[rows], basis.at[step], sem.at[step])

    @pl.loop(0, steps)
    def _(step):
        copy_of(step).start()

    map_copy = pltpu.make_async_copy(map_ref, stored_map, sem.at[steps])
    map_copy.start()
    total[...] = jnp.zeros_like(total)

    @pl.loop(0, steps)
    def _(step):
        columns = pl.ds(pl.multiple_of(step * depth, depth), depth)
        grads = jnp.concatenate([near_ref[:, columns], far_ref[:, columns]], axis=0)
        copy_of(step).wait()
        total[...] += jnp.dot(grads, basis[step], preferred_element_type=jnp.float32)

    map_copy.wait()
    row = lax.broadcasted_iota(jnp.int32, (tokens, tokens), 0)
    block = row >> bits_of(tok_rows)
    wanted = jnp.zeros_like(row)
    for stored in range(tokens // tok_rows):
        wanted = jnp.where(block == stored, stored_map[stored] * tok_rows, wanted)
    wanted += row & (tok_rows - 1)
    held = held_tokens(lax.axis_index("blk"), tokens, tok_rows)
    out_ref[...] = reorder(wanted, held, total[...]).T.astype(jnp.bfloat16)


def scale_kernel(
    groups, aligned_ref, near_ref, far_ref, tiles_ref, eigen_ref, out_ref, damped, tiles, sem
):
    blocks, depth = damped.shape[:2]
    chips, _, width = near_ref.shape
    share = width // groups

    def copy_of(block):
        rows = pl.ds(pl.multiple_of(block * depth, depth), depth)
        return pltpu.make_async_copy(eigen_ref.at[rows], damped.at[block], sem.at[block])

    tiles_copy = pltpu.make_async_copy(tiles_ref, tiles, sem.at[blocks])
    tiles_copy.start()

    @pl.loop(0, blocks)
    def _(block):
        copy_of(block).start()

    tiles_copy.wait()
    odd = lax.rem(lax.axis_index("blk"), 2) == 1

    @pl.loop(0, blocks)
    def _(block):
        rows = pl.ds(pl.multiple_of(block * depth, depth), depth)
        aligned = aligned_ref[rows, :]
        copy_of(block).wait()
        for source in range(2 * chips):
            mine = odd if source % 2 else jnp.logical_not(odd)
            rotated = jnp.where(mine, near_ref[source // 2], far_ref[source // 2])
            grad = jnp.dot(aligned, rotated, preferred_element_type=jnp.float32)
            for first in range(0, width, LANES):
                tile = tiles[(source * width + first) // LANES]
                lanes = pl.ds(pl.multiple_of(tile * LANES, LANES), LANES)
                eigen = damped[block, :, lanes]
                inverse = pl.reciprocal(eigen, approx=True)
                inverse = inverse * (2.0 - eigen * inverse)
                scaled = grad[:, first : first + LANES] * inverse
                place = (first // share * 2 * chips + source) * share + first % share
                out_ref[rows, place : place + LANES] = scaled.astype(jnp.bfloat16)


def window_kernel(scale, basis_out_ref, scaled_ref, basis_ref, *refs):
    send_ref, keep_ref, basis, window, projected, result, sem = refs
    chips, rows, _ = keep_ref.shape
    parts, deep = basis.shape[:2]
    window_copy = pltpu.make_async_copy(
        basis_out_ref.at[pl.ds(0, window.shape[0])], window, sem.at[parts]
    )
    copies = [
        pltpu.make_async_copy(basis_ref.at[pl.ds(part * deep, deep)], basis.at[part], sem.at[part])
        for part in range(parts)
    ]
    for copy in copies:
        copy.start()
    window_copy.start()
    half = projected.shape[0] // 2
    for part in range(parts):
        copies[part].wait()
        columns = slice(part * deep, (part + 1) * deep)

        @pl.loop(0, 2)
        def _(at):
            block = pl.ds(pl.multiple_of(at * half, half), half)
            total = jnp.dot(
                scaled_ref[block, columns], basis[part], preferred_element_type=jnp.float32
            )
            projected[block, :] = total if part == 0 else projected[block, :] + total

    window_copy.wait()
    result[...] = scale * jnp.dot(
        window[...], projected[...].astype(jnp.bfloat16), preferred_element_type=jnp.float32
    )
    core = lax.rem(lax.axis_index("blk"), 2)
    for k in range(chips):
        mine = pl.ds(pl.multiple_of((2 * k + core) * rows, rows), rows)
        keep_ref[k] = result[mine, :]
        other = pl.ds(pl.multiple_of((2 * k + 1 - core) * rows, rows), rows)
        send_ref[k] = result[other, :].astype(jnp.bfloat16)


def add_core_kernel(keys, keep_ref, got_ref, own_ref, *send_refs):
    chip = lax.axis_index("blk") // 2
    for key, ref in zip((0, *keys), (own_ref, *send_refs)):
        at = chip ^ key
        ref[...] = (keep_ref[at] + got_ref[at].astype(jnp.float32)).astype(ref.dtype)


def add_chips_kernel(own_ref, *refs):
    total = own_ref[...]
    for ref in refs[:-1]:
        total += ref[...].astype(jnp.float32)
    refs[-1][...] = total


VMEM = pl.BlockSpec(memory_space=pltpu.VMEM)
SMEM = pl.BlockSpec(memory_space=pltpu.SMEM)
ANY = pl.BlockSpec(memory_space=pl.ANY)


def after(first, *others):
    return lax.optimization_barrier((first, *others))


def ring_body(n, grad_out, activations, basis_out, basis_in, eigenvalues, tile_order, block_map):
    tok_rows, full_out = grad_out.shape
    tile_width = basis_out.shape[1]
    full_in, in_width = basis_in.shape
    tokens = n * tok_rows
    chips = n // 2
    groups = lax.axis_size("grp")

    share = in_width // groups
    own = lax.dynamic_slice(basis_in, (0, lax.axis_index("grp") * share), (WC, share)).T
    first_rows = lax.all_gather(own, ("grp", "blk"), axis=0, tiled=True)

    pairs = chips // 2
    both = jnp.concatenate([grad_out, activations], axis=1)[None]
    got = [lax.ppermute(both, "blk", xor_pairs(n, 4 * key)) for key in range(1, pairs)]
    grads, acts = pl.pallas_call(
        part_kernel,
        out_shape=(
            jax.ShapeDtypeStruct((pairs, tok_rows, full_out), jnp.bfloat16),
            jax.ShapeDtypeStruct((pairs, tok_rows, full_in), jnp.bfloat16),
        ),
        in_specs=[VMEM] * pairs,
        out_specs=(VMEM, VMEM),
        compiler_params=pltpu.CompilerParams(vmem_limit_bytes=8 * MIB),
        name="part",
    )(both, *got)
    acts_got = lax.ppermute(acts, "blk", xor_pairs(n, 2))
    grads_got = lax.ppermute(grads, "blk", xor_pairs(n, 2))

    acts = jnp.concatenate([acts, acts_got], axis=0).reshape(tokens // 2, full_in)
    rotated = pl.pallas_call(
        functools.partial(rotate_in_kernel, tok_rows),
        out_shape=jax.ShapeDtypeStruct((chips, tokens, in_width), jnp.bfloat16),
        in_specs=[VMEM, VMEM, VMEM],
        out_specs=VMEM,
        compiler_params=pltpu.CompilerParams(vmem_limit_bytes=8 * MIB),
        name="rotate_in",
    )(acts, swap(acts, n), basis_in)
    grads_got, rotated = after(grads_got, rotated)
    rotated = exchange(rotated, n, 2)
    grads = jnp.concatenate([grads, grads_got], axis=0).reshape(tokens // 2, full_out)
    grads_far = swap(grads, n)

    depth = 1024
    aligned = pl.pallas_call(
        functools.partial(rotate_out_kernel, tok_rows),
        out_shape=jax.ShapeDtypeStruct((tile_width, tokens), jnp.bfloat16),
        in_specs=[VMEM, VMEM, ANY, ANY],
        out_specs=VMEM,
        scratch_shapes=[
            pltpu.VMEM((full_out // depth, depth, tile_width), jnp.bfloat16),
            pltpu.VMEM((tokens, tile_width), jnp.float32),
            pltpu.SMEM(block_map.shape, jnp.int32),
            pltpu.SemaphoreType.DMA((full_out // depth + 1,)),
        ],
        compiler_params=pltpu.CompilerParams(vmem_limit_bytes=40 * MIB),
        cost_estimate=pl.CostEstimate(
            flops=2 * tokens * full_out * tile_width,
            bytes_accessed=2 * full_out * tile_width,
            transcendentals=0,
        ),
        name="rotate_out",
    )(grads, grads_far, basis_out, block_map)

    rotated_far = swap(rotated, n)
    blocks = 8
    scaled = pl.pallas_call(
        functools.partial(scale_kernel, groups),
        out_shape=jax.ShapeDtypeStruct((tile_width, full_in), jnp.bfloat16),
        in_specs=[VMEM, VMEM, VMEM, ANY, ANY],
        out_specs=VMEM,
        scratch_shapes=[
            pltpu.VMEM((blocks, tile_width // blocks, full_in), jnp.float32),
            pltpu.SMEM(tile_order.shape, jnp.int32),
            pltpu.SemaphoreType.DMA((blocks + 1,)),
        ],
        compiler_params=pltpu.CompilerParams(vmem_limit_bytes=40 * MIB),
        cost_estimate=pl.CostEstimate(
            flops=2 * tile_width * full_in * tokens,
            bytes_accessed=6 * tile_width * full_in,
            transcendentals=tile_width * full_in,
        ),
        name="scale",
    )(aligned, rotated, rotated_far, tile_order, eigenvalues)

    rows = WR // n
    parts = 4
    send, keep = pl.pallas_call(
        functools.partial(window_kernel, 1.0 / tokens),
        out_shape=(
            jax.ShapeDtypeStruct((chips, rows, WC), jnp.bfloat16),
            jax.ShapeDtypeStruct((chips, rows, WC), jnp.float32),
        ),
        in_specs=[ANY, VMEM, ANY],
        out_specs=(VMEM, VMEM),
        scratch_shapes=[
            pltpu.VMEM((parts, full_in // parts, WC), jnp.bfloat16),
            pltpu.VMEM((WR, tile_width), jnp.bfloat16),
            pltpu.VMEM((tile_width, WC), jnp.float32),
            pltpu.VMEM((WR, WC), jnp.float32),
            pltpu.SemaphoreType.DMA((parts + 1,)),
        ],
        compiler_params=pltpu.CompilerParams(vmem_limit_bytes=52 * MIB),
        cost_estimate=pl.CostEstimate(
            flops=2 * tile_width * full_in * WC + 2 * WR * tile_width * WC,
            bytes_accessed=2 * tile_width * full_in + 2 * WC * full_in,
            transcendentals=0,
        ),
        name="window",
    )(basis_out, scaled, first_rows)

    keys = sorted(range(1, chips), key=lambda key: -(key & -2))
    small = pltpu.CompilerParams(vmem_limit_bytes=8 * MIB)
    own, *sends = pl.pallas_call(
        functools.partial(add_core_kernel, keys),
        out_shape=[jax.ShapeDtypeStruct((rows, WC), jnp.float32)]
        + [jax.ShapeDtypeStruct((rows, WC), jnp.bfloat16)] * len(keys),
        in_specs=[VMEM, VMEM],
        out_specs=[VMEM] * chips,
        compiler_params=small,
        name="add_core",
    )(keep, swap(send, n))
    arrived = [lax.ppermute(x, "blk", xor_pairs(n, 2 * key)) for key, x in zip(keys, sends)]
    return pl.pallas_call(
        add_chips_kernel,
        out_shape=jax.ShapeDtypeStruct((rows, WC), jnp.float32),
        in_specs=[VMEM] * chips,
        out_specs=VMEM,
        compiler_params=small,
        name="add_chips",
    )(own, *arrived)


def gather_body(grad_out, activations, basis_out, basis_in, eigenvalues, tile_order, block_map):
    n_blocks = lax.axis_size("blk")
    tile_width = basis_out.shape[1]
    tok_rows = grad_out.shape[0]
    full_in = eigenvalues.shape[1]
    tokens = n_blocks * tok_rows
    dot = functools.partial(jnp.dot, preferred_element_type=jnp.float32)
    in_rows = lax.all_gather(basis_in[:WC], "blk", axis=1, tiled=True)
    acts = lax.all_gather(activations, "blk", axis=0, tiled=True)
    in_tile = dot(acts, basis_in).astype(jnp.bfloat16)
    rotated_in = lax.all_gather(in_tile, "blk", axis=1, tiled=True)
    grads = lax.all_gather(grad_out, "blk", axis=0, tiled=True)
    rotated_out = dot(grads, basis_out).astype(jnp.bfloat16)
    aligned = jnp.take(
        rotated_out.reshape(n_blocks, tok_rows, tile_width), block_map, axis=0
    ).reshape(tokens, tile_width)
    grad_tile = dot(aligned.T, rotated_in) / tokens
    damped = jnp.take(
        eigenvalues.reshape(tile_width, full_in // LANES, LANES), tile_order, axis=1
    ).reshape(tile_width, full_in)
    scaled = (grad_tile / damped).astype(jnp.bfloat16)
    projected = dot(scaled, in_rows.T).astype(jnp.bfloat16)
    return lax.psum_scatter(
        dot(basis_out[:WR], projected), "blk", scatter_dimension=0, tiled=True
    )


def solution(mesh):
    n = mesh.shape["blk"]

    def body(*args):
        wide = args[3].shape[1] % LANES == 0 and args[2].shape[1] % LANES == 0
        doubles = n & (n - 1) == 0 and args[0].shape[0] & (args[0].shape[0] - 1) == 0
        if wide and doubles and WR % (16 * n) == 0:
            return ring_body(n, *args)
        return gather_body(*args)

    placed = (
        P(("grp", "blk"), None),
        P(("grp", "blk"), None),
        P(None, "blk"),
        P(None, "blk"),
        P("blk", None),
        P(),
        P(),
    )
    return jax.shard_map(
        body, mesh=mesh, in_specs=placed, out_specs=P(("grp", "blk"), None), check_vma=False
    )
```

time: 90 us -> 110 us (1.22)
  starting transfers between devices: 35.5 us -> 19.5 us
  between operations: 0.27 us -> 13.5 us
  blocking collectives: 0 us -> 12.9 us
  waiting for transfers between devices: 14.9 us -> 27.3 us
  local copies, waits for them, and re-layouts: 10.8 us -> 7.07 us
  Pallas kernels: 24.8 us -> 28.2 us
  other arithmetic: 3.27 us -> 1.68 us
    all_to_all x0 -> x1, blocking collectives: none -> 12.9 us  [exchange(): return lax.all_to_all(x, 'blk', 0, 0, axis_index_groups=groups, tiled=True)]
    all_gather x0 -> x1, waiting for transfers between devices: none -> 11 us  [ring_body(): first_rows = lax.all_gather(own, ('grp', 'blk'), axis=0, tiled=True)]
    pallas_call x1, Pallas kernels: 1.63 us -> 10.7 us  [ring_body(): pl.pallas_call(functools.partial(window_kernel, 1.0 / tokens), out_shape=...]
    ppermute x8 -> x0, starting transfers between devices: 8.2 us -> none  [the longest x4 5.09 us: ring_body(): to_left = lambda x: lax.ppermute(x, 'blk', shift_pairs(n, -1))]
    pallas_call x3 -> x1, Pallas kernels: 13.8 us -> 6.85 us  [ring_body(): pl.pallas_call(functools.partial(scale_kernel, groups), out_shape=jax.Sha...]
    ppermute x8 -> x0, waiting for transfers between devices: 6.27 us -> none  [the longest x4 6.26 us: ring_body(): to_right = lambda x: lax.ppermute(x, 'blk', shift_pairs(n, 1))]
    all_to_all x1 -> x0, starting transfers between devices: 4.85 us -> none  [exchange(): return lax.all_to_all(x, 'blk', 0, 0, axis_index_groups=groups, tiled=True)]
    unnamed x13 -> x9, local copies, waits for them, and re-layouts: 9.63 us -> 5.93 us
  transfers between devices with their start and end apart: 34 -> 17, of which waited for: 9 -> 10; matrix products, arithmetic and copies ran while one was open for 5% -> 2% of each run, Pallas kernels for 25% -> 15%
where the time goes in v10:
time: 110 us
  Pallas kernels  28.2 us (26%)
  waiting for transfers between devices  27.3 us (25%)
  starting transfers between devices  19.5 us (18%)
  between operations  13.5 us (12%)
  blocking collectives  12.9 us (12%)
  local copies, waits for them, and re-layouts  7.07 us (6%)
  other arithmetic  1.68 us (2%)
    all_to_all x1, blocking collectives, exchange(): return lax.all_to_all(x, 'blk', 0, 0, axis_index_groups=groups, tiled=True)  12.9 us
    ppermute x7, starting transfers between devices, ring_body(): lax.ppermute(x, 'blk', xor_pairs(n, 2 * key))  11.2 us
    all_gather x1, waiting for transfers between devices, ring_body(): first_rows = lax.all_gather(own, ('grp', 'blk'), axis=0, tiled=True)  11 us
    pallas_call x1, Pallas kernels, ring_body(): pl.pallas_call(functools.partial(window_kernel, 1.0 / tokens), out_shape=...  10.7 us
    pallas_call x1, Pallas kernels, ring_body(): pl.pallas_call(functools.partial(rotate_out_kernel, tok_rows), out_shape=...  9.23 us
    pallas_call x1, Pallas kernels, ring_body(): pl.pallas_call(functools.partial(scale_kernel, groups), out_shape=jax.Sha...  6.85 us
    unnamed x9, local copies, waits for them, and re-layouts  5.93 us
    ppermute x3, starting transfers between devices, ring_body(): lax.ppermute(both, 'blk', xor_pairs(n, 4 * key))  5.76 us
  transfers between devices with their start and end apart: 17, of which 10 were waited for; matrix products, arithmetic and copies ran while one was open for 2% of the time, Pallas kernels for 15%

profile of v10, /device:TPU:0, one launch (start us, length us, event | category | flops | bytes accessed | tf_op | source)
XLA Modules:
  0.0 110.1 jit_solution(3067293324160649474)
XLA Ops:
  6.5 0.9 constant_dynamic-slice_fusion
  7.5 0.8 copy.9
  8.2 0.9 maximum_bitcast_fusion.refs_0_
  9.1 5.1 %collective-permute-start.2 = (bf16[1,2,18432]{2,1,0:T(2,128)(2,1)S(1)}, bf16[1,2,18432]{2,1,0:T(2,128)(2,1)S(1)}, u32[]{:S(2)}, u32[]{:S(2)}) collective-permute-start(bf16[1,2,18432]{2,1,0:T(2,128)(2,1)S(1)} %maximum_bitcast_fusion.refs_0_), channel_id=1, source_target_pairs={{0,12},{1,13},{2,14},{3,15},{4,8},{5,9},{6,10},{7,11},{8,4},{9,5},... | collective-permute-start | bytes 221192 | tf_op jit(solution)/shard_map/ppermute | solution.py:220
  14.9 2.1 %collective-permute-done.2.refs_3_ = bf16[1,2,18432]{2,1,0:T(2,128)(2,1)S(1)} collective-permute-done((bf16[1,2,18432]{2,1,0:T(2,128)(2,1)S(1)}, bf16[1,2,18432]{2,1,0:T(2,128)(2,1)S(1)}, u32[]{:S(2)}, u32[]{:S(2)}) %collective-permute-start.2) | collective-permute-done | bytes 73760 | tf_op jit(solution)/shard_map/ppermute | solution.py:220
  17.0 3.5 %collective-permute-done.1.refs_2_ = bf16[1,2,18432]{2,1,0:T(2,128)(2,1)S(1)} collective-permute-done((bf16[1,2,18432]{2,1,0:T(2,128)(2,1)S(1)}, bf16[1,2,18432]{2,1,0:T(2,128)(2,1)S(1)}, u32[]{:S(2)}, u32[]{:S(2)}) %collective-permute-start.1) | collective-permute-done | bytes 73760 | tf_op jit(solution)/shard_map/ppermute | solution.py:220
  20.5 1.6 %collective-permute-start.4 = (bf16[4,2,4096]{2,1,0:T(2,128)(2,1)S(1)}, bf16[4,2,4096]{2,1,0:T(2,128)(2,1)S(1)}, u32[]{:S(2)}, u32[]{:S(2)}) collective-permute-start(bf16[4,2,4096]{2,1,0:T(2,128)(2,1)S(1)} %get-tuple-element.20), channel_id=1, source_target_pairs={{0,2},{1,3},{2,0},{3,1},{4,6},{5,7},{6,4},{7,5},{8,10},{9,11},{10,... | collective-permute-start | bytes 196616 | tf_op jit(solution)/shard_map/ppermute | solution.py:232
  22.6 3.9 %collective-permute-done.4 = bf16[4,2,4096]{2,1,0:T(2,128)(2,1)S(1)} collective-permute-done((bf16[4,2,4096]{2,1,0:T(2,128)(2,1)S(1)}, bf16[4,2,4096]{2,1,0:T(2,128)(2,1)S(1)}, u32[]{:S(2)}, u32[]{:S(2)}) %collective-permute-start.4) | collective-permute-done | bytes 65568 | tf_op jit(solution)/shard_map/ppermute | solution.py:232
  26.8 1.3 %collective-permute-done.5.far_ref = bf16[16,4096]{1,0:T(8,128)(2,1)S(1)} collective-permute-done((bf16[16,4096]{1,0:T(8,128)(2,1)S(1)}, bf16[16,4096]{1,0:T(8,128)(2,1)S(1)}, u32[]{:S(2)}, u32[]{:S(2)}) %collective-permute-start.5) | collective-permute-done | bytes 131104 | tf_op jit(solution)/shard_map/ppermute | solution.py:21
  28.1 1.6 %copy-done.1 = bf16[4096,256]{1,0:T(8,128)(2,1)S(1)} copy-done((bf16[4096,256]{1,0:T(8,128)(2,1)S(1)}, bf16[4096,256]{1,0:T(8,128)(2,1)}, u32[]{:S(2)}) %copy-start.1) | copy-done | bytes 2097176
  31.5 12.9 %all_to_all.5.near_ref = bf16[8,32,256]{2,1,0:T(8,128)(2,1)S(1)} all-to-all(bf16[8,32,256]{2,1,0:T(8,128)(2,1)S(1)} %rotate_in.1), channel_id=1, replica_groups={{0,2,4,6,8,10,12,14},{1,3,5,7,9,11,13,15},{16,18,20,22,24,26,28,30},{17..., dimensions={0} | all-to-all | bytes 262144 | tf_op jit(solution)/shard_map/all_to_all | solution.py:26
  45.0 9.2 %rotate_out.1.aligned_ref = bf16[896,32]{1,0:T(8,128)(2,1)S(1)} custom-call(bf16[16,14336]{1,0:T(8,128)(2,1)S(1)} %reshape.7.near_ref, bf16[16,14336]{1,0:T(8,128)(2,1)S(1)} %collective-permute-done.6.far_ref, bf16[14336,896]{1,0:T(8,128)(2,1)} %basis_out_ref.1, s32[16]{0:T(128)S(1)} %copy-done.3), custom_call_target="tpu_custom_call" | custom-call | flops 822083584 | bytes 25690112 | tf_op jit(solution)/shard_map/rotate_out/pallas_call | solution.py:250
  54.3 6.9 %scale.1.scaled_ref = bf16[896,4096]{1,0:T(8,128)(2,1)S(1)} custom-call(bf16[896,32]{1,0:T(8,128)(2,1)S(1)} %rotate_out.1.aligned_ref, bf16[8,32,256]{2,1,0:T(8,128)(2,1)S(1)} %all_to_all.5.near_ref, bf16[8,32,256]{2,1,0:T(8,128)(2,1)S(1)} %collective-permute-done.7.far_ref, s32[32]{0:T(128)S(1)} %copy-done.2, f32[896,4096]{1,0:T(8,128)} %eigen_ref.1), custom_call_target="tpu_custom_call" | custom-call | flops 234881024 | bytes 22020096 | tf_op jit(solution)/shard_map/scale/pallas_call | solution.py:272
  61.1 2.9 %copy-done = bf16[896,4096]{1,0:T(8,128)(2,1)} copy-done((bf16[896,4096]{1,0:T(8,128)(2,1)}, bf16[896,4096]{1,0:T(8,128)(2,1)S(1)}, u32[]{:S(2)}) %copy-start) | copy-done | bytes 7340056
  64.1 11.0 %all-gather.2.cloned.1.call-done.basis_ref = bf16[4096,512]{1,0:T(8,128)(2,1)} async-done(((bf16[128,512]{1,0:T(8,128)(2,1)}), bf16[4096,512]{1,0:T(8,128)(2,1)}) %all-gather.2.cloned.1.call-update) | async-done | bytes 4194320 | tf_op jit(solution)/shard_map/all_gather | solution.py:216
  75.1 10.7 %window.1 = (bf16[8,48,512]{2,1,0:T(8,128)(2,1)S(1)}, f32[8,48,512]{2,1,0:T(8,128)S(1)}) custom-call(bf16[14336,896]{1,0:T(8,128)(2,1)} %basis_out_ref.1, bf16[896,4096]{1,0:T(8,128)(2,1)} %copy-done, bf16[4096,512]{1,0:T(8,128)(2,1)} %all-gather.2.cloned.1.call-done.basis_ref), custom_call_target="tpu_custom_call" | custom-call | flops 4462739456 | bytes 11534336 | tf_op jit(solution)/shard_map/window/pallas_call | solution.py:293
  86.1 1.5 %collective-permute-done.8.got_ref = bf16[8,48,512]{2,1,0:T(8,128)(2,1)S(1)} collective-permute-done((bf16[8,48,512]{2,1,0:T(8,128)(2,1)S(1)}, bf16[8,48,512]{2,1,0:T(8,128)(2,1)S(1)}, u32[]{:S(2)}, u32[]{:S(2)}) %collective-permute-start.8) | collective-permute-done | bytes 393248 | tf_op jit(solution)/shard_map/ppermute | solution.py:21
  87.7 2.0 %collective-permute-start.9 = (bf16[48,512]{1,0:T(8,128)(2,1)S(1)}, bf16[48,512]{1,0:T(8,128)(2,1)S(1)}, u32[]{:S(2)}, u32[]{:S(2)}) collective-permute-start(bf16[48,512]{1,0:T(8,128)(2,1)S(1)} %get-tuple-element.26), channel_id=1, source_target_pairs={{0,12},{1,13},{2,14},{3,15},{4,8},{5,9},{6,10},{7,11},{8,4},{9,5},... | collective-permute-start | bytes 147464 | tf_op jit(solution)/shard_map/ppermute | solution.py:328
  89.7 2.9 %collective-permute-start.10 = (bf16[48,512]{1,0:T(8,128)(2,1)S(1)}, bf16[48,512]{1,0:T(8,128)(2,1)S(1)}, u32[]{:S(2)}, u32[]{:S(2)}) collective-permute-start(bf16[48,512]{1,0:T(8,128)(2,1)S(1)} %get-tuple-element.27), channel_id=1, source_target_pairs={{0,14},{1,15},{2,12},{3,13},{4,10},{5,11},{6,8},{7,9},{8,6},{9,7},... | collective-permute-start | bytes 147464 | tf_op jit(solution)/shard_map/ppermute | solution.py:328
  92.6 2.8 %collective-permute-start.12 = (bf16[48,512]{1,0:T(8,128)(2,1)S(1)}, bf16[48,512]{1,0:T(8,128)(2,1)S(1)}, u32[]{:S(2)}, u32[]{:S(2)}) collective-permute-start(bf16[48,512]{1,0:T(8,128)(2,1)S(1)} %get-tuple-element.29), channel_id=1, source_target_pairs={{0,10},{1,11},{2,8},{3,9},{4,14},{5,15},{6,12},{7,13},{8,2},{9,3},... | collective-permute-start | bytes 147464 | tf_op jit(solution)/shard_map/ppermute | solution.py:328
  95.4 3.0 %collective-permute-start.14 = (bf16[48,512]{1,0:T(8,128)(2,1)S(1)}, bf16[48,512]{1,0:T(8,128)(2,1)S(1)}, u32[]{:S(2)}, u32[]{:S(2)}) collective-permute-start(bf16[48,512]{1,0:T(8,128)(2,1)S(1)} %get-tuple-element.31), channel_id=1, source_target_pairs={{0,6},{1,7},{2,4},{3,5},{4,2},{5,3},{6,0},{7,1},{8,14},{9,15},{10,... | collective-permute-start | bytes 147464 | tf_op jit(solution)/shard_map/ppermute | solution.py:328
  98.9 2.0 %collective-permute-done.12.refs_3_ = bf16[48,512]{1,0:T(8,128)(2,1)S(1)} collective-permute-done((bf16[48,512]{1,0:T(8,128)(2,1)S(1)}, bf16[48,512]{1,0:T(8,128)(2,1)S(1)}, u32[]{:S(2)}, u32[]{:S(2)}) %collective-permute-start.12) | collective-permute-done | bytes 49184 | tf_op jit(solution)/shard_map/ppermute | solution.py:328
  100.9 1.0 collective-permute-done.14.refs_5_
  102.5 0.7 add_chips.1
  (34 shorter events, 5.4 us)
Async XLA Ops:
  6.5 68.6 %all-gather.2.cloned.1.call-start = ((), (), s32[]{:S(2)}) async-start(), calls=%async_computation.1 | async-start | bytes 4325376 | tf_op jit(solution)/shard_map/all_gather | solution.py:216
  9.1 7.9 %collective-permute-start.2 = (bf16[1,2,18432]{2,1,0:T(2,128)(2,1)S(1)}, bf16[1,2,18432]{2,1,0:T(2,128)(2,1)S(1)}, u32[]{:S(2)}, u32[]{:S(2)}) collective-permute-start(bf16[1,2,18432]{2,1,0:T(2,128)(2,1)S(1)} %maximum_bitcast_fusion.refs_0_), channel_id=1, source_target_pairs={{0,12},{1,13},{2,14},{3,15},{4,8},{5,9},{6,10},{7,11},{8,4},{9,5},... | collective-permute-start | bytes 221192 | tf_op jit(solution)/shard_map/ppermute | solution.py:220
  14.3 6.2 %collective-permute-start.1 = (bf16[1,2,18432]{2,1,0:T(2,128)(2,1)S(1)}, bf16[1,2,18432]{2,1,0:T(2,128)(2,1)S(1)}, u32[]{:S(2)}, u32[]{:S(2)}) collective-permute-start(bf16[1,2,18432]{2,1,0:T(2,128)(2,1)S(1)} %maximum_bitcast_fusion.refs_0_), channel_id=1, source_target_pairs={{0,8},{1,9},{2,10},{3,11},{4,12},{5,13},{6,14},{7,15},{8,0},{9,1},... | collective-permute-start | bytes 221192 | tf_op jit(solution)/shard_map/ppermute | solution.py:220
  14.3 6.2 %collective-permute-start = (bf16[1,2,18432]{2,1,0:T(2,128)(2,1)S(1)}, bf16[1,2,18432]{2,1,0:T(2,128)(2,1)S(1)}, u32[]{:S(2)}, u32[]{:S(2)}) collective-permute-start(bf16[1,2,18432]{2,1,0:T(2,128)(2,1)S(1)} %maximum_bitcast_fusion.refs_0_), channel_id=1, source_target_pairs={{0,4},{1,5},{2,6},{3,7},{4,0},{5,1},{6,2},{7,3},{8,12},{9,13},{10,... | collective-permute-start | bytes 221192 | tf_op jit(solution)/shard_map/ppermute | solution.py:220
  20.5 6.0 %collective-permute-start.4 = (bf16[4,2,4096]{2,1,0:T(2,128)(2,1)S(1)}, bf16[4,2,4096]{2,1,0:T(2,128)(2,1)S(1)}, u32[]{:S(2)}, u32[]{:S(2)}) collective-permute-start(bf16[4,2,4096]{2,1,0:T(2,128)(2,1)S(1)} %get-tuple-element.20), channel_id=1, source_target_pairs={{0,2},{1,3},{2,0},{3,1},{4,6},{5,7},{6,4},{7,5},{8,10},{9,11},{10,... | collective-permute-start | bytes 196616 | tf_op jit(solution)/shard_map/ppermute | solution.py:232
  22.1 8.5 %collective-permute-start.3 = (bf16[4,2,14336]{2,1,0:T(2,128)(2,1)S(1)}, bf16[4,2,14336]{2,1,0:T(2,128)(2,1)S(1)}, u32[]{:S(2)}, u32[]{:S(2)}) collective-permute-start(bf16[4,2,14336]{2,1,0:T(2,128)(2,1)S(1)} %get-tuple-element.19), channel_id=1, source_target_pairs={{0,2},{1,3},{2,0},{3,1},{4,6},{5,7},{6,4},{7,5},{8,10},{9,11},{10,... | collective-permute-start | bytes 688136 | tf_op jit(solution)/shard_map/ppermute | solution.py:233
  26.7 1.4 %collective-permute-start.5 = (bf16[16,4096]{1,0:T(8,128)(2,1)S(1)}, bf16[16,4096]{1,0:T(8,128)(2,1)S(1)}, u32[]{:S(2)}, u32[]{:S(2)}) collective-permute-start(bf16[16,4096]{1,0:T(8,128)(2,1)S(1)} %reshape.6.near_ref), channel_id=1, source_target_pairs={{0,1},{1,0},{2,3},{3,2},{4,5},{5,4},{6,7},{7,6},{8,9},{9,8},{10,11... | collective-permute-start | bytes 393224 | tf_op jit(solution)/shard_map/ppermute | solution.py:21
  28.1 1.6 %copy-start.1 = (bf16[4096,256]{1,0:T(8,128)(2,1)S(1)}, bf16[4096,256]{1,0:T(8,128)(2,1)}, u32[]{:S(2)}) copy-start(bf16[4096,256]{1,0:T(8,128)(2,1)} %basis_ref.2) | copy-start | bytes 6291460
  31.4 12.9 %collective-permute-start.6 = (bf16[16,14336]{1,0:T(8,128)(2,1)S(1)}, bf16[16,14336]{1,0:T(8,128)(2,1)S(1)}, u32[]{:S(2)}, u32[]{:S(2)}) collective-permute-start(bf16[16,14336]{1,0:T(8,128)(2,1)S(1)} %reshape.7.near_ref), channel_id=1, source_target_pairs={{0,1},{1,0},{2,3},{3,2},{4,5},{5,4},{6,7},{7,6},{8,9},{9,8},{10,11... | collective-permute-start | bytes 1376264 | tf_op jit(solution)/shard_map/ppermute | solution.py:21
  44.3 9.9 %copy-start.2 = (s32[32]{0:T(128)S(1)}, s32[32]{0:T(128)}, u32[]{:S(2)}) copy-start(s32[32]{0:T(128)} %tiles_ref.1) | copy-start | bytes 388
  44.3 9.9 %collective-permute-start.7 = (bf16[8,32,256]{2,1,0:T(8,128)(2,1)S(1)}, bf16[8,32,256]{2,1,0:T(8,128)(2,1)S(1)}, u32[]{:S(2)}, u32[]{:S(2)}) collective-permute-start(bf16[8,32,256]{2,1,0:T(8,128)(2,1)S(1)} %all_to_all.5.near_ref), channel_id=1, source_target_pairs={{0,1},{1,0},{2,3},{3,2},{4,5},{5,4},{6,7},{7,6},{8,9},{9,8},{10,11... | collective-permute-start | bytes 393224 | tf_op jit(solution)/shard_map/ppermute | solution.py:21
  44.3 0.7 copy-start.3
  61.1 2.9 %copy-start = (bf16[896,4096]{1,0:T(8,128)(2,1)}, bf16[896,4096]{1,0:T(8,128)(2,1)S(1)}, u32[]{:S(2)}) copy-start(bf16[896,4096]{1,0:T(8,128)(2,1)S(1)} %scale.1.scaled_ref) | copy-start | bytes 22020100
  85.8 1.8 %collective-permute-start.8 = (bf16[8,48,512]{2,1,0:T(8,128)(2,1)S(1)}, bf16[8,48,512]{2,1,0:T(8,128)(2,1)S(1)}, u32[]{:S(2)}, u32[]{:S(2)}) collective-permute-start(bf16[8,48,512]{2,1,0:T(8,128)(2,1)S(1)} %get-tuple-element.24), channel_id=1, source_target_pairs={{0,1},{1,0},{2,3},{3,2},{4,5},{5,4},{6,7},{7,6},{8,9},{9,8},{10,11... | collective-permute-start | bytes 1179656 | tf_op jit(solution)/shard_map/ppermute | solution.py:21
  87.7 7.7 %collective-permute-start.9 = (bf16[48,512]{1,0:T(8,128)(2,1)S(1)}, bf16[48,512]{1,0:T(8,128)(2,1)S(1)}, u32[]{:S(2)}, u32[]{:S(2)}) collective-permute-start(bf16[48,512]{1,0:T(8,128)(2,1)S(1)} %get-tuple-element.26), channel_id=1, source_target_pairs={{0,12},{1,13},{2,14},{3,15},{4,8},{5,9},{6,10},{7,11},{8,4},{9,5},... | collective-permute-start | bytes 147464 | tf_op jit(solution)/shard_map/ppermute | solution.py:328
  89.7 8.7 %collective-permute-start.10 = (bf16[48,512]{1,0:T(8,128)(2,1)S(1)}, bf16[48,512]{1,0:T(8,128)(2,1)S(1)}, u32[]{:S(2)}, u32[]{:S(2)}) collective-permute-start(bf16[48,512]{1,0:T(8,128)(2,1)S(1)} %get-tuple-element.27), channel_id=1, source_target_pairs={{0,14},{1,15},{2,12},{3,13},{4,10},{5,11},{6,8},{7,9},{8,6},{9,7},... | collective-permute-start | bytes 147464 | tf_op jit(solution)/shard_map/ppermute | solution.py:328
  92.6 6.3 %collective-permute-start.11 = (bf16[48,512]{1,0:T(8,128)(2,1)S(1)}, bf16[48,512]{1,0:T(8,128)(2,1)S(1)}, u32[]{:S(2)}, u32[]{:S(2)}) collective-permute-start(bf16[48,512]{1,0:T(8,128)(2,1)S(1)} %get-tuple-element.28), channel_id=1, source_target_pairs={{0,8},{1,9},{2,10},{3,11},{4,12},{5,13},{6,14},{7,15},{8,0},{9,1},... | collective-permute-start | bytes 147464 | tf_op jit(solution)/shard_map/ppermute | solution.py:328
  92.6 8.3 %collective-permute-start.12 = (bf16[48,512]{1,0:T(8,128)(2,1)S(1)}, bf16[48,512]{1,0:T(8,128)(2,1)S(1)}, u32[]{:S(2)}, u32[]{:S(2)}) collective-permute-start(bf16[48,512]{1,0:T(8,128)(2,1)S(1)} %get-tuple-element.29), channel_id=1, source_target_pairs={{0,10},{1,11},{2,8},{3,9},{4,14},{5,15},{6,12},{7,13},{8,2},{9,3},... | collective-permute-start | bytes 147464 | tf_op jit(solution)/shard_map/ppermute | solution.py:328
  95.4 5.5 %collective-permute-start.13 = (bf16[48,512]{1,0:T(8,128)(2,1)S(1)}, bf16[48,512]{1,0:T(8,128)(2,1)S(1)}, u32[]{:S(2)}, u32[]{:S(2)}) collective-permute-start(bf16[48,512]{1,0:T(8,128)(2,1)S(1)} %get-tuple-element.30), channel_id=1, source_target_pairs={{0,4},{1,5},{2,6},{3,7},{4,0},{5,1},{6,2},{7,3},{8,12},{9,13},{10,... | collective-permute-start | bytes 147464 | tf_op jit(solution)/shard_map/ppermute | solution.py:328
  95.4 6.5 %collective-permute-start.14 = (bf16[48,512]{1,0:T(8,128)(2,1)S(1)}, bf16[48,512]{1,0:T(8,128)(2,1)S(1)}, u32[]{:S(2)}, u32[]{:S(2)}) collective-permute-start(bf16[48,512]{1,0:T(8,128)(2,1)S(1)} %get-tuple-element.31), channel_id=1, source_target_pairs={{0,6},{1,7},{2,4},{3,5},{4,2},{5,3},{6,0},{7,1},{8,14},{9,15},{10,... | collective-permute-start | bytes 147464 | tf_op jit(solution)/shard_map/ppermute | solution.py:328
  98.4 4.1 %collective-permute-start.15 = (bf16[48,512]{1,0:T(8,128)(2,1)S(1)}, bf16[48,512]{1,0:T(8,128)(2,1)S(1)}, u32[]{:S(2)}, u32[]{:S(2)}) collective-permute-start(bf16[48,512]{1,0:T(8,128)(2,1)S(1)} %get-tuple-element.32), channel_id=1, source_target_pairs={{0,2},{1,3},{2,0},{3,1},{4,6},{5,7},{6,4},{7,5},{8,10},{9,11},{10,... | collective-permute-start | bytes 147464 | tf_op jit(solution)/shard_map/ppermute | solution.py:328
Sparse Core Ops, SparseCore 0:
  10.2 64.8 all-gather.1

commit v11 on v9

--- a/solution.py
+++ b/solution.py
@@ -78,9 +78,7 @@
 def rotate_in_kernel(tok_rows, near_ref, far_ref, basis_ref, out_ref):
     tokens = out_ref.shape[1]
     acts = jnp.concatenate([near_ref[...], far_ref[...]], axis=0)
-    rotated = lax.dot_general(
-        acts, basis_ref[...], (((1,), (1,)), ((), ())), preferred_element_type=jnp.float32
-    )
+    rotated = jnp.dot(acts, basis_ref[...], preferred_element_type=jnp.float32)
     wanted = lax.broadcasted_iota(jnp.int32, (tokens, tokens), 0)
     held = held_tokens(lax.axis_index("blk"), tokens, tok_rows)
     ordered = reorder(wanted, held, rotated).astype(jnp.bfloat16)
@@ -88,25 +86,10 @@
         out_ref[copy] = ordered
 
 
-def hold_kernel(basis_ref, held_ref, sem):
-    steps, depth = held_ref.shape[:2]
-    copies = [
-        pltpu.make_async_copy(
-            basis_ref.at[pl.ds(step * depth, depth)], held_ref.at[step], sem.at[step]
-        )
-        for step in range(steps)
-    ]
-    for copy in copies:
-        copy.start()
-    for copy in copies:
-        copy.wait()
-
-
 def rotate_out_kernel(
     tok_rows,
     near_ref,
     far_ref,
-    held_ref,
     basis_ref,
     map_ref,
     out_ref,
@@ -116,11 +99,10 @@
     sem,
 ):
     steps, depth = basis.shape[:2]
-    ahead = held_ref.shape[0]
     tokens = total.shape[0]
 
     def copy_of(step):
-        rows = pl.ds(pl.multiple_of((ahead + step) * depth, depth), depth)
+        rows = pl.ds(pl.multiple_of(step * depth, depth), depth)
         return pltpu.make_async_copy(basis_ref.at[rows], basis.at[step], sem.at[step])
 
     def grads_of(step):
@@ -135,16 +117,10 @@
     map_copy.start()
     total[...] = jnp.zeros_like(total)
 
-    @pl.loop(0, ahead)
-    def _(step):
-        total[...] += jnp.dot(grads_of(step), held_ref[step], preferred_element_type=jnp.float32)
-
     @pl.loop(0, steps)
     def _(step):
         copy_of(step).wait()
-        total[...] += jnp.dot(
-            grads_of(ahead + step), basis[step], preferred_element_type=jnp.float32
-        )
+        total[...] += jnp.dot(grads_of(step), basis[step], preferred_element_type=jnp.float32)
 
     map_copy.wait()
     row = lax.broadcasted_iota(jnp.int32, (tokens, tokens), 0)
@@ -268,6 +244,7 @@
 VMEM = pl.BlockSpec(memory_space=pltpu.VMEM)
 SMEM = pl.BlockSpec(memory_space=pltpu.SMEM)
 ANY = pl.BlockSpec(memory_space=pl.ANY)
+CHEAP = pl.CostEstimate(flops=1, bytes_accessed=1, transcendentals=0)
 
 
 def after(first, *others):
@@ -284,13 +261,12 @@
     to_left = lambda x: lax.ppermute(x, "blk", shift_pairs(n, -1))
     steps = chips // 2
 
-    turned = basis_in.T
     own = basis_in[:WC].T
 
     pairs = chips // 2
     both = jnp.concatenate([grad_out, activations], axis=1)[None]
     got = [lax.ppermute(both, "blk", xor_pairs(n, 4 * key)) for key in range(1, pairs)]
-    both, turned, *got = after(both, turned, *got)
+    both, own, *got = after(both, own, *got)
     grads, acts = pl.pallas_call(
         part_kernel,
         out_shape=(
@@ -307,20 +283,6 @@
     grads_got = lax.ppermute(grads, "blk", xor_pairs(n, 2))
     right, left = [own, to_right(own)], [own, to_left(own)]
 
-    depth, ahead = 1024, 4
-    held = pl.pallas_call(
-        hold_kernel,
-        out_shape=jax.ShapeDtypeStruct((ahead, depth, tile_width), jnp.bfloat16),
-        in_specs=[ANY],
-        out_specs=VMEM,
-        scratch_shapes=[pltpu.SemaphoreType.DMA((ahead,))],
-        compiler_params=pltpu.CompilerParams(vmem_limit_bytes=40 * MIB),
-        cost_estimate=pl.CostEstimate(
-            flops=0, bytes_accessed=4 * ahead * depth * tile_width, transcendentals=0
-        ),
-        name="hold",
-    )(basis_out)
-
     acts = jnp.concatenate([acts, acts_got], axis=0).reshape(tokens // 2, full_in)
     rotated = pl.pallas_call(
         functools.partial(rotate_in_kernel, tok_rows),
@@ -328,10 +290,11 @@
         in_specs=[VMEM, VMEM, VMEM],
         out_specs=VMEM,
         compiler_params=pltpu.CompilerParams(vmem_limit_bytes=8 * MIB),
+        cost_estimate=CHEAP,
         name="rotate_in",
-    )(acts, swap(acts, n), turned)
-    grads_got, rotated, held, own_far, right[-1], left[-1] = after(
-        grads_got, rotated, held, swap(own, n), right[-1], left[-1]
+    )(acts, swap(acts, n), basis_in)
+    grads_got, rotated, own_far, right[-1], left[-1] = after(
+        grads_got, rotated, swap(own, n), right[-1], left[-1]
     )
     rotated = exchange(rotated, n, 2)
     near = [right[0], right[1], left[1]]
@@ -349,25 +312,22 @@
     right.append(to_right(right[-1]))
     left.append(to_left(left[-1]))
 
+    depth = 1024
     aligned = pl.pallas_call(
         functools.partial(rotate_out_kernel, tok_rows),
         out_shape=jax.ShapeDtypeStruct((tile_width, tokens), jnp.bfloat16),
-        in_specs=[VMEM, VMEM, VMEM, ANY, ANY],
+        in_specs=[VMEM, VMEM, ANY, ANY],
         out_specs=VMEM,
         scratch_shapes=[
-            pltpu.VMEM((full_out // depth - ahead, depth, tile_width), jnp.bfloat16),
+            pltpu.VMEM((full_out // depth, depth, tile_width), jnp.bfloat16),
             pltpu.VMEM((tokens, tile_width), jnp.float32),
             pltpu.SMEM(block_map.shape, jnp.int32),
-            pltpu.SemaphoreType.DMA((full_out // depth - ahead + 1,)),
+            pltpu.SemaphoreType.DMA((full_out // depth + 1,)),
         ],
         compiler_params=pltpu.CompilerParams(vmem_limit_bytes=40 * MIB),
-        cost_estimate=pl.CostEstimate(
-            flops=2 * tokens * full_out * tile_width,
-            bytes_accessed=2 * full_out * tile_width,
-            transcendentals=0,
-        ),
+        cost_estimate=CHEAP,
         name="rotate_out",
-    )(grads, grads_far, held, basis_out, block_map)
+    )(grads, grads_far, basis_out, block_map)
 
     aligned, rotated, right[-1], left[-1], *far = after(
         aligned, rotated, right[-1], left[-1], *far
@@ -390,11 +350,7 @@
             pltpu.SemaphoreType.DMA((blocks + 1,)),
         ],
         compiler_params=pltpu.CompilerParams(vmem_limit_bytes=40 * MIB),
-        cost_estimate=pl.CostEstimate(
-            flops=2 * tile_width * full_in * tokens,
-            bytes_accessed=6 * tile_width * full_in,
-            transcendentals=tile_width * full_in,
-        ),
+        cost_estimate=CHEAP,
         name="scale",
     )(aligned, rotated, rotated_far, tile_order, eigenvalues)
 
@@ -416,11 +372,7 @@
             pltpu.SemaphoreType.DMA((len(pieces) + 1,)),
         ],
         compiler_params=pltpu.CompilerParams(vmem_limit_bytes=24 * MIB),
-        cost_estimate=pl.CostEstimate(
-            flops=2 * tile_width * full_in * WC,
-            bytes_accessed=2 * tile_width * full_in + 2 * WC * full_in,
-            transcendentals=0,
-        ),
+        cost_estimate=CHEAP,
         name="project",
     )(scaled, basis_out, *pieces)
 
@@ -435,11 +387,7 @@
         out_specs=(VMEM, VMEM),
         scratch_shapes=[pltpu.VMEM((WR, WC), jnp.float32)],
         compiler_params=pltpu.CompilerParams(vmem_limit_bytes=24 * MIB),
-        cost_estimate=pl.CostEstimate(
-            flops=2 * WR * tile_width * WC,
-            bytes_accessed=2 * WR * tile_width + 12 * WR * WC,
-            transcendentals=0,
-        ),
+        cost_estimate=CHEAP,
         name="window",
     )(window, scaled, projected, *last)
 

time: 90 us -> 88 us (0.978)
  waiting for transfers between devices: 14.9 us -> 23 us
  local copies, waits for them, and re-layouts: 10.8 us -> 4.3 us
  other arithmetic: 3.27 us -> 1.68 us
  Pallas kernels: 24.8 us -> 23.6 us
    unnamed x13 -> x11, local copies, waits for them, and re-layouts: 9.63 us -> 3.09 us
    ppermute x1, waiting for transfers between devices: 0.46 us -> 5.33 us  [ring_body(): grads_got = lax.ppermute(grads, 'blk', xor_pairs(n, 2))]
    pallas_call x1 -> x0, Pallas kernels: 3.19 us -> none  [ring_body(): pl.pallas_call(hold_kernel, out_shape=jax.ShapeDtypeStruct((ahead, depth,...]
    pallas_call x1, Pallas kernels: 7.09 us -> 9.21 us  [ring_body(): pl.pallas_call(functools.partial(rotate_out_kernel, tok_rows), out_shape=...]
    ppermute x3, waiting for transfers between devices: 2.63 us -> 4.46 us  [ring_body(): lax.ppermute(both, 'blk', xor_pairs(n, 4 * key))]
    ppermute x13, waiting for transfers between devices: 1.57 us -> 2.96 us  [swap(): return lax.ppermute(x, 'blk', xor_pairs(n, 1))]
    slice x0 -> x1, local copies, waits for them, and re-layouts: none -> 0.97 us  [ring_body(): own = basis_in[:WC].T]
    concatenate x1, other arithmetic: 1.54 us -> 0.6 us  [ring_body(): jnp.concatenate([grads, grads_got], axis=0).reshape(tokens // 2, full_out)]
  transfers between devices with their start and end apart: 34 -> 34, of which waited for: 9 -> 11; matrix products, arithmetic and copies ran while one was open for 5% -> 2% of each run, Pallas kernels for 25% -> 24%
where the time goes in v11:
time: 88 us; the launch traced here: 87.7 us
  starting transfers between devices  34.9 us (40%)
  Pallas kernels  23.6 us (27%)
  waiting for transfers between devices  23 us (26%)
  local copies, waits for them, and re-layouts  4.3 us (5%)
  other arithmetic  1.68 us (2%)
    ppermute x7, starting transfers between devices, ring_body(): lax.ppermute(x, 'blk', xor_pairs(n, 2 * key))  12.1 us
    pallas_call x1, Pallas kernels, ring_body(): pl.pallas_call(functools.partial(rotate_out_kernel, tok_rows), out_shape=...  9.21 us
    pallas_call x1, Pallas kernels, ring_body(): pl.pallas_call(functools.partial(scale_kernel, begun), out_shape=jax.Shap...  6.27 us
    ppermute x4, waiting for transfers between devices, ring_body(): to_right = lambda x: lax.ppermute(x, 'blk', shift_pairs(n, 1))  6.26 us
    ppermute x4, starting transfers between devices, ring_body(): to_left = lambda x: lax.ppermute(x, 'blk', shift_pairs(n, -1))  5.91 us
    ppermute x3, starting transfers between devices, ring_body(): lax.ppermute(both, 'blk', xor_pairs(n, 4 * key))  5.76 us
    ppermute x1, waiting for transfers between devices, ring_body(): grads_got = lax.ppermute(grads, 'blk', xor_pairs(n, 2))  5.33 us
    ppermute x3, waiting for transfers between devices, ring_body(): lax.ppermute(both, 'blk', xor_pairs(n, 4 * key))  4.46 us
  transfers between devices with their start and end apart: 34, of which 11 were waited for; matrix products, arithmetic and copies ran while one was open for 2% of the time, Pallas kernels for 24%

profile of v11, /device:TPU:0, one launch (start us, length us, event | category | flops | bytes accessed | tf_op | source)
XLA Modules:
  0.0 87.7 jit_solution(17856976130195211036)
XLA Ops:
  0.9 5.1 %collective-permute-start.2 = (bf16[1,2,18432]{2,1,0:T(2,128)(2,1)S(1)}, bf16[1,2,18432]{2,1,0:T(2,128)(2,1)S(1)}, u32[]{:S(2)}, u32[]{:S(2)}) collective-permute-start(bf16[1,2,18432]{2,1,0:T(2,128)(2,1)S(1)} %maximum_bitcast_fusion.refs_0_), channel_id=1, source_target_pairs={{0,12},{1,13},{2,14},{3,15},{4,8},{5,9},{6,10},{7,11},{8,4},{9,5},... | collective-permute-start | bytes 221192 | tf_op jit(solution)/shard_map/ppermute | solution.py:268
  8.8 3.5 %collective-permute-done.1.refs_2_ = bf16[1,2,18432]{2,1,0:T(2,128)(2,1)S(1)} collective-permute-done((bf16[1,2,18432]{2,1,0:T(2,128)(2,1)S(1)}, bf16[1,2,18432]{2,1,0:T(2,128)(2,1)S(1)}, u32[]{:S(2)}, u32[]{:S(2)}) %collective-permute-start.1) | collective-permute-done | bytes 73760 | tf_op jit(solution)/shard_map/ppermute | solution.py:268
  12.3 1.6 %collective-permute-start.4 = (bf16[4,2,4096]{2,1,0:T(2,128)(2,1)S(1)}, bf16[4,2,4096]{2,1,0:T(2,128)(2,1)S(1)}, u32[]{:S(2)}, u32[]{:S(2)}) collective-permute-start(bf16[4,2,4096]{2,1,0:T(2,128)(2,1)S(1)} %get-tuple-element.60), channel_id=1, source_target_pairs={{0,2},{1,3},{2,0},{3,1},{4,6},{5,7},{6,4},{7,5},{8,10},{9,11},{10,... | collective-permute-start | bytes 196616 | tf_op jit(solution)/shard_map/ppermute | solution.py:282
  14.4 1.5 %collective-permute-start.7 = (bf16[256,512]{1,0:T(8,128)(2,1)S(1)}, bf16[256,512]{1,0:T(8,128)(2,1)S(1)}, u32[]{:S(2)}, u32[]{:S(2)}) collective-permute-start(bf16[256,512]{1,0:T(8,128)(2,1)S(1)} %bitcast.4), channel_id=1, source_target_pairs={{0,4},{1,5},{4,8},{5,9},{8,12},{9,13},{12,14},{13,15},{14,10},{15,... | collective-permute-start | bytes 786440 | tf_op jit(solution)/shard_map/ppermute | solution.py:260
  17.6 1.3 %collective-permute-done.5.far_ref = bf16[16,4096]{1,0:T(8,128)(2,1)S(1)} collective-permute-done((bf16[16,4096]{1,0:T(8,128)(2,1)S(1)}, bf16[16,4096]{1,0:T(8,128)(2,1)S(1)}, u32[]{:S(2)}, u32[]{:S(2)}) %collective-permute-start.5) | collective-permute-done | bytes 131104 | tf_op jit(solution)/shard_map/ppermute | solution.py:43
  19.0 1.6 %copy-done = bf16[4096,256]{1,0:T(8,128)(2,1)S(1)} copy-done((bf16[4096,256]{1,0:T(8,128)(2,1)S(1)}, bf16[4096,256]{1,0:T(8,128)(2,1)}, u32[]{:S(2)}) %copy-start) | copy-done | bytes 2097176
  20.5 1.3 %rotate_in.1 = bf16[8,32,256]{2,1,0:T(8,128)(2,1)} custom-call(bf16[16,4096]{1,0:T(8,128)(2,1)S(1)} %reshape.6.near_ref, bf16[16,4096]{1,0:T(8,128)(2,1)S(1)} %collective-permute-done.5.far_ref, bf16[4096,256]{1,0:T(8,128)(2,1)S(1)} %copy-done), custom_call_target="tpu_custom_call" | custom-call | flops 1 | bytes 1 | tf_op jit(solution)/shard_map/rotate_in/pallas_call | solution.py:287
  21.8 5.3 %collective-permute-done.3 = bf16[4,2,14336]{2,1,0:T(2,128)(2,1)S(1)} collective-permute-done((bf16[4,2,14336]{2,1,0:T(2,128)(2,1)S(1)}, bf16[4,2,14336]{2,1,0:T(2,128)(2,1)S(1)}, u32[]{:S(2)}, u32[]{:S(2)}) %collective-permute-start.3) | collective-permute-done | bytes 229408 | tf_op jit(solution)/shard_map/ppermute | solution.py:283
  28.6 1.9 %collective-permute-start.11 = (bf16[256,512]{1,0:T(8,128)(2,1)S(1)}, bf16[256,512]{1,0:T(8,128)(2,1)}, u32[]{:S(2)}, u32[]{:S(2)}) collective-permute-start(bf16[256,512]{1,0:T(8,128)(2,1)S(1)} %collective-permute-done.8.refs_4_), channel_id=1, source_target_pairs={{0,2},{1,3},{4,0},{5,1},{8,4},{9,5},{12,8},{13,9},{14,12},{15,13},... | collective-permute-start | bytes 786440 | tf_op jit(solution)/shard_map/ppermute | solution.py:261
  30.5 6.3 %collective-permute-done.10.refs_6_ = bf16[256,512]{1,0:T(8,128)(2,1)S(1)} collective-permute-done((bf16[256,512]{1,0:T(8,128)(2,1)S(1)}, bf16[256,512]{1,0:T(8,128)(2,1)S(1)}, u32[]{:S(2)}, u32[]{:S(2)}) %collective-permute-start.10) | collective-permute-done | bytes 262176 | tf_op jit(solution)/shard_map/ppermute | solution.py:260
  38.5 1.4 %collective-permute-start.15 = (bf16[256,512]{1,0:T(8,128)(2,1)}, bf16[256,512]{1,0:T(8,128)(2,1)S(1)}, u32[]{:S(2)}, u32[]{:S(2)}) collective-permute-start(bf16[256,512]{1,0:T(8,128)(2,1)} %collective-permute-done.11.refs_8_), channel_id=1, source_target_pairs={{0,2},{1,3},{4,0},{5,1},{8,4},{9,5},{12,8},{13,9},{14,12},{15,13},... | collective-permute-start | bytes 786440 | tf_op jit(solution)/shard_map/ppermute | solution.py:261
  39.9 4.3 %all-to-all-start = ((bf16[8,32,256]{2,1,0:T(8,128)(2,1)}), bf16[8,32,256]{2,1,0:T(8,128)(2,1)S(1)}, u32[]{:S(2)}, u32[]{:S(2)}) async-start(bf16[8,32,256]{2,1,0:T(8,128)(2,1)} %rotate_in.1), calls=%async_computation | async-start | bytes 262144 | tf_op jit(solution)/shard_map/all_to_all | solution.py:48
  44.8 9.2 %rotate_out.1.aligned_ref = bf16[896,32]{1,0:T(8,128)(2,1)S(1)} custom-call(bf16[16,14336]{1,0:T(8,128)(2,1)S(1)} %reshape.7.near_ref, bf16[16,14336]{1,0:T(8,128)(2,1)S(1)} %collective-permute-done.9.far_ref, bf16[14336,896]{1,0:T(8,128)(2,1)} %basis_out_ref.1, s32[16]{0:T(128)S(1)} %copy-done.4), custom_call_target="tpu_custom_call" | custom-call | flops 1 | bytes 1 | tf_op jit(solution)/shard_map/rotate_out/pallas_call | solution.py:316
  54.8 2.1 %collective-permute-start.20 = (bf16[128,512]{1,0:T(8,128)(2,1)S(1)}, bf16[128,512]{1,0:T(8,128)(2,1)S(1)}, u32[]{:S(2)}, u32[]{:S(2)}) collective-permute-start(bf16[128,512]{1,0:T(8,128)(2,1)S(1)} %slice.11), channel_id=1, source_target_pairs={{0,2},{1,3},{4,0},{5,1},{8,4},{9,5},{12,8},{13,9},{14,12},{15,13},... | collective-permute-start | bytes 393224 | tf_op jit(solution)/shard_map/ppermute | solution.py:261
  56.9 6.3 %scale.1.scaled_ref = bf16[896,4096]{1,0:T(8,128)(2,1)S(1)} custom-call(bf16[896,32]{1,0:T(8,128)(2,1)S(1)} %rotate_out.1.aligned_ref, bf16[8,32,256]{2,1,0:T(8,128)(2,1)S(1)} %all-to-all-done.near_ref, bf16[8,32,256]{2,1,0:T(8,128)(2,1)S(1)} %collective-permute-done.18.far_ref, s32[32]{0:T(128)S(1)} %copy-done.3, f32[896,4096]{1,0:T(8,128)} %eigen_ref.1), custom_call_target="tpu_custom_call" | custom-call | flops 1 | bytes 1 | tf_op jit(solution)/shard_map/scale/pallas_call | solution.py:342
  63.8 4.4 %project.1 = (f32[896,512]{1,0:T(8,128)S(1)}, bf16[768,896]{1,0:T(8,128)(2,1)S(1)}) custom-call(bf16[896,4096]{1,0:T(8,128)(2,1)S(1)} %scale.1.scaled_ref, bf16[14336,896]{1,0:T(8,128)(2,1)} %basis_out_ref.1, bf16[256,512]{1,0:T(8,128)(2,1)S(1)} %bitcast.6, bf16[256,512]{1,0:T(8,128)(2,1)S(1)} %collective-permute-done.6.refs_1_, ...), custom_call_target="tpu_custom_call" | custom-call | flops 1 | bytes 1 | tf_op jit(solution)/shard_map/project/pallas_call | solution.py:362
  68.3 1.6 %window.1 = (bf16[8,48,512]{2,1,0:T(8,128)(2,1)S(1)}, f32[8,48,512]{2,1,0:T(8,128)S(1)}) custom-call(bf16[768,896]{1,0:T(8,128)(2,1)S(1)} %get-tuple-element.85.window_ref, bf16[896,4096]{1,0:T(8,128)(2,1)S(1)} %scale.1.scaled_ref, f32[896,512]{1,0:T(8,128)S(1)} %get-tuple-element.86.projected_ref, bf16[128,512]{1,0:T(8,128)(2,1)S(1)} %collective-permute-done.19.refs_0_, ...), custom_call_target="tpu_custom_call" | custom-call | flops 1 | bytes 1 | tf_op jit(solution)/shard_map/window/pallas_call | solution.py:380
  70.1 1.6 %collective-permute-done.25.got_ref = bf16[8,48,512]{2,1,0:T(8,128)(2,1)S(1)} collective-permute-done((bf16[8,48,512]{2,1,0:T(8,128)(2,1)S(1)}, bf16[8,48,512]{2,1,0:T(8,128)(2,1)S(1)}, u32[]{:S(2)}, u32[]{:S(2)}) %collective-permute-start.25) | collective-permute-done | bytes 393248 | tf_op jit(solution)/shard_map/ppermute | solution.py:43
  71.8 3.8 %collective-permute-start.26 = (bf16[48,512]{1,0:T(8,128)(2,1)S(1)}, bf16[48,512]{1,0:T(8,128)(2,1)S(1)}, u32[]{:S(2)}, u32[]{:S(2)}) collective-permute-start(bf16[48,512]{1,0:T(8,128)(2,1)S(1)} %get-tuple-element.92), channel_id=1, source_target_pairs={{0,12},{1,13},{2,14},{3,15},{4,8},{5,9},{6,10},{7,11},{8,4},{9,5},... | collective-permute-start | bytes 147464 | tf_op jit(solution)/shard_map/ppermute | solution.py:405
  75.6 1.4 %collective-permute-start.27 = (bf16[48,512]{1,0:T(8,128)(2,1)S(1)}, bf16[48,512]{1,0:T(8,128)(2,1)S(1)}, u32[]{:S(2)}, u32[]{:S(2)}) collective-permute-start(bf16[48,512]{1,0:T(8,128)(2,1)S(1)} %get-tuple-element.93), channel_id=1, source_target_pairs={{0,14},{1,15},{2,12},{3,13},{4,10},{5,11},{6,8},{7,9},{8,6},{9,7},... | collective-permute-start | bytes 147464 | tf_op jit(solution)/shard_map/ppermute | solution.py:405
  77.6 1.9 %collective-permute-start.29 = (bf16[48,512]{1,0:T(8,128)(2,1)S(1)}, bf16[48,512]{1,0:T(8,128)(2,1)S(1)}, u32[]{:S(2)}, u32[]{:S(2)}) collective-permute-start(bf16[48,512]{1,0:T(8,128)(2,1)S(1)} %get-tuple-element.95), channel_id=1, source_target_pairs={{0,10},{1,11},{2,8},{3,9},{4,14},{5,15},{6,12},{7,13},{8,2},{9,3},... | collective-permute-start | bytes 147464 | tf_op jit(solution)/shard_map/ppermute | solution.py:405
  79.5 1.4 %collective-permute-start.30 = (bf16[48,512]{1,0:T(8,128)(2,1)S(1)}, bf16[48,512]{1,0:T(8,128)(2,1)S(1)}, u32[]{:S(2)}, u32[]{:S(2)}) collective-permute-start(bf16[48,512]{1,0:T(8,128)(2,1)S(1)} %get-tuple-element.96), channel_id=1, source_target_pairs={{0,4},{1,5},{2,6},{3,7},{4,0},{5,1},{6,2},{7,3},{8,12},{9,13},{10,... | collective-permute-start | bytes 147464 | tf_op jit(solution)/shard_map/ppermute | solution.py:405
  80.9 2.0 %collective-permute-start.31 = (bf16[48,512]{1,0:T(8,128)(2,1)S(1)}, bf16[48,512]{1,0:T(8,128)(2,1)S(1)}, u32[]{:S(2)}, u32[]{:S(2)}) collective-permute-start(bf16[48,512]{1,0:T(8,128)(2,1)S(1)} %get-tuple-element.97), channel_id=1, source_target_pairs={{0,6},{1,7},{2,4},{3,5},{4,2},{5,3},{6,0},{7,1},{8,14},{9,15},{10,... | collective-permute-start | bytes 147464 | tf_op jit(solution)/shard_map/ppermute | solution.py:405
  85.1 1.0 %collective-permute-done.31.refs_5_ = bf16[48,512]{1,0:T(8,128)(2,1)S(1)} collective-permute-done((bf16[48,512]{1,0:T(8,128)(2,1)S(1)}, bf16[48,512]{1,0:T(8,128)(2,1)S(1)}, u32[]{:S(2)}, u32[]{:S(2)}) %collective-permute-start.31) | collective-permute-done | bytes 49184 | tf_op jit(solution)/shard_map/ppermute | solution.py:405
  (71 shorter events, 15.6 us)
Async XLA Ops:
  0.9 7.9 %collective-permute-start.2 = (bf16[1,2,18432]{2,1,0:T(2,128)(2,1)S(1)}, bf16[1,2,18432]{2,1,0:T(2,128)(2,1)S(1)}, u32[]{:S(2)}, u32[]{:S(2)}) collective-permute-start(bf16[1,2,18432]{2,1,0:T(2,128)(2,1)S(1)} %maximum_bitcast_fusion.refs_0_), channel_id=1, source_target_pairs={{0,12},{1,13},{2,14},{3,15},{4,8},{5,9},{6,10},{7,11},{8,4},{9,5},... | collective-permute-start | bytes 221192 | tf_op jit(solution)/shard_map/ppermute | solution.py:268
  6.0 6.2 %collective-permute-start.1 = (bf16[1,2,18432]{2,1,0:T(2,128)(2,1)S(1)}, bf16[1,2,18432]{2,1,0:T(2,128)(2,1)S(1)}, u32[]{:S(2)}, u32[]{:S(2)}) collective-permute-start(bf16[1,2,18432]{2,1,0:T(2,128)(2,1)S(1)} %maximum_bitcast_fusion.refs_0_), channel_id=1, source_target_pairs={{0,8},{1,9},{2,10},{3,11},{4,12},{5,13},{6,14},{7,15},{8,0},{9,1},... | collective-permute-start | bytes 221192 | tf_op jit(solution)/shard_map/ppermute | solution.py:268
  6.0 6.2 %collective-permute-start = (bf16[1,2,18432]{2,1,0:T(2,128)(2,1)S(1)}, bf16[1,2,18432]{2,1,0:T(2,128)(2,1)S(1)}, u32[]{:S(2)}, u32[]{:S(2)}) collective-permute-start(bf16[1,2,18432]{2,1,0:T(2,128)(2,1)S(1)} %maximum_bitcast_fusion.refs_0_), channel_id=1, source_target_pairs={{0,4},{1,5},{2,6},{3,7},{4,0},{5,1},{6,2},{7,3},{8,12},{9,13},{10,... | collective-permute-start | bytes 221192 | tf_op jit(solution)/shard_map/ppermute | solution.py:268
  13.9 13.3 %collective-permute-start.8 = (bf16[256,512]{1,0:T(8,128)(2,1)S(1)}, bf16[256,512]{1,0:T(8,128)(2,1)S(1)}, u32[]{:S(2)}, u32[]{:S(2)}) collective-permute-start(bf16[256,512]{1,0:T(8,128)(2,1)S(1)} %bitcast.3), channel_id=1, source_target_pairs={{0,2},{1,3},{4,0},{5,1},{8,4},{9,5},{12,8},{13,9},{14,12},{15,13},... | collective-permute-start | bytes 786440 | tf_op jit(solution)/shard_map/ppermute | solution.py:261
  14.4 12.8 %collective-permute-start.7 = (bf16[256,512]{1,0:T(8,128)(2,1)S(1)}, bf16[256,512]{1,0:T(8,128)(2,1)S(1)}, u32[]{:S(2)}, u32[]{:S(2)}) collective-permute-start(bf16[256,512]{1,0:T(8,128)(2,1)S(1)} %bitcast.4), channel_id=1, source_target_pairs={{0,4},{1,5},{4,8},{5,9},{8,12},{9,13},{12,14},{13,15},{14,10},{15,... | collective-permute-start | bytes 786440 | tf_op jit(solution)/shard_map/ppermute | solution.py:260
  15.9 11.3 %collective-permute-start.6 = (bf16[256,512]{1,0:T(8,128)(2,1)S(1)}, bf16[256,512]{1,0:T(8,128)(2,1)S(1)}, u32[]{:S(2)}, u32[]{:S(2)}) collective-permute-start(bf16[256,512]{1,0:T(8,128)(2,1)S(1)} %bitcast.5), channel_id=1, source_target_pairs={{0,1},{1,0},{2,3},{3,2},{4,5},{5,4},{6,7},{7,6},{8,9},{9,8},{10,11... | collective-permute-start | bytes 786440 | tf_op jit(solution)/shard_map/ppermute | solution.py:43
  15.9 11.2 %collective-permute-start.3 = (bf16[4,2,14336]{2,1,0:T(2,128)(2,1)S(1)}, bf16[4,2,14336]{2,1,0:T(2,128)(2,1)S(1)}, u32[]{:S(2)}, u32[]{:S(2)}) collective-permute-start(bf16[4,2,14336]{2,1,0:T(2,128)(2,1)S(1)} %get-tuple-element.59), channel_id=1, source_target_pairs={{0,2},{1,3},{2,0},{3,1},{4,6},{5,7},{6,4},{7,5},{8,10},{9,11},{10,... | collective-permute-start | bytes 688136 | tf_op jit(solution)/shard_map/ppermute | solution.py:283
  27.9 9.6 %collective-permute-start.9 = (bf16[16,14336]{1,0:T(8,128)(2,1)S(1)}, bf16[16,14336]{1,0:T(8,128)(2,1)S(1)}, u32[]{:S(2)}, u32[]{:S(2)}) collective-permute-start(bf16[16,14336]{1,0:T(8,128)(2,1)S(1)} %reshape.7.near_ref), channel_id=1, source_target_pairs={{0,1},{1,0},{2,3},{3,2},{4,5},{5,4},{6,7},{7,6},{8,9},{9,8},{10,11... | collective-permute-start | bytes 1376264 | tf_op jit(solution)/shard_map/ppermute | solution.py:43
  28.5 8.3 %collective-permute-start.10 = (bf16[256,512]{1,0:T(8,128)(2,1)S(1)}, bf16[256,512]{1,0:T(8,128)(2,1)S(1)}, u32[]{:S(2)}, u32[]{:S(2)}) collective-permute-start(bf16[256,512]{1,0:T(8,128)(2,1)S(1)} %collective-permute-done.7.refs_2_), channel_id=1, source_target_pairs={{0,4},{1,5},{4,8},{5,9},{8,12},{9,13},{12,14},{13,15},{14,10},{15,... | collective-permute-start | bytes 786440 | tf_op jit(solution)/shard_map/ppermute | solution.py:260
  28.5 8.3 %collective-permute-start.13 = (bf16[256,512]{1,0:T(8,128)(2,1)S(1)}, bf16[256,512]{1,0:T(8,128)(2,1)S(1)}, u32[]{:S(2)}, u32[]{:S(2)}) collective-permute-start(bf16[256,512]{1,0:T(8,128)(2,1)S(1)} %collective-permute-done.8.refs_4_), channel_id=1, source_target_pairs={{0,1},{1,0},{2,3},{3,2},{4,5},{5,4},{6,7},{7,6},{8,9},{9,8},{10,11... | collective-permute-start | bytes 786440 | tf_op jit(solution)/shard_map/ppermute | solution.py:43
  28.6 8.9 %collective-permute-start.11 = (bf16[256,512]{1,0:T(8,128)(2,1)S(1)}, bf16[256,512]{1,0:T(8,128)(2,1)}, u32[]{:S(2)}, u32[]{:S(2)}) collective-permute-start(bf16[256,512]{1,0:T(8,128)(2,1)S(1)} %collective-permute-done.8.refs_4_), channel_id=1, source_target_pairs={{0,2},{1,3},{4,0},{5,1},{8,4},{9,5},{12,8},{13,9},{14,12},{15,13},... | collective-permute-start | bytes 786440 | tf_op jit(solution)/shard_map/ppermute | solution.py:261
  37.5 16.6 %collective-permute-start.16 = (bf16[256,512]{1,0:T(8,128)(2,1)S(1)}, bf16[256,512]{1,0:T(8,128)(2,1)}, u32[]{:S(2)}, u32[]{:S(2)}) collective-permute-start(bf16[256,512]{1,0:T(8,128)(2,1)S(1)} %collective-permute-done.10.refs_6_), channel_id=1, source_target_pairs={{0,1},{1,0},{2,3},{3,2},{4,5},{5,4},{6,7},{7,6},{8,9},{9,8},{10,11... | collective-permute-start | bytes 786440 | tf_op jit(solution)/shard_map/ppermute | solution.py:43
  37.5 16.6 %collective-permute-start.14 = (bf16[256,512]{1,0:T(8,128)(2,1)S(1)}, bf16[256,512]{1,0:T(8,128)(2,1)S(1)}, u32[]{:S(2)}, u32[]{:S(2)}) collective-permute-start(bf16[256,512]{1,0:T(8,128)(2,1)S(1)} %collective-permute-done.10.refs_6_), channel_id=1, source_target_pairs={{0,4},{1,5},{4,8},{5,9},{8,12},{9,13},{12,14},{13,15},{14,10},{15,... | collective-permute-start | bytes 786440 | tf_op jit(solution)/shard_map/ppermute | solution.py:260
  38.3 15.8 %collective-permute-start.17 = (bf16[256,512]{1,0:T(8,128)(2,1)}, bf16[256,512]{1,0:T(8,128)(2,1)}, u32[]{:S(2)}, u32[]{:S(2)}) collective-permute-start(bf16[256,512]{1,0:T(8,128)(2,1)} %collective-permute-done.11.refs_8_), channel_id=1, source_target_pairs={{0,1},{1,0},{2,3},{3,2},{4,5},{5,4},{6,7},{7,6},{8,9},{9,8},{10,11... | collective-permute-start | bytes 786440 | tf_op jit(solution)/shard_map/ppermute | solution.py:43
  38.5 15.6 %collective-permute-start.15 = (bf16[256,512]{1,0:T(8,128)(2,1)}, bf16[256,512]{1,0:T(8,128)(2,1)S(1)}, u32[]{:S(2)}, u32[]{:S(2)}) collective-permute-start(bf16[256,512]{1,0:T(8,128)(2,1)} %collective-permute-done.11.refs_8_), channel_id=1, source_target_pairs={{0,2},{1,3},{4,0},{5,1},{8,4},{9,5},{12,8},{13,9},{14,12},{15,13},... | collective-permute-start | bytes 786440 | tf_op jit(solution)/shard_map/ppermute | solution.py:261
  39.9 14.2 %all-to-all-start = ((bf16[8,32,256]{2,1,0:T(8,128)(2,1)}), bf16[8,32,256]{2,1,0:T(8,128)(2,1)S(1)}, u32[]{:S(2)}, u32[]{:S(2)}) async-start(bf16[8,32,256]{2,1,0:T(8,128)(2,1)} %rotate_in.1), calls=%async_computation | async-start | bytes 262144 | tf_op jit(solution)/shard_map/all_to_all | solution.py:48
  54.1 9.1 %collective-permute-start.21 = (bf16[256,512]{1,0:T(8,128)(2,1)S(1)}, bf16[256,512]{1,0:T(8,128)(2,1)S(1)}, u32[]{:S(2)}, u32[]{:S(2)}) collective-permute-start(bf16[256,512]{1,0:T(8,128)(2,1)S(1)} %collective-permute-done.14.refs_10_), channel_id=1, source_target_pairs={{0,1},{1,0},{2,3},{3,2},{4,5},{5,4},{6,7},{7,6},{8,9},{9,8},{10,11... | collective-permute-start | bytes 786440 | tf_op jit(solution)/shard_map/ppermute | solution.py:43
  54.2 9.1 %collective-permute-start.22 = (bf16[256,512]{1,0:T(8,128)(2,1)S(1)}, bf16[256,512]{1,0:T(8,128)(2,1)S(1)}, u32[]{:S(2)}, u32[]{:S(2)}) collective-permute-start(bf16[256,512]{1,0:T(8,128)(2,1)S(1)} %collective-permute-done.15.refs_12_), channel_id=1, source_target_pairs={{0,1},{1,0},{2,3},{3,2},{4,5},{5,4},{6,7},{7,6},{8,9},{9,8},{10,11... | collective-permute-start | bytes 786440 | tf_op jit(solution)/shard_map/ppermute | solution.py:43
  54.8 8.4 %collective-permute-start.20 = (bf16[128,512]{1,0:T(8,128)(2,1)S(1)}, bf16[128,512]{1,0:T(8,128)(2,1)S(1)}, u32[]{:S(2)}, u32[]{:S(2)}) collective-permute-start(bf16[128,512]{1,0:T(8,128)(2,1)S(1)} %slice.11), channel_id=1, source_target_pairs={{0,2},{1,3},{4,0},{5,1},{8,4},{9,5},{12,8},{13,9},{14,12},{15,13},... | collective-permute-start | bytes 393224 | tf_op jit(solution)/shard_map/ppermute | solution.py:261
  56.9 6.4 %collective-permute-start.19 = (bf16[128,512]{1,0:T(8,128)(2,1)S(1)}, bf16[128,512]{1,0:T(8,128)(2,1)S(1)}, u32[]{:S(2)}, u32[]{:S(2)}) collective-permute-start(bf16[128,512]{1,0:T(8,128)(2,1)S(1)} %slice.10), channel_id=1, source_target_pairs={{0,4},{1,5},{4,8},{5,9},{8,12},{9,13},{12,14},{13,15},{14,10},{15,... | collective-permute-start | bytes 393224 | tf_op jit(solution)/shard_map/ppermute | solution.py:260
  71.8 9.1 %collective-permute-start.26 = (bf16[48,512]{1,0:T(8,128)(2,1)S(1)}, bf16[48,512]{1,0:T(8,128)(2,1)S(1)}, u32[]{:S(2)}, u32[]{:S(2)}) collective-permute-start(bf16[48,512]{1,0:T(8,128)(2,1)S(1)} %get-tuple-element.92), channel_id=1, source_target_pairs={{0,12},{1,13},{2,14},{3,15},{4,8},{5,9},{6,10},{7,11},{8,4},{9,5},... | collective-permute-start | bytes 147464 | tf_op jit(solution)/shard_map/ppermute | solution.py:405
  75.6 7.3 %collective-permute-start.27 = (bf16[48,512]{1,0:T(8,128)(2,1)S(1)}, bf16[48,512]{1,0:T(8,128)(2,1)S(1)}, u32[]{:S(2)}, u32[]{:S(2)}) collective-permute-start(bf16[48,512]{1,0:T(8,128)(2,1)S(1)} %get-tuple-element.93), channel_id=1, source_target_pairs={{0,14},{1,15},{2,12},{3,13},{4,10},{5,11},{6,8},{7,9},{8,6},{9,7},... | collective-permute-start | bytes 147464 | tf_op jit(solution)/shard_map/ppermute | solution.py:405
  77.0 7.4 %collective-permute-start.28 = (bf16[48,512]{1,0:T(8,128)(2,1)S(1)}, bf16[48,512]{1,0:T(8,128)(2,1)S(1)}, u32[]{:S(2)}, u32[]{:S(2)}) collective-permute-start(bf16[48,512]{1,0:T(8,128)(2,1)S(1)} %get-tuple-element.94), channel_id=1, source_target_pairs={{0,8},{1,9},{2,10},{3,11},{4,12},{5,13},{6,14},{7,15},{8,0},{9,1},... | collective-permute-start | bytes 147464 | tf_op jit(solution)/shard_map/ppermute | solution.py:405
  77.6 7.5 %collective-permute-start.29 = (bf16[48,512]{1,0:T(8,128)(2,1)S(1)}, bf16[48,512]{1,0:T(8,128)(2,1)S(1)}, u32[]{:S(2)}, u32[]{:S(2)}) collective-permute-start(bf16[48,512]{1,0:T(8,128)(2,1)S(1)} %get-tuple-element.95), channel_id=1, source_target_pairs={{0,10},{1,11},{2,8},{3,9},{4,14},{5,15},{6,12},{7,13},{8,2},{9,3},... | collective-permute-start | bytes 147464 | tf_op jit(solution)/shard_map/ppermute | solution.py:405
  (15 other events, 62.1 us)

commit v12 on v11

--- a/solution.py
+++ b/solution.py
@@ -86,42 +86,49 @@
         out_ref[copy] = ordered
 
 
-def rotate_out_kernel(
+def rotate_part(first, near_ref, far_ref, basis_ref, basis, total, sem):
+    steps, depth = basis.shape[:2]
+
+    def copy_of(step):
+        rows = pl.ds(pl.multiple_of((first + step) * depth, depth), depth)
+        return pltpu.make_async_copy(basis_ref.at[rows], basis.at[step], sem.at[step])
+
+    @pl.loop(0, steps)
+    def _(step):
+        copy_of(step).start()
+
+    @pl.loop(0, steps)
+    def _(step):
+        columns = pl.ds(pl.multiple_of((first + step) * depth, depth), depth)
+        grads = jnp.concatenate([near_ref[:, columns], far_ref[:, columns]], axis=0)
+        copy_of(step).wait()
+        total[...] += jnp.dot(grads, basis[step], preferred_element_type=jnp.float32)
+
+
+def rotate_first_kernel(near_ref, far_ref, basis_ref, out_ref, basis, sem):
+    out_ref[...] = jnp.zeros_like(out_ref)
+    rotate_part(0, near_ref, far_ref, basis_ref, basis, out_ref, sem)
+
+
+def rotate_last_kernel(
     tok_rows,
+    first,
     near_ref,
     far_ref,
     basis_ref,
     map_ref,
+    start_ref,
     out_ref,
     basis,
     total,
     stored_map,
     sem,
 ):
-    steps, depth = basis.shape[:2]
     tokens = total.shape[0]
-
-    def copy_of(step):
-        rows = pl.ds(pl.multiple_of(step * depth, depth), depth)
-        return pltpu.make_async_copy(basis_ref.at[rows], basis.at[step], sem.at[step])
-
-    def grads_of(step):
-        columns = pl.ds(pl.multiple_of(step * depth, depth), depth)
-        return jnp.concatenate([near_ref[:, columns], far_ref[:, columns]], axis=0)
-
-    @pl.loop(0, steps)
-    def _(step):
-        copy_of(step).start()
-
-    map_copy = pltpu.make_async_copy(map_ref, stored_map, sem.at[steps])
+    map_copy = pltpu.make_async_copy(map_ref, stored_map, sem.at[basis.shape[0]])
     map_copy.start()
-    total[...] = jnp.zeros_like(total)
-
-    @pl.loop(0, steps)
-    def _(step):
-        copy_of(step).wait()
-        total[...] += jnp.dot(grads_of(step), basis[step], preferred_element_type=jnp.float32)
-
+    total[...] = start_ref[...]
+    rotate_part(first, near_ref, far_ref, basis_ref, basis, total, sem)
     map_copy.wait()
     row = lax.broadcasted_iota(jnp.int32, (tokens, tokens), 0)
     block = row >> bits_of(tok_rows)
@@ -293,8 +300,9 @@
         cost_estimate=CHEAP,
         name="rotate_in",
     )(acts, swap(acts, n), basis_in)
-    grads_got, rotated, own_far, right[-1], left[-1] = after(
-        grads_got, rotated, swap(own, n), right[-1], left[-1]
+    own_far = swap(own, n)
+    grads_got, right[-1], left[-1], own_far, _ = after(
+        grads_got, right[-1], left[-1], own_far, rotated
     )
     rotated = exchange(rotated, n, 2)
     near = [right[0], right[1], left[1]]
@@ -304,35 +312,60 @@
     grads = jnp.concatenate([grads, grads_got], axis=0).reshape(tokens // 2, full_out)
     grads_far = swap(grads, n)
     far = [swap(piece, n) for piece in near[1:]]
-    grads, grads_far, right[-1], left[-1], *far = after(
-        grads, grads_far, right[-1], left[-1], *far
-    )
+    grads, grads_far, *far = after(grads, grads_far, *far)
+    far = [own_far, *far]
+
+    depth = 1024
+    cuts = (0, full_out // depth // 2, full_out // depth)
+    rotate = lambda kernel, count, scratch, shape, dtype, *operands: pl.pallas_call(
+        kernel,
+        out_shape=jax.ShapeDtypeStruct(shape, dtype),
+        in_specs=[VMEM, VMEM, ANY, ANY, VMEM][: len(operands)],
+        out_specs=VMEM,
+        scratch_shapes=[pltpu.VMEM((count, depth, tile_width), jnp.bfloat16)]
+        + scratch
+        + [pltpu.SemaphoreType.DMA((count + 1,))],
+        compiler_params=pltpu.CompilerParams(vmem_limit_bytes=40 * MIB),
+        cost_estimate=CHEAP,
+        name=kernel.func.__name__[:-7],
+    )(*operands)
+    start = rotate(
+        functools.partial(rotate_first_kernel),
+        cuts[1],
+        [],
+        (tokens, tile_width),
+        jnp.float32,
+        grads,
+        grads_far,
+        basis_out,
+    )
+    start, grads, rotated, right[-1], left[-1] = after(
+        start, grads, rotated, right[-1], left[-1]
+    )
+    rotated_far = swap(rotated, n)
     near += [right[-1], left[-1]]
-    far = [own_far, *far, swap(right[-1], n), swap(left[-1], n)]
+    far += [swap(right[-1], n), swap(left[-1], n)]
     right.append(to_right(right[-1]))
     left.append(to_left(left[-1]))
-
-    depth = 1024
-    aligned = pl.pallas_call(
-        functools.partial(rotate_out_kernel, tok_rows),
-        out_shape=jax.ShapeDtypeStruct((tile_width, tokens), jnp.bfloat16),
-        in_specs=[VMEM, VMEM, ANY, ANY],
-        out_specs=VMEM,
-        scratch_shapes=[
-            pltpu.VMEM((full_out // depth, depth, tile_width), jnp.bfloat16),
+    aligned = rotate(
+        functools.partial(rotate_last_kernel, tok_rows, cuts[1]),
+        cuts[2] - cuts[1],
+        [
             pltpu.VMEM((tokens, tile_width), jnp.float32),
             pltpu.SMEM(block_map.shape, jnp.int32),
-            pltpu.SemaphoreType.DMA((full_out // depth + 1,)),
         ],
-        compiler_params=pltpu.CompilerParams(vmem_limit_bytes=40 * MIB),
-        cost_estimate=CHEAP,
-        name="rotate_out",
-    )(grads, grads_far, basis_out, block_map)
-
-    aligned, rotated, right[-1], left[-1], *far = after(
-        aligned, rotated, right[-1], left[-1], *far
-    )
-    rotated_far = swap(rotated, n)
+        (tile_width, tokens),
+        jnp.bfloat16,
+        grads,
+        grads_far,
+        basis_out,
+        block_map,
+        start,
+    )
+
+    aligned, rotated_far, right[-1], left[-1], *far = after(
+        aligned, rotated_far, right[-1], left[-1], *far
+    )
     cut = in_width // 2
     last = [to_right(right[-1][:cut]), to_left(left[-1][cut:])]
     near += [right[-1], left[-1]]

time: 88 us -> 86.1 us (0.978)
  waiting for transfers between devices: 23 us -> 21.4 us
  Pallas kernels: 23.6 us -> 25.1 us
  local copies, waits for them, and re-layouts: 4.3 us -> 2.95 us
    ppermute x4, waiting for transfers between devices: 6.26 us -> 0.88 us  [ring_body(): to_right = lambda x: lax.ppermute(x, 'blk', shift_pairs(n, 1))]
    all_to_all x1, waiting for transfers between devices: 0.01 us -> 2.07 us  [exchange(): return lax.all_to_all(x, 'blk', 0, 0, axis_index_groups=groups, tiled=True)]
    pallas_call x1 -> x2, Pallas kernels: 9.21 us -> 10.7 us  [ring_body(): pl.pallas_call(kernel, out_shape=jax.ShapeDtypeStruct(shape, dtype), in_s...]
    unnamed x11 -> x7, local copies, waits for them, and re-layouts: 3.09 us -> 1.74 us
    ppermute x1, waiting for transfers between devices: 5.33 us -> 6.64 us  [ring_body(): grads_got = lax.ppermute(grads, 'blk', xor_pairs(n, 2))]
    ppermute x7, waiting for transfers between devices: 3.08 us -> 4 us  [ring_body(): lax.ppermute(x, 'blk', xor_pairs(n, 2 * key))]
    ppermute x7, starting transfers between devices: 12.1 us -> 11.2 us  [ring_body(): lax.ppermute(x, 'blk', xor_pairs(n, 2 * key))]
  transfers between devices with their start and end apart: 34 -> 34, of which waited for: 11 -> 12; matrix products, arithmetic and copies ran while one was open for 2% -> 2% of each run, Pallas kernels for 24% -> 26%
where the time goes in v12:
time: 86.1 us; the launch traced here: 85.7 us
  starting transfers between devices  34.4 us (40%)
  Pallas kernels  25.1 us (29%)
  waiting for transfers between devices  21.4 us (25%)
  local copies, waits for them, and re-layouts  2.95 us (3%)
  other arithmetic  1.68 us (2%)
    ppermute x7, starting transfers between devices, ring_body(): lax.ppermute(x, 'blk', xor_pairs(n, 2 * key))  11.2 us
    pallas_call x2, Pallas kernels, ring_body(): pl.pallas_call(kernel, out_shape=jax.ShapeDtypeStruct(shape, dtype), in_s...  10.7 us
    ppermute x1, waiting for transfers between devices, ring_body(): grads_got = lax.ppermute(grads, 'blk', xor_pairs(n, 2))  6.64 us
    ppermute x4, starting transfers between devices, ring_body(): to_left = lambda x: lax.ppermute(x, 'blk', shift_pairs(n, -1))  6.27 us
    pallas_call x1, Pallas kernels, ring_body(): pl.pallas_call(functools.partial(scale_kernel, begun), out_shape=jax.Shap...  6.23 us
    ppermute x3, starting transfers between devices, ring_body(): lax.ppermute(both, 'blk', xor_pairs(n, 4 * key))  5.76 us
    all_to_all x1, starting transfers between devices, exchange(): return lax.all_to_all(x, 'blk', 0, 0, axis_index_groups=groups, tiled=True)  4.95 us
    pallas_call x1, Pallas kernels, ring_body(): pl.pallas_call(functools.partial(project_kernel, (0, 6, len(pieces))), ou...  4.48 us
  transfers between devices with their start and end apart: 34, of which 12 were waited for; matrix products, arithmetic and copies ran while one was open for 2% of the time, Pallas kernels for 26%

profile of v12, /device:TPU:0, one launch (start us, length us, event | category | flops | bytes accessed | tf_op | source)
XLA Modules:
  0.0 85.7 jit_solution(11653508072254806863)
XLA Ops:
  0.9 5.1 %collective-permute-start.2 = (bf16[1,2,18432]{2,1,0:T(2,128)(2,1)S(1)}, bf16[1,2,18432]{2,1,0:T(2,128)(2,1)S(1)}, u32[]{:S(2)}, u32[]{:S(2)}) collective-permute-start(bf16[1,2,18432]{2,1,0:T(2,128)(2,1)S(1)} %maximum_bitcast_fusion.refs_0_), channel_id=1, source_target_pairs={{0,12},{1,13},{2,14},{3,15},{4,8},{5,9},{6,10},{7,11},{8,4},{9,5},... | collective-permute-start | bytes 221192 | tf_op jit(solution)/shard_map/ppermute | solution.py:275
  8.8 3.5 %collective-permute-done.1.refs_2_ = bf16[1,2,18432]{2,1,0:T(2,128)(2,1)S(1)} collective-permute-done((bf16[1,2,18432]{2,1,0:T(2,128)(2,1)S(1)}, bf16[1,2,18432]{2,1,0:T(2,128)(2,1)S(1)}, u32[]{:S(2)}, u32[]{:S(2)}) %collective-permute-start.1) | collective-permute-done | bytes 73760 | tf_op jit(solution)/shard_map/ppermute | solution.py:275
  12.3 1.6 %collective-permute-start.7 = (bf16[4,2,4096]{2,1,0:T(2,128)(2,1)S(1)}, bf16[4,2,4096]{2,1,0:T(2,128)(2,1)S(1)}, u32[]{:S(2)}, u32[]{:S(2)}) collective-permute-start(bf16[4,2,4096]{2,1,0:T(2,128)(2,1)S(1)} %get-tuple-element.63), channel_id=1, source_target_pairs={{0,2},{1,3},{2,0},{3,1},{4,6},{5,7},{6,4},{7,5},{8,10},{9,11},{10,... | collective-permute-start | bytes 196616 | tf_op jit(solution)/shard_map/ppermute | solution.py:289
  14.4 1.5 %collective-permute-start.4 = (bf16[256,512]{1,0:T(8,128)(2,1)S(1)}, bf16[256,512]{1,0:T(8,128)(2,1)S(1)}, u32[]{:S(2)}, u32[]{:S(2)}) collective-permute-start(bf16[256,512]{1,0:T(8,128)(2,1)S(1)} %bitcast.5), channel_id=1, source_target_pairs={{0,4},{1,5},{4,8},{5,9},{8,12},{9,13},{12,14},{13,15},{14,10},{15,... | collective-permute-start | bytes 786440 | tf_op jit(solution)/shard_map/ppermute | solution.py:267
  16.9 1.3 %collective-permute-done.8.far_ref = bf16[16,4096]{1,0:T(8,128)(2,1)S(1)} collective-permute-done((bf16[16,4096]{1,0:T(8,128)(2,1)S(1)}, bf16[16,4096]{1,0:T(8,128)(2,1)S(1)}, u32[]{:S(2)}, u32[]{:S(2)}) %collective-permute-start.8) | collective-permute-done | bytes 131104 | tf_op jit(solution)/shard_map/ppermute | solution.py:43
  18.3 1.6 %copy-done = bf16[4096,256]{1,0:T(8,128)(2,1)S(1)} copy-done((bf16[4096,256]{1,0:T(8,128)(2,1)S(1)}, bf16[4096,256]{1,0:T(8,128)(2,1)}, u32[]{:S(2)}) %copy-start) | copy-done | bytes 2097176
  19.8 1.2 %rotate_in.1 = bf16[8,32,256]{2,1,0:T(8,128)(2,1)} custom-call(bf16[16,4096]{1,0:T(8,128)(2,1)S(1)} %reshape.6.near_ref, bf16[16,4096]{1,0:T(8,128)(2,1)S(1)} %collective-permute-done.8.far_ref, bf16[4096,256]{1,0:T(8,128)(2,1)S(1)} %copy-done), custom_call_target="tpu_custom_call" | custom-call | flops 1 | bytes 1 | tf_op jit(solution)/shard_map/rotate_in/pallas_call | solution.py:294
  21.1 6.6 %collective-permute-done.3 = bf16[4,2,14336]{2,1,0:T(2,128)(2,1)S(1)} collective-permute-done((bf16[4,2,14336]{2,1,0:T(2,128)(2,1)S(1)}, bf16[4,2,14336]{2,1,0:T(2,128)(2,1)S(1)}, u32[]{:S(2)}, u32[]{:S(2)}) %collective-permute-start.3) | collective-permute-done | bytes 229408 | tf_op jit(solution)/shard_map/ppermute | solution.py:290
  29.2 2.0 %collective-permute-start.13 = (bf16[256,512]{1,0:T(8,128)(2,1)S(1)}, bf16[256,512]{1,0:T(8,128)(2,1)S(1)}, u32[]{:S(2)}, u32[]{:S(2)}) collective-permute-start(bf16[256,512]{1,0:T(8,128)(2,1)S(1)} %collective-permute-done.5.refs_4_), channel_id=1, source_target_pairs={{0,2},{1,3},{4,0},{5,1},{8,4},{9,5},{12,8},{13,9},{14,12},{15,13},... | collective-permute-start | bytes 786440 | tf_op jit(solution)/shard_map/ppermute | solution.py:268
  31.2 5.0 %all-to-all-start = ((bf16[8,32,256]{2,1,0:T(8,128)(2,1)}), bf16[8,32,256]{2,1,0:T(8,128)(2,1)S(1)}, u32[]{:S(2)}, u32[]{:S(2)}) async-start(bf16[8,32,256]{2,1,0:T(8,128)(2,1)} %rotate_in.1), calls=%async_computation | async-start | bytes 262144 | tf_op jit(solution)/shard_map/all_to_all | solution.py:48
  36.2 5.2 %rotate_first.1.start_ref = f32[32,896]{1,0:T(8,128)S(1)} custom-call(bf16[16,14336]{1,0:T(8,128)(2,1)S(1)} %reshape.7.near_ref, bf16[16,14336]{1,0:T(8,128)(2,1)S(1)} %collective-permute-done.9.far_ref, bf16[14336,896]{1,0:T(8,128)(2,1)} %basis_out_ref.1), custom_call_target="tpu_custom_call" | custom-call | flops 1 | bytes 1 | tf_op jit(solution)/shard_map/rotate_first/pallas_call | solution.py:320
  41.4 2.1 %all-to-all-done.near_ref = bf16[8,32,256]{2,1,0:T(8,128)(2,1)S(1)} async-done(((bf16[8,32,256]{2,1,0:T(8,128)(2,1)}), bf16[8,32,256]{2,1,0:T(8,128)(2,1)S(1)}, u32[]{:S(2)}, u32[]{:S(2)}) %all-to-all-start) | async-done | bytes 131104 | tf_op jit(solution)/shard_map/all_to_all | solution.py:48
  44.0 1.7 %collective-permute-start.16 = (bf16[256,512]{1,0:T(8,128)(2,1)S(1)}, bf16[256,512]{1,0:T(8,128)(2,1)S(1)}, u32[]{:S(2)}, u32[]{:S(2)}) collective-permute-start(bf16[256,512]{1,0:T(8,128)(2,1)S(1)} %collective-permute-done.13.refs_8_), channel_id=1, source_target_pairs={{0,2},{1,3},{4,0},{5,1},{8,4},{9,5},{12,8},{13,9},{14,12},{15,13},... | collective-permute-start | bytes 786440 | tf_op jit(solution)/shard_map/ppermute | solution.py:268
  45.8 5.5 %rotate_last.1.aligned_ref = bf16[896,32]{1,0:T(8,128)(2,1)S(1)} custom-call(bf16[16,14336]{1,0:T(8,128)(2,1)S(1)} %reshape.7.near_ref, bf16[16,14336]{1,0:T(8,128)(2,1)S(1)} %collective-permute-done.9.far_ref, bf16[14336,896]{1,0:T(8,128)(2,1)} %basis_out_ref.1, s32[16]{0:T(128)S(1)} %copy-done.2, f32[32,896]{1,0:T(8,128)S(1)} %rotate_first.1.start_ref), custom_call_target="tpu_custom_call" | custom-call | flops 1 | bytes 1 | tf_op jit(solution)/shard_map/rotate_last/pallas_call | solution.py:320
  52.9 2.0 %collective-permute-start.20 = (bf16[128,512]{1,0:T(8,128)(2,1)S(1)}, bf16[128,512]{1,0:T(8,128)(2,1)S(1)}, u32[]{:S(2)}, u32[]{:S(2)}) collective-permute-start(bf16[128,512]{1,0:T(8,128)(2,1)S(1)} %slice.11), channel_id=1, source_target_pairs={{0,2},{1,3},{4,0},{5,1},{8,4},{9,5},{12,8},{13,9},{14,12},{15,13},... | collective-permute-start | bytes 393224 | tf_op jit(solution)/shard_map/ppermute | solution.py:268
  55.0 6.2 %scale.1.scaled_ref = bf16[896,4096]{1,0:T(8,128)(2,1)S(1)} custom-call(bf16[896,32]{1,0:T(8,128)(2,1)S(1)} %rotate_last.1.aligned_ref, bf16[8,32,256]{2,1,0:T(8,128)(2,1)S(1)} %all-to-all-done.near_ref, bf16[8,32,256]{2,1,0:T(8,128)(2,1)S(1)} %collective-permute-done.14.far_ref, s32[32]{0:T(128)S(1)} %copy-done.1, f32[896,4096]{1,0:T(8,128)} %eigen_ref.1), custom_call_target="tpu_custom_call" | custom-call | flops 1 | bytes 1 | tf_op jit(solution)/shard_map/scale/pallas_call | solution.py:375
  61.8 4.5 %project.1 = (f32[896,512]{1,0:T(8,128)S(1)}, bf16[768,896]{1,0:T(8,128)(2,1)S(1)}) custom-call(bf16[896,4096]{1,0:T(8,128)(2,1)S(1)} %scale.1.scaled_ref, bf16[14336,896]{1,0:T(8,128)(2,1)} %basis_out_ref.1, bf16[256,512]{1,0:T(8,128)(2,1)S(1)} %bitcast.6, bf16[256,512]{1,0:T(8,128)(2,1)S(1)} %collective-permute-done.6.refs_1_, ...), custom_call_target="tpu_custom_call" | custom-call | flops 1 | bytes 1 | tf_op jit(solution)/shard_map/project/pallas_call | solution.py:395
  66.4 1.6 %window.1 = (bf16[8,48,512]{2,1,0:T(8,128)(2,1)S(1)}, f32[8,48,512]{2,1,0:T(8,128)S(1)}) custom-call(bf16[768,896]{1,0:T(8,128)(2,1)S(1)} %get-tuple-element.89.window_ref, bf16[896,4096]{1,0:T(8,128)(2,1)S(1)} %scale.1.scaled_ref, f32[896,512]{1,0:T(8,128)S(1)} %get-tuple-element.90.projected_ref, bf16[128,512]{1,0:T(8,128)(2,1)S(1)} %collective-permute-done.19.refs_0_, ...), custom_call_target="tpu_custom_call" | custom-call | flops 1 | bytes 1 | tf_op jit(solution)/shard_map/window/pallas_call | solution.py:413
  68.2 1.6 %collective-permute-done.25.got_ref = bf16[8,48,512]{2,1,0:T(8,128)(2,1)S(1)} collective-permute-done((bf16[8,48,512]{2,1,0:T(8,128)(2,1)S(1)}, bf16[8,48,512]{2,1,0:T(8,128)(2,1)S(1)}, u32[]{:S(2)}, u32[]{:S(2)}) %collective-permute-start.25) | collective-permute-done | bytes 393248 | tf_op jit(solution)/shard_map/ppermute | solution.py:43
  69.8 3.3 %collective-permute-start.26 = (bf16[48,512]{1,0:T(8,128)(2,1)S(1)}, bf16[48,512]{1,0:T(8,128)(2,1)S(1)}, u32[]{:S(2)}, u32[]{:S(2)}) collective-permute-start(bf16[48,512]{1,0:T(8,128)(2,1)S(1)} %get-tuple-element.96), channel_id=1, source_target_pairs={{0,12},{1,13},{2,14},{3,15},{4,8},{5,9},{6,10},{7,11},{8,4},{9,5},... | collective-permute-start | bytes 147464 | tf_op jit(solution)/shard_map/ppermute | solution.py:438
  73.1 2.0 %collective-permute-start.27 = (bf16[48,512]{1,0:T(8,128)(2,1)S(1)}, bf16[48,512]{1,0:T(8,128)(2,1)S(1)}, u32[]{:S(2)}, u32[]{:S(2)}) collective-permute-start(bf16[48,512]{1,0:T(8,128)(2,1)S(1)} %get-tuple-element.97), channel_id=1, source_target_pairs={{0,14},{1,15},{2,12},{3,13},{4,10},{5,11},{6,8},{7,9},{8,6},{9,7},... | collective-permute-start | bytes 147464 | tf_op jit(solution)/shard_map/ppermute | solution.py:438
  75.1 2.5 %collective-permute-start.29 = (bf16[48,512]{1,0:T(8,128)(2,1)S(1)}, bf16[48,512]{1,0:T(8,128)(2,1)S(1)}, u32[]{:S(2)}, u32[]{:S(2)}) collective-permute-start(bf16[48,512]{1,0:T(8,128)(2,1)S(1)} %get-tuple-element.99), channel_id=1, source_target_pairs={{0,10},{1,11},{2,8},{3,9},{4,14},{5,15},{6,12},{7,13},{8,2},{9,3},... | collective-permute-start | bytes 147464 | tf_op jit(solution)/shard_map/ppermute | solution.py:438
  78.4 2.5 %collective-permute-start.31 = (bf16[48,512]{1,0:T(8,128)(2,1)S(1)}, bf16[48,512]{1,0:T(8,128)(2,1)S(1)}, u32[]{:S(2)}, u32[]{:S(2)}) collective-permute-start(bf16[48,512]{1,0:T(8,128)(2,1)S(1)} %get-tuple-element.101), channel_id=1, source_target_pairs={{0,6},{1,7},{2,4},{3,5},{4,2},{5,3},{6,0},{7,1},{8,14},{9,15},{10,... | collective-permute-start | bytes 147464 | tf_op jit(solution)/shard_map/ppermute | solution.py:438
  81.1 2.1 %collective-permute-done.29.refs_3_ = bf16[48,512]{1,0:T(8,128)(2,1)S(1)} collective-permute-done((bf16[48,512]{1,0:T(8,128)(2,1)S(1)}, bf16[48,512]{1,0:T(8,128)(2,1)S(1)}, u32[]{:S(2)}, u32[]{:S(2)}) %collective-permute-start.29) | collective-permute-done | bytes 49184 | tf_op jit(solution)/shard_map/ppermute | solution.py:438
  (68 shorter events, 13.2 us)
Async XLA Ops:
  0.9 7.9 %collective-permute-start.2 = (bf16[1,2,18432]{2,1,0:T(2,128)(2,1)S(1)}, bf16[1,2,18432]{2,1,0:T(2,128)(2,1)S(1)}, u32[]{:S(2)}, u32[]{:S(2)}) collective-permute-start(bf16[1,2,18432]{2,1,0:T(2,128)(2,1)S(1)} %maximum_bitcast_fusion.refs_0_), channel_id=1, source_target_pairs={{0,12},{1,13},{2,14},{3,15},{4,8},{5,9},{6,10},{7,11},{8,4},{9,5},... | collective-permute-start | bytes 221192 | tf_op jit(solution)/shard_map/ppermute | solution.py:275
  6.0 6.2 %collective-permute-start.1 = (bf16[1,2,18432]{2,1,0:T(2,128)(2,1)S(1)}, bf16[1,2,18432]{2,1,0:T(2,128)(2,1)S(1)}, u32[]{:S(2)}, u32[]{:S(2)}) collective-permute-start(bf16[1,2,18432]{2,1,0:T(2,128)(2,1)S(1)} %maximum_bitcast_fusion.refs_0_), channel_id=1, source_target_pairs={{0,8},{1,9},{2,10},{3,11},{4,12},{5,13},{6,14},{7,15},{8,0},{9,1},... | collective-permute-start | bytes 221192 | tf_op jit(solution)/shard_map/ppermute | solution.py:275
  6.0 6.2 %collective-permute-start = (bf16[1,2,18432]{2,1,0:T(2,128)(2,1)S(1)}, bf16[1,2,18432]{2,1,0:T(2,128)(2,1)S(1)}, u32[]{:S(2)}, u32[]{:S(2)}) collective-permute-start(bf16[1,2,18432]{2,1,0:T(2,128)(2,1)S(1)} %maximum_bitcast_fusion.refs_0_), channel_id=1, source_target_pairs={{0,4},{1,5},{2,6},{3,7},{4,0},{5,1},{6,2},{7,3},{8,12},{9,13},{10,... | collective-permute-start | bytes 221192 | tf_op jit(solution)/shard_map/ppermute | solution.py:275
  13.9 13.9 %collective-permute-start.6 = (bf16[256,512]{1,0:T(8,128)(2,1)S(1)}, bf16[256,512]{1,0:T(8,128)(2,1)S(1)}, u32[]{:S(2)}, u32[]{:S(2)}) collective-permute-start(bf16[256,512]{1,0:T(8,128)(2,1)S(1)} %bitcast.3), channel_id=1, source_target_pairs={{0,1},{1,0},{2,3},{3,2},{4,5},{5,4},{6,7},{7,6},{8,9},{9,8},{10,11... | collective-permute-start | bytes 786440 | tf_op jit(solution)/shard_map/ppermute | solution.py:43
  13.9 13.9 %collective-permute-start.5 = (bf16[256,512]{1,0:T(8,128)(2,1)S(1)}, bf16[256,512]{1,0:T(8,128)(2,1)S(1)}, u32[]{:S(2)}, u32[]{:S(2)}) collective-permute-start(bf16[256,512]{1,0:T(8,128)(2,1)S(1)} %bitcast.4), channel_id=1, source_target_pairs={{0,2},{1,3},{4,0},{5,1},{8,4},{9,5},{12,8},{13,9},{14,12},{15,13},... | collective-permute-start | bytes 786440 | tf_op jit(solution)/shard_map/ppermute | solution.py:268
  14.4 13.4 %collective-permute-start.4 = (bf16[256,512]{1,0:T(8,128)(2,1)S(1)}, bf16[256,512]{1,0:T(8,128)(2,1)S(1)}, u32[]{:S(2)}, u32[]{:S(2)}) collective-permute-start(bf16[256,512]{1,0:T(8,128)(2,1)S(1)} %bitcast.5), channel_id=1, source_target_pairs={{0,4},{1,5},{4,8},{5,9},{8,12},{9,13},{12,14},{13,15},{14,10},{15,... | collective-permute-start | bytes 786440 | tf_op jit(solution)/shard_map/ppermute | solution.py:267
  15.9 11.8 %collective-permute-start.3 = (bf16[4,2,14336]{2,1,0:T(2,128)(2,1)S(1)}, bf16[4,2,14336]{2,1,0:T(2,128)(2,1)S(1)}, u32[]{:S(2)}, u32[]{:S(2)}) collective-permute-start(bf16[4,2,14336]{2,1,0:T(2,128)(2,1)S(1)} %get-tuple-element.61), channel_id=1, source_target_pairs={{0,2},{1,3},{2,0},{3,1},{4,6},{5,7},{6,4},{7,5},{8,10},{9,11},{10,... | collective-permute-start | bytes 688136 | tf_op jit(solution)/shard_map/ppermute | solution.py:290
  28.5 7.7 %collective-permute-start.9 = (bf16[16,14336]{1,0:T(8,128)(2,1)S(1)}, bf16[16,14336]{1,0:T(8,128)(2,1)S(1)}, u32[]{:S(2)}, u32[]{:S(2)}) collective-permute-start(bf16[16,14336]{1,0:T(8,128)(2,1)S(1)} %reshape.7.near_ref), channel_id=1, source_target_pairs={{0,1},{1,0},{2,3},{3,2},{4,5},{5,4},{6,7},{7,6},{8,9},{9,8},{10,11... | collective-permute-start | bytes 1376264 | tf_op jit(solution)/shard_map/ppermute | solution.py:43
  28.6 7.6 %collective-permute-start.10 = (bf16[256,512]{1,0:T(8,128)(2,1)S(1)}, bf16[256,512]{1,0:T(8,128)(2,1)S(1)}, u32[]{:S(2)}, u32[]{:S(2)}) collective-permute-start(bf16[256,512]{1,0:T(8,128)(2,1)S(1)} %collective-permute-done.4.refs_2_), channel_id=1, source_target_pairs={{0,1},{1,0},{2,3},{3,2},{4,5},{5,4},{6,7},{7,6},{8,9},{9,8},{10,11... | collective-permute-start | bytes 786440 | tf_op jit(solution)/shard_map/ppermute | solution.py:43
  29.1 7.1 %collective-permute-start.11 = (bf16[256,512]{1,0:T(8,128)(2,1)S(1)}, bf16[256,512]{1,0:T(8,128)(2,1)S(1)}, u32[]{:S(2)}, u32[]{:S(2)}) collective-permute-start(bf16[256,512]{1,0:T(8,128)(2,1)S(1)} %collective-permute-done.5.refs_4_), channel_id=1, source_target_pairs={{0,1},{1,0},{2,3},{3,2},{4,5},{5,4},{6,7},{7,6},{8,9},{9,8},{10,11... | collective-permute-start | bytes 786440 | tf_op jit(solution)/shard_map/ppermute | solution.py:43
  29.2 14.3 %collective-permute-start.12 = (bf16[256,512]{1,0:T(8,128)(2,1)S(1)}, bf16[256,512]{1,0:T(8,128)(2,1)S(1)}, u32[]{:S(2)}, u32[]{:S(2)}) collective-permute-start(bf16[256,512]{1,0:T(8,128)(2,1)S(1)} %collective-permute-done.4.refs_2_), channel_id=1, source_target_pairs={{0,4},{1,5},{4,8},{5,9},{8,12},{9,13},{12,14},{13,15},{14,10},{15,... | collective-permute-start | bytes 786440 | tf_op jit(solution)/shard_map/ppermute | solution.py:267
  29.2 14.3 %collective-permute-start.13 = (bf16[256,512]{1,0:T(8,128)(2,1)S(1)}, bf16[256,512]{1,0:T(8,128)(2,1)S(1)}, u32[]{:S(2)}, u32[]{:S(2)}) collective-permute-start(bf16[256,512]{1,0:T(8,128)(2,1)S(1)} %collective-permute-done.5.refs_4_), channel_id=1, source_target_pairs={{0,2},{1,3},{4,0},{5,1},{8,4},{9,5},{12,8},{13,9},{14,12},{15,13},... | collective-permute-start | bytes 786440 | tf_op jit(solution)/shard_map/ppermute | solution.py:268
  31.2 12.3 %all-to-all-start = ((bf16[8,32,256]{2,1,0:T(8,128)(2,1)}), bf16[8,32,256]{2,1,0:T(8,128)(2,1)S(1)}, u32[]{:S(2)}, u32[]{:S(2)}) async-start(bf16[8,32,256]{2,1,0:T(8,128)(2,1)} %rotate_in.1), calls=%async_computation | async-start | bytes 262144 | tf_op jit(solution)/shard_map/all_to_all | solution.py:48
  43.5 7.8 %collective-permute-start.17 = (bf16[256,512]{1,0:T(8,128)(2,1)S(1)}, bf16[256,512]{1,0:T(8,128)(2,1)S(1)}, u32[]{:S(2)}, u32[]{:S(2)}) collective-permute-start(bf16[256,512]{1,0:T(8,128)(2,1)S(1)} %collective-permute-done.12.refs_6_), channel_id=1, source_target_pairs={{0,1},{1,0},{2,3},{3,2},{4,5},{5,4},{6,7},{7,6},{8,9},{9,8},{10,11... | collective-permute-start | bytes 786440 | tf_op jit(solution)/shard_map/ppermute | solution.py:43
  43.5 8.7 %collective-permute-start.15 = (bf16[256,512]{1,0:T(8,128)(2,1)S(1)}, bf16[256,512]{1,0:T(8,128)(2,1)S(1)}, u32[]{:S(2)}, u32[]{:S(2)}) collective-permute-start(bf16[256,512]{1,0:T(8,128)(2,1)S(1)} %collective-permute-done.12.refs_6_), channel_id=1, source_target_pairs={{0,4},{1,5},{4,8},{5,9},{8,12},{9,13},{12,14},{13,15},{14,10},{15,... | collective-permute-start | bytes 786440 | tf_op jit(solution)/shard_map/ppermute | solution.py:267
  43.6 8.6 %collective-permute-start.18 = (bf16[256,512]{1,0:T(8,128)(2,1)S(1)}, bf16[256,512]{1,0:T(8,128)(2,1)S(1)}, u32[]{:S(2)}, u32[]{:S(2)}) collective-permute-start(bf16[256,512]{1,0:T(8,128)(2,1)S(1)} %collective-permute-done.13.refs_8_), channel_id=1, source_target_pairs={{0,1},{1,0},{2,3},{3,2},{4,5},{5,4},{6,7},{7,6},{8,9},{9,8},{10,11... | collective-permute-start | bytes 786440 | tf_op jit(solution)/shard_map/ppermute | solution.py:43
  44.0 8.3 %collective-permute-start.16 = (bf16[256,512]{1,0:T(8,128)(2,1)S(1)}, bf16[256,512]{1,0:T(8,128)(2,1)S(1)}, u32[]{:S(2)}, u32[]{:S(2)}) collective-permute-start(bf16[256,512]{1,0:T(8,128)(2,1)S(1)} %collective-permute-done.13.refs_8_), channel_id=1, source_target_pairs={{0,2},{1,3},{4,0},{5,1},{8,4},{9,5},{12,8},{13,9},{14,12},{15,13},... | collective-permute-start | bytes 786440 | tf_op jit(solution)/shard_map/ppermute | solution.py:268
  52.4 8.9 %collective-permute-start.21 = (bf16[256,512]{1,0:T(8,128)(2,1)S(1)}, bf16[256,512]{1,0:T(8,128)(2,1)S(1)}, u32[]{:S(2)}, u32[]{:S(2)}) collective-permute-start(bf16[256,512]{1,0:T(8,128)(2,1)S(1)} %collective-permute-done.15.refs_10_), channel_id=1, source_target_pairs={{0,1},{1,0},{2,3},{3,2},{4,5},{5,4},{6,7},{7,6},{8,9},{9,8},{10,11... | collective-permute-start | bytes 786440 | tf_op jit(solution)/shard_map/ppermute | solution.py:43
  52.4 8.9 %collective-permute-start.22 = (bf16[256,512]{1,0:T(8,128)(2,1)S(1)}, bf16[256,512]{1,0:T(8,128)(2,1)S(1)}, u32[]{:S(2)}, u32[]{:S(2)}) collective-permute-start(bf16[256,512]{1,0:T(8,128)(2,1)S(1)} %collective-permute-done.16.refs_12_), channel_id=1, source_target_pairs={{0,1},{1,0},{2,3},{3,2},{4,5},{5,4},{6,7},{7,6},{8,9},{9,8},{10,11... | collective-permute-start | bytes 786440 | tf_op jit(solution)/shard_map/ppermute | solution.py:43
  52.9 8.3 %collective-permute-start.20 = (bf16[128,512]{1,0:T(8,128)(2,1)S(1)}, bf16[128,512]{1,0:T(8,128)(2,1)S(1)}, u32[]{:S(2)}, u32[]{:S(2)}) collective-permute-start(bf16[128,512]{1,0:T(8,128)(2,1)S(1)} %slice.11), channel_id=1, source_target_pairs={{0,2},{1,3},{4,0},{5,1},{8,4},{9,5},{12,8},{13,9},{14,12},{15,13},... | collective-permute-start | bytes 393224 | tf_op jit(solution)/shard_map/ppermute | solution.py:268
  54.9 6.3 %collective-permute-start.19 = (bf16[128,512]{1,0:T(8,128)(2,1)S(1)}, bf16[128,512]{1,0:T(8,128)(2,1)S(1)}, u32[]{:S(2)}, u32[]{:S(2)}) collective-permute-start(bf16[128,512]{1,0:T(8,128)(2,1)S(1)} %slice.10), channel_id=1, source_target_pairs={{0,4},{1,5},{4,8},{5,9},{8,12},{9,13},{12,14},{13,15},{14,10},{15,... | collective-permute-start | bytes 393224 | tf_op jit(solution)/shard_map/ppermute | solution.py:267
  69.8 8.6 %collective-permute-start.26 = (bf16[48,512]{1,0:T(8,128)(2,1)S(1)}, bf16[48,512]{1,0:T(8,128)(2,1)S(1)}, u32[]{:S(2)}, u32[]{:S(2)}) collective-permute-start(bf16[48,512]{1,0:T(8,128)(2,1)S(1)} %get-tuple-element.96), channel_id=1, source_target_pairs={{0,12},{1,13},{2,14},{3,15},{4,8},{5,9},{6,10},{7,11},{8,4},{9,5},... | collective-permute-start | bytes 147464 | tf_op jit(solution)/shard_map/ppermute | solution.py:438
  73.1 7.8 %collective-permute-start.27 = (bf16[48,512]{1,0:T(8,128)(2,1)S(1)}, bf16[48,512]{1,0:T(8,128)(2,1)S(1)}, u32[]{:S(2)}, u32[]{:S(2)}) collective-permute-start(bf16[48,512]{1,0:T(8,128)(2,1)S(1)} %get-tuple-element.97), channel_id=1, source_target_pairs={{0,14},{1,15},{2,12},{3,13},{4,10},{5,11},{6,8},{7,9},{8,6},{9,7},... | collective-permute-start | bytes 147464 | tf_op jit(solution)/shard_map/ppermute | solution.py:438
  75.1 8.1 %collective-permute-start.29 = (bf16[48,512]{1,0:T(8,128)(2,1)S(1)}, bf16[48,512]{1,0:T(8,128)(2,1)S(1)}, u32[]{:S(2)}, u32[]{:S(2)}) collective-permute-start(bf16[48,512]{1,0:T(8,128)(2,1)S(1)} %get-tuple-element.99), channel_id=1, source_target_pairs={{0,10},{1,11},{2,8},{3,9},{4,14},{5,15},{6,12},{7,13},{8,2},{9,3},... | collective-permute-start | bytes 147464 | tf_op jit(solution)/shard_map/ppermute | solution.py:438
  (13 other events, 69.3 us)

commit v13 on v12

--- a/solution.py
+++ b/solution.py
@@ -41,11 +41,6 @@
 
 def swap(x, n):
     return lax.ppermute(x, "blk", xor_pairs(n, 1))
-
-
-def exchange(x, n, stride):
-    groups = [list(range(first, n, stride)) for first in range(stride)]
-    return lax.all_to_all(x, "blk", 0, 0, axis_index_groups=groups, tiled=True)
 
 
 def bits_of(size):
@@ -76,38 +71,69 @@
 
 
 def rotate_in_kernel(tok_rows, near_ref, far_ref, basis_ref, out_ref):
-    tokens = out_ref.shape[1]
-    acts = jnp.concatenate([near_ref[...], far_ref[...]], axis=0)
+    tokens = out_ref.shape[0]
+    depth = near_ref.shape[2]
+    acts = jnp.concatenate([ref[...].reshape(-1, depth) for ref in (near_ref, far_ref)], axis=0)
     rotated = jnp.dot(acts, basis_ref[...], preferred_element_type=jnp.float32)
     wanted = lax.broadcasted_iota(jnp.int32, (tokens, tokens), 0)
     held = held_tokens(lax.axis_index("blk"), tokens, tok_rows)
-    ordered = reorder(wanted, held, rotated).astype(jnp.bfloat16)
-    for copy in range(out_ref.shape[0]):
-        out_ref[copy] = ordered
-
-
-def rotate_part(first, near_ref, far_ref, basis_ref, basis, total, sem):
+    out_ref[...] = reorder(wanted, held, rotated).astype(jnp.bfloat16)
+
+
+def stack_kernel(first_ref, last_ref, out_ref):
+    half = first_ref.shape[0]
+    out_ref[:half] = first_ref[...]
+    out_ref[half:] = last_ref[...]
+
+
+def hold_kernel(basis_ref, held_ref, sem):
+    steps, depth = held_ref.shape[:2]
+    copies = [
+        pltpu.make_async_copy(
+            basis_ref.at[pl.ds(step * depth, depth)], held_ref.at[step], sem.at[step]
+        )
+        for step in range(steps)
+    ]
+    for copy in copies:
+        copy.start()
+    for copy in copies:
+        copy.wait()
+
+
+def rotate_part(first, near_ref, far_ref, held_ref, basis_ref, basis, total, sem):
     steps, depth = basis.shape[:2]
+    held = 0 if held_ref is None else held_ref.shape[0]
 
     def copy_of(step):
-        rows = pl.ds(pl.multiple_of((first + step) * depth, depth), depth)
+        rows = pl.ds(pl.multiple_of((first + held + step) * depth, depth), depth)
         return pltpu.make_async_copy(basis_ref.at[rows], basis.at[step], sem.at[step])
+
+    def grads_of(step):
+        columns = pl.ds(pl.multiple_of((first + step) * depth, depth), depth)
+        rows = [ref[:, :, columns].reshape(-1, depth) for ref in (near_ref, far_ref)]
+        return jnp.concatenate(rows, axis=0)
 
     @pl.loop(0, steps)
     def _(step):
         copy_of(step).start()
 
+    if held:
+
+        @pl.loop(0, held)
+        def _(step):
+            part = jnp.dot(grads_of(step), held_ref[step], preferred_element_type=jnp.float32)
+            total[...] += part
+
     @pl.loop(0, steps)
     def _(step):
-        columns = pl.ds(pl.multiple_of((first + step) * depth, depth), depth)
-        grads = jnp.concatenate([near_ref[:, columns], far_ref[:, columns]], axis=0)
+        grads = grads_of(held + step)
         copy_of(step).wait()
         total[...] += jnp.dot(grads, basis[step], preferred_element_type=jnp.float32)
 
 
-def rotate_first_kernel(near_ref, far_ref, basis_ref, out_ref, basis, sem):
+def rotate_first_kernel(near_ref, far_ref, held_ref, basis_ref, out_ref, basis, sem):
     out_ref[...] = jnp.zeros_like(out_ref)
-    rotate_part(0, near_ref, far_ref, basis_ref, basis, out_ref, sem)
+    rotate_part(0, near_ref, far_ref, held_ref, basis_ref, basis, out_ref, sem)
 
 
 def rotate_last_kernel(
@@ -128,7 +154,7 @@
     map_copy = pltpu.make_async_copy(map_ref, stored_map, sem.at[basis.shape[0]])
     map_copy.start()
     total[...] = start_ref[...]
-    rotate_part(first, near_ref, far_ref, basis_ref, basis, total, sem)
+    rotate_part(first, near_ref, far_ref, None, basis_ref, basis, total, sem)
     map_copy.wait()
     row = lax.broadcasted_iota(jnp.int32, (tokens, tokens), 0)
     block = row >> bits_of(tok_rows)
@@ -141,10 +167,12 @@
 
 
 def scale_kernel(
-    begun, aligned_ref, near_ref, far_ref, tiles_ref, eigen_ref, out_ref, damped, tiles, sem
+    begun, aligned_ref, *refs
 ):
+    rotated_refs, (tiles_ref, eigen_ref, out_ref, damped, tiles, sem) = refs[:4], refs[4:]
     blocks, depth = damped.shape[:2]
-    chips, _, width = near_ref.shape
+    pairs, _, width = rotated_refs[0].shape
+    chips = 2 * pairs
 
     def copy_of(block):
         rows = pl.ds(pl.multiple_of(block * depth, depth), depth)
@@ -167,11 +195,12 @@
         copy_of(block).wait()
         place = 0
         for steps in begun:
-            for other, rotated_ref in enumerate((near_ref, far_ref)):
+            for other in range(2):
                 source = ring_source(me, steps, other, chips)
-                grad = jnp.dot(
-                    aligned, rotated_ref[source // 2], preferred_element_type=jnp.float32
-                )
+                key = (source ^ me) // 2
+                same, paired = (ref[key // 2] for ref in rotated_refs[2 * other : 2 * other + 2])
+                rotated = jnp.where(lax.rem(key, 2) == 0, same, paired)
+                grad = jnp.dot(aligned, rotated, preferred_element_type=jnp.float32)
                 for first in range(0, width, LANES):
                     tile = tiles[(source * width + first) // LANES]
                     lanes = pl.ds(pl.multiple_of(tile * LANES, LANES), LANES)
@@ -273,7 +302,19 @@
     pairs = chips // 2
     both = jnp.concatenate([grad_out, activations], axis=1)[None]
     got = [lax.ppermute(both, "blk", xor_pairs(n, 4 * key)) for key in range(1, pairs)]
-    both, own, *got = after(both, own, *got)
+    depth, ahead, later = 1024, 4, 5
+    held = pl.pallas_call(
+        hold_kernel,
+        out_shape=jax.ShapeDtypeStruct((ahead, depth, tile_width), jnp.bfloat16),
+        in_specs=[ANY],
+        out_specs=VMEM,
+        scratch_shapes=[pltpu.SemaphoreType.DMA((ahead,))],
+        compiler_params=pltpu.CompilerParams(vmem_limit_bytes=40 * MIB),
+        cost_estimate=CHEAP,
+        name="hold",
+    )(basis_out)
+
+    both, own, held, *got = after(both, own, held, *got)
     grads, acts = pl.pallas_call(
         part_kernel,
         out_shape=(
@@ -290,37 +331,48 @@
     grads_got = lax.ppermute(grads, "blk", xor_pairs(n, 2))
     right, left = [own, to_right(own)], [own, to_left(own)]
 
-    acts = jnp.concatenate([acts, acts_got], axis=0).reshape(tokens // 2, full_in)
+    acts = jnp.concatenate([acts, acts_got], axis=0)
     rotated = pl.pallas_call(
         functools.partial(rotate_in_kernel, tok_rows),
-        out_shape=jax.ShapeDtypeStruct((chips, tokens, in_width), jnp.bfloat16),
+        out_shape=jax.ShapeDtypeStruct((tokens, in_width), jnp.bfloat16),
         in_specs=[VMEM, VMEM, VMEM],
         out_specs=VMEM,
         compiler_params=pltpu.CompilerParams(vmem_limit_bytes=8 * MIB),
         cost_estimate=CHEAP,
         name="rotate_in",
     )(acts, swap(acts, n), basis_in)
-    own_far = swap(own, n)
-    grads_got, right[-1], left[-1], own_far, _ = after(
-        grads_got, right[-1], left[-1], own_far, rotated
-    )
-    rotated = exchange(rotated, n, 2)
+
+    def doubled(x, key):
+        return pl.pallas_call(
+            stack_kernel,
+            out_shape=jax.ShapeDtypeStruct((2 * x.shape[0], *x.shape[1:]), x.dtype),
+            in_specs=[VMEM, VMEM],
+            out_specs=VMEM,
+            compiler_params=pltpu.CompilerParams(vmem_limit_bytes=8 * MIB),
+            cost_estimate=CHEAP,
+            name="stack",
+        )(x, lax.ppermute(x, "blk", xor_pairs(n, key)))
+
+    rotated = doubled(rotated[None], 4)
+    grads_got, rotated, right[-1], left[-1] = after(grads_got, rotated, right[-1], left[-1])
+    key = 8
+    while key < n:
+        rotated = doubled(rotated, key)
+        key *= 2
     near = [right[0], right[1], left[1]]
     while len(right) < steps - 1:
         right.append(to_right(right[-1]))
         left.append(to_left(left[-1]))
-    grads = jnp.concatenate([grads, grads_got], axis=0).reshape(tokens // 2, full_out)
+    grads = jnp.concatenate([grads, grads_got], axis=0)
     grads_far = swap(grads, n)
-    far = [swap(piece, n) for piece in near[1:]]
-    grads, grads_far, *far = after(grads, grads_far, *far)
-    far = [own_far, *far]
-
-    depth = 1024
-    cuts = (0, full_out // depth // 2, full_out // depth)
+    far = [swap(piece, n) for piece in near]
+    grads, grads_far, rotated, *far = after(grads, grads_far, rotated, *far)
+    rotated = [rotated, lax.ppermute(rotated, "blk", xor_pairs(n, 2))]
+
     rotate = lambda kernel, count, scratch, shape, dtype, *operands: pl.pallas_call(
         kernel,
         out_shape=jax.ShapeDtypeStruct(shape, dtype),
-        in_specs=[VMEM, VMEM, ANY, ANY, VMEM][: len(operands)],
+        in_specs=[ANY if x is basis_out or x is block_map else VMEM for x in operands],
         out_specs=VMEM,
         scratch_shapes=[pltpu.VMEM((count, depth, tile_width), jnp.bfloat16)]
         + scratch
@@ -331,25 +383,26 @@
     )(*operands)
     start = rotate(
         functools.partial(rotate_first_kernel),
-        cuts[1],
+        full_out // depth - ahead - later,
         [],
         (tokens, tile_width),
         jnp.float32,
         grads,
         grads_far,
+        held,
         basis_out,
     )
-    start, grads, rotated, right[-1], left[-1] = after(
-        start, grads, rotated, right[-1], left[-1]
-    )
-    rotated_far = swap(rotated, n)
+    start, grads, right[-1], left[-1], *rotated = after(
+        start, grads, right[-1], left[-1], *rotated
+    )
+    rotated += [swap(x, n) for x in rotated]
     near += [right[-1], left[-1]]
     far += [swap(right[-1], n), swap(left[-1], n)]
     right.append(to_right(right[-1]))
     left.append(to_left(left[-1]))
     aligned = rotate(
-        functools.partial(rotate_last_kernel, tok_rows, cuts[1]),
-        cuts[2] - cuts[1],
+        functools.partial(rotate_last_kernel, tok_rows, full_out // depth - later),
+        later,
         [
             pltpu.VMEM((tokens, tile_width), jnp.float32),
             pltpu.SMEM(block_map.shape, jnp.int32),
@@ -363,9 +416,8 @@
         start,
     )
 
-    aligned, rotated_far, right[-1], left[-1], *far = after(
-        aligned, rotated_far, right[-1], left[-1], *far
-    )
+    aligned, right[-1], left[-1], *both = after(aligned, right[-1], left[-1], *rotated, *far)
+    rotated, far = both[:4], both[4:]
     cut = in_width // 2
     last = [to_right(right[-1][:cut]), to_left(left[-1][cut:])]
     near += [right[-1], left[-1]]
@@ -375,7 +427,7 @@
     scaled = pl.pallas_call(
         functools.partial(scale_kernel, begun),
         out_shape=jax.ShapeDtypeStruct((tile_width, full_in), jnp.bfloat16),
-        in_specs=[VMEM, VMEM, VMEM, ANY, ANY],
+        in_specs=[VMEM] * 5 + [ANY] * 2,
         out_specs=VMEM,
         scratch_shapes=[
             pltpu.VMEM((blocks, tile_width // blocks, full_in), jnp.float32),
@@ -385,7 +437,7 @@
         compiler_params=pltpu.CompilerParams(vmem_limit_bytes=40 * MIB),
         cost_estimate=CHEAP,
         name="scale",
-    )(aligned, rotated, rotated_far, tile_order, eigenvalues)
+    )(aligned, *rotated, tile_order, eigenvalues)
 
     scaled, *last = after(scaled, *last, *far[-2:])
     far[-2:] = last[2:]

time: 86.1 us -> 91 us (1.057)
  local copies, waits for them, and re-layouts: 2.95 us -> 6.6 us
  starting transfers between devices: 34.4 us -> 35.6 us
  Pallas kernels: 25.1 us -> 26.1 us
    ppermute x0 -> x3, waiting for transfers between devices: none -> 5.09 us  [the longest x2 5.09 us: doubled(): lax.ppermute(x, 'blk', xor_pairs(n, key))]
    all_to_all x1 -> x0, starting transfers between devices: 4.95 us -> none  [exchange(): return lax.all_to_all(x, 'blk', 0, 0, axis_index_groups=groups, tiled=True)]
    unnamed x7 -> x13, local copies, waits for them, and re-layouts: 1.74 us -> 6.33 us
    ppermute x3, waiting for transfers between devices: 4.46 us -> 0.01 us  [ring_body(): lax.ppermute(both, 'blk', xor_pairs(n, 4 * key))]
    ppermute x4, starting transfers between devices: 1.69 us -> 4.91 us  [ring_body(): to_right = lambda x: lax.ppermute(x, 'blk', shift_pairs(n, 1))]
    pallas_call x0 -> x3, Pallas kernels: none -> 3.19 us  [the longest x1 3.18 us: ring_body(): pl.pallas_call(hold_kernel, out_shape=jax.ShapeDtypeStruct((ahead, depth,...]
    ppermute x0 -> x3, starting transfers between devices: none -> 3.14 us  [the longest x1 1.89 us: ring_body(): rotated = [rotated, lax.ppermute(rotated, 'blk', xor_pairs(n, 2))]]
    ppermute x1, waiting for transfers between devices: 0.21 us -> 2.55 us  [ring_body(): acts_got = lax.ppermute(acts, 'blk', xor_pairs(n, 2))]
  transfers between devices with their start and end apart: 34 -> 37, of which waited for: 12 -> 12; matrix products, arithmetic and copies ran while one was open for 2% -> 1% of each run, Pallas kernels for 26% -> 26%
where the time goes in v13:
time: 91 us; the launch traced here: 90.7 us
  starting transfers between devices  35.6 us (39%)
  Pallas kernels  26.1 us (29%)
  waiting for transfers between devices  21.2 us (23%)
  local copies, waits for them, and re-layouts  6.6 us (7%)
  other arithmetic  0.91 us (1%)
    ppermute x7, starting transfers between devices, ring_body(): lax.ppermute(x, 'blk', xor_pairs(n, 2 * key))  11.2 us
    pallas_call x2, Pallas kernels, ring_body(): pl.pallas_call(kernel, out_shape=jax.ShapeDtypeStruct(shape, dtype), in_s...  8.59 us
    pallas_call x1, Pallas kernels, ring_body(): pl.pallas_call(functools.partial(scale_kernel, begun), out_shape=jax.Shap...  6.9 us
    unnamed x13, local copies, waits for them, and re-layouts  6.33 us
    ppermute x1, waiting for transfers between devices, ring_body(): grads_got = lax.ppermute(grads, 'blk', xor_pairs(n, 2))  5.94 us
    ppermute x3, starting transfers between devices, ring_body(): lax.ppermute(both, 'blk', xor_pairs(n, 4 * key))  5.76 us
    ppermute x2, waiting for transfers between devices, doubled(): lax.ppermute(x, 'blk', xor_pairs(n, key))  5.09 us
    ppermute x4, starting transfers between devices, ring_body(): to_right = lambda x: lax.ppermute(x, 'blk', shift_pairs(n, 1))  4.91 us
  transfers between devices with their start and end apart: 37, of which 12 were waited for; matrix products, arithmetic and copies ran while one was open for 1% of the time, Pallas kernels for 26%

profile of v13, /device:TPU:0, one launch (start us, length us, event | category | flops | bytes accessed | tf_op | source)
XLA Modules:
  0.0 90.7 jit_solution(1576305888031515808)
XLA Ops:
  0.9 5.1 %collective-permute-start.2 = (bf16[1,2,18432]{2,1,0:T(2,128)(2,1)S(1)}, bf16[1,2,18432]{2,1,0:T(2,128)(2,1)S(1)}, u32[]{:S(2)}, u32[]{:S(2)}) collective-permute-start(bf16[1,2,18432]{2,1,0:T(2,128)(2,1)S(1)} %maximum_bitcast_fusion.refs_0_), channel_id=1, source_target_pairs={{0,12},{1,13},{2,14},{3,15},{4,8},{5,9},{6,10},{7,11},{8,4},{9,5},... | collective-permute-start | bytes 221192 | tf_op jit(solution)/shard_map/ppermute | solution.py:304
  6.7 3.2 %hold.1.held_ref = bf16[4,1024,896]{2,1,0:T(8,128)(2,1)S(1)} custom-call(bf16[14336,896]{1,0:T(8,128)(2,1)} %basis_out_ref.1), custom_call_target="tpu_custom_call" | custom-call | flops 1 | bytes 1 | tf_op jit(solution)/shard_map/hold/pallas_call | solution.py:306
  9.9 2.9 %copy-done = bf16[4,1024,896]{2,1,0:T(8,128)(2,1)} copy-done((bf16[4,1024,896]{2,1,0:T(8,128)(2,1)}, bf16[4,1024,896]{2,1,0:T(8,128)(2,1)S(1)}, u32[]{:S(2)}) %copy-start) | copy-done | bytes 7340056
  13.0 1.7 %collective-permute-start.4 = (bf16[4,2,4096]{2,1,0:T(2,128)(2,1)S(1)}, bf16[4,2,4096]{2,1,0:T(2,128)(2,1)S(1)}, u32[]{:S(2)}, u32[]{:S(2)}) collective-permute-start(bf16[4,2,4096]{2,1,0:T(2,128)(2,1)S(1)} %get-tuple-element.69), channel_id=1, source_target_pairs={{0,2},{1,3},{2,0},{3,1},{4,6},{5,7},{6,4},{7,5},{8,10},{9,11},{10,... | collective-permute-start | bytes 196616 | tf_op jit(solution)/shard_map/ppermute | solution.py:330
  14.8 2.6 %collective-permute-done.4 = bf16[4,2,4096]{2,1,0:T(2,128)(2,1)S(1)} collective-permute-done((bf16[4,2,4096]{2,1,0:T(2,128)(2,1)S(1)}, bf16[4,2,4096]{2,1,0:T(2,128)(2,1)S(1)}, u32[]{:S(2)}, u32[]{:S(2)}) %collective-permute-start.4) | collective-permute-done | bytes 65568 | tf_op jit(solution)/shard_map/ppermute | solution.py:330
  18.0 1.7 %collective-permute-start.8 = (bf16[256,512]{1,0:T(8,128)(2,1)S(1)}, bf16[256,512]{1,0:T(8,128)(2,1)S(1)}, u32[]{:S(2)}, u32[]{:S(2)}) collective-permute-start(bf16[256,512]{1,0:T(8,128)(2,1)S(1)} %bitcast.5), channel_id=1, source_target_pairs={{0,2},{1,3},{4,0},{5,1},{8,4},{9,5},{12,8},{13,9},{14,12},{15,13},... | collective-permute-start | bytes 786440 | tf_op jit(solution)/shard_map/ppermute | solution.py:297
  20.0 1.7 %collective-permute-start.3 = (bf16[4,2,14336]{2,1,0:T(2,128)(2,1)S(1)}, bf16[4,2,14336]{2,1,0:T(2,128)(2,1)S(1)}, u32[]{:S(2)}, u32[]{:S(2)}) collective-permute-start(bf16[4,2,14336]{2,1,0:T(2,128)(2,1)S(1)} %get-tuple-element.68), channel_id=1, source_target_pairs={{0,2},{1,3},{2,0},{3,1},{4,6},{5,7},{6,4},{7,5},{8,10},{9,11},{10,... | collective-permute-start | bytes 688136 | tf_op jit(solution)/shard_map/ppermute | solution.py:331
  23.6 3.0 %collective-permute-done.6.last_ref = bf16[1,32,256]{2,1,0:T(8,128)(2,1)S(1)} collective-permute-done((bf16[1,32,256]{2,1,0:T(8,128)(2,1)S(1)}, bf16[1,32,256]{2,1,0:T(8,128)(2,1)S(1)}, u32[]{:S(2)}, u32[]{:S(2)}) %collective-permute-start.6) | collective-permute-done | bytes 16416 | tf_op jit(solution)/shard_map/ppermute | solution.py:354
  26.6 5.9 %collective-permute-done.3 = bf16[4,2,14336]{2,1,0:T(2,128)(2,1)S(1)} collective-permute-done((bf16[4,2,14336]{2,1,0:T(2,128)(2,1)S(1)}, bf16[4,2,14336]{2,1,0:T(2,128)(2,1)S(1)}, u32[]{:S(2)}, u32[]{:S(2)}) %collective-permute-start.3) | collective-permute-done | bytes 229408 | tf_op jit(solution)/shard_map/ppermute | solution.py:331
  33.4 2.9 %collective-permute-start.14 = (bf16[256,512]{1,0:T(8,128)(2,1)S(1)}, bf16[256,512]{1,0:T(8,128)(2,1)S(1)}, u32[]{:S(2)}, u32[]{:S(2)}) collective-permute-start(bf16[256,512]{1,0:T(8,128)(2,1)S(1)} %collective-permute-done.7.refs_2_), channel_id=1, source_target_pairs={{0,4},{1,5},{4,8},{5,9},{8,12},{9,13},{12,14},{13,15},{14,10},{15,... | collective-permute-start | bytes 786440 | tf_op jit(solution)/shard_map/ppermute | solution.py:296
  36.3 2.1 %collective-permute-done.10.last_ref = bf16[2,32,256]{2,1,0:T(8,128)(2,1)S(1)} collective-permute-done((bf16[2,32,256]{2,1,0:T(8,128)(2,1)S(1)}, bf16[2,32,256]{2,1,0:T(8,128)(2,1)S(1)}, u32[]{:S(2)}, u32[]{:S(2)}) %collective-permute-start.10) | collective-permute-done | bytes 32800 | tf_op jit(solution)/shard_map/ppermute | solution.py:354
  38.5 1.9 %collective-permute-start.16 = (bf16[4,32,256]{2,1,0:T(8,128)(2,1)S(1)}, bf16[4,32,256]{2,1,0:T(8,128)(2,1)S(1)}, u32[]{:S(2)}, u32[]{:S(2)}) collective-permute-start(bf16[4,32,256]{2,1,0:T(8,128)(2,1)S(1)} %stack.3.refs_0_), channel_id=1, source_target_pairs={{0,2},{1,3},{2,0},{3,1},{4,6},{5,7},{6,4},{7,5},{8,10},{9,11},{10,... | collective-permute-start | bytes 196616 | tf_op jit(solution)/shard_map/ppermute | solution.py:370
  40.4 3.1 %copy-done.1 = bf16[4,1024,896]{2,1,0:T(8,128)(2,1)S(1)} copy-done((bf16[4,1024,896]{2,1,0:T(8,128)(2,1)S(1)}, bf16[4,1024,896]{2,1,0:T(8,128)(2,1)}, u32[]{:S(2)}) %copy-start.1) | copy-done | bytes 7340056
  43.5 4.2 %rotate_first.1.start_ref = f32[32,896]{1,0:T(8,128)S(1)} custom-call(bf16[8,2,14336]{2,1,0:T(2,128)(2,1)S(1)} %constant_dynamic-update-slice_fusion.2.near_ref, bf16[8,2,14336]{2,1,0:T(2,128)(2,1)S(1)} %collective-permute-done.9.far_ref, bf16[4,1024,896]{2,1,0:T(8,128)(2,1)S(1)} %copy-done.1, bf16[14336,896]{1,0:T(8,128)(2,1)} %basis_out_ref.1), custom_call_target="tpu_custom_call" | custom-call | flops 1 | bytes 1 | tf_op jit(solution)/shard_map/rotate_first/pallas_call | solution.py:372
  48.3 1.7 %collective-permute-start.18 = (bf16[256,512]{1,0:T(8,128)(2,1)S(1)}, bf16[256,512]{1,0:T(8,128)(2,1)S(1)}, u32[]{:S(2)}, u32[]{:S(2)}) collective-permute-start(bf16[256,512]{1,0:T(8,128)(2,1)S(1)} %collective-permute-done.15.refs_8_), channel_id=1, source_target_pairs={{0,2},{1,3},{4,0},{5,1},{8,4},{9,5},{12,8},{13,9},{14,12},{15,13},... | collective-permute-start | bytes 786440 | tf_op jit(solution)/shard_map/ppermute | solution.py:297
  51.4 4.4 %rotate_last.1.aligned_ref = bf16[896,32]{1,0:T(8,128)(2,1)S(1)} custom-call(bf16[8,2,14336]{2,1,0:T(2,128)(2,1)S(1)} %constant_dynamic-update-slice_fusion.2.near_ref, bf16[8,2,14336]{2,1,0:T(2,128)(2,1)S(1)} %collective-permute-done.9.far_ref, bf16[14336,896]{1,0:T(8,128)(2,1)} %basis_out_ref.1, s32[16]{0:T(128)S(1)} %copy-done.4, ...), custom_call_target="tpu_custom_call" | custom-call | flops 1 | bytes 1 | tf_op jit(solution)/shard_map/rotate_last/pallas_call | solution.py:372
  56.5 1.5 %collective-permute-done.18.refs_12_ = bf16[256,512]{1,0:T(8,128)(2,1)S(1)} collective-permute-done((bf16[256,512]{1,0:T(8,128)(2,1)S(1)}, bf16[256,512]{1,0:T(8,128)(2,1)S(1)}, u32[]{:S(2)}, u32[]{:S(2)}) %collective-permute-start.18) | collective-permute-done | bytes 262176 | tf_op jit(solution)/shard_map/ppermute | solution.py:297
  60.6 6.9 %scale.1.scaled_ref = bf16[896,4096]{1,0:T(8,128)(2,1)S(1)} custom-call(bf16[896,32]{1,0:T(8,128)(2,1)S(1)} %rotate_last.1.aligned_ref, bf16[4,32,256]{2,1,0:T(8,128)(2,1)S(1)} %stack.3.refs_0_, bf16[4,32,256]{2,1,0:T(8,128)(2,1)S(1)} %collective-permute-done.16.refs_1_, bf16[4,32,256]{2,1,0:T(8,128)(2,1)S(1)} %collective-permute-done.19.refs_2_, ...), custom_call_target="tpu_custom_call" | custom-call | flops 1 | bytes 1 | tf_op jit(solution)/shard_map/scale/pallas_call | solution.py:427
  68.1 4.5 %project.1 = (f32[896,512]{1,0:T(8,128)S(1)}, bf16[768,896]{1,0:T(8,128)(2,1)S(1)}) custom-call(bf16[896,4096]{1,0:T(8,128)(2,1)S(1)} %scale.1.scaled_ref, bf16[14336,896]{1,0:T(8,128)(2,1)} %basis_out_ref.1, bf16[256,512]{1,0:T(8,128)(2,1)S(1)} %bitcast.7, bf16[256,512]{1,0:T(8,128)(2,1)S(1)} %collective-permute-done.11.refs_1_, ...), custom_call_target="tpu_custom_call" | custom-call | flops 1 | bytes 1 | tf_op jit(solution)/shard_map/project/pallas_call | solution.py:447
  72.6 1.6 %window.1 = (bf16[8,48,512]{2,1,0:T(8,128)(2,1)S(1)}, f32[8,48,512]{2,1,0:T(8,128)S(1)}) custom-call(bf16[768,896]{1,0:T(8,128)(2,1)S(1)} %get-tuple-element.103.window_ref, bf16[896,4096]{1,0:T(8,128)(2,1)S(1)} %scale.1.scaled_ref, f32[896,512]{1,0:T(8,128)S(1)} %get-tuple-element.104.projected_ref, bf16[128,512]{1,0:T(8,128)(2,1)S(1)} %collective-permute-done.23.refs_0_, ...), custom_call_target="tpu_custom_call" | custom-call | flops 1 | bytes 1 | tf_op jit(solution)/shard_map/window/pallas_call | solution.py:465
  74.4 1.6 %collective-permute-done.29.got_ref = bf16[8,48,512]{2,1,0:T(8,128)(2,1)S(1)} collective-permute-done((bf16[8,48,512]{2,1,0:T(8,128)(2,1)S(1)}, bf16[8,48,512]{2,1,0:T(8,128)(2,1)S(1)}, u32[]{:S(2)}, u32[]{:S(2)}) %collective-permute-start.29) | collective-permute-done | bytes 393248 | tf_op jit(solution)/shard_map/ppermute | solution.py:43
  77.4 2.6 %collective-permute-start.31 = (bf16[48,512]{1,0:T(8,128)(2,1)S(1)}, bf16[48,512]{1,0:T(8,128)(2,1)S(1)}, u32[]{:S(2)}, u32[]{:S(2)}) collective-permute-start(bf16[48,512]{1,0:T(8,128)(2,1)S(1)} %get-tuple-element.111), channel_id=1, source_target_pairs={{0,14},{1,15},{2,12},{3,13},{4,10},{5,11},{6,8},{7,9},{8,6},{9,7},... | collective-permute-start | bytes 147464 | tf_op jit(solution)/shard_map/ppermute | solution.py:490
  80.1 3.8 %collective-permute-start.33 = (bf16[48,512]{1,0:T(8,128)(2,1)S(1)}, bf16[48,512]{1,0:T(8,128)(2,1)S(1)}, u32[]{:S(2)}, u32[]{:S(2)}) collective-permute-start(bf16[48,512]{1,0:T(8,128)(2,1)S(1)} %get-tuple-element.113), channel_id=1, source_target_pairs={{0,10},{1,11},{2,8},{3,9},{4,14},{5,15},{6,12},{7,13},{8,2},{9,3},... | collective-permute-start | bytes 147464 | tf_op jit(solution)/shard_map/ppermute | solution.py:490
  83.8 2.1 %collective-permute-start.35 = (bf16[48,512]{1,0:T(8,128)(2,1)S(1)}, bf16[48,512]{1,0:T(8,128)(2,1)S(1)}, u32[]{:S(2)}, u32[]{:S(2)}) collective-permute-start(bf16[48,512]{1,0:T(8,128)(2,1)S(1)} %get-tuple-element.115), channel_id=1, source_target_pairs={{0,6},{1,7},{2,4},{3,5},{4,2},{5,3},{6,0},{7,1},{8,14},{9,15},{10,... | collective-permute-start | bytes 147464 | tf_op jit(solution)/shard_map/ppermute | solution.py:490
  (82 shorter events, 17.8 us)
Async XLA Ops:
  0.9 12.0 %collective-permute-start.2 = (bf16[1,2,18432]{2,1,0:T(2,128)(2,1)S(1)}, bf16[1,2,18432]{2,1,0:T(2,128)(2,1)S(1)}, u32[]{:S(2)}, u32[]{:S(2)}) collective-permute-start(bf16[1,2,18432]{2,1,0:T(2,128)(2,1)S(1)} %maximum_bitcast_fusion.refs_0_), channel_id=1, source_target_pairs={{0,12},{1,13},{2,14},{3,15},{4,8},{5,9},{6,10},{7,11},{8,4},{9,5},... | collective-permute-start | bytes 221192 | tf_op jit(solution)/shard_map/ppermute | solution.py:304
  6.0 6.9 %collective-permute-start.1 = (bf16[1,2,18432]{2,1,0:T(2,128)(2,1)S(1)}, bf16[1,2,18432]{2,1,0:T(2,128)(2,1)S(1)}, u32[]{:S(2)}, u32[]{:S(2)}) collective-permute-start(bf16[1,2,18432]{2,1,0:T(2,128)(2,1)S(1)} %maximum_bitcast_fusion.refs_0_), channel_id=1, source_target_pairs={{0,8},{1,9},{2,10},{3,11},{4,12},{5,13},{6,14},{7,15},{8,0},{9,1},... | collective-permute-start | bytes 221192 | tf_op jit(solution)/shard_map/ppermute | solution.py:304
  6.0 6.9 %collective-permute-start = (bf16[1,2,18432]{2,1,0:T(2,128)(2,1)S(1)}, bf16[1,2,18432]{2,1,0:T(2,128)(2,1)S(1)}, u32[]{:S(2)}, u32[]{:S(2)}) collective-permute-start(bf16[1,2,18432]{2,1,0:T(2,128)(2,1)S(1)} %maximum_bitcast_fusion.refs_0_), channel_id=1, source_target_pairs={{0,4},{1,5},{2,6},{3,7},{4,0},{5,1},{6,2},{7,3},{8,12},{9,13},{10,... | collective-permute-start | bytes 221192 | tf_op jit(solution)/shard_map/ppermute | solution.py:304
  17.5 15.9 %collective-permute-start.11 = (bf16[256,512]{1,0:T(8,128)(2,1)S(1)}, bf16[256,512]{1,0:T(8,128)(2,1)S(1)}, u32[]{:S(2)}, u32[]{:S(2)}) collective-permute-start(bf16[256,512]{1,0:T(8,128)(2,1)S(1)} %bitcast.4), channel_id=1, source_target_pairs={{0,1},{1,0},{2,3},{3,2},{4,5},{5,4},{6,7},{7,6},{8,9},{9,8},{10,11... | collective-permute-start | bytes 786440 | tf_op jit(solution)/shard_map/ppermute | solution.py:43
  18.0 14.6 %collective-permute-start.8 = (bf16[256,512]{1,0:T(8,128)(2,1)S(1)}, bf16[256,512]{1,0:T(8,128)(2,1)S(1)}, u32[]{:S(2)}, u32[]{:S(2)}) collective-permute-start(bf16[256,512]{1,0:T(8,128)(2,1)S(1)} %bitcast.5), channel_id=1, source_target_pairs={{0,2},{1,3},{4,0},{5,1},{8,4},{9,5},{12,8},{13,9},{14,12},{15,13},... | collective-permute-start | bytes 786440 | tf_op jit(solution)/shard_map/ppermute | solution.py:297
  19.6 12.9 %collective-permute-start.7 = (bf16[256,512]{1,0:T(8,128)(2,1)S(1)}, bf16[256,512]{1,0:T(8,128)(2,1)S(1)}, u32[]{:S(2)}, u32[]{:S(2)}) collective-permute-start(bf16[256,512]{1,0:T(8,128)(2,1)S(1)} %bitcast.6), channel_id=1, source_target_pairs={{0,4},{1,5},{4,8},{5,9},{8,12},{9,13},{12,14},{13,15},{14,10},{15,... | collective-permute-start | bytes 786440 | tf_op jit(solution)/shard_map/ppermute | solution.py:296
  20.0 12.6 %collective-permute-start.3 = (bf16[4,2,14336]{2,1,0:T(2,128)(2,1)S(1)}, bf16[4,2,14336]{2,1,0:T(2,128)(2,1)S(1)}, u32[]{:S(2)}, u32[]{:S(2)}) collective-permute-start(bf16[4,2,14336]{2,1,0:T(2,128)(2,1)S(1)} %get-tuple-element.68), channel_id=1, source_target_pairs={{0,2},{1,3},{2,0},{3,1},{4,6},{5,7},{6,4},{7,5},{8,10},{9,11},{10,... | collective-permute-start | bytes 688136 | tf_op jit(solution)/shard_map/ppermute | solution.py:331
  32.7 5.8 %collective-permute-start.9 = (bf16[8,2,14336]{2,1,0:T(2,128)(2,1)S(1)}, bf16[8,2,14336]{2,1,0:T(2,128)(2,1)S(1)}, u32[]{:S(2)}, u32[]{:S(2)}) collective-permute-start(bf16[8,2,14336]{2,1,0:T(2,128)(2,1)S(1)} %constant_dynamic-update-slice_fusion.2.near_ref), channel_id=1, source_target_pairs={{0,1},{1,0},{2,3},{3,2},{4,5},{5,4},{6,7},{7,6},{8,9},{9,8},{10,11... | collective-permute-start | bytes 1376264 | tf_op jit(solution)/shard_map/ppermute | solution.py:43
  32.8 5.7 %collective-permute-start.12 = (bf16[256,512]{1,0:T(8,128)(2,1)S(1)}, bf16[256,512]{1,0:T(8,128)(2,1)S(1)}, u32[]{:S(2)}, u32[]{:S(2)}) collective-permute-start(bf16[256,512]{1,0:T(8,128)(2,1)S(1)} %collective-permute-done.7.refs_2_), channel_id=1, source_target_pairs={{0,1},{1,0},{2,3},{3,2},{4,5},{5,4},{6,7},{7,6},{8,9},{9,8},{10,11... | collective-permute-start | bytes 786440 | tf_op jit(solution)/shard_map/ppermute | solution.py:43
  33.4 14.3 %collective-permute-start.14 = (bf16[256,512]{1,0:T(8,128)(2,1)S(1)}, bf16[256,512]{1,0:T(8,128)(2,1)S(1)}, u32[]{:S(2)}, u32[]{:S(2)}) collective-permute-start(bf16[256,512]{1,0:T(8,128)(2,1)S(1)} %collective-permute-done.7.refs_2_), channel_id=1, source_target_pairs={{0,4},{1,5},{4,8},{5,9},{8,12},{9,13},{12,14},{13,15},{14,10},{15,... | collective-permute-start | bytes 786440 | tf_op jit(solution)/shard_map/ppermute | solution.py:296
  38.4 9.2 %collective-permute-start.15 = (bf16[256,512]{1,0:T(8,128)(2,1)S(1)}, bf16[256,512]{1,0:T(8,128)(2,1)S(1)}, u32[]{:S(2)}, u32[]{:S(2)}) collective-permute-start(bf16[256,512]{1,0:T(8,128)(2,1)S(1)} %collective-permute-done.8.refs_4_), channel_id=1, source_target_pairs={{0,2},{1,3},{4,0},{5,1},{8,4},{9,5},{12,8},{13,9},{14,12},{15,13},... | collective-permute-start | bytes 786440 | tf_op jit(solution)/shard_map/ppermute | solution.py:297
  38.5 9.2 %collective-permute-start.16 = (bf16[4,32,256]{2,1,0:T(8,128)(2,1)S(1)}, bf16[4,32,256]{2,1,0:T(8,128)(2,1)S(1)}, u32[]{:S(2)}, u32[]{:S(2)}) collective-permute-start(bf16[4,32,256]{2,1,0:T(8,128)(2,1)S(1)} %stack.3.refs_0_), channel_id=1, source_target_pairs={{0,2},{1,3},{2,0},{3,1},{4,6},{5,7},{6,4},{7,5},{8,10},{9,11},{10,... | collective-permute-start | bytes 196616 | tf_op jit(solution)/shard_map/ppermute | solution.py:370
  47.7 8.2 %collective-permute-start.21 = (bf16[256,512]{1,0:T(8,128)(2,1)S(1)}, bf16[256,512]{1,0:T(8,128)(2,1)S(1)}, u32[]{:S(2)}, u32[]{:S(2)}) collective-permute-start(bf16[256,512]{1,0:T(8,128)(2,1)S(1)} %collective-permute-done.14.refs_6_), channel_id=1, source_target_pairs={{0,1},{1,0},{2,3},{3,2},{4,5},{5,4},{6,7},{7,6},{8,9},{9,8},{10,11... | collective-permute-start | bytes 786440 | tf_op jit(solution)/shard_map/ppermute | solution.py:43
  47.8 8.7 %collective-permute-start.17 = (bf16[256,512]{1,0:T(8,128)(2,1)S(1)}, bf16[256,512]{1,0:T(8,128)(2,1)S(1)}, u32[]{:S(2)}, u32[]{:S(2)}) collective-permute-start(bf16[256,512]{1,0:T(8,128)(2,1)S(1)} %collective-permute-done.14.refs_6_), channel_id=1, source_target_pairs={{0,4},{1,5},{4,8},{5,9},{8,12},{9,13},{12,14},{13,15},{14,10},{15,... | collective-permute-start | bytes 786440 | tf_op jit(solution)/shard_map/ppermute | solution.py:296
  48.0 8.5 %collective-permute-start.22 = (bf16[256,512]{1,0:T(8,128)(2,1)S(1)}, bf16[256,512]{1,0:T(8,128)(2,1)S(1)}, u32[]{:S(2)}, u32[]{:S(2)}) collective-permute-start(bf16[256,512]{1,0:T(8,128)(2,1)S(1)} %collective-permute-done.15.refs_8_), channel_id=1, source_target_pairs={{0,1},{1,0},{2,3},{3,2},{4,5},{5,4},{6,7},{7,6},{8,9},{9,8},{10,11... | collective-permute-start | bytes 786440 | tf_op jit(solution)/shard_map/ppermute | solution.py:43
  48.3 9.7 %collective-permute-start.18 = (bf16[256,512]{1,0:T(8,128)(2,1)S(1)}, bf16[256,512]{1,0:T(8,128)(2,1)S(1)}, u32[]{:S(2)}, u32[]{:S(2)}) collective-permute-start(bf16[256,512]{1,0:T(8,128)(2,1)S(1)} %collective-permute-done.15.refs_8_), channel_id=1, source_target_pairs={{0,2},{1,3},{4,0},{5,1},{8,4},{9,5},{12,8},{13,9},{14,12},{15,13},... | collective-permute-start | bytes 786440 | tf_op jit(solution)/shard_map/ppermute | solution.py:297
  57.9 9.6 %collective-permute-start.25 = (bf16[256,512]{1,0:T(8,128)(2,1)S(1)}, bf16[256,512]{1,0:T(8,128)(2,1)S(1)}, u32[]{:S(2)}, u32[]{:S(2)}) collective-permute-start(bf16[256,512]{1,0:T(8,128)(2,1)S(1)} %collective-permute-done.17.refs_10_), channel_id=1, source_target_pairs={{0,1},{1,0},{2,3},{3,2},{4,5},{5,4},{6,7},{7,6},{8,9},{9,8},{10,11... | collective-permute-start | bytes 786440 | tf_op jit(solution)/shard_map/ppermute | solution.py:43
  57.9 9.6 %collective-permute-start.26 = (bf16[256,512]{1,0:T(8,128)(2,1)S(1)}, bf16[256,512]{1,0:T(8,128)(2,1)S(1)}, u32[]{:S(2)}, u32[]{:S(2)}) collective-permute-start(bf16[256,512]{1,0:T(8,128)(2,1)S(1)} %collective-permute-done.18.refs_12_), channel_id=1, source_target_pairs={{0,1},{1,0},{2,3},{3,2},{4,5},{5,4},{6,7},{7,6},{8,9},{9,8},{10,11... | collective-permute-start | bytes 786440 | tf_op jit(solution)/shard_map/ppermute | solution.py:43
  58.5 9.0 %collective-permute-start.24 = (bf16[128,512]{1,0:T(8,128)(2,1)S(1)}, bf16[128,512]{1,0:T(8,128)(2,1)S(1)}, u32[]{:S(2)}, u32[]{:S(2)}) collective-permute-start(bf16[128,512]{1,0:T(8,128)(2,1)S(1)} %slice.11), channel_id=1, source_target_pairs={{0,2},{1,3},{4,0},{5,1},{8,4},{9,5},{12,8},{13,9},{14,12},{15,13},... | collective-permute-start | bytes 393224 | tf_op jit(solution)/shard_map/ppermute | solution.py:297
  59.2 8.3 %collective-permute-start.23 = (bf16[128,512]{1,0:T(8,128)(2,1)S(1)}, bf16[128,512]{1,0:T(8,128)(2,1)S(1)}, u32[]{:S(2)}, u32[]{:S(2)}) collective-permute-start(bf16[128,512]{1,0:T(8,128)(2,1)S(1)} %slice.10), channel_id=1, source_target_pairs={{0,4},{1,5},{4,8},{5,9},{8,12},{9,13},{12,14},{13,15},{14,10},{15,... | collective-permute-start | bytes 393224 | tf_op jit(solution)/shard_map/ppermute | solution.py:296
  76.1 7.7 %collective-permute-start.30 = (bf16[48,512]{1,0:T(8,128)(2,1)S(1)}, bf16[48,512]{1,0:T(8,128)(2,1)S(1)}, u32[]{:S(2)}, u32[]{:S(2)}) collective-permute-start(bf16[48,512]{1,0:T(8,128)(2,1)S(1)} %get-tuple-element.110), channel_id=1, source_target_pairs={{0,12},{1,13},{2,14},{3,15},{4,8},{5,9},{6,10},{7,11},{8,4},{9,5},... | collective-permute-start | bytes 147464 | tf_op jit(solution)/shard_map/ppermute | solution.py:490
  77.4 8.5 %collective-permute-start.31 = (bf16[48,512]{1,0:T(8,128)(2,1)S(1)}, bf16[48,512]{1,0:T(8,128)(2,1)S(1)}, u32[]{:S(2)}, u32[]{:S(2)}) collective-permute-start(bf16[48,512]{1,0:T(8,128)(2,1)S(1)} %get-tuple-element.111), channel_id=1, source_target_pairs={{0,14},{1,15},{2,12},{3,13},{4,10},{5,11},{6,8},{7,9},{8,6},{9,7},... | collective-permute-start | bytes 147464 | tf_op jit(solution)/shard_map/ppermute | solution.py:490
  80.1 7.9 %collective-permute-start.32 = (bf16[48,512]{1,0:T(8,128)(2,1)S(1)}, bf16[48,512]{1,0:T(8,128)(2,1)S(1)}, u32[]{:S(2)}, u32[]{:S(2)}) collective-permute-start(bf16[48,512]{1,0:T(8,128)(2,1)S(1)} %get-tuple-element.112), channel_id=1, source_target_pairs={{0,8},{1,9},{2,10},{3,11},{4,12},{5,13},{6,14},{7,15},{8,0},{9,1},... | collective-permute-start | bytes 147464 | tf_op jit(solution)/shard_map/ppermute | solution.py:490
  80.1 7.9 %collective-permute-start.33 = (bf16[48,512]{1,0:T(8,128)(2,1)S(1)}, bf16[48,512]{1,0:T(8,128)(2,1)S(1)}, u32[]{:S(2)}, u32[]{:S(2)}) collective-permute-start(bf16[48,512]{1,0:T(8,128)(2,1)S(1)} %get-tuple-element.113), channel_id=1, source_target_pairs={{0,10},{1,11},{2,8},{3,9},{4,14},{5,15},{6,12},{7,13},{8,2},{9,3},... | collective-permute-start | bytes 147464 | tf_op jit(solution)/shard_map/ppermute | solution.py:490
  (19 other events, 120.2 us)

commit v14 on v12

--- a/solution.py
+++ b/solution.py
@@ -41,11 +41,6 @@
 
 def swap(x, n):
     return lax.ppermute(x, "blk", xor_pairs(n, 1))
-
-
-def exchange(x, n, stride):
-    groups = [list(range(first, n, stride)) for first in range(stride)]
-    return lax.all_to_all(x, "blk", 0, 0, axis_index_groups=groups, tiled=True)
 
 
 def bits_of(size):
@@ -76,14 +71,19 @@
 
 
 def rotate_in_kernel(tok_rows, near_ref, far_ref, basis_ref, out_ref):
-    tokens = out_ref.shape[1]
-    acts = jnp.concatenate([near_ref[...], far_ref[...]], axis=0)
+    tokens = out_ref.shape[0]
+    depth = near_ref.shape[2]
+    acts = jnp.concatenate([ref[...].reshape(-1, depth) for ref in (near_ref, far_ref)], axis=0)
     rotated = jnp.dot(acts, basis_ref[...], preferred_element_type=jnp.float32)
     wanted = lax.broadcasted_iota(jnp.int32, (tokens, tokens), 0)
     held = held_tokens(lax.axis_index("blk"), tokens, tok_rows)
-    ordered = reorder(wanted, held, rotated).astype(jnp.bfloat16)
-    for copy in range(out_ref.shape[0]):
-        out_ref[copy] = ordered
+    out_ref[...] = reorder(wanted, held, rotated).astype(jnp.bfloat16)
+
+
+def stack_kernel(first_ref, last_ref, out_ref):
+    half = first_ref.shape[0]
+    out_ref[:half] = first_ref[...]
+    out_ref[half:] = last_ref[...]
 
 
 def rotate_part(first, near_ref, far_ref, basis_ref, basis, total, sem):
@@ -100,7 +100,8 @@
     @pl.loop(0, steps)
     def _(step):
         columns = pl.ds(pl.multiple_of((first + step) * depth, depth), depth)
-        grads = jnp.concatenate([near_ref[:, columns], far_ref[:, columns]], axis=0)
+        rows = [ref[:, :, columns].reshape(-1, depth) for ref in (near_ref, far_ref)]
+        grads = jnp.concatenate(rows, axis=0)
         copy_of(step).wait()
         total[...] += jnp.dot(grads, basis[step], preferred_element_type=jnp.float32)
 
@@ -169,9 +170,9 @@
         for steps in begun:
             for other, rotated_ref in enumerate((near_ref, far_ref)):
                 source = ring_source(me, steps, other, chips)
-                grad = jnp.dot(
-                    aligned, rotated_ref[source // 2], preferred_element_type=jnp.float32
-                )
+                key = (source ^ me) // 2
+                rotated = rotated_ref[lax.rem(key, 2) * (chips // 2) + key // 2]
+                grad = jnp.dot(aligned, rotated, preferred_element_type=jnp.float32)
                 for first in range(0, width, LANES):
                     tile = tiles[(source * width + first) // LANES]
                     lanes = pl.ds(pl.multiple_of(tile * LANES, LANES), LANES)
@@ -274,6 +275,7 @@
     both = jnp.concatenate([grad_out, activations], axis=1)[None]
     got = [lax.ppermute(both, "blk", xor_pairs(n, 4 * key)) for key in range(1, pairs)]
     both, own, *got = after(both, own, *got)
+    depth, later = 1024, 7
     grads, acts = pl.pallas_call(
         part_kernel,
         out_shape=(
@@ -290,37 +292,51 @@
     grads_got = lax.ppermute(grads, "blk", xor_pairs(n, 2))
     right, left = [own, to_right(own)], [own, to_left(own)]
 
-    acts = jnp.concatenate([acts, acts_got], axis=0).reshape(tokens // 2, full_in)
+    acts = jnp.concatenate([acts, acts_got], axis=0)
     rotated = pl.pallas_call(
         functools.partial(rotate_in_kernel, tok_rows),
-        out_shape=jax.ShapeDtypeStruct((chips, tokens, in_width), jnp.bfloat16),
+        out_shape=jax.ShapeDtypeStruct((tokens, in_width), jnp.bfloat16),
         in_specs=[VMEM, VMEM, VMEM],
         out_specs=VMEM,
         compiler_params=pltpu.CompilerParams(vmem_limit_bytes=8 * MIB),
         cost_estimate=CHEAP,
         name="rotate_in",
     )(acts, swap(acts, n), basis_in)
+
+    def doubled(x, key):
+        return pl.pallas_call(
+            stack_kernel,
+            out_shape=jax.ShapeDtypeStruct((2 * x.shape[0], *x.shape[1:]), x.dtype),
+            in_specs=[VMEM, VMEM],
+            out_specs=VMEM,
+            compiler_params=pltpu.CompilerParams(vmem_limit_bytes=8 * MIB),
+            cost_estimate=CHEAP,
+            name="stack",
+        )(x, lax.ppermute(x, "blk", xor_pairs(n, key)))
+
     own_far = swap(own, n)
-    grads_got, right[-1], left[-1], own_far, _ = after(
-        grads_got, right[-1], left[-1], own_far, rotated
-    )
-    rotated = exchange(rotated, n, 2)
+    grads_got, rotated, right[-1], left[-1], own_far = after(
+        grads_got, rotated, right[-1], left[-1], own_far
+    )
+    rotated = doubled(rotated[None], 4)
     near = [right[0], right[1], left[1]]
     while len(right) < steps - 1:
         right.append(to_right(right[-1]))
         left.append(to_left(left[-1]))
-    grads = jnp.concatenate([grads, grads_got], axis=0).reshape(tokens // 2, full_out)
+    grads = jnp.concatenate([grads, grads_got], axis=0)
     grads_far = swap(grads, n)
     far = [swap(piece, n) for piece in near[1:]]
-    grads, grads_far, *far = after(grads, grads_far, *far)
+    grads, grads_far, rotated, *far = after(grads, grads_far, rotated, *far)
     far = [own_far, *far]
-
-    depth = 1024
-    cuts = (0, full_out // depth // 2, full_out // depth)
+    key = 8
+    while key < n:
+        rotated = doubled(rotated, key)
+        key *= 2
+
     rotate = lambda kernel, count, scratch, shape, dtype, *operands: pl.pallas_call(
         kernel,
         out_shape=jax.ShapeDtypeStruct(shape, dtype),
-        in_specs=[VMEM, VMEM, ANY, ANY, VMEM][: len(operands)],
+        in_specs=[ANY if x is basis_out or x is block_map else VMEM for x in operands],
         out_specs=VMEM,
         scratch_shapes=[pltpu.VMEM((count, depth, tile_width), jnp.bfloat16)]
         + scratch
@@ -331,7 +347,7 @@
     )(*operands)
     start = rotate(
         functools.partial(rotate_first_kernel),
-        cuts[1],
+        full_out // depth - later,
         [],
         (tokens, tile_width),
         jnp.float32,
@@ -339,17 +355,17 @@
         grads_far,
         basis_out,
     )
-    start, grads, rotated, right[-1], left[-1] = after(
-        start, grads, rotated, right[-1], left[-1]
-    )
-    rotated_far = swap(rotated, n)
+    start, grads, right[-1], left[-1], rotated = after(
+        start, grads, right[-1], left[-1], rotated
+    )
+    rotated = doubled(rotated, 2)
     near += [right[-1], left[-1]]
     far += [swap(right[-1], n), swap(left[-1], n)]
     right.append(to_right(right[-1]))
     left.append(to_left(left[-1]))
     aligned = rotate(
-        functools.partial(rotate_last_kernel, tok_rows, cuts[1]),
-        cuts[2] - cuts[1],
+        functools.partial(rotate_last_kernel, tok_rows, full_out // depth - later),
+        later,
         [
             pltpu.VMEM((tokens, tile_width), jnp.float32),
             pltpu.SMEM(block_map.shape, jnp.int32),
@@ -363,8 +379,8 @@
         start,
     )
 
-    aligned, rotated_far, right[-1], left[-1], *far = after(
-        aligned, rotated_far, right[-1], left[-1], *far
+    aligned, right[-1], left[-1], rotated, *far = after(
+        aligned, right[-1], left[-1], rotated, *far
     )
     cut = in_width // 2
     last = [to_right(right[-1][:cut]), to_left(left[-1][cut:])]
@@ -375,7 +391,7 @@
     scaled = pl.pallas_call(
         functools.partial(scale_kernel, begun),
         out_shape=jax.ShapeDtypeStruct((tile_width, full_in), jnp.bfloat16),
-        in_specs=[VMEM, VMEM, VMEM, ANY, ANY],
+        in_specs=[VMEM] * 3 + [ANY] * 2,
         out_specs=VMEM,
         scratch_shapes=[
             pltpu.VMEM((blocks, tile_width // blocks, full_in), jnp.float32),
@@ -385,7 +401,7 @@
         compiler_params=pltpu.CompilerParams(vmem_limit_bytes=40 * MIB),
         cost_estimate=CHEAP,
         name="scale",
-    )(aligned, rotated, rotated_far, tile_order, eigenvalues)
+    )(aligned, rotated, swap(rotated, n), tile_order, eigenvalues)
 
     scaled, *last = after(scaled, *last, *far[-2:])
     far[-2:] = last[2:]

time: 86.1 us -> 86.2 us (level)
  waiting for transfers between devices: 21.4 us -> 22.7 us
    all_to_all x1 -> x0, starting transfers between devices: 4.95 us -> none  [exchange(): return lax.all_to_all(x, 'blk', 0, 0, axis_index_groups=groups, tiled=True)]
    ppermute x0 -> x3, waiting for transfers between devices: none -> 4.07 us  [doubled(): lax.ppermute(x, 'blk', xor_pairs(n, key))]
    ppermute x4, starting transfers between devices: 1.69 us -> 4.65 us  [ring_body(): to_right = lambda x: lax.ppermute(x, 'blk', shift_pairs(n, 1))]
    ppermute x0 -> x3, starting transfers between devices: none -> 2.29 us  [doubled(): lax.ppermute(x, 'blk', xor_pairs(n, key))]
    all_to_all x1 -> x0, waiting for transfers between devices: 2.07 us -> none  [exchange(): return lax.all_to_all(x, 'blk', 0, 0, axis_index_groups=groups, tiled=True)]
    ppermute x4, starting transfers between devices: 6.27 us -> 4.6 us  [ring_body(): to_left = lambda x: lax.ppermute(x, 'blk', shift_pairs(n, -1))]
    ppermute x1, waiting for transfers between devices: 6.64 us -> 7.61 us  [ring_body(): grads_got = lax.ppermute(grads, 'blk', xor_pairs(n, 2))]
    ppermute x4, waiting for transfers between devices: 0.88 us -> 0.01 us  [ring_body(): to_right = lambda x: lax.ppermute(x, 'blk', shift_pairs(n, 1))]
  transfers between devices with their start and end apart: 34 -> 36, of which waited for: 12 -> 12; matrix products, arithmetic and copies ran while one was open for 2% -> 2% of each run, Pallas kernels for 26% -> 26%
where the time goes in v14:
time: 86.2 us; the launch traced here: 85.9 us
  starting transfers between devices  33.7 us (39%)
  Pallas kernels  25.2 us (29%)
  waiting for transfers between devices  22.7 us (26%)
  local copies, waits for them, and re-layouts  3.17 us (4%)
  other arithmetic  0.91 us (1%)
    ppermute x7, starting transfers between devices, ring_body(): lax.ppermute(x, 'blk', xor_pairs(n, 2 * key))  11.7 us
    pallas_call x2, Pallas kernels, ring_body(): pl.pallas_call(kernel, out_shape=jax.ShapeDtypeStruct(shape, dtype), in_s...  10.7 us
    ppermute x1, waiting for transfers between devices, ring_body(): grads_got = lax.ppermute(grads, 'blk', xor_pairs(n, 2))  7.61 us
    pallas_call x1, Pallas kernels, ring_body(): pl.pallas_call(functools.partial(scale_kernel, begun), out_shape=jax.Shap...  6.97 us
    ppermute x3, starting transfers between devices, ring_body(): lax.ppermute(both, 'blk', xor_pairs(n, 4 * key))  5.76 us
    ppermute x4, starting transfers between devices, ring_body(): to_right = lambda x: lax.ppermute(x, 'blk', shift_pairs(n, 1))  4.65 us
    ppermute x4, starting transfers between devices, ring_body(): to_left = lambda x: lax.ppermute(x, 'blk', shift_pairs(n, -1))  4.6 us
    pallas_call x1, Pallas kernels, ring_body(): pl.pallas_call(functools.partial(project_kernel, (0, 6, len(pieces))), ou...  4.49 us
  transfers between devices with their start and end apart: 36, of which 12 were waited for; matrix products, arithmetic and copies ran while one was open for 2% of the time, Pallas kernels for 26%

profile of v14, /device:TPU:0, one launch (start us, length us, event | category | flops | bytes accessed | tf_op | source)
XLA Modules:
  0.0 85.9 jit_solution(11551512064865090343)
XLA Ops:
  0.9 5.1 %collective-permute-start.2 = (bf16[1,2,18432]{2,1,0:T(2,128)(2,1)S(1)}, bf16[1,2,18432]{2,1,0:T(2,128)(2,1)S(1)}, u32[]{:S(2)}, u32[]{:S(2)}) collective-permute-start(bf16[1,2,18432]{2,1,0:T(2,128)(2,1)S(1)} %maximum_bitcast_fusion.refs_0_), channel_id=1, source_target_pairs={{0,12},{1,13},{2,14},{3,15},{4,8},{5,9},{6,10},{7,11},{8,4},{9,5},... | collective-permute-start | bytes 221192 | tf_op jit(solution)/shard_map/ppermute | solution.py:276
  8.8 3.5 %collective-permute-done.1.refs_2_ = bf16[1,2,18432]{2,1,0:T(2,128)(2,1)S(1)} collective-permute-done((bf16[1,2,18432]{2,1,0:T(2,128)(2,1)S(1)}, bf16[1,2,18432]{2,1,0:T(2,128)(2,1)S(1)}, u32[]{:S(2)}, u32[]{:S(2)}) %collective-permute-start.1) | collective-permute-done | bytes 73760 | tf_op jit(solution)/shard_map/ppermute | solution.py:276
  12.3 1.6 %collective-permute-start.4 = (bf16[4,2,4096]{2,1,0:T(2,128)(2,1)S(1)}, bf16[4,2,4096]{2,1,0:T(2,128)(2,1)S(1)}, u32[]{:S(2)}, u32[]{:S(2)}) collective-permute-start(bf16[4,2,4096]{2,1,0:T(2,128)(2,1)S(1)} %get-tuple-element.64), channel_id=1, source_target_pairs={{0,2},{1,3},{2,0},{3,1},{4,6},{5,7},{6,4},{7,5},{8,10},{9,11},{10,... | collective-permute-start | bytes 196616 | tf_op jit(solution)/shard_map/ppermute | solution.py:291
  14.5 1.5 %collective-permute-start.6 = (bf16[256,512]{1,0:T(8,128)(2,1)S(1)}, bf16[256,512]{1,0:T(8,128)(2,1)S(1)}, u32[]{:S(2)}, u32[]{:S(2)}) collective-permute-start(bf16[256,512]{1,0:T(8,128)(2,1)S(1)} %bitcast.6), channel_id=1, source_target_pairs={{0,4},{1,5},{4,8},{5,9},{8,12},{9,13},{12,14},{13,15},{14,10},{15,... | collective-permute-start | bytes 786440 | tf_op jit(solution)/shard_map/ppermute | solution.py:268
  16.9 1.2 %collective-permute-done.5.far_ref = bf16[8,2,4096]{2,1,0:T(2,128)(2,1)S(1)} collective-permute-done((bf16[8,2,4096]{2,1,0:T(2,128)(2,1)S(1)}, bf16[8,2,4096]{2,1,0:T(2,128)(2,1)S(1)}, u32[]{:S(2)}, u32[]{:S(2)}) %collective-permute-start.5) | collective-permute-done | bytes 131104 | tf_op jit(solution)/shard_map/ppermute | solution.py:43
  18.1 1.6 %copy-done = bf16[4096,256]{1,0:T(8,128)(2,1)S(1)} copy-done((bf16[4096,256]{1,0:T(8,128)(2,1)S(1)}, bf16[4096,256]{1,0:T(8,128)(2,1)}, u32[]{:S(2)}) %copy-start) | copy-done | bytes 2097176
  20.2 7.6 %collective-permute-done.3 = bf16[4,2,14336]{2,1,0:T(2,128)(2,1)S(1)} collective-permute-done((bf16[4,2,14336]{2,1,0:T(2,128)(2,1)S(1)}, bf16[4,2,14336]{2,1,0:T(2,128)(2,1)S(1)}, u32[]{:S(2)}, u32[]{:S(2)}) %collective-permute-start.3) | collective-permute-done | bytes 229408 | tf_op jit(solution)/shard_map/ppermute | solution.py:292
  28.7 2.0 %collective-permute-start.13 = (bf16[256,512]{1,0:T(8,128)(2,1)S(1)}, bf16[256,512]{1,0:T(8,128)(2,1)S(1)}, u32[]{:S(2)}, u32[]{:S(2)}) collective-permute-start(bf16[256,512]{1,0:T(8,128)(2,1)S(1)} %collective-permute-done.6.refs_2_), channel_id=1, source_target_pairs={{0,4},{1,5},{4,8},{5,9},{8,12},{9,13},{12,14},{13,15},{14,10},{15,... | collective-permute-start | bytes 786440 | tf_op jit(solution)/shard_map/ppermute | solution.py:268
  30.7 1.7 %collective-permute-done.10.last_ref = bf16[1,32,256]{2,1,0:T(8,128)(2,1)S(1)} collective-permute-done((bf16[1,32,256]{2,1,0:T(8,128)(2,1)S(1)}, bf16[1,32,256]{2,1,0:T(8,128)(2,1)S(1)}, u32[]{:S(2)}, u32[]{:S(2)}) %collective-permute-start.10) | collective-permute-done | bytes 16416 | tf_op jit(solution)/shard_map/ppermute | solution.py:315
  34.0 5.2 %rotate_first.1.start_ref = f32[32,896]{1,0:T(8,128)S(1)} custom-call(bf16[8,2,14336]{2,1,0:T(2,128)(2,1)S(1)} %constant_dynamic-update-slice_fusion.2.near_ref, bf16[8,2,14336]{2,1,0:T(2,128)(2,1)S(1)} %collective-permute-done.9.far_ref, bf16[14336,896]{1,0:T(8,128)(2,1)} %basis_out_ref.1), custom_call_target="tpu_custom_call" | custom-call | flops 1 | bytes 1 | tf_op jit(solution)/shard_map/rotate_first/pallas_call | solution.py:336
  39.2 1.7 %collective-permute-done.15.last_ref = bf16[2,32,256]{2,1,0:T(8,128)(2,1)S(1)} collective-permute-done((bf16[2,32,256]{2,1,0:T(8,128)(2,1)S(1)}, bf16[2,32,256]{2,1,0:T(8,128)(2,1)S(1)}, u32[]{:S(2)}, u32[]{:S(2)}) %collective-permute-start.15) | collective-permute-done | bytes 32800 | tf_op jit(solution)/shard_map/ppermute | solution.py:315
  41.0 1.1 %collective-permute-start.16 = (bf16[256,512]{1,0:T(8,128)(2,1)S(1)}, bf16[256,512]{1,0:T(8,128)(2,1)S(1)}, u32[]{:S(2)}, u32[]{:S(2)}) collective-permute-start(bf16[256,512]{1,0:T(8,128)(2,1)S(1)} %collective-permute-done.13.refs_6_), channel_id=1, source_target_pairs={{0,4},{1,5},{4,8},{5,9},{8,12},{9,13},{12,14},{13,15},{14,10},{15,... | collective-permute-start | bytes 786440 | tf_op jit(solution)/shard_map/ppermute | solution.py:268
  43.3 1.7 %collective-permute-start.18 = (bf16[4,32,256]{2,1,0:T(8,128)(2,1)S(1)}, bf16[4,32,256]{2,1,0:T(8,128)(2,1)S(1)}, u32[]{:S(2)}, u32[]{:S(2)}) collective-permute-start(bf16[4,32,256]{2,1,0:T(8,128)(2,1)S(1)} %stack.4.first_ref), channel_id=1, source_target_pairs={{0,2},{1,3},{2,0},{3,1},{4,6},{5,7},{6,4},{7,5},{8,10},{9,11},{10,... | collective-permute-start | bytes 196616 | tf_op jit(solution)/shard_map/ppermute | solution.py:315
  44.9 5.5 %rotate_last.1.aligned_ref = bf16[896,32]{1,0:T(8,128)(2,1)S(1)} custom-call(bf16[8,2,14336]{2,1,0:T(2,128)(2,1)S(1)} %constant_dynamic-update-slice_fusion.2.near_ref, bf16[8,2,14336]{2,1,0:T(2,128)(2,1)S(1)} %collective-permute-done.9.far_ref, bf16[14336,896]{1,0:T(8,128)(2,1)} %basis_out_ref.1, s32[16]{0:T(128)S(1)} %copy-done.2, ...), custom_call_target="tpu_custom_call" | custom-call | flops 1 | bytes 1 | tf_op jit(solution)/shard_map/rotate_last/pallas_call | solution.py:336
  51.9 2.1 %collective-permute-start.23 = (bf16[128,512]{1,0:T(8,128)(2,1)S(1)}, bf16[128,512]{1,0:T(8,128)(2,1)S(1)}, u32[]{:S(2)}, u32[]{:S(2)}) collective-permute-start(bf16[128,512]{1,0:T(8,128)(2,1)S(1)} %slice.11), channel_id=1, source_target_pairs={{0,2},{1,3},{4,0},{5,1},{8,4},{9,5},{12,8},{13,9},{14,12},{15,13},... | collective-permute-start | bytes 393224 | tf_op jit(solution)/shard_map/ppermute | solution.py:269
  54.0 7.0 %scale.1.scaled_ref = bf16[896,4096]{1,0:T(8,128)(2,1)S(1)} custom-call(bf16[896,32]{1,0:T(8,128)(2,1)S(1)} %rotate_last.1.aligned_ref, bf16[8,32,256]{2,1,0:T(8,128)(2,1)S(1)} %stack.5.near_ref, bf16[8,32,256]{2,1,0:T(8,128)(2,1)S(1)} %collective-permute-done.21.far_ref, s32[32]{0:T(128)S(1)} %copy-done.1, f32[896,4096]{1,0:T(8,128)} %eigen_ref.1), custom_call_target="tpu_custom_call" | custom-call | flops 1 | bytes 1 | tf_op jit(solution)/shard_map/scale/pallas_call | solution.py:391
  61.6 4.5 %project.1 = (f32[896,512]{1,0:T(8,128)S(1)}, bf16[768,896]{1,0:T(8,128)(2,1)S(1)}) custom-call(bf16[896,4096]{1,0:T(8,128)(2,1)S(1)} %scale.1.scaled_ref, bf16[14336,896]{1,0:T(8,128)(2,1)} %basis_out_ref.1, bf16[256,512]{1,0:T(8,128)(2,1)S(1)} %bitcast.7, bf16[256,512]{1,0:T(8,128)(2,1)S(1)} %collective-permute-done.8.refs_1_, ...), custom_call_target="tpu_custom_call" | custom-call | flops 1 | bytes 1 | tf_op jit(solution)/shard_map/project/pallas_call | solution.py:411
  66.1 1.6 %window.1 = (bf16[8,48,512]{2,1,0:T(8,128)(2,1)S(1)}, f32[8,48,512]{2,1,0:T(8,128)S(1)}) custom-call(bf16[768,896]{1,0:T(8,128)(2,1)S(1)} %get-tuple-element.93.window_ref, bf16[896,4096]{1,0:T(8,128)(2,1)S(1)} %scale.1.scaled_ref, f32[896,512]{1,0:T(8,128)S(1)} %get-tuple-element.94.projected_ref, bf16[128,512]{1,0:T(8,128)(2,1)S(1)} %collective-permute-done.22.refs_0_, ...), custom_call_target="tpu_custom_call" | custom-call | flops 1 | bytes 1 | tf_op jit(solution)/shard_map/window/pallas_call | solution.py:429
  68.2 1.4 %collective-permute-done.28.got_ref = bf16[8,48,512]{2,1,0:T(8,128)(2,1)S(1)} collective-permute-done((bf16[8,48,512]{2,1,0:T(8,128)(2,1)S(1)}, bf16[8,48,512]{2,1,0:T(8,128)(2,1)S(1)}, u32[]{:S(2)}, u32[]{:S(2)}) %collective-permute-start.28) | collective-permute-done | bytes 393248 | tf_op jit(solution)/shard_map/ppermute | solution.py:43
  69.6 4.5 %collective-permute-start.29 = (bf16[48,512]{1,0:T(8,128)(2,1)S(1)}, bf16[48,512]{1,0:T(8,128)(2,1)S(1)}, u32[]{:S(2)}, u32[]{:S(2)}) collective-permute-start(bf16[48,512]{1,0:T(8,128)(2,1)S(1)} %get-tuple-element.100), channel_id=1, source_target_pairs={{0,12},{1,13},{2,14},{3,15},{4,8},{5,9},{6,10},{7,11},{8,4},{9,5},... | collective-permute-start | bytes 147464 | tf_op jit(solution)/shard_map/ppermute | solution.py:454
  75.0 3.1 %collective-permute-start.32 = (bf16[48,512]{1,0:T(8,128)(2,1)S(1)}, bf16[48,512]{1,0:T(8,128)(2,1)S(1)}, u32[]{:S(2)}, u32[]{:S(2)}) collective-permute-start(bf16[48,512]{1,0:T(8,128)(2,1)S(1)} %get-tuple-element.103), channel_id=1, source_target_pairs={{0,10},{1,11},{2,8},{3,9},{4,14},{5,15},{6,12},{7,13},{8,2},{9,3},... | collective-permute-start | bytes 147464 | tf_op jit(solution)/shard_map/ppermute | solution.py:454
  78.1 1.4 %collective-permute-start.33 = (bf16[48,512]{1,0:T(8,128)(2,1)S(1)}, bf16[48,512]{1,0:T(8,128)(2,1)S(1)}, u32[]{:S(2)}, u32[]{:S(2)}) collective-permute-start(bf16[48,512]{1,0:T(8,128)(2,1)S(1)} %get-tuple-element.104), channel_id=1, source_target_pairs={{0,4},{1,5},{2,6},{3,7},{4,0},{5,1},{6,2},{7,3},{8,12},{9,13},{10,... | collective-permute-start | bytes 147464 | tf_op jit(solution)/shard_map/ppermute | solution.py:454
  79.5 1.4 %collective-permute-start.34 = (bf16[48,512]{1,0:T(8,128)(2,1)S(1)}, bf16[48,512]{1,0:T(8,128)(2,1)S(1)}, u32[]{:S(2)}, u32[]{:S(2)}) collective-permute-start(bf16[48,512]{1,0:T(8,128)(2,1)S(1)} %get-tuple-element.105), channel_id=1, source_target_pairs={{0,6},{1,7},{2,4},{3,5},{4,2},{5,3},{6,0},{7,1},{8,14},{9,15},{10,... | collective-permute-start | bytes 147464 | tf_op jit(solution)/shard_map/ppermute | solution.py:454
  81.6 2.2 %collective-permute-done.32.refs_3_ = bf16[48,512]{1,0:T(8,128)(2,1)S(1)} collective-permute-done((bf16[48,512]{1,0:T(8,128)(2,1)S(1)}, bf16[48,512]{1,0:T(8,128)(2,1)S(1)}, u32[]{:S(2)}, u32[]{:S(2)}) %collective-permute-start.32) | collective-permute-done | bytes 49184 | tf_op jit(solution)/shard_map/ppermute | solution.py:454
  (75 shorter events, 15.5 us)
Async XLA Ops:
  0.9 7.9 %collective-permute-start.2 = (bf16[1,2,18432]{2,1,0:T(2,128)(2,1)S(1)}, bf16[1,2,18432]{2,1,0:T(2,128)(2,1)S(1)}, u32[]{:S(2)}, u32[]{:S(2)}) collective-permute-start(bf16[1,2,18432]{2,1,0:T(2,128)(2,1)S(1)} %maximum_bitcast_fusion.refs_0_), channel_id=1, source_target_pairs={{0,12},{1,13},{2,14},{3,15},{4,8},{5,9},{6,10},{7,11},{8,4},{9,5},... | collective-permute-start | bytes 221192 | tf_op jit(solution)/shard_map/ppermute | solution.py:276
  6.0 6.2 %collective-permute-start.1 = (bf16[1,2,18432]{2,1,0:T(2,128)(2,1)S(1)}, bf16[1,2,18432]{2,1,0:T(2,128)(2,1)S(1)}, u32[]{:S(2)}, u32[]{:S(2)}) collective-permute-start(bf16[1,2,18432]{2,1,0:T(2,128)(2,1)S(1)} %maximum_bitcast_fusion.refs_0_), channel_id=1, source_target_pairs={{0,8},{1,9},{2,10},{3,11},{4,12},{5,13},{6,14},{7,15},{8,0},{9,1},... | collective-permute-start | bytes 221192 | tf_op jit(solution)/shard_map/ppermute | solution.py:276
  6.0 6.2 %collective-permute-start = (bf16[1,2,18432]{2,1,0:T(2,128)(2,1)S(1)}, bf16[1,2,18432]{2,1,0:T(2,128)(2,1)S(1)}, u32[]{:S(2)}, u32[]{:S(2)}) collective-permute-start(bf16[1,2,18432]{2,1,0:T(2,128)(2,1)S(1)} %maximum_bitcast_fusion.refs_0_), channel_id=1, source_target_pairs={{0,4},{1,5},{2,6},{3,7},{4,0},{5,1},{6,2},{7,3},{8,12},{9,13},{10,... | collective-permute-start | bytes 221192 | tf_op jit(solution)/shard_map/ppermute | solution.py:276
  13.9 13.9 %collective-permute-start.8 = (bf16[256,512]{1,0:T(8,128)(2,1)S(1)}, bf16[256,512]{1,0:T(8,128)(2,1)S(1)}, u32[]{:S(2)}, u32[]{:S(2)}) collective-permute-start(bf16[256,512]{1,0:T(8,128)(2,1)S(1)} %bitcast.4), channel_id=1, source_target_pairs={{0,1},{1,0},{2,3},{3,2},{4,5},{5,4},{6,7},{7,6},{8,9},{9,8},{10,11... | collective-permute-start | bytes 786440 | tf_op jit(solution)/shard_map/ppermute | solution.py:43
  14.0 13.9 %collective-permute-start.7 = (bf16[256,512]{1,0:T(8,128)(2,1)S(1)}, bf16[256,512]{1,0:T(8,128)(2,1)S(1)}, u32[]{:S(2)}, u32[]{:S(2)}) collective-permute-start(bf16[256,512]{1,0:T(8,128)(2,1)S(1)} %bitcast.5), channel_id=1, source_target_pairs={{0,2},{1,3},{4,0},{5,1},{8,4},{9,5},{12,8},{13,9},{14,12},{15,13},... | collective-permute-start | bytes 786440 | tf_op jit(solution)/shard_map/ppermute | solution.py:269
  14.5 13.3 %collective-permute-start.6 = (bf16[256,512]{1,0:T(8,128)(2,1)S(1)}, bf16[256,512]{1,0:T(8,128)(2,1)S(1)}, u32[]{:S(2)}, u32[]{:S(2)}) collective-permute-start(bf16[256,512]{1,0:T(8,128)(2,1)S(1)} %bitcast.6), channel_id=1, source_target_pairs={{0,4},{1,5},{4,8},{5,9},{8,12},{9,13},{12,14},{13,15},{14,10},{15,... | collective-permute-start | bytes 786440 | tf_op jit(solution)/shard_map/ppermute | solution.py:268
  16.1 11.8 %collective-permute-start.3 = (bf16[4,2,14336]{2,1,0:T(2,128)(2,1)S(1)}, bf16[4,2,14336]{2,1,0:T(2,128)(2,1)S(1)}, u32[]{:S(2)}, u32[]{:S(2)}) collective-permute-start(bf16[4,2,14336]{2,1,0:T(2,128)(2,1)S(1)} %get-tuple-element.63), channel_id=1, source_target_pairs={{0,2},{1,3},{2,0},{3,1},{4,6},{5,7},{6,4},{7,5},{8,10},{9,11},{10,... | collective-permute-start | bytes 688136 | tf_op jit(solution)/shard_map/ppermute | solution.py:292
  28.7 12.2 %collective-permute-start.13 = (bf16[256,512]{1,0:T(8,128)(2,1)S(1)}, bf16[256,512]{1,0:T(8,128)(2,1)S(1)}, u32[]{:S(2)}, u32[]{:S(2)}) collective-permute-start(bf16[256,512]{1,0:T(8,128)(2,1)S(1)} %collective-permute-done.6.refs_2_), channel_id=1, source_target_pairs={{0,4},{1,5},{4,8},{5,9},{8,12},{9,13},{12,14},{13,15},{14,10},{15,... | collective-permute-start | bytes 786440 | tf_op jit(solution)/shard_map/ppermute | solution.py:268
  32.4 8.5 %collective-permute-start.14 = (bf16[256,512]{1,0:T(8,128)(2,1)S(1)}, bf16[256,512]{1,0:T(8,128)(2,1)S(1)}, u32[]{:S(2)}, u32[]{:S(2)}) collective-permute-start(bf16[256,512]{1,0:T(8,128)(2,1)S(1)} %collective-permute-done.7.refs_4_), channel_id=1, source_target_pairs={{0,2},{1,3},{4,0},{5,1},{8,4},{9,5},{12,8},{13,9},{14,12},{15,13},... | collective-permute-start | bytes 786440 | tf_op jit(solution)/shard_map/ppermute | solution.py:269
  33.4 7.5 %collective-permute-start.15 = (bf16[2,32,256]{2,1,0:T(8,128)(2,1)S(1)}, bf16[2,32,256]{2,1,0:T(8,128)(2,1)S(1)}, u32[]{:S(2)}, u32[]{:S(2)}) collective-permute-start(bf16[2,32,256]{2,1,0:T(8,128)(2,1)S(1)} %stack.3.first_ref), channel_id=1, source_target_pairs={{0,8},{1,9},{2,10},{3,11},{4,12},{5,13},{6,14},{7,15},{8,0},{9,1},... | collective-permute-start | bytes 98312 | tf_op jit(solution)/shard_map/ppermute | solution.py:315
  40.9 10.2 %collective-permute-start.19 = (bf16[256,512]{1,0:T(8,128)(2,1)S(1)}, bf16[256,512]{1,0:T(8,128)(2,1)S(1)}, u32[]{:S(2)}, u32[]{:S(2)}) collective-permute-start(bf16[256,512]{1,0:T(8,128)(2,1)S(1)} %collective-permute-done.13.refs_6_), channel_id=1, source_target_pairs={{0,1},{1,0},{2,3},{3,2},{4,5},{5,4},{6,7},{7,6},{8,9},{9,8},{10,11... | collective-permute-start | bytes 786440 | tf_op jit(solution)/shard_map/ppermute | solution.py:43
  41.0 10.1 %collective-permute-start.16 = (bf16[256,512]{1,0:T(8,128)(2,1)S(1)}, bf16[256,512]{1,0:T(8,128)(2,1)S(1)}, u32[]{:S(2)}, u32[]{:S(2)}) collective-permute-start(bf16[256,512]{1,0:T(8,128)(2,1)S(1)} %collective-permute-done.13.refs_6_), channel_id=1, source_target_pairs={{0,4},{1,5},{4,8},{5,9},{8,12},{9,13},{12,14},{13,15},{14,10},{15,... | collective-permute-start | bytes 786440 | tf_op jit(solution)/shard_map/ppermute | solution.py:268
  42.1 9.0 %collective-permute-start.20 = (bf16[256,512]{1,0:T(8,128)(2,1)S(1)}, bf16[256,512]{1,0:T(8,128)(2,1)S(1)}, u32[]{:S(2)}, u32[]{:S(2)}) collective-permute-start(bf16[256,512]{1,0:T(8,128)(2,1)S(1)} %collective-permute-done.14.refs_8_), channel_id=1, source_target_pairs={{0,1},{1,0},{2,3},{3,2},{4,5},{5,4},{6,7},{7,6},{8,9},{9,8},{10,11... | collective-permute-start | bytes 786440 | tf_op jit(solution)/shard_map/ppermute | solution.py:43
  42.3 8.9 %collective-permute-start.17 = (bf16[256,512]{1,0:T(8,128)(2,1)S(1)}, bf16[256,512]{1,0:T(8,128)(2,1)S(1)}, u32[]{:S(2)}, u32[]{:S(2)}) collective-permute-start(bf16[256,512]{1,0:T(8,128)(2,1)S(1)} %collective-permute-done.14.refs_8_), channel_id=1, source_target_pairs={{0,2},{1,3},{4,0},{5,1},{8,4},{9,5},{12,8},{13,9},{14,12},{15,13},... | collective-permute-start | bytes 786440 | tf_op jit(solution)/shard_map/ppermute | solution.py:269
  43.3 7.9 %collective-permute-start.18 = (bf16[4,32,256]{2,1,0:T(8,128)(2,1)S(1)}, bf16[4,32,256]{2,1,0:T(8,128)(2,1)S(1)}, u32[]{:S(2)}, u32[]{:S(2)}) collective-permute-start(bf16[4,32,256]{2,1,0:T(8,128)(2,1)S(1)} %stack.4.first_ref), channel_id=1, source_target_pairs={{0,2},{1,3},{2,0},{3,1},{4,6},{5,7},{6,4},{7,5},{8,10},{9,11},{10,... | collective-permute-start | bytes 196616 | tf_op jit(solution)/shard_map/ppermute | solution.py:315
  51.2 9.8 %collective-permute-start.24 = (bf16[256,512]{1,0:T(8,128)(2,1)S(1)}, bf16[256,512]{1,0:T(8,128)(2,1)S(1)}, u32[]{:S(2)}, u32[]{:S(2)}) collective-permute-start(bf16[256,512]{1,0:T(8,128)(2,1)S(1)} %collective-permute-done.16.refs_10_), channel_id=1, source_target_pairs={{0,1},{1,0},{2,3},{3,2},{4,5},{5,4},{6,7},{7,6},{8,9},{9,8},{10,11... | collective-permute-start | bytes 786440 | tf_op jit(solution)/shard_map/ppermute | solution.py:43
  51.3 9.8 %collective-permute-start.25 = (bf16[256,512]{1,0:T(8,128)(2,1)S(1)}, bf16[256,512]{1,0:T(8,128)(2,1)S(1)}, u32[]{:S(2)}, u32[]{:S(2)}) collective-permute-start(bf16[256,512]{1,0:T(8,128)(2,1)S(1)} %collective-permute-done.17.refs_12_), channel_id=1, source_target_pairs={{0,1},{1,0},{2,3},{3,2},{4,5},{5,4},{6,7},{7,6},{8,9},{9,8},{10,11... | collective-permute-start | bytes 786440 | tf_op jit(solution)/shard_map/ppermute | solution.py:43
  51.9 9.1 %collective-permute-start.23 = (bf16[128,512]{1,0:T(8,128)(2,1)S(1)}, bf16[128,512]{1,0:T(8,128)(2,1)S(1)}, u32[]{:S(2)}, u32[]{:S(2)}) collective-permute-start(bf16[128,512]{1,0:T(8,128)(2,1)S(1)} %slice.11), channel_id=1, source_target_pairs={{0,2},{1,3},{4,0},{5,1},{8,4},{9,5},{12,8},{13,9},{14,12},{15,13},... | collective-permute-start | bytes 393224 | tf_op jit(solution)/shard_map/ppermute | solution.py:269
  54.0 7.0 %collective-permute-start.22 = (bf16[128,512]{1,0:T(8,128)(2,1)S(1)}, bf16[128,512]{1,0:T(8,128)(2,1)S(1)}, u32[]{:S(2)}, u32[]{:S(2)}) collective-permute-start(bf16[128,512]{1,0:T(8,128)(2,1)S(1)} %slice.10), channel_id=1, source_target_pairs={{0,4},{1,5},{4,8},{5,9},{8,12},{9,13},{12,14},{13,15},{14,10},{15,... | collective-permute-start | bytes 393224 | tf_op jit(solution)/shard_map/ppermute | solution.py:268
  69.6 9.8 %collective-permute-start.29 = (bf16[48,512]{1,0:T(8,128)(2,1)S(1)}, bf16[48,512]{1,0:T(8,128)(2,1)S(1)}, u32[]{:S(2)}, u32[]{:S(2)}) collective-permute-start(bf16[48,512]{1,0:T(8,128)(2,1)S(1)} %get-tuple-element.100), channel_id=1, source_target_pairs={{0,12},{1,13},{2,14},{3,15},{4,8},{5,9},{6,10},{7,11},{8,4},{9,5},... | collective-permute-start | bytes 147464 | tf_op jit(solution)/shard_map/ppermute | solution.py:454
  74.2 6.9 %collective-permute-start.30 = (bf16[48,512]{1,0:T(8,128)(2,1)S(1)}, bf16[48,512]{1,0:T(8,128)(2,1)S(1)}, u32[]{:S(2)}, u32[]{:S(2)}) collective-permute-start(bf16[48,512]{1,0:T(8,128)(2,1)S(1)} %get-tuple-element.101), channel_id=1, source_target_pairs={{0,14},{1,15},{2,12},{3,13},{4,10},{5,11},{6,8},{7,9},{8,6},{9,7},... | collective-permute-start | bytes 147464 | tf_op jit(solution)/shard_map/ppermute | solution.py:454
  75.0 6.6 %collective-permute-start.31 = (bf16[48,512]{1,0:T(8,128)(2,1)S(1)}, bf16[48,512]{1,0:T(8,128)(2,1)S(1)}, u32[]{:S(2)}, u32[]{:S(2)}) collective-permute-start(bf16[48,512]{1,0:T(8,128)(2,1)S(1)} %get-tuple-element.102), channel_id=1, source_target_pairs={{0,8},{1,9},{2,10},{3,11},{4,12},{5,13},{6,14},{7,15},{8,0},{9,1},... | collective-permute-start | bytes 147464 | tf_op jit(solution)/shard_map/ppermute | solution.py:454
  75.0 8.8 %collective-permute-start.32 = (bf16[48,512]{1,0:T(8,128)(2,1)S(1)}, bf16[48,512]{1,0:T(8,128)(2,1)S(1)}, u32[]{:S(2)}, u32[]{:S(2)}) collective-permute-start(bf16[48,512]{1,0:T(8,128)(2,1)S(1)} %get-tuple-element.103), channel_id=1, source_target_pairs={{0,10},{1,11},{2,8},{3,9},{4,14},{5,15},{6,12},{7,13},{8,2},{9,3},... | collective-permute-start | bytes 147464 | tf_op jit(solution)/shard_map/ppermute | solution.py:454
  78.1 5.7 %collective-permute-start.33 = (bf16[48,512]{1,0:T(8,128)(2,1)S(1)}, bf16[48,512]{1,0:T(8,128)(2,1)S(1)}, u32[]{:S(2)}, u32[]{:S(2)}) collective-permute-start(bf16[48,512]{1,0:T(8,128)(2,1)S(1)} %get-tuple-element.104), channel_id=1, source_target_pairs={{0,4},{1,5},{2,6},{3,7},{4,0},{5,1},{6,2},{7,3},{8,12},{9,13},{10,... | collective-permute-start | bytes 147464 | tf_op jit(solution)/shard_map/ppermute | solution.py:454
  (15 other events, 74.4 us)

commit v15 on v14

--- a/solution.py
+++ b/solution.py
@@ -290,8 +290,6 @@
     acts, grads, own = after(acts, grads, own)
     acts_got = lax.ppermute(acts, "blk", xor_pairs(n, 2))
     grads_got = lax.ppermute(grads, "blk", xor_pairs(n, 2))
-    right, left = [own, to_right(own)], [own, to_left(own)]
-
     acts = jnp.concatenate([acts, acts_got], axis=0)
     rotated = pl.pallas_call(
         functools.partial(rotate_in_kernel, tok_rows),
@@ -314,20 +312,14 @@
             name="stack",
         )(x, lax.ppermute(x, "blk", xor_pairs(n, key)))
 
-    own_far = swap(own, n)
-    grads_got, rotated, right[-1], left[-1], own_far = after(
-        grads_got, rotated, right[-1], left[-1], own_far
-    )
+    rotated, own = after(rotated, own)
+    right, left = [own, to_right(own)], [own, to_left(own)]
+    grads_got, rotated = after(grads_got, rotated)
     rotated = doubled(rotated[None], 4)
-    near = [right[0], right[1], left[1]]
-    while len(right) < steps - 1:
-        right.append(to_right(right[-1]))
-        left.append(to_left(left[-1]))
     grads = jnp.concatenate([grads, grads_got], axis=0)
     grads_far = swap(grads, n)
-    far = [swap(piece, n) for piece in near[1:]]
-    grads, grads_far, rotated, *far = after(grads, grads_far, rotated, *far)
-    far = [own_far, *far]
+    grads, grads_far, rotated = after(grads, grads_far, rotated)
+    far = [swap(own, n)]
     key = 8
     while key < n:
         rotated = doubled(rotated, key)
@@ -355,11 +347,10 @@
         grads_far,
         basis_out,
     )
-    start, grads, right[-1], left[-1], rotated = after(
-        start, grads, right[-1], left[-1], rotated
+    start, grads, right[-1], left[-1], rotated, *far = after(
+        start, grads, right[-1], left[-1], rotated, *far
     )
     rotated = doubled(rotated, 2)
-    near += [right[-1], left[-1]]
     far += [swap(right[-1], n), swap(left[-1], n)]
     right.append(to_right(right[-1]))
     left.append(to_left(left[-1]))
@@ -382,10 +373,9 @@
     aligned, right[-1], left[-1], rotated, *far = after(
         aligned, right[-1], left[-1], rotated, *far
     )
-    cut = in_width // 2
-    last = [to_right(right[-1][:cut]), to_left(left[-1][cut:])]
-    near += [right[-1], left[-1]]
-    far += [swap(piece, n) for piece in near[len(far) :]]
+    far += [swap(right[-1], n), swap(left[-1], n)]
+    right.append(to_right(right[-1]))
+    left.append(to_left(left[-1]))
     begun = [0] + [at for step in range(1, steps) for at in (step, chips - step)] + [steps]
     blocks = 8
     scaled = pl.pallas_call(
@@ -403,10 +393,11 @@
         name="scale",
     )(aligned, rotated, swap(rotated, n), tile_order, eigenvalues)
 
-    scaled, *last = after(scaled, *last, *far[-2:])
-    far[-2:] = last[2:]
-    last = last[:2]
-    last += [swap(piece, n) for piece in last]
+    scaled, right[-1], left[-1], *far = after(scaled, right[-1], left[-1], *far)
+    cut = in_width // 2
+    last = [to_right(right[-1][:cut]), to_left(left[-1][cut:])]
+    near = [right[at] if at < steps else left[chips - at] for at in begun[:-1]]
+    far += [swap(piece, n) for piece in near[len(far) :]]
     pieces = [piece for pair in zip(near, far) for piece in pair]
     projected, window = pl.pallas_call(
         functools.partial(project_kernel, (0, 6, len(pieces))),
@@ -425,6 +416,8 @@
         name="project",
     )(scaled, basis_out, *pieces)
 
+    projected, *last = after(projected, *last)
+    last += [swap(piece, n) for piece in last]
     rows = WR // n
     send, keep = pl.pallas_call(
         functools.partial(window_kernel, 1.0 / tokens),

time: 86.2 us -> 86.9 us (level)
    ppermute x1, waiting for transfers between devices: 7.61 us -> 0.01 us  [ring_body(): grads_got = lax.ppermute(grads, 'blk', xor_pairs(n, 2))]
    ppermute x1, waiting for transfers between devices: 0.03 us -> 2.89 us  [ring_body(): acts_got = lax.ppermute(acts, 'blk', xor_pairs(n, 2))]
    ppermute x13, waiting for transfers between devices: 2.57 us -> 5.17 us  [swap(): return lax.ppermute(x, 'blk', xor_pairs(n, 1))]
    ppermute x3, waiting for transfers between devices: 4.07 us -> 6.41 us  [doubled(): lax.ppermute(x, 'blk', xor_pairs(n, key))]
    ppermute x3, starting transfers between devices: 2.29 us -> 3.96 us  [doubled(): lax.ppermute(x, 'blk', xor_pairs(n, key))]
    ppermute x7, waiting for transfers between devices: 3.94 us -> 2.56 us  [ring_body(): lax.ppermute(x, 'blk', xor_pairs(n, 2 * key))]
    ppermute x4, starting transfers between devices: 4.6 us -> 3.23 us  [ring_body(): to_left = lambda x: lax.ppermute(x, 'blk', shift_pairs(n, -1))]
  transfers between devices with their start and end apart: 36 -> 36, of which waited for: 12 -> 15; matrix products, arithmetic and copies ran while one was open for 2% -> 2% of each run, Pallas kernels for 26% -> 26%
where the time goes in v15:
time: 86.9 us; the launch traced here: 86.6 us
  starting transfers between devices  34.4 us (40%)
  Pallas kernels  25.2 us (29%)
  waiting for transfers between devices  22.6 us (26%)
  local copies, waits for them, and re-layouts  3.18 us (4%)
  other arithmetic  0.91 us (1%)
    ppermute x7, starting transfers between devices, ring_body(): lax.ppermute(x, 'blk', xor_pairs(n, 2 * key))  11.2 us
    pallas_call x2, Pallas kernels, ring_body(): pl.pallas_call(kernel, out_shape=jax.ShapeDtypeStruct(shape, dtype), in_s...  10.7 us
    pallas_call x1, Pallas kernels, ring_body(): pl.pallas_call(functools.partial(scale_kernel, begun), out_shape=jax.Shap...  7.04 us
    ppermute x3, waiting for transfers between devices, doubled(): lax.ppermute(x, 'blk', xor_pairs(n, key))  6.41 us
    ppermute x3, starting transfers between devices, ring_body(): lax.ppermute(both, 'blk', xor_pairs(n, 4 * key))  5.68 us
    ppermute x13, waiting for transfers between devices, swap(): return lax.ppermute(x, 'blk', xor_pairs(n, 1))  5.17 us
    ppermute x3, waiting for transfers between devices, ring_body(): lax.ppermute(both, 'blk', xor_pairs(n, 4 * key))  5.13 us
    ppermute x4, starting transfers between devices, ring_body(): to_right = lambda x: lax.ppermute(x, 'blk', shift_pairs(n, 1))  5.02 us
  transfers between devices with their start and end apart: 36, of which 15 were waited for; matrix products, arithmetic and copies ran while one was open for 2% of the time, Pallas kernels for 26%

profile of v15, /device:TPU:0, one launch (start us, length us, event | category | flops | bytes accessed | tf_op | source)
XLA Modules:
  0.0 86.6 jit_solution(8021517756573948898)
XLA Ops:
  0.9 3.1 %collective-permute-start = (bf16[1,2,18432]{2,1,0:T(2,128)(2,1)S(1)}, bf16[1,2,18432]{2,1,0:T(2,128)(2,1)S(1)}, u32[]{:S(2)}, u32[]{:S(2)}) collective-permute-start(bf16[1,2,18432]{2,1,0:T(2,128)(2,1)S(1)} %maximum_bitcast_fusion.refs_0_), channel_id=1, source_target_pairs={{0,4},{1,5},{2,6},{3,7},{4,0},{5,1},{6,2},{7,3},{8,12},{9,13},{10,... | collective-permute-start | bytes 221192 | tf_op jit(solution)/shard_map/ppermute | solution.py:276
  4.0 2.6 %collective-permute-start.1 = (bf16[1,2,18432]{2,1,0:T(2,128)(2,1)S(1)}, bf16[1,2,18432]{2,1,0:T(2,128)(2,1)S(1)}, u32[]{:S(2)}, u32[]{:S(2)}) collective-permute-start(bf16[1,2,18432]{2,1,0:T(2,128)(2,1)S(1)} %maximum_bitcast_fusion.refs_0_), channel_id=1, source_target_pairs={{0,8},{1,9},{2,10},{3,11},{4,12},{5,13},{6,14},{7,15},{8,0},{9,1},... | collective-permute-start | bytes 221192 | tf_op jit(solution)/shard_map/ppermute | solution.py:276
  7.7 4.1 %collective-permute-done.1.refs_2_ = bf16[1,2,18432]{2,1,0:T(2,128)(2,1)S(1)} collective-permute-done((bf16[1,2,18432]{2,1,0:T(2,128)(2,1)S(1)}, bf16[1,2,18432]{2,1,0:T(2,128)(2,1)S(1)}, u32[]{:S(2)}, u32[]{:S(2)}) %collective-permute-start.1) | collective-permute-done | bytes 73760 | tf_op jit(solution)/shard_map/ppermute | solution.py:276
  12.9 1.6 %collective-permute-start.4 = (bf16[4,2,4096]{2,1,0:T(2,128)(2,1)S(1)}, bf16[4,2,4096]{2,1,0:T(2,128)(2,1)S(1)}, u32[]{:S(2)}, u32[]{:S(2)}) collective-permute-start(bf16[4,2,4096]{2,1,0:T(2,128)(2,1)S(1)} %get-tuple-element.66), channel_id=1, source_target_pairs={{0,2},{1,3},{2,0},{3,1},{4,6},{5,7},{6,4},{7,5},{8,10},{9,11},{10,... | collective-permute-start | bytes 196616 | tf_op jit(solution)/shard_map/ppermute | solution.py:291
  15.1 2.9 %collective-permute-done.4 = bf16[4,2,4096]{2,1,0:T(2,128)(2,1)S(1)} collective-permute-done((bf16[4,2,4096]{2,1,0:T(2,128)(2,1)S(1)}, bf16[4,2,4096]{2,1,0:T(2,128)(2,1)S(1)}, u32[]{:S(2)}, u32[]{:S(2)}) %collective-permute-start.4) | collective-permute-done | bytes 65568 | tf_op jit(solution)/shard_map/ppermute | solution.py:291
  18.3 1.2 %collective-permute-done.5.far_ref = bf16[8,2,4096]{2,1,0:T(2,128)(2,1)S(1)} collective-permute-done((bf16[8,2,4096]{2,1,0:T(2,128)(2,1)S(1)}, bf16[8,2,4096]{2,1,0:T(2,128)(2,1)S(1)}, u32[]{:S(2)}, u32[]{:S(2)}) %collective-permute-start.5) | collective-permute-done | bytes 131104 | tf_op jit(solution)/shard_map/ppermute | solution.py:43
  19.4 1.6 %copy-done = bf16[4096,256]{1,0:T(8,128)(2,1)S(1)} copy-done((bf16[4096,256]{1,0:T(8,128)(2,1)S(1)}, bf16[4096,256]{1,0:T(8,128)(2,1)}, u32[]{:S(2)}) %copy-start) | copy-done | bytes 2097176
  25.5 6.4 %collective-permute-done.7.last_ref = bf16[1,32,256]{2,1,0:T(8,128)(2,1)S(1)} collective-permute-done((bf16[1,32,256]{2,1,0:T(8,128)(2,1)S(1)}, bf16[1,32,256]{2,1,0:T(8,128)(2,1)S(1)}, u32[]{:S(2)}, u32[]{:S(2)}) %collective-permute-start.7) | collective-permute-done | bytes 16416 | tf_op jit(solution)/shard_map/ppermute | solution.py:313
  31.9 1.3 %collective-permute-start.10 = (bf16[2,32,256]{2,1,0:T(8,128)(2,1)S(1)}, bf16[2,32,256]{2,1,0:T(8,128)(2,1)S(1)}, u32[]{:S(2)}, u32[]{:S(2)}) collective-permute-start(bf16[2,32,256]{2,1,0:T(8,128)(2,1)S(1)} %stack.3.first_ref), channel_id=1, source_target_pairs={{0,8},{1,9},{2,10},{3,11},{4,12},{5,13},{6,14},{7,15},{8,0},{9,1},... | collective-permute-start | bytes 98312 | tf_op jit(solution)/shard_map/ppermute | solution.py:313
  33.2 5.2 %rotate_first.1.start_ref = f32[32,896]{1,0:T(8,128)S(1)} custom-call(bf16[8,2,14336]{2,1,0:T(2,128)(2,1)S(1)} %constant_dynamic-update-slice_fusion.2.near_ref, bf16[8,2,14336]{2,1,0:T(2,128)(2,1)S(1)} %collective-permute-done.6.far_ref, bf16[14336,896]{1,0:T(8,128)(2,1)} %basis_out_ref.1), custom_call_target="tpu_custom_call" | custom-call | flops 1 | bytes 1 | tf_op jit(solution)/shard_map/rotate_first/pallas_call | solution.py:328
  38.8 1.7 %collective-permute-start.13 = (bf16[256,512]{1,0:T(8,128)(2,1)S(1)}, bf16[256,512]{1,0:T(8,128)(2,1)S(1)}, u32[]{:S(2)}, u32[]{:S(2)}) collective-permute-start(bf16[256,512]{1,0:T(8,128)(2,1)S(1)} %collective-permute-done.9.refs_4_), channel_id=1, source_target_pairs={{0,2},{1,3},{4,0},{5,1},{8,4},{9,5},{12,8},{13,9},{14,12},{15,13},... | collective-permute-start | bytes 786440 | tf_op jit(solution)/shard_map/ppermute | solution.py:269
  41.1 1.6 %collective-permute-start.14 = (bf16[4,32,256]{2,1,0:T(8,128)(2,1)S(1)}, bf16[4,32,256]{2,1,0:T(8,128)(2,1)S(1)}, u32[]{:S(2)}, u32[]{:S(2)}) collective-permute-start(bf16[4,32,256]{2,1,0:T(8,128)(2,1)S(1)} %stack.4.first_ref), channel_id=1, source_target_pairs={{0,2},{1,3},{2,0},{3,1},{4,6},{5,7},{6,4},{7,5},{8,10},{9,11},{10,... | collective-permute-start | bytes 196616 | tf_op jit(solution)/shard_map/ppermute | solution.py:313
  42.7 5.5 %rotate_last.1.aligned_ref = bf16[896,32]{1,0:T(8,128)(2,1)S(1)} custom-call(bf16[8,2,14336]{2,1,0:T(2,128)(2,1)S(1)} %constant_dynamic-update-slice_fusion.2.near_ref, bf16[8,2,14336]{2,1,0:T(2,128)(2,1)S(1)} %collective-permute-done.6.far_ref, bf16[14336,896]{1,0:T(8,128)(2,1)} %basis_out_ref.1, s32[16]{0:T(128)S(1)} %copy-done.2, ...), custom_call_target="tpu_custom_call" | custom-call | flops 1 | bytes 1 | tf_op jit(solution)/shard_map/rotate_last/pallas_call | solution.py:328
  48.2 1.8 %collective-permute-start.18 = (bf16[256,512]{1,0:T(8,128)(2,1)S(1)}, bf16[256,512]{1,0:T(8,128)(2,1)S(1)}, u32[]{:S(2)}, u32[]{:S(2)}) collective-permute-start(bf16[256,512]{1,0:T(8,128)(2,1)S(1)} %collective-permute-done.12.refs_6_), channel_id=1, source_target_pairs={{0,4},{1,5},{4,8},{5,9},{8,12},{9,13},{12,14},{13,15},{14,10},{15,... | collective-permute-start | bytes 786440 | tf_op jit(solution)/shard_map/ppermute | solution.py:268
  50.8 1.6 %collective-permute-done.17.far_ref = bf16[8,32,256]{2,1,0:T(8,128)(2,1)S(1)} collective-permute-done((bf16[8,32,256]{2,1,0:T(8,128)(2,1)S(1)}, bf16[8,32,256]{2,1,0:T(8,128)(2,1)S(1)}, u32[]{:S(2)}, u32[]{:S(2)}) %collective-permute-start.17) | collective-permute-done | bytes 131104 | tf_op jit(solution)/shard_map/ppermute | solution.py:43
  52.4 7.0 %scale.1.scaled_ref = bf16[896,4096]{1,0:T(8,128)(2,1)S(1)} custom-call(bf16[896,32]{1,0:T(8,128)(2,1)S(1)} %rotate_last.1.aligned_ref, bf16[8,32,256]{2,1,0:T(8,128)(2,1)S(1)} %stack.5.near_ref, bf16[8,32,256]{2,1,0:T(8,128)(2,1)S(1)} %collective-permute-done.17.far_ref, s32[32]{0:T(128)S(1)} %copy-done.1, f32[896,4096]{1,0:T(8,128)} %eigen_ref.1), custom_call_target="tpu_custom_call" | custom-call | flops 1 | bytes 1 | tf_op jit(solution)/shard_map/scale/pallas_call | solution.py:381
  60.1 1.8 %collective-permute-start.24 = (bf16[128,512]{1,0:T(8,128)(2,1)S(1)}, bf16[128,512]{1,0:T(8,128)(2,1)S(1)}, u32[]{:S(2)}, u32[]{:S(2)}) collective-permute-start(bf16[128,512]{1,0:T(8,128)(2,1)S(1)} %slice.10), channel_id=1, source_target_pairs={{0,4},{1,5},{4,8},{5,9},{8,12},{9,13},{12,14},{13,15},{14,10},{15,... | collective-permute-start | bytes 393224 | tf_op jit(solution)/shard_map/ppermute | solution.py:268
  62.2 4.5 %project.1 = (f32[896,512]{1,0:T(8,128)S(1)}, bf16[768,896]{1,0:T(8,128)(2,1)S(1)}) custom-call(bf16[896,4096]{1,0:T(8,128)(2,1)S(1)} %scale.1.scaled_ref, bf16[14336,896]{1,0:T(8,128)(2,1)} %basis_out_ref.1, bf16[256,512]{1,0:T(8,128)(2,1)S(1)} %bitcast.7, bf16[256,512]{1,0:T(8,128)(2,1)S(1)} %collective-permute-done.11.refs_1_, ...), custom_call_target="tpu_custom_call" | custom-call | flops 1 | bytes 1 | tf_op jit(solution)/shard_map/project/pallas_call | solution.py:402
  68.7 1.6 %window.1 = (bf16[8,48,512]{2,1,0:T(8,128)(2,1)S(1)}, f32[8,48,512]{2,1,0:T(8,128)S(1)}) custom-call(bf16[768,896]{1,0:T(8,128)(2,1)S(1)} %get-tuple-element.96.window_ref, bf16[896,4096]{1,0:T(8,128)(2,1)S(1)} %scale.1.scaled_ref, f32[896,512]{1,0:T(8,128)S(1)} %get-tuple-element.98.projected_ref, bf16[128,512]{1,0:T(8,128)(2,1)S(1)} %collective-permute-done.24.refs_0_, ...), custom_call_target="tpu_custom_call" | custom-call | flops 1 | bytes 1 | tf_op jit(solution)/shard_map/window/pallas_call | solution.py:422
  70.7 1.4 %collective-permute-done.28.got_ref = bf16[8,48,512]{2,1,0:T(8,128)(2,1)S(1)} collective-permute-done((bf16[8,48,512]{2,1,0:T(8,128)(2,1)S(1)}, bf16[8,48,512]{2,1,0:T(8,128)(2,1)S(1)}, u32[]{:S(2)}, u32[]{:S(2)}) %collective-permute-start.28) | collective-permute-done | bytes 393248 | tf_op jit(solution)/shard_map/ppermute | solution.py:43
  73.2 2.6 %collective-permute-start.30 = (bf16[48,512]{1,0:T(8,128)(2,1)S(1)}, bf16[48,512]{1,0:T(8,128)(2,1)S(1)}, u32[]{:S(2)}, u32[]{:S(2)}) collective-permute-start(bf16[48,512]{1,0:T(8,128)(2,1)S(1)} %get-tuple-element.105), channel_id=1, source_target_pairs={{0,14},{1,15},{2,12},{3,13},{4,10},{5,11},{6,8},{7,9},{8,6},{9,7},... | collective-permute-start | bytes 147464 | tf_op jit(solution)/shard_map/ppermute | solution.py:447
  75.8 4.0 %collective-permute-start.32 = (bf16[48,512]{1,0:T(8,128)(2,1)S(1)}, bf16[48,512]{1,0:T(8,128)(2,1)S(1)}, u32[]{:S(2)}, u32[]{:S(2)}) collective-permute-start(bf16[48,512]{1,0:T(8,128)(2,1)S(1)} %get-tuple-element.107), channel_id=1, source_target_pairs={{0,10},{1,11},{2,8},{3,9},{4,14},{5,15},{6,12},{7,13},{8,2},{9,3},... | collective-permute-start | bytes 147464 | tf_op jit(solution)/shard_map/ppermute | solution.py:447
  79.9 1.8 %collective-permute-start.34 = (bf16[48,512]{1,0:T(8,128)(2,1)S(1)}, bf16[48,512]{1,0:T(8,128)(2,1)S(1)}, u32[]{:S(2)}, u32[]{:S(2)}) collective-permute-start(bf16[48,512]{1,0:T(8,128)(2,1)S(1)} %get-tuple-element.109), channel_id=1, source_target_pairs={{0,6},{1,7},{2,4},{3,5},{4,2},{5,3},{6,0},{7,1},{8,14},{9,15},{10,... | collective-permute-start | bytes 147464 | tf_op jit(solution)/shard_map/ppermute | solution.py:447
  81.7 1.7 %collective-permute-start.35 = (bf16[48,512]{1,0:T(8,128)(2,1)S(1)}, bf16[48,512]{1,0:T(8,128)(2,1)S(1)}, u32[]{:S(2)}, u32[]{:S(2)}) collective-permute-start(bf16[48,512]{1,0:T(8,128)(2,1)S(1)} %get-tuple-element.110), channel_id=1, source_target_pairs={{0,2},{1,3},{2,0},{3,1},{4,6},{5,7},{6,4},{7,5},{8,10},{9,11},{10,... | collective-permute-start | bytes 147464 | tf_op jit(solution)/shard_map/ppermute | solution.py:447
  (75 shorter events, 17.8 us)
Async XLA Ops:
  0.9 6.8 %collective-permute-start = (bf16[1,2,18432]{2,1,0:T(2,128)(2,1)S(1)}, bf16[1,2,18432]{2,1,0:T(2,128)(2,1)S(1)}, u32[]{:S(2)}, u32[]{:S(2)}) collective-permute-start(bf16[1,2,18432]{2,1,0:T(2,128)(2,1)S(1)} %maximum_bitcast_fusion.refs_0_), channel_id=1, source_target_pairs={{0,4},{1,5},{2,6},{3,7},{4,0},{5,1},{6,2},{7,3},{8,12},{9,13},{10,... | collective-permute-start | bytes 221192 | tf_op jit(solution)/shard_map/ppermute | solution.py:276
  4.0 7.8 %collective-permute-start.1 = (bf16[1,2,18432]{2,1,0:T(2,128)(2,1)S(1)}, bf16[1,2,18432]{2,1,0:T(2,128)(2,1)S(1)}, u32[]{:S(2)}, u32[]{:S(2)}) collective-permute-start(bf16[1,2,18432]{2,1,0:T(2,128)(2,1)S(1)} %maximum_bitcast_fusion.refs_0_), channel_id=1, source_target_pairs={{0,8},{1,9},{2,10},{3,11},{4,12},{5,13},{6,14},{7,15},{8,0},{9,1},... | collective-permute-start | bytes 221192 | tf_op jit(solution)/shard_map/ppermute | solution.py:276
  6.6 6.3 %collective-permute-start.2 = (bf16[1,2,18432]{2,1,0:T(2,128)(2,1)S(1)}, bf16[1,2,18432]{2,1,0:T(2,128)(2,1)S(1)}, u32[]{:S(2)}, u32[]{:S(2)}) collective-permute-start(bf16[1,2,18432]{2,1,0:T(2,128)(2,1)S(1)} %maximum_bitcast_fusion.refs_0_), channel_id=1, source_target_pairs={{0,12},{1,13},{2,14},{3,15},{4,8},{5,9},{6,10},{7,11},{8,4},{9,5},... | collective-permute-start | bytes 221192 | tf_op jit(solution)/shard_map/ppermute | solution.py:276
  14.5 7.1 %collective-permute-start.3 = (bf16[4,2,14336]{2,1,0:T(2,128)(2,1)S(1)}, bf16[4,2,14336]{2,1,0:T(2,128)(2,1)S(1)}, u32[]{:S(2)}, u32[]{:S(2)}) collective-permute-start(bf16[4,2,14336]{2,1,0:T(2,128)(2,1)S(1)} %get-tuple-element.65), channel_id=1, source_target_pairs={{0,2},{1,3},{2,0},{3,1},{4,6},{5,7},{6,4},{7,5},{8,10},{9,11},{10,... | collective-permute-start | bytes 688136 | tf_op jit(solution)/shard_map/ppermute | solution.py:292
  21.8 10.1 %collective-permute-start.6 = (bf16[8,2,14336]{2,1,0:T(2,128)(2,1)S(1)}, bf16[8,2,14336]{2,1,0:T(2,128)(2,1)S(1)}, u32[]{:S(2)}, u32[]{:S(2)}) collective-permute-start(bf16[8,2,14336]{2,1,0:T(2,128)(2,1)S(1)} %constant_dynamic-update-slice_fusion.2.near_ref), channel_id=1, source_target_pairs={{0,1},{1,0},{2,3},{3,2},{4,5},{5,4},{6,7},{7,6},{8,9},{9,8},{10,11... | collective-permute-start | bytes 1376264 | tf_op jit(solution)/shard_map/ppermute | solution.py:43
  22.0 16.4 %collective-permute-start.11 = (bf16[256,512]{1,0:T(8,128)(2,1)S(1)}, bf16[256,512]{1,0:T(8,128)(2,1)S(1)}, u32[]{:S(2)}, u32[]{:S(2)}) collective-permute-start(bf16[256,512]{1,0:T(8,128)(2,1)S(1)} %bitcast.4), channel_id=1, source_target_pairs={{0,1},{1,0},{2,3},{3,2},{4,5},{5,4},{6,7},{7,6},{8,9},{9,8},{10,11... | collective-permute-start | bytes 786440 | tf_op jit(solution)/shard_map/ppermute | solution.py:43
  22.4 16.1 %collective-permute-start.8 = (bf16[256,512]{1,0:T(8,128)(2,1)S(1)}, bf16[256,512]{1,0:T(8,128)(2,1)S(1)}, u32[]{:S(2)}, u32[]{:S(2)}) collective-permute-start(bf16[256,512]{1,0:T(8,128)(2,1)S(1)} %bitcast.5), channel_id=1, source_target_pairs={{0,4},{1,5},{4,8},{5,9},{8,12},{9,13},{12,14},{13,15},{14,10},{15,... | collective-permute-start | bytes 786440 | tf_op jit(solution)/shard_map/ppermute | solution.py:268
  23.4 15.0 %collective-permute-start.9 = (bf16[256,512]{1,0:T(8,128)(2,1)S(1)}, bf16[256,512]{1,0:T(8,128)(2,1)S(1)}, u32[]{:S(2)}, u32[]{:S(2)}) collective-permute-start(bf16[256,512]{1,0:T(8,128)(2,1)S(1)} %bitcast.6), channel_id=1, source_target_pairs={{0,2},{1,3},{4,0},{5,1},{8,4},{9,5},{12,8},{13,9},{14,12},{15,13},... | collective-permute-start | bytes 786440 | tf_op jit(solution)/shard_map/ppermute | solution.py:269
  24.4 7.5 %collective-permute-start.7 = (bf16[1,32,256]{2,1,0:T(8,128)(2,1)S(1)}, bf16[1,32,256]{2,1,0:T(8,128)(2,1)S(1)}, u32[]{:S(2)}, u32[]{:S(2)}) collective-permute-start(bf16[1,32,256]{2,1,0:T(8,128)(2,1)S(1)} %bitcast.8), channel_id=1, source_target_pairs={{0,4},{1,5},{2,6},{3,7},{4,0},{5,1},{6,2},{7,3},{8,12},{9,13},{10,... | collective-permute-start | bytes 49160 | tf_op jit(solution)/shard_map/ppermute | solution.py:313
  31.9 6.5 %collective-permute-start.10 = (bf16[2,32,256]{2,1,0:T(8,128)(2,1)S(1)}, bf16[2,32,256]{2,1,0:T(8,128)(2,1)S(1)}, u32[]{:S(2)}, u32[]{:S(2)}) collective-permute-start(bf16[2,32,256]{2,1,0:T(8,128)(2,1)S(1)} %stack.3.first_ref), channel_id=1, source_target_pairs={{0,8},{1,9},{2,10},{3,11},{4,12},{5,13},{6,14},{7,15},{8,0},{9,1},... | collective-permute-start | bytes 98312 | tf_op jit(solution)/shard_map/ppermute | solution.py:313
  38.5 9.7 %collective-permute-start.12 = (bf16[256,512]{1,0:T(8,128)(2,1)S(1)}, bf16[256,512]{1,0:T(8,128)(2,1)S(1)}, u32[]{:S(2)}, u32[]{:S(2)}) collective-permute-start(bf16[256,512]{1,0:T(8,128)(2,1)S(1)} %collective-permute-done.8.refs_2_), channel_id=1, source_target_pairs={{0,4},{1,5},{4,8},{5,9},{8,12},{9,13},{12,14},{13,15},{14,10},{15,... | collective-permute-start | bytes 786440 | tf_op jit(solution)/shard_map/ppermute | solution.py:268
  38.8 9.4 %collective-permute-start.13 = (bf16[256,512]{1,0:T(8,128)(2,1)S(1)}, bf16[256,512]{1,0:T(8,128)(2,1)S(1)}, u32[]{:S(2)}, u32[]{:S(2)}) collective-permute-start(bf16[256,512]{1,0:T(8,128)(2,1)S(1)} %collective-permute-done.9.refs_4_), channel_id=1, source_target_pairs={{0,2},{1,3},{4,0},{5,1},{8,4},{9,5},{12,8},{13,9},{14,12},{15,13},... | collective-permute-start | bytes 786440 | tf_op jit(solution)/shard_map/ppermute | solution.py:269
  40.6 7.7 %collective-permute-start.15 = (bf16[256,512]{1,0:T(8,128)(2,1)S(1)}, bf16[256,512]{1,0:T(8,128)(2,1)S(1)}, u32[]{:S(2)}, u32[]{:S(2)}) collective-permute-start(bf16[256,512]{1,0:T(8,128)(2,1)S(1)} %collective-permute-done.8.refs_2_), channel_id=1, source_target_pairs={{0,1},{1,0},{2,3},{3,2},{4,5},{5,4},{6,7},{7,6},{8,9},{9,8},{10,11... | collective-permute-start | bytes 786440 | tf_op jit(solution)/shard_map/ppermute | solution.py:43
  40.6 7.7 %collective-permute-start.16 = (bf16[256,512]{1,0:T(8,128)(2,1)S(1)}, bf16[256,512]{1,0:T(8,128)(2,1)S(1)}, u32[]{:S(2)}, u32[]{:S(2)}) collective-permute-start(bf16[256,512]{1,0:T(8,128)(2,1)S(1)} %collective-permute-done.9.refs_4_), channel_id=1, source_target_pairs={{0,1},{1,0},{2,3},{3,2},{4,5},{5,4},{6,7},{7,6},{8,9},{9,8},{10,11... | collective-permute-start | bytes 786440 | tf_op jit(solution)/shard_map/ppermute | solution.py:43
  41.1 7.1 %collective-permute-start.14 = (bf16[4,32,256]{2,1,0:T(8,128)(2,1)S(1)}, bf16[4,32,256]{2,1,0:T(8,128)(2,1)S(1)}, u32[]{:S(2)}, u32[]{:S(2)}) collective-permute-start(bf16[4,32,256]{2,1,0:T(8,128)(2,1)S(1)} %stack.4.first_ref), channel_id=1, source_target_pairs={{0,2},{1,3},{2,0},{3,1},{4,6},{5,7},{6,4},{7,5},{8,10},{9,11},{10,... | collective-permute-start | bytes 196616 | tf_op jit(solution)/shard_map/ppermute | solution.py:313
  48.2 11.2 %collective-permute-start.18 = (bf16[256,512]{1,0:T(8,128)(2,1)S(1)}, bf16[256,512]{1,0:T(8,128)(2,1)S(1)}, u32[]{:S(2)}, u32[]{:S(2)}) collective-permute-start(bf16[256,512]{1,0:T(8,128)(2,1)S(1)} %collective-permute-done.12.refs_6_), channel_id=1, source_target_pairs={{0,4},{1,5},{4,8},{5,9},{8,12},{9,13},{12,14},{13,15},{14,10},{15,... | collective-permute-start | bytes 786440 | tf_op jit(solution)/shard_map/ppermute | solution.py:268
  50.0 9.4 %collective-permute-start.19 = (bf16[256,512]{1,0:T(8,128)(2,1)S(1)}, bf16[256,512]{1,0:T(8,128)(2,1)S(1)}, u32[]{:S(2)}, u32[]{:S(2)}) collective-permute-start(bf16[256,512]{1,0:T(8,128)(2,1)S(1)} %collective-permute-done.13.refs_8_), channel_id=1, source_target_pairs={{0,2},{1,3},{4,0},{5,1},{8,4},{9,5},{12,8},{13,9},{14,12},{15,13},... | collective-permute-start | bytes 786440 | tf_op jit(solution)/shard_map/ppermute | solution.py:269
  50.3 9.2 %collective-permute-start.20 = (bf16[256,512]{1,0:T(8,128)(2,1)S(1)}, bf16[256,512]{1,0:T(8,128)(2,1)S(1)}, u32[]{:S(2)}, u32[]{:S(2)}) collective-permute-start(bf16[256,512]{1,0:T(8,128)(2,1)S(1)} %collective-permute-done.12.refs_6_), channel_id=1, source_target_pairs={{0,1},{1,0},{2,3},{3,2},{4,5},{5,4},{6,7},{7,6},{8,9},{9,8},{10,11... | collective-permute-start | bytes 786440 | tf_op jit(solution)/shard_map/ppermute | solution.py:43
  50.3 9.2 %collective-permute-start.21 = (bf16[256,512]{1,0:T(8,128)(2,1)S(1)}, bf16[256,512]{1,0:T(8,128)(2,1)S(1)}, u32[]{:S(2)}, u32[]{:S(2)}) collective-permute-start(bf16[256,512]{1,0:T(8,128)(2,1)S(1)} %collective-permute-done.13.refs_8_), channel_id=1, source_target_pairs={{0,1},{1,0},{2,3},{3,2},{4,5},{5,4},{6,7},{7,6},{8,9},{9,8},{10,11... | collective-permute-start | bytes 786440 | tf_op jit(solution)/shard_map/ppermute | solution.py:43
  60.1 6.6 %collective-permute-start.24 = (bf16[128,512]{1,0:T(8,128)(2,1)S(1)}, bf16[128,512]{1,0:T(8,128)(2,1)S(1)}, u32[]{:S(2)}, u32[]{:S(2)}) collective-permute-start(bf16[128,512]{1,0:T(8,128)(2,1)S(1)} %slice.10), channel_id=1, source_target_pairs={{0,4},{1,5},{4,8},{5,9},{8,12},{9,13},{12,14},{13,15},{14,10},{15,... | collective-permute-start | bytes 393224 | tf_op jit(solution)/shard_map/ppermute | solution.py:268
  72.2 7.7 %collective-permute-start.29 = (bf16[48,512]{1,0:T(8,128)(2,1)S(1)}, bf16[48,512]{1,0:T(8,128)(2,1)S(1)}, u32[]{:S(2)}, u32[]{:S(2)}) collective-permute-start(bf16[48,512]{1,0:T(8,128)(2,1)S(1)} %get-tuple-element.104), channel_id=1, source_target_pairs={{0,12},{1,13},{2,14},{3,15},{4,8},{5,9},{6,10},{7,11},{8,4},{9,5},... | collective-permute-start | bytes 147464 | tf_op jit(solution)/shard_map/ppermute | solution.py:447
  73.2 8.4 %collective-permute-start.30 = (bf16[48,512]{1,0:T(8,128)(2,1)S(1)}, bf16[48,512]{1,0:T(8,128)(2,1)S(1)}, u32[]{:S(2)}, u32[]{:S(2)}) collective-permute-start(bf16[48,512]{1,0:T(8,128)(2,1)S(1)} %get-tuple-element.105), channel_id=1, source_target_pairs={{0,14},{1,15},{2,12},{3,13},{4,10},{5,11},{6,8},{7,9},{8,6},{9,7},... | collective-permute-start | bytes 147464 | tf_op jit(solution)/shard_map/ppermute | solution.py:447
  75.8 8.1 %collective-permute-start.31 = (bf16[48,512]{1,0:T(8,128)(2,1)S(1)}, bf16[48,512]{1,0:T(8,128)(2,1)S(1)}, u32[]{:S(2)}, u32[]{:S(2)}) collective-permute-start(bf16[48,512]{1,0:T(8,128)(2,1)S(1)} %get-tuple-element.106), channel_id=1, source_target_pairs={{0,8},{1,9},{2,10},{3,11},{4,12},{5,13},{6,14},{7,15},{8,0},{9,1},... | collective-permute-start | bytes 147464 | tf_op jit(solution)/shard_map/ppermute | solution.py:447
  75.8 8.3 %collective-permute-start.32 = (bf16[48,512]{1,0:T(8,128)(2,1)S(1)}, bf16[48,512]{1,0:T(8,128)(2,1)S(1)}, u32[]{:S(2)}, u32[]{:S(2)}) collective-permute-start(bf16[48,512]{1,0:T(8,128)(2,1)S(1)} %get-tuple-element.107), channel_id=1, source_target_pairs={{0,10},{1,11},{2,8},{3,9},{4,14},{5,15},{6,12},{7,13},{8,2},{9,3},... | collective-permute-start | bytes 147464 | tf_op jit(solution)/shard_map/ppermute | solution.py:447
  (15 other events, 64.6 us)

commit v16 on v15

--- a/solution.py
+++ b/solution.py
@@ -312,10 +312,9 @@
             name="stack",
         )(x, lax.ppermute(x, "blk", xor_pairs(n, key)))
 
-    rotated, own = after(rotated, own)
+    grads_got, rotated = after(grads_got, rotated)
+    rotated, own = after(doubled(rotated[None], 4), own)
     right, left = [own, to_right(own)], [own, to_left(own)]
-    grads_got, rotated = after(grads_got, rotated)
-    rotated = doubled(rotated[None], 4)
     grads = jnp.concatenate([grads, grads_got], axis=0)
     grads_far = swap(grads, n)
     grads, grads_far, rotated = after(grads, grads_far, rotated)

time: 86.9 us -> 86.2 us (level)
  starting transfers between devices: 34.4 us -> 33.3 us
    ppermute x4, starting transfers between devices: 3.23 us -> 5.74 us  [ring_body(): to_left = lambda x: lax.ppermute(x, 'blk', shift_pairs(n, -1))]
    ppermute x4, starting transfers between devices: 5.02 us -> 2.57 us  [ring_body(): to_right = lambda x: lax.ppermute(x, 'blk', shift_pairs(n, 1))]
    ppermute x7, waiting for transfers between devices: 2.56 us -> 4.05 us  [ring_body(): lax.ppermute(x, 'blk', xor_pairs(n, 2 * key))]
  transfers between devices with their start and end apart: 36 -> 36, of which waited for: 15 -> 14; matrix products, arithmetic and copies ran while one was open for 2% -> 2% of each run, Pallas kernels for 26% -> 27%
where the time goes in v16:
time: 86.2 us; the launch traced here: 86 us
  starting transfers between devices  33.3 us (39%)
  Pallas kernels  25.2 us (29%)
  waiting for transfers between devices  23.1 us (27%)
  local copies, waits for them, and re-layouts  3.18 us (4%)
  other arithmetic  0.91 us (1%)
    ppermute x7, starting transfers between devices, ring_body(): lax.ppermute(x, 'blk', xor_pairs(n, 2 * key))  11.2 us
    pallas_call x2, Pallas kernels, ring_body(): pl.pallas_call(kernel, out_shape=jax.ShapeDtypeStruct(shape, dtype), in_s...  10.7 us
    pallas_call x1, Pallas kernels, ring_body(): pl.pallas_call(functools.partial(scale_kernel, begun), out_shape=jax.Shap...  7.06 us
    ppermute x3, waiting for transfers between devices, doubled(): lax.ppermute(x, 'blk', xor_pairs(n, key))  5.79 us
    ppermute x4, starting transfers between devices, ring_body(): to_left = lambda x: lax.ppermute(x, 'blk', shift_pairs(n, -1))  5.74 us
    ppermute x3, starting transfers between devices, ring_body(): lax.ppermute(both, 'blk', xor_pairs(n, 4 * key))  5.68 us
    ppermute x13, waiting for transfers between devices, swap(): return lax.ppermute(x, 'blk', xor_pairs(n, 1))  5.17 us
    ppermute x3, waiting for transfers between devices, ring_body(): lax.ppermute(both, 'blk', xor_pairs(n, 4 * key))  5.13 us
  transfers between devices with their start and end apart: 36, of which 14 were waited for; matrix products, arithmetic and copies ran while one was open for 2% of the time, Pallas kernels for 27%

profile of v16, /device:TPU:0, one launch (start us, length us, event | category | flops | bytes accessed | tf_op | source)
XLA Modules:
  0.0 86.0 jit_solution(17426166594924615190)
XLA Ops:
  0.9 3.1 %collective-permute-start = (bf16[1,2,18432]{2,1,0:T(2,128)(2,1)S(1)}, bf16[1,2,18432]{2,1,0:T(2,128)(2,1)S(1)}, u32[]{:S(2)}, u32[]{:S(2)}) collective-permute-start(bf16[1,2,18432]{2,1,0:T(2,128)(2,1)S(1)} %maximum_bitcast_fusion.refs_0_), channel_id=1, source_target_pairs={{0,4},{1,5},{2,6},{3,7},{4,0},{5,1},{6,2},{7,3},{8,12},{9,13},{10,... | collective-permute-start | bytes 221192 | tf_op jit(solution)/shard_map/ppermute | solution.py:276
  4.0 2.6 %collective-permute-start.1 = (bf16[1,2,18432]{2,1,0:T(2,128)(2,1)S(1)}, bf16[1,2,18432]{2,1,0:T(2,128)(2,1)S(1)}, u32[]{:S(2)}, u32[]{:S(2)}) collective-permute-start(bf16[1,2,18432]{2,1,0:T(2,128)(2,1)S(1)} %maximum_bitcast_fusion.refs_0_), channel_id=1, source_target_pairs={{0,8},{1,9},{2,10},{3,11},{4,12},{5,13},{6,14},{7,15},{8,0},{9,1},... | collective-permute-start | bytes 221192 | tf_op jit(solution)/shard_map/ppermute | solution.py:276
  7.7 4.1 %collective-permute-done.1.refs_2_ = bf16[1,2,18432]{2,1,0:T(2,128)(2,1)S(1)} collective-permute-done((bf16[1,2,18432]{2,1,0:T(2,128)(2,1)S(1)}, bf16[1,2,18432]{2,1,0:T(2,128)(2,1)S(1)}, u32[]{:S(2)}, u32[]{:S(2)}) %collective-permute-start.1) | collective-permute-done | bytes 73760 | tf_op jit(solution)/shard_map/ppermute | solution.py:276
  12.9 1.6 %collective-permute-start.4 = (bf16[4,2,4096]{2,1,0:T(2,128)(2,1)S(1)}, bf16[4,2,4096]{2,1,0:T(2,128)(2,1)S(1)}, u32[]{:S(2)}, u32[]{:S(2)}) collective-permute-start(bf16[4,2,4096]{2,1,0:T(2,128)(2,1)S(1)} %get-tuple-element.66), channel_id=1, source_target_pairs={{0,2},{1,3},{2,0},{3,1},{4,6},{5,7},{6,4},{7,5},{8,10},{9,11},{10,... | collective-permute-start | bytes 196616 | tf_op jit(solution)/shard_map/ppermute | solution.py:291
  15.1 2.9 %collective-permute-done.4 = bf16[4,2,4096]{2,1,0:T(2,128)(2,1)S(1)} collective-permute-done((bf16[4,2,4096]{2,1,0:T(2,128)(2,1)S(1)}, bf16[4,2,4096]{2,1,0:T(2,128)(2,1)S(1)}, u32[]{:S(2)}, u32[]{:S(2)}) %collective-permute-start.4) | collective-permute-done | bytes 65568 | tf_op jit(solution)/shard_map/ppermute | solution.py:291
  19.4 1.6 %copy-done = bf16[4096,256]{1,0:T(8,128)(2,1)S(1)} copy-done((bf16[4096,256]{1,0:T(8,128)(2,1)S(1)}, bf16[4096,256]{1,0:T(8,128)(2,1)}, u32[]{:S(2)}) %copy-start) | copy-done | bytes 2097176
  23.1 2.7 %collective-permute-done.7.last_ref = bf16[1,32,256]{2,1,0:T(8,128)(2,1)S(1)} collective-permute-done((bf16[1,32,256]{2,1,0:T(8,128)(2,1)S(1)}, bf16[1,32,256]{2,1,0:T(8,128)(2,1)S(1)}, u32[]{:S(2)}, u32[]{:S(2)}) %collective-permute-start.7) | collective-permute-done | bytes 16416 | tf_op jit(solution)/shard_map/ppermute | solution.py:313
  27.9 2.0 %collective-permute-start.10 = (bf16[2,32,256]{2,1,0:T(8,128)(2,1)S(1)}, bf16[2,32,256]{2,1,0:T(8,128)(2,1)S(1)}, u32[]{:S(2)}, u32[]{:S(2)}) collective-permute-start(bf16[2,32,256]{2,1,0:T(8,128)(2,1)S(1)} %stack.3.first_ref), channel_id=1, source_target_pairs={{0,8},{1,9},{2,10},{3,11},{4,12},{5,13},{6,14},{7,15},{8,0},{9,1},... | collective-permute-start | bytes 98312 | tf_op jit(solution)/shard_map/ppermute | solution.py:313
  29.9 5.2 %rotate_first.1.start_ref = f32[32,896]{1,0:T(8,128)S(1)} custom-call(bf16[8,2,14336]{2,1,0:T(2,128)(2,1)S(1)} %constant_dynamic-update-slice_fusion.2.near_ref, bf16[8,2,14336]{2,1,0:T(2,128)(2,1)S(1)} %collective-permute-done.6.far_ref, bf16[14336,896]{1,0:T(8,128)(2,1)} %basis_out_ref.1), custom_call_target="tpu_custom_call" | custom-call | flops 1 | bytes 1 | tf_op jit(solution)/shard_map/rotate_first/pallas_call | solution.py:327
  35.1 2.5 %collective-permute-done.10.last_ref = bf16[2,32,256]{2,1,0:T(8,128)(2,1)S(1)} collective-permute-done((bf16[2,32,256]{2,1,0:T(8,128)(2,1)S(1)}, bf16[2,32,256]{2,1,0:T(8,128)(2,1)S(1)}, u32[]{:S(2)}, u32[]{:S(2)}) %collective-permute-start.10) | collective-permute-done | bytes 32800 | tf_op jit(solution)/shard_map/ppermute | solution.py:313
  37.8 1.9 %collective-permute-start.13 = (bf16[256,512]{1,0:T(8,128)(2,1)S(1)}, bf16[256,512]{1,0:T(8,128)(2,1)S(1)}, u32[]{:S(2)}, u32[]{:S(2)}) collective-permute-start(bf16[256,512]{1,0:T(8,128)(2,1)S(1)} %collective-permute-done.9.refs_4_), channel_id=1, source_target_pairs={{0,2},{1,3},{4,0},{5,1},{8,4},{9,5},{12,8},{13,9},{14,12},{15,13},... | collective-permute-start | bytes 786440 | tf_op jit(solution)/shard_map/ppermute | solution.py:269
  40.3 5.5 %rotate_last.1.aligned_ref = bf16[896,32]{1,0:T(8,128)(2,1)S(1)} custom-call(bf16[8,2,14336]{2,1,0:T(2,128)(2,1)S(1)} %constant_dynamic-update-slice_fusion.2.near_ref, bf16[8,2,14336]{2,1,0:T(2,128)(2,1)S(1)} %collective-permute-done.6.far_ref, bf16[14336,896]{1,0:T(8,128)(2,1)} %basis_out_ref.1, s32[16]{0:T(128)S(1)} %copy-done.2, ...), custom_call_target="tpu_custom_call" | custom-call | flops 1 | bytes 1 | tf_op jit(solution)/shard_map/rotate_last/pallas_call | solution.py:327
  47.1 1.4 %collective-permute-start.19 = (bf16[256,512]{1,0:T(8,128)(2,1)S(1)}, bf16[256,512]{1,0:T(8,128)(2,1)S(1)}, u32[]{:S(2)}, u32[]{:S(2)}) collective-permute-start(bf16[256,512]{1,0:T(8,128)(2,1)S(1)} %collective-permute-done.13.refs_8_), channel_id=1, source_target_pairs={{0,2},{1,3},{4,0},{5,1},{8,4},{9,5},{12,8},{13,9},{14,12},{15,13},... | collective-permute-start | bytes 786440 | tf_op jit(solution)/shard_map/ppermute | solution.py:269
  49.0 1.6 %collective-permute-done.17.far_ref = bf16[8,32,256]{2,1,0:T(8,128)(2,1)S(1)} collective-permute-done((bf16[8,32,256]{2,1,0:T(8,128)(2,1)S(1)}, bf16[8,32,256]{2,1,0:T(8,128)(2,1)S(1)}, u32[]{:S(2)}, u32[]{:S(2)}) %collective-permute-start.17) | collective-permute-done | bytes 131104 | tf_op jit(solution)/shard_map/ppermute | solution.py:43
  50.6 7.1 %scale.1.scaled_ref = bf16[896,4096]{1,0:T(8,128)(2,1)S(1)} custom-call(bf16[896,32]{1,0:T(8,128)(2,1)S(1)} %rotate_last.1.aligned_ref, bf16[8,32,256]{2,1,0:T(8,128)(2,1)S(1)} %stack.5.near_ref, bf16[8,32,256]{2,1,0:T(8,128)(2,1)S(1)} %collective-permute-done.17.far_ref, s32[32]{0:T(128)S(1)} %copy-done.1, f32[896,4096]{1,0:T(8,128)} %eigen_ref.1), custom_call_target="tpu_custom_call" | custom-call | flops 1 | bytes 1 | tf_op jit(solution)/shard_map/scale/pallas_call | solution.py:380
  59.0 1.4 %collective-permute-start.25 = (bf16[128,512]{1,0:T(8,128)(2,1)S(1)}, bf16[128,512]{1,0:T(8,128)(2,1)S(1)}, u32[]{:S(2)}, u32[]{:S(2)}) collective-permute-start(bf16[128,512]{1,0:T(8,128)(2,1)S(1)} %slice.11), channel_id=1, source_target_pairs={{0,2},{1,3},{4,0},{5,1},{8,4},{9,5},{12,8},{13,9},{14,12},{15,13},... | collective-permute-start | bytes 393224 | tf_op jit(solution)/shard_map/ppermute | solution.py:269
  60.4 4.5 %project.1 = (f32[896,512]{1,0:T(8,128)S(1)}, bf16[768,896]{1,0:T(8,128)(2,1)S(1)}) custom-call(bf16[896,4096]{1,0:T(8,128)(2,1)S(1)} %scale.1.scaled_ref, bf16[14336,896]{1,0:T(8,128)(2,1)} %basis_out_ref.1, bf16[256,512]{1,0:T(8,128)(2,1)S(1)} %bitcast.7, bf16[256,512]{1,0:T(8,128)(2,1)S(1)} %collective-permute-done.11.refs_1_, ...), custom_call_target="tpu_custom_call" | custom-call | flops 1 | bytes 1 | tf_op jit(solution)/shard_map/project/pallas_call | solution.py:401
  66.5 1.6 %window.1 = (bf16[8,48,512]{2,1,0:T(8,128)(2,1)S(1)}, f32[8,48,512]{2,1,0:T(8,128)S(1)}) custom-call(bf16[768,896]{1,0:T(8,128)(2,1)S(1)} %get-tuple-element.96.window_ref, bf16[896,4096]{1,0:T(8,128)(2,1)S(1)} %scale.1.scaled_ref, f32[896,512]{1,0:T(8,128)S(1)} %get-tuple-element.98.projected_ref, bf16[128,512]{1,0:T(8,128)(2,1)S(1)} %collective-permute-done.24.refs_0_, ...), custom_call_target="tpu_custom_call" | custom-call | flops 1 | bytes 1 | tf_op jit(solution)/shard_map/window/pallas_call | solution.py:421
  68.6 1.4 %collective-permute-done.28.got_ref = bf16[8,48,512]{2,1,0:T(8,128)(2,1)S(1)} collective-permute-done((bf16[8,48,512]{2,1,0:T(8,128)(2,1)S(1)}, bf16[8,48,512]{2,1,0:T(8,128)(2,1)S(1)}, u32[]{:S(2)}, u32[]{:S(2)}) %collective-permute-start.28) | collective-permute-done | bytes 393248 | tf_op jit(solution)/shard_map/ppermute | solution.py:43
  70.0 2.7 %collective-permute-start.29 = (bf16[48,512]{1,0:T(8,128)(2,1)S(1)}, bf16[48,512]{1,0:T(8,128)(2,1)S(1)}, u32[]{:S(2)}, u32[]{:S(2)}) collective-permute-start(bf16[48,512]{1,0:T(8,128)(2,1)S(1)} %get-tuple-element.104), channel_id=1, source_target_pairs={{0,12},{1,13},{2,14},{3,15},{4,8},{5,9},{6,10},{7,11},{8,4},{9,5},... | collective-permute-start | bytes 147464 | tf_op jit(solution)/shard_map/ppermute | solution.py:446
  72.8 2.3 %collective-permute-start.30 = (bf16[48,512]{1,0:T(8,128)(2,1)S(1)}, bf16[48,512]{1,0:T(8,128)(2,1)S(1)}, u32[]{:S(2)}, u32[]{:S(2)}) collective-permute-start(bf16[48,512]{1,0:T(8,128)(2,1)S(1)} %get-tuple-element.105), channel_id=1, source_target_pairs={{0,14},{1,15},{2,12},{3,13},{4,10},{5,11},{6,8},{7,9},{8,6},{9,7},... | collective-permute-start | bytes 147464 | tf_op jit(solution)/shard_map/ppermute | solution.py:446
  75.0 2.7 %collective-permute-start.32 = (bf16[48,512]{1,0:T(8,128)(2,1)S(1)}, bf16[48,512]{1,0:T(8,128)(2,1)S(1)}, u32[]{:S(2)}, u32[]{:S(2)}) collective-permute-start(bf16[48,512]{1,0:T(8,128)(2,1)S(1)} %get-tuple-element.107), channel_id=1, source_target_pairs={{0,10},{1,11},{2,8},{3,9},{4,14},{5,15},{6,12},{7,13},{8,2},{9,3},... | collective-permute-start | bytes 147464 | tf_op jit(solution)/shard_map/ppermute | solution.py:446
  78.1 2.8 %collective-permute-start.34 = (bf16[48,512]{1,0:T(8,128)(2,1)S(1)}, bf16[48,512]{1,0:T(8,128)(2,1)S(1)}, u32[]{:S(2)}, u32[]{:S(2)}) collective-permute-start(bf16[48,512]{1,0:T(8,128)(2,1)S(1)} %get-tuple-element.109), channel_id=1, source_target_pairs={{0,6},{1,7},{2,4},{3,5},{4,2},{5,3},{6,0},{7,1},{8,14},{9,15},{10,... | collective-permute-start | bytes 147464 | tf_op jit(solution)/shard_map/ppermute | solution.py:446
  81.2 2.2 %collective-permute-done.32.refs_3_ = bf16[48,512]{1,0:T(8,128)(2,1)S(1)} collective-permute-done((bf16[48,512]{1,0:T(8,128)(2,1)S(1)}, bf16[48,512]{1,0:T(8,128)(2,1)S(1)}, u32[]{:S(2)}, u32[]{:S(2)}) %collective-permute-start.32) | collective-permute-done | bytes 49184 | tf_op jit(solution)/shard_map/ppermute | solution.py:446
  (75 shorter events, 18.3 us)
Async XLA Ops:
  0.9 6.8 %collective-permute-start = (bf16[1,2,18432]{2,1,0:T(2,128)(2,1)S(1)}, bf16[1,2,18432]{2,1,0:T(2,128)(2,1)S(1)}, u32[]{:S(2)}, u32[]{:S(2)}) collective-permute-start(bf16[1,2,18432]{2,1,0:T(2,128)(2,1)S(1)} %maximum_bitcast_fusion.refs_0_), channel_id=1, source_target_pairs={{0,4},{1,5},{2,6},{3,7},{4,0},{5,1},{6,2},{7,3},{8,12},{9,13},{10,... | collective-permute-start | bytes 221192 | tf_op jit(solution)/shard_map/ppermute | solution.py:276
  4.0 7.8 %collective-permute-start.1 = (bf16[1,2,18432]{2,1,0:T(2,128)(2,1)S(1)}, bf16[1,2,18432]{2,1,0:T(2,128)(2,1)S(1)}, u32[]{:S(2)}, u32[]{:S(2)}) collective-permute-start(bf16[1,2,18432]{2,1,0:T(2,128)(2,1)S(1)} %maximum_bitcast_fusion.refs_0_), channel_id=1, source_target_pairs={{0,8},{1,9},{2,10},{3,11},{4,12},{5,13},{6,14},{7,15},{8,0},{9,1},... | collective-permute-start | bytes 221192 | tf_op jit(solution)/shard_map/ppermute | solution.py:276
  6.6 6.3 %collective-permute-start.2 = (bf16[1,2,18432]{2,1,0:T(2,128)(2,1)S(1)}, bf16[1,2,18432]{2,1,0:T(2,128)(2,1)S(1)}, u32[]{:S(2)}, u32[]{:S(2)}) collective-permute-start(bf16[1,2,18432]{2,1,0:T(2,128)(2,1)S(1)} %maximum_bitcast_fusion.refs_0_), channel_id=1, source_target_pairs={{0,12},{1,13},{2,14},{3,15},{4,8},{5,9},{6,10},{7,11},{8,4},{9,5},... | collective-permute-start | bytes 221192 | tf_op jit(solution)/shard_map/ppermute | solution.py:276
  14.5 7.1 %collective-permute-start.3 = (bf16[4,2,14336]{2,1,0:T(2,128)(2,1)S(1)}, bf16[4,2,14336]{2,1,0:T(2,128)(2,1)S(1)}, u32[]{:S(2)}, u32[]{:S(2)}) collective-permute-start(bf16[4,2,14336]{2,1,0:T(2,128)(2,1)S(1)} %get-tuple-element.65), channel_id=1, source_target_pairs={{0,2},{1,3},{2,0},{3,1},{4,6},{5,7},{6,4},{7,5},{8,10},{9,11},{10,... | collective-permute-start | bytes 688136 | tf_op jit(solution)/shard_map/ppermute | solution.py:292
  21.8 6.1 %collective-permute-start.6 = (bf16[8,2,14336]{2,1,0:T(2,128)(2,1)S(1)}, bf16[8,2,14336]{2,1,0:T(2,128)(2,1)S(1)}, u32[]{:S(2)}, u32[]{:S(2)}) collective-permute-start(bf16[8,2,14336]{2,1,0:T(2,128)(2,1)S(1)} %constant_dynamic-update-slice_fusion.2.near_ref), channel_id=1, source_target_pairs={{0,1},{1,0},{2,3},{3,2},{4,5},{5,4},{6,7},{7,6},{8,9},{9,8},{10,11... | collective-permute-start | bytes 1376264 | tf_op jit(solution)/shard_map/ppermute | solution.py:43
  25.8 11.9 %collective-permute-start.11 = (bf16[256,512]{1,0:T(8,128)(2,1)S(1)}, bf16[256,512]{1,0:T(8,128)(2,1)S(1)}, u32[]{:S(2)}, u32[]{:S(2)}) collective-permute-start(bf16[256,512]{1,0:T(8,128)(2,1)S(1)} %bitcast.4), channel_id=1, source_target_pairs={{0,1},{1,0},{2,3},{3,2},{4,5},{5,4},{6,7},{7,6},{8,9},{9,8},{10,11... | collective-permute-start | bytes 786440 | tf_op jit(solution)/shard_map/ppermute | solution.py:43
  25.8 11.9 %collective-permute-start.8 = (bf16[256,512]{1,0:T(8,128)(2,1)S(1)}, bf16[256,512]{1,0:T(8,128)(2,1)S(1)}, u32[]{:S(2)}, u32[]{:S(2)}) collective-permute-start(bf16[256,512]{1,0:T(8,128)(2,1)S(1)} %bitcast.5), channel_id=1, source_target_pairs={{0,4},{1,5},{4,8},{5,9},{8,12},{9,13},{12,14},{13,15},{14,10},{15,... | collective-permute-start | bytes 786440 | tf_op jit(solution)/shard_map/ppermute | solution.py:268
  26.9 10.8 %collective-permute-start.9 = (bf16[256,512]{1,0:T(8,128)(2,1)S(1)}, bf16[256,512]{1,0:T(8,128)(2,1)S(1)}, u32[]{:S(2)}, u32[]{:S(2)}) collective-permute-start(bf16[256,512]{1,0:T(8,128)(2,1)S(1)} %bitcast.6), channel_id=1, source_target_pairs={{0,2},{1,3},{4,0},{5,1},{8,4},{9,5},{12,8},{13,9},{14,12},{15,13},... | collective-permute-start | bytes 786440 | tf_op jit(solution)/shard_map/ppermute | solution.py:269
  27.9 9.8 %collective-permute-start.10 = (bf16[2,32,256]{2,1,0:T(8,128)(2,1)S(1)}, bf16[2,32,256]{2,1,0:T(8,128)(2,1)S(1)}, u32[]{:S(2)}, u32[]{:S(2)}) collective-permute-start(bf16[2,32,256]{2,1,0:T(8,128)(2,1)S(1)} %stack.3.first_ref), channel_id=1, source_target_pairs={{0,8},{1,9},{2,10},{3,11},{4,12},{5,13},{6,14},{7,15},{8,0},{9,1},... | collective-permute-start | bytes 98312 | tf_op jit(solution)/shard_map/ppermute | solution.py:313
  37.7 8.7 %collective-permute-start.12 = (bf16[256,512]{1,0:T(8,128)(2,1)S(1)}, bf16[256,512]{1,0:T(8,128)(2,1)S(1)}, u32[]{:S(2)}, u32[]{:S(2)}) collective-permute-start(bf16[256,512]{1,0:T(8,128)(2,1)S(1)} %collective-permute-done.8.refs_2_), channel_id=1, source_target_pairs={{0,4},{1,5},{4,8},{5,9},{8,12},{9,13},{12,14},{13,15},{14,10},{15,... | collective-permute-start | bytes 786440 | tf_op jit(solution)/shard_map/ppermute | solution.py:268
  37.8 8.6 %collective-permute-start.13 = (bf16[256,512]{1,0:T(8,128)(2,1)S(1)}, bf16[256,512]{1,0:T(8,128)(2,1)S(1)}, u32[]{:S(2)}, u32[]{:S(2)}) collective-permute-start(bf16[256,512]{1,0:T(8,128)(2,1)S(1)} %collective-permute-done.9.refs_4_), channel_id=1, source_target_pairs={{0,2},{1,3},{4,0},{5,1},{8,4},{9,5},{12,8},{13,9},{14,12},{15,13},... | collective-permute-start | bytes 786440 | tf_op jit(solution)/shard_map/ppermute | solution.py:269
  39.8 6.7 %collective-permute-start.15 = (bf16[256,512]{1,0:T(8,128)(2,1)S(1)}, bf16[256,512]{1,0:T(8,128)(2,1)S(1)}, u32[]{:S(2)}, u32[]{:S(2)}) collective-permute-start(bf16[256,512]{1,0:T(8,128)(2,1)S(1)} %collective-permute-done.8.refs_2_), channel_id=1, source_target_pairs={{0,1},{1,0},{2,3},{3,2},{4,5},{5,4},{6,7},{7,6},{8,9},{9,8},{10,11... | collective-permute-start | bytes 786440 | tf_op jit(solution)/shard_map/ppermute | solution.py:43
  39.8 6.7 %collective-permute-start.16 = (bf16[256,512]{1,0:T(8,128)(2,1)S(1)}, bf16[256,512]{1,0:T(8,128)(2,1)S(1)}, u32[]{:S(2)}, u32[]{:S(2)}) collective-permute-start(bf16[256,512]{1,0:T(8,128)(2,1)S(1)} %collective-permute-done.9.refs_4_), channel_id=1, source_target_pairs={{0,1},{1,0},{2,3},{3,2},{4,5},{5,4},{6,7},{7,6},{8,9},{9,8},{10,11... | collective-permute-start | bytes 786440 | tf_op jit(solution)/shard_map/ppermute | solution.py:43
  40.3 6.1 %collective-permute-start.14 = (bf16[4,32,256]{2,1,0:T(8,128)(2,1)S(1)}, bf16[4,32,256]{2,1,0:T(8,128)(2,1)S(1)}, u32[]{:S(2)}, u32[]{:S(2)}) collective-permute-start(bf16[4,32,256]{2,1,0:T(8,128)(2,1)S(1)} %stack.4.first_ref), channel_id=1, source_target_pairs={{0,2},{1,3},{2,0},{3,1},{4,6},{5,7},{6,4},{7,5},{8,10},{9,11},{10,... | collective-permute-start | bytes 196616 | tf_op jit(solution)/shard_map/ppermute | solution.py:313
  46.4 11.2 %collective-permute-start.18 = (bf16[256,512]{1,0:T(8,128)(2,1)S(1)}, bf16[256,512]{1,0:T(8,128)(2,1)S(1)}, u32[]{:S(2)}, u32[]{:S(2)}) collective-permute-start(bf16[256,512]{1,0:T(8,128)(2,1)S(1)} %collective-permute-done.12.refs_6_), channel_id=1, source_target_pairs={{0,4},{1,5},{4,8},{5,9},{8,12},{9,13},{12,14},{13,15},{14,10},{15,... | collective-permute-start | bytes 786440 | tf_op jit(solution)/shard_map/ppermute | solution.py:268
  47.1 10.6 %collective-permute-start.19 = (bf16[256,512]{1,0:T(8,128)(2,1)S(1)}, bf16[256,512]{1,0:T(8,128)(2,1)S(1)}, u32[]{:S(2)}, u32[]{:S(2)}) collective-permute-start(bf16[256,512]{1,0:T(8,128)(2,1)S(1)} %collective-permute-done.13.refs_8_), channel_id=1, source_target_pairs={{0,2},{1,3},{4,0},{5,1},{8,4},{9,5},{12,8},{13,9},{14,12},{15,13},... | collective-permute-start | bytes 786440 | tf_op jit(solution)/shard_map/ppermute | solution.py:269
  48.5 9.2 %collective-permute-start.20 = (bf16[256,512]{1,0:T(8,128)(2,1)S(1)}, bf16[256,512]{1,0:T(8,128)(2,1)S(1)}, u32[]{:S(2)}, u32[]{:S(2)}) collective-permute-start(bf16[256,512]{1,0:T(8,128)(2,1)S(1)} %collective-permute-done.12.refs_6_), channel_id=1, source_target_pairs={{0,1},{1,0},{2,3},{3,2},{4,5},{5,4},{6,7},{7,6},{8,9},{9,8},{10,11... | collective-permute-start | bytes 786440 | tf_op jit(solution)/shard_map/ppermute | solution.py:43
  48.5 9.2 %collective-permute-start.21 = (bf16[256,512]{1,0:T(8,128)(2,1)S(1)}, bf16[256,512]{1,0:T(8,128)(2,1)S(1)}, u32[]{:S(2)}, u32[]{:S(2)}) collective-permute-start(bf16[256,512]{1,0:T(8,128)(2,1)S(1)} %collective-permute-done.13.refs_8_), channel_id=1, source_target_pairs={{0,1},{1,0},{2,3},{3,2},{4,5},{5,4},{6,7},{7,6},{8,9},{9,8},{10,11... | collective-permute-start | bytes 786440 | tf_op jit(solution)/shard_map/ppermute | solution.py:43
  58.3 6.6 %collective-permute-start.24 = (bf16[128,512]{1,0:T(8,128)(2,1)S(1)}, bf16[128,512]{1,0:T(8,128)(2,1)S(1)}, u32[]{:S(2)}, u32[]{:S(2)}) collective-permute-start(bf16[128,512]{1,0:T(8,128)(2,1)S(1)} %slice.10), channel_id=1, source_target_pairs={{0,4},{1,5},{4,8},{5,9},{8,12},{9,13},{12,14},{13,15},{14,10},{15,... | collective-permute-start | bytes 393224 | tf_op jit(solution)/shard_map/ppermute | solution.py:268
  70.0 8.0 %collective-permute-start.29 = (bf16[48,512]{1,0:T(8,128)(2,1)S(1)}, bf16[48,512]{1,0:T(8,128)(2,1)S(1)}, u32[]{:S(2)}, u32[]{:S(2)}) collective-permute-start(bf16[48,512]{1,0:T(8,128)(2,1)S(1)} %get-tuple-element.104), channel_id=1, source_target_pairs={{0,12},{1,13},{2,14},{3,15},{4,8},{5,9},{6,10},{7,11},{8,4},{9,5},... | collective-permute-start | bytes 147464 | tf_op jit(solution)/shard_map/ppermute | solution.py:446
  72.8 8.1 %collective-permute-start.30 = (bf16[48,512]{1,0:T(8,128)(2,1)S(1)}, bf16[48,512]{1,0:T(8,128)(2,1)S(1)}, u32[]{:S(2)}, u32[]{:S(2)}) collective-permute-start(bf16[48,512]{1,0:T(8,128)(2,1)S(1)} %get-tuple-element.105), channel_id=1, source_target_pairs={{0,14},{1,15},{2,12},{3,13},{4,10},{5,11},{6,8},{7,9},{8,6},{9,7},... | collective-permute-start | bytes 147464 | tf_op jit(solution)/shard_map/ppermute | solution.py:446
  75.0 6.2 %collective-permute-start.31 = (bf16[48,512]{1,0:T(8,128)(2,1)S(1)}, bf16[48,512]{1,0:T(8,128)(2,1)S(1)}, u32[]{:S(2)}, u32[]{:S(2)}) collective-permute-start(bf16[48,512]{1,0:T(8,128)(2,1)S(1)} %get-tuple-element.106), channel_id=1, source_target_pairs={{0,8},{1,9},{2,10},{3,11},{4,12},{5,13},{6,14},{7,15},{8,0},{9,1},... | collective-permute-start | bytes 147464 | tf_op jit(solution)/shard_map/ppermute | solution.py:446
  75.0 8.4 %collective-permute-start.32 = (bf16[48,512]{1,0:T(8,128)(2,1)S(1)}, bf16[48,512]{1,0:T(8,128)(2,1)S(1)}, u32[]{:S(2)}, u32[]{:S(2)}) collective-permute-start(bf16[48,512]{1,0:T(8,128)(2,1)S(1)} %get-tuple-element.107), channel_id=1, source_target_pairs={{0,10},{1,11},{2,8},{3,9},{4,14},{5,15},{6,12},{7,13},{8,2},{9,3},... | collective-permute-start | bytes 147464 | tf_op jit(solution)/shard_map/ppermute | solution.py:446
  78.1 6.7 %collective-permute-start.34 = (bf16[48,512]{1,0:T(8,128)(2,1)S(1)}, bf16[48,512]{1,0:T(8,128)(2,1)S(1)}, u32[]{:S(2)}, u32[]{:S(2)}) collective-permute-start(bf16[48,512]{1,0:T(8,128)(2,1)S(1)} %get-tuple-element.109), channel_id=1, source_target_pairs={{0,6},{1,7},{2,4},{3,5},{4,2},{5,3},{6,0},{7,1},{8,14},{9,15},{10,... | collective-permute-start | bytes 147464 | tf_op jit(solution)/shard_map/ppermute | solution.py:446
  (15 other events, 66.9 us)

commit v17 on v16

--- a/solution.py
+++ b/solution.py
@@ -62,12 +62,9 @@
     return jnp.dot(order, rotated.astype(jnp.bfloat16), preferred_element_type=jnp.float32)
 
 
-def part_kernel(*refs):
-    grads_ref, acts_ref = refs[-2:]
-    first = grads_ref.shape[2]
-    for at, ref in enumerate(refs[:-2]):
-        grads_ref[at] = ref[0, :, :first]
-        acts_ref[at] = ref[0, :, first:]
+def lay_kernel(*refs):
+    for at, ref in enumerate(refs[:-1]):
+        refs[-1][at] = ref[...]
 
 
 def rotate_in_kernel(tok_rows, near_ref, far_ref, basis_ref, out_ref):
@@ -272,24 +269,27 @@
     own = basis_in[:WC].T
 
     pairs = chips // 2
-    both = jnp.concatenate([grad_out, activations], axis=1)[None]
-    got = [lax.ppermute(both, "blk", xor_pairs(n, 4 * key)) for key in range(1, pairs)]
-    both, own, *got = after(both, own, *got)
+
+    def along(x):
+        return [x] + [lax.ppermute(x, "blk", xor_pairs(n, 4 * key)) for key in range(1, pairs)]
+
+    def lay(blocks):
+        return pl.pallas_call(
+            lay_kernel,
+            out_shape=jax.ShapeDtypeStruct((pairs, *blocks[0].shape), jnp.bfloat16),
+            in_specs=[VMEM] * pairs,
+            out_specs=VMEM,
+            compiler_params=pltpu.CompilerParams(vmem_limit_bytes=8 * MIB),
+            cost_estimate=CHEAP,
+            name="lay",
+        )(*blocks)
+
+    acts = lay(along(activations))
+    acts_got = lax.ppermute(acts, "blk", xor_pairs(n, 2))
+    acts_got, *grads = after(acts_got, *along(grad_out))
+    grads = lay(grads)
+    grads_got = lax.ppermute(grads, "blk", xor_pairs(n, 2))
     depth, later = 1024, 7
-    grads, acts = pl.pallas_call(
-        part_kernel,
-        out_shape=(
-            jax.ShapeDtypeStruct((pairs, tok_rows, full_out), jnp.bfloat16),
-            jax.ShapeDtypeStruct((pairs, tok_rows, full_in), jnp.bfloat16),
-        ),
-        in_specs=[VMEM] * pairs,
-        out_specs=(VMEM, VMEM),
-        compiler_params=pltpu.CompilerParams(vmem_limit_bytes=8 * MIB),
-        name="part",
-    )(both, *got)
-    acts, grads, own = after(acts, grads, own)
-    acts_got = lax.ppermute(acts, "blk", xor_pairs(n, 2))
-    grads_got = lax.ppermute(grads, "blk", xor_pairs(n, 2))
     acts = jnp.concatenate([acts, acts_got], axis=0)
     rotated = pl.pallas_call(
         functools.partial(rotate_in_kernel, tok_rows),
@@ -301,7 +301,7 @@
         name="rotate_in",
     )(acts, swap(acts, n), basis_in)
 
-    def doubled(x, key):
+    def stack(x, got):
         return pl.pallas_call(
             stack_kernel,
             out_shape=jax.ShapeDtypeStruct((2 * x.shape[0], *x.shape[1:]), x.dtype),
@@ -310,19 +310,19 @@
             compiler_params=pltpu.CompilerParams(vmem_limit_bytes=8 * MIB),
             cost_estimate=CHEAP,
             name="stack",
-        )(x, lax.ppermute(x, "blk", xor_pairs(n, key)))
-
-    grads_got, rotated = after(grads_got, rotated)
-    rotated, own = after(doubled(rotated[None], 4), own)
+        )(x, got)
+
+    rotated = rotated[None]
+    key = 4
+    while key < n:
+        rotated = stack(rotated, lax.ppermute(rotated, "blk", xor_pairs(n, key)))
+        key *= 2
+    grads_got, rotated, own = after(grads_got, rotated, own)
     right, left = [own, to_right(own)], [own, to_left(own)]
     grads = jnp.concatenate([grads, grads_got], axis=0)
     grads_far = swap(grads, n)
-    grads, grads_far, rotated = after(grads, grads_far, rotated)
     far = [swap(own, n)]
-    key = 8
-    while key < n:
-        rotated = doubled(rotated, key)
-        key *= 2
+    rotated_got = lax.ppermute(rotated, "blk", xor_pairs(n, 2))
 
     rotate = lambda kernel, count, scratch, shape, dtype, *operands: pl.pallas_call(
         kernel,
@@ -346,10 +346,11 @@
         grads_far,
         basis_out,
     )
-    start, grads, right[-1], left[-1], rotated, *far = after(
-        start, grads, right[-1], left[-1], rotated, *far
-    )
-    rotated = doubled(rotated, 2)
+    start, grads, right[-1], left[-1], rotated_got, *far = after(
+        start, grads, right[-1], left[-1], rotated_got, *far
+    )
+    rotated = stack(rotated, rotated_got)
+    rotated_far = swap(rotated, n)
     far += [swap(right[-1], n), swap(left[-1], n)]
     right.append(to_right(right[-1]))
     left.append(to_left(left[-1]))
@@ -369,8 +370,8 @@
         start,
     )
 
-    aligned, right[-1], left[-1], rotated, *far = after(
-        aligned, right[-1], left[-1], rotated, *far
+    aligned, right[-1], left[-1], rotated_far, *far = after(
+        aligned, right[-1], left[-1], rotated_far, *far
     )
     far += [swap(right[-1], n), swap(left[-1], n)]
     right.append(to_right(right[-1]))
@@ -390,7 +391,7 @@
         compiler_params=pltpu.CompilerParams(vmem_limit_bytes=40 * MIB),
         cost_estimate=CHEAP,
         name="scale",
-    )(aligned, rotated, swap(rotated, n), tile_order, eigenvalues)
+    )(aligned, rotated, rotated_far, tile_order, eigenvalues)
 
     scaled, right[-1], left[-1], *far = after(scaled, right[-1], left[-1], *far)
     cut = in_width // 2

time: 86.2 us -> 92.9 us (1.078)
  starting transfers between devices: 33.3 us -> 37.6 us
  waiting for transfers between devices: 23.1 us -> 24.7 us
  local copies, waits for them, and re-layouts: 3.18 us -> 4.27 us
    ppermute x6 -> x9, waiting for transfers between devices: 10.9 us -> 15.7 us  [the longest x6 8.72 us: along(): lax.ppermute(x, 'blk', xor_pairs(n, 4 * key))]
    ppermute x6 -> x9, starting transfers between devices: 8.81 us -> 13.3 us  [the longest x6 10 us: along(): lax.ppermute(x, 'blk', xor_pairs(n, 4 * key))]
    ppermute x4, starting transfers between devices: 2.57 us -> 6.6 us  [ring_body(): to_right = lambda x: lax.ppermute(x, 'blk', shift_pairs(n, 1))]
    ppermute x4, starting transfers between devices: 5.74 us -> 2.31 us  [ring_body(): to_left = lambda x: lax.ppermute(x, 'blk', shift_pairs(n, -1))]
    ppermute x1, waiting for transfers between devices: 2.89 us -> 0.01 us  [ring_body(): acts_got = lax.ppermute(acts, 'blk', xor_pairs(n, 2))]
    ppermute x13, waiting for transfers between devices: 5.17 us -> 3.76 us  [swap(): return lax.ppermute(x, 'blk', xor_pairs(n, 1))]
    unnamed x9 -> x11, local copies, waits for them, and re-layouts: 1.95 us -> 3.28 us
    ppermute x4, waiting for transfers between devices: 0.01 us -> 1.02 us  [ring_body(): to_left = lambda x: lax.ppermute(x, 'blk', shift_pairs(n, -1))]
  transfers between devices with their start and end apart: 36 -> 39, of which waited for: 14 -> 18; matrix products, arithmetic and copies ran while one was open for 2% -> 1% of each run, Pallas kernels for 27% -> 25%
where the time goes in v17:
time: 92.9 us; the launch traced here: 92.6 us
  starting transfers between devices  37.6 us (40%)
  Pallas kernels  25.1 us (27%)
  waiting for transfers between devices  24.7 us (27%)
  local copies, waits for them, and re-layouts  4.27 us (5%)
    pallas_call x2, Pallas kernels, ring_body(): pl.pallas_call(kernel, out_shape=jax.ShapeDtypeStruct(shape, dtype), in_s...  10.7 us
    ppermute x7, starting transfers between devices, ring_body(): lax.ppermute(x, 'blk', xor_pairs(n, 2 * key))  10.6 us
    ppermute x6, starting transfers between devices, along(): lax.ppermute(x, 'blk', xor_pairs(n, 4 * key))  10 us
    ppermute x6, waiting for transfers between devices, along(): lax.ppermute(x, 'blk', xor_pairs(n, 4 * key))  8.72 us
    pallas_call x1, Pallas kernels, ring_body(): pl.pallas_call(functools.partial(scale_kernel, begun), out_shape=jax.Shap...  6.99 us
    ppermute x4, starting transfers between devices, ring_body(): to_right = lambda x: lax.ppermute(x, 'blk', shift_pairs(n, 1))  6.6 us
    ppermute x2, waiting for transfers between devices, ring_body(): rotated = stack(rotated, lax.ppermute(rotated, 'blk', xor_pairs(n, key)))  5.7 us
    pallas_call x1, Pallas kernels, ring_body(): pl.pallas_call(functools.partial(project_kernel, (0, 6, len(pieces))), ou...  4.4 us
  transfers between devices with their start and end apart: 39, of which 18 were waited for; matrix products, arithmetic and copies ran while one was open for 1% of the time, Pallas kernels for 25%

profile of v17, /device:TPU:0, one launch (start us, length us, event | category | flops | bytes accessed | tf_op | source)
XLA Modules:
  0.0 92.6 jit_solution(7606334941617121943)
XLA Ops:
  0.0 3.0 %collective-permute-start = (bf16[2,4096]{1,0:T(2,128)(2,1)}, bf16[2,4096]{1,0:T(2,128)(2,1)S(1)}, u32[]{:S(2)}, u32[]{:S(2)}) collective-permute-start(bf16[2,4096]{1,0:T(2,128)(2,1)} %refs_0_.1), channel_id=1, source_target_pairs={{0,4},{1,5},{2,6},{3,7},{4,0},{5,1},{6,2},{7,3},{8,12},{9,13},{10,... | collective-permute-start | bytes 49160 | tf_op jit(solution)/shard_map/ppermute | solution.py:274
  3.0 2.6 %collective-permute-start.1 = (bf16[2,4096]{1,0:T(2,128)(2,1)}, bf16[2,4096]{1,0:T(2,128)(2,1)S(1)}, u32[]{:S(2)}, u32[]{:S(2)}) collective-permute-start(bf16[2,4096]{1,0:T(2,128)(2,1)} %refs_0_.1), channel_id=1, source_target_pairs={{0,8},{1,9},{2,10},{3,11},{4,12},{5,13},{6,14},{7,15},{8,0},{9,1},... | collective-permute-start | bytes 49160 | tf_op jit(solution)/shard_map/ppermute | solution.py:274
  5.6 2.3 %collective-permute-done.1.refs_2_ = bf16[2,4096]{1,0:T(2,128)(2,1)S(1)} collective-permute-done((bf16[2,4096]{1,0:T(2,128)(2,1)}, bf16[2,4096]{1,0:T(2,128)(2,1)S(1)}, u32[]{:S(2)}, u32[]{:S(2)}) %collective-permute-start.1) | collective-permute-done | bytes 16416 | tf_op jit(solution)/shard_map/ppermute | solution.py:274
  8.0 3.4 %collective-permute-done.2.refs_3_ = bf16[2,4096]{1,0:T(2,128)(2,1)S(1)} collective-permute-done((bf16[2,4096]{1,0:T(2,128)(2,1)}, bf16[2,4096]{1,0:T(2,128)(2,1)S(1)}, u32[]{:S(2)}, u32[]{:S(2)}) %collective-permute-start.2) | collective-permute-done | bytes 16416 | tf_op jit(solution)/shard_map/ppermute | solution.py:274
  12.1 1.5 %collective-permute-start.3 = (bf16[4,2,4096]{2,1,0:T(2,128)(2,1)S(1)}, bf16[4,2,4096]{2,1,0:T(2,128)(2,1)S(1)}, u32[]{:S(2)}, u32[]{:S(2)}) collective-permute-start(bf16[4,2,4096]{2,1,0:T(2,128)(2,1)S(1)} %lay.2), channel_id=1, source_target_pairs={{0,2},{1,3},{2,0},{3,1},{4,6},{5,7},{6,4},{7,5},{8,10},{9,11},{10,... | collective-permute-start | bytes 196616 | tf_op jit(solution)/shard_map/ppermute | solution.py:288
  14.4 3.6 %collective-permute-start.6 = (bf16[2,14336]{1,0:T(2,128)(2,1)}, bf16[2,14336]{1,0:T(2,128)(2,1)S(1)}, u32[]{:S(2)}, u32[]{:S(2)}) collective-permute-start(bf16[2,14336]{1,0:T(2,128)(2,1)} %refs_0_.2), channel_id=1, source_target_pairs={{0,12},{1,13},{2,14},{3,15},{4,8},{5,9},{6,10},{7,11},{8,4},{9,5},... | collective-permute-start | bytes 172040 | tf_op jit(solution)/shard_map/ppermute | solution.py:274
  19.0 2.0 %collective-permute-done.6.refs_3_ = bf16[2,14336]{1,0:T(2,128)(2,1)S(1)} collective-permute-done((bf16[2,14336]{1,0:T(2,128)(2,1)}, bf16[2,14336]{1,0:T(2,128)(2,1)S(1)}, u32[]{:S(2)}, u32[]{:S(2)}) %collective-permute-start.6) | collective-permute-done | bytes 57376 | tf_op jit(solution)/shard_map/ppermute | solution.py:274
  22.6 1.3 %collective-permute-done.8.far_ref = bf16[8,2,4096]{2,1,0:T(2,128)(2,1)S(1)} collective-permute-done((bf16[8,2,4096]{2,1,0:T(2,128)(2,1)S(1)}, bf16[8,2,4096]{2,1,0:T(2,128)(2,1)S(1)}, u32[]{:S(2)}, u32[]{:S(2)}) %collective-permute-start.8) | collective-permute-done | bytes 131104 | tf_op jit(solution)/shard_map/ppermute | solution.py:43
  24.0 1.6 %copy-done = bf16[4096,256]{1,0:T(8,128)(2,1)S(1)} copy-done((bf16[4096,256]{1,0:T(8,128)(2,1)S(1)}, bf16[4096,256]{1,0:T(8,128)(2,1)}, u32[]{:S(2)}) %copy-start) | copy-done | bytes 2097176
  26.1 3.7 %collective-permute-done.9.last_ref = bf16[1,32,256]{2,1,0:T(8,128)(2,1)S(1)} collective-permute-done((bf16[1,32,256]{2,1,0:T(8,128)(2,1)S(1)}, bf16[1,32,256]{2,1,0:T(8,128)(2,1)S(1)}, u32[]{:S(2)}, u32[]{:S(2)}) %collective-permute-start.9) | collective-permute-done | bytes 16416 | tf_op jit(solution)/shard_map/ppermute | solution.py:318
  29.9 1.8 %collective-permute-start.10 = (bf16[2,32,256]{2,1,0:T(8,128)(2,1)S(1)}, bf16[2,32,256]{2,1,0:T(8,128)(2,1)S(1)}, u32[]{:S(2)}, u32[]{:S(2)}) collective-permute-start(bf16[2,32,256]{2,1,0:T(8,128)(2,1)S(1)} %stack.3.first_ref), channel_id=1, source_target_pairs={{0,8},{1,9},{2,10},{3,11},{4,12},{5,13},{6,14},{7,15},{8,0},{9,1},... | collective-permute-start | bytes 98312 | tf_op jit(solution)/shard_map/ppermute | solution.py:318
  32.8 2.0 %collective-permute-done.10.last_ref = bf16[2,32,256]{2,1,0:T(8,128)(2,1)S(1)} collective-permute-done((bf16[2,32,256]{2,1,0:T(8,128)(2,1)S(1)}, bf16[2,32,256]{2,1,0:T(8,128)(2,1)S(1)}, u32[]{:S(2)}, u32[]{:S(2)}) %collective-permute-start.10) | collective-permute-done | bytes 32800 | tf_op jit(solution)/shard_map/ppermute | solution.py:318
  37.5 1.5 %collective-permute-start.14 = (bf16[4,32,256]{2,1,0:T(8,128)(2,1)S(1)}, bf16[4,32,256]{2,1,0:T(8,128)(2,1)S(1)}, u32[]{:S(2)}, u32[]{:S(2)}) collective-permute-start(bf16[4,32,256]{2,1,0:T(8,128)(2,1)S(1)} %stack.4.first_ref), channel_id=1, source_target_pairs={{0,2},{1,3},{2,0},{3,1},{4,6},{5,7},{6,4},{7,5},{8,10},{9,11},{10,... | collective-permute-start | bytes 196616 | tf_op jit(solution)/shard_map/ppermute | solution.py:325
  39.0 5.2 %rotate_first.1.start_ref = f32[32,896]{1,0:T(8,128)S(1)} custom-call(bf16[8,2,14336]{2,1,0:T(2,128)(2,1)S(1)} %pad_maximum_fusion.near_ref, bf16[8,2,14336]{2,1,0:T(2,128)(2,1)S(1)} %collective-permute-done.11.far_ref, bf16[14336,896]{1,0:T(8,128)(2,1)} %basis_out_ref.1), custom_call_target="tpu_custom_call" | custom-call | flops 1 | bytes 1 | tf_op jit(solution)/shard_map/rotate_first/pallas_call | solution.py:327
  48.2 5.5 %rotate_last.1.aligned_ref = bf16[896,32]{1,0:T(8,128)(2,1)S(1)} custom-call(bf16[8,2,14336]{2,1,0:T(2,128)(2,1)S(1)} %pad_maximum_fusion.near_ref, bf16[8,2,14336]{2,1,0:T(2,128)(2,1)S(1)} %collective-permute-done.11.far_ref, bf16[14336,896]{1,0:T(8,128)(2,1)} %basis_out_ref.1, s32[16]{0:T(128)S(1)} %copy-done.4, f32[32,896]{1,0:T(8,128)S(1)} %rotate_first.1.start_ref), custom_call_target="tpu_custom_call" | custom-call | flops 1 | bytes 1 | tf_op jit(solution)/shard_map/rotate_last/pallas_call | solution.py:327
  54.0 2.7 %collective-permute-start.21 = (bf16[256,512]{1,0:T(8,128)(2,1)S(1)}, bf16[256,512]{1,0:T(8,128)(2,1)S(1)}, u32[]{:S(2)}, u32[]{:S(2)}) collective-permute-start(bf16[256,512]{1,0:T(8,128)(2,1)S(1)} %collective-permute-done.16.refs_6_), channel_id=1, source_target_pairs={{0,4},{1,5},{4,8},{5,9},{8,12},{9,13},{12,14},{13,15},{14,10},{15,... | collective-permute-start | bytes 786440 | tf_op jit(solution)/shard_map/ppermute | solution.py:265
  57.2 7.0 %scale.1.scaled_ref = bf16[896,4096]{1,0:T(8,128)(2,1)S(1)} custom-call(bf16[896,32]{1,0:T(8,128)(2,1)S(1)} %rotate_last.1.aligned_ref, bf16[8,32,256]{2,1,0:T(8,128)(2,1)S(1)} %stack.5.near_ref, bf16[8,32,256]{2,1,0:T(8,128)(2,1)S(1)} %collective-permute-done.18.far_ref, s32[32]{0:T(128)S(1)} %copy-done.3, f32[896,4096]{1,0:T(8,128)} %eigen_ref.1), custom_call_target="tpu_custom_call" | custom-call | flops 1 | bytes 1 | tf_op jit(solution)/shard_map/scale/pallas_call | solution.py:381
  64.9 2.1 %collective-permute-start.27 = (bf16[128,512]{1,0:T(8,128)(2,1)S(1)}, bf16[128,512]{1,0:T(8,128)(2,1)S(1)}, u32[]{:S(2)}, u32[]{:S(2)}) collective-permute-start(bf16[128,512]{1,0:T(8,128)(2,1)S(1)} %slice.10), channel_id=1, source_target_pairs={{0,4},{1,5},{4,8},{5,9},{8,12},{9,13},{12,14},{13,15},{14,10},{15,... | collective-permute-start | bytes 393224 | tf_op jit(solution)/shard_map/ppermute | solution.py:265
  67.0 4.4 %project.1 = (f32[896,512]{1,0:T(8,128)S(1)}, bf16[768,896]{1,0:T(8,128)(2,1)S(1)}) custom-call(bf16[896,4096]{1,0:T(8,128)(2,1)S(1)} %scale.1.scaled_ref, bf16[14336,896]{1,0:T(8,128)(2,1)} %basis_out_ref.1, bf16[256,512]{1,0:T(8,128)(2,1)S(1)} %bitcast.5, bf16[256,512]{1,0:T(8,128)(2,1)S(1)} %collective-permute-done.15.refs_1_, ...), custom_call_target="tpu_custom_call" | custom-call | flops 1 | bytes 1 | tf_op jit(solution)/shard_map/project/pallas_call | solution.py:402
  73.7 1.6 %window.1 = (bf16[8,48,512]{2,1,0:T(8,128)(2,1)S(1)}, f32[8,48,512]{2,1,0:T(8,128)S(1)}) custom-call(bf16[768,896]{1,0:T(8,128)(2,1)S(1)} %get-tuple-element.78.window_ref, bf16[896,4096]{1,0:T(8,128)(2,1)S(1)} %scale.1.scaled_ref, f32[896,512]{1,0:T(8,128)S(1)} %get-tuple-element.80.projected_ref, bf16[128,512]{1,0:T(8,128)(2,1)S(1)} %collective-permute-done.27.refs_0_, ...), custom_call_target="tpu_custom_call" | custom-call | flops 1 | bytes 1 | tf_op jit(solution)/shard_map/window/pallas_call | solution.py:422
  75.7 1.4 %collective-permute-done.31.got_ref = bf16[8,48,512]{2,1,0:T(8,128)(2,1)S(1)} collective-permute-done((bf16[8,48,512]{2,1,0:T(8,128)(2,1)S(1)}, bf16[8,48,512]{2,1,0:T(8,128)(2,1)S(1)}, u32[]{:S(2)}, u32[]{:S(2)}) %collective-permute-start.31) | collective-permute-done | bytes 393248 | tf_op jit(solution)/shard_map/ppermute | solution.py:43
  77.2 3.0 %collective-permute-start.32 = (bf16[48,512]{1,0:T(8,128)(2,1)S(1)}, bf16[48,512]{1,0:T(8,128)(2,1)S(1)}, u32[]{:S(2)}, u32[]{:S(2)}) collective-permute-start(bf16[48,512]{1,0:T(8,128)(2,1)S(1)} %get-tuple-element.86), channel_id=1, source_target_pairs={{0,12},{1,13},{2,14},{3,15},{4,8},{5,9},{6,10},{7,11},{8,4},{9,5},... | collective-permute-start | bytes 147464 | tf_op jit(solution)/shard_map/ppermute | solution.py:447
  80.8 4.1 %collective-permute-start.35 = (bf16[48,512]{1,0:T(8,128)(2,1)S(1)}, bf16[48,512]{1,0:T(8,128)(2,1)S(1)}, u32[]{:S(2)}, u32[]{:S(2)}) collective-permute-start(bf16[48,512]{1,0:T(8,128)(2,1)S(1)} %get-tuple-element.89), channel_id=1, source_target_pairs={{0,10},{1,11},{2,8},{3,9},{4,14},{5,15},{6,12},{7,13},{8,2},{9,3},... | collective-permute-start | bytes 147464 | tf_op jit(solution)/shard_map/ppermute | solution.py:447
  88.4 2.1 %collective-permute-done.35.refs_3_ = bf16[48,512]{1,0:T(8,128)(2,1)S(1)} collective-permute-done((bf16[48,512]{1,0:T(8,128)(2,1)S(1)}, bf16[48,512]{1,0:T(8,128)(2,1)S(1)}, u32[]{:S(2)}, u32[]{:S(2)}) %collective-permute-start.35) | collective-permute-done | bytes 49184 | tf_op jit(solution)/shard_map/ppermute | solution.py:447
  (83 shorter events, 22.9 us)
Async XLA Ops:
  0.0 5.6 %collective-permute-start = (bf16[2,4096]{1,0:T(2,128)(2,1)}, bf16[2,4096]{1,0:T(2,128)(2,1)S(1)}, u32[]{:S(2)}, u32[]{:S(2)}) collective-permute-start(bf16[2,4096]{1,0:T(2,128)(2,1)} %refs_0_.1), channel_id=1, source_target_pairs={{0,4},{1,5},{2,6},{3,7},{4,0},{5,1},{6,2},{7,3},{8,12},{9,13},{10,... | collective-permute-start | bytes 49160 | tf_op jit(solution)/shard_map/ppermute | solution.py:274
  5.6 5.7 %collective-permute-start.2 = (bf16[2,4096]{1,0:T(2,128)(2,1)}, bf16[2,4096]{1,0:T(2,128)(2,1)S(1)}, u32[]{:S(2)}, u32[]{:S(2)}) collective-permute-start(bf16[2,4096]{1,0:T(2,128)(2,1)} %refs_0_.1), channel_id=1, source_target_pairs={{0,12},{1,13},{2,14},{3,15},{4,8},{5,9},{6,10},{7,11},{8,4},{9,5},... | collective-permute-start | bytes 49160 | tf_op jit(solution)/shard_map/ppermute | solution.py:274
  12.1 8.9 %collective-permute-start.3 = (bf16[4,2,4096]{2,1,0:T(2,128)(2,1)S(1)}, bf16[4,2,4096]{2,1,0:T(2,128)(2,1)S(1)}, u32[]{:S(2)}, u32[]{:S(2)}) collective-permute-start(bf16[4,2,4096]{2,1,0:T(2,128)(2,1)S(1)} %lay.2), channel_id=1, source_target_pairs={{0,2},{1,3},{2,0},{3,1},{4,6},{5,7},{6,4},{7,5},{8,10},{9,11},{10,... | collective-permute-start | bytes 196616 | tf_op jit(solution)/shard_map/ppermute | solution.py:288
  14.4 6.6 %collective-permute-start.6 = (bf16[2,14336]{1,0:T(2,128)(2,1)}, bf16[2,14336]{1,0:T(2,128)(2,1)S(1)}, u32[]{:S(2)}, u32[]{:S(2)}) collective-permute-start(bf16[2,14336]{1,0:T(2,128)(2,1)} %refs_0_.2), channel_id=1, source_target_pairs={{0,12},{1,13},{2,14},{3,15},{4,8},{5,9},{6,10},{7,11},{8,4},{9,5},... | collective-permute-start | bytes 172040 | tf_op jit(solution)/shard_map/ppermute | solution.py:274
  21.8 12.9 %collective-permute-start.7 = (bf16[4,2,14336]{2,1,0:T(2,128)(2,1)S(1)}, bf16[4,2,14336]{2,1,0:T(2,128)(2,1)S(1)}, u32[]{:S(2)}, u32[]{:S(2)}) collective-permute-start(bf16[4,2,14336]{2,1,0:T(2,128)(2,1)S(1)} %lay.3), channel_id=1, source_target_pairs={{0,2},{1,3},{2,0},{3,1},{4,6},{5,7},{6,4},{7,5},{8,10},{9,11},{10,... | collective-permute-start | bytes 688136 | tf_op jit(solution)/shard_map/ppermute | solution.py:291
  35.4 10.1 %collective-permute-start.12 = (bf16[256,512]{1,0:T(8,128)(2,1)S(1)}, bf16[256,512]{1,0:T(8,128)(2,1)S(1)}, u32[]{:S(2)}, u32[]{:S(2)}) collective-permute-start(bf16[256,512]{1,0:T(8,128)(2,1)S(1)} %bitcast.2), channel_id=1, source_target_pairs={{0,4},{1,5},{4,8},{5,9},{8,12},{9,13},{12,14},{13,15},{14,10},{15,... | collective-permute-start | bytes 786440 | tf_op jit(solution)/shard_map/ppermute | solution.py:265
  36.4 9.2 %collective-permute-start.13 = (bf16[256,512]{1,0:T(8,128)(2,1)S(1)}, bf16[256,512]{1,0:T(8,128)(2,1)S(1)}, u32[]{:S(2)}, u32[]{:S(2)}) collective-permute-start(bf16[256,512]{1,0:T(8,128)(2,1)S(1)} %bitcast.3), channel_id=1, source_target_pairs={{0,2},{1,3},{4,0},{5,1},{8,4},{9,5},{12,8},{13,9},{14,12},{15,13},... | collective-permute-start | bytes 786440 | tf_op jit(solution)/shard_map/ppermute | solution.py:266
  37.5 8.0 %collective-permute-start.15 = (bf16[256,512]{1,0:T(8,128)(2,1)S(1)}, bf16[256,512]{1,0:T(8,128)(2,1)S(1)}, u32[]{:S(2)}, u32[]{:S(2)}) collective-permute-start(bf16[256,512]{1,0:T(8,128)(2,1)S(1)} %bitcast.4), channel_id=1, source_target_pairs={{0,1},{1,0},{2,3},{3,2},{4,5},{5,4},{6,7},{7,6},{8,9},{9,8},{10,11... | collective-permute-start | bytes 786440 | tf_op jit(solution)/shard_map/ppermute | solution.py:43
  37.5 8.0 %collective-permute-start.14 = (bf16[4,32,256]{2,1,0:T(8,128)(2,1)S(1)}, bf16[4,32,256]{2,1,0:T(8,128)(2,1)S(1)}, u32[]{:S(2)}, u32[]{:S(2)}) collective-permute-start(bf16[4,32,256]{2,1,0:T(8,128)(2,1)S(1)} %stack.4.first_ref), channel_id=1, source_target_pairs={{0,2},{1,3},{2,0},{3,1},{4,6},{5,7},{6,4},{7,5},{8,10},{9,11},{10,... | collective-permute-start | bytes 196616 | tf_op jit(solution)/shard_map/ppermute | solution.py:325
  45.5 8.2 %collective-permute-start.16 = (bf16[256,512]{1,0:T(8,128)(2,1)S(1)}, bf16[256,512]{1,0:T(8,128)(2,1)S(1)}, u32[]{:S(2)}, u32[]{:S(2)}) collective-permute-start(bf16[256,512]{1,0:T(8,128)(2,1)S(1)} %collective-permute-done.12.refs_2_), channel_id=1, source_target_pairs={{0,4},{1,5},{4,8},{5,9},{8,12},{9,13},{12,14},{13,15},{14,10},{15,... | collective-permute-start | bytes 786440 | tf_op jit(solution)/shard_map/ppermute | solution.py:265
  46.4 7.6 %collective-permute-start.17 = (bf16[256,512]{1,0:T(8,128)(2,1)S(1)}, bf16[256,512]{1,0:T(8,128)(2,1)S(1)}, u32[]{:S(2)}, u32[]{:S(2)}) collective-permute-start(bf16[256,512]{1,0:T(8,128)(2,1)S(1)} %collective-permute-done.13.refs_4_), channel_id=1, source_target_pairs={{0,2},{1,3},{4,0},{5,1},{8,4},{9,5},{12,8},{13,9},{14,12},{15,13},... | collective-permute-start | bytes 786440 | tf_op jit(solution)/shard_map/ppermute | solution.py:266
  47.6 6.4 %collective-permute-start.19 = (bf16[256,512]{1,0:T(8,128)(2,1)S(1)}, bf16[256,512]{1,0:T(8,128)(2,1)S(1)}, u32[]{:S(2)}, u32[]{:S(2)}) collective-permute-start(bf16[256,512]{1,0:T(8,128)(2,1)S(1)} %collective-permute-done.12.refs_2_), channel_id=1, source_target_pairs={{0,1},{1,0},{2,3},{3,2},{4,5},{5,4},{6,7},{7,6},{8,9},{9,8},{10,11... | collective-permute-start | bytes 786440 | tf_op jit(solution)/shard_map/ppermute | solution.py:43
  47.6 6.4 %collective-permute-start.20 = (bf16[256,512]{1,0:T(8,128)(2,1)S(1)}, bf16[256,512]{1,0:T(8,128)(2,1)S(1)}, u32[]{:S(2)}, u32[]{:S(2)}) collective-permute-start(bf16[256,512]{1,0:T(8,128)(2,1)S(1)} %collective-permute-done.13.refs_4_), channel_id=1, source_target_pairs={{0,1},{1,0},{2,3},{3,2},{4,5},{5,4},{6,7},{7,6},{8,9},{9,8},{10,11... | collective-permute-start | bytes 786440 | tf_op jit(solution)/shard_map/ppermute | solution.py:43
  54.0 10.2 %collective-permute-start.21 = (bf16[256,512]{1,0:T(8,128)(2,1)S(1)}, bf16[256,512]{1,0:T(8,128)(2,1)S(1)}, u32[]{:S(2)}, u32[]{:S(2)}) collective-permute-start(bf16[256,512]{1,0:T(8,128)(2,1)S(1)} %collective-permute-done.16.refs_6_), channel_id=1, source_target_pairs={{0,4},{1,5},{4,8},{5,9},{8,12},{9,13},{12,14},{13,15},{14,10},{15,... | collective-permute-start | bytes 786440 | tf_op jit(solution)/shard_map/ppermute | solution.py:265
  56.7 7.5 %collective-permute-start.22 = (bf16[256,512]{1,0:T(8,128)(2,1)S(1)}, bf16[256,512]{1,0:T(8,128)(2,1)S(1)}, u32[]{:S(2)}, u32[]{:S(2)}) collective-permute-start(bf16[256,512]{1,0:T(8,128)(2,1)S(1)} %collective-permute-done.17.refs_8_), channel_id=1, source_target_pairs={{0,2},{1,3},{4,0},{5,1},{8,4},{9,5},{12,8},{13,9},{14,12},{15,13},... | collective-permute-start | bytes 786440 | tf_op jit(solution)/shard_map/ppermute | solution.py:266
  56.7 7.5 %collective-permute-start.23 = (bf16[256,512]{1,0:T(8,128)(2,1)S(1)}, bf16[256,512]{1,0:T(8,128)(2,1)S(1)}, u32[]{:S(2)}, u32[]{:S(2)}) collective-permute-start(bf16[256,512]{1,0:T(8,128)(2,1)S(1)} %collective-permute-done.16.refs_6_), channel_id=1, source_target_pairs={{0,1},{1,0},{2,3},{3,2},{4,5},{5,4},{6,7},{7,6},{8,9},{9,8},{10,11... | collective-permute-start | bytes 786440 | tf_op jit(solution)/shard_map/ppermute | solution.py:43
  56.7 7.5 %collective-permute-start.24 = (bf16[256,512]{1,0:T(8,128)(2,1)S(1)}, bf16[256,512]{1,0:T(8,128)(2,1)S(1)}, u32[]{:S(2)}, u32[]{:S(2)}) collective-permute-start(bf16[256,512]{1,0:T(8,128)(2,1)S(1)} %collective-permute-done.17.refs_8_), channel_id=1, source_target_pairs={{0,1},{1,0},{2,3},{3,2},{4,5},{5,4},{6,7},{7,6},{8,9},{9,8},{10,11... | collective-permute-start | bytes 786440 | tf_op jit(solution)/shard_map/ppermute | solution.py:43
  64.9 6.5 %collective-permute-start.27 = (bf16[128,512]{1,0:T(8,128)(2,1)S(1)}, bf16[128,512]{1,0:T(8,128)(2,1)S(1)}, u32[]{:S(2)}, u32[]{:S(2)}) collective-permute-start(bf16[128,512]{1,0:T(8,128)(2,1)S(1)} %slice.10), channel_id=1, source_target_pairs={{0,4},{1,5},{4,8},{5,9},{8,12},{9,13},{12,14},{13,15},{14,10},{15,... | collective-permute-start | bytes 393224 | tf_op jit(solution)/shard_map/ppermute | solution.py:265
  77.2 8.3 %collective-permute-start.32 = (bf16[48,512]{1,0:T(8,128)(2,1)S(1)}, bf16[48,512]{1,0:T(8,128)(2,1)S(1)}, u32[]{:S(2)}, u32[]{:S(2)}) collective-permute-start(bf16[48,512]{1,0:T(8,128)(2,1)S(1)} %get-tuple-element.86), channel_id=1, source_target_pairs={{0,12},{1,13},{2,14},{3,15},{4,8},{5,9},{6,10},{7,11},{8,4},{9,5},... | collective-permute-start | bytes 147464 | tf_op jit(solution)/shard_map/ppermute | solution.py:447
  80.2 7.1 %collective-permute-start.33 = (bf16[48,512]{1,0:T(8,128)(2,1)S(1)}, bf16[48,512]{1,0:T(8,128)(2,1)S(1)}, u32[]{:S(2)}, u32[]{:S(2)}) collective-permute-start(bf16[48,512]{1,0:T(8,128)(2,1)S(1)} %get-tuple-element.87), channel_id=1, source_target_pairs={{0,14},{1,15},{2,12},{3,13},{4,10},{5,11},{6,8},{7,9},{8,6},{9,7},... | collective-permute-start | bytes 147464 | tf_op jit(solution)/shard_map/ppermute | solution.py:447
  80.8 7.6 %collective-permute-start.34 = (bf16[48,512]{1,0:T(8,128)(2,1)S(1)}, bf16[48,512]{1,0:T(8,128)(2,1)S(1)}, u32[]{:S(2)}, u32[]{:S(2)}) collective-permute-start(bf16[48,512]{1,0:T(8,128)(2,1)S(1)} %get-tuple-element.88), channel_id=1, source_target_pairs={{0,8},{1,9},{2,10},{3,11},{4,12},{5,13},{6,14},{7,15},{8,0},{9,1},... | collective-permute-start | bytes 147464 | tf_op jit(solution)/shard_map/ppermute | solution.py:447
  80.8 9.7 %collective-permute-start.35 = (bf16[48,512]{1,0:T(8,128)(2,1)S(1)}, bf16[48,512]{1,0:T(8,128)(2,1)S(1)}, u32[]{:S(2)}, u32[]{:S(2)}) collective-permute-start(bf16[48,512]{1,0:T(8,128)(2,1)S(1)} %get-tuple-element.89), channel_id=1, source_target_pairs={{0,10},{1,11},{2,8},{3,9},{4,14},{5,15},{6,12},{7,13},{8,2},{9,3},... | collective-permute-start | bytes 147464 | tf_op jit(solution)/shard_map/ppermute | solution.py:447
  84.9 5.6 %collective-permute-start.36 = (bf16[48,512]{1,0:T(8,128)(2,1)S(1)}, bf16[48,512]{1,0:T(8,128)(2,1)S(1)}, u32[]{:S(2)}, u32[]{:S(2)}) collective-permute-start(bf16[48,512]{1,0:T(8,128)(2,1)S(1)} %get-tuple-element.90), channel_id=1, source_target_pairs={{0,4},{1,5},{2,6},{3,7},{4,0},{5,1},{6,2},{7,3},{8,12},{9,13},{10,... | collective-permute-start | bytes 147464 | tf_op jit(solution)/shard_map/ppermute | solution.py:447
  85.5 6.1 %collective-permute-start.37 = (bf16[48,512]{1,0:T(8,128)(2,1)S(1)}, bf16[48,512]{1,0:T(8,128)(2,1)S(1)}, u32[]{:S(2)}, u32[]{:S(2)}) collective-permute-start(bf16[48,512]{1,0:T(8,128)(2,1)S(1)} %get-tuple-element.91), channel_id=1, source_target_pairs={{0,6},{1,7},{2,4},{3,5},{4,2},{5,3},{6,0},{7,1},{8,14},{9,15},{10,... | collective-permute-start | bytes 147464 | tf_op jit(solution)/shard_map/ppermute | solution.py:447
  (20 other events, 79.4 us)

commit v18 on v15

--- a/solution.py
+++ b/solution.py
@@ -78,6 +78,15 @@
     wanted = lax.broadcasted_iota(jnp.int32, (tokens, tokens), 0)
     held = held_tokens(lax.axis_index("blk"), tokens, tok_rows)
     out_ref[...] = reorder(wanted, held, rotated).astype(jnp.bfloat16)
+
+
+def keep_kernel(basis_ref, kept_ref):
+    kept_ref[...] = basis_ref[...]
+
+
+def lay_kernel(*refs):
+    for at, ref in enumerate(refs[:-1]):
+        refs[-1][at] = ref[...]
 
 
 def stack_kernel(first_ref, last_ref, out_ref):
@@ -142,10 +151,22 @@
 
 
 def scale_kernel(
-    begun, aligned_ref, near_ref, far_ref, tiles_ref, eigen_ref, out_ref, damped, tiles, sem
+    begun,
+    aligned_ref,
+    near_ref,
+    far_ref,
+    tiles_ref,
+    eigen_ref,
+    out_ref,
+    damped,
+    tiles,
+    lanes,
+    rotated,
+    sem,
 ):
     blocks, depth = damped.shape[:2]
     chips, _, width = near_ref.shape
+    per_piece = width // LANES
 
     def copy_of(block):
         rows = pl.ds(pl.multiple_of(block * depth, depth), depth)
@@ -160,28 +181,29 @@
 
     tiles_copy.wait()
     me = lax.axis_index("blk")
+    for at, steps in enumerate(begun):
+        for other, rotated_ref in enumerate((near_ref, far_ref)):
+            source = ring_source(me, steps, other, chips)
+            key = (source ^ me) // 2
+            piece = 2 * at + other
+            rotated[piece] = rotated_ref[lax.rem(key, 2) * (chips // 2) + key // 2]
+            for part in range(per_piece):
+                lanes[piece * per_piece + part] = tiles[source * per_piece + part] * LANES
 
     @pl.loop(0, blocks)
     def _(block):
         rows = pl.ds(pl.multiple_of(block * depth, depth), depth)
         aligned = aligned_ref[rows, :]
         copy_of(block).wait()
-        place = 0
-        for steps in begun:
-            for other, rotated_ref in enumerate((near_ref, far_ref)):
-                source = ring_source(me, steps, other, chips)
-                key = (source ^ me) // 2
-                rotated = rotated_ref[lax.rem(key, 2) * (chips // 2) + key // 2]
-                grad = jnp.dot(aligned, rotated, preferred_element_type=jnp.float32)
-                for first in range(0, width, LANES):
-                    tile = tiles[(source * width + first) // LANES]
-                    lanes = pl.ds(pl.multiple_of(tile * LANES, LANES), LANES)
-                    eigen = damped[block, :, lanes]
-                    inverse = pl.reciprocal(eigen, approx=True)
-                    inverse = inverse * (2.0 - eigen * inverse)
-                    scaled = grad[:, first : first + LANES] * inverse
-                    out_ref[rows, place : place + LANES] = scaled.astype(jnp.bfloat16)
-                    place += LANES
+        for piece in range(2 * chips):
+            grad = jnp.dot(aligned, rotated[piece], preferred_element_type=jnp.float32)
+            for part in range(per_piece):
+                tile = piece * per_piece + part
+                eigen = damped[block, :, pl.ds(pl.multiple_of(lanes[tile], LANES), LANES)]
+                inverse = pl.reciprocal(eigen, approx=True)
+                inverse = inverse * (2.0 - eigen * inverse)
+                scaled = grad[:, part * LANES : (part + 1) * LANES] * inverse
+                out_ref[rows, tile * LANES : (tile + 1) * LANES] = scaled.astype(jnp.bfloat16)
 
 
 def project_kernel(cuts, scaled_ref, basis_out_ref, *refs):
@@ -274,7 +296,16 @@
     pairs = chips // 2
     both = jnp.concatenate([grad_out, activations], axis=1)[None]
     got = [lax.ppermute(both, "blk", xor_pairs(n, 4 * key)) for key in range(1, pairs)]
-    both, own, *got = after(both, own, *got)
+    kept = pl.pallas_call(
+        keep_kernel,
+        out_shape=jax.ShapeDtypeStruct(basis_in.shape, jnp.bfloat16),
+        in_specs=[VMEM],
+        out_specs=VMEM,
+        compiler_params=pltpu.CompilerParams(vmem_limit_bytes=8 * MIB),
+        cost_estimate=CHEAP,
+        name="keep",
+    )(basis_in)
+    both, own, kept, *got = after(both, own, kept, *got)
     depth, later = 1024, 7
     grads, acts = pl.pallas_call(
         part_kernel,
@@ -299,31 +330,30 @@
         compiler_params=pltpu.CompilerParams(vmem_limit_bytes=8 * MIB),
         cost_estimate=CHEAP,
         name="rotate_in",
-    )(acts, swap(acts, n), basis_in)
-
-    def doubled(x, key):
+    )(acts, swap(acts, n), kept)
+
+    def lay(kernel, shape, *blocks):
         return pl.pallas_call(
-            stack_kernel,
-            out_shape=jax.ShapeDtypeStruct((2 * x.shape[0], *x.shape[1:]), x.dtype),
-            in_specs=[VMEM, VMEM],
+            kernel,
+            out_shape=jax.ShapeDtypeStruct(shape, jnp.bfloat16),
+            in_specs=[VMEM] * len(blocks),
             out_specs=VMEM,
             compiler_params=pltpu.CompilerParams(vmem_limit_bytes=8 * MIB),
             cost_estimate=CHEAP,
-            name="stack",
-        )(x, lax.ppermute(x, "blk", xor_pairs(n, key)))
-
+            name=kernel.__name__[:-7],
+        )(*blocks)
+
+    grads_got, _ = after(grads_got, rotated)
+    blocks = [rotated] + [
+        lax.ppermute(rotated, "blk", xor_pairs(n, 4 * key)) for key in range(1, pairs)
+    ]
+    rotated = lay(lay_kernel, (pairs, tokens, in_width), *blocks)
     rotated, own = after(rotated, own)
     right, left = [own, to_right(own)], [own, to_left(own)]
-    grads_got, rotated = after(grads_got, rotated)
-    rotated = doubled(rotated[None], 4)
     grads = jnp.concatenate([grads, grads_got], axis=0)
     grads_far = swap(grads, n)
-    grads, grads_far, rotated = after(grads, grads_far, rotated)
     far = [swap(own, n)]
-    key = 8
-    while key < n:
-        rotated = doubled(rotated, key)
-        key *= 2
+    rotated_got = lax.ppermute(rotated, "blk", xor_pairs(n, 2))
 
     rotate = lambda kernel, count, scratch, shape, dtype, *operands: pl.pallas_call(
         kernel,
@@ -347,10 +377,11 @@
         grads_far,
         basis_out,
     )
-    start, grads, right[-1], left[-1], rotated, *far = after(
-        start, grads, right[-1], left[-1], rotated, *far
-    )
-    rotated = doubled(rotated, 2)
+    start, grads, right[-1], left[-1], rotated_got, *far = after(
+        start, grads, right[-1], left[-1], rotated_got, *far
+    )
+    rotated = lay(stack_kernel, (chips, tokens, in_width), rotated, rotated_got)
+    rotated_far = swap(rotated, n)
     far += [swap(right[-1], n), swap(left[-1], n)]
     right.append(to_right(right[-1]))
     left.append(to_left(left[-1]))
@@ -370,8 +401,8 @@
         start,
     )
 
-    aligned, right[-1], left[-1], rotated, *far = after(
-        aligned, right[-1], left[-1], rotated, *far
+    aligned, right[-1], left[-1], rotated_far, *far = after(
+        aligned, right[-1], left[-1], rotated_far, *far
     )
     far += [swap(right[-1], n), swap(left[-1], n)]
     right.append(to_right(right[-1]))
@@ -386,12 +417,14 @@
         scratch_shapes=[
             pltpu.VMEM((blocks, tile_width // blocks, full_in), jnp.float32),
             pltpu.SMEM(tile_order.shape, jnp.int32),
+            pltpu.SMEM(tile_order.shape, jnp.int32),
+            pltpu.VMEM((n, tokens, in_width), jnp.bfloat16),
             pltpu.SemaphoreType.DMA((blocks + 1,)),
         ],
         compiler_params=pltpu.CompilerParams(vmem_limit_bytes=40 * MIB),
         cost_estimate=CHEAP,
         name="scale",
-    )(aligned, rotated, swap(rotated, n), tile_order, eigenvalues)
+    )(aligned, rotated, rotated_far, tile_order, eigenvalues)
 
     scaled, right[-1], left[-1], *far = after(scaled, right[-1], left[-1], *far)
     cut = in_width // 2

time: 86.9 us -> 83.3 us (0.959)
  waiting for transfers between devices: 22.6 us -> 19.1 us
  starting transfers between devices: 34.4 us -> 35.4 us
    ppermute x4, starting transfers between devices: 3.23 us -> 6.47 us  [ring_body(): to_left = lambda x: lax.ppermute(x, 'blk', shift_pairs(n, -1))]
    ppermute x4, starting transfers between devices: 5.02 us -> 1.83 us  [ring_body(): to_right = lambda x: lax.ppermute(x, 'blk', shift_pairs(n, 1))]
    ppermute x3 -> x4, waiting for transfers between devices: 6.41 us -> 4.34 us  [the longest x3 3.92 us: ring_body(): lax.ppermute(rotated, 'blk', xor_pairs(n, 4 * key))]
    ppermute x13, waiting for transfers between devices: 5.17 us -> 3.58 us  [swap(): return lax.ppermute(x, 'blk', xor_pairs(n, 1))]
    ppermute x3, waiting for transfers between devices: 5.13 us -> 3.56 us  [ring_body(): lax.ppermute(both, 'blk', xor_pairs(n, 4 * key))]
    ppermute x7, waiting for transfers between devices: 2.56 us -> 4.1 us  [ring_body(): lax.ppermute(x, 'blk', xor_pairs(n, 2 * key))]
    ppermute x3 -> x4, starting transfers between devices: 3.96 us -> 5.28 us  [the longest x3 4.45 us: ring_body(): lax.ppermute(rotated, 'blk', xor_pairs(n, 4 * key))]
  transfers between devices with their start and end apart: 36 -> 37, of which waited for: 15 -> 15; matrix products, arithmetic and copies ran while one was open for 2% -> 1% of each run, Pallas kernels for 26% -> 26%
where the time goes in v18:
time: 83.3 us; the launch traced here: 83.1 us
  starting transfers between devices  35.4 us (42%)
  Pallas kernels  24.4 us (29%)
  waiting for transfers between devices  19.1 us (23%)
  local copies, waits for them, and re-layouts  3.01 us (4%)
  other arithmetic  0.91 us (1%)
    ppermute x7, starting transfers between devices, ring_body(): lax.ppermute(x, 'blk', xor_pairs(n, 2 * key))  11.2 us
    pallas_call x2, Pallas kernels, ring_body(): pl.pallas_call(kernel, out_shape=jax.ShapeDtypeStruct(shape, dtype), in_s...  10.7 us
    ppermute x4, starting transfers between devices, ring_body(): to_left = lambda x: lax.ppermute(x, 'blk', shift_pairs(n, -1))  6.47 us
    pallas_call x1, Pallas kernels, ring_body(): pl.pallas_call(functools.partial(scale_kernel, begun), out_shape=jax.Shap...  6.19 us
    ppermute x3, starting transfers between devices, ring_body(): lax.ppermute(both, 'blk', xor_pairs(n, 4 * key))  5.68 us
    ppermute x3, starting transfers between devices, ring_body(): lax.ppermute(rotated, 'blk', xor_pairs(n, 4 * key))  4.45 us
    pallas_call x1, Pallas kernels, ring_body(): pl.pallas_call(functools.partial(project_kernel, (0, 6, len(pieces))), ou...  4.39 us
    ppermute x7, waiting for transfers between devices, ring_body(): lax.ppermute(x, 'blk', xor_pairs(n, 2 * key))  4.1 us
  transfers between devices with their start and end apart: 37, of which 15 were waited for; matrix products, arithmetic and copies ran while one was open for 1% of the time, Pallas kernels for 26%

profile of v18, /device:TPU:0, one launch (start us, length us, event | category | flops | bytes accessed | tf_op | source)
XLA Modules:
  0.0 83.1 jit_solution(6975411931753349821)
XLA Ops:
  0.9 3.1 %collective-permute-start = (bf16[1,2,18432]{2,1,0:T(2,128)(2,1)S(1)}, bf16[1,2,18432]{2,1,0:T(2,128)(2,1)S(1)}, u32[]{:S(2)}, u32[]{:S(2)}) collective-permute-start(bf16[1,2,18432]{2,1,0:T(2,128)(2,1)S(1)} %maximum_bitcast_fusion.refs_0_), channel_id=1, source_target_pairs={{0,4},{1,5},{2,6},{3,7},{4,0},{5,1},{6,2},{7,3},{8,12},{9,13},{10,... | collective-permute-start | bytes 221192 | tf_op jit(solution)/shard_map/ppermute | solution.py:298
  4.0 2.6 %collective-permute-start.1 = (bf16[1,2,18432]{2,1,0:T(2,128)(2,1)S(1)}, bf16[1,2,18432]{2,1,0:T(2,128)(2,1)S(1)}, u32[]{:S(2)}, u32[]{:S(2)}) collective-permute-start(bf16[1,2,18432]{2,1,0:T(2,128)(2,1)S(1)} %maximum_bitcast_fusion.refs_0_), channel_id=1, source_target_pairs={{0,8},{1,9},{2,10},{3,11},{4,12},{5,13},{6,14},{7,15},{8,0},{9,1},... | collective-permute-start | bytes 221192 | tf_op jit(solution)/shard_map/ppermute | solution.py:298
  6.6 1.6 %copy-done = bf16[4096,256]{1,0:T(8,128)(2,1)S(1)} copy-done((bf16[4096,256]{1,0:T(8,128)(2,1)S(1)}, bf16[4096,256]{1,0:T(8,128)(2,1)}, u32[]{:S(2)}) %copy-start) | copy-done | bytes 2097176
  9.3 2.5 %collective-permute-done.1.refs_2_ = bf16[1,2,18432]{2,1,0:T(2,128)(2,1)S(1)} collective-permute-done((bf16[1,2,18432]{2,1,0:T(2,128)(2,1)S(1)}, bf16[1,2,18432]{2,1,0:T(2,128)(2,1)S(1)}, u32[]{:S(2)}, u32[]{:S(2)}) %collective-permute-start.1) | collective-permute-done | bytes 73760 | tf_op jit(solution)/shard_map/ppermute | solution.py:298
  12.9 1.6 %collective-permute-start.4 = (bf16[4,2,4096]{2,1,0:T(2,128)(2,1)S(1)}, bf16[4,2,4096]{2,1,0:T(2,128)(2,1)S(1)}, u32[]{:S(2)}, u32[]{:S(2)}) collective-permute-start(bf16[4,2,4096]{2,1,0:T(2,128)(2,1)S(1)} %get-tuple-element.63), channel_id=1, source_target_pairs={{0,2},{1,3},{2,0},{3,1},{4,6},{5,7},{6,4},{7,5},{8,10},{9,11},{10,... | collective-permute-start | bytes 196616 | tf_op jit(solution)/shard_map/ppermute | solution.py:322
  15.1 2.9 %collective-permute-done.4 = bf16[4,2,4096]{2,1,0:T(2,128)(2,1)S(1)} collective-permute-done((bf16[4,2,4096]{2,1,0:T(2,128)(2,1)S(1)}, bf16[4,2,4096]{2,1,0:T(2,128)(2,1)S(1)}, u32[]{:S(2)}, u32[]{:S(2)}) %collective-permute-start.4) | collective-permute-done | bytes 65568 | tf_op jit(solution)/shard_map/ppermute | solution.py:322
  22.0 1.6 %collective-permute-start.8 = (bf16[32,256]{1,0:T(8,128)(2,1)S(1)}, bf16[32,256]{1,0:T(8,128)(2,1)S(1)}, u32[]{:S(2)}, u32[]{:S(2)}) collective-permute-start(bf16[32,256]{1,0:T(8,128)(2,1)S(1)} %rotate_in.1.refs_0_), channel_id=1, source_target_pairs={{0,8},{1,9},{2,10},{3,11},{4,12},{5,13},{6,14},{7,15},{8,0},{9,1},... | collective-permute-start | bytes 49160 | tf_op jit(solution)/shard_map/ppermute | solution.py:348
  23.7 1.6 %collective-permute-start.9 = (bf16[32,256]{1,0:T(8,128)(2,1)S(1)}, bf16[32,256]{1,0:T(8,128)(2,1)S(1)}, u32[]{:S(2)}, u32[]{:S(2)}) collective-permute-start(bf16[32,256]{1,0:T(8,128)(2,1)S(1)} %rotate_in.1.refs_0_), channel_id=1, source_target_pairs={{0,12},{1,13},{2,14},{3,15},{4,8},{5,9},{6,10},{7,11},{8,4},{9,5},... | collective-permute-start | bytes 49160 | tf_op jit(solution)/shard_map/ppermute | solution.py:348
  25.3 1.4 %collective-permute-done.8.refs_2_ = bf16[32,256]{1,0:T(8,128)(2,1)S(1)} collective-permute-done((bf16[32,256]{1,0:T(8,128)(2,1)S(1)}, bf16[32,256]{1,0:T(8,128)(2,1)S(1)}, u32[]{:S(2)}, u32[]{:S(2)}) %collective-permute-start.8) | collective-permute-done | bytes 16416 | tf_op jit(solution)/shard_map/ppermute | solution.py:348
  26.7 2.5 %collective-permute-done.9.refs_3_ = bf16[32,256]{1,0:T(8,128)(2,1)S(1)} collective-permute-done((bf16[32,256]{1,0:T(8,128)(2,1)S(1)}, bf16[32,256]{1,0:T(8,128)(2,1)S(1)}, u32[]{:S(2)}, u32[]{:S(2)}) %collective-permute-start.9) | collective-permute-done | bytes 16416 | tf_op jit(solution)/shard_map/ppermute | solution.py:348
  29.4 1.9 %collective-permute-start.11 = (bf16[256,512]{1,0:T(8,128)(2,1)S(1)}, bf16[256,512]{1,0:T(8,128)(2,1)S(1)}, u32[]{:S(2)}, u32[]{:S(2)}) collective-permute-start(bf16[256,512]{1,0:T(8,128)(2,1)S(1)} %bitcast.4), channel_id=1, source_target_pairs={{0,2},{1,3},{4,0},{5,1},{8,4},{9,5},{12,8},{13,9},{14,12},{15,13},... | collective-permute-start | bytes 786440 | tf_op jit(solution)/shard_map/ppermute | solution.py:291
  32.2 5.2 %rotate_first.1.start_ref = f32[32,896]{1,0:T(8,128)S(1)} custom-call(bf16[8,2,14336]{2,1,0:T(2,128)(2,1)S(1)} %constant_dynamic-update-slice_fusion.2.near_ref, bf16[8,2,14336]{2,1,0:T(2,128)(2,1)S(1)} %collective-permute-done.6.far_ref, bf16[14336,896]{1,0:T(8,128)(2,1)} %basis_out_ref.1), custom_call_target="tpu_custom_call" | custom-call | flops 1 | bytes 1 | tf_op jit(solution)/shard_map/rotate_first/pallas_call | solution.py:358
  37.9 2.0 %collective-permute-start.15 = (bf16[256,512]{1,0:T(8,128)(2,1)S(1)}, bf16[256,512]{1,0:T(8,128)(2,1)S(1)}, u32[]{:S(2)}, u32[]{:S(2)}) collective-permute-start(bf16[256,512]{1,0:T(8,128)(2,1)S(1)} %collective-permute-done.11.refs_4_), channel_id=1, source_target_pairs={{0,2},{1,3},{4,0},{5,1},{8,4},{9,5},{12,8},{13,9},{14,12},{15,13},... | collective-permute-start | bytes 786440 | tf_op jit(solution)/shard_map/ppermute | solution.py:291
  40.5 5.5 %rotate_last.1.aligned_ref = bf16[896,32]{1,0:T(8,128)(2,1)S(1)} custom-call(bf16[8,2,14336]{2,1,0:T(2,128)(2,1)S(1)} %constant_dynamic-update-slice_fusion.2.near_ref, bf16[8,2,14336]{2,1,0:T(2,128)(2,1)S(1)} %collective-permute-done.6.far_ref, bf16[14336,896]{1,0:T(8,128)(2,1)} %basis_out_ref.1, s32[16]{0:T(128)S(1)} %copy-done.2, ...), custom_call_target="tpu_custom_call" | custom-call | flops 1 | bytes 1 | tf_op jit(solution)/shard_map/rotate_last/pallas_call | solution.py:358
  46.6 1.6 %collective-permute-start.20 = (bf16[256,512]{1,0:T(8,128)(2,1)S(1)}, bf16[256,512]{1,0:T(8,128)(2,1)S(1)}, u32[]{:S(2)}, u32[]{:S(2)}) collective-permute-start(bf16[256,512]{1,0:T(8,128)(2,1)S(1)} %collective-permute-done.15.refs_8_), channel_id=1, source_target_pairs={{0,2},{1,3},{4,0},{5,1},{8,4},{9,5},{12,8},{13,9},{14,12},{15,13},... | collective-permute-start | bytes 786440 | tf_op jit(solution)/shard_map/ppermute | solution.py:291
  48.7 6.2 %scale.1.scaled_ref = bf16[896,4096]{1,0:T(8,128)(2,1)S(1)} custom-call(bf16[896,32]{1,0:T(8,128)(2,1)S(1)} %rotate_last.1.aligned_ref, bf16[8,32,256]{2,1,0:T(8,128)(2,1)S(1)} %stack.1.near_ref, bf16[8,32,256]{2,1,0:T(8,128)(2,1)S(1)} %collective-permute-done.16.far_ref, s32[32]{0:T(128)S(1)} %copy-done.1, f32[896,4096]{1,0:T(8,128)} %eigen_ref.1), custom_call_target="tpu_custom_call" | custom-call | flops 1 | bytes 1 | tf_op jit(solution)/shard_map/scale/pallas_call | solution.py:412
  57.6 4.4 %project.1 = (f32[896,512]{1,0:T(8,128)S(1)}, bf16[768,896]{1,0:T(8,128)(2,1)S(1)}) custom-call(bf16[896,4096]{1,0:T(8,128)(2,1)S(1)} %scale.1.scaled_ref, bf16[14336,896]{1,0:T(8,128)(2,1)} %basis_out_ref.1, bf16[256,512]{1,0:T(8,128)(2,1)S(1)} %bitcast.6, bf16[256,512]{1,0:T(8,128)(2,1)S(1)} %collective-permute-done.13.refs_1_, ...), custom_call_target="tpu_custom_call" | custom-call | flops 1 | bytes 1 | tf_op jit(solution)/shard_map/project/pallas_call | solution.py:435
  63.6 1.6 %window.1 = (bf16[8,48,512]{2,1,0:T(8,128)(2,1)S(1)}, f32[8,48,512]{2,1,0:T(8,128)S(1)}) custom-call(bf16[768,896]{1,0:T(8,128)(2,1)S(1)} %get-tuple-element.90.window_ref, bf16[896,4096]{1,0:T(8,128)(2,1)S(1)} %scale.1.scaled_ref, f32[896,512]{1,0:T(8,128)S(1)} %get-tuple-element.92.projected_ref, bf16[128,512]{1,0:T(8,128)(2,1)S(1)} %collective-permute-done.25.refs_0_, ...), custom_call_target="tpu_custom_call" | custom-call | flops 1 | bytes 1 | tf_op jit(solution)/shard_map/window/pallas_call | solution.py:455
  65.7 1.4 %collective-permute-done.29.got_ref = bf16[8,48,512]{2,1,0:T(8,128)(2,1)S(1)} collective-permute-done((bf16[8,48,512]{2,1,0:T(8,128)(2,1)S(1)}, bf16[8,48,512]{2,1,0:T(8,128)(2,1)S(1)}, u32[]{:S(2)}, u32[]{:S(2)}) %collective-permute-start.29) | collective-permute-done | bytes 393248 | tf_op jit(solution)/shard_map/ppermute | solution.py:43
  67.1 2.4 %collective-permute-start.30 = (bf16[48,512]{1,0:T(8,128)(2,1)S(1)}, bf16[48,512]{1,0:T(8,128)(2,1)S(1)}, u32[]{:S(2)}, u32[]{:S(2)}) collective-permute-start(bf16[48,512]{1,0:T(8,128)(2,1)S(1)} %get-tuple-element.98), channel_id=1, source_target_pairs={{0,12},{1,13},{2,14},{3,15},{4,8},{5,9},{6,10},{7,11},{8,4},{9,5},... | collective-permute-start | bytes 147464 | tf_op jit(solution)/shard_map/ppermute | solution.py:480
  69.5 2.7 %collective-permute-start.31 = (bf16[48,512]{1,0:T(8,128)(2,1)S(1)}, bf16[48,512]{1,0:T(8,128)(2,1)S(1)}, u32[]{:S(2)}, u32[]{:S(2)}) collective-permute-start(bf16[48,512]{1,0:T(8,128)(2,1)S(1)} %get-tuple-element.99), channel_id=1, source_target_pairs={{0,14},{1,15},{2,12},{3,13},{4,10},{5,11},{6,8},{7,9},{8,6},{9,7},... | collective-permute-start | bytes 147464 | tf_op jit(solution)/shard_map/ppermute | solution.py:480
  72.3 2.5 %collective-permute-start.33 = (bf16[48,512]{1,0:T(8,128)(2,1)S(1)}, bf16[48,512]{1,0:T(8,128)(2,1)S(1)}, u32[]{:S(2)}, u32[]{:S(2)}) collective-permute-start(bf16[48,512]{1,0:T(8,128)(2,1)S(1)} %get-tuple-element.101), channel_id=1, source_target_pairs={{0,10},{1,11},{2,8},{3,9},{4,14},{5,15},{6,12},{7,13},{8,2},{9,3},... | collective-permute-start | bytes 147464 | tf_op jit(solution)/shard_map/ppermute | solution.py:480
  74.8 3.3 %collective-permute-start.35 = (bf16[48,512]{1,0:T(8,128)(2,1)S(1)}, bf16[48,512]{1,0:T(8,128)(2,1)S(1)}, u32[]{:S(2)}, u32[]{:S(2)}) collective-permute-start(bf16[48,512]{1,0:T(8,128)(2,1)S(1)} %get-tuple-element.103), channel_id=1, source_target_pairs={{0,6},{1,7},{2,4},{3,5},{4,2},{5,3},{6,0},{7,1},{8,14},{9,15},{10,... | collective-permute-start | bytes 147464 | tf_op jit(solution)/shard_map/ppermute | solution.py:480
  78.4 2.6 %collective-permute-done.33.refs_3_ = bf16[48,512]{1,0:T(8,128)(2,1)S(1)} collective-permute-done((bf16[48,512]{1,0:T(8,128)(2,1)S(1)}, bf16[48,512]{1,0:T(8,128)(2,1)S(1)}, u32[]{:S(2)}, u32[]{:S(2)}) %collective-permute-start.33) | collective-permute-done | bytes 49184 | tf_op jit(solution)/shard_map/ppermute | solution.py:480
  (78 shorter events, 18.1 us)
Async XLA Ops:
  0.9 8.4 %collective-permute-start = (bf16[1,2,18432]{2,1,0:T(2,128)(2,1)S(1)}, bf16[1,2,18432]{2,1,0:T(2,128)(2,1)S(1)}, u32[]{:S(2)}, u32[]{:S(2)}) collective-permute-start(bf16[1,2,18432]{2,1,0:T(2,128)(2,1)S(1)} %maximum_bitcast_fusion.refs_0_), channel_id=1, source_target_pairs={{0,4},{1,5},{2,6},{3,7},{4,0},{5,1},{6,2},{7,3},{8,12},{9,13},{10,... | collective-permute-start | bytes 221192 | tf_op jit(solution)/shard_map/ppermute | solution.py:298
  4.0 7.8 %collective-permute-start.1 = (bf16[1,2,18432]{2,1,0:T(2,128)(2,1)S(1)}, bf16[1,2,18432]{2,1,0:T(2,128)(2,1)S(1)}, u32[]{:S(2)}, u32[]{:S(2)}) collective-permute-start(bf16[1,2,18432]{2,1,0:T(2,128)(2,1)S(1)} %maximum_bitcast_fusion.refs_0_), channel_id=1, source_target_pairs={{0,8},{1,9},{2,10},{3,11},{4,12},{5,13},{6,14},{7,15},{8,0},{9,1},... | collective-permute-start | bytes 221192 | tf_op jit(solution)/shard_map/ppermute | solution.py:298
  6.6 6.3 %collective-permute-start.2 = (bf16[1,2,18432]{2,1,0:T(2,128)(2,1)S(1)}, bf16[1,2,18432]{2,1,0:T(2,128)(2,1)S(1)}, u32[]{:S(2)}, u32[]{:S(2)}) collective-permute-start(bf16[1,2,18432]{2,1,0:T(2,128)(2,1)S(1)} %maximum_bitcast_fusion.refs_0_), channel_id=1, source_target_pairs={{0,12},{1,13},{2,14},{3,15},{4,8},{5,9},{6,10},{7,11},{8,4},{9,5},... | collective-permute-start | bytes 221192 | tf_op jit(solution)/shard_map/ppermute | solution.py:298
  14.5 6.1 %collective-permute-start.3 = (bf16[4,2,14336]{2,1,0:T(2,128)(2,1)S(1)}, bf16[4,2,14336]{2,1,0:T(2,128)(2,1)S(1)}, u32[]{:S(2)}, u32[]{:S(2)}) collective-permute-start(bf16[4,2,14336]{2,1,0:T(2,128)(2,1)S(1)} %get-tuple-element.62), channel_id=1, source_target_pairs={{0,2},{1,3},{2,0},{3,1},{4,6},{5,7},{6,4},{7,5},{8,10},{9,11},{10,... | collective-permute-start | bytes 688136 | tf_op jit(solution)/shard_map/ppermute | solution.py:323
  20.8 11.4 %collective-permute-start.6 = (bf16[8,2,14336]{2,1,0:T(2,128)(2,1)S(1)}, bf16[8,2,14336]{2,1,0:T(2,128)(2,1)S(1)}, u32[]{:S(2)}, u32[]{:S(2)}) collective-permute-start(bf16[8,2,14336]{2,1,0:T(2,128)(2,1)S(1)} %constant_dynamic-update-slice_fusion.2.near_ref), channel_id=1, source_target_pairs={{0,1},{1,0},{2,3},{3,2},{4,5},{5,4},{6,7},{7,6},{8,9},{9,8},{10,11... | collective-permute-start | bytes 1376264 | tf_op jit(solution)/shard_map/ppermute | solution.py:43
  29.2 8.6 %collective-permute-start.10 = (bf16[256,512]{1,0:T(8,128)(2,1)S(1)}, bf16[256,512]{1,0:T(8,128)(2,1)S(1)}, u32[]{:S(2)}, u32[]{:S(2)}) collective-permute-start(bf16[256,512]{1,0:T(8,128)(2,1)S(1)} %bitcast.3), channel_id=1, source_target_pairs={{0,4},{1,5},{4,8},{5,9},{8,12},{9,13},{12,14},{13,15},{14,10},{15,... | collective-permute-start | bytes 786440 | tf_op jit(solution)/shard_map/ppermute | solution.py:290
  29.4 8.4 %collective-permute-start.11 = (bf16[256,512]{1,0:T(8,128)(2,1)S(1)}, bf16[256,512]{1,0:T(8,128)(2,1)S(1)}, u32[]{:S(2)}, u32[]{:S(2)}) collective-permute-start(bf16[256,512]{1,0:T(8,128)(2,1)S(1)} %bitcast.4), channel_id=1, source_target_pairs={{0,2},{1,3},{4,0},{5,1},{8,4},{9,5},{12,8},{13,9},{14,12},{15,13},... | collective-permute-start | bytes 786440 | tf_op jit(solution)/shard_map/ppermute | solution.py:291
  31.3 6.5 %collective-permute-start.13 = (bf16[256,512]{1,0:T(8,128)(2,1)S(1)}, bf16[256,512]{1,0:T(8,128)(2,1)S(1)}, u32[]{:S(2)}, u32[]{:S(2)}) collective-permute-start(bf16[256,512]{1,0:T(8,128)(2,1)S(1)} %bitcast.5), channel_id=1, source_target_pairs={{0,1},{1,0},{2,3},{3,2},{4,5},{5,4},{6,7},{7,6},{8,9},{9,8},{10,11... | collective-permute-start | bytes 786440 | tf_op jit(solution)/shard_map/ppermute | solution.py:43
  31.3 6.5 %collective-permute-start.12 = (bf16[4,32,256]{2,1,0:T(8,128)(2,1)S(1)}, bf16[4,32,256]{2,1,0:T(8,128)(2,1)S(1)}, u32[]{:S(2)}, u32[]{:S(2)}) collective-permute-start(bf16[4,32,256]{2,1,0:T(8,128)(2,1)S(1)} %lay.1.first_ref), channel_id=1, source_target_pairs={{0,2},{1,3},{2,0},{3,1},{4,6},{5,7},{6,4},{7,5},{8,10},{9,11},{10,... | collective-permute-start | bytes 196616 | tf_op jit(solution)/shard_map/ppermute | solution.py:356
  37.8 8.2 %collective-permute-start.14 = (bf16[256,512]{1,0:T(8,128)(2,1)S(1)}, bf16[256,512]{1,0:T(8,128)(2,1)S(1)}, u32[]{:S(2)}, u32[]{:S(2)}) collective-permute-start(bf16[256,512]{1,0:T(8,128)(2,1)S(1)} %collective-permute-done.10.refs_2_), channel_id=1, source_target_pairs={{0,4},{1,5},{4,8},{5,9},{8,12},{9,13},{12,14},{13,15},{14,10},{15,... | collective-permute-start | bytes 786440 | tf_op jit(solution)/shard_map/ppermute | solution.py:290
  37.9 8.2 %collective-permute-start.15 = (bf16[256,512]{1,0:T(8,128)(2,1)S(1)}, bf16[256,512]{1,0:T(8,128)(2,1)S(1)}, u32[]{:S(2)}, u32[]{:S(2)}) collective-permute-start(bf16[256,512]{1,0:T(8,128)(2,1)S(1)} %collective-permute-done.11.refs_4_), channel_id=1, source_target_pairs={{0,2},{1,3},{4,0},{5,1},{8,4},{9,5},{12,8},{13,9},{14,12},{15,13},... | collective-permute-start | bytes 786440 | tf_op jit(solution)/shard_map/ppermute | solution.py:291
  39.9 6.2 %collective-permute-start.17 = (bf16[256,512]{1,0:T(8,128)(2,1)S(1)}, bf16[256,512]{1,0:T(8,128)(2,1)S(1)}, u32[]{:S(2)}, u32[]{:S(2)}) collective-permute-start(bf16[256,512]{1,0:T(8,128)(2,1)S(1)} %collective-permute-done.10.refs_2_), channel_id=1, source_target_pairs={{0,1},{1,0},{2,3},{3,2},{4,5},{5,4},{6,7},{7,6},{8,9},{9,8},{10,11... | collective-permute-start | bytes 786440 | tf_op jit(solution)/shard_map/ppermute | solution.py:43
  39.9 6.2 %collective-permute-start.18 = (bf16[256,512]{1,0:T(8,128)(2,1)S(1)}, bf16[256,512]{1,0:T(8,128)(2,1)S(1)}, u32[]{:S(2)}, u32[]{:S(2)}) collective-permute-start(bf16[256,512]{1,0:T(8,128)(2,1)S(1)} %collective-permute-done.11.refs_4_), channel_id=1, source_target_pairs={{0,1},{1,0},{2,3},{3,2},{4,5},{5,4},{6,7},{7,6},{8,9},{9,8},{10,11... | collective-permute-start | bytes 786440 | tf_op jit(solution)/shard_map/ppermute | solution.py:43
  46.1 8.8 %collective-permute-start.19 = (bf16[256,512]{1,0:T(8,128)(2,1)S(1)}, bf16[256,512]{1,0:T(8,128)(2,1)S(1)}, u32[]{:S(2)}, u32[]{:S(2)}) collective-permute-start(bf16[256,512]{1,0:T(8,128)(2,1)S(1)} %collective-permute-done.14.refs_6_), channel_id=1, source_target_pairs={{0,4},{1,5},{4,8},{5,9},{8,12},{9,13},{12,14},{13,15},{14,10},{15,... | collective-permute-start | bytes 786440 | tf_op jit(solution)/shard_map/ppermute | solution.py:290
  46.6 8.3 %collective-permute-start.20 = (bf16[256,512]{1,0:T(8,128)(2,1)S(1)}, bf16[256,512]{1,0:T(8,128)(2,1)S(1)}, u32[]{:S(2)}, u32[]{:S(2)}) collective-permute-start(bf16[256,512]{1,0:T(8,128)(2,1)S(1)} %collective-permute-done.15.refs_8_), channel_id=1, source_target_pairs={{0,2},{1,3},{4,0},{5,1},{8,4},{9,5},{12,8},{13,9},{14,12},{15,13},... | collective-permute-start | bytes 786440 | tf_op jit(solution)/shard_map/ppermute | solution.py:291
  48.2 6.7 %collective-permute-start.21 = (bf16[256,512]{1,0:T(8,128)(2,1)S(1)}, bf16[256,512]{1,0:T(8,128)(2,1)S(1)}, u32[]{:S(2)}, u32[]{:S(2)}) collective-permute-start(bf16[256,512]{1,0:T(8,128)(2,1)S(1)} %collective-permute-done.14.refs_6_), channel_id=1, source_target_pairs={{0,1},{1,0},{2,3},{3,2},{4,5},{5,4},{6,7},{7,6},{8,9},{9,8},{10,11... | collective-permute-start | bytes 786440 | tf_op jit(solution)/shard_map/ppermute | solution.py:43
  48.2 6.7 %collective-permute-start.22 = (bf16[256,512]{1,0:T(8,128)(2,1)S(1)}, bf16[256,512]{1,0:T(8,128)(2,1)S(1)}, u32[]{:S(2)}, u32[]{:S(2)}) collective-permute-start(bf16[256,512]{1,0:T(8,128)(2,1)S(1)} %collective-permute-done.15.refs_8_), channel_id=1, source_target_pairs={{0,1},{1,0},{2,3},{3,2},{4,5},{5,4},{6,7},{7,6},{8,9},{9,8},{10,11... | collective-permute-start | bytes 786440 | tf_op jit(solution)/shard_map/ppermute | solution.py:43
  55.5 6.5 %collective-permute-start.25 = (bf16[128,512]{1,0:T(8,128)(2,1)S(1)}, bf16[128,512]{1,0:T(8,128)(2,1)S(1)}, u32[]{:S(2)}, u32[]{:S(2)}) collective-permute-start(bf16[128,512]{1,0:T(8,128)(2,1)S(1)} %slice.10), channel_id=1, source_target_pairs={{0,4},{1,5},{4,8},{5,9},{8,12},{9,13},{12,14},{13,15},{14,10},{15,... | collective-permute-start | bytes 393224 | tf_op jit(solution)/shard_map/ppermute | solution.py:290
  67.1 7.7 %collective-permute-start.30 = (bf16[48,512]{1,0:T(8,128)(2,1)S(1)}, bf16[48,512]{1,0:T(8,128)(2,1)S(1)}, u32[]{:S(2)}, u32[]{:S(2)}) collective-permute-start(bf16[48,512]{1,0:T(8,128)(2,1)S(1)} %get-tuple-element.98), channel_id=1, source_target_pairs={{0,12},{1,13},{2,14},{3,15},{4,8},{5,9},{6,10},{7,11},{8,4},{9,5},... | collective-permute-start | bytes 147464 | tf_op jit(solution)/shard_map/ppermute | solution.py:480
  69.5 8.6 %collective-permute-start.31 = (bf16[48,512]{1,0:T(8,128)(2,1)S(1)}, bf16[48,512]{1,0:T(8,128)(2,1)S(1)}, u32[]{:S(2)}, u32[]{:S(2)}) collective-permute-start(bf16[48,512]{1,0:T(8,128)(2,1)S(1)} %get-tuple-element.99), channel_id=1, source_target_pairs={{0,14},{1,15},{2,12},{3,13},{4,10},{5,11},{6,8},{7,9},{8,6},{9,7},... | collective-permute-start | bytes 147464 | tf_op jit(solution)/shard_map/ppermute | solution.py:480
  72.3 6.1 %collective-permute-start.32 = (bf16[48,512]{1,0:T(8,128)(2,1)S(1)}, bf16[48,512]{1,0:T(8,128)(2,1)S(1)}, u32[]{:S(2)}, u32[]{:S(2)}) collective-permute-start(bf16[48,512]{1,0:T(8,128)(2,1)S(1)} %get-tuple-element.100), channel_id=1, source_target_pairs={{0,8},{1,9},{2,10},{3,11},{4,12},{5,13},{6,14},{7,15},{8,0},{9,1},... | collective-permute-start | bytes 147464 | tf_op jit(solution)/shard_map/ppermute | solution.py:480
  72.3 8.7 %collective-permute-start.33 = (bf16[48,512]{1,0:T(8,128)(2,1)S(1)}, bf16[48,512]{1,0:T(8,128)(2,1)S(1)}, u32[]{:S(2)}, u32[]{:S(2)}) collective-permute-start(bf16[48,512]{1,0:T(8,128)(2,1)S(1)} %get-tuple-element.101), channel_id=1, source_target_pairs={{0,10},{1,11},{2,8},{3,9},{4,14},{5,15},{6,12},{7,13},{8,2},{9,3},... | collective-permute-start | bytes 147464 | tf_op jit(solution)/shard_map/ppermute | solution.py:480
  74.8 6.1 %collective-permute-start.34 = (bf16[48,512]{1,0:T(8,128)(2,1)S(1)}, bf16[48,512]{1,0:T(8,128)(2,1)S(1)}, u32[]{:S(2)}, u32[]{:S(2)}) collective-permute-start(bf16[48,512]{1,0:T(8,128)(2,1)S(1)} %get-tuple-element.102), channel_id=1, source_target_pairs={{0,4},{1,5},{2,6},{3,7},{4,0},{5,1},{6,2},{7,3},{8,12},{9,13},{10,... | collective-permute-start | bytes 147464 | tf_op jit(solution)/shard_map/ppermute | solution.py:480
  74.8 7.1 %collective-permute-start.35 = (bf16[48,512]{1,0:T(8,128)(2,1)S(1)}, bf16[48,512]{1,0:T(8,128)(2,1)S(1)}, u32[]{:S(2)}, u32[]{:S(2)}) collective-permute-start(bf16[48,512]{1,0:T(8,128)(2,1)S(1)} %get-tuple-element.103), channel_id=1, source_target_pairs={{0,6},{1,7},{2,4},{3,5},{4,2},{5,3},{6,0},{7,1},{8,14},{9,15},{10,... | collective-permute-start | bytes 147464 | tf_op jit(solution)/shard_map/ppermute | solution.py:480
  (17 other events, 68.5 us)

commit v19 on v18

--- a/solution.py
+++ b/solution.py
@@ -37,6 +37,11 @@
 
 def xor_pairs(n, key):
     return [(b, b ^ key) for b in range(n)]
+
+
+def exchange(x, n, stride):
+    groups = [list(range(first, n, stride)) for first in range(stride)]
+    return lax.all_to_all(x, "blk", 0, 0, axis_index_groups=groups, tiled=True)
 
 
 def swap(x, n):
@@ -71,28 +76,19 @@
 
 
 def rotate_in_kernel(tok_rows, near_ref, far_ref, basis_ref, out_ref):
-    tokens = out_ref.shape[0]
+    tokens = out_ref.shape[1]
     depth = near_ref.shape[2]
     acts = jnp.concatenate([ref[...].reshape(-1, depth) for ref in (near_ref, far_ref)], axis=0)
     rotated = jnp.dot(acts, basis_ref[...], preferred_element_type=jnp.float32)
     wanted = lax.broadcasted_iota(jnp.int32, (tokens, tokens), 0)
     held = held_tokens(lax.axis_index("blk"), tokens, tok_rows)
-    out_ref[...] = reorder(wanted, held, rotated).astype(jnp.bfloat16)
+    ordered = reorder(wanted, held, rotated).astype(jnp.bfloat16)
+    for copy in range(out_ref.shape[0]):
+        out_ref[copy] = ordered
 
 
 def keep_kernel(basis_ref, kept_ref):
     kept_ref[...] = basis_ref[...]
-
-
-def lay_kernel(*refs):
-    for at, ref in enumerate(refs[:-1]):
-        refs[-1][at] = ref[...]
-
-
-def stack_kernel(first_ref, last_ref, out_ref):
-    half = first_ref.shape[0]
-    out_ref[:half] = first_ref[...]
-    out_ref[half:] = last_ref[...]
 
 
 def rotate_part(first, near_ref, far_ref, basis_ref, basis, total, sem):
@@ -184,9 +180,8 @@
     for at, steps in enumerate(begun):
         for other, rotated_ref in enumerate((near_ref, far_ref)):
             source = ring_source(me, steps, other, chips)
-            key = (source ^ me) // 2
             piece = 2 * at + other
-            rotated[piece] = rotated_ref[lax.rem(key, 2) * (chips // 2) + key // 2]
+            rotated[piece] = rotated_ref[source // 2]
             for part in range(per_piece):
                 lanes[piece * per_piece + part] = tiles[source * per_piece + part] * LANES
 
@@ -324,7 +319,7 @@
     acts = jnp.concatenate([acts, acts_got], axis=0)
     rotated = pl.pallas_call(
         functools.partial(rotate_in_kernel, tok_rows),
-        out_shape=jax.ShapeDtypeStruct((tokens, in_width), jnp.bfloat16),
+        out_shape=jax.ShapeDtypeStruct((chips, tokens, in_width), jnp.bfloat16),
         in_specs=[VMEM, VMEM, VMEM],
         out_specs=VMEM,
         compiler_params=pltpu.CompilerParams(vmem_limit_bytes=8 * MIB),
@@ -332,28 +327,12 @@
         name="rotate_in",
     )(acts, swap(acts, n), kept)
 
-    def lay(kernel, shape, *blocks):
-        return pl.pallas_call(
-            kernel,
-            out_shape=jax.ShapeDtypeStruct(shape, jnp.bfloat16),
-            in_specs=[VMEM] * len(blocks),
-            out_specs=VMEM,
-            compiler_params=pltpu.CompilerParams(vmem_limit_bytes=8 * MIB),
-            cost_estimate=CHEAP,
-            name=kernel.__name__[:-7],
-        )(*blocks)
-
-    grads_got, _ = after(grads_got, rotated)
-    blocks = [rotated] + [
-        lax.ppermute(rotated, "blk", xor_pairs(n, 4 * key)) for key in range(1, pairs)
-    ]
-    rotated = lay(lay_kernel, (pairs, tokens, in_width), *blocks)
-    rotated, own = after(rotated, own)
+    grads_got, own, _ = after(grads_got, own, rotated)
+    rotated = exchange(rotated, n, 2)
     right, left = [own, to_right(own)], [own, to_left(own)]
     grads = jnp.concatenate([grads, grads_got], axis=0)
     grads_far = swap(grads, n)
     far = [swap(own, n)]
-    rotated_got = lax.ppermute(rotated, "blk", xor_pairs(n, 2))
 
     rotate = lambda kernel, count, scratch, shape, dtype, *operands: pl.pallas_call(
         kernel,
@@ -377,10 +356,9 @@
         grads_far,
         basis_out,
     )
-    start, grads, right[-1], left[-1], rotated_got, *far = after(
-        start, grads, right[-1], left[-1], rotated_got, *far
-    )
-    rotated = lay(stack_kernel, (chips, tokens, in_width), rotated, rotated_got)
+    start, grads, right[-1], left[-1], rotated, *far = after(
+        start, grads, right[-1], left[-1], rotated, *far
+    )
     rotated_far = swap(rotated, n)
     far += [swap(right[-1], n), swap(left[-1], n)]
     right.append(to_right(right[-1]))

time: 83.3 us -> 80.4 us (0.965)
  waiting for transfers between devices: 19.1 us -> 16.3 us
  starting transfers between devices: 35.4 us -> 34.5 us
    ppermute x4 -> x0, starting transfers between devices: 5.28 us -> none  [the longest x3 4.45 us: ring_body(): lax.ppermute(rotated, 'blk', xor_pairs(n, 4 * key))]
    ppermute x4 -> x0, waiting for transfers between devices: 4.34 us -> none  [the longest x3 3.92 us: ring_body(): lax.ppermute(rotated, 'blk', xor_pairs(n, 4 * key))]
    all_to_all x0 -> x1, starting transfers between devices: none -> 4.33 us  [exchange(): return lax.all_to_all(x, 'blk', 0, 0, axis_index_groups=groups, tiled=True)]
    all_to_all x0 -> x1, waiting for transfers between devices: none -> 2.4 us  [exchange(): return lax.all_to_all(x, 'blk', 0, 0, axis_index_groups=groups, tiled=True)]
    ppermute x4, starting transfers between devices: 6.47 us -> 5.37 us  [ring_body(): to_left = lambda x: lax.ppermute(x, 'blk', shift_pairs(n, -1))]
    ppermute x4, starting transfers between devices: 1.83 us -> 2.9 us  [ring_body(): to_right = lambda x: lax.ppermute(x, 'blk', shift_pairs(n, 1))]
  transfers between devices with their start and end apart: 37 -> 34, of which waited for: 15 -> 11; matrix products, arithmetic and copies ran while one was open for 1% -> 1% of each run, Pallas kernels for 26% -> 28%
where the time goes in v19:
time: 80.4 us; the launch traced here: 80.1 us
  starting transfers between devices  34.5 us (43%)
  Pallas kernels  25.1 us (31%)
  waiting for transfers between devices  16.3 us (20%)
  local copies, waits for them, and re-layouts  3.02 us (4%)
  other arithmetic  0.91 us (1%)
    ppermute x7, starting transfers between devices, ring_body(): lax.ppermute(x, 'blk', xor_pairs(n, 2 * key))  11.2 us
    pallas_call x2, Pallas kernels, ring_body(): pl.pallas_call(kernel, out_shape=jax.ShapeDtypeStruct(shape, dtype), in_s...  10.7 us
    pallas_call x1, Pallas kernels, ring_body(): pl.pallas_call(functools.partial(scale_kernel, begun), out_shape=jax.Shap...  6.26 us
    ppermute x3, starting transfers between devices, ring_body(): lax.ppermute(both, 'blk', xor_pairs(n, 4 * key))  5.68 us
    ppermute x4, starting transfers between devices, ring_body(): to_left = lambda x: lax.ppermute(x, 'blk', shift_pairs(n, -1))  5.37 us
    pallas_call x1, Pallas kernels, ring_body(): pl.pallas_call(functools.partial(project_kernel, (0, 6, len(pieces))), ou...  4.39 us
    all_to_all x1, starting transfers between devices, exchange(): return lax.all_to_all(x, 'blk', 0, 0, axis_index_groups=groups, tiled=True)  4.33 us
    ppermute x7, waiting for transfers between devices, ring_body(): lax.ppermute(x, 'blk', xor_pairs(n, 2 * key))  3.8 us
  transfers between devices with their start and end apart: 34, of which 11 were waited for; matrix products, arithmetic and copies ran while one was open for 1% of the time, Pallas kernels for 28%

profile of v19, /device:TPU:0, one launch (start us, length us, event | category | flops | bytes accessed | tf_op | source)
XLA Modules:
  0.0 80.1 jit_solution(15007711606900166004)
XLA Ops:
  0.9 3.1 %collective-permute-start = (bf16[1,2,18432]{2,1,0:T(2,128)(2,1)S(1)}, bf16[1,2,18432]{2,1,0:T(2,128)(2,1)S(1)}, u32[]{:S(2)}, u32[]{:S(2)}) collective-permute-start(bf16[1,2,18432]{2,1,0:T(2,128)(2,1)S(1)} %maximum_bitcast_fusion.refs_0_), channel_id=1, source_target_pairs={{0,4},{1,5},{2,6},{3,7},{4,0},{5,1},{6,2},{7,3},{8,12},{9,13},{10,... | collective-permute-start | bytes 221192 | tf_op jit(solution)/shard_map/ppermute | solution.py:293
  4.0 2.6 %collective-permute-start.1 = (bf16[1,2,18432]{2,1,0:T(2,128)(2,1)S(1)}, bf16[1,2,18432]{2,1,0:T(2,128)(2,1)S(1)}, u32[]{:S(2)}, u32[]{:S(2)}) collective-permute-start(bf16[1,2,18432]{2,1,0:T(2,128)(2,1)S(1)} %maximum_bitcast_fusion.refs_0_), channel_id=1, source_target_pairs={{0,8},{1,9},{2,10},{3,11},{4,12},{5,13},{6,14},{7,15},{8,0},{9,1},... | collective-permute-start | bytes 221192 | tf_op jit(solution)/shard_map/ppermute | solution.py:293
  6.6 1.6 %copy-done = bf16[4096,256]{1,0:T(8,128)(2,1)S(1)} copy-done((bf16[4096,256]{1,0:T(8,128)(2,1)S(1)}, bf16[4096,256]{1,0:T(8,128)(2,1)}, u32[]{:S(2)}) %copy-start) | copy-done | bytes 2097176
  9.3 2.5 %collective-permute-done.1.refs_2_ = bf16[1,2,18432]{2,1,0:T(2,128)(2,1)S(1)} collective-permute-done((bf16[1,2,18432]{2,1,0:T(2,128)(2,1)S(1)}, bf16[1,2,18432]{2,1,0:T(2,128)(2,1)S(1)}, u32[]{:S(2)}, u32[]{:S(2)}) %collective-permute-start.1) | collective-permute-done | bytes 73760 | tf_op jit(solution)/shard_map/ppermute | solution.py:293
  12.9 1.6 %collective-permute-start.4 = (bf16[4,2,4096]{2,1,0:T(2,128)(2,1)S(1)}, bf16[4,2,4096]{2,1,0:T(2,128)(2,1)S(1)}, u32[]{:S(2)}, u32[]{:S(2)}) collective-permute-start(bf16[4,2,4096]{2,1,0:T(2,128)(2,1)S(1)} %get-tuple-element.63), channel_id=1, source_target_pairs={{0,2},{1,3},{2,0},{3,1},{4,6},{5,7},{6,4},{7,5},{8,10},{9,11},{10,... | collective-permute-start | bytes 196616 | tf_op jit(solution)/shard_map/ppermute | solution.py:317
  15.1 2.9 %collective-permute-done.4 = bf16[4,2,4096]{2,1,0:T(2,128)(2,1)S(1)} collective-permute-done((bf16[4,2,4096]{2,1,0:T(2,128)(2,1)S(1)}, bf16[4,2,4096]{2,1,0:T(2,128)(2,1)S(1)}, u32[]{:S(2)}, u32[]{:S(2)}) %collective-permute-start.4) | collective-permute-done | bytes 65568 | tf_op jit(solution)/shard_map/ppermute | solution.py:317
  18.3 1.2 %collective-permute-done.5.far_ref = bf16[8,2,4096]{2,1,0:T(2,128)(2,1)S(1)} collective-permute-done((bf16[8,2,4096]{2,1,0:T(2,128)(2,1)S(1)}, bf16[8,2,4096]{2,1,0:T(2,128)(2,1)S(1)}, u32[]{:S(2)}, u32[]{:S(2)}) %collective-permute-start.5) | collective-permute-done | bytes 131104 | tf_op jit(solution)/shard_map/ppermute | solution.py:48
  19.4 1.2 %rotate_in.1 = bf16[8,32,256]{2,1,0:T(8,128)(2,1)} custom-call(bf16[8,2,4096]{2,1,0:T(2,128)(2,1)S(1)} %constant_dynamic-update-slice_fusion.near_ref, bf16[8,2,4096]{2,1,0:T(2,128)(2,1)S(1)} %collective-permute-done.5.far_ref, bf16[4096,256]{1,0:T(8,128)(2,1)S(1)} %keep.1.basis_ref), custom_call_target="tpu_custom_call" | custom-call | flops 1 | bytes 1 | tf_op jit(solution)/shard_map/rotate_in/pallas_call | solution.py:320
  23.1 4.3 %all-to-all-start = ((bf16[8,32,256]{2,1,0:T(8,128)(2,1)}), bf16[8,32,256]{2,1,0:T(8,128)(2,1)S(1)}, u32[]{:S(2)}, u32[]{:S(2)}) async-start(bf16[8,32,256]{2,1,0:T(8,128)(2,1)} %rotate_in.1), calls=%async_computation | async-start | bytes 262144 | tf_op jit(solution)/shard_map/all_to_all | solution.py:44
  27.4 5.2 %rotate_first.1.start_ref = f32[32,896]{1,0:T(8,128)S(1)} custom-call(bf16[8,2,14336]{2,1,0:T(2,128)(2,1)S(1)} %constant_dynamic-update-slice_fusion.2.near_ref, bf16[8,2,14336]{2,1,0:T(2,128)(2,1)S(1)} %collective-permute-done.6.far_ref, bf16[14336,896]{1,0:T(8,128)(2,1)} %basis_out_ref.1), custom_call_target="tpu_custom_call" | custom-call | flops 1 | bytes 1 | tf_op jit(solution)/shard_map/rotate_first/pallas_call | solution.py:337
  32.7 2.4 %all-to-all-done.near_ref = bf16[8,32,256]{2,1,0:T(8,128)(2,1)S(1)} async-done(((bf16[8,32,256]{2,1,0:T(8,128)(2,1)}), bf16[8,32,256]{2,1,0:T(8,128)(2,1)S(1)}, u32[]{:S(2)}, u32[]{:S(2)}) %all-to-all-start) | async-done | bytes 131104 | tf_op jit(solution)/shard_map/all_to_all | solution.py:44
  35.2 2.0 %collective-permute-start.11 = (bf16[256,512]{1,0:T(8,128)(2,1)S(1)}, bf16[256,512]{1,0:T(8,128)(2,1)S(1)}, u32[]{:S(2)}, u32[]{:S(2)}) collective-permute-start(bf16[256,512]{1,0:T(8,128)(2,1)S(1)} %collective-permute-done.8.refs_4_), channel_id=1, source_target_pairs={{0,2},{1,3},{4,0},{5,1},{8,4},{9,5},{12,8},{13,9},{14,12},{15,13},... | collective-permute-start | bytes 786440 | tf_op jit(solution)/shard_map/ppermute | solution.py:286
  37.7 5.5 %rotate_last.1.aligned_ref = bf16[896,32]{1,0:T(8,128)(2,1)S(1)} custom-call(bf16[8,2,14336]{2,1,0:T(2,128)(2,1)S(1)} %constant_dynamic-update-slice_fusion.2.near_ref, bf16[8,2,14336]{2,1,0:T(2,128)(2,1)S(1)} %collective-permute-done.6.far_ref, bf16[14336,896]{1,0:T(8,128)(2,1)} %basis_out_ref.1, s32[16]{0:T(128)S(1)} %copy-done.2, ...), custom_call_target="tpu_custom_call" | custom-call | flops 1 | bytes 1 | tf_op jit(solution)/shard_map/rotate_last/pallas_call | solution.py:337
  44.1 1.2 %collective-permute-start.16 = (bf16[256,512]{1,0:T(8,128)(2,1)S(1)}, bf16[256,512]{1,0:T(8,128)(2,1)S(1)}, u32[]{:S(2)}, u32[]{:S(2)}) collective-permute-start(bf16[256,512]{1,0:T(8,128)(2,1)S(1)} %collective-permute-done.11.refs_8_), channel_id=1, source_target_pairs={{0,2},{1,3},{4,0},{5,1},{8,4},{9,5},{12,8},{13,9},{14,12},{15,13},... | collective-permute-start | bytes 786440 | tf_op jit(solution)/shard_map/ppermute | solution.py:286
  45.8 6.3 %scale.1.scaled_ref = bf16[896,4096]{1,0:T(8,128)(2,1)S(1)} custom-call(bf16[896,32]{1,0:T(8,128)(2,1)S(1)} %rotate_last.1.aligned_ref, bf16[8,32,256]{2,1,0:T(8,128)(2,1)S(1)} %all-to-all-done.near_ref, bf16[8,32,256]{2,1,0:T(8,128)(2,1)S(1)} %collective-permute-done.12.far_ref, s32[32]{0:T(128)S(1)} %copy-done.1, f32[896,4096]{1,0:T(8,128)} %eigen_ref.1), custom_call_target="tpu_custom_call" | custom-call | flops 1 | bytes 1 | tf_op jit(solution)/shard_map/scale/pallas_call | solution.py:390
  53.6 1.2 %collective-permute-start.22 = (bf16[128,512]{1,0:T(8,128)(2,1)S(1)}, bf16[128,512]{1,0:T(8,128)(2,1)S(1)}, u32[]{:S(2)}, u32[]{:S(2)}) collective-permute-start(bf16[128,512]{1,0:T(8,128)(2,1)S(1)} %slice.11), channel_id=1, source_target_pairs={{0,2},{1,3},{4,0},{5,1},{8,4},{9,5},{12,8},{13,9},{14,12},{15,13},... | collective-permute-start | bytes 393224 | tf_op jit(solution)/shard_map/ppermute | solution.py:286
  54.9 4.4 %project.1 = (f32[896,512]{1,0:T(8,128)S(1)}, bf16[768,896]{1,0:T(8,128)(2,1)S(1)}) custom-call(bf16[896,4096]{1,0:T(8,128)(2,1)S(1)} %scale.1.scaled_ref, bf16[14336,896]{1,0:T(8,128)(2,1)} %basis_out_ref.1, bf16[256,512]{1,0:T(8,128)(2,1)S(1)} %bitcast.6, bf16[256,512]{1,0:T(8,128)(2,1)S(1)} %collective-permute-done.9.refs_1_, ...), custom_call_target="tpu_custom_call" | custom-call | flops 1 | bytes 1 | tf_op jit(solution)/shard_map/project/pallas_call | solution.py:413
  60.9 1.6 %window.1 = (bf16[8,48,512]{2,1,0:T(8,128)(2,1)S(1)}, f32[8,48,512]{2,1,0:T(8,128)S(1)}) custom-call(bf16[768,896]{1,0:T(8,128)(2,1)S(1)} %get-tuple-element.88.window_ref, bf16[896,4096]{1,0:T(8,128)(2,1)S(1)} %scale.1.scaled_ref, f32[896,512]{1,0:T(8,128)S(1)} %get-tuple-element.90.projected_ref, bf16[128,512]{1,0:T(8,128)(2,1)S(1)} %collective-permute-done.21.refs_0_, ...), custom_call_target="tpu_custom_call" | custom-call | flops 1 | bytes 1 | tf_op jit(solution)/shard_map/window/pallas_call | solution.py:433
  62.9 1.4 %collective-permute-done.25.got_ref = bf16[8,48,512]{2,1,0:T(8,128)(2,1)S(1)} collective-permute-done((bf16[8,48,512]{2,1,0:T(8,128)(2,1)S(1)}, bf16[8,48,512]{2,1,0:T(8,128)(2,1)S(1)}, u32[]{:S(2)}, u32[]{:S(2)}) %collective-permute-start.25) | collective-permute-done | bytes 393248 | tf_op jit(solution)/shard_map/ppermute | solution.py:48
  64.4 2.7 %collective-permute-start.26 = (bf16[48,512]{1,0:T(8,128)(2,1)S(1)}, bf16[48,512]{1,0:T(8,128)(2,1)S(1)}, u32[]{:S(2)}, u32[]{:S(2)}) collective-permute-start(bf16[48,512]{1,0:T(8,128)(2,1)S(1)} %get-tuple-element.96), channel_id=1, source_target_pairs={{0,12},{1,13},{2,14},{3,15},{4,8},{5,9},{6,10},{7,11},{8,4},{9,5},... | collective-permute-start | bytes 147464 | tf_op jit(solution)/shard_map/ppermute | solution.py:458
  67.0 2.2 %collective-permute-start.27 = (bf16[48,512]{1,0:T(8,128)(2,1)S(1)}, bf16[48,512]{1,0:T(8,128)(2,1)S(1)}, u32[]{:S(2)}, u32[]{:S(2)}) collective-permute-start(bf16[48,512]{1,0:T(8,128)(2,1)S(1)} %get-tuple-element.97), channel_id=1, source_target_pairs={{0,14},{1,15},{2,12},{3,13},{4,10},{5,11},{6,8},{7,9},{8,6},{9,7},... | collective-permute-start | bytes 147464 | tf_op jit(solution)/shard_map/ppermute | solution.py:458
  69.2 2.8 %collective-permute-start.29 = (bf16[48,512]{1,0:T(8,128)(2,1)S(1)}, bf16[48,512]{1,0:T(8,128)(2,1)S(1)}, u32[]{:S(2)}, u32[]{:S(2)}) collective-permute-start(bf16[48,512]{1,0:T(8,128)(2,1)S(1)} %get-tuple-element.99), channel_id=1, source_target_pairs={{0,10},{1,11},{2,8},{3,9},{4,14},{5,15},{6,12},{7,13},{8,2},{9,3},... | collective-permute-start | bytes 147464 | tf_op jit(solution)/shard_map/ppermute | solution.py:458
  72.3 2.8 %collective-permute-start.31 = (bf16[48,512]{1,0:T(8,128)(2,1)S(1)}, bf16[48,512]{1,0:T(8,128)(2,1)S(1)}, u32[]{:S(2)}, u32[]{:S(2)}) collective-permute-start(bf16[48,512]{1,0:T(8,128)(2,1)S(1)} %get-tuple-element.101), channel_id=1, source_target_pairs={{0,6},{1,7},{2,4},{3,5},{4,2},{5,3},{6,0},{7,1},{8,14},{9,15},{10,... | collective-permute-start | bytes 147464 | tf_op jit(solution)/shard_map/ppermute | solution.py:458
  75.6 2.1 %collective-permute-done.29.refs_3_ = bf16[48,512]{1,0:T(8,128)(2,1)S(1)} collective-permute-done((bf16[48,512]{1,0:T(8,128)(2,1)S(1)}, bf16[48,512]{1,0:T(8,128)(2,1)S(1)}, u32[]{:S(2)}, u32[]{:S(2)}) %collective-permute-start.29) | collective-permute-done | bytes 49184 | tf_op jit(solution)/shard_map/ppermute | solution.py:458
  (70 shorter events, 15.0 us)
Async XLA Ops:
  0.9 8.4 %collective-permute-start = (bf16[1,2,18432]{2,1,0:T(2,128)(2,1)S(1)}, bf16[1,2,18432]{2,1,0:T(2,128)(2,1)S(1)}, u32[]{:S(2)}, u32[]{:S(2)}) collective-permute-start(bf16[1,2,18432]{2,1,0:T(2,128)(2,1)S(1)} %maximum_bitcast_fusion.refs_0_), channel_id=1, source_target_pairs={{0,4},{1,5},{2,6},{3,7},{4,0},{5,1},{6,2},{7,3},{8,12},{9,13},{10,... | collective-permute-start | bytes 221192 | tf_op jit(solution)/shard_map/ppermute | solution.py:293
  4.0 7.8 %collective-permute-start.1 = (bf16[1,2,18432]{2,1,0:T(2,128)(2,1)S(1)}, bf16[1,2,18432]{2,1,0:T(2,128)(2,1)S(1)}, u32[]{:S(2)}, u32[]{:S(2)}) collective-permute-start(bf16[1,2,18432]{2,1,0:T(2,128)(2,1)S(1)} %maximum_bitcast_fusion.refs_0_), channel_id=1, source_target_pairs={{0,8},{1,9},{2,10},{3,11},{4,12},{5,13},{6,14},{7,15},{8,0},{9,1},... | collective-permute-start | bytes 221192 | tf_op jit(solution)/shard_map/ppermute | solution.py:293
  6.6 6.3 %collective-permute-start.2 = (bf16[1,2,18432]{2,1,0:T(2,128)(2,1)S(1)}, bf16[1,2,18432]{2,1,0:T(2,128)(2,1)S(1)}, u32[]{:S(2)}, u32[]{:S(2)}) collective-permute-start(bf16[1,2,18432]{2,1,0:T(2,128)(2,1)S(1)} %maximum_bitcast_fusion.refs_0_), channel_id=1, source_target_pairs={{0,12},{1,13},{2,14},{3,15},{4,8},{5,9},{6,10},{7,11},{8,4},{9,5},... | collective-permute-start | bytes 221192 | tf_op jit(solution)/shard_map/ppermute | solution.py:293
  14.5 6.2 %collective-permute-start.3 = (bf16[4,2,14336]{2,1,0:T(2,128)(2,1)S(1)}, bf16[4,2,14336]{2,1,0:T(2,128)(2,1)S(1)}, u32[]{:S(2)}, u32[]{:S(2)}) collective-permute-start(bf16[4,2,14336]{2,1,0:T(2,128)(2,1)S(1)} %get-tuple-element.61), channel_id=1, source_target_pairs={{0,2},{1,3},{2,0},{3,1},{4,6},{5,7},{6,4},{7,5},{8,10},{9,11},{10,... | collective-permute-start | bytes 688136 | tf_op jit(solution)/shard_map/ppermute | solution.py:318
  20.8 6.6 %collective-permute-start.6 = (bf16[8,2,14336]{2,1,0:T(2,128)(2,1)S(1)}, bf16[8,2,14336]{2,1,0:T(2,128)(2,1)S(1)}, u32[]{:S(2)}, u32[]{:S(2)}) collective-permute-start(bf16[8,2,14336]{2,1,0:T(2,128)(2,1)S(1)} %constant_dynamic-update-slice_fusion.2.near_ref), channel_id=1, source_target_pairs={{0,1},{1,0},{2,3},{3,2},{4,5},{5,4},{6,7},{7,6},{8,9},{9,8},{10,11... | collective-permute-start | bytes 1376264 | tf_op jit(solution)/shard_map/ppermute | solution.py:48
  21.1 14.0 %collective-permute-start.7 = (bf16[256,512]{1,0:T(8,128)(2,1)S(1)}, bf16[256,512]{1,0:T(8,128)(2,1)S(1)}, u32[]{:S(2)}, u32[]{:S(2)}) collective-permute-start(bf16[256,512]{1,0:T(8,128)(2,1)S(1)} %bitcast.3), channel_id=1, source_target_pairs={{0,4},{1,5},{4,8},{5,9},{8,12},{9,13},{12,14},{13,15},{14,10},{15,... | collective-permute-start | bytes 786440 | tf_op jit(solution)/shard_map/ppermute | solution.py:285
  22.2 12.9 %collective-permute-start.8 = (bf16[256,512]{1,0:T(8,128)(2,1)S(1)}, bf16[256,512]{1,0:T(8,128)(2,1)S(1)}, u32[]{:S(2)}, u32[]{:S(2)}) collective-permute-start(bf16[256,512]{1,0:T(8,128)(2,1)S(1)} %bitcast.4), channel_id=1, source_target_pairs={{0,2},{1,3},{4,0},{5,1},{8,4},{9,5},{12,8},{13,9},{14,12},{15,13},... | collective-permute-start | bytes 786440 | tf_op jit(solution)/shard_map/ppermute | solution.py:286
  23.1 12.0 %collective-permute-start.9 = (bf16[256,512]{1,0:T(8,128)(2,1)S(1)}, bf16[256,512]{1,0:T(8,128)(2,1)S(1)}, u32[]{:S(2)}, u32[]{:S(2)}) collective-permute-start(bf16[256,512]{1,0:T(8,128)(2,1)S(1)} %bitcast.5), channel_id=1, source_target_pairs={{0,1},{1,0},{2,3},{3,2},{4,5},{5,4},{6,7},{7,6},{8,9},{9,8},{10,11... | collective-permute-start | bytes 786440 | tf_op jit(solution)/shard_map/ppermute | solution.py:48
  23.1 12.0 %all-to-all-start = ((bf16[8,32,256]{2,1,0:T(8,128)(2,1)}), bf16[8,32,256]{2,1,0:T(8,128)(2,1)S(1)}, u32[]{:S(2)}, u32[]{:S(2)}) async-start(bf16[8,32,256]{2,1,0:T(8,128)(2,1)} %rotate_in.1), calls=%async_computation | async-start | bytes 262144 | tf_op jit(solution)/shard_map/all_to_all | solution.py:44
  35.1 8.1 %collective-permute-start.10 = (bf16[256,512]{1,0:T(8,128)(2,1)S(1)}, bf16[256,512]{1,0:T(8,128)(2,1)S(1)}, u32[]{:S(2)}, u32[]{:S(2)}) collective-permute-start(bf16[256,512]{1,0:T(8,128)(2,1)S(1)} %collective-permute-done.7.refs_2_), channel_id=1, source_target_pairs={{0,4},{1,5},{4,8},{5,9},{8,12},{9,13},{12,14},{13,15},{14,10},{15,... | collective-permute-start | bytes 786440 | tf_op jit(solution)/shard_map/ppermute | solution.py:285
  35.2 8.1 %collective-permute-start.11 = (bf16[256,512]{1,0:T(8,128)(2,1)S(1)}, bf16[256,512]{1,0:T(8,128)(2,1)S(1)}, u32[]{:S(2)}, u32[]{:S(2)}) collective-permute-start(bf16[256,512]{1,0:T(8,128)(2,1)S(1)} %collective-permute-done.8.refs_4_), channel_id=1, source_target_pairs={{0,2},{1,3},{4,0},{5,1},{8,4},{9,5},{12,8},{13,9},{14,12},{15,13},... | collective-permute-start | bytes 786440 | tf_op jit(solution)/shard_map/ppermute | solution.py:286
  37.2 6.1 %collective-permute-start.13 = (bf16[256,512]{1,0:T(8,128)(2,1)S(1)}, bf16[256,512]{1,0:T(8,128)(2,1)S(1)}, u32[]{:S(2)}, u32[]{:S(2)}) collective-permute-start(bf16[256,512]{1,0:T(8,128)(2,1)S(1)} %collective-permute-done.7.refs_2_), channel_id=1, source_target_pairs={{0,1},{1,0},{2,3},{3,2},{4,5},{5,4},{6,7},{7,6},{8,9},{9,8},{10,11... | collective-permute-start | bytes 786440 | tf_op jit(solution)/shard_map/ppermute | solution.py:48
  37.2 6.1 %collective-permute-start.14 = (bf16[256,512]{1,0:T(8,128)(2,1)S(1)}, bf16[256,512]{1,0:T(8,128)(2,1)S(1)}, u32[]{:S(2)}, u32[]{:S(2)}) collective-permute-start(bf16[256,512]{1,0:T(8,128)(2,1)S(1)} %collective-permute-done.8.refs_4_), channel_id=1, source_target_pairs={{0,1},{1,0},{2,3},{3,2},{4,5},{5,4},{6,7},{7,6},{8,9},{9,8},{10,11... | collective-permute-start | bytes 786440 | tf_op jit(solution)/shard_map/ppermute | solution.py:48
  43.3 8.9 %collective-permute-start.15 = (bf16[256,512]{1,0:T(8,128)(2,1)S(1)}, bf16[256,512]{1,0:T(8,128)(2,1)S(1)}, u32[]{:S(2)}, u32[]{:S(2)}) collective-permute-start(bf16[256,512]{1,0:T(8,128)(2,1)S(1)} %collective-permute-done.10.refs_6_), channel_id=1, source_target_pairs={{0,4},{1,5},{4,8},{5,9},{8,12},{9,13},{12,14},{13,15},{14,10},{15,... | collective-permute-start | bytes 786440 | tf_op jit(solution)/shard_map/ppermute | solution.py:285
  44.1 8.0 %collective-permute-start.16 = (bf16[256,512]{1,0:T(8,128)(2,1)S(1)}, bf16[256,512]{1,0:T(8,128)(2,1)S(1)}, u32[]{:S(2)}, u32[]{:S(2)}) collective-permute-start(bf16[256,512]{1,0:T(8,128)(2,1)S(1)} %collective-permute-done.11.refs_8_), channel_id=1, source_target_pairs={{0,2},{1,3},{4,0},{5,1},{8,4},{9,5},{12,8},{13,9},{14,12},{15,13},... | collective-permute-start | bytes 786440 | tf_op jit(solution)/shard_map/ppermute | solution.py:286
  45.3 6.8 %collective-permute-start.17 = (bf16[256,512]{1,0:T(8,128)(2,1)S(1)}, bf16[256,512]{1,0:T(8,128)(2,1)S(1)}, u32[]{:S(2)}, u32[]{:S(2)}) collective-permute-start(bf16[256,512]{1,0:T(8,128)(2,1)S(1)} %collective-permute-done.10.refs_6_), channel_id=1, source_target_pairs={{0,1},{1,0},{2,3},{3,2},{4,5},{5,4},{6,7},{7,6},{8,9},{9,8},{10,11... | collective-permute-start | bytes 786440 | tf_op jit(solution)/shard_map/ppermute | solution.py:48
  45.3 6.8 %collective-permute-start.18 = (bf16[256,512]{1,0:T(8,128)(2,1)S(1)}, bf16[256,512]{1,0:T(8,128)(2,1)S(1)}, u32[]{:S(2)}, u32[]{:S(2)}) collective-permute-start(bf16[256,512]{1,0:T(8,128)(2,1)S(1)} %collective-permute-done.11.refs_8_), channel_id=1, source_target_pairs={{0,1},{1,0},{2,3},{3,2},{4,5},{5,4},{6,7},{7,6},{8,9},{9,8},{10,11... | collective-permute-start | bytes 786440 | tf_op jit(solution)/shard_map/ppermute | solution.py:48
  52.8 6.5 %collective-permute-start.21 = (bf16[128,512]{1,0:T(8,128)(2,1)S(1)}, bf16[128,512]{1,0:T(8,128)(2,1)S(1)}, u32[]{:S(2)}, u32[]{:S(2)}) collective-permute-start(bf16[128,512]{1,0:T(8,128)(2,1)S(1)} %slice.10), channel_id=1, source_target_pairs={{0,4},{1,5},{4,8},{5,9},{8,12},{9,13},{12,14},{13,15},{14,10},{15,... | collective-permute-start | bytes 393224 | tf_op jit(solution)/shard_map/ppermute | solution.py:285
  53.6 5.6 %collective-permute-start.22 = (bf16[128,512]{1,0:T(8,128)(2,1)S(1)}, bf16[128,512]{1,0:T(8,128)(2,1)S(1)}, u32[]{:S(2)}, u32[]{:S(2)}) collective-permute-start(bf16[128,512]{1,0:T(8,128)(2,1)S(1)} %slice.11), channel_id=1, source_target_pairs={{0,2},{1,3},{4,0},{5,1},{8,4},{9,5},{12,8},{13,9},{14,12},{15,13},... | collective-permute-start | bytes 393224 | tf_op jit(solution)/shard_map/ppermute | solution.py:286
  64.4 8.0 %collective-permute-start.26 = (bf16[48,512]{1,0:T(8,128)(2,1)S(1)}, bf16[48,512]{1,0:T(8,128)(2,1)S(1)}, u32[]{:S(2)}, u32[]{:S(2)}) collective-permute-start(bf16[48,512]{1,0:T(8,128)(2,1)S(1)} %get-tuple-element.96), channel_id=1, source_target_pairs={{0,12},{1,13},{2,14},{3,15},{4,8},{5,9},{6,10},{7,11},{8,4},{9,5},... | collective-permute-start | bytes 147464 | tf_op jit(solution)/shard_map/ppermute | solution.py:458
  67.0 8.1 %collective-permute-start.27 = (bf16[48,512]{1,0:T(8,128)(2,1)S(1)}, bf16[48,512]{1,0:T(8,128)(2,1)S(1)}, u32[]{:S(2)}, u32[]{:S(2)}) collective-permute-start(bf16[48,512]{1,0:T(8,128)(2,1)S(1)} %get-tuple-element.97), channel_id=1, source_target_pairs={{0,14},{1,15},{2,12},{3,13},{4,10},{5,11},{6,8},{7,9},{8,6},{9,7},... | collective-permute-start | bytes 147464 | tf_op jit(solution)/shard_map/ppermute | solution.py:458
  69.2 6.3 %collective-permute-start.28 = (bf16[48,512]{1,0:T(8,128)(2,1)S(1)}, bf16[48,512]{1,0:T(8,128)(2,1)S(1)}, u32[]{:S(2)}, u32[]{:S(2)}) collective-permute-start(bf16[48,512]{1,0:T(8,128)(2,1)S(1)} %get-tuple-element.98), channel_id=1, source_target_pairs={{0,8},{1,9},{2,10},{3,11},{4,12},{5,13},{6,14},{7,15},{8,0},{9,1},... | collective-permute-start | bytes 147464 | tf_op jit(solution)/shard_map/ppermute | solution.py:458
  69.2 8.5 %collective-permute-start.29 = (bf16[48,512]{1,0:T(8,128)(2,1)S(1)}, bf16[48,512]{1,0:T(8,128)(2,1)S(1)}, u32[]{:S(2)}, u32[]{:S(2)}) collective-permute-start(bf16[48,512]{1,0:T(8,128)(2,1)S(1)} %get-tuple-element.99), channel_id=1, source_target_pairs={{0,10},{1,11},{2,8},{3,9},{4,14},{5,15},{6,12},{7,13},{8,2},{9,3},... | collective-permute-start | bytes 147464 | tf_op jit(solution)/shard_map/ppermute | solution.py:458
  72.3 6.5 %collective-permute-start.31 = (bf16[48,512]{1,0:T(8,128)(2,1)S(1)}, bf16[48,512]{1,0:T(8,128)(2,1)S(1)}, u32[]{:S(2)}, u32[]{:S(2)}) collective-permute-start(bf16[48,512]{1,0:T(8,128)(2,1)S(1)} %get-tuple-element.101), channel_id=1, source_target_pairs={{0,6},{1,7},{2,4},{3,5},{4,2},{5,3},{6,0},{7,1},{8,14},{9,15},{10,... | collective-permute-start | bytes 147464 | tf_op jit(solution)/shard_map/ppermute | solution.py:458
  (14 other events, 57.9 us)

commit v20 on v19

--- a/solution.py
+++ b/solution.py
@@ -205,7 +205,6 @@
     pieces = refs[:-4]
     out_ref, window_ref, basis, sem = refs[-4:]
     width = pieces[0].shape[0]
-    rows = out_ref.shape[0] // 2
     copies = [
         pltpu.make_async_copy(piece, basis.at[pl.ds(at * width, width)], sem.at[at])
         for at, piece in enumerate(pieces)
@@ -220,14 +219,8 @@
         for copy in copies[first:last]:
             copy.wait()
         deep = slice(first * width, last * width)
-
-        @pl.loop(0, 2)
-        def _(half):
-            block = pl.ds(pl.multiple_of(half * rows, rows), rows)
-            part = jnp.dot(
-                scaled_ref[block, deep], basis[deep, :], preferred_element_type=jnp.float32
-            )
-            out_ref[block, :] = part if first == 0 else out_ref[block, :] + part
+        part = jnp.dot(scaled_ref[:, deep], basis[deep, :], preferred_element_type=jnp.float32)
+        out_ref[...] = part if first == 0 else out_ref[...] + part
 
     window_copy.wait()
 
@@ -301,7 +294,7 @@
         name="keep",
     )(basis_in)
     both, own, kept, *got = after(both, own, kept, *got)
-    depth, later = 1024, 7
+    depth, later = 512, 14
     grads, acts = pl.pallas_call(
         part_kernel,
         out_shape=(
@@ -356,13 +349,12 @@
         grads_far,
         basis_out,
     )
-    start, grads, right[-1], left[-1], rotated, *far = after(
-        start, grads, right[-1], left[-1], rotated, *far
-    )
-    rotated_far = swap(rotated, n)
+    start, right[-1], left[-1], *far = after(start, right[-1], left[-1], *far)
     far += [swap(right[-1], n), swap(left[-1], n)]
     right.append(to_right(right[-1]))
     left.append(to_left(left[-1]))
+    start, grads, rotated = after(start, grads, rotated)
+    rotated_far = swap(rotated, n)
     aligned = rotate(
         functools.partial(rotate_last_kernel, tok_rows, full_out // depth - later),
         later,
@@ -386,7 +378,7 @@
     right.append(to_right(right[-1]))
     left.append(to_left(left[-1]))
     begun = [0] + [at for step in range(1, steps) for at in (step, chips - step)] + [steps]
-    blocks = 8
+    blocks = 14
     scaled = pl.pallas_call(
         functools.partial(scale_kernel, begun),
         out_shape=jax.ShapeDtypeStruct((tile_width, full_in), jnp.bfloat16),

time: 80.4 us -> 79.7 us (level)
    ppermute x4, starting transfers between devices: 2.9 us -> 6.35 us  [ring_body(): to_right = lambda x: lax.ppermute(x, 'blk', shift_pairs(n, 1))]
    ppermute x4, starting transfers between devices: 5.37 us -> 1.93 us  [ring_body(): to_left = lambda x: lax.ppermute(x, 'blk', shift_pairs(n, -1))]
    all_to_all x1, waiting for transfers between devices: 2.4 us -> 0.01 us  [exchange(): return lax.all_to_all(x, 'blk', 0, 0, axis_index_groups=groups, tiled=True)]
    ppermute x4, waiting for transfers between devices: 0.01 us -> 2.35 us  [ring_body(): to_left = lambda x: lax.ppermute(x, 'blk', shift_pairs(n, -1))]
  transfers between devices with their start and end apart: 34 -> 34, of which waited for: 11 -> 13; matrix products, arithmetic and copies ran while one was open for 1% -> 1% of each run, Pallas kernels for 28% -> 29%
where the time goes in v20:
time: 79.7 us; the launch traced here: 79.3 us
  starting transfers between devices  34.4 us (43%)
  Pallas kernels  25 us (31%)
  waiting for transfers between devices  15.8 us (20%)
  local copies, waits for them, and re-layouts  3.02 us (4%)
  other arithmetic  0.91 us (1%)
    ppermute x7, starting transfers between devices, ring_body(): lax.ppermute(x, 'blk', xor_pairs(n, 2 * key))  11.2 us
    pallas_call x2, Pallas kernels, ring_body(): pl.pallas_call(kernel, out_shape=jax.ShapeDtypeStruct(shape, dtype), in_s...  11 us
    ppermute x4, starting transfers between devices, ring_body(): to_right = lambda x: lax.ppermute(x, 'blk', shift_pairs(n, 1))  6.35 us
    pallas_call x1, Pallas kernels, ring_body(): pl.pallas_call(functools.partial(scale_kernel, begun), out_shape=jax.Shap...  6.31 us
    ppermute x3, starting transfers between devices, ring_body(): lax.ppermute(both, 'blk', xor_pairs(n, 4 * key))  5.68 us
    all_to_all x1, starting transfers between devices, exchange(): return lax.all_to_all(x, 'blk', 0, 0, axis_index_groups=groups, tiled=True)  4.33 us
    pallas_call x1, Pallas kernels, ring_body(): pl.pallas_call(functools.partial(project_kernel, (0, 6, len(pieces))), ou...  3.92 us
    ppermute x13, waiting for transfers between devices, swap(): return lax.ppermute(x, 'blk', xor_pairs(n, 1))  3.59 us
  transfers between devices with their start and end apart: 34, of which 13 were waited for; matrix products, arithmetic and copies ran while one was open for 1% of the time, Pallas kernels for 29%

profile of v20, /device:TPU:0, one launch (start us, length us, event | category | flops | bytes accessed | tf_op | source)
XLA Modules:
  0.0 79.3 jit_solution(3175713828680650302)
XLA Ops:
  0.9 3.1 %collective-permute-start = (bf16[1,2,18432]{2,1,0:T(2,128)(2,1)S(1)}, bf16[1,2,18432]{2,1,0:T(2,128)(2,1)S(1)}, u32[]{:S(2)}, u32[]{:S(2)}) collective-permute-start(bf16[1,2,18432]{2,1,0:T(2,128)(2,1)S(1)} %maximum_bitcast_fusion.refs_0_), channel_id=1, source_target_pairs={{0,4},{1,5},{2,6},{3,7},{4,0},{5,1},{6,2},{7,3},{8,12},{9,13},{10,... | collective-permute-start | bytes 221192 | tf_op jit(solution)/shard_map/ppermute | solution.py:286
  4.0 2.6 %collective-permute-start.1 = (bf16[1,2,18432]{2,1,0:T(2,128)(2,1)S(1)}, bf16[1,2,18432]{2,1,0:T(2,128)(2,1)S(1)}, u32[]{:S(2)}, u32[]{:S(2)}) collective-permute-start(bf16[1,2,18432]{2,1,0:T(2,128)(2,1)S(1)} %maximum_bitcast_fusion.refs_0_), channel_id=1, source_target_pairs={{0,8},{1,9},{2,10},{3,11},{4,12},{5,13},{6,14},{7,15},{8,0},{9,1},... | collective-permute-start | bytes 221192 | tf_op jit(solution)/shard_map/ppermute | solution.py:286
  6.6 1.6 %copy-done = bf16[4096,256]{1,0:T(8,128)(2,1)S(1)} copy-done((bf16[4096,256]{1,0:T(8,128)(2,1)S(1)}, bf16[4096,256]{1,0:T(8,128)(2,1)}, u32[]{:S(2)}) %copy-start) | copy-done | bytes 2097176
  9.3 2.5 %collective-permute-done.1.refs_2_ = bf16[1,2,18432]{2,1,0:T(2,128)(2,1)S(1)} collective-permute-done((bf16[1,2,18432]{2,1,0:T(2,128)(2,1)S(1)}, bf16[1,2,18432]{2,1,0:T(2,128)(2,1)S(1)}, u32[]{:S(2)}, u32[]{:S(2)}) %collective-permute-start.1) | collective-permute-done | bytes 73760 | tf_op jit(solution)/shard_map/ppermute | solution.py:286
  12.9 1.6 %collective-permute-start.4 = (bf16[4,2,4096]{2,1,0:T(2,128)(2,1)S(1)}, bf16[4,2,4096]{2,1,0:T(2,128)(2,1)S(1)}, u32[]{:S(2)}, u32[]{:S(2)}) collective-permute-start(bf16[4,2,4096]{2,1,0:T(2,128)(2,1)S(1)} %get-tuple-element.64), channel_id=1, source_target_pairs={{0,2},{1,3},{2,0},{3,1},{4,6},{5,7},{6,4},{7,5},{8,10},{9,11},{10,... | collective-permute-start | bytes 196616 | tf_op jit(solution)/shard_map/ppermute | solution.py:310
  15.1 2.9 %collective-permute-done.4 = bf16[4,2,4096]{2,1,0:T(2,128)(2,1)S(1)} collective-permute-done((bf16[4,2,4096]{2,1,0:T(2,128)(2,1)S(1)}, bf16[4,2,4096]{2,1,0:T(2,128)(2,1)S(1)}, u32[]{:S(2)}, u32[]{:S(2)}) %collective-permute-start.4) | collective-permute-done | bytes 65568 | tf_op jit(solution)/shard_map/ppermute | solution.py:310
  18.3 1.2 %collective-permute-done.5.far_ref = bf16[8,2,4096]{2,1,0:T(2,128)(2,1)S(1)} collective-permute-done((bf16[8,2,4096]{2,1,0:T(2,128)(2,1)S(1)}, bf16[8,2,4096]{2,1,0:T(2,128)(2,1)S(1)}, u32[]{:S(2)}, u32[]{:S(2)}) %collective-permute-start.5) | collective-permute-done | bytes 131104 | tf_op jit(solution)/shard_map/ppermute | solution.py:48
  19.4 1.2 %rotate_in.1 = bf16[8,32,256]{2,1,0:T(8,128)(2,1)} custom-call(bf16[8,2,4096]{2,1,0:T(2,128)(2,1)S(1)} %constant_dynamic-update-slice_fusion.near_ref, bf16[8,2,4096]{2,1,0:T(2,128)(2,1)S(1)} %collective-permute-done.5.far_ref, bf16[4096,256]{1,0:T(8,128)(2,1)S(1)} %keep.1.basis_ref), custom_call_target="tpu_custom_call" | custom-call | flops 1 | bytes 1 | tf_op jit(solution)/shard_map/rotate_in/pallas_call | solution.py:313
  23.1 4.3 %all-to-all-start = ((bf16[8,32,256]{2,1,0:T(8,128)(2,1)}), bf16[8,32,256]{2,1,0:T(8,128)(2,1)S(1)}, u32[]{:S(2)}, u32[]{:S(2)}) async-start(bf16[8,32,256]{2,1,0:T(8,128)(2,1)} %rotate_in.1), calls=%async_computation | async-start | bytes 262144 | tf_op jit(solution)/shard_map/all_to_all | solution.py:44
  27.4 5.4 %rotate_first.1.start_ref = f32[32,896]{1,0:T(8,128)S(1)} custom-call(bf16[8,2,14336]{2,1,0:T(2,128)(2,1)S(1)} %constant_dynamic-update-slice_fusion.2.near_ref, bf16[8,2,14336]{2,1,0:T(2,128)(2,1)S(1)} %collective-permute-done.6.far_ref, bf16[14336,896]{1,0:T(8,128)(2,1)} %basis_out_ref.1), custom_call_target="tpu_custom_call" | custom-call | flops 1 | bytes 1 | tf_op jit(solution)/shard_map/rotate_first/pallas_call | solution.py:330
  32.9 2.1 %collective-permute-start.10 = (bf16[256,512]{1,0:T(8,128)(2,1)S(1)}, bf16[256,512]{1,0:T(8,128)(2,1)S(1)}, u32[]{:S(2)}, u32[]{:S(2)}) collective-permute-start(bf16[256,512]{1,0:T(8,128)(2,1)S(1)} %collective-permute-done.7.refs_2_), channel_id=1, source_target_pairs={{0,4},{1,5},{4,8},{5,9},{8,12},{9,13},{12,14},{13,15},{14,10},{15,... | collective-permute-start | bytes 786440 | tf_op jit(solution)/shard_map/ppermute | solution.py:278
  35.5 5.7 %rotate_last.1.aligned_ref = bf16[896,32]{1,0:T(8,128)(2,1)S(1)} custom-call(bf16[8,2,14336]{2,1,0:T(2,128)(2,1)S(1)} %constant_dynamic-update-slice_fusion.2.near_ref, bf16[8,2,14336]{2,1,0:T(2,128)(2,1)S(1)} %collective-permute-done.6.far_ref, bf16[14336,896]{1,0:T(8,128)(2,1)} %basis_out_ref.1, s32[16]{0:T(128)S(1)} %copy-done.2, ...), custom_call_target="tpu_custom_call" | custom-call | flops 1 | bytes 1 | tf_op jit(solution)/shard_map/rotate_last/pallas_call | solution.py:330
  41.4 1.5 %collective-permute-done.11.refs_8_ = bf16[256,512]{1,0:T(8,128)(2,1)S(1)} collective-permute-done((bf16[256,512]{1,0:T(8,128)(2,1)S(1)}, bf16[256,512]{1,0:T(8,128)(2,1)S(1)}, u32[]{:S(2)}, u32[]{:S(2)}) %collective-permute-start.11) | collective-permute-done | bytes 262176 | tf_op jit(solution)/shard_map/ppermute | solution.py:279
  42.8 1.5 %collective-permute-start.15 = (bf16[256,512]{1,0:T(8,128)(2,1)S(1)}, bf16[256,512]{1,0:T(8,128)(2,1)S(1)}, u32[]{:S(2)}, u32[]{:S(2)}) collective-permute-start(bf16[256,512]{1,0:T(8,128)(2,1)S(1)} %collective-permute-done.10.refs_6_), channel_id=1, source_target_pairs={{0,4},{1,5},{4,8},{5,9},{8,12},{9,13},{12,14},{13,15},{14,10},{15,... | collective-permute-start | bytes 786440 | tf_op jit(solution)/shard_map/ppermute | solution.py:278
  45.4 6.3 %scale.1.scaled_ref = bf16[896,4096]{1,0:T(8,128)(2,1)S(1)} custom-call(bf16[896,32]{1,0:T(8,128)(2,1)S(1)} %rotate_last.1.aligned_ref, bf16[8,32,256]{2,1,0:T(8,128)(2,1)S(1)} %all-to-all-done.near_ref, bf16[8,32,256]{2,1,0:T(8,128)(2,1)S(1)} %collective-permute-done.12.far_ref, s32[32]{0:T(128)S(1)} %copy-done.1, f32[896,4096]{1,0:T(8,128)} %eigen_ref.1), custom_call_target="tpu_custom_call" | custom-call | flops 1 | bytes 1 | tf_op jit(solution)/shard_map/scale/pallas_call | solution.py:382
  52.3 1.7 %collective-permute-start.21 = (bf16[128,512]{1,0:T(8,128)(2,1)S(1)}, bf16[128,512]{1,0:T(8,128)(2,1)S(1)}, u32[]{:S(2)}, u32[]{:S(2)}) collective-permute-start(bf16[128,512]{1,0:T(8,128)(2,1)S(1)} %slice.10), channel_id=1, source_target_pairs={{0,4},{1,5},{4,8},{5,9},{8,12},{9,13},{12,14},{13,15},{14,10},{15,... | collective-permute-start | bytes 393224 | tf_op jit(solution)/shard_map/ppermute | solution.py:278
  54.4 3.9 %project.1 = (f32[896,512]{1,0:T(8,128)S(1)}, bf16[768,896]{1,0:T(8,128)(2,1)S(1)}) custom-call(bf16[896,4096]{1,0:T(8,128)(2,1)S(1)} %scale.1.scaled_ref, bf16[14336,896]{1,0:T(8,128)(2,1)} %basis_out_ref.1, bf16[256,512]{1,0:T(8,128)(2,1)S(1)} %bitcast.6, bf16[256,512]{1,0:T(8,128)(2,1)S(1)} %collective-permute-done.9.refs_1_, ...), custom_call_target="tpu_custom_call" | custom-call | flops 1 | bytes 1 | tf_op jit(solution)/shard_map/project/pallas_call | solution.py:405
  60.8 1.6 %window.1 = (bf16[8,48,512]{2,1,0:T(8,128)(2,1)S(1)}, f32[8,48,512]{2,1,0:T(8,128)S(1)}) custom-call(bf16[768,896]{1,0:T(8,128)(2,1)S(1)} %get-tuple-element.90.window_ref, bf16[896,4096]{1,0:T(8,128)(2,1)S(1)} %scale.1.scaled_ref, f32[896,512]{1,0:T(8,128)S(1)} %get-tuple-element.92.projected_ref, bf16[128,512]{1,0:T(8,128)(2,1)S(1)} %collective-permute-done.21.refs_0_, ...), custom_call_target="tpu_custom_call" | custom-call | flops 1 | bytes 1 | tf_op jit(solution)/shard_map/window/pallas_call | solution.py:425
  62.8 1.4 %collective-permute-done.25.got_ref = bf16[8,48,512]{2,1,0:T(8,128)(2,1)S(1)} collective-permute-done((bf16[8,48,512]{2,1,0:T(8,128)(2,1)S(1)}, bf16[8,48,512]{2,1,0:T(8,128)(2,1)S(1)}, u32[]{:S(2)}, u32[]{:S(2)}) %collective-permute-start.25) | collective-permute-done | bytes 393248 | tf_op jit(solution)/shard_map/ppermute | solution.py:48
  64.3 2.6 %collective-permute-start.26 = (bf16[48,512]{1,0:T(8,128)(2,1)S(1)}, bf16[48,512]{1,0:T(8,128)(2,1)S(1)}, u32[]{:S(2)}, u32[]{:S(2)}) collective-permute-start(bf16[48,512]{1,0:T(8,128)(2,1)S(1)} %get-tuple-element.98), channel_id=1, source_target_pairs={{0,12},{1,13},{2,14},{3,15},{4,8},{5,9},{6,10},{7,11},{8,4},{9,5},... | collective-permute-start | bytes 147464 | tf_op jit(solution)/shard_map/ppermute | solution.py:450
  68.1 3.9 %collective-permute-start.29 = (bf16[48,512]{1,0:T(8,128)(2,1)S(1)}, bf16[48,512]{1,0:T(8,128)(2,1)S(1)}, u32[]{:S(2)}, u32[]{:S(2)}) collective-permute-start(bf16[48,512]{1,0:T(8,128)(2,1)S(1)} %get-tuple-element.101), channel_id=1, source_target_pairs={{0,10},{1,11},{2,8},{3,9},{4,14},{5,15},{6,12},{7,13},{8,2},{9,3},... | collective-permute-start | bytes 147464 | tf_op jit(solution)/shard_map/ppermute | solution.py:450
  72.2 1.7 %collective-permute-start.31 = (bf16[48,512]{1,0:T(8,128)(2,1)S(1)}, bf16[48,512]{1,0:T(8,128)(2,1)S(1)}, u32[]{:S(2)}, u32[]{:S(2)}) collective-permute-start(bf16[48,512]{1,0:T(8,128)(2,1)S(1)} %get-tuple-element.103), channel_id=1, source_target_pairs={{0,6},{1,7},{2,4},{3,5},{4,2},{5,3},{6,0},{7,1},{8,14},{9,15},{10,... | collective-permute-start | bytes 147464 | tf_op jit(solution)/shard_map/ppermute | solution.py:450
  73.9 1.5 %collective-permute-start.32 = (bf16[48,512]{1,0:T(8,128)(2,1)S(1)}, bf16[48,512]{1,0:T(8,128)(2,1)S(1)}, u32[]{:S(2)}, u32[]{:S(2)}) collective-permute-start(bf16[48,512]{1,0:T(8,128)(2,1)S(1)} %get-tuple-element.104), channel_id=1, source_target_pairs={{0,2},{1,3},{2,0},{3,1},{4,6},{5,7},{6,4},{7,5},{8,10},{9,11},{10,... | collective-permute-start | bytes 147464 | tf_op jit(solution)/shard_map/ppermute | solution.py:450
  75.5 2.0 %collective-permute-done.29.refs_3_ = bf16[48,512]{1,0:T(8,128)(2,1)S(1)} collective-permute-done((bf16[48,512]{1,0:T(8,128)(2,1)S(1)}, bf16[48,512]{1,0:T(8,128)(2,1)S(1)}, u32[]{:S(2)}, u32[]{:S(2)}) %collective-permute-start.29) | collective-permute-done | bytes 49184 | tf_op jit(solution)/shard_map/ppermute | solution.py:450
  (70 shorter events, 15.4 us)
Async XLA Ops:
  0.9 8.4 %collective-permute-start = (bf16[1,2,18432]{2,1,0:T(2,128)(2,1)S(1)}, bf16[1,2,18432]{2,1,0:T(2,128)(2,1)S(1)}, u32[]{:S(2)}, u32[]{:S(2)}) collective-permute-start(bf16[1,2,18432]{2,1,0:T(2,128)(2,1)S(1)} %maximum_bitcast_fusion.refs_0_), channel_id=1, source_target_pairs={{0,4},{1,5},{2,6},{3,7},{4,0},{5,1},{6,2},{7,3},{8,12},{9,13},{10,... | collective-permute-start | bytes 221192 | tf_op jit(solution)/shard_map/ppermute | solution.py:286
  4.0 7.8 %collective-permute-start.1 = (bf16[1,2,18432]{2,1,0:T(2,128)(2,1)S(1)}, bf16[1,2,18432]{2,1,0:T(2,128)(2,1)S(1)}, u32[]{:S(2)}, u32[]{:S(2)}) collective-permute-start(bf16[1,2,18432]{2,1,0:T(2,128)(2,1)S(1)} %maximum_bitcast_fusion.refs_0_), channel_id=1, source_target_pairs={{0,8},{1,9},{2,10},{3,11},{4,12},{5,13},{6,14},{7,15},{8,0},{9,1},... | collective-permute-start | bytes 221192 | tf_op jit(solution)/shard_map/ppermute | solution.py:286
  6.6 6.3 %collective-permute-start.2 = (bf16[1,2,18432]{2,1,0:T(2,128)(2,1)S(1)}, bf16[1,2,18432]{2,1,0:T(2,128)(2,1)S(1)}, u32[]{:S(2)}, u32[]{:S(2)}) collective-permute-start(bf16[1,2,18432]{2,1,0:T(2,128)(2,1)S(1)} %maximum_bitcast_fusion.refs_0_), channel_id=1, source_target_pairs={{0,12},{1,13},{2,14},{3,15},{4,8},{5,9},{6,10},{7,11},{8,4},{9,5},... | collective-permute-start | bytes 221192 | tf_op jit(solution)/shard_map/ppermute | solution.py:286
  14.5 6.2 %collective-permute-start.3 = (bf16[4,2,14336]{2,1,0:T(2,128)(2,1)S(1)}, bf16[4,2,14336]{2,1,0:T(2,128)(2,1)S(1)}, u32[]{:S(2)}, u32[]{:S(2)}) collective-permute-start(bf16[4,2,14336]{2,1,0:T(2,128)(2,1)S(1)} %get-tuple-element.62), channel_id=1, source_target_pairs={{0,2},{1,3},{2,0},{3,1},{4,6},{5,7},{6,4},{7,5},{8,10},{9,11},{10,... | collective-permute-start | bytes 688136 | tf_op jit(solution)/shard_map/ppermute | solution.py:311
  20.8 6.6 %collective-permute-start.6 = (bf16[8,2,14336]{2,1,0:T(2,128)(2,1)S(1)}, bf16[8,2,14336]{2,1,0:T(2,128)(2,1)S(1)}, u32[]{:S(2)}, u32[]{:S(2)}) collective-permute-start(bf16[8,2,14336]{2,1,0:T(2,128)(2,1)S(1)} %constant_dynamic-update-slice_fusion.2.near_ref), channel_id=1, source_target_pairs={{0,1},{1,0},{2,3},{3,2},{4,5},{5,4},{6,7},{7,6},{8,9},{9,8},{10,11... | collective-permute-start | bytes 1376264 | tf_op jit(solution)/shard_map/ppermute | solution.py:48
  21.1 11.8 %collective-permute-start.7 = (bf16[256,512]{1,0:T(8,128)(2,1)S(1)}, bf16[256,512]{1,0:T(8,128)(2,1)S(1)}, u32[]{:S(2)}, u32[]{:S(2)}) collective-permute-start(bf16[256,512]{1,0:T(8,128)(2,1)S(1)} %bitcast.3), channel_id=1, source_target_pairs={{0,4},{1,5},{4,8},{5,9},{8,12},{9,13},{12,14},{13,15},{14,10},{15,... | collective-permute-start | bytes 786440 | tf_op jit(solution)/shard_map/ppermute | solution.py:278
  22.2 10.7 %collective-permute-start.8 = (bf16[256,512]{1,0:T(8,128)(2,1)S(1)}, bf16[256,512]{1,0:T(8,128)(2,1)S(1)}, u32[]{:S(2)}, u32[]{:S(2)}) collective-permute-start(bf16[256,512]{1,0:T(8,128)(2,1)S(1)} %bitcast.4), channel_id=1, source_target_pairs={{0,2},{1,3},{4,0},{5,1},{8,4},{9,5},{12,8},{13,9},{14,12},{15,13},... | collective-permute-start | bytes 786440 | tf_op jit(solution)/shard_map/ppermute | solution.py:279
  23.1 9.8 %collective-permute-start.9 = (bf16[256,512]{1,0:T(8,128)(2,1)S(1)}, bf16[256,512]{1,0:T(8,128)(2,1)S(1)}, u32[]{:S(2)}, u32[]{:S(2)}) collective-permute-start(bf16[256,512]{1,0:T(8,128)(2,1)S(1)} %bitcast.5), channel_id=1, source_target_pairs={{0,1},{1,0},{2,3},{3,2},{4,5},{5,4},{6,7},{7,6},{8,9},{9,8},{10,11... | collective-permute-start | bytes 786440 | tf_op jit(solution)/shard_map/ppermute | solution.py:48
  23.1 12.4 %all-to-all-start = ((bf16[8,32,256]{2,1,0:T(8,128)(2,1)}), bf16[8,32,256]{2,1,0:T(8,128)(2,1)S(1)}, u32[]{:S(2)}, u32[]{:S(2)}) async-start(bf16[8,32,256]{2,1,0:T(8,128)(2,1)} %rotate_in.1), calls=%async_computation | async-start | bytes 262144 | tf_op jit(solution)/shard_map/all_to_all | solution.py:44
  32.9 8.5 %collective-permute-start.10 = (bf16[256,512]{1,0:T(8,128)(2,1)S(1)}, bf16[256,512]{1,0:T(8,128)(2,1)S(1)}, u32[]{:S(2)}, u32[]{:S(2)}) collective-permute-start(bf16[256,512]{1,0:T(8,128)(2,1)S(1)} %collective-permute-done.7.refs_2_), channel_id=1, source_target_pairs={{0,4},{1,5},{4,8},{5,9},{8,12},{9,13},{12,14},{13,15},{14,10},{15,... | collective-permute-start | bytes 786440 | tf_op jit(solution)/shard_map/ppermute | solution.py:278
  34.9 7.9 %collective-permute-start.11 = (bf16[256,512]{1,0:T(8,128)(2,1)S(1)}, bf16[256,512]{1,0:T(8,128)(2,1)S(1)}, u32[]{:S(2)}, u32[]{:S(2)}) collective-permute-start(bf16[256,512]{1,0:T(8,128)(2,1)S(1)} %collective-permute-done.8.refs_4_), channel_id=1, source_target_pairs={{0,2},{1,3},{4,0},{5,1},{8,4},{9,5},{12,8},{13,9},{14,12},{15,13},... | collective-permute-start | bytes 786440 | tf_op jit(solution)/shard_map/ppermute | solution.py:279
  35.0 7.8 %collective-permute-start.13 = (bf16[256,512]{1,0:T(8,128)(2,1)S(1)}, bf16[256,512]{1,0:T(8,128)(2,1)S(1)}, u32[]{:S(2)}, u32[]{:S(2)}) collective-permute-start(bf16[256,512]{1,0:T(8,128)(2,1)S(1)} %collective-permute-done.7.refs_2_), channel_id=1, source_target_pairs={{0,1},{1,0},{2,3},{3,2},{4,5},{5,4},{6,7},{7,6},{8,9},{9,8},{10,11... | collective-permute-start | bytes 786440 | tf_op jit(solution)/shard_map/ppermute | solution.py:48
  35.0 7.8 %collective-permute-start.14 = (bf16[256,512]{1,0:T(8,128)(2,1)S(1)}, bf16[256,512]{1,0:T(8,128)(2,1)S(1)}, u32[]{:S(2)}, u32[]{:S(2)}) collective-permute-start(bf16[256,512]{1,0:T(8,128)(2,1)S(1)} %collective-permute-done.8.refs_4_), channel_id=1, source_target_pairs={{0,1},{1,0},{2,3},{3,2},{4,5},{5,4},{6,7},{7,6},{8,9},{9,8},{10,11... | collective-permute-start | bytes 786440 | tf_op jit(solution)/shard_map/ppermute | solution.py:48
  35.5 5.7 %collective-permute-start.12 = (bf16[8,32,256]{2,1,0:T(8,128)(2,1)S(1)}, bf16[8,32,256]{2,1,0:T(8,128)(2,1)S(1)}, u32[]{:S(2)}, u32[]{:S(2)}) collective-permute-start(bf16[8,32,256]{2,1,0:T(8,128)(2,1)S(1)} %all-to-all-done.near_ref), channel_id=1, source_target_pairs={{0,1},{1,0},{2,3},{3,2},{4,5},{5,4},{6,7},{7,6},{8,9},{9,8},{10,11... | collective-permute-start | bytes 393224 | tf_op jit(solution)/shard_map/ppermute | solution.py:48
  42.8 8.9 %collective-permute-start.15 = (bf16[256,512]{1,0:T(8,128)(2,1)S(1)}, bf16[256,512]{1,0:T(8,128)(2,1)S(1)}, u32[]{:S(2)}, u32[]{:S(2)}) collective-permute-start(bf16[256,512]{1,0:T(8,128)(2,1)S(1)} %collective-permute-done.10.refs_6_), channel_id=1, source_target_pairs={{0,4},{1,5},{4,8},{5,9},{8,12},{9,13},{12,14},{13,15},{14,10},{15,... | collective-permute-start | bytes 786440 | tf_op jit(solution)/shard_map/ppermute | solution.py:278
  44.3 7.4 %collective-permute-start.16 = (bf16[256,512]{1,0:T(8,128)(2,1)S(1)}, bf16[256,512]{1,0:T(8,128)(2,1)S(1)}, u32[]{:S(2)}, u32[]{:S(2)}) collective-permute-start(bf16[256,512]{1,0:T(8,128)(2,1)S(1)} %collective-permute-done.11.refs_8_), channel_id=1, source_target_pairs={{0,2},{1,3},{4,0},{5,1},{8,4},{9,5},{12,8},{13,9},{14,12},{15,13},... | collective-permute-start | bytes 786440 | tf_op jit(solution)/shard_map/ppermute | solution.py:279
  44.8 6.9 %collective-permute-start.17 = (bf16[256,512]{1,0:T(8,128)(2,1)S(1)}, bf16[256,512]{1,0:T(8,128)(2,1)S(1)}, u32[]{:S(2)}, u32[]{:S(2)}) collective-permute-start(bf16[256,512]{1,0:T(8,128)(2,1)S(1)} %collective-permute-done.10.refs_6_), channel_id=1, source_target_pairs={{0,1},{1,0},{2,3},{3,2},{4,5},{5,4},{6,7},{7,6},{8,9},{9,8},{10,11... | collective-permute-start | bytes 786440 | tf_op jit(solution)/shard_map/ppermute | solution.py:48
  44.8 6.9 %collective-permute-start.18 = (bf16[256,512]{1,0:T(8,128)(2,1)S(1)}, bf16[256,512]{1,0:T(8,128)(2,1)S(1)}, u32[]{:S(2)}, u32[]{:S(2)}) collective-permute-start(bf16[256,512]{1,0:T(8,128)(2,1)S(1)} %collective-permute-done.11.refs_8_), channel_id=1, source_target_pairs={{0,1},{1,0},{2,3},{3,2},{4,5},{5,4},{6,7},{7,6},{8,9},{9,8},{10,11... | collective-permute-start | bytes 786440 | tf_op jit(solution)/shard_map/ppermute | solution.py:48
  52.3 6.0 %collective-permute-start.21 = (bf16[128,512]{1,0:T(8,128)(2,1)S(1)}, bf16[128,512]{1,0:T(8,128)(2,1)S(1)}, u32[]{:S(2)}, u32[]{:S(2)}) collective-permute-start(bf16[128,512]{1,0:T(8,128)(2,1)S(1)} %slice.10), channel_id=1, source_target_pairs={{0,4},{1,5},{4,8},{5,9},{8,12},{9,13},{12,14},{13,15},{14,10},{15,... | collective-permute-start | bytes 393224 | tf_op jit(solution)/shard_map/ppermute | solution.py:278
  64.3 7.9 %collective-permute-start.26 = (bf16[48,512]{1,0:T(8,128)(2,1)S(1)}, bf16[48,512]{1,0:T(8,128)(2,1)S(1)}, u32[]{:S(2)}, u32[]{:S(2)}) collective-permute-start(bf16[48,512]{1,0:T(8,128)(2,1)S(1)} %get-tuple-element.98), channel_id=1, source_target_pairs={{0,12},{1,13},{2,14},{3,15},{4,8},{5,9},{6,10},{7,11},{8,4},{9,5},... | collective-permute-start | bytes 147464 | tf_op jit(solution)/shard_map/ppermute | solution.py:450
  66.9 7.1 %collective-permute-start.27 = (bf16[48,512]{1,0:T(8,128)(2,1)S(1)}, bf16[48,512]{1,0:T(8,128)(2,1)S(1)}, u32[]{:S(2)}, u32[]{:S(2)}) collective-permute-start(bf16[48,512]{1,0:T(8,128)(2,1)S(1)} %get-tuple-element.99), channel_id=1, source_target_pairs={{0,14},{1,15},{2,12},{3,13},{4,10},{5,11},{6,8},{7,9},{8,6},{9,7},... | collective-permute-start | bytes 147464 | tf_op jit(solution)/shard_map/ppermute | solution.py:450
  68.0 7.4 %collective-permute-start.28 = (bf16[48,512]{1,0:T(8,128)(2,1)S(1)}, bf16[48,512]{1,0:T(8,128)(2,1)S(1)}, u32[]{:S(2)}, u32[]{:S(2)}) collective-permute-start(bf16[48,512]{1,0:T(8,128)(2,1)S(1)} %get-tuple-element.100), channel_id=1, source_target_pairs={{0,8},{1,9},{2,10},{3,11},{4,12},{5,13},{6,14},{7,15},{8,0},{9,1},... | collective-permute-start | bytes 147464 | tf_op jit(solution)/shard_map/ppermute | solution.py:450
  68.1 9.5 %collective-permute-start.29 = (bf16[48,512]{1,0:T(8,128)(2,1)S(1)}, bf16[48,512]{1,0:T(8,128)(2,1)S(1)}, u32[]{:S(2)}, u32[]{:S(2)}) collective-permute-start(bf16[48,512]{1,0:T(8,128)(2,1)S(1)} %get-tuple-element.101), channel_id=1, source_target_pairs={{0,10},{1,11},{2,8},{3,9},{4,14},{5,15},{6,12},{7,13},{8,2},{9,3},... | collective-permute-start | bytes 147464 | tf_op jit(solution)/shard_map/ppermute | solution.py:450
  72.2 6.3 %collective-permute-start.31 = (bf16[48,512]{1,0:T(8,128)(2,1)S(1)}, bf16[48,512]{1,0:T(8,128)(2,1)S(1)}, u32[]{:S(2)}, u32[]{:S(2)}) collective-permute-start(bf16[48,512]{1,0:T(8,128)(2,1)S(1)} %get-tuple-element.103), channel_id=1, source_target_pairs={{0,6},{1,7},{2,4},{3,5},{4,2},{5,3},{6,0},{7,1},{8,14},{9,15},{10,... | collective-permute-start | bytes 147464 | tf_op jit(solution)/shard_map/ppermute | solution.py:450
  (14 other events, 54.9 us)

commit v21 on v20

--- a/solution.py
+++ b/solution.py
@@ -294,7 +294,7 @@
         name="keep",
     )(basis_in)
     both, own, kept, *got = after(both, own, kept, *got)
-    depth, later = 512, 14
+    depth, later = 1024, 9
     grads, acts = pl.pallas_call(
         part_kernel,
         out_shape=(
@@ -378,7 +378,7 @@
     right.append(to_right(right[-1]))
     left.append(to_left(left[-1]))
     begun = [0] + [at for step in range(1, steps) for at in (step, chips - step)] + [steps]
-    blocks = 14
+    blocks = 8
     scaled = pl.pallas_call(
         functools.partial(scale_kernel, begun),
         out_shape=jax.ShapeDtypeStruct((tile_width, full_in), jnp.bfloat16),
@@ -436,7 +436,7 @@
         name="window",
     )(window, scaled, projected, *last)
 
-    keys = sorted(range(1, chips), key=lambda key: -(key & -2))
+    keys = [*range(chips - 2, 0, -2), *range(chips - 1, 0, -2)]
     small = pltpu.CompilerParams(vmem_limit_bytes=8 * MIB)
     own, *sends = pl.pallas_call(
         functools.partial(add_core_kernel, keys),

time: 79.7 us -> 78.6 us (0.986)
  waiting for transfers between devices: 15.8 us -> 15 us
    ppermute x4, waiting for transfers between devices: 2.35 us -> 1.42 us  [ring_body(): to_left = lambda x: lax.ppermute(x, 'blk', shift_pairs(n, -1))]
    all_to_all x1, waiting for transfers between devices: 0.01 us -> 0.89 us  [exchange(): return lax.all_to_all(x, 'blk', 0, 0, axis_index_groups=groups, tiled=True)]
  transfers between devices with their start and end apart: 34 -> 34, of which waited for: 13 -> 13; matrix products, arithmetic and copies ran while one was open for 1% -> 1% of each run, Pallas kernels for 29% -> 28%
where the time goes in v21:
time: 78.6 us; the launch traced here: 78.2 us
  starting transfers between devices  34.4 us (44%)
  Pallas kernels  24.6 us (31%)
  waiting for transfers between devices  15 us (19%)
  local copies, waits for them, and re-layouts  3.02 us (4%)
  other arithmetic  0.91 us (1%)
    ppermute x7, starting transfers between devices, ring_body(): lax.ppermute(x, 'blk', xor_pairs(n, 2 * key))  11.2 us
    pallas_call x2, Pallas kernels, ring_body(): pl.pallas_call(kernel, out_shape=jax.ShapeDtypeStruct(shape, dtype), in_s...  10.7 us
    pallas_call x1, Pallas kernels, ring_body(): pl.pallas_call(functools.partial(scale_kernel, begun), out_shape=jax.Shap...  6.22 us
    ppermute x4, starting transfers between devices, ring_body(): to_right = lambda x: lax.ppermute(x, 'blk', shift_pairs(n, 1))  5.95 us
    ppermute x3, starting transfers between devices, ring_body(): lax.ppermute(both, 'blk', xor_pairs(n, 4 * key))  5.68 us
    all_to_all x1, starting transfers between devices, exchange(): return lax.all_to_all(x, 'blk', 0, 0, axis_index_groups=groups, tiled=True)  4.33 us
    pallas_call x1, Pallas kernels, ring_body(): pl.pallas_call(functools.partial(project_kernel, (0, 6, len(pieces))), ou...  3.92 us
    ppermute x13, waiting for transfers between devices, swap(): return lax.ppermute(x, 'blk', xor_pairs(n, 1))  3.59 us
  transfers between devices with their start and end apart: 34, of which 13 were waited for; matrix products, arithmetic and copies ran while one was open for 1% of the time, Pallas kernels for 28%

profile of v21, /device:TPU:0, one launch (start us, length us, event | category | flops | bytes accessed | tf_op | source)
XLA Modules:
  0.0 78.2 jit_solution(13874050079408895420)
XLA Ops:
  0.9 3.1 %collective-permute-start = (bf16[1,2,18432]{2,1,0:T(2,128)(2,1)S(1)}, bf16[1,2,18432]{2,1,0:T(2,128)(2,1)S(1)}, u32[]{:S(2)}, u32[]{:S(2)}) collective-permute-start(bf16[1,2,18432]{2,1,0:T(2,128)(2,1)S(1)} %maximum_bitcast_fusion.refs_0_), channel_id=1, source_target_pairs={{0,4},{1,5},{2,6},{3,7},{4,0},{5,1},{6,2},{7,3},{8,12},{9,13},{10,... | collective-permute-start | bytes 221192 | tf_op jit(solution)/shard_map/ppermute | solution.py:286
  4.0 2.6 %collective-permute-start.1 = (bf16[1,2,18432]{2,1,0:T(2,128)(2,1)S(1)}, bf16[1,2,18432]{2,1,0:T(2,128)(2,1)S(1)}, u32[]{:S(2)}, u32[]{:S(2)}) collective-permute-start(bf16[1,2,18432]{2,1,0:T(2,128)(2,1)S(1)} %maximum_bitcast_fusion.refs_0_), channel_id=1, source_target_pairs={{0,8},{1,9},{2,10},{3,11},{4,12},{5,13},{6,14},{7,15},{8,0},{9,1},... | collective-permute-start | bytes 221192 | tf_op jit(solution)/shard_map/ppermute | solution.py:286
  6.6 1.6 %copy-done = bf16[4096,256]{1,0:T(8,128)(2,1)S(1)} copy-done((bf16[4096,256]{1,0:T(8,128)(2,1)S(1)}, bf16[4096,256]{1,0:T(8,128)(2,1)}, u32[]{:S(2)}) %copy-start) | copy-done | bytes 2097176
  9.3 2.5 %collective-permute-done.1.refs_2_ = bf16[1,2,18432]{2,1,0:T(2,128)(2,1)S(1)} collective-permute-done((bf16[1,2,18432]{2,1,0:T(2,128)(2,1)S(1)}, bf16[1,2,18432]{2,1,0:T(2,128)(2,1)S(1)}, u32[]{:S(2)}, u32[]{:S(2)}) %collective-permute-start.1) | collective-permute-done | bytes 73760 | tf_op jit(solution)/shard_map/ppermute | solution.py:286
  12.9 1.6 %collective-permute-start.4 = (bf16[4,2,4096]{2,1,0:T(2,128)(2,1)S(1)}, bf16[4,2,4096]{2,1,0:T(2,128)(2,1)S(1)}, u32[]{:S(2)}, u32[]{:S(2)}) collective-permute-start(bf16[4,2,4096]{2,1,0:T(2,128)(2,1)S(1)} %get-tuple-element.64), channel_id=1, source_target_pairs={{0,2},{1,3},{2,0},{3,1},{4,6},{5,7},{6,4},{7,5},{8,10},{9,11},{10,... | collective-permute-start | bytes 196616 | tf_op jit(solution)/shard_map/ppermute | solution.py:310
  15.1 2.9 %collective-permute-done.4 = bf16[4,2,4096]{2,1,0:T(2,128)(2,1)S(1)} collective-permute-done((bf16[4,2,4096]{2,1,0:T(2,128)(2,1)S(1)}, bf16[4,2,4096]{2,1,0:T(2,128)(2,1)S(1)}, u32[]{:S(2)}, u32[]{:S(2)}) %collective-permute-start.4) | collective-permute-done | bytes 65568 | tf_op jit(solution)/shard_map/ppermute | solution.py:310
  18.3 1.2 %collective-permute-done.5.far_ref = bf16[8,2,4096]{2,1,0:T(2,128)(2,1)S(1)} collective-permute-done((bf16[8,2,4096]{2,1,0:T(2,128)(2,1)S(1)}, bf16[8,2,4096]{2,1,0:T(2,128)(2,1)S(1)}, u32[]{:S(2)}, u32[]{:S(2)}) %collective-permute-start.5) | collective-permute-done | bytes 131104 | tf_op jit(solution)/shard_map/ppermute | solution.py:48
  19.4 1.2 %rotate_in.1 = bf16[8,32,256]{2,1,0:T(8,128)(2,1)} custom-call(bf16[8,2,4096]{2,1,0:T(2,128)(2,1)S(1)} %constant_dynamic-update-slice_fusion.near_ref, bf16[8,2,4096]{2,1,0:T(2,128)(2,1)S(1)} %collective-permute-done.5.far_ref, bf16[4096,256]{1,0:T(8,128)(2,1)S(1)} %keep.1.basis_ref), custom_call_target="tpu_custom_call" | custom-call | flops 1 | bytes 1 | tf_op jit(solution)/shard_map/rotate_in/pallas_call | solution.py:313
  23.1 4.3 %all-to-all-start = ((bf16[8,32,256]{2,1,0:T(8,128)(2,1)}), bf16[8,32,256]{2,1,0:T(8,128)(2,1)S(1)}, u32[]{:S(2)}, u32[]{:S(2)}) async-start(bf16[8,32,256]{2,1,0:T(8,128)(2,1)} %rotate_in.1), calls=%async_computation | async-start | bytes 262144 | tf_op jit(solution)/shard_map/all_to_all | solution.py:44
  27.4 4.2 %rotate_first.1.start_ref = f32[32,896]{1,0:T(8,128)S(1)} custom-call(bf16[8,2,14336]{2,1,0:T(2,128)(2,1)S(1)} %constant_dynamic-update-slice_fusion.2.near_ref, bf16[8,2,14336]{2,1,0:T(2,128)(2,1)S(1)} %collective-permute-done.6.far_ref, bf16[14336,896]{1,0:T(8,128)(2,1)} %basis_out_ref.1), custom_call_target="tpu_custom_call" | custom-call | flops 1 | bytes 1 | tf_op jit(solution)/shard_map/rotate_first/pallas_call | solution.py:330
  31.7 2.1 %collective-permute-start.10 = (bf16[256,512]{1,0:T(8,128)(2,1)S(1)}, bf16[256,512]{1,0:T(8,128)(2,1)S(1)}, u32[]{:S(2)}, u32[]{:S(2)}) collective-permute-start(bf16[256,512]{1,0:T(8,128)(2,1)S(1)} %collective-permute-done.7.refs_2_), channel_id=1, source_target_pairs={{0,4},{1,5},{4,8},{5,9},{8,12},{9,13},{12,14},{13,15},{14,10},{15,... | collective-permute-start | bytes 786440 | tf_op jit(solution)/shard_map/ppermute | solution.py:278
  35.2 6.6 %rotate_last.1.aligned_ref = bf16[896,32]{1,0:T(8,128)(2,1)S(1)} custom-call(bf16[8,2,14336]{2,1,0:T(2,128)(2,1)S(1)} %constant_dynamic-update-slice_fusion.2.near_ref, bf16[8,2,14336]{2,1,0:T(2,128)(2,1)S(1)} %collective-permute-done.6.far_ref, bf16[14336,896]{1,0:T(8,128)(2,1)} %basis_out_ref.1, s32[16]{0:T(128)S(1)} %copy-done.2, ...), custom_call_target="tpu_custom_call" | custom-call | flops 1 | bytes 1 | tf_op jit(solution)/shard_map/rotate_last/pallas_call | solution.py:330
  41.8 1.3 %collective-permute-start.15 = (bf16[256,512]{1,0:T(8,128)(2,1)S(1)}, bf16[256,512]{1,0:T(8,128)(2,1)S(1)}, u32[]{:S(2)}, u32[]{:S(2)}) collective-permute-start(bf16[256,512]{1,0:T(8,128)(2,1)S(1)} %collective-permute-done.10.refs_6_), channel_id=1, source_target_pairs={{0,4},{1,5},{4,8},{5,9},{8,12},{9,13},{12,14},{13,15},{14,10},{15,... | collective-permute-start | bytes 786440 | tf_op jit(solution)/shard_map/ppermute | solution.py:278
  44.4 6.2 %scale.1.scaled_ref = bf16[896,4096]{1,0:T(8,128)(2,1)S(1)} custom-call(bf16[896,32]{1,0:T(8,128)(2,1)S(1)} %rotate_last.1.aligned_ref, bf16[8,32,256]{2,1,0:T(8,128)(2,1)S(1)} %all-to-all-done.near_ref, bf16[8,32,256]{2,1,0:T(8,128)(2,1)S(1)} %collective-permute-done.12.far_ref, s32[32]{0:T(128)S(1)} %copy-done.1, f32[896,4096]{1,0:T(8,128)} %eigen_ref.1), custom_call_target="tpu_custom_call" | custom-call | flops 1 | bytes 1 | tf_op jit(solution)/shard_map/scale/pallas_call | solution.py:382
  51.9 1.5 %collective-permute-start.21 = (bf16[128,512]{1,0:T(8,128)(2,1)S(1)}, bf16[128,512]{1,0:T(8,128)(2,1)S(1)}, u32[]{:S(2)}, u32[]{:S(2)}) collective-permute-start(bf16[128,512]{1,0:T(8,128)(2,1)S(1)} %slice.10), channel_id=1, source_target_pairs={{0,4},{1,5},{4,8},{5,9},{8,12},{9,13},{12,14},{13,15},{14,10},{15,... | collective-permute-start | bytes 393224 | tf_op jit(solution)/shard_map/ppermute | solution.py:278
  54.0 3.9 %project.1 = (f32[896,512]{1,0:T(8,128)S(1)}, bf16[768,896]{1,0:T(8,128)(2,1)S(1)}) custom-call(bf16[896,4096]{1,0:T(8,128)(2,1)S(1)} %scale.1.scaled_ref, bf16[14336,896]{1,0:T(8,128)(2,1)} %basis_out_ref.1, bf16[256,512]{1,0:T(8,128)(2,1)S(1)} %bitcast.6, bf16[256,512]{1,0:T(8,128)(2,1)S(1)} %collective-permute-done.9.refs_1_, ...), custom_call_target="tpu_custom_call" | custom-call | flops 1 | bytes 1 | tf_op jit(solution)/shard_map/project/pallas_call | solution.py:405
  60.2 1.6 %window.1 = (bf16[8,48,512]{2,1,0:T(8,128)(2,1)S(1)}, f32[8,48,512]{2,1,0:T(8,128)S(1)}) custom-call(bf16[768,896]{1,0:T(8,128)(2,1)S(1)} %get-tuple-element.90.window_ref, bf16[896,4096]{1,0:T(8,128)(2,1)S(1)} %scale.1.scaled_ref, f32[896,512]{1,0:T(8,128)S(1)} %get-tuple-element.92.projected_ref, bf16[128,512]{1,0:T(8,128)(2,1)S(1)} %collective-permute-done.21.refs_0_, ...), custom_call_target="tpu_custom_call" | custom-call | flops 1 | bytes 1 | tf_op jit(solution)/shard_map/window/pallas_call | solution.py:425
  62.2 1.4 %collective-permute-done.25.got_ref = bf16[8,48,512]{2,1,0:T(8,128)(2,1)S(1)} collective-permute-done((bf16[8,48,512]{2,1,0:T(8,128)(2,1)S(1)}, bf16[8,48,512]{2,1,0:T(8,128)(2,1)S(1)}, u32[]{:S(2)}, u32[]{:S(2)}) %collective-permute-start.25) | collective-permute-done | bytes 393248 | tf_op jit(solution)/shard_map/ppermute | solution.py:48
  63.7 2.7 %collective-permute-start.26 = (bf16[48,512]{1,0:T(8,128)(2,1)S(1)}, bf16[48,512]{1,0:T(8,128)(2,1)S(1)}, u32[]{:S(2)}, u32[]{:S(2)}) collective-permute-start(bf16[48,512]{1,0:T(8,128)(2,1)S(1)} %get-tuple-element.98), channel_id=1, source_target_pairs={{0,12},{1,13},{2,14},{3,15},{4,8},{5,9},{6,10},{7,11},{8,4},{9,5},... | collective-permute-start | bytes 147464 | tf_op jit(solution)/shard_map/ppermute | solution.py:450
  66.7 1.5 %collective-permute-start.28 = (bf16[48,512]{1,0:T(8,128)(2,1)S(1)}, bf16[48,512]{1,0:T(8,128)(2,1)S(1)}, u32[]{:S(2)}, u32[]{:S(2)}) collective-permute-start(bf16[48,512]{1,0:T(8,128)(2,1)S(1)} %get-tuple-element.100), channel_id=1, source_target_pairs={{0,4},{1,5},{2,6},{3,7},{4,0},{5,1},{6,2},{7,3},{8,12},{9,13},{10,... | collective-permute-start | bytes 147464 | tf_op jit(solution)/shard_map/ppermute | solution.py:450
  68.1 2.7 %collective-permute-start.29 = (bf16[48,512]{1,0:T(8,128)(2,1)S(1)}, bf16[48,512]{1,0:T(8,128)(2,1)S(1)}, u32[]{:S(2)}, u32[]{:S(2)}) collective-permute-start(bf16[48,512]{1,0:T(8,128)(2,1)S(1)} %get-tuple-element.101), channel_id=1, source_target_pairs={{0,14},{1,15},{2,12},{3,13},{4,10},{5,11},{6,8},{7,9},{8,6},{9,7},... | collective-permute-start | bytes 147464 | tf_op jit(solution)/shard_map/ppermute | solution.py:450
  71.0 2.4 %collective-permute-start.31 = (bf16[48,512]{1,0:T(8,128)(2,1)S(1)}, bf16[48,512]{1,0:T(8,128)(2,1)S(1)}, u32[]{:S(2)}, u32[]{:S(2)}) collective-permute-start(bf16[48,512]{1,0:T(8,128)(2,1)S(1)} %get-tuple-element.103), channel_id=1, source_target_pairs={{0,6},{1,7},{2,4},{3,5},{4,2},{5,3},{6,0},{7,1},{8,14},{9,15},{10,... | collective-permute-start | bytes 147464 | tf_op jit(solution)/shard_map/ppermute | solution.py:450
  73.4 1.5 %collective-permute-start.32 = (bf16[48,512]{1,0:T(8,128)(2,1)S(1)}, bf16[48,512]{1,0:T(8,128)(2,1)S(1)}, u32[]{:S(2)}, u32[]{:S(2)}) collective-permute-start(bf16[48,512]{1,0:T(8,128)(2,1)S(1)} %get-tuple-element.104), channel_id=1, source_target_pairs={{0,2},{1,3},{2,0},{3,1},{4,6},{5,7},{6,4},{7,5},{8,10},{9,11},{10,... | collective-permute-start | bytes 147464 | tf_op jit(solution)/shard_map/ppermute | solution.py:450
  74.9 1.7 %collective-permute-done.30.refs_4_ = bf16[48,512]{1,0:T(8,128)(2,1)S(1)} collective-permute-done((bf16[48,512]{1,0:T(8,128)(2,1)S(1)}, bf16[48,512]{1,0:T(8,128)(2,1)S(1)}, u32[]{:S(2)}, u32[]{:S(2)}) %collective-permute-start.30) | collective-permute-done | bytes 49184 | tf_op jit(solution)/shard_map/ppermute | solution.py:450
  (70 shorter events, 15.9 us)
Async XLA Ops:
  0.9 8.4 %collective-permute-start = (bf16[1,2,18432]{2,1,0:T(2,128)(2,1)S(1)}, bf16[1,2,18432]{2,1,0:T(2,128)(2,1)S(1)}, u32[]{:S(2)}, u32[]{:S(2)}) collective-permute-start(bf16[1,2,18432]{2,1,0:T(2,128)(2,1)S(1)} %maximum_bitcast_fusion.refs_0_), channel_id=1, source_target_pairs={{0,4},{1,5},{2,6},{3,7},{4,0},{5,1},{6,2},{7,3},{8,12},{9,13},{10,... | collective-permute-start | bytes 221192 | tf_op jit(solution)/shard_map/ppermute | solution.py:286
  4.0 7.8 %collective-permute-start.1 = (bf16[1,2,18432]{2,1,0:T(2,128)(2,1)S(1)}, bf16[1,2,18432]{2,1,0:T(2,128)(2,1)S(1)}, u32[]{:S(2)}, u32[]{:S(2)}) collective-permute-start(bf16[1,2,18432]{2,1,0:T(2,128)(2,1)S(1)} %maximum_bitcast_fusion.refs_0_), channel_id=1, source_target_pairs={{0,8},{1,9},{2,10},{3,11},{4,12},{5,13},{6,14},{7,15},{8,0},{9,1},... | collective-permute-start | bytes 221192 | tf_op jit(solution)/shard_map/ppermute | solution.py:286
  6.6 6.3 %collective-permute-start.2 = (bf16[1,2,18432]{2,1,0:T(2,128)(2,1)S(1)}, bf16[1,2,18432]{2,1,0:T(2,128)(2,1)S(1)}, u32[]{:S(2)}, u32[]{:S(2)}) collective-permute-start(bf16[1,2,18432]{2,1,0:T(2,128)(2,1)S(1)} %maximum_bitcast_fusion.refs_0_), channel_id=1, source_target_pairs={{0,12},{1,13},{2,14},{3,15},{4,8},{5,9},{6,10},{7,11},{8,4},{9,5},... | collective-permute-start | bytes 221192 | tf_op jit(solution)/shard_map/ppermute | solution.py:286
  14.5 6.2 %collective-permute-start.3 = (bf16[4,2,14336]{2,1,0:T(2,128)(2,1)S(1)}, bf16[4,2,14336]{2,1,0:T(2,128)(2,1)S(1)}, u32[]{:S(2)}, u32[]{:S(2)}) collective-permute-start(bf16[4,2,14336]{2,1,0:T(2,128)(2,1)S(1)} %get-tuple-element.62), channel_id=1, source_target_pairs={{0,2},{1,3},{2,0},{3,1},{4,6},{5,7},{6,4},{7,5},{8,10},{9,11},{10,... | collective-permute-start | bytes 688136 | tf_op jit(solution)/shard_map/ppermute | solution.py:311
  20.8 6.6 %collective-permute-start.6 = (bf16[8,2,14336]{2,1,0:T(2,128)(2,1)S(1)}, bf16[8,2,14336]{2,1,0:T(2,128)(2,1)S(1)}, u32[]{:S(2)}, u32[]{:S(2)}) collective-permute-start(bf16[8,2,14336]{2,1,0:T(2,128)(2,1)S(1)} %constant_dynamic-update-slice_fusion.2.near_ref), channel_id=1, source_target_pairs={{0,1},{1,0},{2,3},{3,2},{4,5},{5,4},{6,7},{7,6},{8,9},{9,8},{10,11... | collective-permute-start | bytes 1376264 | tf_op jit(solution)/shard_map/ppermute | solution.py:48
  21.1 10.6 %collective-permute-start.7 = (bf16[256,512]{1,0:T(8,128)(2,1)S(1)}, bf16[256,512]{1,0:T(8,128)(2,1)S(1)}, u32[]{:S(2)}, u32[]{:S(2)}) collective-permute-start(bf16[256,512]{1,0:T(8,128)(2,1)S(1)} %bitcast.3), channel_id=1, source_target_pairs={{0,4},{1,5},{4,8},{5,9},{8,12},{9,13},{12,14},{13,15},{14,10},{15,... | collective-permute-start | bytes 786440 | tf_op jit(solution)/shard_map/ppermute | solution.py:278
  22.2 9.5 %collective-permute-start.8 = (bf16[256,512]{1,0:T(8,128)(2,1)S(1)}, bf16[256,512]{1,0:T(8,128)(2,1)S(1)}, u32[]{:S(2)}, u32[]{:S(2)}) collective-permute-start(bf16[256,512]{1,0:T(8,128)(2,1)S(1)} %bitcast.4), channel_id=1, source_target_pairs={{0,2},{1,3},{4,0},{5,1},{8,4},{9,5},{12,8},{13,9},{14,12},{15,13},... | collective-permute-start | bytes 786440 | tf_op jit(solution)/shard_map/ppermute | solution.py:279
  23.1 8.5 %collective-permute-start.9 = (bf16[256,512]{1,0:T(8,128)(2,1)S(1)}, bf16[256,512]{1,0:T(8,128)(2,1)S(1)}, u32[]{:S(2)}, u32[]{:S(2)}) collective-permute-start(bf16[256,512]{1,0:T(8,128)(2,1)S(1)} %bitcast.5), channel_id=1, source_target_pairs={{0,1},{1,0},{2,3},{3,2},{4,5},{5,4},{6,7},{7,6},{8,9},{9,8},{10,11... | collective-permute-start | bytes 786440 | tf_op jit(solution)/shard_map/ppermute | solution.py:48
  23.1 12.1 %all-to-all-start = ((bf16[8,32,256]{2,1,0:T(8,128)(2,1)}), bf16[8,32,256]{2,1,0:T(8,128)(2,1)S(1)}, u32[]{:S(2)}, u32[]{:S(2)}) async-start(bf16[8,32,256]{2,1,0:T(8,128)(2,1)} %rotate_in.1), calls=%async_computation | async-start | bytes 262144 | tf_op jit(solution)/shard_map/all_to_all | solution.py:44
  31.7 10.1 %collective-permute-start.10 = (bf16[256,512]{1,0:T(8,128)(2,1)S(1)}, bf16[256,512]{1,0:T(8,128)(2,1)S(1)}, u32[]{:S(2)}, u32[]{:S(2)}) collective-permute-start(bf16[256,512]{1,0:T(8,128)(2,1)S(1)} %collective-permute-done.7.refs_2_), channel_id=1, source_target_pairs={{0,4},{1,5},{4,8},{5,9},{8,12},{9,13},{12,14},{13,15},{14,10},{15,... | collective-permute-start | bytes 786440 | tf_op jit(solution)/shard_map/ppermute | solution.py:278
  33.7 8.1 %collective-permute-start.11 = (bf16[256,512]{1,0:T(8,128)(2,1)S(1)}, bf16[256,512]{1,0:T(8,128)(2,1)S(1)}, u32[]{:S(2)}, u32[]{:S(2)}) collective-permute-start(bf16[256,512]{1,0:T(8,128)(2,1)S(1)} %collective-permute-done.8.refs_4_), channel_id=1, source_target_pairs={{0,2},{1,3},{4,0},{5,1},{8,4},{9,5},{12,8},{13,9},{14,12},{15,13},... | collective-permute-start | bytes 786440 | tf_op jit(solution)/shard_map/ppermute | solution.py:279
  33.8 8.0 %collective-permute-start.13 = (bf16[256,512]{1,0:T(8,128)(2,1)S(1)}, bf16[256,512]{1,0:T(8,128)(2,1)S(1)}, u32[]{:S(2)}, u32[]{:S(2)}) collective-permute-start(bf16[256,512]{1,0:T(8,128)(2,1)S(1)} %collective-permute-done.7.refs_2_), channel_id=1, source_target_pairs={{0,1},{1,0},{2,3},{3,2},{4,5},{5,4},{6,7},{7,6},{8,9},{9,8},{10,11... | collective-permute-start | bytes 786440 | tf_op jit(solution)/shard_map/ppermute | solution.py:48
  33.8 8.0 %collective-permute-start.14 = (bf16[256,512]{1,0:T(8,128)(2,1)S(1)}, bf16[256,512]{1,0:T(8,128)(2,1)S(1)}, u32[]{:S(2)}, u32[]{:S(2)}) collective-permute-start(bf16[256,512]{1,0:T(8,128)(2,1)S(1)} %collective-permute-done.8.refs_4_), channel_id=1, source_target_pairs={{0,1},{1,0},{2,3},{3,2},{4,5},{5,4},{6,7},{7,6},{8,9},{9,8},{10,11... | collective-permute-start | bytes 786440 | tf_op jit(solution)/shard_map/ppermute | solution.py:48
  35.2 6.6 %collective-permute-start.12 = (bf16[8,32,256]{2,1,0:T(8,128)(2,1)S(1)}, bf16[8,32,256]{2,1,0:T(8,128)(2,1)S(1)}, u32[]{:S(2)}, u32[]{:S(2)}) collective-permute-start(bf16[8,32,256]{2,1,0:T(8,128)(2,1)S(1)} %all-to-all-done.near_ref), channel_id=1, source_target_pairs={{0,1},{1,0},{2,3},{3,2},{4,5},{5,4},{6,7},{7,6},{8,9},{9,8},{10,11... | collective-permute-start | bytes 393224 | tf_op jit(solution)/shard_map/ppermute | solution.py:48
  41.8 8.8 %collective-permute-start.15 = (bf16[256,512]{1,0:T(8,128)(2,1)S(1)}, bf16[256,512]{1,0:T(8,128)(2,1)S(1)}, u32[]{:S(2)}, u32[]{:S(2)}) collective-permute-start(bf16[256,512]{1,0:T(8,128)(2,1)S(1)} %collective-permute-done.10.refs_6_), channel_id=1, source_target_pairs={{0,4},{1,5},{4,8},{5,9},{8,12},{9,13},{12,14},{13,15},{14,10},{15,... | collective-permute-start | bytes 786440 | tf_op jit(solution)/shard_map/ppermute | solution.py:278
  43.1 8.3 %collective-permute-start.16 = (bf16[256,512]{1,0:T(8,128)(2,1)S(1)}, bf16[256,512]{1,0:T(8,128)(2,1)S(1)}, u32[]{:S(2)}, u32[]{:S(2)}) collective-permute-start(bf16[256,512]{1,0:T(8,128)(2,1)S(1)} %collective-permute-done.11.refs_8_), channel_id=1, source_target_pairs={{0,2},{1,3},{4,0},{5,1},{8,4},{9,5},{12,8},{13,9},{14,12},{15,13},... | collective-permute-start | bytes 786440 | tf_op jit(solution)/shard_map/ppermute | solution.py:279
  43.9 7.5 %collective-permute-start.17 = (bf16[256,512]{1,0:T(8,128)(2,1)S(1)}, bf16[256,512]{1,0:T(8,128)(2,1)S(1)}, u32[]{:S(2)}, u32[]{:S(2)}) collective-permute-start(bf16[256,512]{1,0:T(8,128)(2,1)S(1)} %collective-permute-done.10.refs_6_), channel_id=1, source_target_pairs={{0,1},{1,0},{2,3},{3,2},{4,5},{5,4},{6,7},{7,6},{8,9},{9,8},{10,11... | collective-permute-start | bytes 786440 | tf_op jit(solution)/shard_map/ppermute | solution.py:48
  43.9 7.5 %collective-permute-start.18 = (bf16[256,512]{1,0:T(8,128)(2,1)S(1)}, bf16[256,512]{1,0:T(8,128)(2,1)S(1)}, u32[]{:S(2)}, u32[]{:S(2)}) collective-permute-start(bf16[256,512]{1,0:T(8,128)(2,1)S(1)} %collective-permute-done.11.refs_8_), channel_id=1, source_target_pairs={{0,1},{1,0},{2,3},{3,2},{4,5},{5,4},{6,7},{7,6},{8,9},{9,8},{10,11... | collective-permute-start | bytes 786440 | tf_op jit(solution)/shard_map/ppermute | solution.py:48
  51.9 6.0 %collective-permute-start.21 = (bf16[128,512]{1,0:T(8,128)(2,1)S(1)}, bf16[128,512]{1,0:T(8,128)(2,1)S(1)}, u32[]{:S(2)}, u32[]{:S(2)}) collective-permute-start(bf16[128,512]{1,0:T(8,128)(2,1)S(1)} %slice.10), channel_id=1, source_target_pairs={{0,4},{1,5},{4,8},{5,9},{8,12},{9,13},{12,14},{13,15},{14,10},{15,... | collective-permute-start | bytes 393224 | tf_op jit(solution)/shard_map/ppermute | solution.py:278
  63.7 7.4 %collective-permute-start.26 = (bf16[48,512]{1,0:T(8,128)(2,1)S(1)}, bf16[48,512]{1,0:T(8,128)(2,1)S(1)}, u32[]{:S(2)}, u32[]{:S(2)}) collective-permute-start(bf16[48,512]{1,0:T(8,128)(2,1)S(1)} %get-tuple-element.98), channel_id=1, source_target_pairs={{0,12},{1,13},{2,14},{3,15},{4,8},{5,9},{6,10},{7,11},{8,4},{9,5},... | collective-permute-start | bytes 147464 | tf_op jit(solution)/shard_map/ppermute | solution.py:450
  66.4 7.0 %collective-permute-start.27 = (bf16[48,512]{1,0:T(8,128)(2,1)S(1)}, bf16[48,512]{1,0:T(8,128)(2,1)S(1)}, u32[]{:S(2)}, u32[]{:S(2)}) collective-permute-start(bf16[48,512]{1,0:T(8,128)(2,1)S(1)} %get-tuple-element.99), channel_id=1, source_target_pairs={{0,8},{1,9},{2,10},{3,11},{4,12},{5,13},{6,14},{7,15},{8,0},{9,1},... | collective-permute-start | bytes 147464 | tf_op jit(solution)/shard_map/ppermute | solution.py:450
  66.7 8.2 %collective-permute-start.28 = (bf16[48,512]{1,0:T(8,128)(2,1)S(1)}, bf16[48,512]{1,0:T(8,128)(2,1)S(1)}, u32[]{:S(2)}, u32[]{:S(2)}) collective-permute-start(bf16[48,512]{1,0:T(8,128)(2,1)S(1)} %get-tuple-element.100), channel_id=1, source_target_pairs={{0,4},{1,5},{2,6},{3,7},{4,0},{5,1},{6,2},{7,3},{8,12},{9,13},{10,... | collective-permute-start | bytes 147464 | tf_op jit(solution)/shard_map/ppermute | solution.py:450
  68.1 6.8 %collective-permute-start.29 = (bf16[48,512]{1,0:T(8,128)(2,1)S(1)}, bf16[48,512]{1,0:T(8,128)(2,1)S(1)}, u32[]{:S(2)}, u32[]{:S(2)}) collective-permute-start(bf16[48,512]{1,0:T(8,128)(2,1)S(1)} %get-tuple-element.101), channel_id=1, source_target_pairs={{0,14},{1,15},{2,12},{3,13},{4,10},{5,11},{6,8},{7,9},{8,6},{9,7},... | collective-permute-start | bytes 147464 | tf_op jit(solution)/shard_map/ppermute | solution.py:450
  71.0 6.0 %collective-permute-start.31 = (bf16[48,512]{1,0:T(8,128)(2,1)S(1)}, bf16[48,512]{1,0:T(8,128)(2,1)S(1)}, u32[]{:S(2)}, u32[]{:S(2)}) collective-permute-start(bf16[48,512]{1,0:T(8,128)(2,1)S(1)} %get-tuple-element.103), channel_id=1, source_target_pairs={{0,6},{1,7},{2,4},{3,5},{4,2},{5,3},{6,0},{7,1},{8,14},{9,15},{10,... | collective-permute-start | bytes 147464 | tf_op jit(solution)/shard_map/ppermute | solution.py:450
  (14 other events, 54.8 us)

commit v22 on v21

--- a/solution.py
+++ b/solution.py
@@ -46,6 +46,19 @@
 
 def swap(x, n):
     return lax.ppermute(x, "blk", xor_pairs(n, 1))
+
+
+def swap_both(first, last, n):
+    both = pl.pallas_call(
+        lay_kernel,
+        out_shape=jax.ShapeDtypeStruct((2, *first.shape), first.dtype),
+        in_specs=[VMEM, VMEM],
+        out_specs=VMEM,
+        compiler_params=pltpu.CompilerParams(vmem_limit_bytes=8 * MIB),
+        cost_estimate=CHEAP,
+        name="lay",
+    )(first, last)
+    return swap(both, n)
 
 
 def bits_of(size):
@@ -65,6 +78,11 @@
 def reorder(wanted, held, rotated):
     order = jnp.where(wanted == held, 1.0, 0.0).astype(jnp.bfloat16)
     return jnp.dot(order, rotated.astype(jnp.bfloat16), preferred_element_type=jnp.float32)
+
+
+def lay_kernel(first_ref, last_ref, out_ref):
+    out_ref[0] = first_ref[...]
+    out_ref[1] = last_ref[...]
 
 
 def part_kernel(*refs):
@@ -202,8 +220,11 @@
 
 
 def project_kernel(cuts, scaled_ref, basis_out_ref, *refs):
-    pieces = refs[:-4]
     out_ref, window_ref, basis, sem = refs[-4:]
+    near = refs[: cuts[-1] // 2]
+    own_far, *pairs = refs[len(near) : -4]
+    far = [own_far] + [pair.at[at] for pair in pairs for at in range(2)]
+    pieces = [piece for pair in zip(near, far) for piece in pair]
     width = pieces[0].shape[0]
     copies = [
         pltpu.make_async_copy(piece, basis.at[pl.ds(at * width, width)], sem.at[at])
@@ -225,15 +246,24 @@
     window_copy.wait()
 
 
-def window_kernel(scale, window_ref, scaled_ref, projected_ref, *refs):
-    pieces = refs[:-3]
-    send_ref, keep_ref, result = refs[-3:]
+def window_kernel(
+    scale,
+    window_ref,
+    scaled_ref,
+    projected_ref,
+    first_ref,
+    last_ref,
+    far_ref,
+    send_ref,
+    keep_ref,
+    result,
+):
     chips, rows, _ = keep_ref.shape
-    width = pieces[0].shape[0]
-    total = projected_ref[...]
-    first = scaled_ref.shape[1] - width * len(pieces)
-    basis = jnp.concatenate([piece[...] for piece in pieces], axis=0)
-    total += jnp.dot(scaled_ref[:, first:], basis, preferred_element_type=jnp.float32)
+    basis = jnp.concatenate([first_ref[...], last_ref[...], far_ref[0], far_ref[1]], axis=0)
+    columns = slice(scaled_ref.shape[1] - basis.shape[0], None)
+    total = projected_ref[...] + jnp.dot(
+        scaled_ref[:, columns], basis, preferred_element_type=jnp.float32
+    )
     result[...] = scale * jnp.dot(
         window_ref[...], total.astype(jnp.bfloat16), preferred_element_type=jnp.float32
     )
@@ -350,7 +380,7 @@
         basis_out,
     )
     start, right[-1], left[-1], *far = after(start, right[-1], left[-1], *far)
-    far += [swap(right[-1], n), swap(left[-1], n)]
+    far += [swap_both(right[-1], left[-1], n)]
     right.append(to_right(right[-1]))
     left.append(to_left(left[-1]))
     start, grads, rotated = after(start, grads, rotated)
@@ -374,7 +404,7 @@
     aligned, right[-1], left[-1], rotated_far, *far = after(
         aligned, right[-1], left[-1], rotated_far, *far
     )
-    far += [swap(right[-1], n), swap(left[-1], n)]
+    far += [swap_both(right[-1], left[-1], n)]
     right.append(to_right(right[-1]))
     left.append(to_left(left[-1]))
     begun = [0] + [at for step in range(1, steps) for at in (step, chips - step)] + [steps]
@@ -400,27 +430,27 @@
     cut = in_width // 2
     last = [to_right(right[-1][:cut]), to_left(left[-1][cut:])]
     near = [right[at] if at < steps else left[chips - at] for at in begun[:-1]]
-    far += [swap(piece, n) for piece in near[len(far) :]]
-    pieces = [piece for pair in zip(near, far) for piece in pair]
+    far += [swap_both(right[-1], left[-1], n)]
+    count = 2 * len(near)
     projected, window = pl.pallas_call(
-        functools.partial(project_kernel, (0, 6, len(pieces))),
+        functools.partial(project_kernel, (0, 6, count)),
         out_shape=(
             jax.ShapeDtypeStruct((tile_width, WC), jnp.float32),
             jax.ShapeDtypeStruct((WR, tile_width), jnp.bfloat16),
         ),
-        in_specs=[VMEM] + [ANY] * (len(pieces) + 1),
+        in_specs=[VMEM] + [ANY] * (1 + len(near) + len(far)),
         out_specs=(VMEM, VMEM),
         scratch_shapes=[
-            pltpu.VMEM((len(pieces) * in_width, WC), jnp.bfloat16),
-            pltpu.SemaphoreType.DMA((len(pieces) + 1,)),
+            pltpu.VMEM((count * in_width, WC), jnp.bfloat16),
+            pltpu.SemaphoreType.DMA((count + 1,)),
         ],
         compiler_params=pltpu.CompilerParams(vmem_limit_bytes=24 * MIB),
         cost_estimate=CHEAP,
         name="project",
-    )(scaled, basis_out, *pieces)
+    )(scaled, basis_out, *near, *far)
 
     projected, *last = after(projected, *last)
-    last += [swap(piece, n) for piece in last]
+    last.append(swap_both(*last, n))
     rows = WR // n
     send, keep = pl.pallas_call(
         functools.partial(window_kernel, 1.0 / tokens),
@@ -428,7 +458,7 @@
             jax.ShapeDtypeStruct((chips, rows, WC), jnp.bfloat16),
             jax.ShapeDtypeStruct((chips, rows, WC), jnp.float32),
         ),
-        in_specs=[VMEM] * 7,
+        in_specs=[VMEM] * 6,
         out_specs=(VMEM, VMEM),
         scratch_shapes=[pltpu.VMEM((WR, WC), jnp.float32)],
         compiler_params=pltpu.CompilerParams(vmem_limit_bytes=24 * MIB),

time: 78.6 us -> 87.9 us (1.12)
  waiting for transfers between devices: 15 us -> 23.5 us
  local copies, waits for them, and re-layouts: 3.02 us -> 4.49 us
    all_to_all x1, waiting for transfers between devices: 0.89 us -> 6.2 us  [exchange(): return lax.all_to_all(x, 'blk', 0, 0, axis_index_groups=groups, tiled=True)]
    ppermute x4, waiting for transfers between devices: 0.01 us -> 2.41 us  [ring_body(): to_right = lambda x: lax.ppermute(x, 'blk', shift_pairs(n, 1))]
    ppermute x4, starting transfers between devices: 5.95 us -> 3.6 us  [ring_body(): to_right = lambda x: lax.ppermute(x, 'blk', shift_pairs(n, 1))]
    ppermute x4, starting transfers between devices: 2.38 us -> 4.6 us  [ring_body(): to_left = lambda x: lax.ppermute(x, 'blk', shift_pairs(n, -1))]
    unnamed x9 -> x17, local copies, waits for them, and re-layouts: 1.95 us -> 3.42 us
    ppermute x13 -> x9, starting transfers between devices: 2.74 us -> 1.3 us  [swap(): return lax.ppermute(x, 'blk', xor_pairs(n, 1))]
    ppermute x13 -> x9, waiting for transfers between devices: 3.59 us -> 4.27 us  [swap(): return lax.ppermute(x, 'blk', xor_pairs(n, 1))]
    pallas_call x1 -> x5, Pallas kernels: 3.92 us -> 4.05 us  [the longest x1 3.93 us: ring_body(): pl.pallas_call(functools.partial(project_kernel, (0, 6, count)), out_shap...]
  transfers between devices with their start and end apart: 34 -> 30, of which waited for: 13 -> 14; matrix products, arithmetic and copies ran while one was open for 1% -> 0% of each run, Pallas kernels for 28% -> 25%
where the time goes in v22:
time: 87.9 us; the launch traced here: 87.6 us
  starting transfers between devices  33.7 us (38%)
  Pallas kernels  24.7 us (28%)
  waiting for transfers between devices  23.5 us (27%)
  local copies, waits for them, and re-layouts  4.49 us (5%)
  other arithmetic  0.91 us (1%)
    ppermute x7, starting transfers between devices, ring_body(): lax.ppermute(x, 'blk', xor_pairs(n, 2 * key))  12 us
    pallas_call x2, Pallas kernels, ring_body(): pl.pallas_call(kernel, out_shape=jax.ShapeDtypeStruct(shape, dtype), in_s...  10.7 us
    all_to_all x1, waiting for transfers between devices, exchange(): return lax.all_to_all(x, 'blk', 0, 0, axis_index_groups=groups, tiled=True)  6.2 us
    pallas_call x1, Pallas kernels, ring_body(): pl.pallas_call(functools.partial(scale_kernel, begun), out_shape=jax.Shap...  6.19 us
    ppermute x3, starting transfers between devices, ring_body(): lax.ppermute(both, 'blk', xor_pairs(n, 4 * key))  5.68 us
    ppermute x4, starting transfers between devices, ring_body(): to_left = lambda x: lax.ppermute(x, 'blk', shift_pairs(n, -1))  4.6 us
    all_to_all x1, starting transfers between devices, exchange(): return lax.all_to_all(x, 'blk', 0, 0, axis_index_groups=groups, tiled=True)  4.39 us
    ppermute x9, waiting for transfers between devices, swap(): return lax.ppermute(x, 'blk', xor_pairs(n, 1))  4.27 us
  transfers between devices with their start and end apart: 30, of which 14 were waited for; matrix products, arithmetic and copies ran while one was open for 0% of the time, Pallas kernels for 25%

profile of v22, /device:TPU:0, one launch (start us, length us, event | category | flops | bytes accessed | tf_op | source)
XLA Modules:
  0.0 87.6 jit_solution(5543465823957060458)
XLA Ops:
  0.9 3.1 %collective-permute-start = (bf16[1,2,18432]{2,1,0:T(2,128)(2,1)S(1)}, bf16[1,2,18432]{2,1,0:T(2,128)(2,1)S(1)}, u32[]{:S(2)}, u32[]{:S(2)}) collective-permute-start(bf16[1,2,18432]{2,1,0:T(2,128)(2,1)S(1)} %maximum_bitcast_fusion.refs_0_), channel_id=1, source_target_pairs={{0,4},{1,5},{2,6},{3,7},{4,0},{5,1},{6,2},{7,3},{8,12},{9,13},{10,... | collective-permute-start | bytes 221192 | tf_op jit(solution)/shard_map/ppermute | solution.py:316
  4.0 2.6 %collective-permute-start.1 = (bf16[1,2,18432]{2,1,0:T(2,128)(2,1)S(1)}, bf16[1,2,18432]{2,1,0:T(2,128)(2,1)S(1)}, u32[]{:S(2)}, u32[]{:S(2)}) collective-permute-start(bf16[1,2,18432]{2,1,0:T(2,128)(2,1)S(1)} %maximum_bitcast_fusion.refs_0_), channel_id=1, source_target_pairs={{0,8},{1,9},{2,10},{3,11},{4,12},{5,13},{6,14},{7,15},{8,0},{9,1},... | collective-permute-start | bytes 221192 | tf_op jit(solution)/shard_map/ppermute | solution.py:316
  6.6 1.6 %copy-done = bf16[4096,256]{1,0:T(8,128)(2,1)S(1)} copy-done((bf16[4096,256]{1,0:T(8,128)(2,1)S(1)}, bf16[4096,256]{1,0:T(8,128)(2,1)}, u32[]{:S(2)}) %copy-start) | copy-done | bytes 2097176
  9.3 2.5 %collective-permute-done.1.refs_2_ = bf16[1,2,18432]{2,1,0:T(2,128)(2,1)S(1)} collective-permute-done((bf16[1,2,18432]{2,1,0:T(2,128)(2,1)S(1)}, bf16[1,2,18432]{2,1,0:T(2,128)(2,1)S(1)}, u32[]{:S(2)}, u32[]{:S(2)}) %collective-permute-start.1) | collective-permute-done | bytes 73760 | tf_op jit(solution)/shard_map/ppermute | solution.py:316
  12.9 1.6 %collective-permute-start.4 = (bf16[4,2,4096]{2,1,0:T(2,128)(2,1)S(1)}, bf16[4,2,4096]{2,1,0:T(2,128)(2,1)S(1)}, u32[]{:S(2)}, u32[]{:S(2)}) collective-permute-start(bf16[4,2,4096]{2,1,0:T(2,128)(2,1)S(1)} %get-tuple-element.61), channel_id=1, source_target_pairs={{0,2},{1,3},{2,0},{3,1},{4,6},{5,7},{6,4},{7,5},{8,10},{9,11},{10,... | collective-permute-start | bytes 196616 | tf_op jit(solution)/shard_map/ppermute | solution.py:340
  15.1 2.9 %collective-permute-done.4 = bf16[4,2,4096]{2,1,0:T(2,128)(2,1)S(1)} collective-permute-done((bf16[4,2,4096]{2,1,0:T(2,128)(2,1)S(1)}, bf16[4,2,4096]{2,1,0:T(2,128)(2,1)S(1)}, u32[]{:S(2)}, u32[]{:S(2)}) %collective-permute-start.4) | collective-permute-done | bytes 65568 | tf_op jit(solution)/shard_map/ppermute | solution.py:340
  23.1 4.2 %rotate_first.1.start_ref = f32[32,896]{1,0:T(8,128)S(1)} custom-call(bf16[8,2,14336]{2,1,0:T(2,128)(2,1)S(1)} %constant_dynamic-update-slice_fusion.2.near_ref, bf16[8,2,14336]{2,1,0:T(2,128)(2,1)S(1)} %collective-permute-done.6.far_ref, bf16[14336,896]{1,0:T(8,128)(2,1)} %basis_out_ref.1), custom_call_target="tpu_custom_call" | custom-call | flops 1 | bytes 1 | tf_op jit(solution)/shard_map/rotate_first/pallas_call | solution.py:360
  27.3 2.4 %collective-permute-done.7.first_ref.refs_1_ = bf16[256,512]{1,0:T(8,128)(2,1)S(1)} collective-permute-done((bf16[256,512]{1,0:T(8,128)(2,1)S(1)}, bf16[256,512]{1,0:T(8,128)(2,1)S(1)}, u32[]{:S(2)}, u32[]{:S(2)}) %collective-permute-start.7) | collective-permute-done | bytes 262176 | tf_op jit(solution)/shard_map/ppermute | solution.py:308
  31.5 4.4 %all-to-all-start = ((bf16[8,32,256]{2,1,0:T(8,128)(2,1)}), bf16[8,32,256]{2,1,0:T(8,128)(2,1)S(1)}, u32[]{:S(2)}, u32[]{:S(2)}) async-start(bf16[8,32,256]{2,1,0:T(8,128)(2,1)} %rotate_in.1), calls=%async_computation | async-start | bytes 262144 | tf_op jit(solution)/shard_map/all_to_all | solution.py:44
  35.9 2.0 %collective-permute-start.10 = (bf16[256,512]{1,0:T(8,128)(2,1)S(1)}, bf16[256,512]{1,0:T(8,128)(2,1)S(1)}, u32[]{:S(2)}, u32[]{:S(2)}) collective-permute-start(bf16[256,512]{1,0:T(8,128)(2,1)S(1)} %collective-permute-done.7.first_ref.refs_1_), channel_id=1, source_target_pairs={{0,4},{1,5},{4,8},{5,9},{8,12},{9,13},{12,14},{13,15},{14,10},{15,... | collective-permute-start | bytes 786440 | tf_op jit(solution)/shard_map/ppermute | solution.py:308
  37.9 6.2 %all-to-all-done.near_ref = bf16[8,32,256]{2,1,0:T(8,128)(2,1)S(1)} async-done(((bf16[8,32,256]{2,1,0:T(8,128)(2,1)}), bf16[8,32,256]{2,1,0:T(8,128)(2,1)S(1)}, u32[]{:S(2)}, u32[]{:S(2)}) %all-to-all-start) | async-done | bytes 131104 | tf_op jit(solution)/shard_map/all_to_all | solution.py:44
  45.0 6.6 %rotate_last.1.aligned_ref = bf16[896,32]{1,0:T(8,128)(2,1)S(1)} custom-call(bf16[8,2,14336]{2,1,0:T(2,128)(2,1)S(1)} %constant_dynamic-update-slice_fusion.2.near_ref, bf16[8,2,14336]{2,1,0:T(2,128)(2,1)S(1)} %collective-permute-done.6.far_ref, bf16[14336,896]{1,0:T(8,128)(2,1)} %basis_out_ref.1, s32[16]{0:T(128)S(1)} %copy-done.6, f32[32,896]{1,0:T(8,128)S(1)} %copy-done.2), custom_call_target="tpu_custom_call" | custom-call | flops 1 | bytes 1 | tf_op jit(solution)/shard_map/rotate_last/pallas_call | solution.py:360
  52.3 2.0 %collective-permute-start.15 = (bf16[256,512]{1,0:T(8,128)(2,1)S(1)}, bf16[256,512]{1,0:T(8,128)(2,1)S(1)}, u32[]{:S(2)}, u32[]{:S(2)}) collective-permute-start(bf16[256,512]{1,0:T(8,128)(2,1)S(1)} %collective-permute-done.11.last_ref.refs_4_), channel_id=1, source_target_pairs={{0,2},{1,3},{4,0},{5,1},{8,4},{9,5},{12,8},{13,9},{14,12},{15,13},... | collective-permute-start | bytes 786440 | tf_op jit(solution)/shard_map/ppermute | solution.py:309
  54.3 6.2 %scale.1.scaled_ref = bf16[896,4096]{1,0:T(8,128)(2,1)S(1)} custom-call(bf16[896,32]{1,0:T(8,128)(2,1)S(1)} %rotate_last.1.aligned_ref, bf16[8,32,256]{2,1,0:T(8,128)(2,1)S(1)} %all-to-all-done.near_ref, bf16[8,32,256]{2,1,0:T(8,128)(2,1)S(1)} %collective-permute-done.12.far_ref, s32[32]{0:T(128)S(1)} %copy-done.5, f32[896,4096]{1,0:T(8,128)} %eigen_ref.1), custom_call_target="tpu_custom_call" | custom-call | flops 1 | bytes 1 | tf_op jit(solution)/shard_map/scale/pallas_call | solution.py:412
  61.2 1.6 %collective-permute-start.19 = (bf16[128,512]{1,0:T(8,128)(2,1)S(1)}, bf16[128,512]{1,0:T(8,128)(2,1)S(1)}, u32[]{:S(2)}, u32[]{:S(2)}) collective-permute-start(bf16[128,512]{1,0:T(8,128)(2,1)S(1)} %slice.11), channel_id=1, source_target_pairs={{0,2},{1,3},{4,0},{5,1},{8,4},{9,5},{12,8},{13,9},{14,12},{15,13},... | collective-permute-start | bytes 393224 | tf_op jit(solution)/shard_map/ppermute | solution.py:309
  62.9 3.9 %project.1 = (f32[896,512]{1,0:T(8,128)S(1)}, bf16[768,896]{1,0:T(8,128)(2,1)S(1)}) custom-call(bf16[896,4096]{1,0:T(8,128)(2,1)S(1)} %scale.1.scaled_ref, bf16[14336,896]{1,0:T(8,128)(2,1)} %basis_out_ref.1, bf16[256,512]{1,0:T(8,128)(2,1)S(1)} %bitcast.6, bf16[256,512]{1,0:T(8,128)(2,1)S(1)} %collective-permute-done.7.first_ref.refs_1_, ...), custom_call_target="tpu_custom_call" | custom-call | flops 1 | bytes 1 | tf_op jit(solution)/shard_map/project/pallas_call | solution.py:435
  67.0 1.5 %collective-permute-done.20.far_ref = bf16[2,128,512]{2,1,0:T(8,128)(2,1)S(1)} collective-permute-done((bf16[2,128,512]{2,1,0:T(8,128)(2,1)S(1)}, bf16[2,128,512]{2,1,0:T(8,128)(2,1)S(1)}, u32[]{:S(2)}, u32[]{:S(2)}) %collective-permute-start.20) | collective-permute-done | bytes 262176 | tf_op jit(solution)/shard_map/ppermute | solution.py:48
  68.5 1.6 %window.1 = (bf16[8,48,512]{2,1,0:T(8,128)(2,1)S(1)}, f32[8,48,512]{2,1,0:T(8,128)S(1)}) custom-call(bf16[768,896]{1,0:T(8,128)(2,1)S(1)} %get-tuple-element.84.window_ref, bf16[896,4096]{1,0:T(8,128)(2,1)S(1)} %scale.1.scaled_ref, f32[896,512]{1,0:T(8,128)S(1)} %get-tuple-element.86.projected_ref, bf16[128,512]{1,0:T(8,128)(2,1)S(1)} %collective-permute-done.18.first_ref, ...), custom_call_target="tpu_custom_call" | custom-call | flops 1 | bytes 1 | tf_op jit(solution)/shard_map/window/pallas_call | solution.py:455
  70.3 1.6 %collective-permute-done.21.got_ref = bf16[8,48,512]{2,1,0:T(8,128)(2,1)S(1)} collective-permute-done((bf16[8,48,512]{2,1,0:T(8,128)(2,1)S(1)}, bf16[8,48,512]{2,1,0:T(8,128)(2,1)S(1)}, u32[]{:S(2)}, u32[]{:S(2)}) %collective-permute-start.21) | collective-permute-done | bytes 393248 | tf_op jit(solution)/shard_map/ppermute | solution.py:48
  72.0 2.0 %collective-permute-start.22 = (bf16[48,512]{1,0:T(8,128)(2,1)S(1)}, bf16[48,512]{1,0:T(8,128)(2,1)S(1)}, u32[]{:S(2)}, u32[]{:S(2)}) collective-permute-start(bf16[48,512]{1,0:T(8,128)(2,1)S(1)} %get-tuple-element.92), channel_id=1, source_target_pairs={{0,12},{1,13},{2,14},{3,15},{4,8},{5,9},{6,10},{7,11},{8,4},{9,5},... | collective-permute-start | bytes 147464 | tf_op jit(solution)/shard_map/ppermute | solution.py:480
  74.0 2.4 %collective-permute-start.24 = (bf16[48,512]{1,0:T(8,128)(2,1)S(1)}, bf16[48,512]{1,0:T(8,128)(2,1)S(1)}, u32[]{:S(2)}, u32[]{:S(2)}) collective-permute-start(bf16[48,512]{1,0:T(8,128)(2,1)S(1)} %get-tuple-element.94), channel_id=1, source_target_pairs={{0,4},{1,5},{2,6},{3,7},{4,0},{5,1},{6,2},{7,3},{8,12},{9,13},{10,... | collective-permute-start | bytes 147464 | tf_op jit(solution)/shard_map/ppermute | solution.py:480
  76.4 3.1 %collective-permute-start.25 = (bf16[48,512]{1,0:T(8,128)(2,1)S(1)}, bf16[48,512]{1,0:T(8,128)(2,1)S(1)}, u32[]{:S(2)}, u32[]{:S(2)}) collective-permute-start(bf16[48,512]{1,0:T(8,128)(2,1)S(1)} %get-tuple-element.95), channel_id=1, source_target_pairs={{0,14},{1,15},{2,12},{3,13},{4,10},{5,11},{6,8},{7,9},{8,6},{9,7},... | collective-permute-start | bytes 147464 | tf_op jit(solution)/shard_map/ppermute | solution.py:480
  79.5 3.3 %collective-permute-start.27 = (bf16[48,512]{1,0:T(8,128)(2,1)S(1)}, bf16[48,512]{1,0:T(8,128)(2,1)S(1)}, u32[]{:S(2)}, u32[]{:S(2)}) collective-permute-start(bf16[48,512]{1,0:T(8,128)(2,1)S(1)} %get-tuple-element.97), channel_id=1, source_target_pairs={{0,6},{1,7},{2,4},{3,5},{4,2},{5,3},{6,0},{7,1},{8,14},{9,15},{10,... | collective-permute-start | bytes 147464 | tf_op jit(solution)/shard_map/ppermute | solution.py:480
  84.0 1.8 %collective-permute-done.26.refs_4_ = bf16[48,512]{1,0:T(8,128)(2,1)S(1)} collective-permute-done((bf16[48,512]{1,0:T(8,128)(2,1)S(1)}, bf16[48,512]{1,0:T(8,128)(2,1)S(1)}, u32[]{:S(2)}, u32[]{:S(2)}) %collective-permute-start.26) | collective-permute-done | bytes 49184 | tf_op jit(solution)/shard_map/ppermute | solution.py:480
  (74 shorter events, 16.4 us)
Async XLA Ops:
  0.9 8.4 %collective-permute-start = (bf16[1,2,18432]{2,1,0:T(2,128)(2,1)S(1)}, bf16[1,2,18432]{2,1,0:T(2,128)(2,1)S(1)}, u32[]{:S(2)}, u32[]{:S(2)}) collective-permute-start(bf16[1,2,18432]{2,1,0:T(2,128)(2,1)S(1)} %maximum_bitcast_fusion.refs_0_), channel_id=1, source_target_pairs={{0,4},{1,5},{2,6},{3,7},{4,0},{5,1},{6,2},{7,3},{8,12},{9,13},{10,... | collective-permute-start | bytes 221192 | tf_op jit(solution)/shard_map/ppermute | solution.py:316
  4.0 7.8 %collective-permute-start.1 = (bf16[1,2,18432]{2,1,0:T(2,128)(2,1)S(1)}, bf16[1,2,18432]{2,1,0:T(2,128)(2,1)S(1)}, u32[]{:S(2)}, u32[]{:S(2)}) collective-permute-start(bf16[1,2,18432]{2,1,0:T(2,128)(2,1)S(1)} %maximum_bitcast_fusion.refs_0_), channel_id=1, source_target_pairs={{0,8},{1,9},{2,10},{3,11},{4,12},{5,13},{6,14},{7,15},{8,0},{9,1},... | collective-permute-start | bytes 221192 | tf_op jit(solution)/shard_map/ppermute | solution.py:316
  6.6 6.3 %collective-permute-start.2 = (bf16[1,2,18432]{2,1,0:T(2,128)(2,1)S(1)}, bf16[1,2,18432]{2,1,0:T(2,128)(2,1)S(1)}, u32[]{:S(2)}, u32[]{:S(2)}) collective-permute-start(bf16[1,2,18432]{2,1,0:T(2,128)(2,1)S(1)} %maximum_bitcast_fusion.refs_0_), channel_id=1, source_target_pairs={{0,12},{1,13},{2,14},{3,15},{4,8},{5,9},{6,10},{7,11},{8,4},{9,5},... | collective-permute-start | bytes 221192 | tf_op jit(solution)/shard_map/ppermute | solution.py:316
  12.9 5.1 %collective-permute-start.4 = (bf16[4,2,4096]{2,1,0:T(2,128)(2,1)S(1)}, bf16[4,2,4096]{2,1,0:T(2,128)(2,1)S(1)}, u32[]{:S(2)}, u32[]{:S(2)}) collective-permute-start(bf16[4,2,4096]{2,1,0:T(2,128)(2,1)S(1)} %get-tuple-element.61), channel_id=1, source_target_pairs={{0,2},{1,3},{2,0},{3,1},{4,6},{5,7},{6,4},{7,5},{8,10},{9,11},{10,... | collective-permute-start | bytes 196616 | tf_op jit(solution)/shard_map/ppermute | solution.py:340
  14.5 6.2 %collective-permute-start.3 = (bf16[4,2,14336]{2,1,0:T(2,128)(2,1)S(1)}, bf16[4,2,14336]{2,1,0:T(2,128)(2,1)S(1)}, u32[]{:S(2)}, u32[]{:S(2)}) collective-permute-start(bf16[4,2,14336]{2,1,0:T(2,128)(2,1)S(1)} %get-tuple-element.59), channel_id=1, source_target_pairs={{0,2},{1,3},{2,0},{3,1},{4,6},{5,7},{6,4},{7,5},{8,10},{9,11},{10,... | collective-permute-start | bytes 688136 | tf_op jit(solution)/shard_map/ppermute | solution.py:341
  21.1 8.6 %collective-permute-start.7 = (bf16[256,512]{1,0:T(8,128)(2,1)S(1)}, bf16[256,512]{1,0:T(8,128)(2,1)S(1)}, u32[]{:S(2)}, u32[]{:S(2)}) collective-permute-start(bf16[256,512]{1,0:T(8,128)(2,1)S(1)} %bitcast.3), channel_id=1, source_target_pairs={{0,4},{1,5},{4,8},{5,9},{8,12},{9,13},{12,14},{13,15},{14,10},{15,... | collective-permute-start | bytes 786440 | tf_op jit(solution)/shard_map/ppermute | solution.py:308
  22.2 8.6 %collective-permute-start.8 = (bf16[256,512]{1,0:T(8,128)(2,1)S(1)}, bf16[256,512]{1,0:T(8,128)(2,1)S(1)}, u32[]{:S(2)}, u32[]{:S(2)}) collective-permute-start(bf16[256,512]{1,0:T(8,128)(2,1)S(1)} %bitcast.4), channel_id=1, source_target_pairs={{0,2},{1,3},{4,0},{5,1},{8,4},{9,5},{12,8},{13,9},{14,12},{15,13},... | collective-permute-start | bytes 786440 | tf_op jit(solution)/shard_map/ppermute | solution.py:309
  23.1 7.7 %collective-permute-start.9 = (bf16[256,512]{1,0:T(8,128)(2,1)S(1)}, bf16[256,512]{1,0:T(8,128)(2,1)S(1)}, u32[]{:S(2)}, u32[]{:S(2)}) collective-permute-start(bf16[256,512]{1,0:T(8,128)(2,1)S(1)} %bitcast.5), channel_id=1, source_target_pairs={{0,1},{1,0},{2,3},{3,2},{4,5},{5,4},{6,7},{7,6},{8,9},{9,8},{10,11... | collective-permute-start | bytes 786440 | tf_op jit(solution)/shard_map/ppermute | solution.py:48
  30.8 20.8 %collective-permute-start.13 = (bf16[2,256,512]{2,1,0:T(8,128)(2,1)S(1)}, bf16[2,256,512]{2,1,0:T(8,128)(2,1)S(1)}, u32[]{:S(2)}, u32[]{:S(2)}) collective-permute-start(bf16[2,256,512]{2,1,0:T(8,128)(2,1)S(1)} %lay.4), channel_id=1, source_target_pairs={{0,1},{1,0},{2,3},{3,2},{4,5},{5,4},{6,7},{7,6},{8,9},{9,8},{10,11... | collective-permute-start | bytes 1572872 | tf_op jit(solution)/shard_map/ppermute | solution.py:48
  31.5 12.6 %all-to-all-start = ((bf16[8,32,256]{2,1,0:T(8,128)(2,1)}), bf16[8,32,256]{2,1,0:T(8,128)(2,1)S(1)}, u32[]{:S(2)}, u32[]{:S(2)}) async-start(bf16[8,32,256]{2,1,0:T(8,128)(2,1)} %rotate_in.1), calls=%async_computation | async-start | bytes 262144 | tf_op jit(solution)/shard_map/all_to_all | solution.py:44
  35.9 15.7 %collective-permute-start.10 = (bf16[256,512]{1,0:T(8,128)(2,1)S(1)}, bf16[256,512]{1,0:T(8,128)(2,1)S(1)}, u32[]{:S(2)}, u32[]{:S(2)}) collective-permute-start(bf16[256,512]{1,0:T(8,128)(2,1)S(1)} %collective-permute-done.7.first_ref.refs_1_), channel_id=1, source_target_pairs={{0,4},{1,5},{4,8},{5,9},{8,12},{9,13},{12,14},{13,15},{14,10},{15,... | collective-permute-start | bytes 786440 | tf_op jit(solution)/shard_map/ppermute | solution.py:308
  37.9 13.7 %collective-permute-start.11 = (bf16[256,512]{1,0:T(8,128)(2,1)S(1)}, bf16[256,512]{1,0:T(8,128)(2,1)S(1)}, u32[]{:S(2)}, u32[]{:S(2)}) collective-permute-start(bf16[256,512]{1,0:T(8,128)(2,1)S(1)} %collective-permute-done.8.last_ref.refs_2_), channel_id=1, source_target_pairs={{0,2},{1,3},{4,0},{5,1},{8,4},{9,5},{12,8},{13,9},{14,12},{15,13},... | collective-permute-start | bytes 786440 | tf_op jit(solution)/shard_map/ppermute | solution.py:309
  44.1 7.5 %collective-permute-start.12 = (bf16[8,32,256]{2,1,0:T(8,128)(2,1)S(1)}, bf16[8,32,256]{2,1,0:T(8,128)(2,1)S(1)}, u32[]{:S(2)}, u32[]{:S(2)}) collective-permute-start(bf16[8,32,256]{2,1,0:T(8,128)(2,1)S(1)} %all-to-all-done.near_ref), channel_id=1, source_target_pairs={{0,1},{1,0},{2,3},{3,2},{4,5},{5,4},{6,7},{7,6},{8,9},{9,8},{10,11... | collective-permute-start | bytes 393224 | tf_op jit(solution)/shard_map/ppermute | solution.py:48
  51.7 8.9 %collective-permute-start.16 = (bf16[2,256,512]{2,1,0:T(8,128)(2,1)S(1)}, bf16[2,256,512]{2,1,0:T(8,128)(2,1)S(1)}, u32[]{:S(2)}, u32[]{:S(2)}) collective-permute-start(bf16[2,256,512]{2,1,0:T(8,128)(2,1)S(1)} %lay.5), channel_id=1, source_target_pairs={{0,1},{1,0},{2,3},{3,2},{4,5},{5,4},{6,7},{7,6},{8,9},{9,8},{10,11... | collective-permute-start | bytes 1572872 | tf_op jit(solution)/shard_map/ppermute | solution.py:48
  52.3 8.3 %collective-permute-start.14 = (bf16[256,512]{1,0:T(8,128)(2,1)S(1)}, bf16[256,512]{1,0:T(8,128)(2,1)S(1)}, u32[]{:S(2)}, u32[]{:S(2)}) collective-permute-start(bf16[256,512]{1,0:T(8,128)(2,1)S(1)} %collective-permute-done.10.first_ref.refs_3_), channel_id=1, source_target_pairs={{0,4},{1,5},{4,8},{5,9},{8,12},{9,13},{12,14},{13,15},{14,10},{15,... | collective-permute-start | bytes 786440 | tf_op jit(solution)/shard_map/ppermute | solution.py:308
  52.3 8.3 %collective-permute-start.15 = (bf16[256,512]{1,0:T(8,128)(2,1)S(1)}, bf16[256,512]{1,0:T(8,128)(2,1)S(1)}, u32[]{:S(2)}, u32[]{:S(2)}) collective-permute-start(bf16[256,512]{1,0:T(8,128)(2,1)S(1)} %collective-permute-done.11.last_ref.refs_4_), channel_id=1, source_target_pairs={{0,2},{1,3},{4,0},{5,1},{8,4},{9,5},{12,8},{13,9},{14,12},{15,13},... | collective-permute-start | bytes 786440 | tf_op jit(solution)/shard_map/ppermute | solution.py:309
  60.8 6.0 %collective-permute-start.18 = (bf16[128,512]{1,0:T(8,128)(2,1)S(1)}, bf16[128,512]{1,0:T(8,128)(2,1)S(1)}, u32[]{:S(2)}, u32[]{:S(2)}) collective-permute-start(bf16[128,512]{1,0:T(8,128)(2,1)S(1)} %slice.10), channel_id=1, source_target_pairs={{0,4},{1,5},{4,8},{5,9},{8,12},{9,13},{12,14},{13,15},{14,10},{15,... | collective-permute-start | bytes 393224 | tf_op jit(solution)/shard_map/ppermute | solution.py:308
  61.2 5.6 %collective-permute-start.19 = (bf16[128,512]{1,0:T(8,128)(2,1)S(1)}, bf16[128,512]{1,0:T(8,128)(2,1)S(1)}, u32[]{:S(2)}, u32[]{:S(2)}) collective-permute-start(bf16[128,512]{1,0:T(8,128)(2,1)S(1)} %slice.11), channel_id=1, source_target_pairs={{0,2},{1,3},{4,0},{5,1},{8,4},{9,5},{12,8},{13,9},{14,12},{15,13},... | collective-permute-start | bytes 393224 | tf_op jit(solution)/shard_map/ppermute | solution.py:309
  72.0 7.5 %collective-permute-start.22 = (bf16[48,512]{1,0:T(8,128)(2,1)S(1)}, bf16[48,512]{1,0:T(8,128)(2,1)S(1)}, u32[]{:S(2)}, u32[]{:S(2)}) collective-permute-start(bf16[48,512]{1,0:T(8,128)(2,1)S(1)} %get-tuple-element.92), channel_id=1, source_target_pairs={{0,12},{1,13},{2,14},{3,15},{4,8},{5,9},{6,10},{7,11},{8,4},{9,5},... | collective-permute-start | bytes 147464 | tf_op jit(solution)/shard_map/ppermute | solution.py:480
  73.9 8.9 %collective-permute-start.23 = (bf16[48,512]{1,0:T(8,128)(2,1)S(1)}, bf16[48,512]{1,0:T(8,128)(2,1)S(1)}, u32[]{:S(2)}, u32[]{:S(2)}) collective-permute-start(bf16[48,512]{1,0:T(8,128)(2,1)S(1)} %get-tuple-element.93), channel_id=1, source_target_pairs={{0,8},{1,9},{2,10},{3,11},{4,12},{5,13},{6,14},{7,15},{8,0},{9,1},... | collective-permute-start | bytes 147464 | tf_op jit(solution)/shard_map/ppermute | solution.py:480
  74.0 10.0 %collective-permute-start.24 = (bf16[48,512]{1,0:T(8,128)(2,1)S(1)}, bf16[48,512]{1,0:T(8,128)(2,1)S(1)}, u32[]{:S(2)}, u32[]{:S(2)}) collective-permute-start(bf16[48,512]{1,0:T(8,128)(2,1)S(1)} %get-tuple-element.94), channel_id=1, source_target_pairs={{0,4},{1,5},{2,6},{3,7},{4,0},{5,1},{6,2},{7,3},{8,12},{9,13},{10,... | collective-permute-start | bytes 147464 | tf_op jit(solution)/shard_map/ppermute | solution.py:480
  76.4 7.6 %collective-permute-start.25 = (bf16[48,512]{1,0:T(8,128)(2,1)S(1)}, bf16[48,512]{1,0:T(8,128)(2,1)S(1)}, u32[]{:S(2)}, u32[]{:S(2)}) collective-permute-start(bf16[48,512]{1,0:T(8,128)(2,1)S(1)} %get-tuple-element.95), channel_id=1, source_target_pairs={{0,14},{1,15},{2,12},{3,13},{4,10},{5,11},{6,8},{7,9},{8,6},{9,7},... | collective-permute-start | bytes 147464 | tf_op jit(solution)/shard_map/ppermute | solution.py:480
  79.5 6.3 %collective-permute-start.26 = (bf16[48,512]{1,0:T(8,128)(2,1)S(1)}, bf16[48,512]{1,0:T(8,128)(2,1)S(1)}, u32[]{:S(2)}, u32[]{:S(2)}) collective-permute-start(bf16[48,512]{1,0:T(8,128)(2,1)S(1)} %get-tuple-element.96), channel_id=1, source_target_pairs={{0,10},{1,11},{2,8},{3,9},{4,14},{5,15},{6,12},{7,13},{8,2},{9,3},... | collective-permute-start | bytes 147464 | tf_op jit(solution)/shard_map/ppermute | solution.py:480
  79.5 6.4 %collective-permute-start.27 = (bf16[48,512]{1,0:T(8,128)(2,1)S(1)}, bf16[48,512]{1,0:T(8,128)(2,1)S(1)}, u32[]{:S(2)}, u32[]{:S(2)}) collective-permute-start(bf16[48,512]{1,0:T(8,128)(2,1)S(1)} %get-tuple-element.97), channel_id=1, source_target_pairs={{0,6},{1,7},{2,4},{3,5},{4,2},{5,3},{6,0},{7,1},{8,14},{9,15},{10,... | collective-permute-start | bytes 147464 | tf_op jit(solution)/shard_map/ppermute | solution.py:480
  (14 other events, 79.0 us)

commit v23 on v21

--- a/solution.py
+++ b/solution.py
@@ -283,7 +283,8 @@
 
     pairs = chips // 2
     both = jnp.concatenate([grad_out, activations], axis=1)[None]
-    got = [lax.ppermute(both, "blk", xor_pairs(n, 4 * key)) for key in range(1, pairs)]
+    got = [lax.ppermute(both, "blk", xor_pairs(n, 4 * key)) for key in range(pairs - 1, 0, -1)]
+    got.reverse()
     kept = pl.pallas_call(
         keep_kernel,
         out_shape=jax.ShapeDtypeStruct(basis_in.shape, jnp.bfloat16),
@@ -436,7 +437,7 @@
         name="window",
     )(window, scaled, projected, *last)
 
-    keys = [*range(chips - 2, 0, -2), *range(chips - 1, 0, -2)]
+    keys = [*range(2, chips, 2), *range(1, chips, 2)]
     small = pltpu.CompilerParams(vmem_limit_bytes=8 * MIB)
     own, *sends = pl.pallas_call(
         functools.partial(add_core_kernel, keys),

time: 78.6 us -> 80.6 us (1.025)
  waiting for transfers between devices: 15 us -> 17.1 us
    ppermute x7, waiting for transfers between devices: 2.66 us -> 4.72 us  [ring_body(): lax.ppermute(x, 'blk', xor_pairs(n, 2 * key))]
  transfers between devices with their start and end apart: 34 -> 34, of which waited for: 13 -> 12; matrix products, arithmetic and copies ran while one was open for 1% -> 1% of each run, Pallas kernels for 28% -> 28%
where the time goes in v23:
time: 80.6 us; the launch traced here: 80.3 us
  starting transfers between devices  34.4 us (43%)
  Pallas kernels  24.6 us (31%)
  waiting for transfers between devices  17.1 us (21%)
  local copies, waits for them, and re-layouts  3.02 us (4%)
  other arithmetic  0.91 us (1%)
    ppermute x7, starting transfers between devices, ring_body(): lax.ppermute(x, 'blk', xor_pairs(n, 2 * key))  11.2 us
    pallas_call x2, Pallas kernels, ring_body(): pl.pallas_call(kernel, out_shape=jax.ShapeDtypeStruct(shape, dtype), in_s...  10.7 us
    pallas_call x1, Pallas kernels, ring_body(): pl.pallas_call(functools.partial(scale_kernel, begun), out_shape=jax.Shap...  6.22 us
    ppermute x4, starting transfers between devices, ring_body(): to_right = lambda x: lax.ppermute(x, 'blk', shift_pairs(n, 1))  5.95 us
    ppermute x3, starting transfers between devices, ring_body(): lax.ppermute(both, 'blk', xor_pairs(n, 4 * key))  5.68 us
    ppermute x7, waiting for transfers between devices, ring_body(): lax.ppermute(x, 'blk', xor_pairs(n, 2 * key))  4.72 us
    all_to_all x1, starting transfers between devices, exchange(): return lax.all_to_all(x, 'blk', 0, 0, axis_index_groups=groups, tiled=True)  4.33 us
    pallas_call x1, Pallas kernels, ring_body(): pl.pallas_call(functools.partial(project_kernel, (0, 6, len(pieces))), ou...  3.92 us
  transfers between devices with their start and end apart: 34, of which 12 were waited for; matrix products, arithmetic and copies ran while one was open for 1% of the time, Pallas kernels for 28%

profile of v23, /device:TPU:0, one launch (start us, length us, event | category | flops | bytes accessed | tf_op | source)
XLA Modules:
  0.0 80.3 jit_solution(8347938439617720910)
XLA Ops:
  0.9 3.1 %collective-permute-start = (bf16[1,2,18432]{2,1,0:T(2,128)(2,1)S(1)}, bf16[1,2,18432]{2,1,0:T(2,128)(2,1)S(1)}, u32[]{:S(2)}, u32[]{:S(2)}) collective-permute-start(bf16[1,2,18432]{2,1,0:T(2,128)(2,1)S(1)} %maximum_bitcast_fusion.refs_0_), channel_id=1, source_target_pairs={{0,4},{1,5},{2,6},{3,7},{4,0},{5,1},{6,2},{7,3},{8,12},{9,13},{10,... | collective-permute-start | bytes 221192 | tf_op jit(solution)/shard_map/ppermute | solution.py:286
  4.0 2.6 %collective-permute-start.1 = (bf16[1,2,18432]{2,1,0:T(2,128)(2,1)S(1)}, bf16[1,2,18432]{2,1,0:T(2,128)(2,1)S(1)}, u32[]{:S(2)}, u32[]{:S(2)}) collective-permute-start(bf16[1,2,18432]{2,1,0:T(2,128)(2,1)S(1)} %maximum_bitcast_fusion.refs_0_), channel_id=1, source_target_pairs={{0,8},{1,9},{2,10},{3,11},{4,12},{5,13},{6,14},{7,15},{8,0},{9,1},... | collective-permute-start | bytes 221192 | tf_op jit(solution)/shard_map/ppermute | solution.py:286
  6.6 1.6 %copy-done = bf16[4096,256]{1,0:T(8,128)(2,1)S(1)} copy-done((bf16[4096,256]{1,0:T(8,128)(2,1)S(1)}, bf16[4096,256]{1,0:T(8,128)(2,1)}, u32[]{:S(2)}) %copy-start) | copy-done | bytes 2097176
  9.3 2.5 %collective-permute-done.1.refs_2_ = bf16[1,2,18432]{2,1,0:T(2,128)(2,1)S(1)} collective-permute-done((bf16[1,2,18432]{2,1,0:T(2,128)(2,1)S(1)}, bf16[1,2,18432]{2,1,0:T(2,128)(2,1)S(1)}, u32[]{:S(2)}, u32[]{:S(2)}) %collective-permute-start.1) | collective-permute-done | bytes 73760 | tf_op jit(solution)/shard_map/ppermute | solution.py:286
  12.9 1.6 %collective-permute-start.4 = (bf16[4,2,4096]{2,1,0:T(2,128)(2,1)S(1)}, bf16[4,2,4096]{2,1,0:T(2,128)(2,1)S(1)}, u32[]{:S(2)}, u32[]{:S(2)}) collective-permute-start(bf16[4,2,4096]{2,1,0:T(2,128)(2,1)S(1)} %get-tuple-element.64), channel_id=1, source_target_pairs={{0,2},{1,3},{2,0},{3,1},{4,6},{5,7},{6,4},{7,5},{8,10},{9,11},{10,... | collective-permute-start | bytes 196616 | tf_op jit(solution)/shard_map/ppermute | solution.py:311
  15.1 2.9 %collective-permute-done.4 = bf16[4,2,4096]{2,1,0:T(2,128)(2,1)S(1)} collective-permute-done((bf16[4,2,4096]{2,1,0:T(2,128)(2,1)S(1)}, bf16[4,2,4096]{2,1,0:T(2,128)(2,1)S(1)}, u32[]{:S(2)}, u32[]{:S(2)}) %collective-permute-start.4) | collective-permute-done | bytes 65568 | tf_op jit(solution)/shard_map/ppermute | solution.py:311
  18.3 1.2 %collective-permute-done.5.far_ref = bf16[8,2,4096]{2,1,0:T(2,128)(2,1)S(1)} collective-permute-done((bf16[8,2,4096]{2,1,0:T(2,128)(2,1)S(1)}, bf16[8,2,4096]{2,1,0:T(2,128)(2,1)S(1)}, u32[]{:S(2)}, u32[]{:S(2)}) %collective-permute-start.5) | collective-permute-done | bytes 131104 | tf_op jit(solution)/shard_map/ppermute | solution.py:48
  19.4 1.2 %rotate_in.1 = bf16[8,32,256]{2,1,0:T(8,128)(2,1)} custom-call(bf16[8,2,4096]{2,1,0:T(2,128)(2,1)S(1)} %constant_dynamic-update-slice_fusion.near_ref, bf16[8,2,4096]{2,1,0:T(2,128)(2,1)S(1)} %collective-permute-done.5.far_ref, bf16[4096,256]{1,0:T(8,128)(2,1)S(1)} %keep.1.basis_ref), custom_call_target="tpu_custom_call" | custom-call | flops 1 | bytes 1 | tf_op jit(solution)/shard_map/rotate_in/pallas_call | solution.py:314
  23.1 4.3 %all-to-all-start = ((bf16[8,32,256]{2,1,0:T(8,128)(2,1)}), bf16[8,32,256]{2,1,0:T(8,128)(2,1)S(1)}, u32[]{:S(2)}, u32[]{:S(2)}) async-start(bf16[8,32,256]{2,1,0:T(8,128)(2,1)} %rotate_in.1), calls=%async_computation | async-start | bytes 262144 | tf_op jit(solution)/shard_map/all_to_all | solution.py:44
  27.4 4.2 %rotate_first.1.start_ref = f32[32,896]{1,0:T(8,128)S(1)} custom-call(bf16[8,2,14336]{2,1,0:T(2,128)(2,1)S(1)} %constant_dynamic-update-slice_fusion.2.near_ref, bf16[8,2,14336]{2,1,0:T(2,128)(2,1)S(1)} %collective-permute-done.6.far_ref, bf16[14336,896]{1,0:T(8,128)(2,1)} %basis_out_ref.1), custom_call_target="tpu_custom_call" | custom-call | flops 1 | bytes 1 | tf_op jit(solution)/shard_map/rotate_first/pallas_call | solution.py:331
  31.7 2.1 %collective-permute-start.10 = (bf16[256,512]{1,0:T(8,128)(2,1)S(1)}, bf16[256,512]{1,0:T(8,128)(2,1)S(1)}, u32[]{:S(2)}, u32[]{:S(2)}) collective-permute-start(bf16[256,512]{1,0:T(8,128)(2,1)S(1)} %collective-permute-done.7.refs_2_), channel_id=1, source_target_pairs={{0,4},{1,5},{4,8},{5,9},{8,12},{9,13},{12,14},{13,15},{14,10},{15,... | collective-permute-start | bytes 786440 | tf_op jit(solution)/shard_map/ppermute | solution.py:278
  35.2 6.6 %rotate_last.1.aligned_ref = bf16[896,32]{1,0:T(8,128)(2,1)S(1)} custom-call(bf16[8,2,14336]{2,1,0:T(2,128)(2,1)S(1)} %constant_dynamic-update-slice_fusion.2.near_ref, bf16[8,2,14336]{2,1,0:T(2,128)(2,1)S(1)} %collective-permute-done.6.far_ref, bf16[14336,896]{1,0:T(8,128)(2,1)} %basis_out_ref.1, s32[16]{0:T(128)S(1)} %copy-done.2, ...), custom_call_target="tpu_custom_call" | custom-call | flops 1 | bytes 1 | tf_op jit(solution)/shard_map/rotate_last/pallas_call | solution.py:331
  41.8 1.3 %collective-permute-start.15 = (bf16[256,512]{1,0:T(8,128)(2,1)S(1)}, bf16[256,512]{1,0:T(8,128)(2,1)S(1)}, u32[]{:S(2)}, u32[]{:S(2)}) collective-permute-start(bf16[256,512]{1,0:T(8,128)(2,1)S(1)} %collective-permute-done.10.refs_6_), channel_id=1, source_target_pairs={{0,4},{1,5},{4,8},{5,9},{8,12},{9,13},{12,14},{13,15},{14,10},{15,... | collective-permute-start | bytes 786440 | tf_op jit(solution)/shard_map/ppermute | solution.py:278
  44.4 6.2 %scale.1.scaled_ref = bf16[896,4096]{1,0:T(8,128)(2,1)S(1)} custom-call(bf16[896,32]{1,0:T(8,128)(2,1)S(1)} %rotate_last.1.aligned_ref, bf16[8,32,256]{2,1,0:T(8,128)(2,1)S(1)} %all-to-all-done.near_ref, bf16[8,32,256]{2,1,0:T(8,128)(2,1)S(1)} %collective-permute-done.12.far_ref, s32[32]{0:T(128)S(1)} %copy-done.1, f32[896,4096]{1,0:T(8,128)} %eigen_ref.1), custom_call_target="tpu_custom_call" | custom-call | flops 1 | bytes 1 | tf_op jit(solution)/shard_map/scale/pallas_call | solution.py:383
  51.9 1.5 %collective-permute-start.21 = (bf16[128,512]{1,0:T(8,128)(2,1)S(1)}, bf16[128,512]{1,0:T(8,128)(2,1)S(1)}, u32[]{:S(2)}, u32[]{:S(2)}) collective-permute-start(bf16[128,512]{1,0:T(8,128)(2,1)S(1)} %slice.10), channel_id=1, source_target_pairs={{0,4},{1,5},{4,8},{5,9},{8,12},{9,13},{12,14},{13,15},{14,10},{15,... | collective-permute-start | bytes 393224 | tf_op jit(solution)/shard_map/ppermute | solution.py:278
  54.0 3.9 %project.1 = (f32[896,512]{1,0:T(8,128)S(1)}, bf16[768,896]{1,0:T(8,128)(2,1)S(1)}) custom-call(bf16[896,4096]{1,0:T(8,128)(2,1)S(1)} %scale.1.scaled_ref, bf16[14336,896]{1,0:T(8,128)(2,1)} %basis_out_ref.1, bf16[256,512]{1,0:T(8,128)(2,1)S(1)} %bitcast.6, bf16[256,512]{1,0:T(8,128)(2,1)S(1)} %collective-permute-done.9.refs_1_, ...), custom_call_target="tpu_custom_call" | custom-call | flops 1 | bytes 1 | tf_op jit(solution)/shard_map/project/pallas_call | solution.py:406
  60.2 1.6 %window.1 = (bf16[8,48,512]{2,1,0:T(8,128)(2,1)S(1)}, f32[8,48,512]{2,1,0:T(8,128)S(1)}) custom-call(bf16[768,896]{1,0:T(8,128)(2,1)S(1)} %get-tuple-element.90.window_ref, bf16[896,4096]{1,0:T(8,128)(2,1)S(1)} %scale.1.scaled_ref, f32[896,512]{1,0:T(8,128)S(1)} %get-tuple-element.92.projected_ref, bf16[128,512]{1,0:T(8,128)(2,1)S(1)} %collective-permute-done.21.refs_0_, ...), custom_call_target="tpu_custom_call" | custom-call | flops 1 | bytes 1 | tf_op jit(solution)/shard_map/window/pallas_call | solution.py:426
  62.2 1.4 %collective-permute-done.25.got_ref = bf16[8,48,512]{2,1,0:T(8,128)(2,1)S(1)} collective-permute-done((bf16[8,48,512]{2,1,0:T(8,128)(2,1)S(1)}, bf16[8,48,512]{2,1,0:T(8,128)(2,1)S(1)}, u32[]{:S(2)}, u32[]{:S(2)}) %collective-permute-start.25) | collective-permute-done | bytes 393248 | tf_op jit(solution)/shard_map/ppermute | solution.py:48
  63.7 1.5 %collective-permute-start.26 = (bf16[48,512]{1,0:T(8,128)(2,1)S(1)}, bf16[48,512]{1,0:T(8,128)(2,1)S(1)}, u32[]{:S(2)}, u32[]{:S(2)}) collective-permute-start(bf16[48,512]{1,0:T(8,128)(2,1)S(1)} %get-tuple-element.98), channel_id=1, source_target_pairs={{0,4},{1,5},{2,6},{3,7},{4,0},{5,1},{6,2},{7,3},{8,12},{9,13},{10,... | collective-permute-start | bytes 147464 | tf_op jit(solution)/shard_map/ppermute | solution.py:451
  65.2 1.8 %collective-permute-start.27 = (bf16[48,512]{1,0:T(8,128)(2,1)S(1)}, bf16[48,512]{1,0:T(8,128)(2,1)S(1)}, u32[]{:S(2)}, u32[]{:S(2)}) collective-permute-start(bf16[48,512]{1,0:T(8,128)(2,1)S(1)} %get-tuple-element.99), channel_id=1, source_target_pairs={{0,8},{1,9},{2,10},{3,11},{4,12},{5,13},{6,14},{7,15},{8,0},{9,1},... | collective-permute-start | bytes 147464 | tf_op jit(solution)/shard_map/ppermute | solution.py:451
  68.7 1.5 %collective-permute-start.30 = (bf16[48,512]{1,0:T(8,128)(2,1)S(1)}, bf16[48,512]{1,0:T(8,128)(2,1)S(1)}, u32[]{:S(2)}, u32[]{:S(2)}) collective-permute-start(bf16[48,512]{1,0:T(8,128)(2,1)S(1)} %get-tuple-element.102), channel_id=1, source_target_pairs={{0,6},{1,7},{2,4},{3,5},{4,2},{5,3},{6,0},{7,1},{8,14},{9,15},{10,... | collective-permute-start | bytes 147464 | tf_op jit(solution)/shard_map/ppermute | solution.py:451
  70.1 2.7 %collective-permute-start.31 = (bf16[48,512]{1,0:T(8,128)(2,1)S(1)}, bf16[48,512]{1,0:T(8,128)(2,1)S(1)}, u32[]{:S(2)}, u32[]{:S(2)}) collective-permute-start(bf16[48,512]{1,0:T(8,128)(2,1)S(1)} %get-tuple-element.103), channel_id=1, source_target_pairs={{0,10},{1,11},{2,8},{3,9},{4,14},{5,15},{6,12},{7,13},{8,2},{9,3},... | collective-permute-start | bytes 147464 | tf_op jit(solution)/shard_map/ppermute | solution.py:451
  72.8 2.1 %collective-permute-start.32 = (bf16[48,512]{1,0:T(8,128)(2,1)S(1)}, bf16[48,512]{1,0:T(8,128)(2,1)S(1)}, u32[]{:S(2)}, u32[]{:S(2)}) collective-permute-start(bf16[48,512]{1,0:T(8,128)(2,1)S(1)} %get-tuple-element.104), channel_id=1, source_target_pairs={{0,14},{1,15},{2,12},{3,13},{4,10},{5,11},{6,8},{7,9},{8,6},{9,7},... | collective-permute-start | bytes 147464 | tf_op jit(solution)/shard_map/ppermute | solution.py:451
  76.0 3.6 %collective-permute-done.32.refs_6_ = bf16[48,512]{1,0:T(8,128)(2,1)S(1)} collective-permute-done((bf16[48,512]{1,0:T(8,128)(2,1)S(1)}, bf16[48,512]{1,0:T(8,128)(2,1)S(1)}, u32[]{:S(2)}, u32[]{:S(2)}) %collective-permute-start.32) | collective-permute-done | bytes 49184 | tf_op jit(solution)/shard_map/ppermute | solution.py:451
  (70 shorter events, 17.4 us)
Async XLA Ops:
  0.9 8.4 %collective-permute-start = (bf16[1,2,18432]{2,1,0:T(2,128)(2,1)S(1)}, bf16[1,2,18432]{2,1,0:T(2,128)(2,1)S(1)}, u32[]{:S(2)}, u32[]{:S(2)}) collective-permute-start(bf16[1,2,18432]{2,1,0:T(2,128)(2,1)S(1)} %maximum_bitcast_fusion.refs_0_), channel_id=1, source_target_pairs={{0,4},{1,5},{2,6},{3,7},{4,0},{5,1},{6,2},{7,3},{8,12},{9,13},{10,... | collective-permute-start | bytes 221192 | tf_op jit(solution)/shard_map/ppermute | solution.py:286
  4.0 7.8 %collective-permute-start.1 = (bf16[1,2,18432]{2,1,0:T(2,128)(2,1)S(1)}, bf16[1,2,18432]{2,1,0:T(2,128)(2,1)S(1)}, u32[]{:S(2)}, u32[]{:S(2)}) collective-permute-start(bf16[1,2,18432]{2,1,0:T(2,128)(2,1)S(1)} %maximum_bitcast_fusion.refs_0_), channel_id=1, source_target_pairs={{0,8},{1,9},{2,10},{3,11},{4,12},{5,13},{6,14},{7,15},{8,0},{9,1},... | collective-permute-start | bytes 221192 | tf_op jit(solution)/shard_map/ppermute | solution.py:286
  6.6 6.3 %collective-permute-start.2 = (bf16[1,2,18432]{2,1,0:T(2,128)(2,1)S(1)}, bf16[1,2,18432]{2,1,0:T(2,128)(2,1)S(1)}, u32[]{:S(2)}, u32[]{:S(2)}) collective-permute-start(bf16[1,2,18432]{2,1,0:T(2,128)(2,1)S(1)} %maximum_bitcast_fusion.refs_0_), channel_id=1, source_target_pairs={{0,12},{1,13},{2,14},{3,15},{4,8},{5,9},{6,10},{7,11},{8,4},{9,5},... | collective-permute-start | bytes 221192 | tf_op jit(solution)/shard_map/ppermute | solution.py:286
  14.5 6.2 %collective-permute-start.3 = (bf16[4,2,14336]{2,1,0:T(2,128)(2,1)S(1)}, bf16[4,2,14336]{2,1,0:T(2,128)(2,1)S(1)}, u32[]{:S(2)}, u32[]{:S(2)}) collective-permute-start(bf16[4,2,14336]{2,1,0:T(2,128)(2,1)S(1)} %get-tuple-element.62), channel_id=1, source_target_pairs={{0,2},{1,3},{2,0},{3,1},{4,6},{5,7},{6,4},{7,5},{8,10},{9,11},{10,... | collective-permute-start | bytes 688136 | tf_op jit(solution)/shard_map/ppermute | solution.py:312
  20.8 6.6 %collective-permute-start.6 = (bf16[8,2,14336]{2,1,0:T(2,128)(2,1)S(1)}, bf16[8,2,14336]{2,1,0:T(2,128)(2,1)S(1)}, u32[]{:S(2)}, u32[]{:S(2)}) collective-permute-start(bf16[8,2,14336]{2,1,0:T(2,128)(2,1)S(1)} %constant_dynamic-update-slice_fusion.2.near_ref), channel_id=1, source_target_pairs={{0,1},{1,0},{2,3},{3,2},{4,5},{5,4},{6,7},{7,6},{8,9},{9,8},{10,11... | collective-permute-start | bytes 1376264 | tf_op jit(solution)/shard_map/ppermute | solution.py:48
  21.1 10.6 %collective-permute-start.7 = (bf16[256,512]{1,0:T(8,128)(2,1)S(1)}, bf16[256,512]{1,0:T(8,128)(2,1)S(1)}, u32[]{:S(2)}, u32[]{:S(2)}) collective-permute-start(bf16[256,512]{1,0:T(8,128)(2,1)S(1)} %bitcast.3), channel_id=1, source_target_pairs={{0,4},{1,5},{4,8},{5,9},{8,12},{9,13},{12,14},{13,15},{14,10},{15,... | collective-permute-start | bytes 786440 | tf_op jit(solution)/shard_map/ppermute | solution.py:278
  22.2 9.5 %collective-permute-start.8 = (bf16[256,512]{1,0:T(8,128)(2,1)S(1)}, bf16[256,512]{1,0:T(8,128)(2,1)S(1)}, u32[]{:S(2)}, u32[]{:S(2)}) collective-permute-start(bf16[256,512]{1,0:T(8,128)(2,1)S(1)} %bitcast.4), channel_id=1, source_target_pairs={{0,2},{1,3},{4,0},{5,1},{8,4},{9,5},{12,8},{13,9},{14,12},{15,13},... | collective-permute-start | bytes 786440 | tf_op jit(solution)/shard_map/ppermute | solution.py:279
  23.1 8.5 %collective-permute-start.9 = (bf16[256,512]{1,0:T(8,128)(2,1)S(1)}, bf16[256,512]{1,0:T(8,128)(2,1)S(1)}, u32[]{:S(2)}, u32[]{:S(2)}) collective-permute-start(bf16[256,512]{1,0:T(8,128)(2,1)S(1)} %bitcast.5), channel_id=1, source_target_pairs={{0,1},{1,0},{2,3},{3,2},{4,5},{5,4},{6,7},{7,6},{8,9},{9,8},{10,11... | collective-permute-start | bytes 786440 | tf_op jit(solution)/shard_map/ppermute | solution.py:48
  23.1 12.1 %all-to-all-start = ((bf16[8,32,256]{2,1,0:T(8,128)(2,1)}), bf16[8,32,256]{2,1,0:T(8,128)(2,1)S(1)}, u32[]{:S(2)}, u32[]{:S(2)}) async-start(bf16[8,32,256]{2,1,0:T(8,128)(2,1)} %rotate_in.1), calls=%async_computation | async-start | bytes 262144 | tf_op jit(solution)/shard_map/all_to_all | solution.py:44
  31.7 10.1 %collective-permute-start.10 = (bf16[256,512]{1,0:T(8,128)(2,1)S(1)}, bf16[256,512]{1,0:T(8,128)(2,1)S(1)}, u32[]{:S(2)}, u32[]{:S(2)}) collective-permute-start(bf16[256,512]{1,0:T(8,128)(2,1)S(1)} %collective-permute-done.7.refs_2_), channel_id=1, source_target_pairs={{0,4},{1,5},{4,8},{5,9},{8,12},{9,13},{12,14},{13,15},{14,10},{15,... | collective-permute-start | bytes 786440 | tf_op jit(solution)/shard_map/ppermute | solution.py:278
  33.7 8.1 %collective-permute-start.11 = (bf16[256,512]{1,0:T(8,128)(2,1)S(1)}, bf16[256,512]{1,0:T(8,128)(2,1)S(1)}, u32[]{:S(2)}, u32[]{:S(2)}) collective-permute-start(bf16[256,512]{1,0:T(8,128)(2,1)S(1)} %collective-permute-done.8.refs_4_), channel_id=1, source_target_pairs={{0,2},{1,3},{4,0},{5,1},{8,4},{9,5},{12,8},{13,9},{14,12},{15,13},... | collective-permute-start | bytes 786440 | tf_op jit(solution)/shard_map/ppermute | solution.py:279
  33.8 8.0 %collective-permute-start.13 = (bf16[256,512]{1,0:T(8,128)(2,1)S(1)}, bf16[256,512]{1,0:T(8,128)(2,1)S(1)}, u32[]{:S(2)}, u32[]{:S(2)}) collective-permute-start(bf16[256,512]{1,0:T(8,128)(2,1)S(1)} %collective-permute-done.7.refs_2_), channel_id=1, source_target_pairs={{0,1},{1,0},{2,3},{3,2},{4,5},{5,4},{6,7},{7,6},{8,9},{9,8},{10,11... | collective-permute-start | bytes 786440 | tf_op jit(solution)/shard_map/ppermute | solution.py:48
  33.8 8.0 %collective-permute-start.14 = (bf16[256,512]{1,0:T(8,128)(2,1)S(1)}, bf16[256,512]{1,0:T(8,128)(2,1)S(1)}, u32[]{:S(2)}, u32[]{:S(2)}) collective-permute-start(bf16[256,512]{1,0:T(8,128)(2,1)S(1)} %collective-permute-done.8.refs_4_), channel_id=1, source_target_pairs={{0,1},{1,0},{2,3},{3,2},{4,5},{5,4},{6,7},{7,6},{8,9},{9,8},{10,11... | collective-permute-start | bytes 786440 | tf_op jit(solution)/shard_map/ppermute | solution.py:48
  35.2 6.6 %collective-permute-start.12 = (bf16[8,32,256]{2,1,0:T(8,128)(2,1)S(1)}, bf16[8,32,256]{2,1,0:T(8,128)(2,1)S(1)}, u32[]{:S(2)}, u32[]{:S(2)}) collective-permute-start(bf16[8,32,256]{2,1,0:T(8,128)(2,1)S(1)} %all-to-all-done.near_ref), channel_id=1, source_target_pairs={{0,1},{1,0},{2,3},{3,2},{4,5},{5,4},{6,7},{7,6},{8,9},{9,8},{10,11... | collective-permute-start | bytes 393224 | tf_op jit(solution)/shard_map/ppermute | solution.py:48
  41.8 8.8 %collective-permute-start.15 = (bf16[256,512]{1,0:T(8,128)(2,1)S(1)}, bf16[256,512]{1,0:T(8,128)(2,1)S(1)}, u32[]{:S(2)}, u32[]{:S(2)}) collective-permute-start(bf16[256,512]{1,0:T(8,128)(2,1)S(1)} %collective-permute-done.10.refs_6_), channel_id=1, source_target_pairs={{0,4},{1,5},{4,8},{5,9},{8,12},{9,13},{12,14},{13,15},{14,10},{15,... | collective-permute-start | bytes 786440 | tf_op jit(solution)/shard_map/ppermute | solution.py:278
  43.1 8.3 %collective-permute-start.16 = (bf16[256,512]{1,0:T(8,128)(2,1)S(1)}, bf16[256,512]{1,0:T(8,128)(2,1)S(1)}, u32[]{:S(2)}, u32[]{:S(2)}) collective-permute-start(bf16[256,512]{1,0:T(8,128)(2,1)S(1)} %collective-permute-done.11.refs_8_), channel_id=1, source_target_pairs={{0,2},{1,3},{4,0},{5,1},{8,4},{9,5},{12,8},{13,9},{14,12},{15,13},... | collective-permute-start | bytes 786440 | tf_op jit(solution)/shard_map/ppermute | solution.py:279
  43.9 7.5 %collective-permute-start.17 = (bf16[256,512]{1,0:T(8,128)(2,1)S(1)}, bf16[256,512]{1,0:T(8,128)(2,1)S(1)}, u32[]{:S(2)}, u32[]{:S(2)}) collective-permute-start(bf16[256,512]{1,0:T(8,128)(2,1)S(1)} %collective-permute-done.10.refs_6_), channel_id=1, source_target_pairs={{0,1},{1,0},{2,3},{3,2},{4,5},{5,4},{6,7},{7,6},{8,9},{9,8},{10,11... | collective-permute-start | bytes 786440 | tf_op jit(solution)/shard_map/ppermute | solution.py:48
  43.9 7.5 %collective-permute-start.18 = (bf16[256,512]{1,0:T(8,128)(2,1)S(1)}, bf16[256,512]{1,0:T(8,128)(2,1)S(1)}, u32[]{:S(2)}, u32[]{:S(2)}) collective-permute-start(bf16[256,512]{1,0:T(8,128)(2,1)S(1)} %collective-permute-done.11.refs_8_), channel_id=1, source_target_pairs={{0,1},{1,0},{2,3},{3,2},{4,5},{5,4},{6,7},{7,6},{8,9},{9,8},{10,11... | collective-permute-start | bytes 786440 | tf_op jit(solution)/shard_map/ppermute | solution.py:48
  63.7 6.5 %collective-permute-start.26 = (bf16[48,512]{1,0:T(8,128)(2,1)S(1)}, bf16[48,512]{1,0:T(8,128)(2,1)S(1)}, u32[]{:S(2)}, u32[]{:S(2)}) collective-permute-start(bf16[48,512]{1,0:T(8,128)(2,1)S(1)} %get-tuple-element.98), channel_id=1, source_target_pairs={{0,4},{1,5},{2,6},{3,7},{4,0},{5,1},{6,2},{7,3},{8,12},{9,13},{10,... | collective-permute-start | bytes 147464 | tf_op jit(solution)/shard_map/ppermute | solution.py:451
  65.2 7.6 %collective-permute-start.27 = (bf16[48,512]{1,0:T(8,128)(2,1)S(1)}, bf16[48,512]{1,0:T(8,128)(2,1)S(1)}, u32[]{:S(2)}, u32[]{:S(2)}) collective-permute-start(bf16[48,512]{1,0:T(8,128)(2,1)S(1)} %get-tuple-element.99), channel_id=1, source_target_pairs={{0,8},{1,9},{2,10},{3,11},{4,12},{5,13},{6,14},{7,15},{8,0},{9,1},... | collective-permute-start | bytes 147464 | tf_op jit(solution)/shard_map/ppermute | solution.py:451
  67.0 7.9 %collective-permute-start.28 = (bf16[48,512]{1,0:T(8,128)(2,1)S(1)}, bf16[48,512]{1,0:T(8,128)(2,1)S(1)}, u32[]{:S(2)}, u32[]{:S(2)}) collective-permute-start(bf16[48,512]{1,0:T(8,128)(2,1)S(1)} %get-tuple-element.100), channel_id=1, source_target_pairs={{0,12},{1,13},{2,14},{3,15},{4,8},{5,9},{6,10},{7,11},{8,4},{9,5},... | collective-permute-start | bytes 147464 | tf_op jit(solution)/shard_map/ppermute | solution.py:451
  68.1 6.8 %collective-permute-start.29 = (bf16[48,512]{1,0:T(8,128)(2,1)S(1)}, bf16[48,512]{1,0:T(8,128)(2,1)S(1)}, u32[]{:S(2)}, u32[]{:S(2)}) collective-permute-start(bf16[48,512]{1,0:T(8,128)(2,1)S(1)} %get-tuple-element.101), channel_id=1, source_target_pairs={{0,2},{1,3},{2,0},{3,1},{4,6},{5,7},{6,4},{7,5},{8,10},{9,11},{10,... | collective-permute-start | bytes 147464 | tf_op jit(solution)/shard_map/ppermute | solution.py:451
  68.7 6.2 %collective-permute-start.30 = (bf16[48,512]{1,0:T(8,128)(2,1)S(1)}, bf16[48,512]{1,0:T(8,128)(2,1)S(1)}, u32[]{:S(2)}, u32[]{:S(2)}) collective-permute-start(bf16[48,512]{1,0:T(8,128)(2,1)S(1)} %get-tuple-element.102), channel_id=1, source_target_pairs={{0,6},{1,7},{2,4},{3,5},{4,2},{5,3},{6,0},{7,1},{8,14},{9,15},{10,... | collective-permute-start | bytes 147464 | tf_op jit(solution)/shard_map/ppermute | solution.py:451
  72.8 6.8 %collective-permute-start.32 = (bf16[48,512]{1,0:T(8,128)(2,1)S(1)}, bf16[48,512]{1,0:T(8,128)(2,1)S(1)}, u32[]{:S(2)}, u32[]{:S(2)}) collective-permute-start(bf16[48,512]{1,0:T(8,128)(2,1)S(1)} %get-tuple-element.104), channel_id=1, source_target_pairs={{0,14},{1,15},{2,12},{3,13},{4,10},{5,11},{6,8},{7,9},{8,6},{9,7},... | collective-permute-start | bytes 147464 | tf_op jit(solution)/shard_map/ppermute | solution.py:451
  (14 other events, 56.6 us)

commit v24 on v21

--- a/solution.py
+++ b/solution.py
@@ -436,7 +436,7 @@
         name="window",
     )(window, scaled, projected, *last)
 
-    keys = [*range(chips - 2, 0, -2), *range(chips - 1, 0, -2)]
+    keys = [*range(chips - 1, 0, -2), *range(chips - 2, 0, -2)]
     small = pltpu.CompilerParams(vmem_limit_bytes=8 * MIB)
     own, *sends = pl.pallas_call(
         functools.partial(add_core_kernel, keys),

time: 78.6 us -> 79.2 us (level)
  transfers between devices with their start and end apart: 34 -> 34, of which waited for: 13 -> 12; matrix products, arithmetic and copies ran while one was open for 1% -> 1% of each run, Pallas kernels for 28% -> 28%
where the time goes in v24:
time: 79.2 us; the launch traced here: 78.8 us
  starting transfers between devices  34.4 us (43%)
  Pallas kernels  24.6 us (31%)
  waiting for transfers between devices  15.6 us (20%)
  local copies, waits for them, and re-layouts  3.02 us (4%)
  other arithmetic  0.91 us (1%)
    ppermute x7, starting transfers between devices, ring_body(): lax.ppermute(x, 'blk', xor_pairs(n, 2 * key))  11.2 us
    pallas_call x2, Pallas kernels, ring_body(): pl.pallas_call(kernel, out_shape=jax.ShapeDtypeStruct(shape, dtype), in_s...  10.7 us
    pallas_call x1, Pallas kernels, ring_body(): pl.pallas_call(functools.partial(scale_kernel, begun), out_shape=jax.Shap...  6.19 us
    ppermute x4, starting transfers between devices, ring_body(): to_right = lambda x: lax.ppermute(x, 'blk', shift_pairs(n, 1))  5.95 us
    ppermute x3, starting transfers between devices, ring_body(): lax.ppermute(both, 'blk', xor_pairs(n, 4 * key))  5.68 us
    all_to_all x1, starting transfers between devices, exchange(): return lax.all_to_all(x, 'blk', 0, 0, axis_index_groups=groups, tiled=True)  4.33 us
    pallas_call x1, Pallas kernels, ring_body(): pl.pallas_call(functools.partial(project_kernel, (0, 6, len(pieces))), ou...  3.92 us
    ppermute x13, waiting for transfers between devices, swap(): return lax.ppermute(x, 'blk', xor_pairs(n, 1))  3.59 us
  transfers between devices with their start and end apart: 34, of which 12 were waited for; matrix products, arithmetic and copies ran while one was open for 1% of the time, Pallas kernels for 28%

profile of v24, /device:TPU:0, one launch (start us, length us, event | category | flops | bytes accessed | tf_op | source)
XLA Modules:
  0.0 78.8 jit_solution(8948254193398456228)
XLA Ops:
  0.9 3.1 %collective-permute-start = (bf16[1,2,18432]{2,1,0:T(2,128)(2,1)S(1)}, bf16[1,2,18432]{2,1,0:T(2,128)(2,1)S(1)}, u32[]{:S(2)}, u32[]{:S(2)}) collective-permute-start(bf16[1,2,18432]{2,1,0:T(2,128)(2,1)S(1)} %maximum_bitcast_fusion.refs_0_), channel_id=1, source_target_pairs={{0,4},{1,5},{2,6},{3,7},{4,0},{5,1},{6,2},{7,3},{8,12},{9,13},{10,... | collective-permute-start | bytes 221192 | tf_op jit(solution)/shard_map/ppermute | solution.py:286
  4.0 2.6 %collective-permute-start.1 = (bf16[1,2,18432]{2,1,0:T(2,128)(2,1)S(1)}, bf16[1,2,18432]{2,1,0:T(2,128)(2,1)S(1)}, u32[]{:S(2)}, u32[]{:S(2)}) collective-permute-start(bf16[1,2,18432]{2,1,0:T(2,128)(2,1)S(1)} %maximum_bitcast_fusion.refs_0_), channel_id=1, source_target_pairs={{0,8},{1,9},{2,10},{3,11},{4,12},{5,13},{6,14},{7,15},{8,0},{9,1},... | collective-permute-start | bytes 221192 | tf_op jit(solution)/shard_map/ppermute | solution.py:286
  6.6 1.6 %copy-done = bf16[4096,256]{1,0:T(8,128)(2,1)S(1)} copy-done((bf16[4096,256]{1,0:T(8,128)(2,1)S(1)}, bf16[4096,256]{1,0:T(8,128)(2,1)}, u32[]{:S(2)}) %copy-start) | copy-done | bytes 2097176
  9.3 2.5 %collective-permute-done.1.refs_2_ = bf16[1,2,18432]{2,1,0:T(2,128)(2,1)S(1)} collective-permute-done((bf16[1,2,18432]{2,1,0:T(2,128)(2,1)S(1)}, bf16[1,2,18432]{2,1,0:T(2,128)(2,1)S(1)}, u32[]{:S(2)}, u32[]{:S(2)}) %collective-permute-start.1) | collective-permute-done | bytes 73760 | tf_op jit(solution)/shard_map/ppermute | solution.py:286
  12.9 1.6 %collective-permute-start.4 = (bf16[4,2,4096]{2,1,0:T(2,128)(2,1)S(1)}, bf16[4,2,4096]{2,1,0:T(2,128)(2,1)S(1)}, u32[]{:S(2)}, u32[]{:S(2)}) collective-permute-start(bf16[4,2,4096]{2,1,0:T(2,128)(2,1)S(1)} %get-tuple-element.64), channel_id=1, source_target_pairs={{0,2},{1,3},{2,0},{3,1},{4,6},{5,7},{6,4},{7,5},{8,10},{9,11},{10,... | collective-permute-start | bytes 196616 | tf_op jit(solution)/shard_map/ppermute | solution.py:310
  15.1 2.9 %collective-permute-done.4 = bf16[4,2,4096]{2,1,0:T(2,128)(2,1)S(1)} collective-permute-done((bf16[4,2,4096]{2,1,0:T(2,128)(2,1)S(1)}, bf16[4,2,4096]{2,1,0:T(2,128)(2,1)S(1)}, u32[]{:S(2)}, u32[]{:S(2)}) %collective-permute-start.4) | collective-permute-done | bytes 65568 | tf_op jit(solution)/shard_map/ppermute | solution.py:310
  19.4 1.2 %rotate_in.1 = bf16[8,32,256]{2,1,0:T(8,128)(2,1)} custom-call(bf16[8,2,4096]{2,1,0:T(2,128)(2,1)S(1)} %constant_dynamic-update-slice_fusion.near_ref, bf16[8,2,4096]{2,1,0:T(2,128)(2,1)S(1)} %collective-permute-done.5.far_ref, bf16[4096,256]{1,0:T(8,128)(2,1)S(1)} %keep.1.basis_ref), custom_call_target="tpu_custom_call" | custom-call | flops 1 | bytes 1 | tf_op jit(solution)/shard_map/rotate_in/pallas_call | solution.py:313
  23.1 4.3 %all-to-all-start = ((bf16[8,32,256]{2,1,0:T(8,128)(2,1)}), bf16[8,32,256]{2,1,0:T(8,128)(2,1)S(1)}, u32[]{:S(2)}, u32[]{:S(2)}) async-start(bf16[8,32,256]{2,1,0:T(8,128)(2,1)} %rotate_in.1), calls=%async_computation | async-start | bytes 262144 | tf_op jit(solution)/shard_map/all_to_all | solution.py:44
  27.4 4.2 %rotate_first.1.start_ref = f32[32,896]{1,0:T(8,128)S(1)} custom-call(bf16[8,2,14336]{2,1,0:T(2,128)(2,1)S(1)} %constant_dynamic-update-slice_fusion.2.near_ref, bf16[8,2,14336]{2,1,0:T(2,128)(2,1)S(1)} %collective-permute-done.6.far_ref, bf16[14336,896]{1,0:T(8,128)(2,1)} %basis_out_ref.1), custom_call_target="tpu_custom_call" | custom-call | flops 1 | bytes 1 | tf_op jit(solution)/shard_map/rotate_first/pallas_call | solution.py:330
  31.7 2.1 %collective-permute-start.10 = (bf16[256,512]{1,0:T(8,128)(2,1)S(1)}, bf16[256,512]{1,0:T(8,128)(2,1)S(1)}, u32[]{:S(2)}, u32[]{:S(2)}) collective-permute-start(bf16[256,512]{1,0:T(8,128)(2,1)S(1)} %collective-permute-done.7.refs_2_), channel_id=1, source_target_pairs={{0,4},{1,5},{4,8},{5,9},{8,12},{9,13},{12,14},{13,15},{14,10},{15,... | collective-permute-start | bytes 786440 | tf_op jit(solution)/shard_map/ppermute | solution.py:278
  35.2 6.6 %rotate_last.1.aligned_ref = bf16[896,32]{1,0:T(8,128)(2,1)S(1)} custom-call(bf16[8,2,14336]{2,1,0:T(2,128)(2,1)S(1)} %constant_dynamic-update-slice_fusion.2.near_ref, bf16[8,2,14336]{2,1,0:T(2,128)(2,1)S(1)} %collective-permute-done.6.far_ref, bf16[14336,896]{1,0:T(8,128)(2,1)} %basis_out_ref.1, s32[16]{0:T(128)S(1)} %copy-done.2, ...), custom_call_target="tpu_custom_call" | custom-call | flops 1 | bytes 1 | tf_op jit(solution)/shard_map/rotate_last/pallas_call | solution.py:330
  41.8 1.3 %collective-permute-start.15 = (bf16[256,512]{1,0:T(8,128)(2,1)S(1)}, bf16[256,512]{1,0:T(8,128)(2,1)S(1)}, u32[]{:S(2)}, u32[]{:S(2)}) collective-permute-start(bf16[256,512]{1,0:T(8,128)(2,1)S(1)} %collective-permute-done.10.refs_6_), channel_id=1, source_target_pairs={{0,4},{1,5},{4,8},{5,9},{8,12},{9,13},{12,14},{13,15},{14,10},{15,... | collective-permute-start | bytes 786440 | tf_op jit(solution)/shard_map/ppermute | solution.py:278
  44.4 6.2 %scale.1.scaled_ref = bf16[896,4096]{1,0:T(8,128)(2,1)S(1)} custom-call(bf16[896,32]{1,0:T(8,128)(2,1)S(1)} %rotate_last.1.aligned_ref, bf16[8,32,256]{2,1,0:T(8,128)(2,1)S(1)} %all-to-all-done.near_ref, bf16[8,32,256]{2,1,0:T(8,128)(2,1)S(1)} %collective-permute-done.12.far_ref, s32[32]{0:T(128)S(1)} %copy-done.1, f32[896,4096]{1,0:T(8,128)} %eigen_ref.1), custom_call_target="tpu_custom_call" | custom-call | flops 1 | bytes 1 | tf_op jit(solution)/shard_map/scale/pallas_call | solution.py:382
  51.9 1.5 %collective-permute-start.21 = (bf16[128,512]{1,0:T(8,128)(2,1)S(1)}, bf16[128,512]{1,0:T(8,128)(2,1)S(1)}, u32[]{:S(2)}, u32[]{:S(2)}) collective-permute-start(bf16[128,512]{1,0:T(8,128)(2,1)S(1)} %slice.10), channel_id=1, source_target_pairs={{0,4},{1,5},{4,8},{5,9},{8,12},{9,13},{12,14},{13,15},{14,10},{15,... | collective-permute-start | bytes 393224 | tf_op jit(solution)/shard_map/ppermute | solution.py:278
  54.0 3.9 %project.1 = (f32[896,512]{1,0:T(8,128)S(1)}, bf16[768,896]{1,0:T(8,128)(2,1)S(1)}) custom-call(bf16[896,4096]{1,0:T(8,128)(2,1)S(1)} %scale.1.scaled_ref, bf16[14336,896]{1,0:T(8,128)(2,1)} %basis_out_ref.1, bf16[256,512]{1,0:T(8,128)(2,1)S(1)} %bitcast.6, bf16[256,512]{1,0:T(8,128)(2,1)S(1)} %collective-permute-done.9.refs_1_, ...), custom_call_target="tpu_custom_call" | custom-call | flops 1 | bytes 1 | tf_op jit(solution)/shard_map/project/pallas_call | solution.py:405
  60.2 1.6 %window.1 = (bf16[8,48,512]{2,1,0:T(8,128)(2,1)S(1)}, f32[8,48,512]{2,1,0:T(8,128)S(1)}) custom-call(bf16[768,896]{1,0:T(8,128)(2,1)S(1)} %get-tuple-element.90.window_ref, bf16[896,4096]{1,0:T(8,128)(2,1)S(1)} %scale.1.scaled_ref, f32[896,512]{1,0:T(8,128)S(1)} %get-tuple-element.92.projected_ref, bf16[128,512]{1,0:T(8,128)(2,1)S(1)} %collective-permute-done.21.refs_0_, ...), custom_call_target="tpu_custom_call" | custom-call | flops 1 | bytes 1 | tf_op jit(solution)/shard_map/window/pallas_call | solution.py:425
  62.2 1.4 %collective-permute-done.25.got_ref = bf16[8,48,512]{2,1,0:T(8,128)(2,1)S(1)} collective-permute-done((bf16[8,48,512]{2,1,0:T(8,128)(2,1)S(1)}, bf16[8,48,512]{2,1,0:T(8,128)(2,1)S(1)}, u32[]{:S(2)}, u32[]{:S(2)}) %collective-permute-start.25) | collective-permute-done | bytes 393248 | tf_op jit(solution)/shard_map/ppermute | solution.py:48
  63.7 2.7 %collective-permute-start.26 = (bf16[48,512]{1,0:T(8,128)(2,1)S(1)}, bf16[48,512]{1,0:T(8,128)(2,1)S(1)}, u32[]{:S(2)}, u32[]{:S(2)}) collective-permute-start(bf16[48,512]{1,0:T(8,128)(2,1)S(1)} %get-tuple-element.98), channel_id=1, source_target_pairs={{0,14},{1,15},{2,12},{3,13},{4,10},{5,11},{6,8},{7,9},{8,6},{9,7},... | collective-permute-start | bytes 147464 | tf_op jit(solution)/shard_map/ppermute | solution.py:450
  67.6 1.5 %collective-permute-start.28 = (bf16[48,512]{1,0:T(8,128)(2,1)S(1)}, bf16[48,512]{1,0:T(8,128)(2,1)S(1)}, u32[]{:S(2)}, u32[]{:S(2)}) collective-permute-start(bf16[48,512]{1,0:T(8,128)(2,1)S(1)} %get-tuple-element.100), channel_id=1, source_target_pairs={{0,6},{1,7},{2,4},{3,5},{4,2},{5,3},{6,0},{7,1},{8,14},{9,15},{10,... | collective-permute-start | bytes 147464 | tf_op jit(solution)/shard_map/ppermute | solution.py:450
  69.0 1.5 %collective-permute-start.29 = (bf16[48,512]{1,0:T(8,128)(2,1)S(1)}, bf16[48,512]{1,0:T(8,128)(2,1)S(1)}, u32[]{:S(2)}, u32[]{:S(2)}) collective-permute-start(bf16[48,512]{1,0:T(8,128)(2,1)S(1)} %get-tuple-element.101), channel_id=1, source_target_pairs={{0,2},{1,3},{2,0},{3,1},{4,6},{5,7},{6,4},{7,5},{8,10},{9,11},{10,... | collective-permute-start | bytes 147464 | tf_op jit(solution)/shard_map/ppermute | solution.py:450
  70.5 2.7 %collective-permute-start.30 = (bf16[48,512]{1,0:T(8,128)(2,1)S(1)}, bf16[48,512]{1,0:T(8,128)(2,1)S(1)}, u32[]{:S(2)}, u32[]{:S(2)}) collective-permute-start(bf16[48,512]{1,0:T(8,128)(2,1)S(1)} %get-tuple-element.102), channel_id=1, source_target_pairs={{0,12},{1,13},{2,14},{3,15},{4,8},{5,9},{6,10},{7,11},{8,4},{9,5},... | collective-permute-start | bytes 147464 | tf_op jit(solution)/shard_map/ppermute | solution.py:450
  73.2 1.7 %collective-permute-start.32 = (bf16[48,512]{1,0:T(8,128)(2,1)S(1)}, bf16[48,512]{1,0:T(8,128)(2,1)S(1)}, u32[]{:S(2)}, u32[]{:S(2)}) collective-permute-start(bf16[48,512]{1,0:T(8,128)(2,1)S(1)} %get-tuple-element.104), channel_id=1, source_target_pairs={{0,4},{1,5},{2,6},{3,7},{4,0},{5,1},{6,2},{7,3},{8,12},{9,13},{10,... | collective-permute-start | bytes 147464 | tf_op jit(solution)/shard_map/ppermute | solution.py:450
  74.9 1.7 %collective-permute-done.30.refs_4_ = bf16[48,512]{1,0:T(8,128)(2,1)S(1)} collective-permute-done((bf16[48,512]{1,0:T(8,128)(2,1)S(1)}, bf16[48,512]{1,0:T(8,128)(2,1)S(1)}, u32[]{:S(2)}, u32[]{:S(2)}) %collective-permute-start.30) | collective-permute-done | bytes 49184 | tf_op jit(solution)/shard_map/ppermute | solution.py:450
  76.6 1.6 %collective-permute-done.31.refs_5_ = bf16[48,512]{1,0:T(8,128)(2,1)S(1)} collective-permute-done((bf16[48,512]{1,0:T(8,128)(2,1)S(1)}, bf16[48,512]{1,0:T(8,128)(2,1)S(1)}, u32[]{:S(2)}, u32[]{:S(2)}) %collective-permute-start.31) | collective-permute-done | bytes 49184 | tf_op jit(solution)/shard_map/ppermute | solution.py:450
  (70 shorter events, 16.9 us)
Async XLA Ops:
  0.9 8.4 %collective-permute-start = (bf16[1,2,18432]{2,1,0:T(2,128)(2,1)S(1)}, bf16[1,2,18432]{2,1,0:T(2,128)(2,1)S(1)}, u32[]{:S(2)}, u32[]{:S(2)}) collective-permute-start(bf16[1,2,18432]{2,1,0:T(2,128)(2,1)S(1)} %maximum_bitcast_fusion.refs_0_), channel_id=1, source_target_pairs={{0,4},{1,5},{2,6},{3,7},{4,0},{5,1},{6,2},{7,3},{8,12},{9,13},{10,... | collective-permute-start | bytes 221192 | tf_op jit(solution)/shard_map/ppermute | solution.py:286
  4.0 7.8 %collective-permute-start.1 = (bf16[1,2,18432]{2,1,0:T(2,128)(2,1)S(1)}, bf16[1,2,18432]{2,1,0:T(2,128)(2,1)S(1)}, u32[]{:S(2)}, u32[]{:S(2)}) collective-permute-start(bf16[1,2,18432]{2,1,0:T(2,128)(2,1)S(1)} %maximum_bitcast_fusion.refs_0_), channel_id=1, source_target_pairs={{0,8},{1,9},{2,10},{3,11},{4,12},{5,13},{6,14},{7,15},{8,0},{9,1},... | collective-permute-start | bytes 221192 | tf_op jit(solution)/shard_map/ppermute | solution.py:286
  6.6 6.3 %collective-permute-start.2 = (bf16[1,2,18432]{2,1,0:T(2,128)(2,1)S(1)}, bf16[1,2,18432]{2,1,0:T(2,128)(2,1)S(1)}, u32[]{:S(2)}, u32[]{:S(2)}) collective-permute-start(bf16[1,2,18432]{2,1,0:T(2,128)(2,1)S(1)} %maximum_bitcast_fusion.refs_0_), channel_id=1, source_target_pairs={{0,12},{1,13},{2,14},{3,15},{4,8},{5,9},{6,10},{7,11},{8,4},{9,5},... | collective-permute-start | bytes 221192 | tf_op jit(solution)/shard_map/ppermute | solution.py:286
  14.5 6.2 %collective-permute-start.3 = (bf16[4,2,14336]{2,1,0:T(2,128)(2,1)S(1)}, bf16[4,2,14336]{2,1,0:T(2,128)(2,1)S(1)}, u32[]{:S(2)}, u32[]{:S(2)}) collective-permute-start(bf16[4,2,14336]{2,1,0:T(2,128)(2,1)S(1)} %get-tuple-element.62), channel_id=1, source_target_pairs={{0,2},{1,3},{2,0},{3,1},{4,6},{5,7},{6,4},{7,5},{8,10},{9,11},{10,... | collective-permute-start | bytes 688136 | tf_op jit(solution)/shard_map/ppermute | solution.py:311
  20.8 6.6 %collective-permute-start.6 = (bf16[8,2,14336]{2,1,0:T(2,128)(2,1)S(1)}, bf16[8,2,14336]{2,1,0:T(2,128)(2,1)S(1)}, u32[]{:S(2)}, u32[]{:S(2)}) collective-permute-start(bf16[8,2,14336]{2,1,0:T(2,128)(2,1)S(1)} %constant_dynamic-update-slice_fusion.2.near_ref), channel_id=1, source_target_pairs={{0,1},{1,0},{2,3},{3,2},{4,5},{5,4},{6,7},{7,6},{8,9},{9,8},{10,11... | collective-permute-start | bytes 1376264 | tf_op jit(solution)/shard_map/ppermute | solution.py:48
  21.1 10.6 %collective-permute-start.7 = (bf16[256,512]{1,0:T(8,128)(2,1)S(1)}, bf16[256,512]{1,0:T(8,128)(2,1)S(1)}, u32[]{:S(2)}, u32[]{:S(2)}) collective-permute-start(bf16[256,512]{1,0:T(8,128)(2,1)S(1)} %bitcast.3), channel_id=1, source_target_pairs={{0,4},{1,5},{4,8},{5,9},{8,12},{9,13},{12,14},{13,15},{14,10},{15,... | collective-permute-start | bytes 786440 | tf_op jit(solution)/shard_map/ppermute | solution.py:278
  22.2 9.5 %collective-permute-start.8 = (bf16[256,512]{1,0:T(8,128)(2,1)S(1)}, bf16[256,512]{1,0:T(8,128)(2,1)S(1)}, u32[]{:S(2)}, u32[]{:S(2)}) collective-permute-start(bf16[256,512]{1,0:T(8,128)(2,1)S(1)} %bitcast.4), channel_id=1, source_target_pairs={{0,2},{1,3},{4,0},{5,1},{8,4},{9,5},{12,8},{13,9},{14,12},{15,13},... | collective-permute-start | bytes 786440 | tf_op jit(solution)/shard_map/ppermute | solution.py:279
  23.1 8.5 %collective-permute-start.9 = (bf16[256,512]{1,0:T(8,128)(2,1)S(1)}, bf16[256,512]{1,0:T(8,128)(2,1)S(1)}, u32[]{:S(2)}, u32[]{:S(2)}) collective-permute-start(bf16[256,512]{1,0:T(8,128)(2,1)S(1)} %bitcast.5), channel_id=1, source_target_pairs={{0,1},{1,0},{2,3},{3,2},{4,5},{5,4},{6,7},{7,6},{8,9},{9,8},{10,11... | collective-permute-start | bytes 786440 | tf_op jit(solution)/shard_map/ppermute | solution.py:48
  23.1 12.1 %all-to-all-start = ((bf16[8,32,256]{2,1,0:T(8,128)(2,1)}), bf16[8,32,256]{2,1,0:T(8,128)(2,1)S(1)}, u32[]{:S(2)}, u32[]{:S(2)}) async-start(bf16[8,32,256]{2,1,0:T(8,128)(2,1)} %rotate_in.1), calls=%async_computation | async-start | bytes 262144 | tf_op jit(solution)/shard_map/all_to_all | solution.py:44
  31.7 10.1 %collective-permute-start.10 = (bf16[256,512]{1,0:T(8,128)(2,1)S(1)}, bf16[256,512]{1,0:T(8,128)(2,1)S(1)}, u32[]{:S(2)}, u32[]{:S(2)}) collective-permute-start(bf16[256,512]{1,0:T(8,128)(2,1)S(1)} %collective-permute-done.7.refs_2_), channel_id=1, source_target_pairs={{0,4},{1,5},{4,8},{5,9},{8,12},{9,13},{12,14},{13,15},{14,10},{15,... | collective-permute-start | bytes 786440 | tf_op jit(solution)/shard_map/ppermute | solution.py:278
  33.7 8.1 %collective-permute-start.11 = (bf16[256,512]{1,0:T(8,128)(2,1)S(1)}, bf16[256,512]{1,0:T(8,128)(2,1)S(1)}, u32[]{:S(2)}, u32[]{:S(2)}) collective-permute-start(bf16[256,512]{1,0:T(8,128)(2,1)S(1)} %collective-permute-done.8.refs_4_), channel_id=1, source_target_pairs={{0,2},{1,3},{4,0},{5,1},{8,4},{9,5},{12,8},{13,9},{14,12},{15,13},... | collective-permute-start | bytes 786440 | tf_op jit(solution)/shard_map/ppermute | solution.py:279
  33.8 8.0 %collective-permute-start.13 = (bf16[256,512]{1,0:T(8,128)(2,1)S(1)}, bf16[256,512]{1,0:T(8,128)(2,1)S(1)}, u32[]{:S(2)}, u32[]{:S(2)}) collective-permute-start(bf16[256,512]{1,0:T(8,128)(2,1)S(1)} %collective-permute-done.7.refs_2_), channel_id=1, source_target_pairs={{0,1},{1,0},{2,3},{3,2},{4,5},{5,4},{6,7},{7,6},{8,9},{9,8},{10,11... | collective-permute-start | bytes 786440 | tf_op jit(solution)/shard_map/ppermute | solution.py:48
  33.8 8.0 %collective-permute-start.14 = (bf16[256,512]{1,0:T(8,128)(2,1)S(1)}, bf16[256,512]{1,0:T(8,128)(2,1)S(1)}, u32[]{:S(2)}, u32[]{:S(2)}) collective-permute-start(bf16[256,512]{1,0:T(8,128)(2,1)S(1)} %collective-permute-done.8.refs_4_), channel_id=1, source_target_pairs={{0,1},{1,0},{2,3},{3,2},{4,5},{5,4},{6,7},{7,6},{8,9},{9,8},{10,11... | collective-permute-start | bytes 786440 | tf_op jit(solution)/shard_map/ppermute | solution.py:48
  35.2 6.6 %collective-permute-start.12 = (bf16[8,32,256]{2,1,0:T(8,128)(2,1)S(1)}, bf16[8,32,256]{2,1,0:T(8,128)(2,1)S(1)}, u32[]{:S(2)}, u32[]{:S(2)}) collective-permute-start(bf16[8,32,256]{2,1,0:T(8,128)(2,1)S(1)} %all-to-all-done.near_ref), channel_id=1, source_target_pairs={{0,1},{1,0},{2,3},{3,2},{4,5},{5,4},{6,7},{7,6},{8,9},{9,8},{10,11... | collective-permute-start | bytes 393224 | tf_op jit(solution)/shard_map/ppermute | solution.py:48
  41.8 8.8 %collective-permute-start.15 = (bf16[256,512]{1,0:T(8,128)(2,1)S(1)}, bf16[256,512]{1,0:T(8,128)(2,1)S(1)}, u32[]{:S(2)}, u32[]{:S(2)}) collective-permute-start(bf16[256,512]{1,0:T(8,128)(2,1)S(1)} %collective-permute-done.10.refs_6_), channel_id=1, source_target_pairs={{0,4},{1,5},{4,8},{5,9},{8,12},{9,13},{12,14},{13,15},{14,10},{15,... | collective-permute-start | bytes 786440 | tf_op jit(solution)/shard_map/ppermute | solution.py:278
  43.1 8.3 %collective-permute-start.16 = (bf16[256,512]{1,0:T(8,128)(2,1)S(1)}, bf16[256,512]{1,0:T(8,128)(2,1)S(1)}, u32[]{:S(2)}, u32[]{:S(2)}) collective-permute-start(bf16[256,512]{1,0:T(8,128)(2,1)S(1)} %collective-permute-done.11.refs_8_), channel_id=1, source_target_pairs={{0,2},{1,3},{4,0},{5,1},{8,4},{9,5},{12,8},{13,9},{14,12},{15,13},... | collective-permute-start | bytes 786440 | tf_op jit(solution)/shard_map/ppermute | solution.py:279
  43.9 7.5 %collective-permute-start.17 = (bf16[256,512]{1,0:T(8,128)(2,1)S(1)}, bf16[256,512]{1,0:T(8,128)(2,1)S(1)}, u32[]{:S(2)}, u32[]{:S(2)}) collective-permute-start(bf16[256,512]{1,0:T(8,128)(2,1)S(1)} %collective-permute-done.10.refs_6_), channel_id=1, source_target_pairs={{0,1},{1,0},{2,3},{3,2},{4,5},{5,4},{6,7},{7,6},{8,9},{9,8},{10,11... | collective-permute-start | bytes 786440 | tf_op jit(solution)/shard_map/ppermute | solution.py:48
  43.9 7.5 %collective-permute-start.18 = (bf16[256,512]{1,0:T(8,128)(2,1)S(1)}, bf16[256,512]{1,0:T(8,128)(2,1)S(1)}, u32[]{:S(2)}, u32[]{:S(2)}) collective-permute-start(bf16[256,512]{1,0:T(8,128)(2,1)S(1)} %collective-permute-done.11.refs_8_), channel_id=1, source_target_pairs={{0,1},{1,0},{2,3},{3,2},{4,5},{5,4},{6,7},{7,6},{8,9},{9,8},{10,11... | collective-permute-start | bytes 786440 | tf_op jit(solution)/shard_map/ppermute | solution.py:48
  51.9 6.0 %collective-permute-start.21 = (bf16[128,512]{1,0:T(8,128)(2,1)S(1)}, bf16[128,512]{1,0:T(8,128)(2,1)S(1)}, u32[]{:S(2)}, u32[]{:S(2)}) collective-permute-start(bf16[128,512]{1,0:T(8,128)(2,1)S(1)} %slice.10), channel_id=1, source_target_pairs={{0,4},{1,5},{4,8},{5,9},{8,12},{9,13},{12,14},{13,15},{14,10},{15,... | collective-permute-start | bytes 393224 | tf_op jit(solution)/shard_map/ppermute | solution.py:278
  63.7 9.5 %collective-permute-start.26 = (bf16[48,512]{1,0:T(8,128)(2,1)S(1)}, bf16[48,512]{1,0:T(8,128)(2,1)S(1)}, u32[]{:S(2)}, u32[]{:S(2)}) collective-permute-start(bf16[48,512]{1,0:T(8,128)(2,1)S(1)} %get-tuple-element.98), channel_id=1, source_target_pairs={{0,14},{1,15},{2,12},{3,13},{4,10},{5,11},{6,8},{7,9},{8,6},{9,7},... | collective-permute-start | bytes 147464 | tf_op jit(solution)/shard_map/ppermute | solution.py:450
  66.4 6.8 %collective-permute-start.27 = (bf16[48,512]{1,0:T(8,128)(2,1)S(1)}, bf16[48,512]{1,0:T(8,128)(2,1)S(1)}, u32[]{:S(2)}, u32[]{:S(2)}) collective-permute-start(bf16[48,512]{1,0:T(8,128)(2,1)S(1)} %get-tuple-element.99), channel_id=1, source_target_pairs={{0,10},{1,11},{2,8},{3,9},{4,14},{5,15},{6,12},{7,13},{8,2},{9,3},... | collective-permute-start | bytes 147464 | tf_op jit(solution)/shard_map/ppermute | solution.py:450
  67.6 7.3 %collective-permute-start.28 = (bf16[48,512]{1,0:T(8,128)(2,1)S(1)}, bf16[48,512]{1,0:T(8,128)(2,1)S(1)}, u32[]{:S(2)}, u32[]{:S(2)}) collective-permute-start(bf16[48,512]{1,0:T(8,128)(2,1)S(1)} %get-tuple-element.100), channel_id=1, source_target_pairs={{0,6},{1,7},{2,4},{3,5},{4,2},{5,3},{6,0},{7,1},{8,14},{9,15},{10,... | collective-permute-start | bytes 147464 | tf_op jit(solution)/shard_map/ppermute | solution.py:450
  69.0 5.9 %collective-permute-start.29 = (bf16[48,512]{1,0:T(8,128)(2,1)S(1)}, bf16[48,512]{1,0:T(8,128)(2,1)S(1)}, u32[]{:S(2)}, u32[]{:S(2)}) collective-permute-start(bf16[48,512]{1,0:T(8,128)(2,1)S(1)} %get-tuple-element.101), channel_id=1, source_target_pairs={{0,2},{1,3},{2,0},{3,1},{4,6},{5,7},{6,4},{7,5},{8,10},{9,11},{10,... | collective-permute-start | bytes 147464 | tf_op jit(solution)/shard_map/ppermute | solution.py:450
  70.5 6.1 %collective-permute-start.30 = (bf16[48,512]{1,0:T(8,128)(2,1)S(1)}, bf16[48,512]{1,0:T(8,128)(2,1)S(1)}, u32[]{:S(2)}, u32[]{:S(2)}) collective-permute-start(bf16[48,512]{1,0:T(8,128)(2,1)S(1)} %get-tuple-element.102), channel_id=1, source_target_pairs={{0,12},{1,13},{2,14},{3,15},{4,8},{5,9},{6,10},{7,11},{8,4},{9,5},... | collective-permute-start | bytes 147464 | tf_op jit(solution)/shard_map/ppermute | solution.py:450
  (14 other events, 54.7 us)

commit v25 on v21

--- a/solution.py
+++ b/solution.py
@@ -225,17 +225,26 @@
     window_copy.wait()
 
 
-def window_kernel(scale, window_ref, scaled_ref, projected_ref, *refs):
+def mix_kernel(window_ref, scaled_ref, projected_ref, part_ref, mixed_ref):
+    part_ref[...] = jnp.dot(
+        window_ref[...],
+        projected_ref[...].astype(jnp.bfloat16),
+        preferred_element_type=jnp.float32,
+    )
+    columns = slice(scaled_ref.shape[1] - mixed_ref.shape[1], None)
+    mixed = jnp.dot(
+        window_ref[...], scaled_ref[:, columns], preferred_element_type=jnp.float32
+    )
+    mixed_ref[...] = mixed.astype(jnp.bfloat16)
+
+
+def window_kernel(scale, part_ref, mixed_ref, *refs):
     pieces = refs[:-3]
     send_ref, keep_ref, result = refs[-3:]
     chips, rows, _ = keep_ref.shape
-    width = pieces[0].shape[0]
-    total = projected_ref[...]
-    first = scaled_ref.shape[1] - width * len(pieces)
     basis = jnp.concatenate([piece[...] for piece in pieces], axis=0)
-    total += jnp.dot(scaled_ref[:, first:], basis, preferred_element_type=jnp.float32)
-    result[...] = scale * jnp.dot(
-        window_ref[...], total.astype(jnp.bfloat16), preferred_element_type=jnp.float32
+    result[...] = scale * (
+        part_ref[...] + jnp.dot(mixed_ref[...], basis, preferred_element_type=jnp.float32)
     )
     core = lax.rem(lax.axis_index("blk"), 2)
     for k in range(chips):
@@ -422,19 +431,31 @@
     projected, *last = after(projected, *last)
     last += [swap(piece, n) for piece in last]
     rows = WR // n
+    part, mixed = pl.pallas_call(
+        mix_kernel,
+        out_shape=(
+            jax.ShapeDtypeStruct((WR, WC), jnp.float32),
+            jax.ShapeDtypeStruct((WR, 2 * in_width), jnp.bfloat16),
+        ),
+        in_specs=[VMEM] * 3,
+        out_specs=(VMEM, VMEM),
+        compiler_params=pltpu.CompilerParams(vmem_limit_bytes=24 * MIB),
+        cost_estimate=CHEAP,
+        name="mix",
+    )(window, scaled, projected)
     send, keep = pl.pallas_call(
         functools.partial(window_kernel, 1.0 / tokens),
         out_shape=(
             jax.ShapeDtypeStruct((chips, rows, WC), jnp.bfloat16),
             jax.ShapeDtypeStruct((chips, rows, WC), jnp.float32),
         ),
-        in_specs=[VMEM] * 7,
+        in_specs=[VMEM] * 6,
         out_specs=(VMEM, VMEM),
         scratch_shapes=[pltpu.VMEM((WR, WC), jnp.float32)],
         compiler_params=pltpu.CompilerParams(vmem_limit_bytes=24 * MIB),
         cost_estimate=CHEAP,
         name="window",
-    )(window, scaled, projected, *last)
+    )(part, mixed, *last)
 
     keys = [*range(chips - 2, 0, -2), *range(chips - 1, 0, -2)]
     small = pltpu.CompilerParams(vmem_limit_bytes=8 * MIB)

time: 78.6 us -> 78.5 us (level)
  Pallas kernels: 24.6 us -> 25.6 us
    pallas_call x0 -> x1, Pallas kernels: none -> 1.79 us  [ring_body(): pl.pallas_call(mix_kernel, out_shape=(jax.ShapeDtypeStruct((WR, WC), jnp....]
    pallas_call x1, Pallas kernels: 1.62 us -> 0.78 us  [ring_body(): pl.pallas_call(functools.partial(window_kernel, 1.0 / tokens), out_shape=...]
  transfers between devices with their start and end apart: 34 -> 34, of which waited for: 13 -> 12; matrix products, arithmetic and copies ran while one was open for 1% -> 1% of each run, Pallas kernels for 28% -> 31%
where the time goes in v25:
time: 78.5 us; the launch traced here: 78.2 us
  starting transfers between devices  34.1 us (43%)
  Pallas kernels  25.6 us (33%)
  waiting for transfers between devices  14.3 us (18%)
  local copies, waits for them, and re-layouts  3.02 us (4%)
  other arithmetic  0.91 us (1%)
    ppermute x7, starting transfers between devices, ring_body(): lax.ppermute(x, 'blk', xor_pairs(n, 2 * key))  11.2 us
    pallas_call x2, Pallas kernels, ring_body(): pl.pallas_call(kernel, out_shape=jax.ShapeDtypeStruct(shape, dtype), in_s...  10.7 us
    pallas_call x1, Pallas kernels, ring_body(): pl.pallas_call(functools.partial(scale_kernel, begun), out_shape=jax.Shap...  6.22 us
    ppermute x4, starting transfers between devices, ring_body(): to_right = lambda x: lax.ppermute(x, 'blk', shift_pairs(n, 1))  5.95 us
    ppermute x3, starting transfers between devices, ring_body(): lax.ppermute(both, 'blk', xor_pairs(n, 4 * key))  5.68 us
    all_to_all x1, starting transfers between devices, exchange(): return lax.all_to_all(x, 'blk', 0, 0, axis_index_groups=groups, tiled=True)  4.33 us
    pallas_call x1, Pallas kernels, ring_body(): pl.pallas_call(functools.partial(project_kernel, (0, 6, len(pieces))), ou...  3.92 us
    ppermute x3, waiting for transfers between devices, ring_body(): lax.ppermute(both, 'blk', xor_pairs(n, 4 * key))  3.56 us
  transfers between devices with their start and end apart: 34, of which 12 were waited for; matrix products, arithmetic and copies ran while one was open for 1% of the time, Pallas kernels for 31%

profile of v25, /device:TPU:0, one launch (start us, length us, event | category | flops | bytes accessed | tf_op | source)
XLA Modules:
  0.0 78.2 jit_solution(5285289428592867441)
XLA Ops:
  0.9 3.1 %collective-permute-start = (bf16[1,2,18432]{2,1,0:T(2,128)(2,1)S(1)}, bf16[1,2,18432]{2,1,0:T(2,128)(2,1)S(1)}, u32[]{:S(2)}, u32[]{:S(2)}) collective-permute-start(bf16[1,2,18432]{2,1,0:T(2,128)(2,1)S(1)} %maximum_bitcast_fusion.refs_0_), channel_id=1, source_target_pairs={{0,4},{1,5},{2,6},{3,7},{4,0},{5,1},{6,2},{7,3},{8,12},{9,13},{10,... | collective-permute-start | bytes 221192 | tf_op jit(solution)/shard_map/ppermute | solution.py:295
  4.0 2.6 %collective-permute-start.1 = (bf16[1,2,18432]{2,1,0:T(2,128)(2,1)S(1)}, bf16[1,2,18432]{2,1,0:T(2,128)(2,1)S(1)}, u32[]{:S(2)}, u32[]{:S(2)}) collective-permute-start(bf16[1,2,18432]{2,1,0:T(2,128)(2,1)S(1)} %maximum_bitcast_fusion.refs_0_), channel_id=1, source_target_pairs={{0,8},{1,9},{2,10},{3,11},{4,12},{5,13},{6,14},{7,15},{8,0},{9,1},... | collective-permute-start | bytes 221192 | tf_op jit(solution)/shard_map/ppermute | solution.py:295
  6.6 1.6 %copy-done = bf16[4096,256]{1,0:T(8,128)(2,1)S(1)} copy-done((bf16[4096,256]{1,0:T(8,128)(2,1)S(1)}, bf16[4096,256]{1,0:T(8,128)(2,1)}, u32[]{:S(2)}) %copy-start) | copy-done | bytes 2097176
  9.3 2.5 %collective-permute-done.1.refs_2_ = bf16[1,2,18432]{2,1,0:T(2,128)(2,1)S(1)} collective-permute-done((bf16[1,2,18432]{2,1,0:T(2,128)(2,1)S(1)}, bf16[1,2,18432]{2,1,0:T(2,128)(2,1)S(1)}, u32[]{:S(2)}, u32[]{:S(2)}) %collective-permute-start.1) | collective-permute-done | bytes 73760 | tf_op jit(solution)/shard_map/ppermute | solution.py:295
  12.9 1.6 %collective-permute-start.4 = (bf16[4,2,4096]{2,1,0:T(2,128)(2,1)S(1)}, bf16[4,2,4096]{2,1,0:T(2,128)(2,1)S(1)}, u32[]{:S(2)}, u32[]{:S(2)}) collective-permute-start(bf16[4,2,4096]{2,1,0:T(2,128)(2,1)S(1)} %get-tuple-element.66), channel_id=1, source_target_pairs={{0,2},{1,3},{2,0},{3,1},{4,6},{5,7},{6,4},{7,5},{8,10},{9,11},{10,... | collective-permute-start | bytes 196616 | tf_op jit(solution)/shard_map/ppermute | solution.py:319
  15.1 2.9 %collective-permute-done.4 = bf16[4,2,4096]{2,1,0:T(2,128)(2,1)S(1)} collective-permute-done((bf16[4,2,4096]{2,1,0:T(2,128)(2,1)S(1)}, bf16[4,2,4096]{2,1,0:T(2,128)(2,1)S(1)}, u32[]{:S(2)}, u32[]{:S(2)}) %collective-permute-start.4) | collective-permute-done | bytes 65568 | tf_op jit(solution)/shard_map/ppermute | solution.py:319
  18.3 1.2 %collective-permute-done.5.far_ref = bf16[8,2,4096]{2,1,0:T(2,128)(2,1)S(1)} collective-permute-done((bf16[8,2,4096]{2,1,0:T(2,128)(2,1)S(1)}, bf16[8,2,4096]{2,1,0:T(2,128)(2,1)S(1)}, u32[]{:S(2)}, u32[]{:S(2)}) %collective-permute-start.5) | collective-permute-done | bytes 131104 | tf_op jit(solution)/shard_map/ppermute | solution.py:48
  19.4 1.2 %rotate_in.1 = bf16[8,32,256]{2,1,0:T(8,128)(2,1)} custom-call(bf16[8,2,4096]{2,1,0:T(2,128)(2,1)S(1)} %constant_dynamic-update-slice_fusion.near_ref, bf16[8,2,4096]{2,1,0:T(2,128)(2,1)S(1)} %collective-permute-done.5.far_ref, bf16[4096,256]{1,0:T(8,128)(2,1)S(1)} %keep.1.basis_ref), custom_call_target="tpu_custom_call" | custom-call | flops 1 | bytes 1 | tf_op jit(solution)/shard_map/rotate_in/pallas_call | solution.py:322
  23.1 4.3 %all-to-all-start = ((bf16[8,32,256]{2,1,0:T(8,128)(2,1)}), bf16[8,32,256]{2,1,0:T(8,128)(2,1)S(1)}, u32[]{:S(2)}, u32[]{:S(2)}) async-start(bf16[8,32,256]{2,1,0:T(8,128)(2,1)} %rotate_in.1), calls=%async_computation | async-start | bytes 262144 | tf_op jit(solution)/shard_map/all_to_all | solution.py:44
  27.5 4.2 %rotate_first.1.start_ref = f32[32,896]{1,0:T(8,128)S(1)} custom-call(bf16[8,2,14336]{2,1,0:T(2,128)(2,1)S(1)} %constant_dynamic-update-slice_fusion.2.near_ref, bf16[8,2,14336]{2,1,0:T(2,128)(2,1)S(1)} %collective-permute-done.6.far_ref, bf16[14336,896]{1,0:T(8,128)(2,1)} %basis_out_ref.1), custom_call_target="tpu_custom_call" | custom-call | flops 1 | bytes 1 | tf_op jit(solution)/shard_map/rotate_first/pallas_call | solution.py:339
  31.7 2.1 %collective-permute-start.10 = (bf16[256,512]{1,0:T(8,128)(2,1)S(1)}, bf16[256,512]{1,0:T(8,128)(2,1)S(1)}, u32[]{:S(2)}, u32[]{:S(2)}) collective-permute-start(bf16[256,512]{1,0:T(8,128)(2,1)S(1)} %collective-permute-done.7.refs_2_), channel_id=1, source_target_pairs={{0,4},{1,5},{4,8},{5,9},{8,12},{9,13},{12,14},{13,15},{14,10},{15,... | collective-permute-start | bytes 786440 | tf_op jit(solution)/shard_map/ppermute | solution.py:287
  35.2 6.6 %rotate_last.1.aligned_ref = bf16[896,32]{1,0:T(8,128)(2,1)S(1)} custom-call(bf16[8,2,14336]{2,1,0:T(2,128)(2,1)S(1)} %constant_dynamic-update-slice_fusion.2.near_ref, bf16[8,2,14336]{2,1,0:T(2,128)(2,1)S(1)} %collective-permute-done.6.far_ref, bf16[14336,896]{1,0:T(8,128)(2,1)} %basis_out_ref.1, s32[16]{0:T(128)S(1)} %copy-done.2, ...), custom_call_target="tpu_custom_call" | custom-call | flops 1 | bytes 1 | tf_op jit(solution)/shard_map/rotate_last/pallas_call | solution.py:339
  41.8 1.3 %collective-permute-start.15 = (bf16[256,512]{1,0:T(8,128)(2,1)S(1)}, bf16[256,512]{1,0:T(8,128)(2,1)S(1)}, u32[]{:S(2)}, u32[]{:S(2)}) collective-permute-start(bf16[256,512]{1,0:T(8,128)(2,1)S(1)} %collective-permute-done.10.refs_6_), channel_id=1, source_target_pairs={{0,4},{1,5},{4,8},{5,9},{8,12},{9,13},{12,14},{13,15},{14,10},{15,... | collective-permute-start | bytes 786440 | tf_op jit(solution)/shard_map/ppermute | solution.py:287
  44.4 6.2 %scale.1.scaled_ref = bf16[896,4096]{1,0:T(8,128)(2,1)S(1)} custom-call(bf16[896,32]{1,0:T(8,128)(2,1)S(1)} %rotate_last.1.aligned_ref, bf16[8,32,256]{2,1,0:T(8,128)(2,1)S(1)} %all-to-all-done.near_ref, bf16[8,32,256]{2,1,0:T(8,128)(2,1)S(1)} %collective-permute-done.12.far_ref, s32[32]{0:T(128)S(1)} %copy-done.1, f32[896,4096]{1,0:T(8,128)} %eigen_ref.1), custom_call_target="tpu_custom_call" | custom-call | flops 1 | bytes 1 | tf_op jit(solution)/shard_map/scale/pallas_call | solution.py:391
  51.9 1.5 %collective-permute-start.21 = (bf16[128,512]{1,0:T(8,128)(2,1)S(1)}, bf16[128,512]{1,0:T(8,128)(2,1)S(1)}, u32[]{:S(2)}, u32[]{:S(2)}) collective-permute-start(bf16[128,512]{1,0:T(8,128)(2,1)S(1)} %slice.10), channel_id=1, source_target_pairs={{0,4},{1,5},{4,8},{5,9},{8,12},{9,13},{12,14},{13,15},{14,10},{15,... | collective-permute-start | bytes 393224 | tf_op jit(solution)/shard_map/ppermute | solution.py:287
  54.0 3.9 %project.1 = (f32[896,512]{1,0:T(8,128)S(1)}, bf16[768,896]{1,0:T(8,128)(2,1)S(1)}) custom-call(bf16[896,4096]{1,0:T(8,128)(2,1)S(1)} %scale.1.scaled_ref, bf16[14336,896]{1,0:T(8,128)(2,1)} %basis_out_ref.1, bf16[256,512]{1,0:T(8,128)(2,1)S(1)} %bitcast.6, bf16[256,512]{1,0:T(8,128)(2,1)S(1)} %collective-permute-done.9.refs_1_, ...), custom_call_target="tpu_custom_call" | custom-call | flops 1 | bytes 1 | tf_op jit(solution)/shard_map/project/pallas_call | solution.py:414
  59.2 1.8 %mix.1 = (f32[768,512]{1,0:T(8,128)S(1)}, bf16[768,512]{1,0:T(8,128)(2,1)S(1)}) custom-call(bf16[768,896]{1,0:T(8,128)(2,1)S(1)} %get-tuple-element.92.window_ref, bf16[896,4096]{1,0:T(8,128)(2,1)S(1)} %scale.1.scaled_ref, f32[896,512]{1,0:T(8,128)S(1)} %get-tuple-element.94.projected_ref), custom_call_target="tpu_custom_call" | custom-call | flops 1 | bytes 1 | tf_op jit(solution)/shard_map/mix/pallas_call | solution.py:434
  61.9 1.7 %collective-permute-done.25.got_ref = bf16[8,48,512]{2,1,0:T(8,128)(2,1)S(1)} collective-permute-done((bf16[8,48,512]{2,1,0:T(8,128)(2,1)S(1)}, bf16[8,48,512]{2,1,0:T(8,128)(2,1)S(1)}, u32[]{:S(2)}, u32[]{:S(2)}) %collective-permute-start.25) | collective-permute-done | bytes 393248 | tf_op jit(solution)/shard_map/ppermute | solution.py:48
  63.6 2.7 %collective-permute-start.26 = (bf16[48,512]{1,0:T(8,128)(2,1)S(1)}, bf16[48,512]{1,0:T(8,128)(2,1)S(1)}, u32[]{:S(2)}, u32[]{:S(2)}) collective-permute-start(bf16[48,512]{1,0:T(8,128)(2,1)S(1)} %get-tuple-element.102), channel_id=1, source_target_pairs={{0,12},{1,13},{2,14},{3,15},{4,8},{5,9},{6,10},{7,11},{8,4},{9,5},... | collective-permute-start | bytes 147464 | tf_op jit(solution)/shard_map/ppermute | solution.py:471
  66.6 1.5 %collective-permute-start.28 = (bf16[48,512]{1,0:T(8,128)(2,1)S(1)}, bf16[48,512]{1,0:T(8,128)(2,1)S(1)}, u32[]{:S(2)}, u32[]{:S(2)}) collective-permute-start(bf16[48,512]{1,0:T(8,128)(2,1)S(1)} %get-tuple-element.104), channel_id=1, source_target_pairs={{0,4},{1,5},{2,6},{3,7},{4,0},{5,1},{6,2},{7,3},{8,12},{9,13},{10,... | collective-permute-start | bytes 147464 | tf_op jit(solution)/shard_map/ppermute | solution.py:471
  68.1 2.7 %collective-permute-start.29 = (bf16[48,512]{1,0:T(8,128)(2,1)S(1)}, bf16[48,512]{1,0:T(8,128)(2,1)S(1)}, u32[]{:S(2)}, u32[]{:S(2)}) collective-permute-start(bf16[48,512]{1,0:T(8,128)(2,1)S(1)} %get-tuple-element.105), channel_id=1, source_target_pairs={{0,14},{1,15},{2,12},{3,13},{4,10},{5,11},{6,8},{7,9},{8,6},{9,7},... | collective-permute-start | bytes 147464 | tf_op jit(solution)/shard_map/ppermute | solution.py:471
  71.0 2.4 %collective-permute-start.31 = (bf16[48,512]{1,0:T(8,128)(2,1)S(1)}, bf16[48,512]{1,0:T(8,128)(2,1)S(1)}, u32[]{:S(2)}, u32[]{:S(2)}) collective-permute-start(bf16[48,512]{1,0:T(8,128)(2,1)S(1)} %get-tuple-element.107), channel_id=1, source_target_pairs={{0,6},{1,7},{2,4},{3,5},{4,2},{5,3},{6,0},{7,1},{8,14},{9,15},{10,... | collective-permute-start | bytes 147464 | tf_op jit(solution)/shard_map/ppermute | solution.py:471
  73.4 1.5 %collective-permute-start.32 = (bf16[48,512]{1,0:T(8,128)(2,1)S(1)}, bf16[48,512]{1,0:T(8,128)(2,1)S(1)}, u32[]{:S(2)}, u32[]{:S(2)}) collective-permute-start(bf16[48,512]{1,0:T(8,128)(2,1)S(1)} %get-tuple-element.108), channel_id=1, source_target_pairs={{0,2},{1,3},{2,0},{3,1},{4,6},{5,7},{6,4},{7,5},{8,10},{9,11},{10,... | collective-permute-start | bytes 147464 | tf_op jit(solution)/shard_map/ppermute | solution.py:471
  75.0 1.6 %collective-permute-done.30.refs_4_ = bf16[48,512]{1,0:T(8,128)(2,1)S(1)} collective-permute-done((bf16[48,512]{1,0:T(8,128)(2,1)S(1)}, bf16[48,512]{1,0:T(8,128)(2,1)S(1)}, u32[]{:S(2)}, u32[]{:S(2)}) %collective-permute-start.30) | collective-permute-done | bytes 49184 | tf_op jit(solution)/shard_map/ppermute | solution.py:471
  (71 shorter events, 15.4 us)
Async XLA Ops:
  0.9 8.4 %collective-permute-start = (bf16[1,2,18432]{2,1,0:T(2,128)(2,1)S(1)}, bf16[1,2,18432]{2,1,0:T(2,128)(2,1)S(1)}, u32[]{:S(2)}, u32[]{:S(2)}) collective-permute-start(bf16[1,2,18432]{2,1,0:T(2,128)(2,1)S(1)} %maximum_bitcast_fusion.refs_0_), channel_id=1, source_target_pairs={{0,4},{1,5},{2,6},{3,7},{4,0},{5,1},{6,2},{7,3},{8,12},{9,13},{10,... | collective-permute-start | bytes 221192 | tf_op jit(solution)/shard_map/ppermute | solution.py:295
  4.0 7.8 %collective-permute-start.1 = (bf16[1,2,18432]{2,1,0:T(2,128)(2,1)S(1)}, bf16[1,2,18432]{2,1,0:T(2,128)(2,1)S(1)}, u32[]{:S(2)}, u32[]{:S(2)}) collective-permute-start(bf16[1,2,18432]{2,1,0:T(2,128)(2,1)S(1)} %maximum_bitcast_fusion.refs_0_), channel_id=1, source_target_pairs={{0,8},{1,9},{2,10},{3,11},{4,12},{5,13},{6,14},{7,15},{8,0},{9,1},... | collective-permute-start | bytes 221192 | tf_op jit(solution)/shard_map/ppermute | solution.py:295
  6.6 6.3 %collective-permute-start.2 = (bf16[1,2,18432]{2,1,0:T(2,128)(2,1)S(1)}, bf16[1,2,18432]{2,1,0:T(2,128)(2,1)S(1)}, u32[]{:S(2)}, u32[]{:S(2)}) collective-permute-start(bf16[1,2,18432]{2,1,0:T(2,128)(2,1)S(1)} %maximum_bitcast_fusion.refs_0_), channel_id=1, source_target_pairs={{0,12},{1,13},{2,14},{3,15},{4,8},{5,9},{6,10},{7,11},{8,4},{9,5},... | collective-permute-start | bytes 221192 | tf_op jit(solution)/shard_map/ppermute | solution.py:295
  14.5 6.2 %collective-permute-start.3 = (bf16[4,2,14336]{2,1,0:T(2,128)(2,1)S(1)}, bf16[4,2,14336]{2,1,0:T(2,128)(2,1)S(1)}, u32[]{:S(2)}, u32[]{:S(2)}) collective-permute-start(bf16[4,2,14336]{2,1,0:T(2,128)(2,1)S(1)} %get-tuple-element.64), channel_id=1, source_target_pairs={{0,2},{1,3},{2,0},{3,1},{4,6},{5,7},{6,4},{7,5},{8,10},{9,11},{10,... | collective-permute-start | bytes 688136 | tf_op jit(solution)/shard_map/ppermute | solution.py:320
  20.9 6.6 %collective-permute-start.6 = (bf16[8,2,14336]{2,1,0:T(2,128)(2,1)S(1)}, bf16[8,2,14336]{2,1,0:T(2,128)(2,1)S(1)}, u32[]{:S(2)}, u32[]{:S(2)}) collective-permute-start(bf16[8,2,14336]{2,1,0:T(2,128)(2,1)S(1)} %constant_dynamic-update-slice_fusion.2.near_ref), channel_id=1, source_target_pairs={{0,1},{1,0},{2,3},{3,2},{4,5},{5,4},{6,7},{7,6},{8,9},{9,8},{10,11... | collective-permute-start | bytes 1376264 | tf_op jit(solution)/shard_map/ppermute | solution.py:48
  21.1 10.6 %collective-permute-start.7 = (bf16[256,512]{1,0:T(8,128)(2,1)S(1)}, bf16[256,512]{1,0:T(8,128)(2,1)S(1)}, u32[]{:S(2)}, u32[]{:S(2)}) collective-permute-start(bf16[256,512]{1,0:T(8,128)(2,1)S(1)} %bitcast.3), channel_id=1, source_target_pairs={{0,4},{1,5},{4,8},{5,9},{8,12},{9,13},{12,14},{13,15},{14,10},{15,... | collective-permute-start | bytes 786440 | tf_op jit(solution)/shard_map/ppermute | solution.py:287
  22.2 9.5 %collective-permute-start.8 = (bf16[256,512]{1,0:T(8,128)(2,1)S(1)}, bf16[256,512]{1,0:T(8,128)(2,1)S(1)}, u32[]{:S(2)}, u32[]{:S(2)}) collective-permute-start(bf16[256,512]{1,0:T(8,128)(2,1)S(1)} %bitcast.4), channel_id=1, source_target_pairs={{0,2},{1,3},{4,0},{5,1},{8,4},{9,5},{12,8},{13,9},{14,12},{15,13},... | collective-permute-start | bytes 786440 | tf_op jit(solution)/shard_map/ppermute | solution.py:288
  23.1 8.5 %collective-permute-start.9 = (bf16[256,512]{1,0:T(8,128)(2,1)S(1)}, bf16[256,512]{1,0:T(8,128)(2,1)S(1)}, u32[]{:S(2)}, u32[]{:S(2)}) collective-permute-start(bf16[256,512]{1,0:T(8,128)(2,1)S(1)} %bitcast.5), channel_id=1, source_target_pairs={{0,1},{1,0},{2,3},{3,2},{4,5},{5,4},{6,7},{7,6},{8,9},{9,8},{10,11... | collective-permute-start | bytes 786440 | tf_op jit(solution)/shard_map/ppermute | solution.py:48
  23.1 12.1 %all-to-all-start = ((bf16[8,32,256]{2,1,0:T(8,128)(2,1)}), bf16[8,32,256]{2,1,0:T(8,128)(2,1)S(1)}, u32[]{:S(2)}, u32[]{:S(2)}) async-start(bf16[8,32,256]{2,1,0:T(8,128)(2,1)} %rotate_in.1), calls=%async_computation | async-start | bytes 262144 | tf_op jit(solution)/shard_map/all_to_all | solution.py:44
  31.7 10.1 %collective-permute-start.10 = (bf16[256,512]{1,0:T(8,128)(2,1)S(1)}, bf16[256,512]{1,0:T(8,128)(2,1)S(1)}, u32[]{:S(2)}, u32[]{:S(2)}) collective-permute-start(bf16[256,512]{1,0:T(8,128)(2,1)S(1)} %collective-permute-done.7.refs_2_), channel_id=1, source_target_pairs={{0,4},{1,5},{4,8},{5,9},{8,12},{9,13},{12,14},{13,15},{14,10},{15,... | collective-permute-start | bytes 786440 | tf_op jit(solution)/shard_map/ppermute | solution.py:287
  33.7 8.1 %collective-permute-start.11 = (bf16[256,512]{1,0:T(8,128)(2,1)S(1)}, bf16[256,512]{1,0:T(8,128)(2,1)S(1)}, u32[]{:S(2)}, u32[]{:S(2)}) collective-permute-start(bf16[256,512]{1,0:T(8,128)(2,1)S(1)} %collective-permute-done.8.refs_4_), channel_id=1, source_target_pairs={{0,2},{1,3},{4,0},{5,1},{8,4},{9,5},{12,8},{13,9},{14,12},{15,13},... | collective-permute-start | bytes 786440 | tf_op jit(solution)/shard_map/ppermute | solution.py:288
  33.8 8.0 %collective-permute-start.13 = (bf16[256,512]{1,0:T(8,128)(2,1)S(1)}, bf16[256,512]{1,0:T(8,128)(2,1)S(1)}, u32[]{:S(2)}, u32[]{:S(2)}) collective-permute-start(bf16[256,512]{1,0:T(8,128)(2,1)S(1)} %collective-permute-done.7.refs_2_), channel_id=1, source_target_pairs={{0,1},{1,0},{2,3},{3,2},{4,5},{5,4},{6,7},{7,6},{8,9},{9,8},{10,11... | collective-permute-start | bytes 786440 | tf_op jit(solution)/shard_map/ppermute | solution.py:48
  33.8 8.0 %collective-permute-start.14 = (bf16[256,512]{1,0:T(8,128)(2,1)S(1)}, bf16[256,512]{1,0:T(8,128)(2,1)S(1)}, u32[]{:S(2)}, u32[]{:S(2)}) collective-permute-start(bf16[256,512]{1,0:T(8,128)(2,1)S(1)} %collective-permute-done.8.refs_4_), channel_id=1, source_target_pairs={{0,1},{1,0},{2,3},{3,2},{4,5},{5,4},{6,7},{7,6},{8,9},{9,8},{10,11... | collective-permute-start | bytes 786440 | tf_op jit(solution)/shard_map/ppermute | solution.py:48
  35.2 6.6 %collective-permute-start.12 = (bf16[8,32,256]{2,1,0:T(8,128)(2,1)S(1)}, bf16[8,32,256]{2,1,0:T(8,128)(2,1)S(1)}, u32[]{:S(2)}, u32[]{:S(2)}) collective-permute-start(bf16[8,32,256]{2,1,0:T(8,128)(2,1)S(1)} %all-to-all-done.near_ref), channel_id=1, source_target_pairs={{0,1},{1,0},{2,3},{3,2},{4,5},{5,4},{6,7},{7,6},{8,9},{9,8},{10,11... | collective-permute-start | bytes 393224 | tf_op jit(solution)/shard_map/ppermute | solution.py:48
  41.8 8.8 %collective-permute-start.15 = (bf16[256,512]{1,0:T(8,128)(2,1)S(1)}, bf16[256,512]{1,0:T(8,128)(2,1)S(1)}, u32[]{:S(2)}, u32[]{:S(2)}) collective-permute-start(bf16[256,512]{1,0:T(8,128)(2,1)S(1)} %collective-permute-done.10.refs_6_), channel_id=1, source_target_pairs={{0,4},{1,5},{4,8},{5,9},{8,12},{9,13},{12,14},{13,15},{14,10},{15,... | collective-permute-start | bytes 786440 | tf_op jit(solution)/shard_map/ppermute | solution.py:287
  43.1 8.3 %collective-permute-start.16 = (bf16[256,512]{1,0:T(8,128)(2,1)S(1)}, bf16[256,512]{1,0:T(8,128)(2,1)S(1)}, u32[]{:S(2)}, u32[]{:S(2)}) collective-permute-start(bf16[256,512]{1,0:T(8,128)(2,1)S(1)} %collective-permute-done.11.refs_8_), channel_id=1, source_target_pairs={{0,2},{1,3},{4,0},{5,1},{8,4},{9,5},{12,8},{13,9},{14,12},{15,13},... | collective-permute-start | bytes 786440 | tf_op jit(solution)/shard_map/ppermute | solution.py:288
  43.9 7.5 %collective-permute-start.17 = (bf16[256,512]{1,0:T(8,128)(2,1)S(1)}, bf16[256,512]{1,0:T(8,128)(2,1)S(1)}, u32[]{:S(2)}, u32[]{:S(2)}) collective-permute-start(bf16[256,512]{1,0:T(8,128)(2,1)S(1)} %collective-permute-done.10.refs_6_), channel_id=1, source_target_pairs={{0,1},{1,0},{2,3},{3,2},{4,5},{5,4},{6,7},{7,6},{8,9},{9,8},{10,11... | collective-permute-start | bytes 786440 | tf_op jit(solution)/shard_map/ppermute | solution.py:48
  43.9 7.5 %collective-permute-start.18 = (bf16[256,512]{1,0:T(8,128)(2,1)S(1)}, bf16[256,512]{1,0:T(8,128)(2,1)S(1)}, u32[]{:S(2)}, u32[]{:S(2)}) collective-permute-start(bf16[256,512]{1,0:T(8,128)(2,1)S(1)} %collective-permute-done.11.refs_8_), channel_id=1, source_target_pairs={{0,1},{1,0},{2,3},{3,2},{4,5},{5,4},{6,7},{7,6},{8,9},{9,8},{10,11... | collective-permute-start | bytes 786440 | tf_op jit(solution)/shard_map/ppermute | solution.py:48
  51.9 6.0 %collective-permute-start.21 = (bf16[128,512]{1,0:T(8,128)(2,1)S(1)}, bf16[128,512]{1,0:T(8,128)(2,1)S(1)}, u32[]{:S(2)}, u32[]{:S(2)}) collective-permute-start(bf16[128,512]{1,0:T(8,128)(2,1)S(1)} %slice.10), channel_id=1, source_target_pairs={{0,4},{1,5},{4,8},{5,9},{8,12},{9,13},{12,14},{13,15},{14,10},{15,... | collective-permute-start | bytes 393224 | tf_op jit(solution)/shard_map/ppermute | solution.py:287
  63.6 7.4 %collective-permute-start.26 = (bf16[48,512]{1,0:T(8,128)(2,1)S(1)}, bf16[48,512]{1,0:T(8,128)(2,1)S(1)}, u32[]{:S(2)}, u32[]{:S(2)}) collective-permute-start(bf16[48,512]{1,0:T(8,128)(2,1)S(1)} %get-tuple-element.102), channel_id=1, source_target_pairs={{0,12},{1,13},{2,14},{3,15},{4,8},{5,9},{6,10},{7,11},{8,4},{9,5},... | collective-permute-start | bytes 147464 | tf_op jit(solution)/shard_map/ppermute | solution.py:471
  66.4 7.0 %collective-permute-start.27 = (bf16[48,512]{1,0:T(8,128)(2,1)S(1)}, bf16[48,512]{1,0:T(8,128)(2,1)S(1)}, u32[]{:S(2)}, u32[]{:S(2)}) collective-permute-start(bf16[48,512]{1,0:T(8,128)(2,1)S(1)} %get-tuple-element.103), channel_id=1, source_target_pairs={{0,8},{1,9},{2,10},{3,11},{4,12},{5,13},{6,14},{7,15},{8,0},{9,1},... | collective-permute-start | bytes 147464 | tf_op jit(solution)/shard_map/ppermute | solution.py:471
  66.6 8.2 %collective-permute-start.28 = (bf16[48,512]{1,0:T(8,128)(2,1)S(1)}, bf16[48,512]{1,0:T(8,128)(2,1)S(1)}, u32[]{:S(2)}, u32[]{:S(2)}) collective-permute-start(bf16[48,512]{1,0:T(8,128)(2,1)S(1)} %get-tuple-element.104), channel_id=1, source_target_pairs={{0,4},{1,5},{2,6},{3,7},{4,0},{5,1},{6,2},{7,3},{8,12},{9,13},{10,... | collective-permute-start | bytes 147464 | tf_op jit(solution)/shard_map/ppermute | solution.py:471
  68.1 6.9 %collective-permute-start.29 = (bf16[48,512]{1,0:T(8,128)(2,1)S(1)}, bf16[48,512]{1,0:T(8,128)(2,1)S(1)}, u32[]{:S(2)}, u32[]{:S(2)}) collective-permute-start(bf16[48,512]{1,0:T(8,128)(2,1)S(1)} %get-tuple-element.105), channel_id=1, source_target_pairs={{0,14},{1,15},{2,12},{3,13},{4,10},{5,11},{6,8},{7,9},{8,6},{9,7},... | collective-permute-start | bytes 147464 | tf_op jit(solution)/shard_map/ppermute | solution.py:471
  70.7 5.9 %collective-permute-start.30 = (bf16[48,512]{1,0:T(8,128)(2,1)S(1)}, bf16[48,512]{1,0:T(8,128)(2,1)S(1)}, u32[]{:S(2)}, u32[]{:S(2)}) collective-permute-start(bf16[48,512]{1,0:T(8,128)(2,1)S(1)} %get-tuple-element.106), channel_id=1, source_target_pairs={{0,10},{1,11},{2,8},{3,9},{4,14},{5,15},{6,12},{7,13},{8,2},{9,3},... | collective-permute-start | bytes 147464 | tf_op jit(solution)/shard_map/ppermute | solution.py:471
  (14 other events, 56.3 us)

commit v26 on v25

--- a/solution.py
+++ b/solution.py
@@ -225,17 +225,20 @@
     window_copy.wait()
 
 
-def mix_kernel(window_ref, scaled_ref, projected_ref, part_ref, mixed_ref):
+def mix_kernel(window_ref, scaled_ref, mixed_ref):
+    columns = slice(scaled_ref.shape[1] - mixed_ref.shape[1], None)
+    mixed = jnp.dot(
+        window_ref[...], scaled_ref[:, columns], preferred_element_type=jnp.float32
+    )
+    mixed_ref[...] = mixed.astype(jnp.bfloat16)
+
+
+def most_kernel(window_ref, projected_ref, part_ref):
     part_ref[...] = jnp.dot(
         window_ref[...],
         projected_ref[...].astype(jnp.bfloat16),
         preferred_element_type=jnp.float32,
     )
-    columns = slice(scaled_ref.shape[1] - mixed_ref.shape[1], None)
-    mixed = jnp.dot(
-        window_ref[...], scaled_ref[:, columns], preferred_element_type=jnp.float32
-    )
-    mixed_ref[...] = mixed.astype(jnp.bfloat16)
 
 
 def window_kernel(scale, part_ref, mixed_ref, *refs):
@@ -428,21 +431,22 @@
         name="project",
     )(scaled, basis_out, *pieces)
 
-    projected, *last = after(projected, *last)
+    def product(kernel, shape, dtype, *operands):
+        return pl.pallas_call(
+            kernel,
+            out_shape=jax.ShapeDtypeStruct(shape, dtype),
+            in_specs=[VMEM] * len(operands),
+            out_specs=VMEM,
+            compiler_params=pltpu.CompilerParams(vmem_limit_bytes=24 * MIB),
+            cost_estimate=CHEAP,
+            name=kernel.__name__[:-7],
+        )(*operands)
+
+    mixed = product(mix_kernel, (WR, 2 * in_width), jnp.bfloat16, window, scaled)
+    projected, mixed, *last = after(projected, mixed, *last)
     last += [swap(piece, n) for piece in last]
+    part = product(most_kernel, (WR, WC), jnp.float32, window, projected)
     rows = WR // n
-    part, mixed = pl.pallas_call(
-        mix_kernel,
-        out_shape=(
-            jax.ShapeDtypeStruct((WR, WC), jnp.float32),
-            jax.ShapeDtypeStruct((WR, 2 * in_width), jnp.bfloat16),
-        ),
-        in_specs=[VMEM] * 3,
-        out_specs=(VMEM, VMEM),
-        compiler_params=pltpu.CompilerParams(vmem_limit_bytes=24 * MIB),
-        cost_estimate=CHEAP,
-        name="mix",
-    )(window, scaled, projected)
     send, keep = pl.pallas_call(
         functools.partial(window_kernel, 1.0 / tokens),
         out_shape=(

time: 78.5 us -> 78.5 us (level)
    pallas_call x1 -> x2, Pallas kernels: 1.79 us -> 1.94 us  [product(): pl.pallas_call(kernel, out_shape=jax.ShapeDtypeStruct(shape, dtype), in_s...]
  transfers between devices with their start and end apart: 34 -> 34, of which waited for: 12 -> 10; matrix products, arithmetic and copies ran while one was open for 1% -> 1% of each run, Pallas kernels for 31% -> 31%
where the time goes in v26:
time: 78.5 us; the launch traced here: 78.1 us
  starting transfers between devices  34.5 us (44%)
  Pallas kernels  25.7 us (33%)
  waiting for transfers between devices  13.7 us (17%)
  local copies, waits for them, and re-layouts  3.02 us (4%)
  other arithmetic  0.91 us (1%)
    ppermute x7, starting transfers between devices, ring_body(): lax.ppermute(x, 'blk', xor_pairs(n, 2 * key))  11.2 us
    pallas_call x2, Pallas kernels, ring_body(): pl.pallas_call(kernel, out_shape=jax.ShapeDtypeStruct(shape, dtype), in_s...  10.7 us
    pallas_call x1, Pallas kernels, ring_body(): pl.pallas_call(functools.partial(scale_kernel, begun), out_shape=jax.Shap...  6.22 us
    ppermute x4, starting transfers between devices, ring_body(): to_right = lambda x: lax.ppermute(x, 'blk', shift_pairs(n, 1))  5.95 us
    ppermute x3, starting transfers between devices, ring_body(): lax.ppermute(both, 'blk', xor_pairs(n, 4 * key))  5.68 us
    all_to_all x1, starting transfers between devices, exchange(): return lax.all_to_all(x, 'blk', 0, 0, axis_index_groups=groups, tiled=True)  4.33 us
    pallas_call x1, Pallas kernels, ring_body(): pl.pallas_call(functools.partial(project_kernel, (0, 6, len(pieces))), ou...  3.92 us
    ppermute x3, waiting for transfers between devices, ring_body(): lax.ppermute(both, 'blk', xor_pairs(n, 4 * key))  3.56 us
  transfers between devices with their start and end apart: 34, of which 10 were waited for; matrix products, arithmetic and copies ran while one was open for 1% of the time, Pallas kernels for 31%

profile of v26, /device:TPU:0, one launch (start us, length us, event | category | flops | bytes accessed | tf_op | source)
XLA Modules:
  0.0 78.1 jit_solution(2057426479196084717)
XLA Ops:
  0.9 3.1 %collective-permute-start = (bf16[1,2,18432]{2,1,0:T(2,128)(2,1)S(1)}, bf16[1,2,18432]{2,1,0:T(2,128)(2,1)S(1)}, u32[]{:S(2)}, u32[]{:S(2)}) collective-permute-start(bf16[1,2,18432]{2,1,0:T(2,128)(2,1)S(1)} %maximum_bitcast_fusion.refs_0_), channel_id=1, source_target_pairs={{0,4},{1,5},{2,6},{3,7},{4,0},{5,1},{6,2},{7,3},{8,12},{9,13},{10,... | collective-permute-start | bytes 221192 | tf_op jit(solution)/shard_map/ppermute | solution.py:298
  4.0 2.6 %collective-permute-start.1 = (bf16[1,2,18432]{2,1,0:T(2,128)(2,1)S(1)}, bf16[1,2,18432]{2,1,0:T(2,128)(2,1)S(1)}, u32[]{:S(2)}, u32[]{:S(2)}) collective-permute-start(bf16[1,2,18432]{2,1,0:T(2,128)(2,1)S(1)} %maximum_bitcast_fusion.refs_0_), channel_id=1, source_target_pairs={{0,8},{1,9},{2,10},{3,11},{4,12},{5,13},{6,14},{7,15},{8,0},{9,1},... | collective-permute-start | bytes 221192 | tf_op jit(solution)/shard_map/ppermute | solution.py:298
  6.6 1.6 %copy-done = bf16[4096,256]{1,0:T(8,128)(2,1)S(1)} copy-done((bf16[4096,256]{1,0:T(8,128)(2,1)S(1)}, bf16[4096,256]{1,0:T(8,128)(2,1)}, u32[]{:S(2)}) %copy-start) | copy-done | bytes 2097176
  9.3 2.5 %collective-permute-done.1.refs_2_ = bf16[1,2,18432]{2,1,0:T(2,128)(2,1)S(1)} collective-permute-done((bf16[1,2,18432]{2,1,0:T(2,128)(2,1)S(1)}, bf16[1,2,18432]{2,1,0:T(2,128)(2,1)S(1)}, u32[]{:S(2)}, u32[]{:S(2)}) %collective-permute-start.1) | collective-permute-done | bytes 73760 | tf_op jit(solution)/shard_map/ppermute | solution.py:298
  12.9 1.6 %collective-permute-start.4 = (bf16[4,2,4096]{2,1,0:T(2,128)(2,1)S(1)}, bf16[4,2,4096]{2,1,0:T(2,128)(2,1)S(1)}, u32[]{:S(2)}, u32[]{:S(2)}) collective-permute-start(bf16[4,2,4096]{2,1,0:T(2,128)(2,1)S(1)} %get-tuple-element.65), channel_id=1, source_target_pairs={{0,2},{1,3},{2,0},{3,1},{4,6},{5,7},{6,4},{7,5},{8,10},{9,11},{10,... | collective-permute-start | bytes 196616 | tf_op jit(solution)/shard_map/ppermute | solution.py:322
  15.1 2.9 %collective-permute-done.4 = bf16[4,2,4096]{2,1,0:T(2,128)(2,1)S(1)} collective-permute-done((bf16[4,2,4096]{2,1,0:T(2,128)(2,1)S(1)}, bf16[4,2,4096]{2,1,0:T(2,128)(2,1)S(1)}, u32[]{:S(2)}, u32[]{:S(2)}) %collective-permute-start.4) | collective-permute-done | bytes 65568 | tf_op jit(solution)/shard_map/ppermute | solution.py:322
  18.3 1.2 %collective-permute-done.5.far_ref = bf16[8,2,4096]{2,1,0:T(2,128)(2,1)S(1)} collective-permute-done((bf16[8,2,4096]{2,1,0:T(2,128)(2,1)S(1)}, bf16[8,2,4096]{2,1,0:T(2,128)(2,1)S(1)}, u32[]{:S(2)}, u32[]{:S(2)}) %collective-permute-start.5) | collective-permute-done | bytes 131104 | tf_op jit(solution)/shard_map/ppermute | solution.py:48
  19.4 1.2 %rotate_in.1 = bf16[8,32,256]{2,1,0:T(8,128)(2,1)} custom-call(bf16[8,2,4096]{2,1,0:T(2,128)(2,1)S(1)} %constant_dynamic-update-slice_fusion.near_ref, bf16[8,2,4096]{2,1,0:T(2,128)(2,1)S(1)} %collective-permute-done.5.far_ref, bf16[4096,256]{1,0:T(8,128)(2,1)S(1)} %keep.1.basis_ref), custom_call_target="tpu_custom_call" | custom-call | flops 1 | bytes 1 | tf_op jit(solution)/shard_map/rotate_in/pallas_call | solution.py:325
  21.1 1.1 %collective-permute-start.7 = (bf16[256,512]{1,0:T(8,128)(2,1)S(1)}, bf16[256,512]{1,0:T(8,128)(2,1)S(1)}, u32[]{:S(2)}, u32[]{:S(2)}) collective-permute-start(bf16[256,512]{1,0:T(8,128)(2,1)S(1)} %bitcast.3), channel_id=1, source_target_pairs={{0,4},{1,5},{4,8},{5,9},{8,12},{9,13},{12,14},{13,15},{14,10},{15,... | collective-permute-start | bytes 786440 | tf_op jit(solution)/shard_map/ppermute | solution.py:290
  23.1 4.3 %all-to-all-start = ((bf16[8,32,256]{2,1,0:T(8,128)(2,1)}), bf16[8,32,256]{2,1,0:T(8,128)(2,1)S(1)}, u32[]{:S(2)}, u32[]{:S(2)}) async-start(bf16[8,32,256]{2,1,0:T(8,128)(2,1)} %rotate_in.1), calls=%async_computation | async-start | bytes 262144 | tf_op jit(solution)/shard_map/all_to_all | solution.py:44
  27.4 4.2 %rotate_first.1.start_ref = f32[32,896]{1,0:T(8,128)S(1)} custom-call(bf16[8,2,14336]{2,1,0:T(2,128)(2,1)S(1)} %constant_dynamic-update-slice_fusion.2.near_ref, bf16[8,2,14336]{2,1,0:T(2,128)(2,1)S(1)} %collective-permute-done.6.far_ref, bf16[14336,896]{1,0:T(8,128)(2,1)} %basis_out_ref.1), custom_call_target="tpu_custom_call" | custom-call | flops 1 | bytes 1 | tf_op jit(solution)/shard_map/rotate_first/pallas_call | solution.py:342
  31.7 2.1 %collective-permute-start.10 = (bf16[256,512]{1,0:T(8,128)(2,1)S(1)}, bf16[256,512]{1,0:T(8,128)(2,1)S(1)}, u32[]{:S(2)}, u32[]{:S(2)}) collective-permute-start(bf16[256,512]{1,0:T(8,128)(2,1)S(1)} %collective-permute-done.7.refs_2_), channel_id=1, source_target_pairs={{0,4},{1,5},{4,8},{5,9},{8,12},{9,13},{12,14},{13,15},{14,10},{15,... | collective-permute-start | bytes 786440 | tf_op jit(solution)/shard_map/ppermute | solution.py:290
  35.2 6.6 %rotate_last.1.aligned_ref = bf16[896,32]{1,0:T(8,128)(2,1)S(1)} custom-call(bf16[8,2,14336]{2,1,0:T(2,128)(2,1)S(1)} %constant_dynamic-update-slice_fusion.2.near_ref, bf16[8,2,14336]{2,1,0:T(2,128)(2,1)S(1)} %collective-permute-done.6.far_ref, bf16[14336,896]{1,0:T(8,128)(2,1)} %basis_out_ref.1, s32[16]{0:T(128)S(1)} %copy-done.2, ...), custom_call_target="tpu_custom_call" | custom-call | flops 1 | bytes 1 | tf_op jit(solution)/shard_map/rotate_last/pallas_call | solution.py:342
  41.8 1.3 %collective-permute-start.15 = (bf16[256,512]{1,0:T(8,128)(2,1)S(1)}, bf16[256,512]{1,0:T(8,128)(2,1)S(1)}, u32[]{:S(2)}, u32[]{:S(2)}) collective-permute-start(bf16[256,512]{1,0:T(8,128)(2,1)S(1)} %collective-permute-done.10.refs_6_), channel_id=1, source_target_pairs={{0,4},{1,5},{4,8},{5,9},{8,12},{9,13},{12,14},{13,15},{14,10},{15,... | collective-permute-start | bytes 786440 | tf_op jit(solution)/shard_map/ppermute | solution.py:290
  44.4 6.2 %scale.1.scaled_ref = bf16[896,4096]{1,0:T(8,128)(2,1)S(1)} custom-call(bf16[896,32]{1,0:T(8,128)(2,1)S(1)} %rotate_last.1.aligned_ref, bf16[8,32,256]{2,1,0:T(8,128)(2,1)S(1)} %all-to-all-done.near_ref, bf16[8,32,256]{2,1,0:T(8,128)(2,1)S(1)} %collective-permute-done.12.far_ref, s32[32]{0:T(128)S(1)} %copy-done.1, f32[896,4096]{1,0:T(8,128)} %eigen_ref.1), custom_call_target="tpu_custom_call" | custom-call | flops 1 | bytes 1 | tf_op jit(solution)/shard_map/scale/pallas_call | solution.py:394
  51.9 1.5 %collective-permute-start.21 = (bf16[128,512]{1,0:T(8,128)(2,1)S(1)}, bf16[128,512]{1,0:T(8,128)(2,1)S(1)}, u32[]{:S(2)}, u32[]{:S(2)}) collective-permute-start(bf16[128,512]{1,0:T(8,128)(2,1)S(1)} %slice.10), channel_id=1, source_target_pairs={{0,4},{1,5},{4,8},{5,9},{8,12},{9,13},{12,14},{13,15},{14,10},{15,... | collective-permute-start | bytes 393224 | tf_op jit(solution)/shard_map/ppermute | solution.py:290
  54.0 3.9 %project.1 = (f32[896,512]{1,0:T(8,128)S(1)}, bf16[768,896]{1,0:T(8,128)(2,1)S(1)}) custom-call(bf16[896,4096]{1,0:T(8,128)(2,1)S(1)} %scale.1.scaled_ref, bf16[14336,896]{1,0:T(8,128)(2,1)} %basis_out_ref.1, bf16[256,512]{1,0:T(8,128)(2,1)S(1)} %bitcast.6, bf16[256,512]{1,0:T(8,128)(2,1)S(1)} %collective-permute-done.9.refs_1_, ...), custom_call_target="tpu_custom_call" | custom-call | flops 1 | bytes 1 | tf_op jit(solution)/shard_map/project/pallas_call | solution.py:417
  61.7 1.4 %collective-permute-done.25.got_ref = bf16[8,48,512]{2,1,0:T(8,128)(2,1)S(1)} collective-permute-done((bf16[8,48,512]{2,1,0:T(8,128)(2,1)S(1)}, bf16[8,48,512]{2,1,0:T(8,128)(2,1)S(1)}, u32[]{:S(2)}, u32[]{:S(2)}) %collective-permute-start.25) | collective-permute-done | bytes 393248 | tf_op jit(solution)/shard_map/ppermute | solution.py:48
  63.2 3.3 %collective-permute-start.26 = (bf16[48,512]{1,0:T(8,128)(2,1)S(1)}, bf16[48,512]{1,0:T(8,128)(2,1)S(1)}, u32[]{:S(2)}, u32[]{:S(2)}) collective-permute-start(bf16[48,512]{1,0:T(8,128)(2,1)S(1)} %get-tuple-element.100), channel_id=1, source_target_pairs={{0,12},{1,13},{2,14},{3,15},{4,8},{5,9},{6,10},{7,11},{8,4},{9,5},... | collective-permute-start | bytes 147464 | tf_op jit(solution)/shard_map/ppermute | solution.py:475
  66.5 1.1 %collective-permute-start.28 = (bf16[48,512]{1,0:T(8,128)(2,1)S(1)}, bf16[48,512]{1,0:T(8,128)(2,1)S(1)}, u32[]{:S(2)}, u32[]{:S(2)}) collective-permute-start(bf16[48,512]{1,0:T(8,128)(2,1)S(1)} %get-tuple-element.102), channel_id=1, source_target_pairs={{0,4},{1,5},{2,6},{3,7},{4,0},{5,1},{6,2},{7,3},{8,12},{9,13},{10,... | collective-permute-start | bytes 147464 | tf_op jit(solution)/shard_map/ppermute | solution.py:475
  67.7 3.3 %collective-permute-start.29 = (bf16[48,512]{1,0:T(8,128)(2,1)S(1)}, bf16[48,512]{1,0:T(8,128)(2,1)S(1)}, u32[]{:S(2)}, u32[]{:S(2)}) collective-permute-start(bf16[48,512]{1,0:T(8,128)(2,1)S(1)} %get-tuple-element.103), channel_id=1, source_target_pairs={{0,14},{1,15},{2,12},{3,13},{4,10},{5,11},{6,8},{7,9},{8,6},{9,7},... | collective-permute-start | bytes 147464 | tf_op jit(solution)/shard_map/ppermute | solution.py:475
  70.9 2.4 %collective-permute-start.31 = (bf16[48,512]{1,0:T(8,128)(2,1)S(1)}, bf16[48,512]{1,0:T(8,128)(2,1)S(1)}, u32[]{:S(2)}, u32[]{:S(2)}) collective-permute-start(bf16[48,512]{1,0:T(8,128)(2,1)S(1)} %get-tuple-element.105), channel_id=1, source_target_pairs={{0,6},{1,7},{2,4},{3,5},{4,2},{5,3},{6,0},{7,1},{8,14},{9,15},{10,... | collective-permute-start | bytes 147464 | tf_op jit(solution)/shard_map/ppermute | solution.py:475
  73.3 1.1 %collective-permute-start.32 = (bf16[48,512]{1,0:T(8,128)(2,1)S(1)}, bf16[48,512]{1,0:T(8,128)(2,1)S(1)}, u32[]{:S(2)}, u32[]{:S(2)}) collective-permute-start(bf16[48,512]{1,0:T(8,128)(2,1)S(1)} %get-tuple-element.106), channel_id=1, source_target_pairs={{0,2},{1,3},{2,0},{3,1},{4,6},{5,7},{6,4},{7,5},{8,10},{9,11},{10,... | collective-permute-start | bytes 147464 | tf_op jit(solution)/shard_map/ppermute | solution.py:475
  74.6 2.2 %collective-permute-done.30.refs_4_ = bf16[48,512]{1,0:T(8,128)(2,1)S(1)} collective-permute-done((bf16[48,512]{1,0:T(8,128)(2,1)S(1)}, bf16[48,512]{1,0:T(8,128)(2,1)S(1)}, u32[]{:S(2)}, u32[]{:S(2)}) %collective-permute-start.30) | collective-permute-done | bytes 49184 | tf_op jit(solution)/shard_map/ppermute | solution.py:475
  (72 shorter events, 15.3 us)
Async XLA Ops:
  0.9 8.4 %collective-permute-start = (bf16[1,2,18432]{2,1,0:T(2,128)(2,1)S(1)}, bf16[1,2,18432]{2,1,0:T(2,128)(2,1)S(1)}, u32[]{:S(2)}, u32[]{:S(2)}) collective-permute-start(bf16[1,2,18432]{2,1,0:T(2,128)(2,1)S(1)} %maximum_bitcast_fusion.refs_0_), channel_id=1, source_target_pairs={{0,4},{1,5},{2,6},{3,7},{4,0},{5,1},{6,2},{7,3},{8,12},{9,13},{10,... | collective-permute-start | bytes 221192 | tf_op jit(solution)/shard_map/ppermute | solution.py:298
  4.0 7.8 %collective-permute-start.1 = (bf16[1,2,18432]{2,1,0:T(2,128)(2,1)S(1)}, bf16[1,2,18432]{2,1,0:T(2,128)(2,1)S(1)}, u32[]{:S(2)}, u32[]{:S(2)}) collective-permute-start(bf16[1,2,18432]{2,1,0:T(2,128)(2,1)S(1)} %maximum_bitcast_fusion.refs_0_), channel_id=1, source_target_pairs={{0,8},{1,9},{2,10},{3,11},{4,12},{5,13},{6,14},{7,15},{8,0},{9,1},... | collective-permute-start | bytes 221192 | tf_op jit(solution)/shard_map/ppermute | solution.py:298
  6.6 6.3 %collective-permute-start.2 = (bf16[1,2,18432]{2,1,0:T(2,128)(2,1)S(1)}, bf16[1,2,18432]{2,1,0:T(2,128)(2,1)S(1)}, u32[]{:S(2)}, u32[]{:S(2)}) collective-permute-start(bf16[1,2,18432]{2,1,0:T(2,128)(2,1)S(1)} %maximum_bitcast_fusion.refs_0_), channel_id=1, source_target_pairs={{0,12},{1,13},{2,14},{3,15},{4,8},{5,9},{6,10},{7,11},{8,4},{9,5},... | collective-permute-start | bytes 221192 | tf_op jit(solution)/shard_map/ppermute | solution.py:298
  14.5 6.2 %collective-permute-start.3 = (bf16[4,2,14336]{2,1,0:T(2,128)(2,1)S(1)}, bf16[4,2,14336]{2,1,0:T(2,128)(2,1)S(1)}, u32[]{:S(2)}, u32[]{:S(2)}) collective-permute-start(bf16[4,2,14336]{2,1,0:T(2,128)(2,1)S(1)} %get-tuple-element.63), channel_id=1, source_target_pairs={{0,2},{1,3},{2,0},{3,1},{4,6},{5,7},{6,4},{7,5},{8,10},{9,11},{10,... | collective-permute-start | bytes 688136 | tf_op jit(solution)/shard_map/ppermute | solution.py:323
  20.8 6.6 %collective-permute-start.6 = (bf16[8,2,14336]{2,1,0:T(2,128)(2,1)S(1)}, bf16[8,2,14336]{2,1,0:T(2,128)(2,1)S(1)}, u32[]{:S(2)}, u32[]{:S(2)}) collective-permute-start(bf16[8,2,14336]{2,1,0:T(2,128)(2,1)S(1)} %constant_dynamic-update-slice_fusion.2.near_ref), channel_id=1, source_target_pairs={{0,1},{1,0},{2,3},{3,2},{4,5},{5,4},{6,7},{7,6},{8,9},{9,8},{10,11... | collective-permute-start | bytes 1376264 | tf_op jit(solution)/shard_map/ppermute | solution.py:48
  21.1 10.6 %collective-permute-start.7 = (bf16[256,512]{1,0:T(8,128)(2,1)S(1)}, bf16[256,512]{1,0:T(8,128)(2,1)S(1)}, u32[]{:S(2)}, u32[]{:S(2)}) collective-permute-start(bf16[256,512]{1,0:T(8,128)(2,1)S(1)} %bitcast.3), channel_id=1, source_target_pairs={{0,4},{1,5},{4,8},{5,9},{8,12},{9,13},{12,14},{13,15},{14,10},{15,... | collective-permute-start | bytes 786440 | tf_op jit(solution)/shard_map/ppermute | solution.py:290
  22.2 9.5 %collective-permute-start.8 = (bf16[256,512]{1,0:T(8,128)(2,1)S(1)}, bf16[256,512]{1,0:T(8,128)(2,1)S(1)}, u32[]{:S(2)}, u32[]{:S(2)}) collective-permute-start(bf16[256,512]{1,0:T(8,128)(2,1)S(1)} %bitcast.4), channel_id=1, source_target_pairs={{0,2},{1,3},{4,0},{5,1},{8,4},{9,5},{12,8},{13,9},{14,12},{15,13},... | collective-permute-start | bytes 786440 | tf_op jit(solution)/shard_map/ppermute | solution.py:291
  23.1 8.5 %collective-permute-start.9 = (bf16[256,512]{1,0:T(8,128)(2,1)S(1)}, bf16[256,512]{1,0:T(8,128)(2,1)S(1)}, u32[]{:S(2)}, u32[]{:S(2)}) collective-permute-start(bf16[256,512]{1,0:T(8,128)(2,1)S(1)} %bitcast.5), channel_id=1, source_target_pairs={{0,1},{1,0},{2,3},{3,2},{4,5},{5,4},{6,7},{7,6},{8,9},{9,8},{10,11... | collective-permute-start | bytes 786440 | tf_op jit(solution)/shard_map/ppermute | solution.py:48
  23.1 12.1 %all-to-all-start = ((bf16[8,32,256]{2,1,0:T(8,128)(2,1)}), bf16[8,32,256]{2,1,0:T(8,128)(2,1)S(1)}, u32[]{:S(2)}, u32[]{:S(2)}) async-start(bf16[8,32,256]{2,1,0:T(8,128)(2,1)} %rotate_in.1), calls=%async_computation | async-start | bytes 262144 | tf_op jit(solution)/shard_map/all_to_all | solution.py:44
  31.7 10.1 %collective-permute-start.10 = (bf16[256,512]{1,0:T(8,128)(2,1)S(1)}, bf16[256,512]{1,0:T(8,128)(2,1)S(1)}, u32[]{:S(2)}, u32[]{:S(2)}) collective-permute-start(bf16[256,512]{1,0:T(8,128)(2,1)S(1)} %collective-permute-done.7.refs_2_), channel_id=1, source_target_pairs={{0,4},{1,5},{4,8},{5,9},{8,12},{9,13},{12,14},{13,15},{14,10},{15,... | collective-permute-start | bytes 786440 | tf_op jit(solution)/shard_map/ppermute | solution.py:290
  33.7 8.1 %collective-permute-start.11 = (bf16[256,512]{1,0:T(8,128)(2,1)S(1)}, bf16[256,512]{1,0:T(8,128)(2,1)S(1)}, u32[]{:S(2)}, u32[]{:S(2)}) collective-permute-start(bf16[256,512]{1,0:T(8,128)(2,1)S(1)} %collective-permute-done.8.refs_4_), channel_id=1, source_target_pairs={{0,2},{1,3},{4,0},{5,1},{8,4},{9,5},{12,8},{13,9},{14,12},{15,13},... | collective-permute-start | bytes 786440 | tf_op jit(solution)/shard_map/ppermute | solution.py:291
  33.8 8.0 %collective-permute-start.13 = (bf16[256,512]{1,0:T(8,128)(2,1)S(1)}, bf16[256,512]{1,0:T(8,128)(2,1)S(1)}, u32[]{:S(2)}, u32[]{:S(2)}) collective-permute-start(bf16[256,512]{1,0:T(8,128)(2,1)S(1)} %collective-permute-done.7.refs_2_), channel_id=1, source_target_pairs={{0,1},{1,0},{2,3},{3,2},{4,5},{5,4},{6,7},{7,6},{8,9},{9,8},{10,11... | collective-permute-start | bytes 786440 | tf_op jit(solution)/shard_map/ppermute | solution.py:48
  33.8 8.0 %collective-permute-start.14 = (bf16[256,512]{1,0:T(8,128)(2,1)S(1)}, bf16[256,512]{1,0:T(8,128)(2,1)S(1)}, u32[]{:S(2)}, u32[]{:S(2)}) collective-permute-start(bf16[256,512]{1,0:T(8,128)(2,1)S(1)} %collective-permute-done.8.refs_4_), channel_id=1, source_target_pairs={{0,1},{1,0},{2,3},{3,2},{4,5},{5,4},{6,7},{7,6},{8,9},{9,8},{10,11... | collective-permute-start | bytes 786440 | tf_op jit(solution)/shard_map/ppermute | solution.py:48
  35.2 6.6 %collective-permute-start.12 = (bf16[8,32,256]{2,1,0:T(8,128)(2,1)S(1)}, bf16[8,32,256]{2,1,0:T(8,128)(2,1)S(1)}, u32[]{:S(2)}, u32[]{:S(2)}) collective-permute-start(bf16[8,32,256]{2,1,0:T(8,128)(2,1)S(1)} %all-to-all-done.near_ref), channel_id=1, source_target_pairs={{0,1},{1,0},{2,3},{3,2},{4,5},{5,4},{6,7},{7,6},{8,9},{9,8},{10,11... | collective-permute-start | bytes 393224 | tf_op jit(solution)/shard_map/ppermute | solution.py:48
  41.8 8.8 %collective-permute-start.15 = (bf16[256,512]{1,0:T(8,128)(2,1)S(1)}, bf16[256,512]{1,0:T(8,128)(2,1)S(1)}, u32[]{:S(2)}, u32[]{:S(2)}) collective-permute-start(bf16[256,512]{1,0:T(8,128)(2,1)S(1)} %collective-permute-done.10.refs_6_), channel_id=1, source_target_pairs={{0,4},{1,5},{4,8},{5,9},{8,12},{9,13},{12,14},{13,15},{14,10},{15,... | collective-permute-start | bytes 786440 | tf_op jit(solution)/shard_map/ppermute | solution.py:290
  43.1 8.3 %collective-permute-start.16 = (bf16[256,512]{1,0:T(8,128)(2,1)S(1)}, bf16[256,512]{1,0:T(8,128)(2,1)S(1)}, u32[]{:S(2)}, u32[]{:S(2)}) collective-permute-start(bf16[256,512]{1,0:T(8,128)(2,1)S(1)} %collective-permute-done.11.refs_8_), channel_id=1, source_target_pairs={{0,2},{1,3},{4,0},{5,1},{8,4},{9,5},{12,8},{13,9},{14,12},{15,13},... | collective-permute-start | bytes 786440 | tf_op jit(solution)/shard_map/ppermute | solution.py:291
  43.9 7.5 %collective-permute-start.17 = (bf16[256,512]{1,0:T(8,128)(2,1)S(1)}, bf16[256,512]{1,0:T(8,128)(2,1)S(1)}, u32[]{:S(2)}, u32[]{:S(2)}) collective-permute-start(bf16[256,512]{1,0:T(8,128)(2,1)S(1)} %collective-permute-done.10.refs_6_), channel_id=1, source_target_pairs={{0,1},{1,0},{2,3},{3,2},{4,5},{5,4},{6,7},{7,6},{8,9},{9,8},{10,11... | collective-permute-start | bytes 786440 | tf_op jit(solution)/shard_map/ppermute | solution.py:48
  43.9 7.5 %collective-permute-start.18 = (bf16[256,512]{1,0:T(8,128)(2,1)S(1)}, bf16[256,512]{1,0:T(8,128)(2,1)S(1)}, u32[]{:S(2)}, u32[]{:S(2)}) collective-permute-start(bf16[256,512]{1,0:T(8,128)(2,1)S(1)} %collective-permute-done.11.refs_8_), channel_id=1, source_target_pairs={{0,1},{1,0},{2,3},{3,2},{4,5},{5,4},{6,7},{7,6},{8,9},{9,8},{10,11... | collective-permute-start | bytes 786440 | tf_op jit(solution)/shard_map/ppermute | solution.py:48
  51.9 7.0 %collective-permute-start.21 = (bf16[128,512]{1,0:T(8,128)(2,1)S(1)}, bf16[128,512]{1,0:T(8,128)(2,1)S(1)}, u32[]{:S(2)}, u32[]{:S(2)}) collective-permute-start(bf16[128,512]{1,0:T(8,128)(2,1)S(1)} %slice.10), channel_id=1, source_target_pairs={{0,4},{1,5},{4,8},{5,9},{8,12},{9,13},{12,14},{13,15},{14,10},{15,... | collective-permute-start | bytes 393224 | tf_op jit(solution)/shard_map/ppermute | solution.py:290
  63.2 7.7 %collective-permute-start.26 = (bf16[48,512]{1,0:T(8,128)(2,1)S(1)}, bf16[48,512]{1,0:T(8,128)(2,1)S(1)}, u32[]{:S(2)}, u32[]{:S(2)}) collective-permute-start(bf16[48,512]{1,0:T(8,128)(2,1)S(1)} %get-tuple-element.100), channel_id=1, source_target_pairs={{0,12},{1,13},{2,14},{3,15},{4,8},{5,9},{6,10},{7,11},{8,4},{9,5},... | collective-permute-start | bytes 147464 | tf_op jit(solution)/shard_map/ppermute | solution.py:475
  66.5 6.8 %collective-permute-start.27 = (bf16[48,512]{1,0:T(8,128)(2,1)S(1)}, bf16[48,512]{1,0:T(8,128)(2,1)S(1)}, u32[]{:S(2)}, u32[]{:S(2)}) collective-permute-start(bf16[48,512]{1,0:T(8,128)(2,1)S(1)} %get-tuple-element.101), channel_id=1, source_target_pairs={{0,8},{1,9},{2,10},{3,11},{4,12},{5,13},{6,14},{7,15},{8,0},{9,1},... | collective-permute-start | bytes 147464 | tf_op jit(solution)/shard_map/ppermute | solution.py:475
  66.5 7.9 %collective-permute-start.28 = (bf16[48,512]{1,0:T(8,128)(2,1)S(1)}, bf16[48,512]{1,0:T(8,128)(2,1)S(1)}, u32[]{:S(2)}, u32[]{:S(2)}) collective-permute-start(bf16[48,512]{1,0:T(8,128)(2,1)S(1)} %get-tuple-element.102), channel_id=1, source_target_pairs={{0,4},{1,5},{2,6},{3,7},{4,0},{5,1},{6,2},{7,3},{8,12},{9,13},{10,... | collective-permute-start | bytes 147464 | tf_op jit(solution)/shard_map/ppermute | solution.py:475
  67.7 7.0 %collective-permute-start.29 = (bf16[48,512]{1,0:T(8,128)(2,1)S(1)}, bf16[48,512]{1,0:T(8,128)(2,1)S(1)}, u32[]{:S(2)}, u32[]{:S(2)}) collective-permute-start(bf16[48,512]{1,0:T(8,128)(2,1)S(1)} %get-tuple-element.103), channel_id=1, source_target_pairs={{0,14},{1,15},{2,12},{3,13},{4,10},{5,11},{6,8},{7,9},{8,6},{9,7},... | collective-permute-start | bytes 147464 | tf_op jit(solution)/shard_map/ppermute | solution.py:475
  70.9 5.9 %collective-permute-start.30 = (bf16[48,512]{1,0:T(8,128)(2,1)S(1)}, bf16[48,512]{1,0:T(8,128)(2,1)S(1)}, u32[]{:S(2)}, u32[]{:S(2)}) collective-permute-start(bf16[48,512]{1,0:T(8,128)(2,1)S(1)} %get-tuple-element.104), channel_id=1, source_target_pairs={{0,10},{1,11},{2,8},{3,9},{4,14},{5,15},{6,12},{7,13},{8,2},{9,3},... | collective-permute-start | bytes 147464 | tf_op jit(solution)/shard_map/ppermute | solution.py:475
  (14 other events, 55.2 us)

commit v27 on v21

--- a/solution.py
+++ b/solution.py
@@ -201,18 +201,14 @@
                 out_ref[rows, tile * LANES : (tile + 1) * LANES] = scaled.astype(jnp.bfloat16)
 
 
-def project_kernel(cuts, scaled_ref, basis_out_ref, *refs):
-    pieces = refs[:-4]
-    out_ref, window_ref, basis, sem = refs[-4:]
+def project_kernel(cuts, scaled_ref, *refs):
+    pieces = refs[:-3]
+    out_ref, basis, sem = refs[-3:]
     width = pieces[0].shape[0]
     copies = [
         pltpu.make_async_copy(piece, basis.at[pl.ds(at * width, width)], sem.at[at])
         for at, piece in enumerate(pieces)
     ]
-    window_copy = pltpu.make_async_copy(
-        basis_out_ref.at[pl.ds(0, window_ref.shape[0])], window_ref, sem.at[len(pieces)]
-    )
-    window_copy.start()
     for copy in copies:
         copy.start()
     for first, last in zip(cuts[:-1], cuts[1:]):
@@ -222,21 +218,33 @@
         part = jnp.dot(scaled_ref[:, deep], basis[deep, :], preferred_element_type=jnp.float32)
         out_ref[...] = part if first == 0 else out_ref[...] + part
 
-    window_copy.wait()
-
-
-def window_kernel(scale, window_ref, scaled_ref, projected_ref, *refs):
+
+def mix_kernel(basis_out_ref, scaled_ref, window_ref, near_ref, far_ref, sem):
+    copy = pltpu.make_async_copy(
+        basis_out_ref.at[pl.ds(0, window_ref.shape[0])], window_ref, sem.at[0]
+    )
+    copy.start()
+    copy.wait()
+    width = near_ref.shape[1]
+    first = scaled_ref.shape[1] - 2 * width
+    mixed = jnp.dot(window_ref[...], scaled_ref[:, first:], preferred_element_type=jnp.float32)
+    near_ref[...] = mixed[:, :width].astype(jnp.bfloat16)
+    far_ref[...] = mixed[:, width:].astype(jnp.bfloat16)
+
+
+def window_kernel(scale, window_ref, projected_ref, near_ref, got_ref, *refs):
     pieces = refs[:-3]
     send_ref, keep_ref, result = refs[-3:]
     chips, rows, _ = keep_ref.shape
-    width = pieces[0].shape[0]
-    total = projected_ref[...]
-    first = scaled_ref.shape[1] - width * len(pieces)
     basis = jnp.concatenate([piece[...] for piece in pieces], axis=0)
-    total += jnp.dot(scaled_ref[:, first:], basis, preferred_element_type=jnp.float32)
-    result[...] = scale * jnp.dot(
-        window_ref[...], total.astype(jnp.bfloat16), preferred_element_type=jnp.float32
-    )
+    mixed = near_ref[...].astype(jnp.float32) + got_ref[...].astype(jnp.float32)
+    total = jnp.dot(
+        window_ref[...],
+        projected_ref[...].astype(jnp.bfloat16),
+        preferred_element_type=jnp.float32,
+    )
+    total += jnp.dot(mixed.astype(jnp.bfloat16), basis, preferred_element_type=jnp.float32)
+    result[...] = scale * total
     core = lax.rem(lax.axis_index("blk"), 2)
     for k in range(chips):
         mine = pl.ds(pl.multiple_of((2 * k + core) * rows, rows), rows)
@@ -396,31 +404,42 @@
         name="scale",
     )(aligned, rotated, rotated_far, tile_order, eigenvalues)
 
-    scaled, right[-1], left[-1], *far = after(scaled, right[-1], left[-1], *far)
+    mix = (WR, in_width)
+    window, mixed, mixed_far = pl.pallas_call(
+        mix_kernel,
+        out_shape=tuple(
+            jax.ShapeDtypeStruct(shape, jnp.bfloat16) for shape in ((WR, tile_width), mix, mix)
+        ),
+        in_specs=[ANY, VMEM],
+        out_specs=(VMEM,) * 3,
+        scratch_shapes=[pltpu.SemaphoreType.DMA((1,))],
+        compiler_params=pltpu.CompilerParams(vmem_limit_bytes=40 * MIB),
+        cost_estimate=CHEAP,
+        name="mix",
+    )(basis_out, scaled)
+    scaled, mixed, mixed_far, right[-1], left[-1], *far = after(
+        scaled, mixed, mixed_far, right[-1], left[-1], *far
+    )
+    mixed_got = swap(mixed_far, n)
     cut = in_width // 2
     last = [to_right(right[-1][:cut]), to_left(left[-1][cut:])]
     near = [right[at] if at < steps else left[chips - at] for at in begun[:-1]]
     far += [swap(piece, n) for piece in near[len(far) :]]
     pieces = [piece for pair in zip(near, far) for piece in pair]
-    projected, window = pl.pallas_call(
+    projected = pl.pallas_call(
         functools.partial(project_kernel, (0, 6, len(pieces))),
-        out_shape=(
-            jax.ShapeDtypeStruct((tile_width, WC), jnp.float32),
-            jax.ShapeDtypeStruct((WR, tile_width), jnp.bfloat16),
-        ),
-        in_specs=[VMEM] + [ANY] * (len(pieces) + 1),
-        out_specs=(VMEM, VMEM),
+        out_shape=jax.ShapeDtypeStruct((tile_width, WC), jnp.float32),
+        in_specs=[VMEM] + [ANY] * len(pieces),
+        out_specs=VMEM,
         scratch_shapes=[
             pltpu.VMEM((len(pieces) * in_width, WC), jnp.bfloat16),
-            pltpu.SemaphoreType.DMA((len(pieces) + 1,)),
+            pltpu.SemaphoreType.DMA((len(pieces),)),
         ],
         compiler_params=pltpu.CompilerParams(vmem_limit_bytes=24 * MIB),
         cost_estimate=CHEAP,
         name="project",
-    )(scaled, basis_out, *pieces)
-
-    projected, *last = after(projected, *last)
-    last += [swap(piece, n) for piece in last]
+    )(scaled, *pieces)
+
     rows = WR // n
     send, keep = pl.pallas_call(
         functools.partial(window_kernel, 1.0 / tokens),
@@ -428,13 +447,13 @@
             jax.ShapeDtypeStruct((chips, rows, WC), jnp.bfloat16),
             jax.ShapeDtypeStruct((chips, rows, WC), jnp.float32),
         ),
-        in_specs=[VMEM] * 7,
+        in_specs=[VMEM] * 6,
         out_specs=(VMEM, VMEM),
         scratch_shapes=[pltpu.VMEM((WR, WC), jnp.float32)],
         compiler_params=pltpu.CompilerParams(vmem_limit_bytes=24 * MIB),
         cost_estimate=CHEAP,
         name="window",
-    )(window, scaled, projected, *last)
+    )(window, projected, mixed, mixed_got, *last)
 
     keys = [*range(chips - 2, 0, -2), *range(chips - 1, 0, -2)]
     small = pltpu.CompilerParams(vmem_limit_bytes=8 * MIB)

time: 78.6 us -> 78.8 us (level)
  Pallas kernels: 24.6 us -> 26.6 us
  waiting for transfers between devices: 15 us -> 14 us
    pallas_call x0 -> x1, Pallas kernels: none -> 2.33 us  [ring_body(): pl.pallas_call(mix_kernel, out_shape=tuple((jax.ShapeDtypeStruct(shape, j...]
    ppermute x13 -> x12, starting transfers between devices: 2.74 us -> 2.03 us  [swap(): return lax.ppermute(x, 'blk', xor_pairs(n, 1))]
    ppermute x13 -> x12, waiting for transfers between devices: 3.59 us -> 2.9 us  [swap(): return lax.ppermute(x, 'blk', xor_pairs(n, 1))]
  transfers between devices with their start and end apart: 34 -> 33, of which waited for: 13 -> 10; matrix products, arithmetic and copies ran while one was open for 1% -> 1% of each run, Pallas kernels for 28% -> 31%
where the time goes in v27:
time: 78.8 us; the launch traced here: 78.5 us
  starting transfers between devices  33.7 us (43%)
  Pallas kernels  26.6 us (34%)
  waiting for transfers between devices  14 us (18%)
  local copies, waits for them, and re-layouts  3.02 us (4%)
  other arithmetic  0.91 us (1%)
    ppermute x7, starting transfers between devices, ring_body(): lax.ppermute(x, 'blk', xor_pairs(n, 2 * key))  11.2 us
    pallas_call x2, Pallas kernels, ring_body(): pl.pallas_call(kernel, out_shape=jax.ShapeDtypeStruct(shape, dtype), in_s...  10.7 us
    pallas_call x1, Pallas kernels, ring_body(): pl.pallas_call(functools.partial(scale_kernel, begun), out_shape=jax.Shap...  6.16 us
    ppermute x4, starting transfers between devices, ring_body(): to_right = lambda x: lax.ppermute(x, 'blk', shift_pairs(n, 1))  5.74 us
    ppermute x3, starting transfers between devices, ring_body(): lax.ppermute(both, 'blk', xor_pairs(n, 4 * key))  5.68 us
    all_to_all x1, starting transfers between devices, exchange(): return lax.all_to_all(x, 'blk', 0, 0, axis_index_groups=groups, tiled=True)  4.33 us
    pallas_call x1, Pallas kernels, ring_body(): pl.pallas_call(functools.partial(project_kernel, (0, 6, len(pieces))), ou...  3.91 us
    ppermute x3, waiting for transfers between devices, ring_body(): lax.ppermute(both, 'blk', xor_pairs(n, 4 * key))  3.56 us
  transfers between devices with their start and end apart: 33, of which 10 were waited for; matrix products, arithmetic and copies ran while one was open for 1% of the time, Pallas kernels for 31%

profile of v27, /device:TPU:0, one launch (start us, length us, event | category | flops | bytes accessed | tf_op | source)
XLA Modules:
  0.0 78.5 jit_solution(2276337279995210978)
XLA Ops:
  0.9 3.1 %collective-permute-start = (bf16[1,2,18432]{2,1,0:T(2,128)(2,1)S(1)}, bf16[1,2,18432]{2,1,0:T(2,128)(2,1)S(1)}, u32[]{:S(2)}, u32[]{:S(2)}) collective-permute-start(bf16[1,2,18432]{2,1,0:T(2,128)(2,1)S(1)} %maximum_bitcast_fusion.refs_0_), channel_id=1, source_target_pairs={{0,4},{1,5},{2,6},{3,7},{4,0},{5,1},{6,2},{7,3},{8,12},{9,13},{10,... | collective-permute-start | bytes 221192 | tf_op jit(solution)/shard_map/ppermute | solution.py:294
  4.0 2.6 %collective-permute-start.1 = (bf16[1,2,18432]{2,1,0:T(2,128)(2,1)S(1)}, bf16[1,2,18432]{2,1,0:T(2,128)(2,1)S(1)}, u32[]{:S(2)}, u32[]{:S(2)}) collective-permute-start(bf16[1,2,18432]{2,1,0:T(2,128)(2,1)S(1)} %maximum_bitcast_fusion.refs_0_), channel_id=1, source_target_pairs={{0,8},{1,9},{2,10},{3,11},{4,12},{5,13},{6,14},{7,15},{8,0},{9,1},... | collective-permute-start | bytes 221192 | tf_op jit(solution)/shard_map/ppermute | solution.py:294
  6.6 1.6 %copy-done = bf16[4096,256]{1,0:T(8,128)(2,1)S(1)} copy-done((bf16[4096,256]{1,0:T(8,128)(2,1)S(1)}, bf16[4096,256]{1,0:T(8,128)(2,1)}, u32[]{:S(2)}) %copy-start) | copy-done | bytes 2097176
  9.3 2.5 %collective-permute-done.1.refs_2_ = bf16[1,2,18432]{2,1,0:T(2,128)(2,1)S(1)} collective-permute-done((bf16[1,2,18432]{2,1,0:T(2,128)(2,1)S(1)}, bf16[1,2,18432]{2,1,0:T(2,128)(2,1)S(1)}, u32[]{:S(2)}, u32[]{:S(2)}) %collective-permute-start.1) | collective-permute-done | bytes 73760 | tf_op jit(solution)/shard_map/ppermute | solution.py:294
  12.9 1.6 %collective-permute-start.4 = (bf16[4,2,4096]{2,1,0:T(2,128)(2,1)S(1)}, bf16[4,2,4096]{2,1,0:T(2,128)(2,1)S(1)}, u32[]{:S(2)}, u32[]{:S(2)}) collective-permute-start(bf16[4,2,4096]{2,1,0:T(2,128)(2,1)S(1)} %get-tuple-element.64), channel_id=1, source_target_pairs={{0,2},{1,3},{2,0},{3,1},{4,6},{5,7},{6,4},{7,5},{8,10},{9,11},{10,... | collective-permute-start | bytes 196616 | tf_op jit(solution)/shard_map/ppermute | solution.py:318
  15.1 2.9 %collective-permute-done.4 = bf16[4,2,4096]{2,1,0:T(2,128)(2,1)S(1)} collective-permute-done((bf16[4,2,4096]{2,1,0:T(2,128)(2,1)S(1)}, bf16[4,2,4096]{2,1,0:T(2,128)(2,1)S(1)}, u32[]{:S(2)}, u32[]{:S(2)}) %collective-permute-start.4) | collective-permute-done | bytes 65568 | tf_op jit(solution)/shard_map/ppermute | solution.py:318
  19.4 1.2 %rotate_in.1 = bf16[8,32,256]{2,1,0:T(8,128)(2,1)} custom-call(bf16[8,2,4096]{2,1,0:T(2,128)(2,1)S(1)} %constant_dynamic-update-slice_fusion.near_ref, bf16[8,2,4096]{2,1,0:T(2,128)(2,1)S(1)} %collective-permute-done.5.far_ref, bf16[4096,256]{1,0:T(8,128)(2,1)S(1)} %keep.1.basis_ref), custom_call_target="tpu_custom_call" | custom-call | flops 1 | bytes 1 | tf_op jit(solution)/shard_map/rotate_in/pallas_call | solution.py:321
  23.1 4.3 %all-to-all-start = ((bf16[8,32,256]{2,1,0:T(8,128)(2,1)}), bf16[8,32,256]{2,1,0:T(8,128)(2,1)S(1)}, u32[]{:S(2)}, u32[]{:S(2)}) async-start(bf16[8,32,256]{2,1,0:T(8,128)(2,1)} %rotate_in.1), calls=%async_computation | async-start | bytes 262144 | tf_op jit(solution)/shard_map/all_to_all | solution.py:44
  27.4 4.2 %rotate_first.1.start_ref = f32[32,896]{1,0:T(8,128)S(1)} custom-call(bf16[8,2,14336]{2,1,0:T(2,128)(2,1)S(1)} %constant_dynamic-update-slice_fusion.2.near_ref, bf16[8,2,14336]{2,1,0:T(2,128)(2,1)S(1)} %collective-permute-done.6.far_ref, bf16[14336,896]{1,0:T(8,128)(2,1)} %basis_out_ref.1), custom_call_target="tpu_custom_call" | custom-call | flops 1 | bytes 1 | tf_op jit(solution)/shard_map/rotate_first/pallas_call | solution.py:338
  31.7 2.1 %collective-permute-start.10 = (bf16[256,512]{1,0:T(8,128)(2,1)S(1)}, bf16[256,512]{1,0:T(8,128)(2,1)S(1)}, u32[]{:S(2)}, u32[]{:S(2)}) collective-permute-start(bf16[256,512]{1,0:T(8,128)(2,1)S(1)} %collective-permute-done.7.refs_2_), channel_id=1, source_target_pairs={{0,4},{1,5},{4,8},{5,9},{8,12},{9,13},{12,14},{13,15},{14,10},{15,... | collective-permute-start | bytes 786440 | tf_op jit(solution)/shard_map/ppermute | solution.py:286
  35.2 6.6 %rotate_last.1.aligned_ref = bf16[896,32]{1,0:T(8,128)(2,1)S(1)} custom-call(bf16[8,2,14336]{2,1,0:T(2,128)(2,1)S(1)} %constant_dynamic-update-slice_fusion.2.near_ref, bf16[8,2,14336]{2,1,0:T(2,128)(2,1)S(1)} %collective-permute-done.6.far_ref, bf16[14336,896]{1,0:T(8,128)(2,1)} %basis_out_ref.1, s32[16]{0:T(128)S(1)} %copy-done.2, ...), custom_call_target="tpu_custom_call" | custom-call | flops 1 | bytes 1 | tf_op jit(solution)/shard_map/rotate_last/pallas_call | solution.py:338
  41.8 1.3 %collective-permute-start.15 = (bf16[256,512]{1,0:T(8,128)(2,1)S(1)}, bf16[256,512]{1,0:T(8,128)(2,1)S(1)}, u32[]{:S(2)}, u32[]{:S(2)}) collective-permute-start(bf16[256,512]{1,0:T(8,128)(2,1)S(1)} %collective-permute-done.10.refs_6_), channel_id=1, source_target_pairs={{0,4},{1,5},{4,8},{5,9},{8,12},{9,13},{12,14},{13,15},{14,10},{15,... | collective-permute-start | bytes 786440 | tf_op jit(solution)/shard_map/ppermute | solution.py:286
  44.4 6.2 %scale.1.scaled_ref = bf16[896,4096]{1,0:T(8,128)(2,1)S(1)} custom-call(bf16[896,32]{1,0:T(8,128)(2,1)S(1)} %rotate_last.1.aligned_ref, bf16[8,32,256]{2,1,0:T(8,128)(2,1)S(1)} %all-to-all-done.near_ref, bf16[8,32,256]{2,1,0:T(8,128)(2,1)S(1)} %collective-permute-done.12.far_ref, s32[32]{0:T(128)S(1)} %copy-done.1, f32[896,4096]{1,0:T(8,128)} %eigen_ref.1), custom_call_target="tpu_custom_call" | custom-call | flops 1 | bytes 1 | tf_op jit(solution)/shard_map/scale/pallas_call | solution.py:390
  50.6 2.3 %mix.1 = (bf16[768,896]{1,0:T(8,128)(2,1)S(1)}, bf16[768,256]{1,0:T(8,128)(2,1)S(1)}, bf16[768,256]{1,0:T(8,128)(2,1)S(1)}) custom-call(bf16[14336,896]{1,0:T(8,128)(2,1)} %basis_out_ref.1, bf16[896,4096]{1,0:T(8,128)(2,1)S(1)} %scale.1.scaled_ref), custom_call_target="tpu_custom_call" | custom-call | flops 1 | bytes 1 | tf_op jit(solution)/shard_map/mix/pallas_call | solution.py:408
  53.6 1.3 %collective-permute-start.22 = (bf16[128,512]{1,0:T(8,128)(2,1)S(1)}, bf16[128,512]{1,0:T(8,128)(2,1)S(1)}, u32[]{:S(2)}, u32[]{:S(2)}) collective-permute-start(bf16[128,512]{1,0:T(8,128)(2,1)S(1)} %slice.10), channel_id=1, source_target_pairs={{0,4},{1,5},{4,8},{5,9},{8,12},{9,13},{12,14},{13,15},{14,10},{15,... | collective-permute-start | bytes 393224 | tf_op jit(solution)/shard_map/ppermute | solution.py:286
  55.7 3.9 %project.1.projected_ref = f32[896,512]{1,0:T(8,128)S(1)} custom-call(bf16[896,4096]{1,0:T(8,128)(2,1)S(1)} %scale.1.scaled_ref, bf16[256,512]{1,0:T(8,128)(2,1)S(1)} %bitcast.6, bf16[256,512]{1,0:T(8,128)(2,1)S(1)} %collective-permute-done.9.refs_1_, bf16[256,512]{1,0:T(8,128)(2,1)S(1)} %collective-permute-done.7.refs_2_, ...), custom_call_target="tpu_custom_call" | custom-call | flops 1 | bytes 1 | tf_op jit(solution)/shard_map/project/pallas_call | solution.py:429
  60.5 1.4 %window.1 = (bf16[8,48,512]{2,1,0:T(8,128)(2,1)S(1)}, f32[8,48,512]{2,1,0:T(8,128)S(1)}) custom-call(bf16[768,896]{1,0:T(8,128)(2,1)S(1)} %get-tuple-element.77.window_ref, f32[896,512]{1,0:T(8,128)S(1)} %project.1.projected_ref, bf16[768,256]{1,0:T(8,128)(2,1)S(1)} %get-tuple-element.93.near_ref, bf16[768,256]{1,0:T(8,128)(2,1)S(1)} %collective-permute-done.21.got_ref, ...), custom_call_target="tpu_custom_call" | custom-call | flops 1 | bytes 1 | tf_op jit(solution)/shard_map/window/pallas_call | solution.py:444
  62.0 1.7 %collective-permute-done.24.got_ref = bf16[8,48,512]{2,1,0:T(8,128)(2,1)S(1)} collective-permute-done((bf16[8,48,512]{2,1,0:T(8,128)(2,1)S(1)}, bf16[8,48,512]{2,1,0:T(8,128)(2,1)S(1)}, u32[]{:S(2)}, u32[]{:S(2)}) %collective-permute-start.24) | collective-permute-done | bytes 393248 | tf_op jit(solution)/shard_map/ppermute | solution.py:48
  63.7 3.3 %collective-permute-start.25 = (bf16[48,512]{1,0:T(8,128)(2,1)S(1)}, bf16[48,512]{1,0:T(8,128)(2,1)S(1)}, u32[]{:S(2)}, u32[]{:S(2)}) collective-permute-start(bf16[48,512]{1,0:T(8,128)(2,1)S(1)} %get-tuple-element.98), channel_id=1, source_target_pairs={{0,12},{1,13},{2,14},{3,15},{4,8},{5,9},{6,10},{7,11},{8,4},{9,5},... | collective-permute-start | bytes 147464 | tf_op jit(solution)/shard_map/ppermute | solution.py:469
  67.0 1.2 %collective-permute-start.27 = (bf16[48,512]{1,0:T(8,128)(2,1)S(1)}, bf16[48,512]{1,0:T(8,128)(2,1)S(1)}, u32[]{:S(2)}, u32[]{:S(2)}) collective-permute-start(bf16[48,512]{1,0:T(8,128)(2,1)S(1)} %get-tuple-element.100), channel_id=1, source_target_pairs={{0,4},{1,5},{2,6},{3,7},{4,0},{5,1},{6,2},{7,3},{8,12},{9,13},{10,... | collective-permute-start | bytes 147464 | tf_op jit(solution)/shard_map/ppermute | solution.py:469
  68.2 3.1 %collective-permute-start.28 = (bf16[48,512]{1,0:T(8,128)(2,1)S(1)}, bf16[48,512]{1,0:T(8,128)(2,1)S(1)}, u32[]{:S(2)}, u32[]{:S(2)}) collective-permute-start(bf16[48,512]{1,0:T(8,128)(2,1)S(1)} %get-tuple-element.101), channel_id=1, source_target_pairs={{0,14},{1,15},{2,12},{3,13},{4,10},{5,11},{6,8},{7,9},{8,6},{9,7},... | collective-permute-start | bytes 147464 | tf_op jit(solution)/shard_map/ppermute | solution.py:469
  71.4 2.3 %collective-permute-start.30 = (bf16[48,512]{1,0:T(8,128)(2,1)S(1)}, bf16[48,512]{1,0:T(8,128)(2,1)S(1)}, u32[]{:S(2)}, u32[]{:S(2)}) collective-permute-start(bf16[48,512]{1,0:T(8,128)(2,1)S(1)} %get-tuple-element.103), channel_id=1, source_target_pairs={{0,6},{1,7},{2,4},{3,5},{4,2},{5,3},{6,0},{7,1},{8,14},{9,15},{10,... | collective-permute-start | bytes 147464 | tf_op jit(solution)/shard_map/ppermute | solution.py:469
  73.7 1.3 %collective-permute-start.31 = (bf16[48,512]{1,0:T(8,128)(2,1)S(1)}, bf16[48,512]{1,0:T(8,128)(2,1)S(1)}, u32[]{:S(2)}, u32[]{:S(2)}) collective-permute-start(bf16[48,512]{1,0:T(8,128)(2,1)S(1)} %get-tuple-element.104), channel_id=1, source_target_pairs={{0,2},{1,3},{2,0},{3,1},{4,6},{5,7},{6,4},{7,5},{8,10},{9,11},{10,... | collective-permute-start | bytes 147464 | tf_op jit(solution)/shard_map/ppermute | solution.py:469
  75.0 2.2 %collective-permute-done.29.refs_4_ = bf16[48,512]{1,0:T(8,128)(2,1)S(1)} collective-permute-done((bf16[48,512]{1,0:T(8,128)(2,1)S(1)}, bf16[48,512]{1,0:T(8,128)(2,1)S(1)}, u32[]{:S(2)}, u32[]{:S(2)}) %collective-permute-start.29) | collective-permute-done | bytes 49184 | tf_op jit(solution)/shard_map/ppermute | solution.py:469
  (69 shorter events, 14.2 us)
Async XLA Ops:
  0.9 8.4 %collective-permute-start = (bf16[1,2,18432]{2,1,0:T(2,128)(2,1)S(1)}, bf16[1,2,18432]{2,1,0:T(2,128)(2,1)S(1)}, u32[]{:S(2)}, u32[]{:S(2)}) collective-permute-start(bf16[1,2,18432]{2,1,0:T(2,128)(2,1)S(1)} %maximum_bitcast_fusion.refs_0_), channel_id=1, source_target_pairs={{0,4},{1,5},{2,6},{3,7},{4,0},{5,1},{6,2},{7,3},{8,12},{9,13},{10,... | collective-permute-start | bytes 221192 | tf_op jit(solution)/shard_map/ppermute | solution.py:294
  4.0 7.8 %collective-permute-start.1 = (bf16[1,2,18432]{2,1,0:T(2,128)(2,1)S(1)}, bf16[1,2,18432]{2,1,0:T(2,128)(2,1)S(1)}, u32[]{:S(2)}, u32[]{:S(2)}) collective-permute-start(bf16[1,2,18432]{2,1,0:T(2,128)(2,1)S(1)} %maximum_bitcast_fusion.refs_0_), channel_id=1, source_target_pairs={{0,8},{1,9},{2,10},{3,11},{4,12},{5,13},{6,14},{7,15},{8,0},{9,1},... | collective-permute-start | bytes 221192 | tf_op jit(solution)/shard_map/ppermute | solution.py:294
  6.6 6.3 %collective-permute-start.2 = (bf16[1,2,18432]{2,1,0:T(2,128)(2,1)S(1)}, bf16[1,2,18432]{2,1,0:T(2,128)(2,1)S(1)}, u32[]{:S(2)}, u32[]{:S(2)}) collective-permute-start(bf16[1,2,18432]{2,1,0:T(2,128)(2,1)S(1)} %maximum_bitcast_fusion.refs_0_), channel_id=1, source_target_pairs={{0,12},{1,13},{2,14},{3,15},{4,8},{5,9},{6,10},{7,11},{8,4},{9,5},... | collective-permute-start | bytes 221192 | tf_op jit(solution)/shard_map/ppermute | solution.py:294
  14.5 6.2 %collective-permute-start.3 = (bf16[4,2,14336]{2,1,0:T(2,128)(2,1)S(1)}, bf16[4,2,14336]{2,1,0:T(2,128)(2,1)S(1)}, u32[]{:S(2)}, u32[]{:S(2)}) collective-permute-start(bf16[4,2,14336]{2,1,0:T(2,128)(2,1)S(1)} %get-tuple-element.62), channel_id=1, source_target_pairs={{0,2},{1,3},{2,0},{3,1},{4,6},{5,7},{6,4},{7,5},{8,10},{9,11},{10,... | collective-permute-start | bytes 688136 | tf_op jit(solution)/shard_map/ppermute | solution.py:319
  20.8 6.6 %collective-permute-start.6 = (bf16[8,2,14336]{2,1,0:T(2,128)(2,1)S(1)}, bf16[8,2,14336]{2,1,0:T(2,128)(2,1)S(1)}, u32[]{:S(2)}, u32[]{:S(2)}) collective-permute-start(bf16[8,2,14336]{2,1,0:T(2,128)(2,1)S(1)} %constant_dynamic-update-slice_fusion.2.near_ref), channel_id=1, source_target_pairs={{0,1},{1,0},{2,3},{3,2},{4,5},{5,4},{6,7},{7,6},{8,9},{9,8},{10,11... | collective-permute-start | bytes 1376264 | tf_op jit(solution)/shard_map/ppermute | solution.py:48
  21.1 10.6 %collective-permute-start.7 = (bf16[256,512]{1,0:T(8,128)(2,1)S(1)}, bf16[256,512]{1,0:T(8,128)(2,1)S(1)}, u32[]{:S(2)}, u32[]{:S(2)}) collective-permute-start(bf16[256,512]{1,0:T(8,128)(2,1)S(1)} %bitcast.3), channel_id=1, source_target_pairs={{0,4},{1,5},{4,8},{5,9},{8,12},{9,13},{12,14},{13,15},{14,10},{15,... | collective-permute-start | bytes 786440 | tf_op jit(solution)/shard_map/ppermute | solution.py:286
  22.2 9.5 %collective-permute-start.8 = (bf16[256,512]{1,0:T(8,128)(2,1)S(1)}, bf16[256,512]{1,0:T(8,128)(2,1)S(1)}, u32[]{:S(2)}, u32[]{:S(2)}) collective-permute-start(bf16[256,512]{1,0:T(8,128)(2,1)S(1)} %bitcast.4), channel_id=1, source_target_pairs={{0,2},{1,3},{4,0},{5,1},{8,4},{9,5},{12,8},{13,9},{14,12},{15,13},... | collective-permute-start | bytes 786440 | tf_op jit(solution)/shard_map/ppermute | solution.py:287
  23.1 8.5 %collective-permute-start.9 = (bf16[256,512]{1,0:T(8,128)(2,1)S(1)}, bf16[256,512]{1,0:T(8,128)(2,1)S(1)}, u32[]{:S(2)}, u32[]{:S(2)}) collective-permute-start(bf16[256,512]{1,0:T(8,128)(2,1)S(1)} %bitcast.5), channel_id=1, source_target_pairs={{0,1},{1,0},{2,3},{3,2},{4,5},{5,4},{6,7},{7,6},{8,9},{9,8},{10,11... | collective-permute-start | bytes 786440 | tf_op jit(solution)/shard_map/ppermute | solution.py:48
  23.1 12.1 %all-to-all-start = ((bf16[8,32,256]{2,1,0:T(8,128)(2,1)}), bf16[8,32,256]{2,1,0:T(8,128)(2,1)S(1)}, u32[]{:S(2)}, u32[]{:S(2)}) async-start(bf16[8,32,256]{2,1,0:T(8,128)(2,1)} %rotate_in.1), calls=%async_computation | async-start | bytes 262144 | tf_op jit(solution)/shard_map/all_to_all | solution.py:44
  31.7 10.1 %collective-permute-start.10 = (bf16[256,512]{1,0:T(8,128)(2,1)S(1)}, bf16[256,512]{1,0:T(8,128)(2,1)S(1)}, u32[]{:S(2)}, u32[]{:S(2)}) collective-permute-start(bf16[256,512]{1,0:T(8,128)(2,1)S(1)} %collective-permute-done.7.refs_2_), channel_id=1, source_target_pairs={{0,4},{1,5},{4,8},{5,9},{8,12},{9,13},{12,14},{13,15},{14,10},{15,... | collective-permute-start | bytes 786440 | tf_op jit(solution)/shard_map/ppermute | solution.py:286
  33.7 8.1 %collective-permute-start.11 = (bf16[256,512]{1,0:T(8,128)(2,1)S(1)}, bf16[256,512]{1,0:T(8,128)(2,1)S(1)}, u32[]{:S(2)}, u32[]{:S(2)}) collective-permute-start(bf16[256,512]{1,0:T(8,128)(2,1)S(1)} %collective-permute-done.8.refs_4_), channel_id=1, source_target_pairs={{0,2},{1,3},{4,0},{5,1},{8,4},{9,5},{12,8},{13,9},{14,12},{15,13},... | collective-permute-start | bytes 786440 | tf_op jit(solution)/shard_map/ppermute | solution.py:287
  33.8 8.0 %collective-permute-start.13 = (bf16[256,512]{1,0:T(8,128)(2,1)S(1)}, bf16[256,512]{1,0:T(8,128)(2,1)S(1)}, u32[]{:S(2)}, u32[]{:S(2)}) collective-permute-start(bf16[256,512]{1,0:T(8,128)(2,1)S(1)} %collective-permute-done.7.refs_2_), channel_id=1, source_target_pairs={{0,1},{1,0},{2,3},{3,2},{4,5},{5,4},{6,7},{7,6},{8,9},{9,8},{10,11... | collective-permute-start | bytes 786440 | tf_op jit(solution)/shard_map/ppermute | solution.py:48
  33.8 8.0 %collective-permute-start.14 = (bf16[256,512]{1,0:T(8,128)(2,1)S(1)}, bf16[256,512]{1,0:T(8,128)(2,1)S(1)}, u32[]{:S(2)}, u32[]{:S(2)}) collective-permute-start(bf16[256,512]{1,0:T(8,128)(2,1)S(1)} %collective-permute-done.8.refs_4_), channel_id=1, source_target_pairs={{0,1},{1,0},{2,3},{3,2},{4,5},{5,4},{6,7},{7,6},{8,9},{9,8},{10,11... | collective-permute-start | bytes 786440 | tf_op jit(solution)/shard_map/ppermute | solution.py:48
  35.2 6.6 %collective-permute-start.12 = (bf16[8,32,256]{2,1,0:T(8,128)(2,1)S(1)}, bf16[8,32,256]{2,1,0:T(8,128)(2,1)S(1)}, u32[]{:S(2)}, u32[]{:S(2)}) collective-permute-start(bf16[8,32,256]{2,1,0:T(8,128)(2,1)S(1)} %all-to-all-done.near_ref), channel_id=1, source_target_pairs={{0,1},{1,0},{2,3},{3,2},{4,5},{5,4},{6,7},{7,6},{8,9},{9,8},{10,11... | collective-permute-start | bytes 393224 | tf_op jit(solution)/shard_map/ppermute | solution.py:48
  41.8 11.1 %collective-permute-start.15 = (bf16[256,512]{1,0:T(8,128)(2,1)S(1)}, bf16[256,512]{1,0:T(8,128)(2,1)S(1)}, u32[]{:S(2)}, u32[]{:S(2)}) collective-permute-start(bf16[256,512]{1,0:T(8,128)(2,1)S(1)} %collective-permute-done.10.refs_6_), channel_id=1, source_target_pairs={{0,4},{1,5},{4,8},{5,9},{8,12},{9,13},{12,14},{13,15},{14,10},{15,... | collective-permute-start | bytes 786440 | tf_op jit(solution)/shard_map/ppermute | solution.py:286
  43.1 9.8 %collective-permute-start.16 = (bf16[256,512]{1,0:T(8,128)(2,1)S(1)}, bf16[256,512]{1,0:T(8,128)(2,1)S(1)}, u32[]{:S(2)}, u32[]{:S(2)}) collective-permute-start(bf16[256,512]{1,0:T(8,128)(2,1)S(1)} %collective-permute-done.11.refs_8_), channel_id=1, source_target_pairs={{0,2},{1,3},{4,0},{5,1},{8,4},{9,5},{12,8},{13,9},{14,12},{15,13},... | collective-permute-start | bytes 786440 | tf_op jit(solution)/shard_map/ppermute | solution.py:287
  43.9 9.0 %collective-permute-start.17 = (bf16[256,512]{1,0:T(8,128)(2,1)S(1)}, bf16[256,512]{1,0:T(8,128)(2,1)S(1)}, u32[]{:S(2)}, u32[]{:S(2)}) collective-permute-start(bf16[256,512]{1,0:T(8,128)(2,1)S(1)} %collective-permute-done.10.refs_6_), channel_id=1, source_target_pairs={{0,1},{1,0},{2,3},{3,2},{4,5},{5,4},{6,7},{7,6},{8,9},{9,8},{10,11... | collective-permute-start | bytes 786440 | tf_op jit(solution)/shard_map/ppermute | solution.py:48
  43.9 9.0 %collective-permute-start.18 = (bf16[256,512]{1,0:T(8,128)(2,1)S(1)}, bf16[256,512]{1,0:T(8,128)(2,1)S(1)}, u32[]{:S(2)}, u32[]{:S(2)}) collective-permute-start(bf16[256,512]{1,0:T(8,128)(2,1)S(1)} %collective-permute-done.11.refs_8_), channel_id=1, source_target_pairs={{0,1},{1,0},{2,3},{3,2},{4,5},{5,4},{6,7},{7,6},{8,9},{9,8},{10,11... | collective-permute-start | bytes 786440 | tf_op jit(solution)/shard_map/ppermute | solution.py:48
  53.0 7.6 %collective-permute-start.21 = (bf16[768,256]{1,0:T(8,128)(2,1)S(1)}, bf16[768,256]{1,0:T(8,128)(2,1)S(1)}, u32[]{:S(2)}, u32[]{:S(2)}) collective-permute-start(bf16[768,256]{1,0:T(8,128)(2,1)S(1)} %get-tuple-element.94), channel_id=1, source_target_pairs={{0,1},{1,0},{2,3},{3,2},{4,5},{5,4},{6,7},{7,6},{8,9},{9,8},{10,11... | collective-permute-start | bytes 1179656 | tf_op jit(solution)/shard_map/ppermute | solution.py:48
  53.6 6.0 %collective-permute-start.22 = (bf16[128,512]{1,0:T(8,128)(2,1)S(1)}, bf16[128,512]{1,0:T(8,128)(2,1)S(1)}, u32[]{:S(2)}, u32[]{:S(2)}) collective-permute-start(bf16[128,512]{1,0:T(8,128)(2,1)S(1)} %slice.10), channel_id=1, source_target_pairs={{0,4},{1,5},{4,8},{5,9},{8,12},{9,13},{12,14},{13,15},{14,10},{15,... | collective-permute-start | bytes 393224 | tf_op jit(solution)/shard_map/ppermute | solution.py:286
  63.7 7.6 %collective-permute-start.25 = (bf16[48,512]{1,0:T(8,128)(2,1)S(1)}, bf16[48,512]{1,0:T(8,128)(2,1)S(1)}, u32[]{:S(2)}, u32[]{:S(2)}) collective-permute-start(bf16[48,512]{1,0:T(8,128)(2,1)S(1)} %get-tuple-element.98), channel_id=1, source_target_pairs={{0,12},{1,13},{2,14},{3,15},{4,8},{5,9},{6,10},{7,11},{8,4},{9,5},... | collective-permute-start | bytes 147464 | tf_op jit(solution)/shard_map/ppermute | solution.py:469
  67.0 6.7 %collective-permute-start.26 = (bf16[48,512]{1,0:T(8,128)(2,1)S(1)}, bf16[48,512]{1,0:T(8,128)(2,1)S(1)}, u32[]{:S(2)}, u32[]{:S(2)}) collective-permute-start(bf16[48,512]{1,0:T(8,128)(2,1)S(1)} %get-tuple-element.99), channel_id=1, source_target_pairs={{0,8},{1,9},{2,10},{3,11},{4,12},{5,13},{6,14},{7,15},{8,0},{9,1},... | collective-permute-start | bytes 147464 | tf_op jit(solution)/shard_map/ppermute | solution.py:469
  67.0 8.0 %collective-permute-start.27 = (bf16[48,512]{1,0:T(8,128)(2,1)S(1)}, bf16[48,512]{1,0:T(8,128)(2,1)S(1)}, u32[]{:S(2)}, u32[]{:S(2)}) collective-permute-start(bf16[48,512]{1,0:T(8,128)(2,1)S(1)} %get-tuple-element.100), channel_id=1, source_target_pairs={{0,4},{1,5},{2,6},{3,7},{4,0},{5,1},{6,2},{7,3},{8,12},{9,13},{10,... | collective-permute-start | bytes 147464 | tf_op jit(solution)/shard_map/ppermute | solution.py:469
  68.2 6.8 %collective-permute-start.28 = (bf16[48,512]{1,0:T(8,128)(2,1)S(1)}, bf16[48,512]{1,0:T(8,128)(2,1)S(1)}, u32[]{:S(2)}, u32[]{:S(2)}) collective-permute-start(bf16[48,512]{1,0:T(8,128)(2,1)S(1)} %get-tuple-element.101), channel_id=1, source_target_pairs={{0,14},{1,15},{2,12},{3,13},{4,10},{5,11},{6,8},{7,9},{8,6},{9,7},... | collective-permute-start | bytes 147464 | tf_op jit(solution)/shard_map/ppermute | solution.py:469
  (13 other events, 57.7 us)

commit v28 on v27

--- a/solution.py
+++ b/solution.py
@@ -153,7 +153,9 @@
     far_ref,
     tiles_ref,
     eigen_ref,
+    basis_out_ref,
     out_ref,
+    window_ref,
     damped,
     tiles,
     lanes,
@@ -175,6 +177,10 @@
     def _(block):
         copy_of(block).start()
 
+    window_copy = pltpu.make_async_copy(
+        basis_out_ref.at[pl.ds(0, window_ref.shape[0])], window_ref, sem.at[blocks + 1]
+    )
+    window_copy.start()
     tiles_copy.wait()
     me = lax.axis_index("blk")
     for at, steps in enumerate(begun):
@@ -199,6 +205,8 @@
                 inverse = inverse * (2.0 - eigen * inverse)
                 scaled = grad[:, part * LANES : (part + 1) * LANES] * inverse
                 out_ref[rows, tile * LANES : (tile + 1) * LANES] = scaled.astype(jnp.bfloat16)
+
+    window_copy.wait()
 
 
 def project_kernel(cuts, scaled_ref, *refs):
@@ -219,12 +227,7 @@
         out_ref[...] = part if first == 0 else out_ref[...] + part
 
 
-def mix_kernel(basis_out_ref, scaled_ref, window_ref, near_ref, far_ref, sem):
-    copy = pltpu.make_async_copy(
-        basis_out_ref.at[pl.ds(0, window_ref.shape[0])], window_ref, sem.at[0]
-    )
-    copy.start()
-    copy.wait()
+def mix_kernel(window_ref, scaled_ref, near_ref, far_ref):
     width = near_ref.shape[1]
     first = scaled_ref.shape[1] - 2 * width
     mixed = jnp.dot(window_ref[...], scaled_ref[:, first:], preferred_element_type=jnp.float32)
@@ -387,36 +390,36 @@
     left.append(to_left(left[-1]))
     begun = [0] + [at for step in range(1, steps) for at in (step, chips - step)] + [steps]
     blocks = 8
-    scaled = pl.pallas_call(
+    scaled, window = pl.pallas_call(
         functools.partial(scale_kernel, begun),
-        out_shape=jax.ShapeDtypeStruct((tile_width, full_in), jnp.bfloat16),
-        in_specs=[VMEM] * 3 + [ANY] * 2,
-        out_specs=VMEM,
+        out_shape=(
+            jax.ShapeDtypeStruct((tile_width, full_in), jnp.bfloat16),
+            jax.ShapeDtypeStruct((WR, tile_width), jnp.bfloat16),
+        ),
+        in_specs=[VMEM] * 3 + [ANY] * 3,
+        out_specs=(VMEM, VMEM),
         scratch_shapes=[
             pltpu.VMEM((blocks, tile_width // blocks, full_in), jnp.float32),
             pltpu.SMEM(tile_order.shape, jnp.int32),
             pltpu.SMEM(tile_order.shape, jnp.int32),
             pltpu.VMEM((n, tokens, in_width), jnp.bfloat16),
-            pltpu.SemaphoreType.DMA((blocks + 1,)),
+            pltpu.SemaphoreType.DMA((blocks + 2,)),
         ],
         compiler_params=pltpu.CompilerParams(vmem_limit_bytes=40 * MIB),
         cost_estimate=CHEAP,
         name="scale",
-    )(aligned, rotated, rotated_far, tile_order, eigenvalues)
+    )(aligned, rotated, rotated_far, tile_order, eigenvalues, basis_out)
 
     mix = (WR, in_width)
-    window, mixed, mixed_far = pl.pallas_call(
+    mixed, mixed_far = pl.pallas_call(
         mix_kernel,
-        out_shape=tuple(
-            jax.ShapeDtypeStruct(shape, jnp.bfloat16) for shape in ((WR, tile_width), mix, mix)
-        ),
-        in_specs=[ANY, VMEM],
-        out_specs=(VMEM,) * 3,
-        scratch_shapes=[pltpu.SemaphoreType.DMA((1,))],
+        out_shape=(jax.ShapeDtypeStruct(mix, jnp.bfloat16),) * 2,
+        in_specs=[VMEM, VMEM],
+        out_specs=(VMEM, VMEM),
         compiler_params=pltpu.CompilerParams(vmem_limit_bytes=40 * MIB),
         cost_estimate=CHEAP,
         name="mix",
-    )(basis_out, scaled)
+    )(window, scaled)
     scaled, mixed, mixed_far, right[-1], left[-1], *far = after(
         scaled, mixed, mixed_far, right[-1], left[-1], *far
     )

time: 78.8 us -> 77.6 us (0.985)
  Pallas kernels: 26.6 us -> 25.3 us
    pallas_call x2, Pallas kernels: 8.49 us -> 7.22 us  [the longest x1 6.25 us: ring_body(): pl.pallas_call(functools.partial(scale_kernel, begun), out_shape=(jax.Sha...]
  transfers between devices with their start and end apart: 33 -> 33, of which waited for: 10 -> 10; matrix products, arithmetic and copies ran while one was open for 1% -> 1% of each run, Pallas kernels for 31% -> 30%
where the time goes in v28:
time: 77.6 us; the launch traced here: 77.2 us
  starting transfers between devices  33.7 us (43%)
  Pallas kernels  25.3 us (33%)
  waiting for transfers between devices  14 us (18%)
  local copies, waits for them, and re-layouts  3.02 us (4%)
  other arithmetic  0.91 us (1%)
    ppermute x7, starting transfers between devices, ring_body(): lax.ppermute(x, 'blk', xor_pairs(n, 2 * key))  11.2 us
    pallas_call x2, Pallas kernels, ring_body(): pl.pallas_call(kernel, out_shape=jax.ShapeDtypeStruct(shape, dtype), in_s...  10.7 us
    pallas_call x1, Pallas kernels, ring_body(): pl.pallas_call(functools.partial(scale_kernel, begun), out_shape=(jax.Sha...  6.25 us
    ppermute x3, starting transfers between devices, ring_body(): lax.ppermute(both, 'blk', xor_pairs(n, 4 * key))  5.68 us
    ppermute x4, starting transfers between devices, ring_body(): to_right = lambda x: lax.ppermute(x, 'blk', shift_pairs(n, 1))  5.67 us
    all_to_all x1, starting transfers between devices, exchange(): return lax.all_to_all(x, 'blk', 0, 0, axis_index_groups=groups, tiled=True)  4.33 us
    pallas_call x1, Pallas kernels, ring_body(): pl.pallas_call(functools.partial(project_kernel, (0, 6, len(pieces))), ou...  3.92 us
    ppermute x3, waiting for transfers between devices, ring_body(): lax.ppermute(both, 'blk', xor_pairs(n, 4 * key))  3.56 us
  transfers between devices with their start and end apart: 33, of which 10 were waited for; matrix products, arithmetic and copies ran while one was open for 1% of the time, Pallas kernels for 30%

profile of v28, /device:TPU:0, one launch (start us, length us, event | category | flops | bytes accessed | tf_op | source)
XLA Modules:
  0.0 77.2 jit_solution(3582147025191306449)
XLA Ops:
  0.9 3.1 %collective-permute-start = (bf16[1,2,18432]{2,1,0:T(2,128)(2,1)S(1)}, bf16[1,2,18432]{2,1,0:T(2,128)(2,1)S(1)}, u32[]{:S(2)}, u32[]{:S(2)}) collective-permute-start(bf16[1,2,18432]{2,1,0:T(2,128)(2,1)S(1)} %maximum_bitcast_fusion.refs_0_), channel_id=1, source_target_pairs={{0,4},{1,5},{2,6},{3,7},{4,0},{5,1},{6,2},{7,3},{8,12},{9,13},{10,... | collective-permute-start | bytes 221192 | tf_op jit(solution)/shard_map/ppermute | solution.py:297
  4.0 2.6 %collective-permute-start.1 = (bf16[1,2,18432]{2,1,0:T(2,128)(2,1)S(1)}, bf16[1,2,18432]{2,1,0:T(2,128)(2,1)S(1)}, u32[]{:S(2)}, u32[]{:S(2)}) collective-permute-start(bf16[1,2,18432]{2,1,0:T(2,128)(2,1)S(1)} %maximum_bitcast_fusion.refs_0_), channel_id=1, source_target_pairs={{0,8},{1,9},{2,10},{3,11},{4,12},{5,13},{6,14},{7,15},{8,0},{9,1},... | collective-permute-start | bytes 221192 | tf_op jit(solution)/shard_map/ppermute | solution.py:297
  6.6 1.6 %copy-done = bf16[4096,256]{1,0:T(8,128)(2,1)S(1)} copy-done((bf16[4096,256]{1,0:T(8,128)(2,1)S(1)}, bf16[4096,256]{1,0:T(8,128)(2,1)}, u32[]{:S(2)}) %copy-start) | copy-done | bytes 2097176
  9.3 2.5 %collective-permute-done.1.refs_2_ = bf16[1,2,18432]{2,1,0:T(2,128)(2,1)S(1)} collective-permute-done((bf16[1,2,18432]{2,1,0:T(2,128)(2,1)S(1)}, bf16[1,2,18432]{2,1,0:T(2,128)(2,1)S(1)}, u32[]{:S(2)}, u32[]{:S(2)}) %collective-permute-start.1) | collective-permute-done | bytes 73760 | tf_op jit(solution)/shard_map/ppermute | solution.py:297
  12.9 1.6 %collective-permute-start.4 = (bf16[4,2,4096]{2,1,0:T(2,128)(2,1)S(1)}, bf16[4,2,4096]{2,1,0:T(2,128)(2,1)S(1)}, u32[]{:S(2)}, u32[]{:S(2)}) collective-permute-start(bf16[4,2,4096]{2,1,0:T(2,128)(2,1)S(1)} %get-tuple-element.65), channel_id=1, source_target_pairs={{0,2},{1,3},{2,0},{3,1},{4,6},{5,7},{6,4},{7,5},{8,10},{9,11},{10,... | collective-permute-start | bytes 196616 | tf_op jit(solution)/shard_map/ppermute | solution.py:321
  15.1 2.9 %collective-permute-done.4 = bf16[4,2,4096]{2,1,0:T(2,128)(2,1)S(1)} collective-permute-done((bf16[4,2,4096]{2,1,0:T(2,128)(2,1)S(1)}, bf16[4,2,4096]{2,1,0:T(2,128)(2,1)S(1)}, u32[]{:S(2)}, u32[]{:S(2)}) %collective-permute-start.4) | collective-permute-done | bytes 65568 | tf_op jit(solution)/shard_map/ppermute | solution.py:321
  18.3 1.2 %collective-permute-done.5.far_ref = bf16[8,2,4096]{2,1,0:T(2,128)(2,1)S(1)} collective-permute-done((bf16[8,2,4096]{2,1,0:T(2,128)(2,1)S(1)}, bf16[8,2,4096]{2,1,0:T(2,128)(2,1)S(1)}, u32[]{:S(2)}, u32[]{:S(2)}) %collective-permute-start.5) | collective-permute-done | bytes 131104 | tf_op jit(solution)/shard_map/ppermute | solution.py:48
  19.4 1.2 %rotate_in.1 = bf16[8,32,256]{2,1,0:T(8,128)(2,1)} custom-call(bf16[8,2,4096]{2,1,0:T(2,128)(2,1)S(1)} %constant_dynamic-update-slice_fusion.near_ref, bf16[8,2,4096]{2,1,0:T(2,128)(2,1)S(1)} %collective-permute-done.5.far_ref, bf16[4096,256]{1,0:T(8,128)(2,1)S(1)} %keep.1.basis_ref), custom_call_target="tpu_custom_call" | custom-call | flops 1 | bytes 1 | tf_op jit(solution)/shard_map/rotate_in/pallas_call | solution.py:324
  23.1 4.3 %all-to-all-start = ((bf16[8,32,256]{2,1,0:T(8,128)(2,1)}), bf16[8,32,256]{2,1,0:T(8,128)(2,1)S(1)}, u32[]{:S(2)}, u32[]{:S(2)}) async-start(bf16[8,32,256]{2,1,0:T(8,128)(2,1)} %rotate_in.1), calls=%async_computation | async-start | bytes 262144 | tf_op jit(solution)/shard_map/all_to_all | solution.py:44
  27.4 4.2 %rotate_first.1.start_ref = f32[32,896]{1,0:T(8,128)S(1)} custom-call(bf16[8,2,14336]{2,1,0:T(2,128)(2,1)S(1)} %constant_dynamic-update-slice_fusion.2.near_ref, bf16[8,2,14336]{2,1,0:T(2,128)(2,1)S(1)} %collective-permute-done.6.far_ref, bf16[14336,896]{1,0:T(8,128)(2,1)} %basis_out_ref.1), custom_call_target="tpu_custom_call" | custom-call | flops 1 | bytes 1 | tf_op jit(solution)/shard_map/rotate_first/pallas_call | solution.py:341
  31.7 2.1 %collective-permute-start.10 = (bf16[256,512]{1,0:T(8,128)(2,1)S(1)}, bf16[256,512]{1,0:T(8,128)(2,1)S(1)}, u32[]{:S(2)}, u32[]{:S(2)}) collective-permute-start(bf16[256,512]{1,0:T(8,128)(2,1)S(1)} %collective-permute-done.7.refs_2_), channel_id=1, source_target_pairs={{0,4},{1,5},{4,8},{5,9},{8,12},{9,13},{12,14},{13,15},{14,10},{15,... | collective-permute-start | bytes 786440 | tf_op jit(solution)/shard_map/ppermute | solution.py:289
  35.2 6.6 %rotate_last.1.aligned_ref = bf16[896,32]{1,0:T(8,128)(2,1)S(1)} custom-call(bf16[8,2,14336]{2,1,0:T(2,128)(2,1)S(1)} %constant_dynamic-update-slice_fusion.2.near_ref, bf16[8,2,14336]{2,1,0:T(2,128)(2,1)S(1)} %collective-permute-done.6.far_ref, bf16[14336,896]{1,0:T(8,128)(2,1)} %basis_out_ref.1, s32[16]{0:T(128)S(1)} %copy-done.1, ...), custom_call_target="tpu_custom_call" | custom-call | flops 1 | bytes 1 | tf_op jit(solution)/shard_map/rotate_last/pallas_call | solution.py:341
  41.8 1.3 %collective-permute-start.15 = (bf16[256,512]{1,0:T(8,128)(2,1)S(1)}, bf16[256,512]{1,0:T(8,128)(2,1)S(1)}, u32[]{:S(2)}, u32[]{:S(2)}) collective-permute-start(bf16[256,512]{1,0:T(8,128)(2,1)S(1)} %collective-permute-done.10.refs_6_), channel_id=1, source_target_pairs={{0,4},{1,5},{4,8},{5,9},{8,12},{9,13},{12,14},{13,15},{14,10},{15,... | collective-permute-start | bytes 786440 | tf_op jit(solution)/shard_map/ppermute | solution.py:289
  44.4 6.2 %scale.1 = (bf16[896,4096]{1,0:T(8,128)(2,1)S(1)}, bf16[768,896]{1,0:T(8,128)(2,1)S(1)}) custom-call(bf16[896,32]{1,0:T(8,128)(2,1)S(1)} %rotate_last.1.aligned_ref, bf16[8,32,256]{2,1,0:T(8,128)(2,1)S(1)} %all-to-all-done.near_ref, bf16[8,32,256]{2,1,0:T(8,128)(2,1)S(1)} %collective-permute-done.12.far_ref, s32[32]{0:T(128)S(1)} %copy-done.2, ...), custom_call_target="tpu_custom_call" | custom-call | flops 1 | bytes 1 | tf_op jit(solution)/shard_map/scale/pallas_call | solution.py:393
  52.4 1.2 %collective-permute-start.22 = (bf16[128,512]{1,0:T(8,128)(2,1)S(1)}, bf16[128,512]{1,0:T(8,128)(2,1)S(1)}, u32[]{:S(2)}, u32[]{:S(2)}) collective-permute-start(bf16[128,512]{1,0:T(8,128)(2,1)S(1)} %slice.10), channel_id=1, source_target_pairs={{0,4},{1,5},{4,8},{5,9},{8,12},{9,13},{12,14},{13,15},{14,10},{15,... | collective-permute-start | bytes 393224 | tf_op jit(solution)/shard_map/ppermute | solution.py:289
  54.5 3.9 %project.1.projected_ref = f32[896,512]{1,0:T(8,128)S(1)} custom-call(bf16[896,4096]{1,0:T(8,128)(2,1)S(1)} %get-tuple-element.87.scaled_ref, bf16[256,512]{1,0:T(8,128)(2,1)S(1)} %bitcast.6, bf16[256,512]{1,0:T(8,128)(2,1)S(1)} %collective-permute-done.9.refs_1_, bf16[256,512]{1,0:T(8,128)(2,1)S(1)} %collective-permute-done.7.refs_2_, ...), custom_call_target="tpu_custom_call" | custom-call | flops 1 | bytes 1 | tf_op jit(solution)/shard_map/project/pallas_call | solution.py:432
  59.2 1.4 %window.1 = (bf16[8,48,512]{2,1,0:T(8,128)(2,1)S(1)}, f32[8,48,512]{2,1,0:T(8,128)S(1)}) custom-call(bf16[768,896]{1,0:T(8,128)(2,1)S(1)} %get-tuple-element.78.window_ref, f32[896,512]{1,0:T(8,128)S(1)} %project.1.projected_ref, bf16[768,256]{1,0:T(8,128)(2,1)S(1)} %get-tuple-element.95.near_ref, bf16[768,256]{1,0:T(8,128)(2,1)S(1)} %collective-permute-done.21.got_ref, ...), custom_call_target="tpu_custom_call" | custom-call | flops 1 | bytes 1 | tf_op jit(solution)/shard_map/window/pallas_call | solution.py:447
  60.6 1.7 %collective-permute-done.24.got_ref = bf16[8,48,512]{2,1,0:T(8,128)(2,1)S(1)} collective-permute-done((bf16[8,48,512]{2,1,0:T(8,128)(2,1)S(1)}, bf16[8,48,512]{2,1,0:T(8,128)(2,1)S(1)}, u32[]{:S(2)}, u32[]{:S(2)}) %collective-permute-start.24) | collective-permute-done | bytes 393248 | tf_op jit(solution)/shard_map/ppermute | solution.py:48
  62.4 3.3 %collective-permute-start.25 = (bf16[48,512]{1,0:T(8,128)(2,1)S(1)}, bf16[48,512]{1,0:T(8,128)(2,1)S(1)}, u32[]{:S(2)}, u32[]{:S(2)}) collective-permute-start(bf16[48,512]{1,0:T(8,128)(2,1)S(1)} %get-tuple-element.100), channel_id=1, source_target_pairs={{0,12},{1,13},{2,14},{3,15},{4,8},{5,9},{6,10},{7,11},{8,4},{9,5},... | collective-permute-start | bytes 147464 | tf_op jit(solution)/shard_map/ppermute | solution.py:472
  65.7 1.2 %collective-permute-start.27 = (bf16[48,512]{1,0:T(8,128)(2,1)S(1)}, bf16[48,512]{1,0:T(8,128)(2,1)S(1)}, u32[]{:S(2)}, u32[]{:S(2)}) collective-permute-start(bf16[48,512]{1,0:T(8,128)(2,1)S(1)} %get-tuple-element.102), channel_id=1, source_target_pairs={{0,4},{1,5},{2,6},{3,7},{4,0},{5,1},{6,2},{7,3},{8,12},{9,13},{10,... | collective-permute-start | bytes 147464 | tf_op jit(solution)/shard_map/ppermute | solution.py:472
  66.9 3.2 %collective-permute-start.28 = (bf16[48,512]{1,0:T(8,128)(2,1)S(1)}, bf16[48,512]{1,0:T(8,128)(2,1)S(1)}, u32[]{:S(2)}, u32[]{:S(2)}) collective-permute-start(bf16[48,512]{1,0:T(8,128)(2,1)S(1)} %get-tuple-element.103), channel_id=1, source_target_pairs={{0,14},{1,15},{2,12},{3,13},{4,10},{5,11},{6,8},{7,9},{8,6},{9,7},... | collective-permute-start | bytes 147464 | tf_op jit(solution)/shard_map/ppermute | solution.py:472
  70.1 2.4 %collective-permute-start.30 = (bf16[48,512]{1,0:T(8,128)(2,1)S(1)}, bf16[48,512]{1,0:T(8,128)(2,1)S(1)}, u32[]{:S(2)}, u32[]{:S(2)}) collective-permute-start(bf16[48,512]{1,0:T(8,128)(2,1)S(1)} %get-tuple-element.105), channel_id=1, source_target_pairs={{0,6},{1,7},{2,4},{3,5},{4,2},{5,3},{6,0},{7,1},{8,14},{9,15},{10,... | collective-permute-start | bytes 147464 | tf_op jit(solution)/shard_map/ppermute | solution.py:472
  72.4 1.2 %collective-permute-start.31 = (bf16[48,512]{1,0:T(8,128)(2,1)S(1)}, bf16[48,512]{1,0:T(8,128)(2,1)S(1)}, u32[]{:S(2)}, u32[]{:S(2)}) collective-permute-start(bf16[48,512]{1,0:T(8,128)(2,1)S(1)} %get-tuple-element.106), channel_id=1, source_target_pairs={{0,2},{1,3},{2,0},{3,1},{4,6},{5,7},{6,4},{7,5},{8,10},{9,11},{10,... | collective-permute-start | bytes 147464 | tf_op jit(solution)/shard_map/ppermute | solution.py:472
  73.7 2.2 %collective-permute-done.29.refs_4_ = bf16[48,512]{1,0:T(8,128)(2,1)S(1)} collective-permute-done((bf16[48,512]{1,0:T(8,128)(2,1)S(1)}, bf16[48,512]{1,0:T(8,128)(2,1)S(1)}, u32[]{:S(2)}, u32[]{:S(2)}) %collective-permute-start.29) | collective-permute-done | bytes 49184 | tf_op jit(solution)/shard_map/ppermute | solution.py:472
  (69 shorter events, 14.1 us)
Async XLA Ops:
  0.9 8.4 %collective-permute-start = (bf16[1,2,18432]{2,1,0:T(2,128)(2,1)S(1)}, bf16[1,2,18432]{2,1,0:T(2,128)(2,1)S(1)}, u32[]{:S(2)}, u32[]{:S(2)}) collective-permute-start(bf16[1,2,18432]{2,1,0:T(2,128)(2,1)S(1)} %maximum_bitcast_fusion.refs_0_), channel_id=1, source_target_pairs={{0,4},{1,5},{2,6},{3,7},{4,0},{5,1},{6,2},{7,3},{8,12},{9,13},{10,... | collective-permute-start | bytes 221192 | tf_op jit(solution)/shard_map/ppermute | solution.py:297
  4.0 7.8 %collective-permute-start.1 = (bf16[1,2,18432]{2,1,0:T(2,128)(2,1)S(1)}, bf16[1,2,18432]{2,1,0:T(2,128)(2,1)S(1)}, u32[]{:S(2)}, u32[]{:S(2)}) collective-permute-start(bf16[1,2,18432]{2,1,0:T(2,128)(2,1)S(1)} %maximum_bitcast_fusion.refs_0_), channel_id=1, source_target_pairs={{0,8},{1,9},{2,10},{3,11},{4,12},{5,13},{6,14},{7,15},{8,0},{9,1},... | collective-permute-start | bytes 221192 | tf_op jit(solution)/shard_map/ppermute | solution.py:297
  6.6 6.3 %collective-permute-start.2 = (bf16[1,2,18432]{2,1,0:T(2,128)(2,1)S(1)}, bf16[1,2,18432]{2,1,0:T(2,128)(2,1)S(1)}, u32[]{:S(2)}, u32[]{:S(2)}) collective-permute-start(bf16[1,2,18432]{2,1,0:T(2,128)(2,1)S(1)} %maximum_bitcast_fusion.refs_0_), channel_id=1, source_target_pairs={{0,12},{1,13},{2,14},{3,15},{4,8},{5,9},{6,10},{7,11},{8,4},{9,5},... | collective-permute-start | bytes 221192 | tf_op jit(solution)/shard_map/ppermute | solution.py:297
  14.5 6.2 %collective-permute-start.3 = (bf16[4,2,14336]{2,1,0:T(2,128)(2,1)S(1)}, bf16[4,2,14336]{2,1,0:T(2,128)(2,1)S(1)}, u32[]{:S(2)}, u32[]{:S(2)}) collective-permute-start(bf16[4,2,14336]{2,1,0:T(2,128)(2,1)S(1)} %get-tuple-element.63), channel_id=1, source_target_pairs={{0,2},{1,3},{2,0},{3,1},{4,6},{5,7},{6,4},{7,5},{8,10},{9,11},{10,... | collective-permute-start | bytes 688136 | tf_op jit(solution)/shard_map/ppermute | solution.py:322
  20.8 6.6 %collective-permute-start.6 = (bf16[8,2,14336]{2,1,0:T(2,128)(2,1)S(1)}, bf16[8,2,14336]{2,1,0:T(2,128)(2,1)S(1)}, u32[]{:S(2)}, u32[]{:S(2)}) collective-permute-start(bf16[8,2,14336]{2,1,0:T(2,128)(2,1)S(1)} %constant_dynamic-update-slice_fusion.2.near_ref), channel_id=1, source_target_pairs={{0,1},{1,0},{2,3},{3,2},{4,5},{5,4},{6,7},{7,6},{8,9},{9,8},{10,11... | collective-permute-start | bytes 1376264 | tf_op jit(solution)/shard_map/ppermute | solution.py:48
  21.1 10.6 %collective-permute-start.7 = (bf16[256,512]{1,0:T(8,128)(2,1)S(1)}, bf16[256,512]{1,0:T(8,128)(2,1)S(1)}, u32[]{:S(2)}, u32[]{:S(2)}) collective-permute-start(bf16[256,512]{1,0:T(8,128)(2,1)S(1)} %bitcast.3), channel_id=1, source_target_pairs={{0,4},{1,5},{4,8},{5,9},{8,12},{9,13},{12,14},{13,15},{14,10},{15,... | collective-permute-start | bytes 786440 | tf_op jit(solution)/shard_map/ppermute | solution.py:289
  22.2 9.5 %collective-permute-start.8 = (bf16[256,512]{1,0:T(8,128)(2,1)S(1)}, bf16[256,512]{1,0:T(8,128)(2,1)S(1)}, u32[]{:S(2)}, u32[]{:S(2)}) collective-permute-start(bf16[256,512]{1,0:T(8,128)(2,1)S(1)} %bitcast.4), channel_id=1, source_target_pairs={{0,2},{1,3},{4,0},{5,1},{8,4},{9,5},{12,8},{13,9},{14,12},{15,13},... | collective-permute-start | bytes 786440 | tf_op jit(solution)/shard_map/ppermute | solution.py:290
  23.1 8.5 %collective-permute-start.9 = (bf16[256,512]{1,0:T(8,128)(2,1)S(1)}, bf16[256,512]{1,0:T(8,128)(2,1)S(1)}, u32[]{:S(2)}, u32[]{:S(2)}) collective-permute-start(bf16[256,512]{1,0:T(8,128)(2,1)S(1)} %bitcast.5), channel_id=1, source_target_pairs={{0,1},{1,0},{2,3},{3,2},{4,5},{5,4},{6,7},{7,6},{8,9},{9,8},{10,11... | collective-permute-start | bytes 786440 | tf_op jit(solution)/shard_map/ppermute | solution.py:48
  23.1 12.1 %all-to-all-start = ((bf16[8,32,256]{2,1,0:T(8,128)(2,1)}), bf16[8,32,256]{2,1,0:T(8,128)(2,1)S(1)}, u32[]{:S(2)}, u32[]{:S(2)}) async-start(bf16[8,32,256]{2,1,0:T(8,128)(2,1)} %rotate_in.1), calls=%async_computation | async-start | bytes 262144 | tf_op jit(solution)/shard_map/all_to_all | solution.py:44
  31.7 10.1 %collective-permute-start.10 = (bf16[256,512]{1,0:T(8,128)(2,1)S(1)}, bf16[256,512]{1,0:T(8,128)(2,1)S(1)}, u32[]{:S(2)}, u32[]{:S(2)}) collective-permute-start(bf16[256,512]{1,0:T(8,128)(2,1)S(1)} %collective-permute-done.7.refs_2_), channel_id=1, source_target_pairs={{0,4},{1,5},{4,8},{5,9},{8,12},{9,13},{12,14},{13,15},{14,10},{15,... | collective-permute-start | bytes 786440 | tf_op jit(solution)/shard_map/ppermute | solution.py:289
  33.7 8.1 %collective-permute-start.11 = (bf16[256,512]{1,0:T(8,128)(2,1)S(1)}, bf16[256,512]{1,0:T(8,128)(2,1)S(1)}, u32[]{:S(2)}, u32[]{:S(2)}) collective-permute-start(bf16[256,512]{1,0:T(8,128)(2,1)S(1)} %collective-permute-done.8.refs_4_), channel_id=1, source_target_pairs={{0,2},{1,3},{4,0},{5,1},{8,4},{9,5},{12,8},{13,9},{14,12},{15,13},... | collective-permute-start | bytes 786440 | tf_op jit(solution)/shard_map/ppermute | solution.py:290
  33.8 8.0 %collective-permute-start.13 = (bf16[256,512]{1,0:T(8,128)(2,1)S(1)}, bf16[256,512]{1,0:T(8,128)(2,1)S(1)}, u32[]{:S(2)}, u32[]{:S(2)}) collective-permute-start(bf16[256,512]{1,0:T(8,128)(2,1)S(1)} %collective-permute-done.7.refs_2_), channel_id=1, source_target_pairs={{0,1},{1,0},{2,3},{3,2},{4,5},{5,4},{6,7},{7,6},{8,9},{9,8},{10,11... | collective-permute-start | bytes 786440 | tf_op jit(solution)/shard_map/ppermute | solution.py:48
  33.8 8.0 %collective-permute-start.14 = (bf16[256,512]{1,0:T(8,128)(2,1)S(1)}, bf16[256,512]{1,0:T(8,128)(2,1)S(1)}, u32[]{:S(2)}, u32[]{:S(2)}) collective-permute-start(bf16[256,512]{1,0:T(8,128)(2,1)S(1)} %collective-permute-done.8.refs_4_), channel_id=1, source_target_pairs={{0,1},{1,0},{2,3},{3,2},{4,5},{5,4},{6,7},{7,6},{8,9},{9,8},{10,11... | collective-permute-start | bytes 786440 | tf_op jit(solution)/shard_map/ppermute | solution.py:48
  35.2 6.6 %collective-permute-start.12 = (bf16[8,32,256]{2,1,0:T(8,128)(2,1)S(1)}, bf16[8,32,256]{2,1,0:T(8,128)(2,1)S(1)}, u32[]{:S(2)}, u32[]{:S(2)}) collective-permute-start(bf16[8,32,256]{2,1,0:T(8,128)(2,1)S(1)} %all-to-all-done.near_ref), channel_id=1, source_target_pairs={{0,1},{1,0},{2,3},{3,2},{4,5},{5,4},{6,7},{7,6},{8,9},{9,8},{10,11... | collective-permute-start | bytes 393224 | tf_op jit(solution)/shard_map/ppermute | solution.py:48
  41.8 9.8 %collective-permute-start.15 = (bf16[256,512]{1,0:T(8,128)(2,1)S(1)}, bf16[256,512]{1,0:T(8,128)(2,1)S(1)}, u32[]{:S(2)}, u32[]{:S(2)}) collective-permute-start(bf16[256,512]{1,0:T(8,128)(2,1)S(1)} %collective-permute-done.10.refs_6_), channel_id=1, source_target_pairs={{0,4},{1,5},{4,8},{5,9},{8,12},{9,13},{12,14},{13,15},{14,10},{15,... | collective-permute-start | bytes 786440 | tf_op jit(solution)/shard_map/ppermute | solution.py:289
  43.1 8.6 %collective-permute-start.16 = (bf16[256,512]{1,0:T(8,128)(2,1)S(1)}, bf16[256,512]{1,0:T(8,128)(2,1)S(1)}, u32[]{:S(2)}, u32[]{:S(2)}) collective-permute-start(bf16[256,512]{1,0:T(8,128)(2,1)S(1)} %collective-permute-done.11.refs_8_), channel_id=1, source_target_pairs={{0,2},{1,3},{4,0},{5,1},{8,4},{9,5},{12,8},{13,9},{14,12},{15,13},... | collective-permute-start | bytes 786440 | tf_op jit(solution)/shard_map/ppermute | solution.py:290
  43.9 7.8 %collective-permute-start.17 = (bf16[256,512]{1,0:T(8,128)(2,1)S(1)}, bf16[256,512]{1,0:T(8,128)(2,1)S(1)}, u32[]{:S(2)}, u32[]{:S(2)}) collective-permute-start(bf16[256,512]{1,0:T(8,128)(2,1)S(1)} %collective-permute-done.10.refs_6_), channel_id=1, source_target_pairs={{0,1},{1,0},{2,3},{3,2},{4,5},{5,4},{6,7},{7,6},{8,9},{9,8},{10,11... | collective-permute-start | bytes 786440 | tf_op jit(solution)/shard_map/ppermute | solution.py:48
  43.9 7.8 %collective-permute-start.18 = (bf16[256,512]{1,0:T(8,128)(2,1)S(1)}, bf16[256,512]{1,0:T(8,128)(2,1)S(1)}, u32[]{:S(2)}, u32[]{:S(2)}) collective-permute-start(bf16[256,512]{1,0:T(8,128)(2,1)S(1)} %collective-permute-done.11.refs_8_), channel_id=1, source_target_pairs={{0,1},{1,0},{2,3},{3,2},{4,5},{5,4},{6,7},{7,6},{8,9},{9,8},{10,11... | collective-permute-start | bytes 786440 | tf_op jit(solution)/shard_map/ppermute | solution.py:48
  51.7 7.5 %collective-permute-start.21 = (bf16[768,256]{1,0:T(8,128)(2,1)S(1)}, bf16[768,256]{1,0:T(8,128)(2,1)S(1)}, u32[]{:S(2)}, u32[]{:S(2)}) collective-permute-start(bf16[768,256]{1,0:T(8,128)(2,1)S(1)} %get-tuple-element.96), channel_id=1, source_target_pairs={{0,1},{1,0},{2,3},{3,2},{4,5},{5,4},{6,7},{7,6},{8,9},{9,8},{10,11... | collective-permute-start | bytes 1179656 | tf_op jit(solution)/shard_map/ppermute | solution.py:48
  52.4 6.0 %collective-permute-start.22 = (bf16[128,512]{1,0:T(8,128)(2,1)S(1)}, bf16[128,512]{1,0:T(8,128)(2,1)S(1)}, u32[]{:S(2)}, u32[]{:S(2)}) collective-permute-start(bf16[128,512]{1,0:T(8,128)(2,1)S(1)} %slice.10), channel_id=1, source_target_pairs={{0,4},{1,5},{4,8},{5,9},{8,12},{9,13},{12,14},{13,15},{14,10},{15,... | collective-permute-start | bytes 393224 | tf_op jit(solution)/shard_map/ppermute | solution.py:289
  62.4 7.7 %collective-permute-start.25 = (bf16[48,512]{1,0:T(8,128)(2,1)S(1)}, bf16[48,512]{1,0:T(8,128)(2,1)S(1)}, u32[]{:S(2)}, u32[]{:S(2)}) collective-permute-start(bf16[48,512]{1,0:T(8,128)(2,1)S(1)} %get-tuple-element.100), channel_id=1, source_target_pairs={{0,12},{1,13},{2,14},{3,15},{4,8},{5,9},{6,10},{7,11},{8,4},{9,5},... | collective-permute-start | bytes 147464 | tf_op jit(solution)/shard_map/ppermute | solution.py:472
  65.7 6.8 %collective-permute-start.26 = (bf16[48,512]{1,0:T(8,128)(2,1)S(1)}, bf16[48,512]{1,0:T(8,128)(2,1)S(1)}, u32[]{:S(2)}, u32[]{:S(2)}) collective-permute-start(bf16[48,512]{1,0:T(8,128)(2,1)S(1)} %get-tuple-element.101), channel_id=1, source_target_pairs={{0,8},{1,9},{2,10},{3,11},{4,12},{5,13},{6,14},{7,15},{8,0},{9,1},... | collective-permute-start | bytes 147464 | tf_op jit(solution)/shard_map/ppermute | solution.py:472
  65.7 8.0 %collective-permute-start.27 = (bf16[48,512]{1,0:T(8,128)(2,1)S(1)}, bf16[48,512]{1,0:T(8,128)(2,1)S(1)}, u32[]{:S(2)}, u32[]{:S(2)}) collective-permute-start(bf16[48,512]{1,0:T(8,128)(2,1)S(1)} %get-tuple-element.102), channel_id=1, source_target_pairs={{0,4},{1,5},{2,6},{3,7},{4,0},{5,1},{6,2},{7,3},{8,12},{9,13},{10,... | collective-permute-start | bytes 147464 | tf_op jit(solution)/shard_map/ppermute | solution.py:472
  66.9 6.8 %collective-permute-start.28 = (bf16[48,512]{1,0:T(8,128)(2,1)S(1)}, bf16[48,512]{1,0:T(8,128)(2,1)S(1)}, u32[]{:S(2)}, u32[]{:S(2)}) collective-permute-start(bf16[48,512]{1,0:T(8,128)(2,1)S(1)} %get-tuple-element.103), channel_id=1, source_target_pairs={{0,14},{1,15},{2,12},{3,13},{4,10},{5,11},{6,8},{7,9},{8,6},{9,7},... | collective-permute-start | bytes 147464 | tf_op jit(solution)/shard_map/ppermute | solution.py:472
  (13 other events, 57.7 us)
